TPU v7x, 32 devices: a whole 2x2x4 slice. The times are simulated.
32 devices in a mesh: seq: 4 (over x, core), clus: 8 (over z, y).
Axes of the slice: x: 2, y: 2, z: 4, core: 2. Of those that a mesh axis runs over, the one named last changes fastest.
Arguments:
- features: bfloat16 [4096, 1024], P(('seq', 'clus')), may hold values from -6 to 6
- shortlist: int32 [4096, 16], P(('seq', 'clus')), may hold values from 0 to 63, all different within a row; in each aligned block of 128 rows (0 to 127, 128 to 255, ...) at most 40 rows name the same one
- positives: int32 [4096, 4], P(('seq', 'clus')), may hold values from 0 to 2047
- cluster_sizes: int32 [64], P('clus'), may hold values from 1 to 128, 6144 in all
- weights: bfloat16 [8192, 1024], P('clus'), may hold values from -0.1875 to 0.1875
Outputs:
- feature_grad: bfloat16 [4096, 1024], P(('seq', 'clus'))
- weight_grad: bfloat16 [8192, 1024], P('clus', 'seq')
Inputs may be any that keep to these rules, and one draw needn't show every extreme that they name: `shortlist`: the 16 ids of a row are distinct; within the rows of one device (aligned blocks of 128 rows) no cluster is named by more than 40 rows, a bound that some block reaches. `positives`: a value q names offset q % 128 of the cluster at shortlist place q // 128; values may repeat, and offsets at or past that cluster's size name nothing. `cluster_sizes`: some cluster has exactly 128 labels.
All inputs are finite; a program needn't handle non-finite values.
Results may differ from a plain program's by a relative error of at most 0.018.
Values may be sent and summed in bfloat16 or wider, within the bound.
No kernel may reach another device: no remote copies, remote signals or barrier semaphores. Data moves between devices by JAX's collectives and lax.ppermute only.
A program may use at most 64 MiB of HBM per device.

v0:
```python
import math

import jax
import jax.numpy as jnp
from jax import lax
from jax.sharding import PartitionSpec as P

BLOCK = 128


def block_plan(short_block, cluster_ids, most_slots):
    hit_table = (short_block[:, :, None] == cluster_ids[None, None, :]).astype(jnp.int32)
    member = jnp.sum(hit_table, axis=1)
    position = jnp.sum(
        hit_table * jnp.arange(short_block.shape[1], dtype=jnp.int32)[None, :, None], axis=1
    )
    ranking = jnp.cumsum(member, axis=0) - member
    slot_ids = jnp.arange(most_slots, dtype=jnp.int32)
    chosen = member[:, :, None] * (ranking[:, :, None] == slot_ids[None, None, :]).astype(jnp.int32)
    owner_row = jnp.sum(
        chosen * jnp.arange(short_block.shape[0], dtype=jnp.int32)[:, None, None], axis=0
    )
    short_place = jnp.sum(chosen * position[:, :, None], axis=0)
    filled = jnp.sum(chosen, axis=0)
    return (owner_row, short_place, filled, ranking)


def slot_targets(pos_rows, short_place, filled):
    matches = (pos_rows // BLOCK == short_place[..., None]) & (filled[..., None] > 0)
    return jnp.where(matches, pos_rows % BLOCK, -1)


def cluster_work(tile_rows, targets, filled, local_weights, local_sizes):
    label_ids = jnp.arange(BLOCK, dtype=jnp.int32)
    logits = jnp.einsum(
        "krd,kod->kro", tile_rows, local_weights, preferred_element_type=jnp.float32
    )
    positive = jnp.any(targets[:, :, :, None] == label_ids[None, None, None, :], axis=2)
    target_sign = jnp.where(positive, 1.0, -1.0)
    live_entry = (label_ids[None, None, :] < local_sizes[:, None, None]) & (filled[:, :, None] > 0)
    hinge_slope = jnp.where(
        live_entry, -2.0 * target_sign * jnp.maximum(1.0 - target_sign * logits, 0.0), 0.0
    ).astype(jnp.bfloat16)
    pair_grads = jnp.einsum(
        "kro,kod->krd", hinge_slope, local_weights, preferred_element_type=jnp.float32
    ).astype(jnp.bfloat16)
    label_part = jnp.einsum(
        "kro,krd->kod", hinge_slope, tile_rows, preferred_element_type=jnp.float32
    )
    return (pair_grads, label_part)


def local(features, shortlist, positives, cluster_sizes, weights):
    inst_rows = features.shape[0]
    feature_width = features.shape[1]
    top_count = shortlist.shape[1]
    clus_count = lax.axis_size("clus")
    local_count = cluster_sizes.shape[0]
    all_clusters = local_count * clus_count
    most_slots = max(2, inst_rows * top_count * 5 // (4 * all_clusters))
    all_ids = jnp.arange(all_clusters, dtype=jnp.int32)
    own_owner, own_place, own_filled, own_rank = block_plan(shortlist, all_ids, most_slots)
    pair_rank = jnp.take_along_axis(own_rank, shortlist, axis=1)
    group_feat, group_short, group_pos = (
        lax.all_gather(features, "clus", axis=0, tiled=True),
        lax.all_gather(shortlist, "clus", axis=0, tiled=True),
        lax.all_gather(positives, "clus", axis=0, tiled=True),
    )
    local_ids = lax.axis_index("clus") * local_count + jnp.arange(local_count, dtype=jnp.int32)

    def plan_one(short_block):
        owner_row, short_place, filled_slots, ranking = block_plan(
            short_block, local_ids, most_slots
        )
        return (owner_row, short_place, filled_slots)

    owner_blocks, place_blocks, filled_blocks = jax.vmap(plan_one)(
        group_short.reshape(clus_count, inst_rows, top_count)
    )
    block_offsets = jnp.arange(clus_count, dtype=jnp.int32)[:, None, None] * inst_rows
    slot_total = clus_count * most_slots
    global_owner = jnp.transpose(owner_blocks + block_offsets, (1, 0, 2)).reshape(
        local_count, slot_total
    )
    short_place = jnp.transpose(place_blocks, (1, 0, 2)).reshape(local_count, slot_total)
    filled = jnp.transpose(filled_blocks, (1, 0, 2)).reshape(local_count, slot_total)
    tile_rows = group_feat[global_owner] * filled.astype(jnp.bfloat16)[:, :, None]
    targets = slot_targets(group_pos[global_owner], short_place, filled)
    local_weights = weights.reshape(local_count, BLOCK, feature_width)
    pair_grads, label_part = cluster_work(tile_rows, targets, filled, local_weights, cluster_sizes)
    returned = lax.all_to_all(pair_grads, "clus", split_axis=1, concat_axis=0, tiled=True)
    flat_grads = returned.reshape(all_clusters * most_slots, feature_width)
    gathered = flat_grads[shortlist * most_slots + pair_rank]
    feature_grad = jnp.sum(gathered, axis=1, dtype=jnp.float32).astype(jnp.bfloat16)
    summed = lax.psum_scatter(
        label_part.reshape(local_count * BLOCK, feature_width).astype(jnp.bfloat16),
        "seq",
        scatter_dimension=1,
        tiled=True,
    ).astype(jnp.float32)
    pairs_mean = inst_rows * lax.axis_size("seq") * top_count // local_count
    weight_grad = (summed * (1.0 / math.sqrt(pairs_mean))).astype(jnp.bfloat16)
    return (feature_grad, weight_grad)


def solution(mesh):
    return jax.shard_map(
        local,
        mesh=mesh,
        in_specs=(
            P(("seq", "clus"), None),
            P(("seq", "clus"), None),
            P(("seq", "clus"), None),
            P("clus"),
            P("clus", None),
        ),
        out_specs=(P(("seq", "clus"), None), P("clus", "seq")),
        check_vma=False,
    )
```

profile of v0, /device:TPU:0, one launch (start us, length us, event | category | flops | bytes accessed | tf_op | source)
XLA Modules:
  0.0 280.3 jit_solution(7584628260551258498)
XLA Ops:
  7.2 0.7 all-gather.2.cloned.1.call-update
  7.9 0.8 copy.84
  8.7 32.6 %all_gather.9 = s32[1024,16]{0,1:T(8,128)S(1)} all-gather(s32[128,16]{0,1:T(8,128)} %param.6), channel_id=1, replica_groups=mesh['seq'=4,'clus'=8] {'clus'}, dimensions={0}, use_global_device_ids=true | all-gather | bytes 73728 | tf_op jit(solution)/shard_map/all_gather | solution.py:66
  41.4 0.2 fusion.33
  41.5 0.2 copy.80
  41.8 23.3 %fusion.34 = s32[8,128,8]{2,0,1:T(8,128)S(1)} fusion(s32[8,128,8]{2,0,1:T(8,128)S(1)} %copy.80), kind=kOutput, calls=%fused_computation.57 | output fusion | flops 1040384 | bytes 65536 | tf_op jit(solution)/shard_map/vmap(jit(cumsum))/reduce_window_sum | solution.py:17
  65.1 0.2 copy.82
  65.3 3.3 %fusion.30 = (s32[8,8,40]{2,1,0:T(8,128)S(1)}, s32[8,8,40]{2,1,0:T(8,128)S(1)}, s32[8,8,40]{2,1,0:T(8,128)S(1)}) fusion(s32[8,128,8]{1,2,0:T(8,128)S(1)} %get-tuple-element.2, s32[8,128,8]{1,2,0:T(8,128)S(1)} %get-tuple-element.3, s32[8,128,8]{1,2,0:T(8,128)S(1)} %copy.82), kind=kLoop, calls=%fused_computation.33 | loop fusion | flops 2286080 | bytes 129024 | tf_op jit(solution)/shard_map/vmap()/reduce_sum | solution.py:23
  69.2 31.4 %all_gather.10 = s32[1024,4]{1,0:T(8,128)S(1)} all-gather(s32[128,4]{1,0:T(8,128)S(1)} %copy.84), channel_id=1, replica_groups=mesh['seq'=4,'clus'=8] {'clus'}, dimensions={0}, use_global_device_ids=true | all-gather | bytes 18432 | tf_op jit(solution)/shard_map/all_gather | solution.py:67
  100.6 5.6 %gather_fusion = s32[2560,4]{1,0:T(8,128)} fusion(s32[1024,4]{1,0:T(8,128)S(1)} %all_gather.10, s32[3072]{0:T(1024)S(1)} %pad_clamp_fusion), kind=kCustom, calls=%fused_computation | custom fusion | bytes 92160 | tf_op jit(solution)/shard_map/gather | solution.py:88
  106.2 3.8 %fusion.28 = s32[8,320,4]{2,1,0:T(8,128)S(1)} fusion(s32[8,320,4]{2,1,0:T(8,128)} %bitcast.38, s32[8,320]{1,0:T(8,128)S(1)} %eq.77, pred[8,320]{1,0:T(8,128)(4,1)S(1)} %gt.17), kind=kLoop, calls=%fused_computation.31 | loop fusion | flops 225280 | bytes 94720 | tf_op jit(solution)/shard_map/jit(_where)/select_n | solution.py:30
  110.0 0.5 copy.87
  110.5 2.1 fusion
  112.7 14.0 %gather_fusion.1 = bf16[2560,1024]{1,0:T(8,128)(2,1)} fusion(bf16[1024,1024]{1,0:T(8,128)(2,1)} %all-gather.2.cloned.1.call-done, s32[3072]{0:T(1024)S(1)} %pad_clamp_fusion), kind=kCustom, calls=%fused_computation.1 | custom fusion | bytes 10496000 | tf_op jit(solution)/shard_map/gather | solution.py:87
  126.6 3.7 %fusion.24 = bf16[8,320,128]{2,1,0:T(8,128)(2,1)S(1)} fusion(bf16[8,128,1024]{2,1,0:T(8,128)(2,1)S(1)} %bitcast.33, bf16[8,320,1024]{2,1,0:T(8,128)(2,1)} %bitcast.36, bf16[8,320]{1,0:T(8,128)(2,1)S(1)} %convert_element_type.43, pred[8,320,128]{2,1,0:T(8,128)(4,1)S(1)} %fusion, pred[8,320]{1,0:T(8,128)(4,1)S(1)} %gt.17, ...), kind=kOutput, calls=%fused_computation.29 | convolution fusion | flops 676659200 | bytes 8331776 | tf_op jit(solution)/shard_map/krd,kod->kro/dot_general | solution.py:35
  130.4 1.5 convolution_convert_fusion
  131.9 5.3 %copy.89 = bf16[8,320,1024]{2,0,1:T(8,128)(2,1)} copy(bf16[8,320,1024]{2,1,0:T(8,128)(2,1)S(1)} %convolution_convert_fusion) | data formatting | bytes 10485760 | tf_op jit(solution)/shard_map/convert_element_type | solution.py:46
  137.2 5.7 %all-to-all-start = ((bf16[8,320,1024]{2,0,1:T(8,128)(2,1)}), bf16[8,320,1024]{2,0,1:T(8,128)(2,1)}, u32[]{:S(2)}, u32[]{:S(2)}) async-start(bf16[8,320,1024]{2,0,1:T(8,128)(2,1)} %copy.89), calls=%async_computation | async-start | bytes 10485760 | tf_op jit(solution)/shard_map/all_to_all | solution.py:91
  142.8 0.3 reduce-scatter.2.cloned.1.call-start
  143.1 5.2 %fusion.7 = bf16[8,128,1024]{2,1,0:T(8,128)(2,1)} fusion(bf16[8,320,128]{2,1,0:T(8,128)(2,1)S(1)} %fusion.24, bf16[8,320,1024]{2,1,0:T(8,128)(2,1)} %bitcast.37, bf16[8,320]{1,0:T(8,128)(2,1)S(1)} %convert_element_type.43), kind=kOutput, calls=%fused_computation.22 | convolution fusion | flops 674758656 | bytes 8000512 | tf_op jit(solution)/shard_map/kro,krd->kod/dot_general | solution.py:47
  148.3 0.7 copy-done.1
  149.1 0.1 copy.91
  149.2 0.1 copy.93
  149.4 0.2 reduce_window_sum.23
  149.5 13.6 %gather_fusion.3 = s32[2048]{0:T(1024)S(1)} fusion(s32[128,64]{1,0:T(8,128)S(1)} %sub.23, s32[2048]{0:T(1024)S(1)} %reshape.172), kind=kCustom, calls=%fused_computation.3 | custom fusion | bytes 32768 | tf_op jit(solution)/shard_map/jit(take_along_axis)/gather | solution.py:63
  163.3 0.1 copy.95
  163.5 17.5 %reduce-scatter.2.cloned.1.call-done = bf16[1024,256]{1,0:T(8,128)(2,1)} async-done(((bf16[1024,1024]{1,0:T(8,128)(2,1)}), bf16[1024,256]{1,0:T(8,128)(2,1)}) %reduce-scatter.2.cloned.1.call-update) | async-done | bytes 524304 | tf_op jit(solution)/shard_map/reduce_scatter | solution.py:95
  181.0 1.9 multiply_convert_fusion
  183.0 63.4 %all-to-all-done = bf16[8,320,1024]{2,0,1:T(8,128)(2,1)} async-done(((bf16[8,320,1024]{2,0,1:T(8,128)(2,1)}), bf16[8,320,1024]{2,0,1:T(8,128)(2,1)}, u32[]{:S(2)}, u32[]{:S(2)}) %all-to-all-start) | async-done | bytes 5242912 | tf_op jit(solution)/shard_map/all_to_all | solution.py:91
  246.3 7.9 %copy.90 = bf16[8,8,40,1024]{3,2,0,1:T(8,128)(2,1)} copy(bf16[8,8,40,1024]{3,0,2,1:T(8,128)(2,1)} %bitcast.7) | data formatting | bytes 10485760 | tf_op jit(solution)/shard_map/all_to_all | solution.py:91
  254.3 14.1 %gather_fusion.2 = bf16[2048,1024]{1,0:T(8,128)(2,1)} fusion(bf16[2560,1024]{1,0:T(8,128)(2,1)} %bitcast.35, s32[2048]{0:T(1024)S(1)} %broadcast_clamp_fusion), kind=kCustom, calls=%fused_computation.2 | custom fusion | bytes 8396800 | tf_op jit(solution)/shard_map/gather | solution.py:93
  268.4 5.0 %bitcast_reduce_fusion = bf16[128,1024]{1,0:T(8,128)(2,1)} fusion(bf16[2048,1024]{1,0:T(8,128)(2,1)} %gather_fusion.2), kind=kLoop, calls=%fused_computation.10 | loop fusion | flops 1966080 | bytes 4456448 | tf_op jit(solution)/shard_map/reduce_sum | solution.py:94
  (35 shorter events, 1.1 us)
Async XLA Ops:
  7.2 119.5 %copy-start = (bf16[1024,1024]{1,0:T(8,128)(2,1)S(1)}, bf16[1024,1024]{1,0:T(8,128)(2,1)}, u32[]{:S(2)}) copy-start(bf16[1024,1024]{1,0:T(8,128)(2,1)} %param.9) | copy-start | bytes 6291460
  7.2 105.5 %all-gather.2.cloned.1.call-start = ((), (), s32[]{:S(2)}) async-start(), calls=%async_computation.2 | async-start | bytes 2359296 | tf_op jit(solution)/shard_map/all_gather | solution.py:65
  110.0 2.6 copy-start.2
  137.2 109.2 %all-to-all-start = ((bf16[8,320,1024]{2,0,1:T(8,128)(2,1)}), bf16[8,320,1024]{2,0,1:T(8,128)(2,1)}, u32[]{:S(2)}, u32[]{:S(2)}) async-start(bf16[8,320,1024]{2,0,1:T(8,128)(2,1)} %copy.89), calls=%async_computation | async-start | bytes 10485760 | tf_op jit(solution)/shard_map/all_to_all | solution.py:91
  142.8 38.2 %reduce-scatter.2.cloned.1.call-start = ((), (), s32[]{:S(2)}) async-start(), calls=%async_computation.3 | async-start | bytes 2621440 | tf_op jit(solution)/shard_map/reduce_scatter | solution.py:95
  148.3 0.7 copy-start.1
Sparse Core Ops, SparseCore 0:
  10.1 52.2 all-gather.1
  148.4 32.5 reduce-scatter.1
where the time goes:
time: 281 us; the launch traced here: 280 us
  waiting for transfers between devices  81.6 us (29%)
  blocking collectives  64 us (23%)
  local copies, waits for them, and re-layouts  63.9 us (23%)
  other arithmetic  40.1 us (14%)
  between operations  14.2 us (5%)
  matrix products  10.4 us (4%)
  starting transfers between devices  5.96 us (2%)
    all_to_all x1, waiting for transfers between devices, local(): lax.all_to_all(pair_grads, 'clus', split_axis=1, concat_axis=0, tiled=True)  63.4 us
    all_gather x1, blocking collectives, local(): lax.all_gather(shortlist, 'clus', axis=0, tiled=True)  32.6 us
    all_gather x1, blocking collectives, local(): lax.all_gather(positives, 'clus', axis=0, tiled=True)  31.4 us
    another operation x2, other arithmetic, block_plan(): ranking = jnp.cumsum(member, axis=0) - member  23.5 us
    reduce_scatter x1, waiting for transfers between devices, local(): lax.psum_scatter(label_part.reshape(local_count * BLOCK, feature_width).a...  17.5 us
    gather x1, local copies, waits for them, and re-layouts, local(): gathered = flat_grads[shortlist * most_slots + pair_rank]  14.1 us
    gather x1, local copies, waits for them, and re-layouts, local(): group_feat[global_owner] * filled.astype(jnp.bfloat16)[:, :, None]  14 us
    gather x5, local copies, waits for them, and re-layouts, local(): pair_rank = jnp.take_along_axis(own_rank, shortlist, axis=1)  13.9 us
  transfers between devices with their start and end apart: 3, of which 2 were waited for; matrix products, arithmetic and copies ran while one was open for 22% of the time, Pallas kernels for 0%

commit v1 on v0

v1 whole, which is shorter than its diff:
```python
import functools
import math

import jax
import jax.numpy as jnp
from jax import lax
from jax.experimental import pallas as pl
from jax.experimental.pallas import tpu as pltpu
from jax.sharding import PartitionSpec as P

BLOCK = 128
LANES = 128
CHUNK = 256
VMEM_LIMIT = 40 * 1024 * 1024


def pack_kernel(all_clusters, feat_ref, short_ref, pos_ref, out_ref):
    rows, width = feat_ref.shape
    top_count, pos_count = short_ref.shape[1], pos_ref.shape[1]
    meta_width = out_ref.shape[1] - width
    out_ref[:, :width] = feat_ref[...]
    short = short_ref[...]
    places = pos_ref[...] // BLOCK
    offsets = pos_ref[...] % BLOCK
    targets = jnp.zeros_like(places)
    for j in range(top_count):
        targets = targets + jnp.where(places == j, short[:, j : j + 1], 0)
    column = lax.broadcasted_iota(jnp.int32, (rows, meta_width), 1)
    meta = jnp.zeros((rows, meta_width), jnp.int32)
    for j in range(top_count):
        meta = jnp.where(column == short[:, j : j + 1], 1, meta)
    for q in range(pos_count):
        meta = jnp.where(column == all_clusters + q, targets[:, q : q + 1], meta)
        meta = jnp.where(column == all_clusters + pos_count + q, offsets[:, q : q + 1], meta)
    out_ref[:, width:] = meta.astype(jnp.float32).astype(jnp.bfloat16)


def pack(features, shortlist, positives, all_clusters):
    rows, width = features.shape
    meta_width = -(-(all_clusters + 2 * positives.shape[1]) // LANES) * LANES
    return pl.pallas_call(
        functools.partial(pack_kernel, all_clusters),
        out_shape=jax.ShapeDtypeStruct((rows, width + meta_width), jnp.bfloat16),
        compiler_params=pltpu.CompilerParams(vmem_limit_bytes=VMEM_LIMIT),
        name="pack",
    )(features, shortlist, positives)


def block_kernel(block_count, all_clusters, pos_count, first_ref, *refs):
    x_refs = refs[:block_count]
    w_ref, live_ref = refs[block_count : block_count + 2]
    grad_refs = refs[block_count + 2 : 2 * block_count + 2]
    slope_refs = refs[2 * block_count + 2 :]
    labels, width = w_ref.shape
    rows = [ref.shape[0] for ref in x_refs]
    starts = [sum(rows[:k]) for k in range(block_count)]

    def joined(values):
        return values[0] if block_count == 1 else jnp.concatenate(values, axis=0)

    x = joined([ref[:, :width] for ref in x_refs])
    meta = joined([ref[:, width:] for ref in x_refs])
    numbers = meta.astype(jnp.float32)
    first = first_ref[0].astype(jnp.float32)
    target = [
        (numbers[:, all_clusters + q : all_clusters + q + 1] - first) * BLOCK
        + numbers[:, all_clusters + pos_count + q : all_clusters + pos_count + q + 1]
        for q in range(pos_count)
    ]
    total = None
    for start in range(0, labels, CHUNK):
        w_part = w_ref[start : start + CHUNK, :]
        logits = lax.dot_general(
            x, w_part, (((1,), (1,)), ((), ())), preferred_element_type=jnp.float32
        )
        live = jnp.dot(
            meta, live_ref[:, start : start + CHUNK], preferred_element_type=jnp.float32
        )
        label = (
            lax.broadcasted_iota(jnp.int32, (1, CHUNK), 1) + start
        ).astype(jnp.float32)
        positive = target[0] == label
        for q in range(1, pos_count):
            positive = positive | (target[q] == label)
        turned = jnp.where(positive, -1.0, 1.0)
        slope = (turned * live * jnp.maximum(1.0 + turned * logits, 0.0)).astype(jnp.bfloat16)
        for ref, at, count in zip(slope_refs, starts, rows):
            ref[:, start : start + CHUNK] = slope[at : at + count]
        part = jnp.dot(slope, w_part, preferred_element_type=jnp.float32)
        total = part if total is None else total + part
    for ref, at, count in zip(grad_refs, starts, rows):
        ref[...] = total[at : at + count].astype(jnp.bfloat16)


def block_work(blocks, weights, live_table, first, all_clusters, pos_count):
    labels, width = weights.shape
    count = len(blocks)
    rows = [block.shape[0] for block in blocks]
    out = pl.pallas_call(
        functools.partial(block_kernel, count, all_clusters, pos_count),
        out_shape=[jax.ShapeDtypeStruct((r, width), jnp.bfloat16) for r in rows]
        + [jax.ShapeDtypeStruct((r, labels), jnp.bfloat16) for r in rows],
        in_specs=[pl.BlockSpec(memory_space=pltpu.SMEM)]
        + [pl.BlockSpec(memory_space=pltpu.VMEM)] * (count + 2),
        compiler_params=pltpu.CompilerParams(vmem_limit_bytes=VMEM_LIMIT),
        cost_estimate=pl.CostEstimate(
            flops=4 * sum(rows) * labels * width,
            bytes_accessed=2 * labels * width + 6 * sum(rows) * width,
            transcendentals=0,
        ),
        name="block_work",
    )(first, *blocks, weights, live_table)
    return out[:count], out[count:]


def weight_kernel(block_count, column_blocks, scale, own_ref, *refs):
    x_refs = refs[:block_count]
    s_refs = refs[block_count : 2 * block_count]
    out_refs = refs[2 * block_count :]
    labels, part_width = out_refs[0].shape
    slopes = jnp.concatenate([ref[...] for ref in s_refs], axis=0)
    for ref, q in zip(out_refs, column_blocks):
        at = pl.multiple_of((own_ref[0] ^ q) * part_width, part_width)
        x = jnp.concatenate([r[:, pl.ds(at, part_width)] for r in x_refs], axis=0)
        part = lax.dot_general(
            slopes, x, (((0,), (0,)), ((), ())), preferred_element_type=jnp.float32
        )
        ref[...] = (part * scale).astype(jnp.bfloat16)


def weight_work(blocks, slopes, own, column_blocks, part_width, scale):
    count = len(blocks)
    labels = slopes[0].shape[1]
    rows = sum(block.shape[0] for block in blocks)
    return pl.pallas_call(
        functools.partial(weight_kernel, count, column_blocks, scale),
        out_shape=[jax.ShapeDtypeStruct((labels, part_width), jnp.bfloat16)] * len(column_blocks),
        in_specs=[pl.BlockSpec(memory_space=pltpu.SMEM)]
        + [pl.BlockSpec(memory_space=pltpu.VMEM)] * (2 * count),
        compiler_params=pltpu.CompilerParams(vmem_limit_bytes=VMEM_LIMIT),
        cost_estimate=pl.CostEstimate(
            flops=2 * rows * labels * part_width * len(column_blocks),
            bytes_accessed=2 * rows * (labels + 1024) + 2 * labels * part_width,
            transcendentals=0,
        ),
        name="weight_work",
    )(own, *blocks, *slopes)


def add(*parts):
    total = parts[0].astype(jnp.float32)
    for part in parts[1:]:
        total = total + part.astype(jnp.float32)
    return total.astype(jnp.bfloat16)


def local(features, shortlist, positives, cluster_sizes, weights):
    inst_rows, width = features.shape
    top_count, pos_count = shortlist.shape[1], positives.shape[1]
    clus_count, seq_count = lax.axis_size("clus"), lax.axis_size("seq")
    local_count = cluster_sizes.shape[0]
    all_clusters = local_count * clus_count
    part_width = width // seq_count
    labels = weights.shape[0]

    ring = list(range(0, clus_count, 2)) + list(range(1, clus_count, 2))[::-1]
    onward = [(ring[k], ring[(k + 1) % clus_count]) for k in range(clus_count)]
    back = [(b, a) for a, b in onward]

    def send(array, pairs):
        return lax.ppermute(array, "clus", pairs)

    packed = pack(features, shortlist, positives, all_clusters)
    first = lax.axis_index("clus") * local_count
    column = jnp.arange(labels, dtype=jnp.int32)
    size = jnp.repeat(cluster_sizes, BLOCK)
    named = jnp.arange(packed.shape[1] - width, dtype=jnp.int32)[:, None] == first + column // BLOCK
    live_table = jnp.where(named & (column % BLOCK < size), 2.0, 0.0).astype(jnp.bfloat16)
    first = first.astype(jnp.int32).reshape(1)

    def work(blocks):
        return block_work(blocks, weights, live_table, first, all_clusters, pos_count)

    half, steps = inst_rows // 2, clus_count // 2
    used, slopes = [packed], []
    parts = {}
    from_back, from_front = packed, packed
    for k in range(1, steps + 1):
        if k == steps:
            from_back, from_front = from_back[:half], from_front[half:]
        arriving = send(from_back, onward), send(from_front, back)
        if k == 1:
            (own_part,), own_slopes = work([packed])
            slopes += own_slopes
        else:
            parts[k - 1], new_slopes = work([from_back_held, from_front_held])
            slopes += new_slopes
        from_back, from_front = arriving
        from_back_held, from_front_held = arriving
        used += [from_back, from_front]
    parts[steps], new_slopes = work([from_back_held, from_front_held])
    slopes += new_slopes

    scale = 1.0 / math.sqrt(inst_rows * seq_count * top_count // local_count)
    own = lax.axis_index("seq").astype(jnp.int32).reshape(1)

    def seq_send(array, bit):
        return lax.ppermute(array, "seq", [(k, k ^ bit) for k in range(seq_count)])

    away = [q for q in range(seq_count) if q & 1]
    kept = [q for q in range(seq_count) if not q & 1]
    slots = dict(zip(away, weight_work(used, slopes, own, away, part_width, scale)))
    slots.update(zip(kept, weight_work(used, slopes, own, kept, part_width, scale)))
    bit = 1
    while bit < seq_count:
        going = [q for q in sorted(slots) if q & bit]
        for q in going:
            slots[q ^ bit] = add(slots[q ^ bit], seq_send(slots.pop(q), bit))
        bit *= 2
    weight_grad = slots[0]

    to_back, to_front = parts[steps]
    for k in range(steps, 0, -1):
        got_back, got_front = send(to_front, onward), send(to_back, back)
        if k == steps:
            near_back, near_front = parts[k - 1] if k > 1 else (own_part, None)
            if k > 1:
                to_back = jnp.concatenate([add(near_back[:half], got_front), near_back[half:]], axis=0)
                to_front = jnp.concatenate([near_front[:half], add(near_front[half:], got_back)], axis=0)
        elif k > 1:
            near_back, near_front = parts[k - 1]
            to_back, to_front = add(near_back, got_front), add(near_front, got_back)
    feature_grad = add(own_part, got_back, got_front)
    return (feature_grad, weight_grad)


def solution(mesh):
    return jax.shard_map(
        local,
        mesh=mesh,
        in_specs=(
            P(("seq", "clus"), None),
            P(("seq", "clus"), None),
            P(("seq", "clus"), None),
            P("clus"),
            P("clus", None),
        ),
        out_specs=(P(("seq", "clus"), None), P("clus", "seq")),
        check_vma=False,
    )
```

time: 281 us -> 69.8 us (0.25)
  blocking collectives: 64 us -> 0 us
  local copies, waits for them, and re-layouts: 63.9 us -> 4.17 us
  waiting for transfers between devices: 81.6 us -> 29 us
  other arithmetic: 40.1 us -> 3.21 us
  starting transfers between devices: 5.96 us -> 20 us
  between operations: 14.2 us -> 0.8 us
  Pallas kernels: 0 us -> 12.3 us
  matrix products: 10.4 us -> 0 us
    all_gather x2 -> x0, blocking collectives: 64 us -> none  [the longest x1 32.6 us: local(): lax.all_gather(shortlist, 'clus', axis=0, tiled=True)]
    all_to_all x1 -> x0, waiting for transfers between devices: 63.4 us -> none  [local(): lax.all_to_all(pair_grads, 'clus', split_axis=1, concat_axis=0, tiled=True)]
    gather x8 -> x0, local copies, waits for them, and re-layouts: 47.6 us -> none  [the longest x1 14.1 us: local(): gathered = flat_grads[shortlist * most_slots + pair_rank]]
    ppermute x0 -> x19, waiting for transfers between devices: none -> 29 us  [the longest x16 29 us: send(): return lax.ppermute(array, 'clus', pairs)]
    another operation x2 -> x0, other arithmetic: 23.5 us -> none  [block_plan(): ranking = jnp.cumsum(member, axis=0) - member]
    ppermute x0 -> x19, starting transfers between devices: none -> 20 us  [the longest x16 17.9 us: send(): return lax.ppermute(array, 'clus', pairs)]
    reduce_scatter x1 -> x0, waiting for transfers between devices: 17.5 us -> none  [local(): lax.psum_scatter(label_part.reshape(local_count * BLOCK, feature_width).a...]
    pallas_call x0 -> x8, Pallas kernels: none -> 12.3 us  [the longest x5 9.16 us: block_work(): pl.pallas_call(functools.partial(block_kernel, count, all_clusters, pos_c...]
  transfers between devices with their start and end apart: 3 -> 19, of which waited for: 2 -> 9; matrix products, arithmetic and copies ran while one was open for 22% -> 3% of each run, Pallas kernels for 0% -> 15%
where the time goes in v1:
time: 69.8 us; the launch traced here: 69.5 us
  waiting for transfers between devices  29 us (42%)
  starting transfers between devices  20 us (29%)
  Pallas kernels  12.3 us (18%)
  local copies, waits for them, and re-layouts  4.17 us (6%)
  other arithmetic  3.21 us (5%)
  between operations  0.8 us (1%)
    ppermute x16, waiting for transfers between devices, send(): return lax.ppermute(array, 'clus', pairs)  29 us
    ppermute x16, starting transfers between devices, send(): return lax.ppermute(array, 'clus', pairs)  17.9 us
    pallas_call x5, Pallas kernels, block_work(): pl.pallas_call(functools.partial(block_kernel, count, all_clusters, pos_c...  9.16 us
    unnamed x8, local copies, waits for them, and re-layouts  4.12 us
    pallas_call x2, Pallas kernels, weight_work(): pl.pallas_call(functools.partial(weight_kernel, count, column_blocks, sca...  2.59 us
    convert_element_type x9, other arithmetic, add(): return total.astype(jnp.bfloat16)  2.34 us
    ppermute x3, starting transfers between devices, seq_send(): return lax.ppermute(array, 'seq', [(k, k ^ bit) for k in range(seq_count)])  2.11 us
  transfers between devices with their start and end apart: 19, of which 9 were waited for; matrix products, arithmetic and copies ran while one was open for 3% of the time, Pallas kernels for 15%

profile of v1, /device:TPU:0, one launch (start us, length us, event | category | flops | bytes accessed | tf_op | source)
XLA Modules:
  0.0 69.5 jit_solution(15182897085084638296)
XLA Ops:
  0.6 0.8 %copy.7.short_ref = s32[128,16]{1,0:T(8,128)S(1)} copy(s32[128,16]{0,1:T(8,128)} %param.6) | data formatting | bytes 16384 | tf_op args[1]
  1.4 0.8 %copy.8.pos_ref = s32[128,4]{1,0:T(8,128)S(1)} copy(s32[128,4]{0,1:T(4,128)} %param.7) | data formatting | bytes 4096 | tf_op args[2]
  2.2 0.9 %copy-done.2 = bf16[128,1024]{1,0:T(8,128)(2,1)S(1)} copy-done((bf16[128,1024]{1,0:T(8,128)(2,1)S(1)}, bf16[128,1024]{1,0:T(8,128)(2,1)}, u32[]{:S(2)}) %copy-start.2) | copy-done | bytes 262168
  3.8 3.0 %collective-permute-start.1 = (bf16[128,1152]{1,0:T(8,128)(2,1)S(1)}, bf16[128,1152]{1,0:T(8,128)(2,1)S(1)}, u32[]{:S(2)}, u32[]{:S(2)}) collective-permute-start(bf16[128,1152]{1,0:T(8,128)(2,1)S(1)} %pack.1.refs_0_), channel_id=1, source_target_pairs={{2,0},{4,2},{6,4},{7,6},{5,7},{3,5},{1,3},{0,1},{10,8},{12,10},{14... | collective-permute-start | bytes 884744 | tf_op jit(solution)/shard_map/ppermute | solution.py:171
  6.9 6.9 %collective-permute-done.1.refs_1_.refs_2_ = bf16[128,1152]{1,0:T(8,128)(2,1)S(1)} collective-permute-done((bf16[128,1152]{1,0:T(8,128)(2,1)S(1)}, bf16[128,1152]{1,0:T(8,128)(2,1)S(1)}, u32[]{:S(2)}, u32[]{:S(2)}) %collective-permute-start.1) | collective-permute-done | bytes 294944 | tf_op jit(solution)/shard_map/ppermute | solution.py:171
  13.9 1.7 %collective-permute-start.3 = (bf16[128,1152]{1,0:T(8,128)(2,1)S(1)}, bf16[128,1152]{1,0:T(8,128)(2,1)S(1)}, u32[]{:S(2)}, u32[]{:S(2)}) collective-permute-start(bf16[128,1152]{1,0:T(8,128)(2,1)S(1)} %collective-permute-done.1.refs_1_.refs_2_), channel_id=1, source_target_pairs={{2,0},{4,2},{6,4},{7,6},{5,7},{3,5},{1,3},{0,1},{10,8},{12,10},{14... | collective-permute-start | bytes 884744 | tf_op jit(solution)/shard_map/ppermute | solution.py:171
  15.9 0.7 %fusion.8 = pred[1024]{0:T(1024)(128)(4,1)S(1)} fusion(s32[8]{0:T(128)} %param.8), kind=kLoop, calls=%fused_computation.26 | loop fusion | flops 7168 | bytes 1056 | tf_op jit(solution)/shard_map/lt | solution.py:178
  16.6 5.4 %collective-permute-done.3.refs_1_.refs_4_ = bf16[128,1152]{1,0:T(8,128)(2,1)S(1)} collective-permute-done((bf16[128,1152]{1,0:T(8,128)(2,1)S(1)}, bf16[128,1152]{1,0:T(8,128)(2,1)S(1)}, u32[]{:S(2)}, u32[]{:S(2)}) %collective-permute-start.3) | collective-permute-done | bytes 294944 | tf_op jit(solution)/shard_map/ppermute | solution.py:171
  22.0 1.4 %collective-permute-start.5 = (bf16[128,1152]{1,0:T(8,128)(2,1)S(1)}, bf16[128,1152]{1,0:T(8,128)(2,1)S(1)}, u32[]{:S(2)}, u32[]{:S(2)}) collective-permute-start(bf16[128,1152]{1,0:T(8,128)(2,1)S(1)} %collective-permute-done.3.refs_1_.refs_4_), channel_id=1, source_target_pairs={{2,0},{4,2},{6,4},{7,6},{5,7},{3,5},{1,3},{0,1},{10,8},{12,10},{14... | collective-permute-start | bytes 884744 | tf_op jit(solution)/shard_map/ppermute | solution.py:171
  24.2 1.6 %copy-done = bf16[1024,1024]{1,0:T(8,128)(2,1)S(1)} copy-done((bf16[1024,1024]{1,0:T(8,128)(2,1)S(1)}, bf16[1024,1024]{1,0:T(8,128)(2,1)}, u32[]{:S(2)}) %copy-start) | copy-done | bytes 2097176
  25.8 1.7 %block_work.5 = (bf16[128,1024]{1,0:T(8,128)(2,1)S(1)}, bf16[128,1024]{1,0:T(8,128)(2,1)S(1)}) custom-call(s32[1]{0:T(128)} %bitcast.first_ref, bf16[128,1152]{1,0:T(8,128)(2,1)S(1)} %pack.1.refs_0_, bf16[1024,1024]{1,0:T(8,128)(2,1)S(1)} %copy-done, bf16[128,1024]{1,0:T(8,128)(2,1)S(1)} %select_convert_fusion.refs_2_.refs_3_), custom_call_target="tpu_custom_call" | custom-call | flops 536870912 | bytes 2883584 | tf_op jit(solution)/shard_map/block_work/pallas_call | solution.py:99
  27.5 1.9 %collective-permute-done.5.refs_1_.refs_6_ = bf16[128,1152]{1,0:T(8,128)(2,1)S(1)} collective-permute-done((bf16[128,1152]{1,0:T(8,128)(2,1)S(1)}, bf16[128,1152]{1,0:T(8,128)(2,1)S(1)}, u32[]{:S(2)}, u32[]{:S(2)}) %collective-permute-start.5) | collective-permute-done | bytes 294944 | tf_op jit(solution)/shard_map/ppermute | solution.py:171
  29.3 1.2 %collective-permute-start.7 = (bf16[64,1152]{1,0:T(8,128)(2,1)S(1)}, bf16[64,1152]{1,0:T(8,128)(2,1)S(1)}, u32[]{:S(2)}, u32[]{:S(2)}) collective-permute-start(bf16[64,1152]{1,0:T(8,128)(2,1)S(1)} %slice.25), channel_id=1, source_target_pairs={{2,0},{4,2},{6,4},{7,6},{5,7},{3,5},{1,3},{0,1},{10,8},{12,10},{14... | collective-permute-start | bytes 442376 | tf_op jit(solution)/shard_map/ppermute | solution.py:171
  30.6 0.9 %collective-permute-start.6 = (bf16[64,1152]{1,0:T(8,128)(2,1)S(1)}, bf16[64,1152]{1,0:T(8,128)(2,1)S(1)}, u32[]{:S(2)}, u32[]{:S(2)}) collective-permute-start(bf16[64,1152]{1,0:T(8,128)(2,1)S(1)} %slice.24), channel_id=1, source_target_pairs={{0,2},{2,4},{4,6},{6,7},{7,5},{5,3},{3,1},{1,0},{8,10},{10,12},{12... | collective-permute-start | bytes 442376 | tf_op jit(solution)/shard_map/ppermute | solution.py:171
  31.5 1.9 %block_work.6 = (bf16[128,1024]{1,0:T(8,128)(2,1)S(1)}, bf16[128,1024]{1,0:T(8,128)(2,1)S(1)}, bf16[128,1024]{1,0:T(8,128)(2,1)S(1)}, bf16[128,1024]{1,0:T(8,128)(2,1)S(1)}) custom-call(s32[1]{0:T(128)} %bitcast.first_ref, bf16[128,1152]{1,0:T(8,128)(2,1)S(1)} %collective-permute-done.refs_0_.refs_1_, ...), custom_call_target="tpu_custom_call" | custom-call | flops 1073741824 | bytes 3670016 | tf_op jit(solution)/shard_map/block_work/pallas_call | solution.py:99
  33.4 1.9 %block_work.7 = (bf16[128,1024]{1,0:T(8,128)(2,1)S(1)}, bf16[128,1024]{1,0:T(8,128)(2,1)S(1)}, bf16[128,1024]{1,0:T(8,128)(2,1)S(1)}, bf16[128,1024]{1,0:T(8,128)(2,1)S(1)}) custom-call(s32[1]{0:T(128)} %bitcast.first_ref, bf16[128,1152]{1,0:T(8,128)(2,1)S(1)} %collective-permute-done.2.refs_0_.refs_3_, ...), custom_call_target="tpu_custom_call" | custom-call | flops 1073741824 | bytes 3670016 | tf_op jit(solution)/shard_map/block_work/pallas_call | solution.py:99
  35.8 1.7 %block_work.9 = (bf16[64,1024]{1,0:T(8,128)(2,1)S(1)}, bf16[64,1024]{1,0:T(8,128)(2,1)S(1)}, bf16[64,1024]{1,0:T(8,128)(2,1)S(1)}, bf16[64,1024]{1,0:T(8,128)(2,1)S(1)}) custom-call(s32[1]{0:T(128)} %bitcast.first_ref, bf16[64,1152]{1,0:T(8,128)(2,1)S(1)} %collective-permute-done.6.refs_0_.refs_7_, ...), custom_call_target="tpu_custom_call" | custom-call | flops 536870912 | bytes 2883584 | tf_op jit(solution)/shard_map/block_work/pallas_call | solution.py:99
  37.5 1.6 %collective-permute-start.12 = (bf16[64,1024]{1,0:T(8,128)(2,1)S(1)}, bf16[64,1024]{1,0:T(8,128)(2,1)S(1)}, u32[]{:S(2)}, u32[]{:S(2)}) collective-permute-start(bf16[64,1024]{1,0:T(8,128)(2,1)S(1)} %get-tuple-element.32), channel_id=1, source_target_pairs={{2,0},{4,2},{6,4},{7,6},{5,7},{3,5},{1,3},{0,1},{10,8},{12,10},{14... | collective-permute-start | bytes 393224 | tf_op jit(solution)/shard_map/ppermute | solution.py:171
  39.1 1.9 %block_work.8 = (bf16[128,1024]{1,0:T(8,128)(2,1)S(1)}, bf16[128,1024]{1,0:T(8,128)(2,1)S(1)}, bf16[128,1024]{1,0:T(8,128)(2,1)S(1)}, bf16[128,1024]{1,0:T(8,128)(2,1)S(1)}) custom-call(s32[1]{0:T(128)} %bitcast.first_ref, bf16[128,1152]{1,0:T(8,128)(2,1)S(1)} %collective-permute-done.4.refs_0_.refs_5_, ...), custom_call_target="tpu_custom_call" | custom-call | flops 1073741824 | bytes 3670016 | tf_op jit(solution)/shard_map/block_work/pallas_call | solution.py:99
  41.6 1.3 %weight_work.3 = (bf16[1024,256]{1,0:T(8,128)(2,1)S(1)}, bf16[1024,256]{1,0:T(8,128)(2,1)S(1)}) custom-call(s32[1]{0:T(128)} %bitcast.2.own_ref, bf16[128,1152]{1,0:T(8,128)(2,1)S(1)} %pack.1.refs_0_, bf16[128,1152]{1,0:T(8,128)(2,1)S(1)} %collective-permute-done.refs_0_.refs_1_, bf16[128,1152]{1,0:T(8,128)(2,1)S(1)} %collective-permute-done.1.refs_1_.refs_2_, ...), custom_call_target="tpu_custom_call" | custom-call | flops 1073741824 | bytes 4718592 | tf_op jit(solution)/shard_map/weight_work/pallas_call | solution.py:135
  43.5 1.6 %collective-permute-start.13 = (bf16[128,1024]{1,0:T(8,128)(2,1)S(1)}, bf16[128,1024]{1,0:T(8,128)(2,1)S(1)}, u32[]{:S(2)}, u32[]{:S(2)}) collective-permute-start(bf16[128,1024]{1,0:T(8,128)(2,1)S(1)} %pad_maximum_fusion.1), channel_id=1, source_target_pairs={{2,0},{4,2},{6,4},{7,6},{5,7},{3,5},{1,3},{0,1},{10,8},{12,10},{14... | collective-permute-start | bytes 786440 | tf_op jit(solution)/shard_map/ppermute | solution.py:171
  45.2 0.9 %collective-permute-done.8 = bf16[64,1024]{1,0:T(8,128)(2,1)S(1)} collective-permute-done((bf16[64,1024]{1,0:T(8,128)(2,1)S(1)}, bf16[64,1024]{1,0:T(8,128)(2,1)S(1)}, u32[]{:S(2)}, u32[]{:S(2)}) %collective-permute-start.8) | collective-permute-done | bytes 131104 | tf_op jit(solution)/shard_map/ppermute | solution.py:171
  46.7 1.3 %weight_work.2 = (bf16[1024,256]{1,0:T(8,128)(2,1)S(1)}, bf16[1024,256]{1,0:T(8,128)(2,1)S(1)}) custom-call(s32[1]{0:T(128)} %bitcast.2.own_ref, bf16[128,1152]{1,0:T(8,128)(2,1)S(1)} %pack.1.refs_0_, bf16[128,1152]{1,0:T(8,128)(2,1)S(1)} %collective-permute-done.refs_0_.refs_1_, bf16[128,1152]{1,0:T(8,128)(2,1)S(1)} %collective-permute-done.1.refs_1_.refs_2_, ...), custom_call_target="tpu_custom_call" | custom-call | flops 1073741824 | bytes 4718592 | tf_op jit(solution)/shard_map/weight_work/pallas_call | solution.py:135
  48.0 3.9 %collective-permute-done.13 = bf16[128,1024]{1,0:T(8,128)(2,1)S(1)} collective-permute-done((bf16[128,1024]{1,0:T(8,128)(2,1)S(1)}, bf16[128,1024]{1,0:T(8,128)(2,1)S(1)}, u32[]{:S(2)}, u32[]{:S(2)}) %collective-permute-start.13) | collective-permute-done | bytes 262176 | tf_op jit(solution)/shard_map/ppermute | solution.py:171
  52.0 1.6 %collective-permute-start.14 = (bf16[128,1024]{1,0:T(8,128)(2,1)S(1)}, bf16[128,1024]{1,0:T(8,128)(2,1)S(1)}, u32[]{:S(2)}, u32[]{:S(2)}) collective-permute-start(bf16[128,1024]{1,0:T(8,128)(2,1)S(1)} %add_convert_fusion.5), channel_id=1, source_target_pairs={{2,0},{4,2},{6,4},{7,6},{5,7},{3,5},{1,3},{0,1},{10,8},{12,10},{14... | collective-permute-start | bytes 786440 | tf_op jit(solution)/shard_map/ppermute | solution.py:171
  54.3 1.5 %collective-permute-start.18 = (bf16[1024,256]{1,0:T(8,128)(2,1)S(1)}, bf16[1024,256]{1,0:T(8,128)(2,1)S(1)}, u32[]{:S(2)}, u32[]{:S(2)}) collective-permute-start(bf16[1024,256]{1,0:T(8,128)(2,1)S(1)} %add_convert_fusion.1), channel_id=1, source_target_pairs={{0,16},{8,24},{16,0},{24,8},{1,17},{9,25},{17,1},{25,9},{2,18},{10... | collective-permute-start | bytes 1572872 | tf_op jit(solution)/shard_map/ppermute | solution.py:208
  55.9 3.6 %collective-permute-done.14 = bf16[128,1024]{1,0:T(8,128)(2,1)S(1)} collective-permute-done((bf16[128,1024]{1,0:T(8,128)(2,1)S(1)}, bf16[128,1024]{1,0:T(8,128)(2,1)S(1)}, u32[]{:S(2)}, u32[]{:S(2)}) %collective-permute-start.14) | collective-permute-done | bytes 262176 | tf_op jit(solution)/shard_map/ppermute | solution.py:171
  59.5 1.6 %collective-permute-start.15 = (bf16[128,1024]{1,0:T(8,128)(2,1)S(1)}, bf16[128,1024]{1,0:T(8,128)(2,1)S(1)}, u32[]{:S(2)}, u32[]{:S(2)}) collective-permute-start(bf16[128,1024]{1,0:T(8,128)(2,1)S(1)} %add_convert_fusion.4), channel_id=1, source_target_pairs={{2,0},{4,2},{6,4},{7,6},{5,7},{3,5},{1,3},{0,1},{10,8},{12,10},{14... | collective-permute-start | bytes 786440 | tf_op jit(solution)/shard_map/ppermute | solution.py:171
  61.7 4.4 %collective-permute-done.15 = bf16[128,1024]{1,0:T(8,128)(2,1)S(1)} collective-permute-done((bf16[128,1024]{1,0:T(8,128)(2,1)S(1)}, bf16[128,1024]{1,0:T(8,128)(2,1)S(1)}, u32[]{:S(2)}, u32[]{:S(2)}) %collective-permute-start.15) | collective-permute-done | bytes 262176 | tf_op jit(solution)/shard_map/ppermute | solution.py:171
  66.1 1.5 %collective-permute-done.11 = bf16[128,1024]{1,0:T(8,128)(2,1)S(1)} collective-permute-done((bf16[128,1024]{1,0:T(8,128)(2,1)S(1)}, bf16[128,1024]{1,0:T(8,128)(2,1)S(1)}, u32[]{:S(2)}, u32[]{:S(2)}) %collective-permute-start.11) | collective-permute-done | bytes 262176 | tf_op jit(solution)/shard_map/ppermute | solution.py:171
  67.6 0.8 %add_convert_fusion.3 = bf16[128,1024]{1,0:T(8,128)(2,1)} fusion(bf16[128,1024]{1,0:T(8,128)(2,1)S(1)} %collective-permute-done.15, bf16[128,1024]{1,0:T(8,128)(2,1)S(1)} %collective-permute-done.11, bf16[128,1024]{1,0:T(8,128)(2,1)S(1)} %get-tuple-element.24), kind=kLoop, calls=%fused_computation.3 | loop fusion | flops 786432 | bytes 1048576 | tf_op jit(solution)/shard_map/convert_element_type | solution.py:154
  68.5 1.0 %add_convert_fusion = bf16[1024,256]{1,0:T(8,128)(2,1)} fusion(bf16[1024,256]{1,0:T(8,128)(2,1)S(1)} %collective-permute-done.18, bf16[1024,256]{1,0:T(8,128)(2,1)S(1)} %collective-permute-done.16, bf16[1024,256]{1,0:T(8,128)(2,1)S(1)} %get-tuple-element.42), kind=kLoop, calls=%fused_computation | loop fusion | flops 2097152 | bytes 2097152 | tf_op jit(solution)/shard_map/convert_element_type | solution.py:154
  (40 shorter events, 5.5 us)
Async XLA Ops:
  2.2 0.9 %copy-start.2 = (bf16[128,1024]{1,0:T(8,128)(2,1)S(1)}, bf16[128,1024]{1,0:T(8,128)(2,1)}, u32[]{:S(2)}) copy-start(bf16[128,1024]{1,0:T(8,128)(2,1)} %feat_ref.1) | copy-start | bytes 786436
  3.8 10.1 %collective-permute-start.1 = (bf16[128,1152]{1,0:T(8,128)(2,1)S(1)}, bf16[128,1152]{1,0:T(8,128)(2,1)S(1)}, u32[]{:S(2)}, u32[]{:S(2)}) collective-permute-start(bf16[128,1152]{1,0:T(8,128)(2,1)S(1)} %pack.1.refs_0_), channel_id=1, source_target_pairs={{2,0},{4,2},{6,4},{7,6},{5,7},{3,5},{1,3},{0,1},{10,8},{12,10},{14... | collective-permute-start | bytes 884744 | tf_op jit(solution)/shard_map/ppermute | solution.py:171
  6.8 8.8 %collective-permute-start = (bf16[128,1152]{1,0:T(8,128)(2,1)S(1)}, bf16[128,1152]{1,0:T(8,128)(2,1)S(1)}, u32[]{:S(2)}, u32[]{:S(2)}) collective-permute-start(bf16[128,1152]{1,0:T(8,128)(2,1)S(1)} %pack.1.refs_0_), channel_id=1, source_target_pairs={{0,2},{2,4},{4,6},{6,7},{7,5},{5,3},{3,1},{1,0},{8,10},{10,12},{12... | collective-permute-start | bytes 884744 | tf_op jit(solution)/shard_map/ppermute | solution.py:171
  13.9 8.2 %collective-permute-start.3 = (bf16[128,1152]{1,0:T(8,128)(2,1)S(1)}, bf16[128,1152]{1,0:T(8,128)(2,1)S(1)}, u32[]{:S(2)}, u32[]{:S(2)}) collective-permute-start(bf16[128,1152]{1,0:T(8,128)(2,1)S(1)} %collective-permute-done.1.refs_1_.refs_2_), channel_id=1, source_target_pairs={{2,0},{4,2},{6,4},{7,6},{5,7},{3,5},{1,3},{0,1},{10,8},{12,10},{14... | collective-permute-start | bytes 884744 | tf_op jit(solution)/shard_map/ppermute | solution.py:171
  15.5 7.9 %collective-permute-start.2 = (bf16[128,1152]{1,0:T(8,128)(2,1)S(1)}, bf16[128,1152]{1,0:T(8,128)(2,1)S(1)}, u32[]{:S(2)}, u32[]{:S(2)}) collective-permute-start(bf16[128,1152]{1,0:T(8,128)(2,1)S(1)} %collective-permute-done.refs_0_.refs_1_), channel_id=1, source_target_pairs={{0,2},{2,4},{4,6},{6,7},{7,5},{5,3},{3,1},{1,0},{8,10},{10,12},{12... | collective-permute-start | bytes 884744 | tf_op jit(solution)/shard_map/ppermute | solution.py:171
  22.0 7.3 %collective-permute-start.5 = (bf16[128,1152]{1,0:T(8,128)(2,1)S(1)}, bf16[128,1152]{1,0:T(8,128)(2,1)S(1)}, u32[]{:S(2)}, u32[]{:S(2)}) collective-permute-start(bf16[128,1152]{1,0:T(8,128)(2,1)S(1)} %collective-permute-done.3.refs_1_.refs_4_), channel_id=1, source_target_pairs={{2,0},{4,2},{6,4},{7,6},{5,7},{3,5},{1,3},{0,1},{10,8},{12,10},{14... | collective-permute-start | bytes 884744 | tf_op jit(solution)/shard_map/ppermute | solution.py:171
  23.4 7.2 %collective-permute-start.4 = (bf16[128,1152]{1,0:T(8,128)(2,1)S(1)}, bf16[128,1152]{1,0:T(8,128)(2,1)S(1)}, u32[]{:S(2)}, u32[]{:S(2)}) collective-permute-start(bf16[128,1152]{1,0:T(8,128)(2,1)S(1)} %collective-permute-done.2.refs_0_.refs_3_), channel_id=1, source_target_pairs={{0,2},{2,4},{4,6},{6,7},{7,5},{5,3},{3,1},{1,0},{8,10},{10,12},{12... | collective-permute-start | bytes 884744 | tf_op jit(solution)/shard_map/ppermute | solution.py:171
  24.2 1.6 %copy-start = (bf16[1024,1024]{1,0:T(8,128)(2,1)S(1)}, bf16[1024,1024]{1,0:T(8,128)(2,1)}, u32[]{:S(2)}) copy-start(bf16[1024,1024]{1,0:T(8,128)(2,1)} %refs_2_.7) | copy-start | bytes 6291460
  25.8 5.7 %copy-start.1 = (bf16[1024,1024]{1,0:T(8,128)(2,1)S(1)}, bf16[1024,1024]{1,0:T(8,128)(2,1)}, u32[]{:S(2)}) copy-start(bf16[1024,1024]{1,0:T(8,128)(2,1)} %refs_2_.7) | copy-start | bytes 6291460
  29.3 6.1 %collective-permute-start.7 = (bf16[64,1152]{1,0:T(8,128)(2,1)S(1)}, bf16[64,1152]{1,0:T(8,128)(2,1)S(1)}, u32[]{:S(2)}, u32[]{:S(2)}) collective-permute-start(bf16[64,1152]{1,0:T(8,128)(2,1)S(1)} %slice.25), channel_id=1, source_target_pairs={{2,0},{4,2},{6,4},{7,6},{5,7},{3,5},{1,3},{0,1},{10,8},{12,10},{14... | collective-permute-start | bytes 442376 | tf_op jit(solution)/shard_map/ppermute | solution.py:171
  30.6 5.2 %collective-permute-start.6 = (bf16[64,1152]{1,0:T(8,128)(2,1)S(1)}, bf16[64,1152]{1,0:T(8,128)(2,1)S(1)}, u32[]{:S(2)}, u32[]{:S(2)}) collective-permute-start(bf16[64,1152]{1,0:T(8,128)(2,1)S(1)} %slice.24), channel_id=1, source_target_pairs={{0,2},{2,4},{4,6},{6,7},{7,5},{5,3},{3,1},{1,0},{8,10},{10,12},{12... | collective-permute-start | bytes 442376 | tf_op jit(solution)/shard_map/ppermute | solution.py:171
  37.5 6.0 %collective-permute-start.12 = (bf16[64,1024]{1,0:T(8,128)(2,1)S(1)}, bf16[64,1024]{1,0:T(8,128)(2,1)S(1)}, u32[]{:S(2)}, u32[]{:S(2)}) collective-permute-start(bf16[64,1024]{1,0:T(8,128)(2,1)S(1)} %get-tuple-element.32), channel_id=1, source_target_pairs={{2,0},{4,2},{6,4},{7,6},{5,7},{3,5},{1,3},{0,1},{10,8},{12,10},{14... | collective-permute-start | bytes 393224 | tf_op jit(solution)/shard_map/ppermute | solution.py:171
  41.1 5.0 %collective-permute-start.8 = (bf16[64,1024]{1,0:T(8,128)(2,1)S(1)}, bf16[64,1024]{1,0:T(8,128)(2,1)S(1)}, u32[]{:S(2)}, u32[]{:S(2)}) collective-permute-start(bf16[64,1024]{1,0:T(8,128)(2,1)S(1)} %get-tuple-element.28), channel_id=1, source_target_pairs={{0,2},{2,4},{4,6},{6,7},{7,5},{5,3},{3,1},{1,0},{8,10},{10,12},{12... | collective-permute-start | bytes 393224 | tf_op jit(solution)/shard_map/ppermute | solution.py:171
  42.9 25.6 %collective-permute-start.16 = (bf16[1024,256]{1,0:T(8,128)(2,1)S(1)}, bf16[1024,256]{1,0:T(8,128)(2,1)S(1)}, u32[]{:S(2)}, u32[]{:S(2)}) collective-permute-start(bf16[1024,256]{1,0:T(8,128)(2,1)S(1)} %get-tuple-element.43), channel_id=1, source_target_pairs={{0,8},{8,0},{16,24},{24,16},{1,9},{9,1},{17,25},{25,17},{2,10},{10... | collective-permute-start | bytes 1572872 | tf_op jit(solution)/shard_map/ppermute | solution.py:208
  43.0 11.2 %collective-permute-start.17 = (bf16[1024,256]{1,0:T(8,128)(2,1)S(1)}, bf16[1024,256]{1,0:T(8,128)(2,1)S(1)}, u32[]{:S(2)}, u32[]{:S(2)}) collective-permute-start(bf16[1024,256]{1,0:T(8,128)(2,1)S(1)} %get-tuple-element.45), channel_id=1, source_target_pairs={{0,8},{8,0},{16,24},{24,16},{1,9},{9,1},{17,25},{25,17},{2,10},{10... | collective-permute-start | bytes 1572872 | tf_op jit(solution)/shard_map/ppermute | solution.py:208
  43.5 8.3 %collective-permute-start.13 = (bf16[128,1024]{1,0:T(8,128)(2,1)S(1)}, bf16[128,1024]{1,0:T(8,128)(2,1)S(1)}, u32[]{:S(2)}, u32[]{:S(2)}) collective-permute-start(bf16[128,1024]{1,0:T(8,128)(2,1)S(1)} %pad_maximum_fusion.1), channel_id=1, source_target_pairs={{2,0},{4,2},{6,4},{7,6},{5,7},{3,5},{1,3},{0,1},{10,8},{12,10},{14... | collective-permute-start | bytes 786440 | tf_op jit(solution)/shard_map/ppermute | solution.py:171
  46.2 7.4 %collective-permute-start.9 = (bf16[128,1024]{1,0:T(8,128)(2,1)S(1)}, bf16[128,1024]{1,0:T(8,128)(2,1)S(1)}, u32[]{:S(2)}, u32[]{:S(2)}) collective-permute-start(bf16[128,1024]{1,0:T(8,128)(2,1)S(1)} %pad_maximum_fusion), channel_id=1, source_target_pairs={{0,2},{2,4},{4,6},{6,7},{7,5},{5,3},{3,1},{1,0},{8,10},{10,12},{12... | collective-permute-start | bytes 786440 | tf_op jit(solution)/shard_map/ppermute | solution.py:171
  52.0 7.5 %collective-permute-start.14 = (bf16[128,1024]{1,0:T(8,128)(2,1)S(1)}, bf16[128,1024]{1,0:T(8,128)(2,1)S(1)}, u32[]{:S(2)}, u32[]{:S(2)}) collective-permute-start(bf16[128,1024]{1,0:T(8,128)(2,1)S(1)} %add_convert_fusion.5), channel_id=1, source_target_pairs={{2,0},{4,2},{6,4},{7,6},{5,7},{3,5},{1,3},{0,1},{10,8},{12,10},{14... | collective-permute-start | bytes 786440 | tf_op jit(solution)/shard_map/ppermute | solution.py:171
  53.6 7.5 %collective-permute-start.10 = (bf16[128,1024]{1,0:T(8,128)(2,1)S(1)}, bf16[128,1024]{1,0:T(8,128)(2,1)S(1)}, u32[]{:S(2)}, u32[]{:S(2)}) collective-permute-start(bf16[128,1024]{1,0:T(8,128)(2,1)S(1)} %add_convert_fusion.7), channel_id=1, source_target_pairs={{0,2},{2,4},{4,6},{6,7},{7,5},{5,3},{3,1},{1,0},{8,10},{10,12},{12... | collective-permute-start | bytes 786440 | tf_op jit(solution)/shard_map/ppermute | solution.py:171
  54.3 14.2 %collective-permute-start.18 = (bf16[1024,256]{1,0:T(8,128)(2,1)S(1)}, bf16[1024,256]{1,0:T(8,128)(2,1)S(1)}, u32[]{:S(2)}, u32[]{:S(2)}) collective-permute-start(bf16[1024,256]{1,0:T(8,128)(2,1)S(1)} %add_convert_fusion.1), channel_id=1, source_target_pairs={{0,16},{8,24},{16,0},{24,8},{1,17},{9,25},{17,1},{25,9},{2,18},{10... | collective-permute-start | bytes 1572872 | tf_op jit(solution)/shard_map/ppermute | solution.py:208
  59.5 6.6 %collective-permute-start.15 = (bf16[128,1024]{1,0:T(8,128)(2,1)S(1)}, bf16[128,1024]{1,0:T(8,128)(2,1)S(1)}, u32[]{:S(2)}, u32[]{:S(2)}) collective-permute-start(bf16[128,1024]{1,0:T(8,128)(2,1)S(1)} %add_convert_fusion.4), channel_id=1, source_target_pairs={{2,0},{4,2},{6,4},{7,6},{5,7},{3,5},{1,3},{0,1},{10,8},{12,10},{14... | collective-permute-start | bytes 786440 | tf_op jit(solution)/shard_map/ppermute | solution.py:171
  61.2 6.4 %collective-permute-start.11 = (bf16[128,1024]{1,0:T(8,128)(2,1)S(1)}, bf16[128,1024]{1,0:T(8,128)(2,1)S(1)}, u32[]{:S(2)}, u32[]{:S(2)}) collective-permute-start(bf16[128,1024]{1,0:T(8,128)(2,1)S(1)} %add_convert_fusion.6), channel_id=1, source_target_pairs={{0,2},{2,4},{4,6},{6,7},{7,5},{5,3},{3,1},{1,0},{8,10},{10,12},{12... | collective-permute-start | bytes 786440 | tf_op jit(solution)/shard_map/ppermute | solution.py:171

commit v2 on v1

v2 whole, which is shorter than its diff:
```python
import functools
import math

import jax
import jax.numpy as jnp
from jax import lax
from jax.experimental import pallas as pl
from jax.experimental.pallas import tpu as pltpu
from jax.sharding import PartitionSpec as P

BLOCK = 128
LANES = 128
FIELD_ROWS = 8
CHUNK = 256
VMEM_LIMIT = 24 * 1024 * 1024
WHOLE_VMEM = 60 * 1024 * 1024


def pack_kernel(feat_ref, short_ref, pos_ref, a_ref, b_ref, sem_a, sem_b):
    half, width = b_ref.shape
    copy_a = pltpu.make_async_copy(feat_ref.at[pl.ds(0, half)], a_ref.at[pl.ds(0, half)], sem_a)
    copy_b = pltpu.make_async_copy(feat_ref.at[pl.ds(half, half)], b_ref, sem_b)
    copy_a.start()
    copy_b.start()
    top_count, rows = short_ref.shape
    short = short_ref[...]
    places = pos_ref[...] // BLOCK
    offsets = pos_ref[...] % BLOCK
    targets = jnp.zeros_like(places)
    for j in range(top_count):
        targets = targets + jnp.where(places == j, short[j : j + 1, :], 0)
    fields = jnp.concatenate([short, targets, offsets], axis=0)
    groups = [
        fields[at : at + FIELD_ROWS] for at in range(0, fields.shape[0], FIELD_ROWS)
    ]
    groups.append(jnp.zeros((FIELD_ROWS, width - rows * len(groups)), jnp.int32))
    meta = jnp.concatenate(groups, axis=1)
    a_ref[half:, :] = meta.astype(jnp.float32).astype(jnp.bfloat16)
    copy_a.wait()
    copy_b.wait()


def pack(features, shortlist, positives):
    rows, width = features.shape
    half = rows // 2
    return pl.pallas_call(
        pack_kernel,
        out_shape=[
            jax.ShapeDtypeStruct((half + FIELD_ROWS, width), jnp.bfloat16),
            jax.ShapeDtypeStruct((half, width), jnp.bfloat16),
        ],
        in_specs=[
            pl.BlockSpec(memory_space=pltpu.HBM),
            pl.BlockSpec(memory_space=pltpu.VMEM),
            pl.BlockSpec(memory_space=pltpu.VMEM),
        ],
        out_specs=[pl.BlockSpec(memory_space=pltpu.VMEM)] * 2,
        scratch_shapes=[pltpu.SemaphoreType.DMA, pltpu.SemaphoreType.DMA],
        compiler_params=pltpu.CompilerParams(vmem_limit_bytes=WHOLE_VMEM),
        name="pack",
    )(features, shortlist.T, positives.T)


def block_kernel(block_count, top_count, pos_count, first_ref, size_ref, *refs):
    x_refs = refs[: 2 * block_count]
    w_ref = refs[2 * block_count]
    grad_refs = refs[2 * block_count + 1 : 4 * block_count + 1]
    slope_refs = refs[4 * block_count + 1 :]
    labels, width = w_ref.shape
    local_count = labels // BLOCK
    half = grad_refs[0].shape[0]
    rows = 2 * half
    first = first_ref[0].astype(jnp.float32)

    lane = lax.broadcasted_iota(jnp.int32, (LANES, BLOCK), 1)
    row = lax.broadcasted_iota(jnp.int32, (LANES, BLOCK), 0)
    live_table = jnp.concatenate(
        [
            jnp.where((row == c) & (lane < size_ref[c]), 2.0, 0.0).astype(jnp.bfloat16)
            for c in range(local_count)
        ],
        axis=1,
    )

    named, pieces = [], []
    cluster = lax.broadcasted_iota(jnp.int32, (FIELD_ROWS, rows), 0).astype(jnp.float32) + first
    for b in range(block_count):
        a_ref, b_ref = x_refs[2 * b], x_refs[2 * b + 1]
        pieces += [a_ref[:half, :], b_ref[...]]
        groups = -(-(top_count + 2 * pos_count) // FIELD_ROWS)
        meta = a_ref[half:, : groups * rows].astype(jnp.float32)
        field = [
            meta[f % FIELD_ROWS : f % FIELD_ROWS + 1, f // FIELD_ROWS * rows : (f // FIELD_ROWS + 1) * rows]
            for f in range(top_count + 2 * pos_count)
        ]
        member = jnp.zeros((FIELD_ROWS, rows), jnp.float32)
        for j in range(top_count):
            member = jnp.where(cluster == field[j], 1.0, member)
        target = [
            (field[top_count + q] - first) * BLOCK + field[top_count + pos_count + q]
            for q in range(pos_count)
        ]
        rest = jnp.zeros((LANES - FIELD_ROWS - pos_count, rows), jnp.float32)
        named.append(jnp.concatenate([member] + target + [rest], axis=0).T)

    x = jnp.concatenate(pieces, axis=0)
    named = jnp.concatenate(named, axis=0) if block_count > 1 else named[0]
    target = [named[:, FIELD_ROWS + q : FIELD_ROWS + q + 1] for q in range(pos_count)]
    member = jnp.where(
        lax.broadcasted_iota(jnp.int32, named.shape, 1) < FIELD_ROWS, named, 0.0
    ).astype(jnp.bfloat16)
    for start in range(0, labels, CHUNK):
        logits = lax.dot_general(
            x,
            w_ref[start : start + CHUNK, :],
            (((1,), (1,)), ((), ())),
            preferred_element_type=jnp.float32,
        )
        live = jnp.dot(
            member, live_table[:, start : start + CHUNK], preferred_element_type=jnp.float32
        )
        label = (
            lax.broadcasted_iota(jnp.int32, (1, CHUNK), 1) + start
        ).astype(jnp.float32)
        positive = target[0] == label
        for q in range(1, pos_count):
            positive = positive | (target[q] == label)
        turned = jnp.where(positive, -1.0, 1.0)
        slope = (turned * live * jnp.maximum(1.0 + turned * logits, 0.0)).astype(jnp.bfloat16)
        for b, ref in enumerate(slope_refs):
            ref[:, start : start + CHUNK] = slope[b * rows : (b + 1) * rows]
    slope = jnp.concatenate([ref[...] for ref in slope_refs], axis=0)
    for start in range(0, width, CHUNK):
        part = jnp.dot(
            slope, w_ref[:, start : start + CHUNK], preferred_element_type=jnp.float32
        ).astype(jnp.bfloat16)
        for p, ref in enumerate(grad_refs):
            ref[:, start : start + CHUNK] = part[p * half : (p + 1) * half]


def block_work(blocks, weights, first, sizes, top_count, pos_count):
    labels, width = weights.shape
    count = len(blocks)
    half = blocks[0][1].shape[0]
    out = pl.pallas_call(
        functools.partial(block_kernel, count, top_count, pos_count),
        out_shape=[jax.ShapeDtypeStruct((half, width), jnp.bfloat16)] * (2 * count)
        + [jax.ShapeDtypeStruct((2 * half, labels), jnp.bfloat16)] * count,
        in_specs=[pl.BlockSpec(memory_space=pltpu.SMEM)] * 2
        + [pl.BlockSpec(memory_space=pltpu.VMEM)] * (2 * count + 1),
        compiler_params=pltpu.CompilerParams(vmem_limit_bytes=VMEM_LIMIT),
        cost_estimate=pl.CostEstimate(
            flops=8 * count * half * labels * width,
            bytes_accessed=2 * labels * width + 12 * count * half * width,
            transcendentals=0,
        ),
        name="block_work",
    )(first, sizes, *[piece for block in blocks for piece in block], weights)
    grads = [(out[2 * b], out[2 * b + 1]) for b in range(count)]
    return grads, list(out[2 * count :])


def weight_kernel(block_count, column_blocks, scale, own_ref, *refs):
    x_refs = refs[: 2 * block_count]
    s_refs = refs[2 * block_count : 3 * block_count]
    out_refs = refs[3 * block_count :]
    part_width = out_refs[0].shape[1]
    half = x_refs[1].shape[0]
    slopes = jnp.concatenate([ref[...] for ref in s_refs], axis=0)
    for ref, q in zip(out_refs, column_blocks):
        at = pl.multiple_of((own_ref[0] ^ q) * part_width, part_width)
        x = jnp.concatenate([r[:half, pl.ds(at, part_width)] for r in x_refs], axis=0)
        part = lax.dot_general(
            slopes, x, (((0,), (0,)), ((), ())), preferred_element_type=jnp.float32
        )
        ref[...] = (part * scale).astype(jnp.bfloat16)


def weight_work(blocks, slopes, own, column_blocks, part_width, scale):
    count = len(blocks)
    rows, labels = slopes[0].shape
    rows *= count
    return pl.pallas_call(
        functools.partial(weight_kernel, count, column_blocks, scale),
        out_shape=[jax.ShapeDtypeStruct((labels, part_width), jnp.bfloat16)] * len(column_blocks),
        in_specs=[pl.BlockSpec(memory_space=pltpu.SMEM)]
        + [pl.BlockSpec(memory_space=pltpu.VMEM)] * (3 * count),
        compiler_params=pltpu.CompilerParams(vmem_limit_bytes=VMEM_LIMIT),
        cost_estimate=pl.CostEstimate(
            flops=2 * rows * labels * part_width * len(column_blocks),
            bytes_accessed=2 * rows * (labels + 1024) + 2 * labels * part_width,
            transcendentals=0,
        ),
        name="weight_work",
    )(own, *[piece for block in blocks for piece in block], *slopes)


def add(*parts):
    total = parts[0].astype(jnp.float32)
    for part in parts[1:]:
        total = total + part.astype(jnp.float32)
    return total.astype(jnp.bfloat16)


def behind(array, other):
    return lax.optimization_barrier((array, other))[0]


def local(features, shortlist, positives, cluster_sizes, weights):
    inst_rows, width = features.shape
    top_count, pos_count = shortlist.shape[1], positives.shape[1]
    clus_count, seq_count = lax.axis_size("clus"), lax.axis_size("seq")
    local_count = cluster_sizes.shape[0]
    part_width = width // seq_count
    steps = clus_count // 2

    ring = list(range(0, clus_count, 2)) + list(range(1, clus_count, 2))[::-1]
    up = [(ring[k], ring[(k + 1) % clus_count]) for k in range(clus_count)]
    down = [(b, a) for a, b in up]

    def send_up(array):
        return lax.ppermute(array, "clus", up)

    def send_down(array):
        return lax.ppermute(array, "clus", down)

    first = (lax.axis_index("clus") * local_count).astype(jnp.int32).reshape(1)

    def work(blocks):
        return block_work(blocks, weights, first, cluster_sizes, top_count, pos_count)

    own = tuple(pack(features, shortlist, positives))
    below, above = {0: own}, {0: own}
    below_grad, above_grad = {}, {}
    used, slopes = [], []

    def take(blocks):
        grads, found = work(blocks)
        used.extend(blocks)
        slopes.extend(found)
        return grads

    for k in range(1, steps + 1):
        here_below, here_above = below[k - 1], above[k - 1]
        if k > 2:
            here_below = [behind(piece, below_grad[k - 2][0]) for piece in here_below]
            here_above = [behind(piece, below_grad[k - 2][0]) for piece in here_above]
        a_up = send_up(here_below[0])
        b_down = send_down(here_above[1])
        if k < steps:
            b_up = send_up(here_below[1])
            a_down = send_down(here_above[0])
            below[k], above[k] = (a_up, b_up), (a_down, b_down)
        else:
            opposite = (a_up, b_down)
        if k > 1:
            below_grad[k - 1], above_grad[k - 1] = take([below[k - 1], above[k - 1]])

    last = steps - 1
    b_going_down, a_going_up = below_grad[last][1], above_grad[last][0]
    b_from_above, a_from_below = send_down(b_going_down), send_up(a_going_up)
    (far_grad, own_grad) = take([opposite, own])
    a_from_above, b_from_below = send_down(far_grad[0]), send_up(far_grad[1])
    for k in range(last, 0, -1):
        a_down, b_up = add(below_grad[k][0], a_from_above), add(above_grad[k][1], b_from_below)
        if k > 1:
            b_down = add(below_grad[k - 1][1], behind(b_from_above, far_grad[0]))
            a_up = add(above_grad[k - 1][0], behind(a_from_below, far_grad[0]))
            b_from_above, a_from_below = send_down(b_down), send_up(a_up)
        a_from_above, b_from_below = send_down(a_down), send_up(b_up)

    scale = 1.0 / math.sqrt(inst_rows * seq_count * top_count // local_count)
    own_seq = lax.axis_index("seq").astype(jnp.int32).reshape(1)

    def seq_send(array, bit):
        return lax.ppermute(array, "seq", [(k, k ^ bit) for k in range(seq_count)])

    away = [q for q in range(seq_count) if q & 1]
    kept = [q for q in range(seq_count) if not q & 1]
    slots = dict(zip(away, weight_work(used, slopes, own_seq, away, part_width, scale)))
    slots.update(zip(kept, weight_work(used, slopes, own_seq, kept, part_width, scale)))
    bit = 1
    while bit < seq_count:
        for q in [q for q in sorted(slots, reverse=True) if q & bit]:
            slots[q ^ bit] = add(slots[q ^ bit], seq_send(slots.pop(q), bit))
        bit *= 2
    weight_grad = slots[0]

    feature_grad = jnp.concatenate(
        [
            add(behind(own_grad[0], weight_grad), a_from_above, a_from_below),
            add(behind(own_grad[1], weight_grad), b_from_above, b_from_below),
        ],
        axis=0,
    )
    return (feature_grad, weight_grad)


def solution(mesh):
    return jax.shard_map(
        local,
        mesh=mesh,
        in_specs=(
            P(("seq", "clus"), None),
            P(("seq", "clus"), None),
            P(("seq", "clus"), None),
            P("clus"),
            P("clus", None),
        ),
        out_specs=(P(("seq", "clus"), None), P("clus", "seq")),
        check_vma=False,
    )
```

time: 69.8 us -> 86.1 us (1.23)
  starting transfers between devices: 20 us -> 32.3 us
  waiting for transfers between devices: 29 us -> 20.2 us
  local copies, waits for them, and re-layouts: 4.17 us -> 11.1 us
  Pallas kernels: 12.3 us -> 17 us
  other arithmetic: 3.21 us -> 4.16 us
    ppermute x16 -> x28, starting transfers between devices: 17.9 us -> 30.3 us  [the longest x14 25 us: send_up(): return lax.ppermute(array, 'clus', up)]
    ppermute x16 -> x28, waiting for transfers between devices: 29 us -> 16.9 us  [the longest x14 9.86 us: send_down(): return lax.ppermute(array, 'clus', down)]
    unnamed x8 -> x56, local copies, waits for them, and re-layouts: 4.12 us -> 11.1 us
    ppermute x3, waiting for transfers between devices: 0.01 us -> 3.33 us  [seq_send(): return lax.ppermute(array, 'seq', [(k, k ^ bit) for k in range(seq_count)])]
    pallas_call x6 -> x5, Pallas kernels: 9.76 us -> 12.4 us  [the longest x4 10.1 us: block_work(): pl.pallas_call(functools.partial(block_kernel, count, top_count, pos_coun...]
    pallas_call x2, Pallas kernels: 2.59 us -> 4.58 us  [weight_work(): pl.pallas_call(functools.partial(weight_kernel, count, column_blocks, sca...]
    convert_element_type x9 -> x14, other arithmetic: 2.34 us -> 3.44 us  [add(): return total.astype(jnp.bfloat16)]
  transfers between devices with their start and end apart: 19 -> 31, of which waited for: 9 -> 8; matrix products, arithmetic and copies ran while one was open for 3% -> 4% of each run, Pallas kernels for 15% -> 17%
where the time goes in v2:
time: 86.1 us; the launch traced here: 85.8 us
  starting transfers between devices  32.3 us (38%)
  waiting for transfers between devices  20.2 us (23%)
  Pallas kernels  17 us (20%)
  local copies, waits for them, and re-layouts  11.1 us (13%)
  other arithmetic  4.16 us (5%)
  between operations  0.95 us (1%)
    ppermute x14, starting transfers between devices, send_up(): return lax.ppermute(array, 'clus', up)  25 us
    unnamed x56, local copies, waits for them, and re-layouts  11.1 us
    pallas_call x4, Pallas kernels, block_work(): pl.pallas_call(functools.partial(block_kernel, count, top_count, pos_coun...  10.1 us
    ppermute x14, waiting for transfers between devices, send_down(): return lax.ppermute(array, 'clus', down)  9.86 us
    ppermute x14, waiting for transfers between devices, send_up(): return lax.ppermute(array, 'clus', up)  7.05 us
    ppermute x14, starting transfers between devices, send_down(): return lax.ppermute(array, 'clus', down)  5.29 us
    pallas_call x2, Pallas kernels, weight_work(): pl.pallas_call(functools.partial(weight_kernel, count, column_blocks, sca...  4.58 us
    convert_element_type x14, other arithmetic, add(): return total.astype(jnp.bfloat16)  3.44 us
  transfers between devices with their start and end apart: 31, of which 8 were waited for; matrix products, arithmetic and copies ran while one was open for 4% of the time, Pallas kernels for 17%

profile of v2, /device:TPU:0, one launch (start us, length us, event | category | flops | bytes accessed | tf_op | source)
XLA Modules:
  0.0 85.8 jit_solution(6476461474346910719)
XLA Ops:
  0.6 2.4 %pack.1 = (bf16[72,1024]{1,0:T(8,128)(2,1)}, bf16[64,1024]{1,0:T(8,128)(2,1)}) custom-call(bf16[128,1024]{1,0:T(8,128)(2,1)} %feat_ref.1, s32[16,128]{1,0:T(8,128)} %bitcast.4, s32[4,128]{1,0:T(4,128)} %bitcast.5), custom_call_target="tpu_custom_call" | custom-call | tf_op jit(solution)/shard_map/pack/pallas_call | solution.py:46
  3.0 3.1 %collective-permute-start = (bf16[72,1024]{1,0:T(8,128)(2,1)}, bf16[72,1024]{1,0:T(8,128)(2,1)S(1)}, u32[]{:S(2)}, u32[]{:S(2)}) collective-permute-start(bf16[72,1024]{1,0:T(8,128)(2,1)} %get-tuple-element.44.refs_2_.refs_14_), channel_id=1, source_target_pairs={{0,2},{2,4},{4,6},{6,7},{7,5},{5,3},{3,1},{1,0},{8,10},{10,12},{12... | collective-permute-start | bytes 442376 | tf_op jit(solution)/shard_map/ppermute | solution.py:222
  6.1 2.0 %collective-permute-start.4 = (bf16[64,1024]{1,0:T(8,128)(2,1)}, bf16[64,1024]{1,0:T(8,128)(2,1)S(1)}, u32[]{:S(2)}, u32[]{:S(2)}) collective-permute-start(bf16[64,1024]{1,0:T(8,128)(2,1)} %get-tuple-element.45.refs_3_.refs_15_), channel_id=1, source_target_pairs={{2,0},{4,2},{6,4},{7,6},{5,7},{3,5},{1,3},{0,1},{10,8},{12,10},{14... | collective-permute-start | bytes 393224 | tf_op jit(solution)/shard_map/ppermute | solution.py:225
  8.2 2.5 %collective-permute-done.refs_0_ = bf16[72,1024]{1,0:T(8,128)(2,1)S(1)} collective-permute-done((bf16[72,1024]{1,0:T(8,128)(2,1)}, bf16[72,1024]{1,0:T(8,128)(2,1)S(1)}, u32[]{:S(2)}, u32[]{:S(2)}) %collective-permute-start) | collective-permute-done | bytes 147488 | tf_op jit(solution)/shard_map/ppermute | solution.py:222
  10.7 2.4 %collective-permute-start.1 = (bf16[72,1024]{1,0:T(8,128)(2,1)S(1)}, bf16[72,1024]{1,0:T(8,128)(2,1)S(1)}, u32[]{:S(2)}, u32[]{:S(2)}) collective-permute-start(bf16[72,1024]{1,0:T(8,128)(2,1)S(1)} %collective-permute-done.refs_0_), channel_id=1, source_target_pairs={{0,2},{2,4},{4,6},{6,7},{7,5},{5,3},{3,1},{1,0},{8,10},{10,12},{12... | collective-permute-start | bytes 442376 | tf_op jit(solution)/shard_map/ppermute | solution.py:222
  13.1 2.5 %collective-permute-done.4.refs_3_ = bf16[64,1024]{1,0:T(8,128)(2,1)S(1)} collective-permute-done((bf16[64,1024]{1,0:T(8,128)(2,1)}, bf16[64,1024]{1,0:T(8,128)(2,1)S(1)}, u32[]{:S(2)}, u32[]{:S(2)}) %collective-permute-start.4) | collective-permute-done | bytes 131104 | tf_op jit(solution)/shard_map/ppermute | solution.py:225
  15.7 1.9 %collective-permute-start.6 = (bf16[64,1024]{1,0:T(8,128)(2,1)S(1)}, bf16[64,1024]{1,0:T(8,128)(2,1)S(1)}, u32[]{:S(2)}, u32[]{:S(2)}) collective-permute-start(bf16[64,1024]{1,0:T(8,128)(2,1)S(1)} %collective-permute-done.2.refs_1_), channel_id=1, source_target_pairs={{0,2},{2,4},{4,6},{6,7},{7,5},{5,3},{3,1},{1,0},{8,10},{10,12},{12... | collective-permute-start | bytes 393224 | tf_op jit(solution)/shard_map/ppermute | solution.py:222
  17.6 1.6 %copy-done.24 = bf16[1024,1024]{1,0:T(8,128)(2,1)S(1)} copy-done((bf16[1024,1024]{1,0:T(8,128)(2,1)S(1)}, bf16[1024,1024]{1,0:T(8,128)(2,1)}, u32[]{:S(2)}) %copy-start.24) | copy-done | bytes 2097176
  19.9 2.2 %block_work.4 = (bf16[64,1024]{1,0:T(8,128)(2,1)S(1)}, bf16[64,1024]{1,0:T(8,128)(2,1)S(1)}, bf16[64,1024]{1,0:T(8,128)(2,1)S(1)}, bf16[64,1024]{1,0:T(8,128)(2,...) custom-call(s32[1]{0:T(128)} %bitcast.first_ref, s32[8]{0:T(128)S(1)} %copy-done.26, ...), custom_call_target="tpu_custom_call" | custom-call | flops 1073741824 | bytes 3670016 | tf_op jit(solution)/shard_map/block_work/pallas_call | solution.py:145
  24.8 1.6 %collective-permute-start.5 = (bf16[72,1024]{1,0:T(8,128)(2,1)S(1)}, bf16[72,1024]{1,0:T(8,128)(2,1)S(1)}, u32[]{:S(2)}, u32[]{:S(2)}) collective-permute-start(bf16[72,1024]{1,0:T(8,128)(2,1)S(1)} %collective-permute-done.1.refs_0_.refs_4_), channel_id=1, source_target_pairs={{0,2},{2,4},{4,6},{6,7},{7,5},{5,3},{3,1},{1,0},{8,10},{10,12},{12... | collective-permute-start | bytes 442376 | tf_op jit(solution)/shard_map/ppermute | solution.py:222
  26.9 1.9 %collective-permute-start.12 = (bf16[64,1024]{1,0:T(8,128)(2,1)S(1)}, bf16[64,1024]{1,0:T(8,128)(2,1)S(1)}, u32[]{:S(2)}, u32[]{:S(2)}) collective-permute-start(bf16[64,1024]{1,0:T(8,128)(2,1)S(1)} %collective-permute-done.6.refs_1_.refs_5_), channel_id=1, source_target_pairs={{0,2},{2,4},{4,6},{6,7},{7,5},{5,3},{3,1},{1,0},{8,10},{10,12},{12... | collective-permute-start | bytes 393224 | tf_op jit(solution)/shard_map/ppermute | solution.py:222
  28.8 2.2 %block_work.5 = (bf16[64,1024]{1,0:T(8,128)(2,1)S(1)}, bf16[64,1024]{1,0:T(8,128)(2,1)S(1)}, bf16[64,1024]{1,0:T(8,128)(2,1)S(1)}, bf16[64,1024]{1,0:T(8,128)(2,...) custom-call(s32[1]{0:T(128)} %bitcast.first_ref, s32[8]{0:T(128)S(1)} %copy-done.26, ...), custom_call_target="tpu_custom_call" | custom-call | flops 1073741824 | bytes 3670016 | tf_op jit(solution)/shard_map/block_work/pallas_call | solution.py:145
  33.7 1.6 %collective-permute-start.9 = (bf16[72,1024]{1,0:T(8,128)(2,1)S(1)}, bf16[72,1024]{1,0:T(8,128)(2,1)S(1)}, u32[]{:S(2)}, u32[]{:S(2)}) collective-permute-start(bf16[72,1024]{1,0:T(8,128)(2,1)S(1)} %collective-permute-done.5.refs_0_.refs_8_), channel_id=1, source_target_pairs={{0,2},{2,4},{4,6},{6,7},{7,5},{5,3},{3,1},{1,0},{8,10},{10,12},{12... | collective-permute-start | bytes 442376 | tf_op jit(solution)/shard_map/ppermute | solution.py:222
  35.8 2.9 %block_work.7 = (bf16[64,1024]{1,0:T(8,128)(2,1)S(1)}, bf16[64,1024]{1,0:T(8,128)(2,1)}, bf16[64,1024]{1,0:T(8,128)(2,1)}, bf16[64,1024]{1,0:T(8,128)(2,1)S(1)},...) custom-call(s32[1]{0:T(128)} %bitcast.first_ref, s32[8]{0:T(128)S(1)} %copy-done.26, ...), custom_call_target="tpu_custom_call" | custom-call | flops 1073741824 | bytes 3670016 | tf_op jit(solution)/shard_map/block_work/pallas_call | solution.py:145
  40.8 1.9 %collective-permute-start.21 = (bf16[64,1024]{1,0:T(8,128)(2,1)}, bf16[64,1024]{1,0:T(8,128)(2,1)}, u32[]{:S(2)}, u32[]{:S(2)}) collective-permute-start(bf16[64,1024]{1,0:T(8,128)(2,1)} %get-tuple-element.72), channel_id=1, source_target_pairs={{0,2},{2,4},{4,6},{6,7},{7,5},{5,3},{3,1},{1,0},{8,10},{10,12},{12... | collective-permute-start | bytes 393224 | tf_op jit(solution)/shard_map/ppermute | solution.py:222
  42.8 1.7 %copy-done.25 = bf16[1024,1024]{1,0:T(8,128)(2,1)S(1)} copy-done((bf16[1024,1024]{1,0:T(8,128)(2,1)S(1)}, bf16[1024,1024]{1,0:T(8,128)(2,1)}, u32[]{:S(2)}) %copy-start.25) | copy-done | bytes 2097176
  44.4 2.6 %block_work.6 = (bf16[64,1024]{1,0:T(8,128)(2,1)S(1)}, bf16[64,1024]{1,0:T(8,128)(2,1)S(1)}, bf16[64,1024]{1,0:T(8,128)(2,1)S(1)}, bf16[64,1024]{1,0:T(8,128)(2,...) custom-call(s32[1]{0:T(128)} %bitcast.first_ref, s32[8]{0:T(128)S(1)} %copy-done.27, ...), custom_call_target="tpu_custom_call" | custom-call | flops 1073741824 | bytes 3670016 | tf_op jit(solution)/shard_map/block_work/pallas_call | solution.py:145
  47.3 0.9 %add_convert_fusion.11 = bf16[64,1024]{1,0:T(8,128)(2,1)S(1)} fusion(bf16[64,1024]{1,0:T(8,128)(2,1)} %collective-permute-done.21, bf16[64,1024]{1,0:T(8,128)(2,1)S(1)} %copy-done.23), kind=kLoop, calls=%fused_computation.12 | loop fusion | flops 262144 | bytes 393216 | tf_op jit(solution)/shard_map/convert_element_type | solution.py:202
  48.2 1.9 %collective-permute-start.22 = (bf16[64,1024]{1,0:T(8,128)(2,1)S(1)}, bf16[64,1024]{1,0:T(8,128)(2,1)S(1)}, u32[]{:S(2)}, u32[]{:S(2)}) collective-permute-start(bf16[64,1024]{1,0:T(8,128)(2,1)S(1)} %add_convert_fusion.11), channel_id=1, source_target_pairs={{0,2},{2,4},{4,6},{6,7},{7,5},{5,3},{3,1},{1,0},{8,10},{10,12},{12... | collective-permute-start | bytes 393224 | tf_op jit(solution)/shard_map/ppermute | solution.py:222
  51.3 1.9 %collective-permute-start.27 = (bf16[64,1024]{1,0:T(8,128)(2,1)S(1)}, bf16[64,1024]{1,0:T(8,128)(2,1)S(1)}, u32[]{:S(2)}, u32[]{:S(2)}) collective-permute-start(bf16[64,1024]{1,0:T(8,128)(2,1)S(1)} %get-tuple-element.85), channel_id=1, source_target_pairs={{0,2},{2,4},{4,6},{6,7},{7,5},{5,3},{3,1},{1,0},{8,10},{10,12},{12... | collective-permute-start | bytes 393224 | tf_op jit(solution)/shard_map/ppermute | solution.py:222
  53.2 2.2 %weight_work.3 = (bf16[1024,256]{1,0:T(8,128)(2,1)S(1)}, bf16[1024,256]{1,0:T(8,128)(2,1)S(1)}) custom-call(s32[1]{0:T(128)} %bitcast.3.own_ref, bf16[72,1024]{1,0:T(8,128)(2,1)S(1)} %collective-permute-done.refs_0_, bf16[64,1024]{1,0:T(8,128)(2,1)S(1)} %collective-permute-done.2.refs_1_, bf16[72,1024]{1,0:T(8,128)(2,1)S(1)} %collective-permute-done.3.refs_2_, ...), custom_call_target="tpu_custom_call" | custom-call | flops 1073741824 | bytes 4718592 | tf_op jit(solution)/shard_map/weight_work/pallas_call | solution.py:183
  55.5 2.4 %weight_work.2 = (bf16[1024,256]{1,0:T(8,128)(2,1)S(1)}, bf16[1024,256]{1,0:T(8,128)(2,1)S(1)}) custom-call(s32[1]{0:T(128)} %bitcast.3.own_ref, bf16[72,1024]{1,0:T(8,128)(2,1)S(1)} %collective-permute-done.refs_0_, bf16[64,1024]{1,0:T(8,128)(2,1)S(1)} %collective-permute-done.2.refs_1_, bf16[72,1024]{1,0:T(8,128)(2,1)S(1)} %collective-permute-done.3.refs_2_, ...), custom_call_target="tpu_custom_call" | custom-call | flops 1073741824 | bytes 4718592 | tf_op jit(solution)/shard_map/weight_work/pallas_call | solution.py:183
  58.4 1.6 %collective-permute-start.23 = (bf16[64,1024]{1,0:T(8,128)(2,1)S(1)}, bf16[64,1024]{1,0:T(8,128)(2,1)S(1)}, u32[]{:S(2)}, u32[]{:S(2)}) collective-permute-start(bf16[64,1024]{1,0:T(8,128)(2,1)S(1)} %add_convert_fusion.10), channel_id=1, source_target_pairs={{0,2},{2,4},{4,6},{6,7},{7,5},{5,3},{3,1},{1,0},{8,10},{10,12},{12... | collective-permute-start | bytes 393224 | tf_op jit(solution)/shard_map/ppermute | solution.py:222
  60.6 1.6 %collective-permute-start.28 = (bf16[64,1024]{1,0:T(8,128)(2,1)S(1)}, bf16[64,1024]{1,0:T(8,128)(2,1)S(1)}, u32[]{:S(2)}, u32[]{:S(2)}) collective-permute-start(bf16[64,1024]{1,0:T(8,128)(2,1)S(1)} %add_convert_fusion.6), channel_id=1, source_target_pairs={{0,2},{2,4},{4,6},{6,7},{7,5},{5,3},{3,1},{1,0},{8,10},{10,12},{12... | collective-permute-start | bytes 393224 | tf_op jit(solution)/shard_map/ppermute | solution.py:222
  62.3 4.5 %collective-permute-done.28 = bf16[64,1024]{1,0:T(8,128)(2,1)S(1)} collective-permute-done((bf16[64,1024]{1,0:T(8,128)(2,1)S(1)}, bf16[64,1024]{1,0:T(8,128)(2,1)S(1)}, u32[]{:S(2)}, u32[]{:S(2)}) %collective-permute-start.28) | collective-permute-done | bytes 131104 | tf_op jit(solution)/shard_map/ppermute | solution.py:222
  67.1 1.8 %collective-permute-start.29 = (bf16[64,1024]{1,0:T(8,128)(2,1)S(1)}, bf16[64,1024]{1,0:T(8,128)(2,1)S(1)}, u32[]{:S(2)}, u32[]{:S(2)}) collective-permute-start(bf16[64,1024]{1,0:T(8,128)(2,1)S(1)} %add_convert_fusion.5), channel_id=1, source_target_pairs={{0,2},{2,4},{4,6},{6,7},{7,5},{5,3},{3,1},{1,0},{8,10},{10,12},{12... | collective-permute-start | bytes 393224 | tf_op jit(solution)/shard_map/ppermute | solution.py:222
  69.1 2.7 %collective-permute-done.18 = bf16[64,1024]{1,0:T(8,128)(2,1)S(1)} collective-permute-done((bf16[64,1024]{1,0:T(8,128)(2,1)S(1)}, bf16[64,1024]{1,0:T(8,128)(2,1)S(1)}, u32[]{:S(2)}, u32[]{:S(2)}) %collective-permute-start.18) | collective-permute-done | bytes 131104 | tf_op jit(solution)/shard_map/ppermute | solution.py:225
  71.8 1.5 %collective-permute-start.16 = (bf16[1024,256]{1,0:T(8,128)(2,1)S(1)}, bf16[1024,256]{1,0:T(8,128)(2,1)S(1)}, u32[]{:S(2)}, u32[]{:S(2)}) collective-permute-start(bf16[1024,256]{1,0:T(8,128)(2,1)S(1)} %add_convert_fusion.1), channel_id=1, source_target_pairs={{0,16},{8,24},{16,0},{24,8},{1,17},{9,25},{17,1},{25,9},{2,18},{10... | collective-permute-start | bytes 1572872 | tf_op jit(solution)/shard_map/ppermute | solution.py:276
  73.9 4.4 %collective-permute-done.19 = bf16[64,1024]{1,0:T(8,128)(2,1)S(1)} collective-permute-done((bf16[64,1024]{1,0:T(8,128)(2,1)S(1)}, bf16[64,1024]{1,0:T(8,128)(2,1)S(1)}, u32[]{:S(2)}, u32[]{:S(2)}) %collective-permute-start.19) | collective-permute-done | bytes 131104 | tf_op jit(solution)/shard_map/ppermute | solution.py:225
  78.4 1.6 %collective-permute-start.30 = (bf16[64,1024]{1,0:T(8,128)(2,1)S(1)}, bf16[64,1024]{1,0:T(8,128)(2,1)S(1)}, u32[]{:S(2)}, u32[]{:S(2)}) collective-permute-start(bf16[64,1024]{1,0:T(8,128)(2,1)S(1)} %add_convert_fusion.4), channel_id=1, source_target_pairs={{0,2},{2,4},{4,6},{6,7},{7,5},{5,3},{3,1},{1,0},{8,10},{10,12},{12... | collective-permute-start | bytes 393224 | tf_op jit(solution)/shard_map/ppermute | solution.py:222
  80.5 3.3 %collective-permute-done.16 = bf16[1024,256]{1,0:T(8,128)(2,1)S(1)} collective-permute-done((bf16[1024,256]{1,0:T(8,128)(2,1)S(1)}, bf16[1024,256]{1,0:T(8,128)(2,1)S(1)}, u32[]{:S(2)}, u32[]{:S(2)}) %collective-permute-start.16) | collective-permute-done | bytes 524320 | tf_op jit(solution)/shard_map/ppermute | solution.py:276
  83.8 1.0 %add_convert_fusion = bf16[1024,256]{1,0:T(8,128)(2,1)} fusion(bf16[1024,256]{1,0:T(8,128)(2,1)S(1)} %collective-permute-done.16, bf16[1024,256]{1,0:T(8,128)(2,1)S(1)} %collective-permute-done.14, bf16[1024,256]{1,0:T(8,128)(2,1)S(1)} %get-tuple-element.63), kind=kLoop, calls=%fused_computation | loop fusion | flops 2097152 | bytes 2097152 | tf_op jit(solution)/shard_map/convert_element_type | solution.py:202
  (108 shorter events, 14.2 us)
Async XLA Ops:
  3.0 7.6 %collective-permute-start = (bf16[72,1024]{1,0:T(8,128)(2,1)}, bf16[72,1024]{1,0:T(8,128)(2,1)S(1)}, u32[]{:S(2)}, u32[]{:S(2)}) collective-permute-start(bf16[72,1024]{1,0:T(8,128)(2,1)} %get-tuple-element.44.refs_2_.refs_14_), channel_id=1, source_target_pairs={{0,2},{2,4},{4,6},{6,7},{7,5},{5,3},{3,1},{1,0},{8,10},{10,12},{12... | collective-permute-start | bytes 442376 | tf_op jit(solution)/shard_map/ppermute | solution.py:222
  6.1 6.9 %collective-permute-start.3 = (bf16[72,1024]{1,0:T(8,128)(2,1)}, bf16[72,1024]{1,0:T(8,128)(2,1)S(1)}, u32[]{:S(2)}, u32[]{:S(2)}) collective-permute-start(bf16[72,1024]{1,0:T(8,128)(2,1)} %get-tuple-element.44.refs_2_.refs_14_), channel_id=1, source_target_pairs={{2,0},{4,2},{6,4},{7,6},{5,7},{3,5},{1,3},{0,1},{10,8},{12,10},{14... | collective-permute-start | bytes 442376 | tf_op jit(solution)/shard_map/ppermute | solution.py:225
  6.1 9.5 %collective-permute-start.4 = (bf16[64,1024]{1,0:T(8,128)(2,1)}, bf16[64,1024]{1,0:T(8,128)(2,1)S(1)}, u32[]{:S(2)}, u32[]{:S(2)}) collective-permute-start(bf16[64,1024]{1,0:T(8,128)(2,1)} %get-tuple-element.45.refs_3_.refs_15_), channel_id=1, source_target_pairs={{2,0},{4,2},{6,4},{7,6},{5,7},{3,5},{1,3},{0,1},{10,8},{12,10},{14... | collective-permute-start | bytes 393224 | tf_op jit(solution)/shard_map/ppermute | solution.py:225
  8.1 7.6 %collective-permute-start.2 = (bf16[64,1024]{1,0:T(8,128)(2,1)}, bf16[64,1024]{1,0:T(8,128)(2,1)S(1)}, u32[]{:S(2)}, u32[]{:S(2)}) collective-permute-start(bf16[64,1024]{1,0:T(8,128)(2,1)} %get-tuple-element.45.refs_3_.refs_15_), channel_id=1, source_target_pairs={{0,2},{2,4},{4,6},{6,7},{7,5},{5,3},{3,1},{1,0},{8,10},{10,12},{12... | collective-permute-start | bytes 393224 | tf_op jit(solution)/shard_map/ppermute | solution.py:222
  10.7 14.1 %collective-permute-start.1 = (bf16[72,1024]{1,0:T(8,128)(2,1)S(1)}, bf16[72,1024]{1,0:T(8,128)(2,1)S(1)}, u32[]{:S(2)}, u32[]{:S(2)}) collective-permute-start(bf16[72,1024]{1,0:T(8,128)(2,1)S(1)} %collective-permute-done.refs_0_), channel_id=1, source_target_pairs={{0,2},{2,4},{4,6},{6,7},{7,5},{5,3},{3,1},{1,0},{8,10},{10,12},{12... | collective-permute-start | bytes 442376 | tf_op jit(solution)/shard_map/ppermute | solution.py:222
  13.1 13.3 %collective-permute-start.7 = (bf16[72,1024]{1,0:T(8,128)(2,1)S(1)}, bf16[72,1024]{1,0:T(8,128)(2,1)S(1)}, u32[]{:S(2)}, u32[]{:S(2)}) collective-permute-start(bf16[72,1024]{1,0:T(8,128)(2,1)S(1)} %collective-permute-done.3.refs_2_), channel_id=1, source_target_pairs={{2,0},{4,2},{6,4},{7,6},{5,7},{3,5},{1,3},{0,1},{10,8},{12,10},{14... | collective-permute-start | bytes 442376 | tf_op jit(solution)/shard_map/ppermute | solution.py:225
  15.6 11.2 %collective-permute-start.8 = (bf16[64,1024]{1,0:T(8,128)(2,1)S(1)}, bf16[64,1024]{1,0:T(8,128)(2,1)S(1)}, u32[]{:S(2)}, u32[]{:S(2)}) collective-permute-start(bf16[64,1024]{1,0:T(8,128)(2,1)S(1)} %collective-permute-done.4.refs_3_), channel_id=1, source_target_pairs={{2,0},{4,2},{6,4},{7,6},{5,7},{3,5},{1,3},{0,1},{10,8},{12,10},{14... | collective-permute-start | bytes 393224 | tf_op jit(solution)/shard_map/ppermute | solution.py:225
  15.7 11.2 %collective-permute-start.6 = (bf16[64,1024]{1,0:T(8,128)(2,1)S(1)}, bf16[64,1024]{1,0:T(8,128)(2,1)S(1)}, u32[]{:S(2)}, u32[]{:S(2)}) collective-permute-start(bf16[64,1024]{1,0:T(8,128)(2,1)S(1)} %collective-permute-done.2.refs_1_), channel_id=1, source_target_pairs={{0,2},{2,4},{4,6},{6,7},{7,5},{5,3},{3,1},{1,0},{8,10},{10,12},{12... | collective-permute-start | bytes 393224 | tf_op jit(solution)/shard_map/ppermute | solution.py:222
  24.8 8.9 %collective-permute-start.5 = (bf16[72,1024]{1,0:T(8,128)(2,1)S(1)}, bf16[72,1024]{1,0:T(8,128)(2,1)S(1)}, u32[]{:S(2)}, u32[]{:S(2)}) collective-permute-start(bf16[72,1024]{1,0:T(8,128)(2,1)S(1)} %collective-permute-done.1.refs_0_.refs_4_), channel_id=1, source_target_pairs={{0,2},{2,4},{4,6},{6,7},{7,5},{5,3},{3,1},{1,0},{8,10},{10,12},{12... | collective-permute-start | bytes 442376 | tf_op jit(solution)/shard_map/ppermute | solution.py:222
  26.3 9.4 %collective-permute-start.13 = (bf16[72,1024]{1,0:T(8,128)(2,1)S(1)}, bf16[72,1024]{1,0:T(8,128)(2,1)S(1)}, u32[]{:S(2)}, u32[]{:S(2)}) collective-permute-start(bf16[72,1024]{1,0:T(8,128)(2,1)S(1)} %collective-permute-done.7.refs_2_.refs_6_), channel_id=1, source_target_pairs={{2,0},{4,2},{6,4},{7,6},{5,7},{3,5},{1,3},{0,1},{10,8},{12,10},{14... | collective-permute-start | bytes 442376 | tf_op jit(solution)/shard_map/ppermute | solution.py:225
  26.8 8.5 %collective-permute-start.10 = (bf16[64,1024]{1,0:T(8,128)(2,1)S(1)}, bf16[64,1024]{1,0:T(8,128)(2,1)S(1)}, u32[]{:S(2)}, u32[]{:S(2)}) collective-permute-start(bf16[64,1024]{1,0:T(8,128)(2,1)S(1)} %collective-permute-done.8.refs_3_.refs_7_), channel_id=1, source_target_pairs={{2,0},{4,2},{6,4},{7,6},{5,7},{3,5},{1,3},{0,1},{10,8},{12,10},{14... | collective-permute-start | bytes 393224 | tf_op jit(solution)/shard_map/ppermute | solution.py:225
  26.9 8.9 %collective-permute-start.12 = (bf16[64,1024]{1,0:T(8,128)(2,1)S(1)}, bf16[64,1024]{1,0:T(8,128)(2,1)S(1)}, u32[]{:S(2)}, u32[]{:S(2)}) collective-permute-start(bf16[64,1024]{1,0:T(8,128)(2,1)S(1)} %collective-permute-done.6.refs_1_.refs_5_), channel_id=1, source_target_pairs={{0,2},{2,4},{4,6},{6,7},{7,5},{5,3},{3,1},{1,0},{8,10},{10,12},{12... | collective-permute-start | bytes 393224 | tf_op jit(solution)/shard_map/ppermute | solution.py:222
  33.7 9.0 %collective-permute-start.9 = (bf16[72,1024]{1,0:T(8,128)(2,1)S(1)}, bf16[72,1024]{1,0:T(8,128)(2,1)S(1)}, u32[]{:S(2)}, u32[]{:S(2)}) collective-permute-start(bf16[72,1024]{1,0:T(8,128)(2,1)S(1)} %collective-permute-done.5.refs_0_.refs_8_), channel_id=1, source_target_pairs={{0,2},{2,4},{4,6},{6,7},{7,5},{5,3},{3,1},{1,0},{8,10},{10,12},{12... | collective-permute-start | bytes 442376 | tf_op jit(solution)/shard_map/ppermute | solution.py:222
  35.3 7.4 %collective-permute-start.11 = (bf16[64,1024]{1,0:T(8,128)(2,1)S(1)}, bf16[64,1024]{1,0:T(8,128)(2,1)}, u32[]{:S(2)}, u32[]{:S(2)}) collective-permute-start(bf16[64,1024]{1,0:T(8,128)(2,1)S(1)} %collective-permute-done.10.refs_3_.refs_11_), channel_id=1, source_target_pairs={{2,0},{4,2},{6,4},{7,6},{5,7},{3,5},{1,3},{0,1},{10,8},{12,10},{14... | collective-permute-start | bytes 393224 | tf_op jit(solution)/shard_map/ppermute | solution.py:225
  40.7 6.6 %collective-permute-start.24 = (bf16[64,1024]{1,0:T(8,128)(2,1)}, bf16[64,1024]{1,0:T(8,128)(2,1)}, u32[]{:S(2)}, u32[]{:S(2)}) collective-permute-start(bf16[64,1024]{1,0:T(8,128)(2,1)} %get-tuple-element.79), channel_id=1, source_target_pairs={{2,0},{4,2},{6,4},{7,6},{5,7},{3,5},{1,3},{0,1},{10,8},{12,10},{14... | collective-permute-start | bytes 393224 | tf_op jit(solution)/shard_map/ppermute | solution.py:225
  40.8 6.5 %collective-permute-start.21 = (bf16[64,1024]{1,0:T(8,128)(2,1)}, bf16[64,1024]{1,0:T(8,128)(2,1)}, u32[]{:S(2)}, u32[]{:S(2)}) collective-permute-start(bf16[64,1024]{1,0:T(8,128)(2,1)} %get-tuple-element.72), channel_id=1, source_target_pairs={{0,2},{2,4},{4,6},{6,7},{7,5},{5,3},{3,1},{1,0},{8,10},{10,12},{12... | collective-permute-start | bytes 393224 | tf_op jit(solution)/shard_map/ppermute | solution.py:222
  47.1 13.6 %collective-permute-start.17 = (bf16[64,1024]{1,0:T(8,128)(2,1)S(1)}, bf16[64,1024]{1,0:T(8,128)(2,1)S(1)}, u32[]{:S(2)}, u32[]{:S(2)}) collective-permute-start(bf16[64,1024]{1,0:T(8,128)(2,1)S(1)} %get-tuple-element.69), channel_id=1, source_target_pairs={{2,0},{4,2},{6,4},{7,6},{5,7},{3,5},{1,3},{0,1},{10,8},{12,10},{14... | collective-permute-start | bytes 393224 | tf_op jit(solution)/shard_map/ppermute | solution.py:225
  48.2 9.7 %collective-permute-start.22 = (bf16[64,1024]{1,0:T(8,128)(2,1)S(1)}, bf16[64,1024]{1,0:T(8,128)(2,1)S(1)}, u32[]{:S(2)}, u32[]{:S(2)}) collective-permute-start(bf16[64,1024]{1,0:T(8,128)(2,1)S(1)} %add_convert_fusion.11), channel_id=1, source_target_pairs={{0,2},{2,4},{4,6},{6,7},{7,5},{5,3},{3,1},{1,0},{8,10},{10,12},{12... | collective-permute-start | bytes 393224 | tf_op jit(solution)/shard_map/ppermute | solution.py:222
  51.1 7.3 %collective-permute-start.25 = (bf16[64,1024]{1,0:T(8,128)(2,1)S(1)}, bf16[64,1024]{1,0:T(8,128)(2,1)S(1)}, u32[]{:S(2)}, u32[]{:S(2)}) collective-permute-start(bf16[64,1024]{1,0:T(8,128)(2,1)S(1)} %add_convert_fusion.8), channel_id=1, source_target_pairs={{2,0},{4,2},{6,4},{7,6},{5,7},{3,5},{1,3},{0,1},{10,8},{12,10},{14... | collective-permute-start | bytes 393224 | tf_op jit(solution)/shard_map/ppermute | solution.py:225
  51.3 8.8 %collective-permute-start.27 = (bf16[64,1024]{1,0:T(8,128)(2,1)S(1)}, bf16[64,1024]{1,0:T(8,128)(2,1)S(1)}, u32[]{:S(2)}, u32[]{:S(2)}) collective-permute-start(bf16[64,1024]{1,0:T(8,128)(2,1)S(1)} %get-tuple-element.85), channel_id=1, source_target_pairs={{0,2},{2,4},{4,6},{6,7},{7,5},{5,3},{3,1},{1,0},{8,10},{10,12},{12... | collective-permute-start | bytes 393224 | tf_op jit(solution)/shard_map/ppermute | solution.py:222
  55.4 24.5 %collective-permute-start.14 = (bf16[1024,256]{1,0:T(8,128)(2,1)S(1)}, bf16[1024,256]{1,0:T(8,128)(2,1)S(1)}, u32[]{:S(2)}, u32[]{:S(2)}) collective-permute-start(bf16[1024,256]{1,0:T(8,128)(2,1)S(1)} %get-tuple-element.64), channel_id=1, source_target_pairs={{0,8},{8,0},{16,24},{24,16},{1,9},{9,1},{17,25},{25,17},{2,10},{10... | collective-permute-start | bytes 1572872 | tf_op jit(solution)/shard_map/ppermute | solution.py:276
  57.9 9.2 %collective-permute-start.15 = (bf16[1024,256]{1,0:T(8,128)(2,1)S(1)}, bf16[1024,256]{1,0:T(8,128)(2,1)S(1)}, u32[]{:S(2)}, u32[]{:S(2)}) collective-permute-start(bf16[1024,256]{1,0:T(8,128)(2,1)S(1)} %get-tuple-element.66), channel_id=1, source_target_pairs={{0,8},{8,0},{16,24},{24,16},{1,9},{9,1},{17,25},{25,17},{2,10},{10... | collective-permute-start | bytes 1572872 | tf_op jit(solution)/shard_map/ppermute | solution.py:276
  58.3 21.6 %copy-start.5 = (bf16[64,1024]{1,0:T(8,128)(2,1)S(1)}, bf16[64,1024]{1,0:T(8,128)(2,1)}, u32[]{:S(2)}) copy-start(bf16[64,1024]{1,0:T(8,128)(2,1)} %copy-done.4) | copy-start | bytes 393220
  58.4 26.5 %collective-permute-start.23 = (bf16[64,1024]{1,0:T(8,128)(2,1)S(1)}, bf16[64,1024]{1,0:T(8,128)(2,1)S(1)}, u32[]{:S(2)}, u32[]{:S(2)}) collective-permute-start(bf16[64,1024]{1,0:T(8,128)(2,1)S(1)} %add_convert_fusion.10), channel_id=1, source_target_pairs={{0,2},{2,4},{4,6},{6,7},{7,5},{5,3},{3,1},{1,0},{8,10},{10,12},{12... | collective-permute-start | bytes 393224 | tf_op jit(solution)/shard_map/ppermute | solution.py:222
  60.1 24.8 %collective-permute-start.26 = (bf16[64,1024]{1,0:T(8,128)(2,1)S(1)}, bf16[64,1024]{1,0:T(8,128)(2,1)S(1)}, u32[]{:S(2)}, u32[]{:S(2)}) collective-permute-start(bf16[64,1024]{1,0:T(8,128)(2,1)S(1)} %add_convert_fusion.7), channel_id=1, source_target_pairs={{2,0},{4,2},{6,4},{7,6},{5,7},{3,5},{1,3},{0,1},{10,8},{12,10},{14... | collective-permute-start | bytes 393224 | tf_op jit(solution)/shard_map/ppermute | solution.py:225
  60.6 6.2 %collective-permute-start.28 = (bf16[64,1024]{1,0:T(8,128)(2,1)S(1)}, bf16[64,1024]{1,0:T(8,128)(2,1)S(1)}, u32[]{:S(2)}, u32[]{:S(2)}) collective-permute-start(bf16[64,1024]{1,0:T(8,128)(2,1)S(1)} %add_convert_fusion.6), channel_id=1, source_target_pairs={{0,2},{2,4},{4,6},{6,7},{7,5},{5,3},{3,1},{1,0},{8,10},{10,12},{12... | collective-permute-start | bytes 393224 | tf_op jit(solution)/shard_map/ppermute | solution.py:222
  66.8 5.0 %collective-permute-start.18 = (bf16[64,1024]{1,0:T(8,128)(2,1)S(1)}, bf16[64,1024]{1,0:T(8,128)(2,1)S(1)}, u32[]{:S(2)}, u32[]{:S(2)}) collective-permute-start(bf16[64,1024]{1,0:T(8,128)(2,1)S(1)} %add_convert_fusion.14), channel_id=1, source_target_pairs={{2,0},{4,2},{6,4},{7,6},{5,7},{3,5},{1,3},{0,1},{10,8},{12,10},{14... | collective-permute-start | bytes 393224 | tf_op jit(solution)/shard_map/ppermute | solution.py:225
  67.1 6.2 %collective-permute-start.29 = (bf16[64,1024]{1,0:T(8,128)(2,1)S(1)}, bf16[64,1024]{1,0:T(8,128)(2,1)S(1)}, u32[]{:S(2)}, u32[]{:S(2)}) collective-permute-start(bf16[64,1024]{1,0:T(8,128)(2,1)S(1)} %add_convert_fusion.5), channel_id=1, source_target_pairs={{0,2},{2,4},{4,6},{6,7},{7,5},{5,3},{3,1},{1,0},{8,10},{10,12},{12... | collective-permute-start | bytes 393224 | tf_op jit(solution)/shard_map/ppermute | solution.py:222
  71.8 12.0 %collective-permute-start.16 = (bf16[1024,256]{1,0:T(8,128)(2,1)S(1)}, bf16[1024,256]{1,0:T(8,128)(2,1)S(1)}, u32[]{:S(2)}, u32[]{:S(2)}) collective-permute-start(bf16[1024,256]{1,0:T(8,128)(2,1)S(1)} %add_convert_fusion.1), channel_id=1, source_target_pairs={{0,16},{8,24},{16,0},{24,8},{1,17},{9,25},{17,1},{25,9},{2,18},{10... | collective-permute-start | bytes 1572872 | tf_op jit(solution)/shard_map/ppermute | solution.py:276
  73.3 5.0 %collective-permute-start.19 = (bf16[64,1024]{1,0:T(8,128)(2,1)S(1)}, bf16[64,1024]{1,0:T(8,128)(2,1)S(1)}, u32[]{:S(2)}, u32[]{:S(2)}) collective-permute-start(bf16[64,1024]{1,0:T(8,128)(2,1)S(1)} %add_convert_fusion.13), channel_id=1, source_target_pairs={{2,0},{4,2},{6,4},{7,6},{5,7},{3,5},{1,3},{0,1},{10,8},{12,10},{14... | collective-permute-start | bytes 393224 | tf_op jit(solution)/shard_map/ppermute | solution.py:225
  78.4 6.5 %collective-permute-start.30 = (bf16[64,1024]{1,0:T(8,128)(2,1)S(1)}, bf16[64,1024]{1,0:T(8,128)(2,1)S(1)}, u32[]{:S(2)}, u32[]{:S(2)}) collective-permute-start(bf16[64,1024]{1,0:T(8,128)(2,1)S(1)} %add_convert_fusion.4), channel_id=1, source_target_pairs={{0,2},{2,4},{4,6},{6,7},{7,5},{5,3},{3,1},{1,0},{8,10},{10,12},{12... | collective-permute-start | bytes 393224 | tf_op jit(solution)/shard_map/ppermute | solution.py:222
  80.0 5.0 %collective-permute-start.20 = (bf16[64,1024]{1,0:T(8,128)(2,1)S(1)}, bf16[64,1024]{1,0:T(8,128)(2,1)S(1)}, u32[]{:S(2)}, u32[]{:S(2)}) collective-permute-start(bf16[64,1024]{1,0:T(8,128)(2,1)S(1)} %add_convert_fusion.12), channel_id=1, source_target_pairs={{2,0},{4,2},{6,4},{7,6},{5,7},{3,5},{1,3},{0,1},{10,8},{12,10},{14... | collective-permute-start | bytes 393224 | tf_op jit(solution)/shard_map/ppermute | solution.py:225
  (27 other events, 123.3 us)

commit v3 on v2

--- a/solution.py
+++ b/solution.py
@@ -13,15 +13,12 @@
 FIELD_ROWS = 8
 CHUNK = 256
 VMEM_LIMIT = 24 * 1024 * 1024
-WHOLE_VMEM = 60 * 1024 * 1024
-
-
-def pack_kernel(feat_ref, short_ref, pos_ref, a_ref, b_ref, sem_a, sem_b):
+
+
+def pack_kernel(feat_ref, short_ref, pos_ref, a_ref, b_ref):
     half, width = b_ref.shape
-    copy_a = pltpu.make_async_copy(feat_ref.at[pl.ds(0, half)], a_ref.at[pl.ds(0, half)], sem_a)
-    copy_b = pltpu.make_async_copy(feat_ref.at[pl.ds(half, half)], b_ref, sem_b)
-    copy_a.start()
-    copy_b.start()
+    a_ref[:half, :] = feat_ref[:half, :]
+    b_ref[...] = feat_ref[half:, :]
     top_count, rows = short_ref.shape
     short = short_ref[...]
     places = pos_ref[...] // BLOCK
@@ -36,8 +33,6 @@
     groups.append(jnp.zeros((FIELD_ROWS, width - rows * len(groups)), jnp.int32))
     meta = jnp.concatenate(groups, axis=1)
     a_ref[half:, :] = meta.astype(jnp.float32).astype(jnp.bfloat16)
-    copy_a.wait()
-    copy_b.wait()
 
 
 def pack(features, shortlist, positives):
@@ -49,14 +44,9 @@
             jax.ShapeDtypeStruct((half + FIELD_ROWS, width), jnp.bfloat16),
             jax.ShapeDtypeStruct((half, width), jnp.bfloat16),
         ],
-        in_specs=[
-            pl.BlockSpec(memory_space=pltpu.HBM),
-            pl.BlockSpec(memory_space=pltpu.VMEM),
-            pl.BlockSpec(memory_space=pltpu.VMEM),
-        ],
+        in_specs=[pl.BlockSpec(memory_space=pltpu.VMEM)] * 3,
         out_specs=[pl.BlockSpec(memory_space=pltpu.VMEM)] * 2,
-        scratch_shapes=[pltpu.SemaphoreType.DMA, pltpu.SemaphoreType.DMA],
-        compiler_params=pltpu.CompilerParams(vmem_limit_bytes=WHOLE_VMEM),
+        compiler_params=pltpu.CompilerParams(vmem_limit_bytes=VMEM_LIMIT),
         name="pack",
     )(features, shortlist.T, positives.T)
 
@@ -202,8 +192,22 @@
     return total.astype(jnp.bfloat16)
 
 
-def behind(array, other):
-    return lax.optimization_barrier((array, other))[0]
+def behind(array, *others):
+    return lax.optimization_barrier((array, *others))[0]
+
+
+class Turn:
+    def __init__(self):
+        self.before = []
+
+    def passed(self, array):
+        self.before.append(array)
+
+    def __call__(self, array):
+        if self.before:
+            array = behind(array, *self.before)
+        self.before = [array]
+        return array
 
 
 def local(features, shortlist, positives, cluster_sizes, weights):
@@ -233,6 +237,7 @@
     below, above = {0: own}, {0: own}
     below_grad, above_grad = {}, {}
     used, slopes = [], []
+    turn = Turn()
 
     def take(blocks):
         grads, found = work(blocks)
@@ -257,17 +262,13 @@
             below_grad[k - 1], above_grad[k - 1] = take([below[k - 1], above[k - 1]])
 
     last = steps - 1
-    b_going_down, a_going_up = below_grad[last][1], above_grad[last][0]
-    b_from_above, a_from_below = send_down(b_going_down), send_up(a_going_up)
+    b_from_above = send_down(turn(below_grad[last][1]))
+    a_from_below = send_up(turn(above_grad[last][0]))
     (far_grad, own_grad) = take([opposite, own])
-    a_from_above, b_from_below = send_down(far_grad[0]), send_up(far_grad[1])
-    for k in range(last, 0, -1):
-        a_down, b_up = add(below_grad[k][0], a_from_above), add(above_grad[k][1], b_from_below)
-        if k > 1:
-            b_down = add(below_grad[k - 1][1], behind(b_from_above, far_grad[0]))
-            a_up = add(above_grad[k - 1][0], behind(a_from_below, far_grad[0]))
-            b_from_above, a_from_below = send_down(b_down), send_up(a_up)
-        a_from_above, b_from_below = send_down(a_down), send_up(b_up)
+    turn.passed(far_grad[0])
+    a_from_above = send_down(turn(far_grad[0]))
+    b_from_below = send_up(turn(far_grad[1]))
+    b_from_above, a_from_below = behind(b_from_above, far_grad[0]), behind(a_from_below, far_grad[0])
 
     scale = 1.0 / math.sqrt(inst_rows * seq_count * top_count // local_count)
     own_seq = lax.axis_index("seq").astype(jnp.int32).reshape(1)
@@ -275,16 +276,46 @@
     def seq_send(array, bit):
         return lax.ppermute(array, "seq", [(k, k ^ bit) for k in range(seq_count)])
 
-    away = [q for q in range(seq_count) if q & 1]
-    kept = [q for q in range(seq_count) if not q & 1]
-    slots = dict(zip(away, weight_work(used, slopes, own_seq, away, part_width, scale)))
-    slots.update(zip(kept, weight_work(used, slopes, own_seq, kept, part_width, scale)))
-    bit = 1
-    while bit < seq_count:
-        for q in [q for q in sorted(slots, reverse=True) if q & bit]:
-            slots[q ^ bit] = add(slots[q ^ bit], seq_send(slots.pop(q), bit))
-        bit *= 2
-    weight_grad = slots[0]
+    terms = {}
+
+    def weigh(slots):
+        parts = weight_work(used, slopes, own_seq, slots, part_width, scale)
+        turn.passed(parts[0])
+        terms.update({q: [part] for q, part in zip(slots, parts)})
+
+    def halve(bit, slots):
+        for q in slots:
+            values = terms.pop(q)
+            going = turn(add(*values) if len(values) > 1 else values[0])
+            terms[q ^ bit].append(seq_send(going, bit))
+
+    near, far = list(range(seq_count // 2)), list(range(seq_count // 2, seq_count))
+
+    def weigh_far():
+        weigh(far)
+        halve(1, far[1::2])
+
+    def weigh_near():
+        weigh(near)
+        halve(1, near[1::2])
+        bit = 2
+        while bit < seq_count:
+            halve(bit, [q for q in sorted(terms, reverse=True) if q & bit])
+            bit *= 2
+
+    for k in range(last, 0, -1):
+        a_down, b_up = (below_grad[k][0], a_from_above), (above_grad[k][1], b_from_below)
+        if k > 1:
+            b_down, a_up = (below_grad[k - 1][1], b_from_above), (above_grad[k - 1][0], a_from_below)
+            b_from_above = send_down(turn(add(*b_down)))
+            a_from_below = send_up(turn(add(*a_up)))
+        if k == last:
+            weigh_far()
+        a_from_above = send_down(turn(add(*a_down)))
+        b_from_below = send_up(turn(add(*b_up)))
+        if k == last:
+            weigh_near()
+    weight_grad = add(*terms[0])
 
     feature_grad = jnp.concatenate(
         [

time: 86.1 us -> 81.8 us (0.950)
  waiting for transfers between devices: 20.2 us -> 16.3 us
  Pallas kernels: 17 us -> 14.7 us
  local copies, waits for them, and re-layouts: 11.1 us -> 13.3 us
    ppermute x14, starting transfers between devices: 5.29 us -> 14.2 us  [send_down(): return lax.ppermute(array, 'clus', down)]
    ppermute x14, starting transfers between devices: 25 us -> 16.8 us  [send_up(): return lax.ppermute(array, 'clus', up)]
    ppermute x14, waiting for transfers between devices: 9.86 us -> 6.01 us  [send_down(): return lax.ppermute(array, 'clus', down)]
    ppermute x3, waiting for transfers between devices: 3.33 us -> 0.01 us  [seq_send(): return lax.ppermute(array, 'seq', [(k, k ^ bit) for k in range(seq_count)])]
    ppermute x14, waiting for transfers between devices: 7.05 us -> 10.2 us  [send_up(): return lax.ppermute(array, 'clus', up)]
    pallas_call x1, Pallas kernels: 2.39 us -> 0.05 us  [pack(): pl.pallas_call(pack_kernel, out_shape=[jax.ShapeDtypeStruct((half + FIELD...]
    unnamed x56 -> x58, local copies, waits for them, and re-layouts: 11.1 us -> 13.3 us
    convert_element_type x14 -> x13, other arithmetic: 3.44 us -> 2.6 us  [add(): return total.astype(jnp.bfloat16)]
  transfers between devices with their start and end apart: 31 -> 31, of which waited for: 8 -> 7; matrix products, arithmetic and copies ran while one was open for 4% -> 3% of each run, Pallas kernels for 17% -> 18%
where the time goes in v3:
time: 81.8 us; the launch traced here: 81.4 us
  starting transfers between devices  32.9 us (40%)
  waiting for transfers between devices  16.3 us (20%)
  Pallas kernels  14.7 us (18%)
  local copies, waits for them, and re-layouts  13.3 us (16%)
  other arithmetic  3.32 us (4%)
  between operations  0.96 us (1%)
    ppermute x14, starting transfers between devices, send_up(): return lax.ppermute(array, 'clus', up)  16.8 us
    ppermute x14, starting transfers between devices, send_down(): return lax.ppermute(array, 'clus', down)  14.2 us
    unnamed x58, local copies, waits for them, and re-layouts  13.3 us
    ppermute x14, waiting for transfers between devices, send_up(): return lax.ppermute(array, 'clus', up)  10.2 us
    pallas_call x4, Pallas kernels, block_work(): pl.pallas_call(functools.partial(block_kernel, count, top_count, pos_coun...  10 us
    ppermute x14, waiting for transfers between devices, send_down(): return lax.ppermute(array, 'clus', down)  6.01 us
    pallas_call x2, Pallas kernels, weight_work(): pl.pallas_call(functools.partial(weight_kernel, count, column_blocks, sca...  4.57 us
    convert_element_type x13, other arithmetic, add(): return total.astype(jnp.bfloat16)  2.6 us
  transfers between devices with their start and end apart: 31, of which 7 were waited for; matrix products, arithmetic and copies ran while one was open for 3% of the time, Pallas kernels for 18%

profile of v3, /device:TPU:0, one launch (start us, length us, event | category | flops | bytes accessed | tf_op | source)
XLA Modules:
  0.0 81.4 jit_solution(4907951492754232822)
XLA Ops:
  0.6 0.9 %copy-done.2 = bf16[128,1024]{1,0:T(8,128)(2,1)S(1)} copy-done((bf16[128,1024]{1,0:T(8,128)(2,1)S(1)}, bf16[128,1024]{1,0:T(8,128)(2,1)}, u32[]{:S(2)}) %copy-start.2) | copy-done | bytes 262168
  3.0 3.1 %collective-permute-start = (bf16[72,1024]{1,0:T(8,128)(2,1)S(1)}, bf16[72,1024]{1,0:T(8,128)(2,1)S(1)}, u32[]{:S(2)}, u32[]{:S(2)}) collective-permute-start(bf16[72,1024]{1,0:T(8,128)(2,1)S(1)} %get-tuple-element.58.refs_2_.refs_14_), channel_id=1, source_target_pairs={{0,2},{2,4},{4,6},{6,7},{7,5},{5,3},{3,1},{1,0},{8,10},{10,12},{12... | collective-permute-start | bytes 442376 | tf_op jit(solution)/shard_map/ppermute | solution.py:226
  6.1 2.0 %collective-permute-start.2 = (bf16[64,1024]{1,0:T(8,128)(2,1)S(1)}, bf16[64,1024]{1,0:T(8,128)(2,1)S(1)}, u32[]{:S(2)}, u32[]{:S(2)}) collective-permute-start(bf16[64,1024]{1,0:T(8,128)(2,1)S(1)} %get-tuple-element.59.refs_3_.refs_15_), channel_id=1, source_target_pairs={{0,2},{2,4},{4,6},{6,7},{7,5},{5,3},{3,1},{1,0},{8,10},{10,12},{12... | collective-permute-start | bytes 393224 | tf_op jit(solution)/shard_map/ppermute | solution.py:226
  8.1 2.6 %collective-permute-done.refs_0_ = bf16[72,1024]{1,0:T(8,128)(2,1)S(1)} collective-permute-done((bf16[72,1024]{1,0:T(8,128)(2,1)S(1)}, bf16[72,1024]{1,0:T(8,128)(2,1)S(1)}, u32[]{:S(2)}, u32[]{:S(2)}) %collective-permute-start) | collective-permute-done | bytes 147488 | tf_op jit(solution)/shard_map/ppermute | solution.py:226
  10.7 2.1 %collective-permute-start.1 = (bf16[72,1024]{1,0:T(8,128)(2,1)S(1)}, bf16[72,1024]{1,0:T(8,128)(2,1)S(1)}, u32[]{:S(2)}, u32[]{:S(2)}) collective-permute-start(bf16[72,1024]{1,0:T(8,128)(2,1)S(1)} %collective-permute-done.refs_0_), channel_id=1, source_target_pairs={{0,2},{2,4},{4,6},{6,7},{7,5},{5,3},{3,1},{1,0},{8,10},{10,12},{12... | collective-permute-start | bytes 442376 | tf_op jit(solution)/shard_map/ppermute | solution.py:226
  13.5 2.1 %collective-permute-start.6 = (bf16[64,1024]{1,0:T(8,128)(2,1)S(1)}, bf16[64,1024]{1,0:T(8,128)(2,1)S(1)}, u32[]{:S(2)}, u32[]{:S(2)}) collective-permute-start(bf16[64,1024]{1,0:T(8,128)(2,1)S(1)} %collective-permute-done.2.refs_1_), channel_id=1, source_target_pairs={{0,2},{2,4},{4,6},{6,7},{7,5},{5,3},{3,1},{1,0},{8,10},{10,12},{12... | collective-permute-start | bytes 393224 | tf_op jit(solution)/shard_map/ppermute | solution.py:226
  15.6 1.6 %copy-done.25 = bf16[1024,1024]{1,0:T(8,128)(2,1)S(1)} copy-done((bf16[1024,1024]{1,0:T(8,128)(2,1)S(1)}, bf16[1024,1024]{1,0:T(8,128)(2,1)}, u32[]{:S(2)}) %copy-start.25) | copy-done | bytes 2097176
  17.9 2.3 %block_work.4 = (bf16[64,1024]{1,0:T(8,128)(2,1)S(1)}, bf16[64,1024]{1,0:T(8,128)(2,1)S(1)}, bf16[64,1024]{1,0:T(8,128)(2,1)S(1)}, bf16[64,1024]{1,0:T(8,128)(2,...) custom-call(s32[1]{0:T(128)} %bitcast.first_ref, s32[8]{0:T(128)S(1)} %copy-done.27, ...), custom_call_target="tpu_custom_call" | custom-call | flops 1073741824 | bytes 3670016 | tf_op jit(solution)/shard_map/block_work/pallas_call | solution.py:135
  22.7 2.0 %collective-permute-start.5 = (bf16[72,1024]{1,0:T(8,128)(2,1)S(1)}, bf16[72,1024]{1,0:T(8,128)(2,1)S(1)}, u32[]{:S(2)}, u32[]{:S(2)}) collective-permute-start(bf16[72,1024]{1,0:T(8,128)(2,1)S(1)} %collective-permute-done.1.refs_0_.refs_4_), channel_id=1, source_target_pairs={{0,2},{2,4},{4,6},{6,7},{7,5},{5,3},{3,1},{1,0},{8,10},{10,12},{12... | collective-permute-start | bytes 442376 | tf_op jit(solution)/shard_map/ppermute | solution.py:226
  24.8 2.0 %collective-permute-start.10 = (bf16[64,1024]{1,0:T(8,128)(2,1)S(1)}, bf16[64,1024]{1,0:T(8,128)(2,1)S(1)}, u32[]{:S(2)}, u32[]{:S(2)}) collective-permute-start(bf16[64,1024]{1,0:T(8,128)(2,1)S(1)} %collective-permute-done.8.refs_3_.refs_7_), channel_id=1, source_target_pairs={{2,0},{4,2},{6,4},{7,6},{5,7},{3,5},{1,3},{0,1},{10,8},{12,10},{14... | collective-permute-start | bytes 393224 | tf_op jit(solution)/shard_map/ppermute | solution.py:229
  26.8 2.2 %block_work.5 = (bf16[64,1024]{1,0:T(8,128)(2,1)S(1)}, bf16[64,1024]{1,0:T(8,128)(2,1)S(1)}, bf16[64,1024]{1,0:T(8,128)(2,1)S(1)}, bf16[64,1024]{1,0:T(8,128)(2,...) custom-call(s32[1]{0:T(128)} %bitcast.first_ref, s32[8]{0:T(128)S(1)} %copy-done.27, ...), custom_call_target="tpu_custom_call" | custom-call | flops 1073741824 | bytes 3670016 | tf_op jit(solution)/shard_map/block_work/pallas_call | solution.py:135
  31.7 2.0 %collective-permute-start.9 = (bf16[72,1024]{1,0:T(8,128)(2,1)S(1)}, bf16[72,1024]{1,0:T(8,128)(2,1)S(1)}, u32[]{:S(2)}, u32[]{:S(2)}) collective-permute-start(bf16[72,1024]{1,0:T(8,128)(2,1)S(1)} %collective-permute-done.5.refs_0_.refs_8_), channel_id=1, source_target_pairs={{0,2},{2,4},{4,6},{6,7},{7,5},{5,3},{3,1},{1,0},{8,10},{10,12},{12... | collective-permute-start | bytes 442376 | tf_op jit(solution)/shard_map/ppermute | solution.py:226
  33.7 2.9 %block_work.7 = (bf16[64,1024]{1,0:T(8,128)(2,1)S(1)}, bf16[64,1024]{1,0:T(8,128)(2,1)}, bf16[64,1024]{1,0:T(8,128)(2,1)}, bf16[64,1024]{1,0:T(8,128)(2,1)S(1)},...) custom-call(s32[1]{0:T(128)} %bitcast.first_ref, s32[8]{0:T(128)S(1)} %copy-done.27, ...), custom_call_target="tpu_custom_call" | custom-call | flops 1073741824 | bytes 3670016 | tf_op jit(solution)/shard_map/block_work/pallas_call | solution.py:135
  38.6 1.9 %collective-permute-start.17 = (bf16[64,1024]{1,0:T(8,128)(2,1)}, bf16[64,1024]{1,0:T(8,128)(2,1)}, u32[]{:S(2)}, u32[]{:S(2)}) collective-permute-start(bf16[64,1024]{1,0:T(8,128)(2,1)} %get-tuple-element.83), channel_id=1, source_target_pairs={{2,0},{4,2},{6,4},{7,6},{5,7},{3,5},{1,3},{0,1},{10,8},{12,10},{14... | collective-permute-start | bytes 393224 | tf_op jit(solution)/shard_map/ppermute | solution.py:229
  40.7 1.6 %copy-done.26 = bf16[1024,1024]{1,0:T(8,128)(2,1)S(1)} copy-done((bf16[1024,1024]{1,0:T(8,128)(2,1)S(1)}, bf16[1024,1024]{1,0:T(8,128)(2,1)}, u32[]{:S(2)}) %copy-start.26) | copy-done | bytes 2097176
  42.3 2.6 %block_work.6 = (bf16[64,1024]{1,0:T(8,128)(2,1)S(1)}, bf16[64,1024]{1,0:T(8,128)(2,1)S(1)}, bf16[64,1024]{1,0:T(8,128)(2,1)S(1)}, bf16[64,1024]{1,0:T(8,128)(2,...) custom-call(s32[1]{0:T(128)} %bitcast.first_ref, s32[8]{0:T(128)S(1)} %copy-done.28, ...), custom_call_target="tpu_custom_call" | custom-call | flops 1073741824 | bytes 3670016 | tf_op jit(solution)/shard_map/block_work/pallas_call | solution.py:135
  44.9 2.0 %collective-permute-start.15 = (bf16[64,1024]{1,0:T(8,128)(2,1)S(1)}, bf16[64,1024]{1,0:T(8,128)(2,1)S(1)}, u32[]{:S(2)}, u32[]{:S(2)}) collective-permute-start(bf16[64,1024]{1,0:T(8,128)(2,1)S(1)} %get-tuple-element.85), channel_id=1, source_target_pairs={{2,0},{4,2},{6,4},{7,6},{5,7},{3,5},{1,3},{0,1},{10,8},{12,10},{14... | collective-permute-start | bytes 393224 | tf_op jit(solution)/shard_map/ppermute | solution.py:229
  47.2 1.0 %add_convert_fusion.10 = (bf16[64,1024]{1,0:T(8,128)(2,1)S(1)}, bf16[64,1024]{1,0:T(8,128)(2,1)S(1)}) fusion(bf16[64,1024]{1,0:T(8,128)(2,1)} %collective-permute-done.17, bf16[64,1024]{1,0:T(8,128)(2,1)S(1)} %copy-done.20, bf16[64,1024]{1,0:T(8,128)(2,1)} %collective-permute-done.16, bf16[64,1024]{1,0:T(8,128)(2,1)S(1)} %copy-done.22), kind=kLoop, calls=%fused_computation.11 | loop fusion | flops 524288 | bytes 786432 | tf_op jit(solution)/shard_map/convert_element_type | solution.py:192
  48.2 1.8 %collective-permute-start.23 = (bf16[64,1024]{1,0:T(8,128)(2,1)S(1)}, bf16[64,1024]{1,0:T(8,128)(2,1)S(1)}, u32[]{:S(2)}, u32[]{:S(2)}) collective-permute-start(bf16[64,1024]{1,0:T(8,128)(2,1)S(1)} %get-tuple-element.93), channel_id=1, source_target_pairs={{2,0},{4,2},{6,4},{7,6},{5,7},{3,5},{1,3},{0,1},{10,8},{12,10},{14... | collective-permute-start | bytes 393224 | tf_op jit(solution)/shard_map/ppermute | solution.py:229
  50.3 2.2 %weight_work.3 = (bf16[1024,256]{1,0:T(8,128)(2,1)S(1)}, bf16[1024,256]{1,0:T(8,128)(2,1)S(1)}) custom-call(s32[1]{0:T(128)} %bitcast.3.own_ref, bf16[72,1024]{1,0:T(8,128)(2,1)S(1)} %collective-permute-done.refs_0_, bf16[64,1024]{1,0:T(8,128)(2,1)S(1)} %collective-permute-done.2.refs_1_, bf16[72,1024]{1,0:T(8,128)(2,1)S(1)} %collective-permute-done.3.refs_2_, ...), custom_call_target="tpu_custom_call" | custom-call | flops 1073741824 | bytes 4718592 | tf_op jit(solution)/shard_map/weight_work/pallas_call | solution.py:173
  52.7 2.4 %weight_work.2 = (bf16[1024,256]{1,0:T(8,128)(2,1)S(1)}, bf16[1024,256]{1,0:T(8,128)(2,1)S(1)}) custom-call(s32[1]{0:T(128)} %bitcast.3.own_ref, bf16[72,1024]{1,0:T(8,128)(2,1)S(1)} %collective-permute-done.refs_0_, bf16[64,1024]{1,0:T(8,128)(2,1)S(1)} %collective-permute-done.2.refs_1_, bf16[72,1024]{1,0:T(8,128)(2,1)S(1)} %collective-permute-done.3.refs_2_, ...), custom_call_target="tpu_custom_call" | custom-call | flops 1073741824 | bytes 4718592 | tf_op jit(solution)/shard_map/weight_work/pallas_call | solution.py:173
  55.1 1.8 %collective-permute-start.21 = (bf16[64,1024]{1,0:T(8,128)(2,1)S(1)}, bf16[64,1024]{1,0:T(8,128)(2,1)S(1)}, u32[]{:S(2)}, u32[]{:S(2)}) collective-permute-start(bf16[64,1024]{1,0:T(8,128)(2,1)S(1)} %add_convert_fusion.12), channel_id=1, source_target_pairs={{2,0},{4,2},{6,4},{7,6},{5,7},{3,5},{1,3},{0,1},{10,8},{12,10},{14... | collective-permute-start | bytes 393224 | tf_op jit(solution)/shard_map/ppermute | solution.py:229
  57.4 3.6 %collective-permute-done.21 = bf16[64,1024]{1,0:T(8,128)(2,1)S(1)} collective-permute-done((bf16[64,1024]{1,0:T(8,128)(2,1)S(1)}, bf16[64,1024]{1,0:T(8,128)(2,1)S(1)}, u32[]{:S(2)}, u32[]{:S(2)}) %collective-permute-start.21) | collective-permute-done | bytes 131104 | tf_op jit(solution)/shard_map/ppermute | solution.py:229
  61.2 1.7 %collective-permute-start.20 = (bf16[1024,256]{1,0:T(8,128)(2,1)S(1)}, bf16[1024,256]{1,0:T(8,128)(2,1)S(1)}, u32[]{:S(2)}, u32[]{:S(2)}) collective-permute-start(bf16[1024,256]{1,0:T(8,128)(2,1)S(1)} %add_convert_fusion.1), channel_id=1, source_target_pairs={{0,16},{8,24},{16,0},{24,8},{1,17},{9,25},{17,1},{25,9},{2,18},{10... | collective-permute-start | bytes 1572872 | tf_op jit(solution)/shard_map/ppermute | solution.py:277
  62.9 1.5 %collective-permute-start.24 = (bf16[64,1024]{1,0:T(8,128)(2,1)S(1)}, bf16[64,1024]{1,0:T(8,128)(2,1)S(1)}, u32[]{:S(2)}, u32[]{:S(2)}) collective-permute-start(bf16[64,1024]{1,0:T(8,128)(2,1)S(1)} %add_convert_fusion.9), channel_id=1, source_target_pairs={{2,0},{4,2},{6,4},{7,6},{5,7},{3,5},{1,3},{0,1},{10,8},{12,10},{14... | collective-permute-start | bytes 393224 | tf_op jit(solution)/shard_map/ppermute | solution.py:229
  64.5 1.6 %collective-permute-start.28 = (bf16[64,1024]{1,0:T(8,128)(2,1)S(1)}, bf16[64,1024]{1,0:T(8,128)(2,1)S(1)}, u32[]{:S(2)}, u32[]{:S(2)}) collective-permute-start(bf16[64,1024]{1,0:T(8,128)(2,1)S(1)} %add_convert_fusion.7), channel_id=1, source_target_pairs={{2,0},{4,2},{6,4},{7,6},{5,7},{3,5},{1,3},{0,1},{10,8},{12,10},{14... | collective-permute-start | bytes 393224 | tf_op jit(solution)/shard_map/ppermute | solution.py:229
  66.6 2.4 %collective-permute-done.24 = bf16[64,1024]{1,0:T(8,128)(2,1)S(1)} collective-permute-done((bf16[64,1024]{1,0:T(8,128)(2,1)S(1)}, bf16[64,1024]{1,0:T(8,128)(2,1)S(1)}, u32[]{:S(2)}, u32[]{:S(2)}) %collective-permute-start.24) | collective-permute-done | bytes 131104 | tf_op jit(solution)/shard_map/ppermute | solution.py:229
  69.0 1.6 %collective-permute-start.29 = (bf16[64,1024]{1,0:T(8,128)(2,1)S(1)}, bf16[64,1024]{1,0:T(8,128)(2,1)S(1)}, u32[]{:S(2)}, u32[]{:S(2)}) collective-permute-start(bf16[64,1024]{1,0:T(8,128)(2,1)S(1)} %add_convert_fusion.5), channel_id=1, source_target_pairs={{0,2},{2,4},{4,6},{6,7},{7,5},{5,3},{3,1},{1,0},{8,10},{10,12},{12... | collective-permute-start | bytes 393224 | tf_op jit(solution)/shard_map/ppermute | solution.py:226
  70.6 3.3 %collective-permute-done.29 = bf16[64,1024]{1,0:T(8,128)(2,1)S(1)} collective-permute-done((bf16[64,1024]{1,0:T(8,128)(2,1)S(1)}, bf16[64,1024]{1,0:T(8,128)(2,1)S(1)}, u32[]{:S(2)}, u32[]{:S(2)}) %collective-permute-start.29) | collective-permute-done | bytes 131104 | tf_op jit(solution)/shard_map/ppermute | solution.py:226
  73.9 1.5 %collective-permute-start.26 = (bf16[64,1024]{1,0:T(8,128)(2,1)S(1)}, bf16[64,1024]{1,0:T(8,128)(2,1)S(1)}, u32[]{:S(2)}, u32[]{:S(2)}) collective-permute-start(bf16[64,1024]{1,0:T(8,128)(2,1)S(1)} %add_convert_fusion.6), channel_id=1, source_target_pairs={{2,0},{4,2},{6,4},{7,6},{5,7},{3,5},{1,3},{0,1},{10,8},{12,10},{14... | collective-permute-start | bytes 393224 | tf_op jit(solution)/shard_map/ppermute | solution.py:229
  76.1 1.0 %add_convert_fusion = bf16[1024,256]{1,0:T(8,128)(2,1)} fusion(bf16[1024,256]{1,0:T(8,128)(2,1)S(1)} %collective-permute-done.20, bf16[1024,256]{1,0:T(8,128)(2,1)S(1)} %collective-permute-done.18, bf16[1024,256]{1,0:T(8,128)(2,1)S(1)} %get-tuple-element.77), kind=kLoop, calls=%fused_computation | loop fusion | flops 1572864 | bytes 2097152 | tf_op jit(solution)/shard_map/convert_element_type | solution.py:192
  77.1 3.4 %collective-permute-done.30 = bf16[64,1024]{1,0:T(8,128)(2,1)S(1)} collective-permute-done((bf16[64,1024]{1,0:T(8,128)(2,1)S(1)}, bf16[64,1024]{1,0:T(8,128)(2,1)S(1)}, u32[]{:S(2)}, u32[]{:S(2)}) %collective-permute-start.30) | collective-permute-done | bytes 131104 | tf_op jit(solution)/shard_map/ppermute | solution.py:226
  (109 shorter events, 13.5 us)
Async XLA Ops:
  3.0 7.7 %collective-permute-start = (bf16[72,1024]{1,0:T(8,128)(2,1)S(1)}, bf16[72,1024]{1,0:T(8,128)(2,1)S(1)}, u32[]{:S(2)}, u32[]{:S(2)}) collective-permute-start(bf16[72,1024]{1,0:T(8,128)(2,1)S(1)} %get-tuple-element.58.refs_2_.refs_14_), channel_id=1, source_target_pairs={{0,2},{2,4},{4,6},{6,7},{7,5},{5,3},{3,1},{1,0},{8,10},{10,12},{12... | collective-permute-start | bytes 442376 | tf_op jit(solution)/shard_map/ppermute | solution.py:226
  6.1 6.7 %collective-permute-start.3 = (bf16[72,1024]{1,0:T(8,128)(2,1)S(1)}, bf16[72,1024]{1,0:T(8,128)(2,1)S(1)}, u32[]{:S(2)}, u32[]{:S(2)}) collective-permute-start(bf16[72,1024]{1,0:T(8,128)(2,1)S(1)} %get-tuple-element.58.refs_2_.refs_14_), channel_id=1, source_target_pairs={{2,0},{4,2},{6,4},{7,6},{5,7},{3,5},{1,3},{0,1},{10,8},{12,10},{14... | collective-permute-start | bytes 442376 | tf_op jit(solution)/shard_map/ppermute | solution.py:229
  6.1 7.4 %collective-permute-start.2 = (bf16[64,1024]{1,0:T(8,128)(2,1)S(1)}, bf16[64,1024]{1,0:T(8,128)(2,1)S(1)}, u32[]{:S(2)}, u32[]{:S(2)}) collective-permute-start(bf16[64,1024]{1,0:T(8,128)(2,1)S(1)} %get-tuple-element.59.refs_3_.refs_15_), channel_id=1, source_target_pairs={{0,2},{2,4},{4,6},{6,7},{7,5},{5,3},{3,1},{1,0},{8,10},{10,12},{12... | collective-permute-start | bytes 393224 | tf_op jit(solution)/shard_map/ppermute | solution.py:226
  8.1 7.5 %collective-permute-start.4 = (bf16[64,1024]{1,0:T(8,128)(2,1)S(1)}, bf16[64,1024]{1,0:T(8,128)(2,1)S(1)}, u32[]{:S(2)}, u32[]{:S(2)}) collective-permute-start(bf16[64,1024]{1,0:T(8,128)(2,1)S(1)} %get-tuple-element.59.refs_3_.refs_15_), channel_id=1, source_target_pairs={{2,0},{4,2},{6,4},{7,6},{5,7},{3,5},{1,3},{0,1},{10,8},{12,10},{14... | collective-permute-start | bytes 393224 | tf_op jit(solution)/shard_map/ppermute | solution.py:229
  10.7 12.0 %collective-permute-start.1 = (bf16[72,1024]{1,0:T(8,128)(2,1)S(1)}, bf16[72,1024]{1,0:T(8,128)(2,1)S(1)}, u32[]{:S(2)}, u32[]{:S(2)}) collective-permute-start(bf16[72,1024]{1,0:T(8,128)(2,1)S(1)} %collective-permute-done.refs_0_), channel_id=1, source_target_pairs={{0,2},{2,4},{4,6},{6,7},{7,5},{5,3},{3,1},{1,0},{8,10},{10,12},{12... | collective-permute-start | bytes 442376 | tf_op jit(solution)/shard_map/ppermute | solution.py:226
  12.8 11.9 %collective-permute-start.7 = (bf16[72,1024]{1,0:T(8,128)(2,1)S(1)}, bf16[72,1024]{1,0:T(8,128)(2,1)S(1)}, u32[]{:S(2)}, u32[]{:S(2)}) collective-permute-start(bf16[72,1024]{1,0:T(8,128)(2,1)S(1)} %collective-permute-done.3.refs_2_), channel_id=1, source_target_pairs={{2,0},{4,2},{6,4},{7,6},{5,7},{3,5},{1,3},{0,1},{10,8},{12,10},{14... | collective-permute-start | bytes 442376 | tf_op jit(solution)/shard_map/ppermute | solution.py:229
  13.5 13.2 %collective-permute-start.6 = (bf16[64,1024]{1,0:T(8,128)(2,1)S(1)}, bf16[64,1024]{1,0:T(8,128)(2,1)S(1)}, u32[]{:S(2)}, u32[]{:S(2)}) collective-permute-start(bf16[64,1024]{1,0:T(8,128)(2,1)S(1)} %collective-permute-done.2.refs_1_), channel_id=1, source_target_pairs={{0,2},{2,4},{4,6},{6,7},{7,5},{5,3},{3,1},{1,0},{8,10},{10,12},{12... | collective-permute-start | bytes 393224 | tf_op jit(solution)/shard_map/ppermute | solution.py:226
  15.6 9.1 %collective-permute-start.8 = (bf16[64,1024]{1,0:T(8,128)(2,1)S(1)}, bf16[64,1024]{1,0:T(8,128)(2,1)S(1)}, u32[]{:S(2)}, u32[]{:S(2)}) collective-permute-start(bf16[64,1024]{1,0:T(8,128)(2,1)S(1)} %collective-permute-done.4.refs_3_), channel_id=1, source_target_pairs={{2,0},{4,2},{6,4},{7,6},{5,7},{3,5},{1,3},{0,1},{10,8},{12,10},{14... | collective-permute-start | bytes 393224 | tf_op jit(solution)/shard_map/ppermute | solution.py:229
  22.7 9.0 %collective-permute-start.5 = (bf16[72,1024]{1,0:T(8,128)(2,1)S(1)}, bf16[72,1024]{1,0:T(8,128)(2,1)S(1)}, u32[]{:S(2)}, u32[]{:S(2)}) collective-permute-start(bf16[72,1024]{1,0:T(8,128)(2,1)S(1)} %collective-permute-done.1.refs_0_.refs_4_), channel_id=1, source_target_pairs={{0,2},{2,4},{4,6},{6,7},{7,5},{5,3},{3,1},{1,0},{8,10},{10,12},{12... | collective-permute-start | bytes 442376 | tf_op jit(solution)/shard_map/ppermute | solution.py:226
  24.7 9.0 %collective-permute-start.13 = (bf16[72,1024]{1,0:T(8,128)(2,1)S(1)}, bf16[72,1024]{1,0:T(8,128)(2,1)S(1)}, u32[]{:S(2)}, u32[]{:S(2)}) collective-permute-start(bf16[72,1024]{1,0:T(8,128)(2,1)S(1)} %collective-permute-done.7.refs_2_.refs_6_), channel_id=1, source_target_pairs={{2,0},{4,2},{6,4},{7,6},{5,7},{3,5},{1,3},{0,1},{10,8},{12,10},{14... | collective-permute-start | bytes 442376 | tf_op jit(solution)/shard_map/ppermute | solution.py:229
  24.8 8.9 %collective-permute-start.10 = (bf16[64,1024]{1,0:T(8,128)(2,1)S(1)}, bf16[64,1024]{1,0:T(8,128)(2,1)S(1)}, u32[]{:S(2)}, u32[]{:S(2)}) collective-permute-start(bf16[64,1024]{1,0:T(8,128)(2,1)S(1)} %collective-permute-done.8.refs_3_.refs_7_), channel_id=1, source_target_pairs={{2,0},{4,2},{6,4},{7,6},{5,7},{3,5},{1,3},{0,1},{10,8},{12,10},{14... | collective-permute-start | bytes 393224 | tf_op jit(solution)/shard_map/ppermute | solution.py:229
  26.7 7.0 %collective-permute-start.12 = (bf16[64,1024]{1,0:T(8,128)(2,1)S(1)}, bf16[64,1024]{1,0:T(8,128)(2,1)S(1)}, u32[]{:S(2)}, u32[]{:S(2)}) collective-permute-start(bf16[64,1024]{1,0:T(8,128)(2,1)S(1)} %collective-permute-done.6.refs_1_.refs_5_), channel_id=1, source_target_pairs={{0,2},{2,4},{4,6},{6,7},{7,5},{5,3},{3,1},{1,0},{8,10},{10,12},{12... | collective-permute-start | bytes 393224 | tf_op jit(solution)/shard_map/ppermute | solution.py:226
  31.7 9.0 %collective-permute-start.9 = (bf16[72,1024]{1,0:T(8,128)(2,1)S(1)}, bf16[72,1024]{1,0:T(8,128)(2,1)S(1)}, u32[]{:S(2)}, u32[]{:S(2)}) collective-permute-start(bf16[72,1024]{1,0:T(8,128)(2,1)S(1)} %collective-permute-done.5.refs_0_.refs_8_), channel_id=1, source_target_pairs={{0,2},{2,4},{4,6},{6,7},{7,5},{5,3},{3,1},{1,0},{8,10},{10,12},{12... | collective-permute-start | bytes 442376 | tf_op jit(solution)/shard_map/ppermute | solution.py:226
  33.7 7.0 %collective-permute-start.11 = (bf16[64,1024]{1,0:T(8,128)(2,1)S(1)}, bf16[64,1024]{1,0:T(8,128)(2,1)}, u32[]{:S(2)}, u32[]{:S(2)}) collective-permute-start(bf16[64,1024]{1,0:T(8,128)(2,1)S(1)} %collective-permute-done.10.refs_3_.refs_11_), channel_id=1, source_target_pairs={{2,0},{4,2},{6,4},{7,6},{5,7},{3,5},{1,3},{0,1},{10,8},{12,10},{14... | collective-permute-start | bytes 393224 | tf_op jit(solution)/shard_map/ppermute | solution.py:229
  38.6 8.4 %collective-permute-start.17 = (bf16[64,1024]{1,0:T(8,128)(2,1)}, bf16[64,1024]{1,0:T(8,128)(2,1)}, u32[]{:S(2)}, u32[]{:S(2)}) collective-permute-start(bf16[64,1024]{1,0:T(8,128)(2,1)} %get-tuple-element.83), channel_id=1, source_target_pairs={{2,0},{4,2},{6,4},{7,6},{5,7},{3,5},{1,3},{0,1},{10,8},{12,10},{14... | collective-permute-start | bytes 393224 | tf_op jit(solution)/shard_map/ppermute | solution.py:229
  40.5 6.7 %collective-permute-start.16 = (bf16[64,1024]{1,0:T(8,128)(2,1)}, bf16[64,1024]{1,0:T(8,128)(2,1)}, u32[]{:S(2)}, u32[]{:S(2)}) collective-permute-start(bf16[64,1024]{1,0:T(8,128)(2,1)} %get-tuple-element.84), channel_id=1, source_target_pairs={{0,2},{2,4},{4,6},{6,7},{7,5},{5,3},{3,1},{1,0},{8,10},{10,12},{12... | collective-permute-start | bytes 393224 | tf_op jit(solution)/shard_map/ppermute | solution.py:226
  44.9 10.1 %collective-permute-start.15 = (bf16[64,1024]{1,0:T(8,128)(2,1)S(1)}, bf16[64,1024]{1,0:T(8,128)(2,1)S(1)}, u32[]{:S(2)}, u32[]{:S(2)}) collective-permute-start(bf16[64,1024]{1,0:T(8,128)(2,1)S(1)} %get-tuple-element.85), channel_id=1, source_target_pairs={{2,0},{4,2},{6,4},{7,6},{5,7},{3,5},{1,3},{0,1},{10,8},{12,10},{14... | collective-permute-start | bytes 393224 | tf_op jit(solution)/shard_map/ppermute | solution.py:229
  46.9 10.0 %collective-permute-start.14 = (bf16[64,1024]{1,0:T(8,128)(2,1)S(1)}, bf16[64,1024]{1,0:T(8,128)(2,1)S(1)}, u32[]{:S(2)}, u32[]{:S(2)}) collective-permute-start(bf16[64,1024]{1,0:T(8,128)(2,1)S(1)} %get-tuple-element.86), channel_id=1, source_target_pairs={{0,2},{2,4},{4,6},{6,7},{7,5},{5,3},{3,1},{1,0},{8,10},{10,12},{12... | collective-permute-start | bytes 393224 | tf_op jit(solution)/shard_map/ppermute | solution.py:226
  48.2 9.1 %collective-permute-start.23 = (bf16[64,1024]{1,0:T(8,128)(2,1)S(1)}, bf16[64,1024]{1,0:T(8,128)(2,1)S(1)}, u32[]{:S(2)}, u32[]{:S(2)}) collective-permute-start(bf16[64,1024]{1,0:T(8,128)(2,1)S(1)} %get-tuple-element.93), channel_id=1, source_target_pairs={{2,0},{4,2},{6,4},{7,6},{5,7},{3,5},{1,3},{0,1},{10,8},{12,10},{14... | collective-permute-start | bytes 393224 | tf_op jit(solution)/shard_map/ppermute | solution.py:229
  50.0 7.3 %collective-permute-start.22 = (bf16[64,1024]{1,0:T(8,128)(2,1)S(1)}, bf16[64,1024]{1,0:T(8,128)(2,1)S(1)}, u32[]{:S(2)}, u32[]{:S(2)}) collective-permute-start(bf16[64,1024]{1,0:T(8,128)(2,1)S(1)} %get-tuple-element.94), channel_id=1, source_target_pairs={{0,2},{2,4},{4,6},{6,7},{7,5},{5,3},{3,1},{1,0},{8,10},{10,12},{12... | collective-permute-start | bytes 393224 | tf_op jit(solution)/shard_map/ppermute | solution.py:226
  52.6 8.4 %collective-permute-start.19 = (bf16[1024,256]{1,0:T(8,128)(2,1)S(1)}, bf16[1024,256]{1,0:T(8,128)(2,1)S(1)}, u32[]{:S(2)}, u32[]{:S(2)}) collective-permute-start(bf16[1024,256]{1,0:T(8,128)(2,1)S(1)} %get-tuple-element.96), channel_id=1, source_target_pairs={{0,8},{8,0},{16,24},{24,16},{1,9},{9,1},{17,25},{25,17},{2,10},{10... | collective-permute-start | bytes 1572872 | tf_op jit(solution)/shard_map/ppermute | solution.py:277
  55.1 20.4 %copy-start.4 = (bf16[64,1024]{1,0:T(8,128)(2,1)S(1)}, bf16[64,1024]{1,0:T(8,128)(2,1)}, u32[]{:S(2)}) copy-start(bf16[64,1024]{1,0:T(8,128)(2,1)} %copy-done.3) | copy-start | bytes 393220
  55.1 5.8 %collective-permute-start.21 = (bf16[64,1024]{1,0:T(8,128)(2,1)S(1)}, bf16[64,1024]{1,0:T(8,128)(2,1)S(1)}, u32[]{:S(2)}, u32[]{:S(2)}) collective-permute-start(bf16[64,1024]{1,0:T(8,128)(2,1)S(1)} %add_convert_fusion.12), channel_id=1, source_target_pairs={{2,0},{4,2},{6,4},{7,6},{5,7},{3,5},{1,3},{0,1},{10,8},{12,10},{14... | collective-permute-start | bytes 393224 | tf_op jit(solution)/shard_map/ppermute | solution.py:229
  57.0 7.4 %collective-permute-start.25 = (bf16[64,1024]{1,0:T(8,128)(2,1)S(1)}, bf16[64,1024]{1,0:T(8,128)(2,1)S(1)}, u32[]{:S(2)}, u32[]{:S(2)}) collective-permute-start(bf16[64,1024]{1,0:T(8,128)(2,1)S(1)} %add_convert_fusion.13), channel_id=1, source_target_pairs={{0,2},{2,4},{4,6},{6,7},{7,5},{5,3},{3,1},{1,0},{8,10},{10,12},{12... | collective-permute-start | bytes 393224 | tf_op jit(solution)/shard_map/ppermute | solution.py:226
  57.3 18.2 %collective-permute-start.18 = (bf16[1024,256]{1,0:T(8,128)(2,1)S(1)}, bf16[1024,256]{1,0:T(8,128)(2,1)S(1)}, u32[]{:S(2)}, u32[]{:S(2)}) collective-permute-start(bf16[1024,256]{1,0:T(8,128)(2,1)S(1)} %get-tuple-element.99), channel_id=1, source_target_pairs={{0,8},{8,0},{16,24},{24,16},{1,9},{9,1},{17,25},{25,17},{2,10},{10... | collective-permute-start | bytes 1572872 | tf_op jit(solution)/shard_map/ppermute | solution.py:277
  61.2 14.9 %collective-permute-start.20 = (bf16[1024,256]{1,0:T(8,128)(2,1)S(1)}, bf16[1024,256]{1,0:T(8,128)(2,1)S(1)}, u32[]{:S(2)}, u32[]{:S(2)}) collective-permute-start(bf16[1024,256]{1,0:T(8,128)(2,1)S(1)} %add_convert_fusion.1), channel_id=1, source_target_pairs={{0,16},{8,24},{16,0},{24,8},{1,17},{9,25},{17,1},{25,9},{2,18},{10... | collective-permute-start | bytes 1572872 | tf_op jit(solution)/shard_map/ppermute | solution.py:277
  62.9 6.1 %collective-permute-start.24 = (bf16[64,1024]{1,0:T(8,128)(2,1)S(1)}, bf16[64,1024]{1,0:T(8,128)(2,1)S(1)}, u32[]{:S(2)}, u32[]{:S(2)}) collective-permute-start(bf16[64,1024]{1,0:T(8,128)(2,1)S(1)} %add_convert_fusion.9), channel_id=1, source_target_pairs={{2,0},{4,2},{6,4},{7,6},{5,7},{3,5},{1,3},{0,1},{10,8},{12,10},{14... | collective-permute-start | bytes 393224 | tf_op jit(solution)/shard_map/ppermute | solution.py:229
  64.5 12.6 %collective-permute-start.28 = (bf16[64,1024]{1,0:T(8,128)(2,1)S(1)}, bf16[64,1024]{1,0:T(8,128)(2,1)S(1)}, u32[]{:S(2)}, u32[]{:S(2)}) collective-permute-start(bf16[64,1024]{1,0:T(8,128)(2,1)S(1)} %add_convert_fusion.7), channel_id=1, source_target_pairs={{2,0},{4,2},{6,4},{7,6},{5,7},{3,5},{1,3},{0,1},{10,8},{12,10},{14... | collective-permute-start | bytes 393224 | tf_op jit(solution)/shard_map/ppermute | solution.py:229
  66.1 14.5 %collective-permute-start.27 = (bf16[64,1024]{1,0:T(8,128)(2,1)S(1)}, bf16[64,1024]{1,0:T(8,128)(2,1)S(1)}, u32[]{:S(2)}, u32[]{:S(2)}) collective-permute-start(bf16[64,1024]{1,0:T(8,128)(2,1)S(1)} %add_convert_fusion.8), channel_id=1, source_target_pairs={{0,2},{2,4},{4,6},{6,7},{7,5},{5,3},{3,1},{1,0},{8,10},{10,12},{12... | collective-permute-start | bytes 393224 | tf_op jit(solution)/shard_map/ppermute | solution.py:226
  69.0 5.0 %collective-permute-start.29 = (bf16[64,1024]{1,0:T(8,128)(2,1)S(1)}, bf16[64,1024]{1,0:T(8,128)(2,1)S(1)}, u32[]{:S(2)}, u32[]{:S(2)}) collective-permute-start(bf16[64,1024]{1,0:T(8,128)(2,1)S(1)} %add_convert_fusion.5), channel_id=1, source_target_pairs={{0,2},{2,4},{4,6},{6,7},{7,5},{5,3},{3,1},{1,0},{8,10},{10,12},{12... | collective-permute-start | bytes 393224 | tf_op jit(solution)/shard_map/ppermute | solution.py:226
  73.9 6.7 %collective-permute-start.26 = (bf16[64,1024]{1,0:T(8,128)(2,1)S(1)}, bf16[64,1024]{1,0:T(8,128)(2,1)S(1)}, u32[]{:S(2)}, u32[]{:S(2)}) collective-permute-start(bf16[64,1024]{1,0:T(8,128)(2,1)S(1)} %add_convert_fusion.6), channel_id=1, source_target_pairs={{2,0},{4,2},{6,4},{7,6},{5,7},{3,5},{1,3},{0,1},{10,8},{12,10},{14... | collective-permute-start | bytes 393224 | tf_op jit(solution)/shard_map/ppermute | solution.py:229
  75.5 5.0 %collective-permute-start.30 = (bf16[64,1024]{1,0:T(8,128)(2,1)S(1)}, bf16[64,1024]{1,0:T(8,128)(2,1)S(1)}, u32[]{:S(2)}, u32[]{:S(2)}) collective-permute-start(bf16[64,1024]{1,0:T(8,128)(2,1)S(1)} %add_convert_fusion.3), channel_id=1, source_target_pairs={{0,2},{2,4},{4,6},{6,7},{7,5},{5,3},{3,1},{1,0},{8,10},{10,12},{12... | collective-permute-start | bytes 393224 | tf_op jit(solution)/shard_map/ppermute | solution.py:226
  (28 other events, 95.0 us)

commit v4 on v2

v4 whole, which is shorter than its diff:
```python
import functools
import math

import jax
import jax.numpy as jnp
from jax import lax
from jax.experimental import pallas as pl
from jax.experimental.pallas import tpu as pltpu
from jax.sharding import PartitionSpec as P

BLOCK = 128
LANES = 128
FIELD_ROWS = 8
CHUNK = 256
VMEM_LIMIT = 40 * 1024 * 1024


def pack_kernel(feat_ref, short_ref, pos_ref, out_ref):
    rows, width = feat_ref.shape
    out_ref[:rows, :] = feat_ref[...]
    short = short_ref[...]
    places = pos_ref[...] // BLOCK
    offsets = pos_ref[...] % BLOCK
    targets = jnp.zeros_like(places)
    for j in range(short.shape[0]):
        targets = targets + jnp.where(places == j, short[j : j + 1, :], 0)
    fields = jnp.concatenate([short, targets, offsets], axis=0)
    groups = [
        fields[at : at + FIELD_ROWS] for at in range(0, fields.shape[0], FIELD_ROWS)
    ]
    groups.append(jnp.zeros((FIELD_ROWS, width - rows * len(groups)), jnp.int32))
    meta = jnp.concatenate(groups, axis=1)
    out_ref[rows:, :] = meta.astype(jnp.float32).astype(jnp.bfloat16)


def pack(features, shortlist, positives):
    rows, width = features.shape
    return pl.pallas_call(
        pack_kernel,
        out_shape=jax.ShapeDtypeStruct((rows + FIELD_ROWS, width), jnp.bfloat16),
        in_specs=[pl.BlockSpec(memory_space=pltpu.VMEM)] * 3,
        compiler_params=pltpu.CompilerParams(vmem_limit_bytes=VMEM_LIMIT),
        name="pack",
    )(features, shortlist.T, positives.T)


def block_kernel(piece_rows, top_count, pos_count, first_ref, size_ref, *refs):
    block_count = len(piece_rows)
    piece_count = sum(len(pieces) for pieces in piece_rows)
    x_refs = refs[:piece_count]
    w_ref = refs[piece_count]
    grad_refs = refs[piece_count + 1 : 2 * piece_count + 1]
    slope_refs = refs[2 * piece_count + 1 :]
    labels, width = w_ref.shape
    local_count = labels // BLOCK
    rows = slope_refs[0].shape[0]
    first = first_ref[0].astype(jnp.float32)

    lane = lax.broadcasted_iota(jnp.int32, (LANES, BLOCK), 1)
    row = lax.broadcasted_iota(jnp.int32, (LANES, BLOCK), 0)
    live_table = jnp.concatenate(
        [
            jnp.where((row == c) & (lane < size_ref[c]), 2.0, 0.0).astype(jnp.bfloat16)
            for c in range(local_count)
        ],
        axis=1,
    )

    named, pieces = [], []
    cluster = lax.broadcasted_iota(jnp.int32, (FIELD_ROWS, rows), 0).astype(jnp.float32) + first
    at = 0
    for b in range(block_count):
        block_refs = x_refs[at : at + len(piece_rows[b])]
        at += len(piece_rows[b])
        pieces += [ref[:count, :] for ref, count in zip(block_refs, piece_rows[b])]
        groups = -(-(top_count + 2 * pos_count) // FIELD_ROWS)
        meta = block_refs[0][piece_rows[b][0] :, : groups * rows].astype(jnp.float32)
        field = [
            meta[f % FIELD_ROWS : f % FIELD_ROWS + 1, f // FIELD_ROWS * rows : (f // FIELD_ROWS + 1) * rows]
            for f in range(top_count + 2 * pos_count)
        ]
        member = jnp.zeros((FIELD_ROWS, rows), jnp.float32)
        for j in range(top_count):
            member = jnp.where(cluster == field[j], 1.0, member)
        target = [
            (field[top_count + q] - first) * BLOCK + field[top_count + pos_count + q]
            for q in range(pos_count)
        ]
        rest = jnp.zeros((LANES - FIELD_ROWS - pos_count, rows), jnp.float32)
        named.append(jnp.concatenate([member] + target + [rest], axis=0).T)

    x = jnp.concatenate(pieces, axis=0) if len(pieces) > 1 else pieces[0]
    named = jnp.concatenate(named, axis=0) if block_count > 1 else named[0]
    target = [named[:, FIELD_ROWS + q : FIELD_ROWS + q + 1] for q in range(pos_count)]
    member = jnp.where(
        lax.broadcasted_iota(jnp.int32, named.shape, 1) < FIELD_ROWS, named, 0.0
    ).astype(jnp.bfloat16)
    for start in range(0, labels, CHUNK):
        logits = lax.dot_general(
            x,
            w_ref[start : start + CHUNK, :],
            (((1,), (1,)), ((), ())),
            preferred_element_type=jnp.float32,
        )
        live = jnp.dot(
            member, live_table[:, start : start + CHUNK], preferred_element_type=jnp.float32
        )
        label = (
            lax.broadcasted_iota(jnp.int32, (1, CHUNK), 1) + start
        ).astype(jnp.float32)
        positive = target[0] == label
        for q in range(1, pos_count):
            positive = positive | (target[q] == label)
        turned = jnp.where(positive, -1.0, 1.0)
        slope = (turned * live * jnp.maximum(1.0 + turned * logits, 0.0)).astype(jnp.bfloat16)
        for b, ref in enumerate(slope_refs):
            ref[:, start : start + CHUNK] = slope[b * rows : (b + 1) * rows]
    slope = [ref[...] for ref in slope_refs]
    slope = jnp.concatenate(slope, axis=0) if block_count > 1 else slope[0]
    for start in range(0, width, CHUNK):
        part = jnp.dot(
            slope, w_ref[:, start : start + CHUNK], preferred_element_type=jnp.float32
        ).astype(jnp.bfloat16)
        at = 0
        for ref in grad_refs:
            ref[:, start : start + CHUNK] = part[at : at + ref.shape[0]]
            at += ref.shape[0]


def block_work(blocks, weights, first, sizes, top_count, pos_count):
    labels, width = weights.shape
    piece_rows = [
        [piece.shape[0] - (FIELD_ROWS if p == 0 else 0) for p, piece in enumerate(pieces)]
        for pieces in blocks
    ]
    flat_rows = sum(piece_rows, [])
    out = pl.pallas_call(
        functools.partial(block_kernel, piece_rows, top_count, pos_count),
        out_shape=[jax.ShapeDtypeStruct((rows, width), jnp.bfloat16) for rows in flat_rows]
        + [jax.ShapeDtypeStruct((sum(rows), labels), jnp.bfloat16) for rows in piece_rows],
        in_specs=[pl.BlockSpec(memory_space=pltpu.SMEM)] * 2
        + [pl.BlockSpec(memory_space=pltpu.VMEM)] * (len(flat_rows) + 1),
        compiler_params=pltpu.CompilerParams(vmem_limit_bytes=VMEM_LIMIT),
        cost_estimate=pl.CostEstimate(
            flops=4 * sum(flat_rows) * labels * width,
            bytes_accessed=2 * labels * width + 6 * sum(flat_rows) * width,
            transcendentals=0,
        ),
        name="block_work",
    )(first, sizes, *[piece for pieces in blocks for piece in pieces], weights)
    return list(out[: len(flat_rows)]), list(out[len(flat_rows) :])


def weight_kernel(piece_rows, column_blocks, scale, own_ref, *refs):
    piece_count = len(piece_rows)
    out_refs = refs[len(refs) - len(column_blocks) :]
    x_refs, s_refs = refs[:piece_count], refs[piece_count : len(refs) - len(column_blocks)]
    part_width = out_refs[0].shape[1]
    slopes = jnp.concatenate([ref[...] for ref in s_refs], axis=0)
    for ref, q in zip(out_refs, column_blocks):
        at = pl.multiple_of((own_ref[0] ^ q) * part_width, part_width)
        x = jnp.concatenate(
            [r[:rows, pl.ds(at, part_width)] for r, rows in zip(x_refs, piece_rows)], axis=0
        )
        part = lax.dot_general(
            slopes, x, (((0,), (0,)), ((), ())), preferred_element_type=jnp.float32
        )
        ref[...] = (part * scale).astype(jnp.bfloat16)


def weight_work(blocks, slopes, own, column_blocks, part_width, scale):
    pieces = [piece for block in blocks for piece in block]
    piece_rows = [
        piece.shape[0] - (FIELD_ROWS if p == 0 else 0)
        for block in blocks
        for p, piece in enumerate(block)
    ]
    labels = slopes[0].shape[1]
    rows = sum(piece_rows)
    return pl.pallas_call(
        functools.partial(weight_kernel, piece_rows, column_blocks, scale),
        out_shape=[jax.ShapeDtypeStruct((labels, part_width), jnp.bfloat16)] * len(column_blocks),
        in_specs=[pl.BlockSpec(memory_space=pltpu.SMEM)]
        + [pl.BlockSpec(memory_space=pltpu.VMEM)] * (len(pieces) + len(slopes)),
        compiler_params=pltpu.CompilerParams(vmem_limit_bytes=VMEM_LIMIT),
        cost_estimate=pl.CostEstimate(
            flops=2 * rows * labels * part_width * len(column_blocks),
            bytes_accessed=2 * rows * (labels + 1024) + 2 * labels * part_width,
            transcendentals=0,
        ),
        name="weight_work",
    )(own, *pieces, *slopes)


def add(*parts):
    total = parts[0].astype(jnp.float32)
    for part in parts[1:]:
        total = total + part.astype(jnp.float32)
    return total.astype(jnp.bfloat16)


def after(array, *others):
    return lax.optimization_barrier((array, *others))[0]


def local(features, shortlist, positives, cluster_sizes, weights):
    inst_rows, width = features.shape
    top_count, pos_count = shortlist.shape[1], positives.shape[1]
    clus_count, seq_count = lax.axis_size("clus"), lax.axis_size("seq")
    local_count = cluster_sizes.shape[0]
    part_width = width // seq_count
    half, steps = inst_rows // 2, clus_count // 2

    ring = list(range(0, clus_count, 2)) + list(range(1, clus_count, 2))[::-1]
    onward = []
    for s in range(seq_count):
        places = [s * clus_count + c for c in (ring if s % 2 == 0 else ring[::-1])]
        onward += list(zip(places, places[1:] + places[:1]))
    back = [(b, a) for a, b in onward]

    def send(array, pairs):
        return lax.ppermute(array, ("seq", "clus"), pairs)

    first = (lax.axis_index("clus") * local_count).astype(jnp.int32).reshape(1)
    used, slopes = [], []

    def take(*blocks):
        grads, found = block_work(blocks, weights, first, cluster_sizes, top_count, pos_count)
        used.extend(blocks)
        slopes.extend(found)
        return grads

    own = pack(features, shortlist, positives)
    behind_x, front_x = own, own
    parts = {}
    for k in range(1, steps + 1):
        if k > 1:
            behind_x, front_x = after(behind_x, parts[k - 2][0]), after(front_x, parts[k - 2][0])
        if k < steps:
            going = behind_x, front_x
        else:
            going = (
                jnp.concatenate([behind_x[:half], behind_x[inst_rows:]], axis=0),
                front_x[half:inst_rows],
            )
        arriving = send(going[0], onward), send(going[1], back)
        parts[k - 1] = take([own]) if k == 1 else take([behind_x], [front_x])
        behind_x, front_x = arriving
    to_back, to_front = take([after(behind_x, parts[steps - 1][0]), front_x])

    scale = 1.0 / math.sqrt(inst_rows * seq_count * top_count // local_count)
    own_seq = lax.axis_index("seq").astype(jnp.int32).reshape(1)

    def seq_send(array, bit):
        return lax.ppermute(array, "seq", [(k, k ^ bit) for k in range(seq_count)])

    far, near = list(range(seq_count // 2, seq_count)), list(range(seq_count // 2))
    terms = dict(zip(far, weight_work(used, slopes, own_seq, far, part_width, scale)))
    terms.update(zip(near, weight_work(used, slopes, own_seq, near, part_width, scale)))
    terms = {q: [term] for q, term in terms.items()}
    bit = 1
    while bit < seq_count:
        for q in [q for q in sorted(terms, reverse=True) if q & bit]:
            values = terms.pop(q)
            terms[q ^ bit].append(seq_send(add(*values) if len(values) > 1 else values[0], bit))
        bit *= 2
    weight_grad = add(*terms[0])

    for k in range(steps, 0, -1):
        from_front, from_behind = send(to_back, back), send(to_front, onward)
        if k == steps:
            near_behind, near_front = parts[k - 1]
            to_back = jnp.concatenate([add(near_behind[:half], from_front), near_behind[half:]], axis=0)
            to_front = jnp.concatenate([near_front[:half], add(near_front[half:], from_behind)], axis=0)
        elif k > 1:
            near_behind, near_front = parts[k - 1]
            to_back, to_front = add(near_behind, from_front), add(near_front, from_behind)
    feature_grad = add(after(parts[0][0], weight_grad), from_front, from_behind)
    return (feature_grad, weight_grad)


def solution(mesh):
    return jax.shard_map(
        local,
        mesh=mesh,
        in_specs=(
            P(("seq", "clus"), None),
            P(("seq", "clus"), None),
            P(("seq", "clus"), None),
            P("clus"),
            P("clus", None),
        ),
        out_specs=(P(("seq", "clus"), None), P("clus", "seq")),
        check_vma=False,
    )
```

time: 86.1 us -> 72.7 us (0.84)
  starting transfers between devices: 32.3 us -> 19.6 us
  waiting for transfers between devices: 20.2 us -> 26.1 us
  Pallas kernels: 17 us -> 12.9 us
  local copies, waits for them, and re-layouts: 11.1 us -> 9.56 us
  other arithmetic: 4.16 us -> 3.05 us
    ppermute x28 -> x16, starting transfers between devices: 30.3 us -> 16.6 us  [send(): return lax.ppermute(array, ('seq', 'clus'), pairs)]
    ppermute x28 -> x16, waiting for transfers between devices: 16.9 us -> 24.4 us  [send(): return lax.ppermute(array, ('seq', 'clus'), pairs)]
    pallas_call x7 -> x8, Pallas kernels: 17 us -> 12.9 us  [the longest x5 10.2 us: block_work(): pl.pallas_call(functools.partial(block_kernel, piece_rows, top_count, pos...]
    unnamed x56 -> x66, local copies, waits for them, and re-layouts: 11.1 us -> 8.86 us
    ppermute x3, waiting for transfers between devices: 3.33 us -> 1.69 us  [seq_send(): return lax.ppermute(array, 'seq', [(k, k ^ bit) for k in range(seq_count)])]
    ppermute x3, starting transfers between devices: 1.97 us -> 3.07 us  [seq_send(): return lax.ppermute(array, 'seq', [(k, k ^ bit) for k in range(seq_count)])]
    convert_element_type x14 -> x9, other arithmetic: 3.44 us -> 2.34 us  [add(): return total.astype(jnp.bfloat16)]
  transfers between devices with their start and end apart: 31 -> 19, of which waited for: 8 -> 11; matrix products, arithmetic and copies ran while one was open for 4% -> 4% of each run, Pallas kernels for 17% -> 15%
where the time goes in v4:
time: 72.7 us; the launch traced here: 72.2 us
  waiting for transfers between devices  26.1 us (36%)
  starting transfers between devices  19.6 us (27%)
  Pallas kernels  12.9 us (18%)
  local copies, waits for them, and re-layouts  9.56 us (13%)
  other arithmetic  3.05 us (4%)
  between operations  1.01 us (1%)
    ppermute x16, waiting for transfers between devices, send(): return lax.ppermute(array, ('seq', 'clus'), pairs)  24.4 us
    ppermute x16, starting transfers between devices, send(): return lax.ppermute(array, ('seq', 'clus'), pairs)  16.6 us
    pallas_call x5, Pallas kernels, block_work(): pl.pallas_call(functools.partial(block_kernel, piece_rows, top_count, pos...  10.2 us
    unnamed x66, local copies, waits for them, and re-layouts  8.86 us
    ppermute x3, starting transfers between devices, seq_send(): return lax.ppermute(array, 'seq', [(k, k ^ bit) for k in range(seq_count)])  3.07 us
    pallas_call x2, Pallas kernels, weight_work(): pl.pallas_call(functools.partial(weight_kernel, piece_rows, column_blocks...  2.63 us
    convert_element_type x9, other arithmetic, add(): return total.astype(jnp.bfloat16)  2.34 us
    ppermute x3, waiting for transfers between devices, seq_send(): return lax.ppermute(array, 'seq', [(k, k ^ bit) for k in range(seq_count)])  1.69 us
  transfers between devices with their start and end apart: 19, of which 11 were waited for; matrix products, arithmetic and copies ran while one was open for 4% of the time, Pallas kernels for 15%

profile of v4, /device:TPU:0, one launch (start us, length us, event | category | flops | bytes accessed | tf_op | source)
XLA Modules:
  0.0 72.2 jit_solution(7781079614244065893)
XLA Ops:
  0.7 0.9 %copy-done.26 = bf16[128,1024]{1,0:T(8,128)(2,1)S(1)} copy-done((bf16[128,1024]{1,0:T(8,128)(2,1)S(1)}, bf16[128,1024]{1,0:T(8,128)(2,1)}, u32[]{:S(2)}) %copy-start.26) | copy-done | bytes 262168
  3.0 3.1 %collective-permute-start = (bf16[136,1024]{1,0:T(8,128)(2,1)S(1)}, bf16[136,1024]{1,0:T(8,128)(2,1)S(1)}, u32[]{:S(2)}, u32[]{:S(2)}) collective-permute-start(bf16[136,1024]{1,0:T(8,128)(2,1)S(1)} %pack.1.refs_0_), channel_id=1, source_target_pairs={{0,2},{2,4},{4,6},{6,7},{7,5},{5,3},{3,1},{1,0},{9,11},{11,13},{13... | collective-permute-start | bytes 835592 | tf_op jit(solution)/shard_map/ppermute | solution.py:222
  6.1 1.6 %copy-done = bf16[1024,1024]{1,0:T(8,128)(2,1)S(1)} copy-done((bf16[1024,1024]{1,0:T(8,128)(2,1)S(1)}, bf16[1024,1024]{1,0:T(8,128)(2,1)}, u32[]{:S(2)}) %copy-start) | copy-done | bytes 2097176
  8.4 1.8 %block_work.5 = (bf16[128,1024]{1,0:T(8,128)(2,1)S(1)}, bf16[128,1024]{1,0:T(8,128)(2,1)S(1)}) custom-call(s32[1]{0:T(128)} %bitcast.first_ref, s32[8]{0:T(128)S(1)} %copy-done.31, bf16[136,1024]{1,0:T(8,128)(2,1)S(1)} %pack.1.refs_0_, bf16[1024,1024]{1,0:T(8,128)(2,1)S(1)} %copy-done), custom_call_target="tpu_custom_call" | custom-call | flops 536870912 | bytes 2883584 | tf_op jit(solution)/shard_map/block_work/pallas_call | solution.py:137
  10.8 0.7 copy-done.27
  11.5 1.5 %collective-permute-done.refs_0_.refs_1_ = bf16[136,1024]{1,0:T(8,128)(2,1)S(1)} collective-permute-done((bf16[136,1024]{1,0:T(8,128)(2,1)S(1)}, bf16[136,1024]{1,0:T(8,128)(2,1)S(1)}, u32[]{:S(2)}, u32[]{:S(2)}) %collective-permute-start) | collective-permute-done | bytes 278560 | tf_op jit(solution)/shard_map/ppermute | solution.py:222
  13.0 1.6 %collective-permute-start.2 = (bf16[136,1024]{1,0:T(8,128)(2,1)S(1)}, bf16[136,1024]{1,0:T(8,128)(2,1)S(1)}, u32[]{:S(2)}, u32[]{:S(2)}) collective-permute-start(bf16[136,1024]{1,0:T(8,128)(2,1)S(1)} %collective-permute-done.refs_0_.refs_1_), channel_id=1, source_target_pairs={{0,2},{2,4},{4,6},{6,7},{7,5},{5,3},{3,1},{1,0},{9,11},{11,13},{13... | collective-permute-start | bytes 835592 | tf_op jit(solution)/shard_map/ppermute | solution.py:222
  14.6 0.9 %collective-permute-start.3 = (bf16[136,1024]{1,0:T(8,128)(2,1)S(1)}, bf16[136,1024]{1,0:T(8,128)(2,1)S(1)}, u32[]{:S(2)}, u32[]{:S(2)}) collective-permute-start(bf16[136,1024]{1,0:T(8,128)(2,1)S(1)} %collective-permute-done.1.refs_1_.refs_2_), channel_id=1, source_target_pairs={{2,0},{4,2},{6,4},{7,6},{5,7},{3,5},{1,3},{0,1},{11,9},{13,11},{15... | collective-permute-start | bytes 835592 | tf_op jit(solution)/shard_map/ppermute | solution.py:222
  15.5 2.2 %block_work.6 = (bf16[128,1024]{1,0:T(8,128)(2,1)S(1)}, bf16[128,1024]{1,0:T(8,128)(2,1)S(1)}, bf16[128,1024]{1,0:T(8,128)(2,1)S(1)}, bf16[128,1024]{1,0:T(8,128)(2,1)S(1)}) custom-call(s32[1]{0:T(128)} %bitcast.first_ref, s32[8]{0:T(128)S(1)} %copy-done.32, bf16[136,1024]{1,0:T(8,128)(2,1)S(1)} %collective-permute-done.refs_0_.refs_1_, ...), custom_call_target="tpu_custom_call" | custom-call | flops 1073741824 | bytes 3670016 | tf_op jit(solution)/shard_map/block_work/pallas_call | solution.py:137
  18.4 0.7 copy-done.12
  19.1 0.7 copy-done.18
  19.8 2.5 %collective-permute-done.2.refs_0_.refs_3_ = bf16[136,1024]{1,0:T(8,128)(2,1)S(1)} collective-permute-done((bf16[136,1024]{1,0:T(8,128)(2,1)S(1)}, bf16[136,1024]{1,0:T(8,128)(2,1)S(1)}, u32[]{:S(2)}, u32[]{:S(2)}) %collective-permute-start.2) | collective-permute-done | bytes 278560 | tf_op jit(solution)/shard_map/ppermute | solution.py:222
  22.4 2.1 %collective-permute-start.5 = (bf16[136,1024]{1,0:T(8,128)(2,1)S(1)}, bf16[136,1024]{1,0:T(8,128)(2,1)S(1)}, u32[]{:S(2)}, u32[]{:S(2)}) collective-permute-start(bf16[136,1024]{1,0:T(8,128)(2,1)S(1)} %collective-permute-done.3.refs_1_.refs_4_), channel_id=1, source_target_pairs={{2,0},{4,2},{6,4},{7,6},{5,7},{3,5},{1,3},{0,1},{11,9},{13,11},{15... | collective-permute-start | bytes 835592 | tf_op jit(solution)/shard_map/ppermute | solution.py:222
  24.4 2.2 %block_work.7 = (bf16[128,1024]{1,0:T(8,128)(2,1)S(1)}, bf16[128,1024]{1,0:T(8,128)(2,1)S(1)}, bf16[128,1024]{1,0:T(8,128)(2,1)S(1)}, bf16[128,1024]{1,0:T(8,128)(2,1)S(1)}) custom-call(s32[1]{0:T(128)} %bitcast.first_ref, s32[8]{0:T(128)S(1)} %copy-done.32, bf16[136,1024]{1,0:T(8,128)(2,1)S(1)} %collective-permute-done.2.refs_0_.refs_3_, ...), custom_call_target="tpu_custom_call" | custom-call | flops 1073741824 | bytes 3670016 | tf_op jit(solution)/shard_map/block_work/pallas_call | solution.py:137
  27.4 3.1 %collective-permute-done.4.refs_0_.refs_5_ = bf16[136,1024]{1,0:T(8,128)(2,1)S(1)} collective-permute-done((bf16[136,1024]{1,0:T(8,128)(2,1)S(1)}, bf16[136,1024]{1,0:T(8,128)(2,1)S(1)}, u32[]{:S(2)}, u32[]{:S(2)}) %collective-permute-start.4) | collective-permute-done | bytes 278560 | tf_op jit(solution)/shard_map/ppermute | solution.py:222
  32.2 1.7 %collective-permute-start.7 = (bf16[64,1024]{1,0:T(8,128)(2,1)}, bf16[64,1024]{1,0:T(8,128)(2,1)S(1)}, u32[]{:S(2)}, u32[]{:S(2)}) collective-permute-start(bf16[64,1024]{1,0:T(8,128)(2,1)} %slice.23), channel_id=1, source_target_pairs={{2,0},{4,2},{6,4},{7,6},{5,7},{3,5},{1,3},{0,1},{11,9},{13,11},{15... | collective-permute-start | bytes 393224 | tf_op jit(solution)/shard_map/ppermute | solution.py:222
  33.9 2.2 %block_work.8 = (bf16[128,1024]{1,0:T(8,128)(2,1)S(1)}, bf16[128,1024]{1,0:T(8,128)(2,1)S(1)}, bf16[128,1024]{1,0:T(8,128)(2,1)S(1)}, bf16[128,1024]{1,0:T(8,128)(2,1)S(1)}) custom-call(s32[1]{0:T(128)} %bitcast.first_ref, s32[8]{0:T(128)S(1)} %copy-done.32, bf16[136,1024]{1,0:T(8,128)(2,1)S(1)} %collective-permute-done.4.refs_0_.refs_5_, ...), custom_call_target="tpu_custom_call" | custom-call | flops 1073741824 | bytes 3670016 | tf_op jit(solution)/shard_map/block_work/pallas_call | solution.py:137
  36.6 0.8 %collective-permute-done.7.refs_1_.refs_8_ = bf16[64,1024]{1,0:T(8,128)(2,1)S(1)} collective-permute-done((bf16[64,1024]{1,0:T(8,128)(2,1)}, bf16[64,1024]{1,0:T(8,128)(2,1)S(1)}, u32[]{:S(2)}, u32[]{:S(2)}) %collective-permute-start.7) | collective-permute-done | bytes 131104 | tf_op jit(solution)/shard_map/ppermute | solution.py:222
  37.4 1.8 %block_work.9 = (bf16[64,1024]{1,0:T(8,128)(2,1)S(1)}, bf16[64,1024]{1,0:T(8,128)(2,1)S(1)}, bf16[128,1024]{1,0:T(8,128)(2,1)S(1)}) custom-call(s32[1]{0:T(128)} %bitcast.first_ref, s32[8]{0:T(128)S(1)} %copy-done.32, bf16[72,1024]{1,0:T(8,128)(2,1)S(1)} %collective-permute-done.6.refs_0_.refs_7_, ...), custom_call_target="tpu_custom_call" | custom-call | flops 536870912 | bytes 2883584 | tf_op jit(solution)/shard_map/block_work/pallas_call | solution.py:137
  39.6 1.6 %collective-permute-start.11 = (bf16[64,1024]{1,0:T(8,128)(2,1)S(1)}, bf16[64,1024]{1,0:T(8,128)(2,1)S(1)}, u32[]{:S(2)}, u32[]{:S(2)}) collective-permute-start(bf16[64,1024]{1,0:T(8,128)(2,1)S(1)} %get-tuple-element.55), channel_id=1, source_target_pairs={{2,0},{4,2},{6,4},{7,6},{5,7},{3,5},{1,3},{0,1},{11,9},{13,11},{15... | collective-permute-start | bytes 393224 | tf_op jit(solution)/shard_map/ppermute | solution.py:222
  41.3 1.3 %weight_work.3 = (bf16[1024,256]{1,0:T(8,128)(2,1)S(1)}, bf16[1024,256]{1,0:T(8,128)(2,1)S(1)}) custom-call(s32[1]{0:T(128)} %bitcast.3.own_ref, bf16[136,1024]{1,0:T(8,128)(2,1)S(1)} %pack.1.refs_0_, bf16[136,1024]{1,0:T(8,128)(2,1)S(1)} %collective-permute-done.refs_0_.refs_1_, bf16[136,1024]{1,0:T(8,128)(2,1)S(1)} %copy-done.3, ...), custom_call_target="tpu_custom_call" | custom-call | flops 1073741824 | bytes 4718592 | tf_op jit(solution)/shard_map/weight_work/pallas_call | solution.py:180
  42.7 1.3 %weight_work.2 = (bf16[1024,256]{1,0:T(8,128)(2,1)S(1)}, bf16[1024,256]{1,0:T(8,128)(2,1)S(1)}) custom-call(s32[1]{0:T(128)} %bitcast.3.own_ref, bf16[136,1024]{1,0:T(8,128)(2,1)S(1)} %pack.1.refs_0_, bf16[136,1024]{1,0:T(8,128)(2,1)S(1)} %collective-permute-done.refs_0_.refs_1_, bf16[136,1024]{1,0:T(8,128)(2,1)S(1)} %copy-done.3, ...), custom_call_target="tpu_custom_call" | custom-call | flops 1073741824 | bytes 4718592 | tf_op jit(solution)/shard_map/weight_work/pallas_call | solution.py:180
  45.2 1.6 %collective-permute-start.12 = (bf16[128,1024]{1,0:T(8,128)(2,1)S(1)}, bf16[128,1024]{1,0:T(8,128)(2,1)S(1)}, u32[]{:S(2)}, u32[]{:S(2)}) collective-permute-start(bf16[128,1024]{1,0:T(8,128)(2,1)S(1)} %pad_maximum_fusion), channel_id=1, source_target_pairs={{2,0},{4,2},{6,4},{7,6},{5,7},{3,5},{1,3},{0,1},{11,9},{13,11},{15... | collective-permute-start | bytes 786440 | tf_op jit(solution)/shard_map/ppermute | solution.py:222
  46.9 6.4 %collective-permute-done.16 = bf16[128,1024]{1,0:T(8,128)(2,1)S(1)} collective-permute-done((bf16[128,1024]{1,0:T(8,128)(2,1)S(1)}, bf16[128,1024]{1,0:T(8,128)(2,1)S(1)}, u32[]{:S(2)}, u32[]{:S(2)}) %collective-permute-start.16) | collective-permute-done | bytes 262176 | tf_op jit(solution)/shard_map/ppermute | solution.py:222
  54.2 2.4 %collective-permute-start.10 = (bf16[1024,256]{1,0:T(8,128)(2,1)S(1)}, bf16[1024,256]{1,0:T(8,128)(2,1)S(1)}, u32[]{:S(2)}, u32[]{:S(2)}) collective-permute-start(bf16[1024,256]{1,0:T(8,128)(2,1)S(1)} %add_convert_fusion.1), channel_id=1, source_target_pairs={{0,16},{8,24},{16,0},{24,8},{1,17},{9,25},{17,1},{25,9},{2,18},{10... | collective-permute-start | bytes 1572872 | tf_op jit(solution)/shard_map/ppermute | solution.py:255
  57.2 5.0 %collective-permute-done.17 = bf16[128,1024]{1,0:T(8,128)(2,1)S(1)} collective-permute-done((bf16[128,1024]{1,0:T(8,128)(2,1)S(1)}, bf16[128,1024]{1,0:T(8,128)(2,1)S(1)}, u32[]{:S(2)}, u32[]{:S(2)}) %collective-permute-start.17) | collective-permute-done | bytes 262176 | tf_op jit(solution)/shard_map/ppermute | solution.py:222
  62.4 0.9 %collective-permute-start.18 = (bf16[128,1024]{1,0:T(8,128)(2,1)S(1)}, bf16[128,1024]{1,0:T(8,128)(2,1)S(1)}, u32[]{:S(2)}, u32[]{:S(2)}) collective-permute-start(bf16[128,1024]{1,0:T(8,128)(2,1)S(1)} %add_convert_fusion.3), channel_id=1, source_target_pairs={{0,2},{2,4},{4,6},{6,7},{7,5},{5,3},{3,1},{1,0},{9,11},{11,13},{13... | collective-permute-start | bytes 786440 | tf_op jit(solution)/shard_map/ppermute | solution.py:222
  63.2 1.6 %collective-permute-done.13 = bf16[128,1024]{1,0:T(8,128)(2,1)S(1)} collective-permute-done((bf16[128,1024]{1,0:T(8,128)(2,1)S(1)}, bf16[128,1024]{1,0:T(8,128)(2,1)S(1)}, u32[]{:S(2)}, u32[]{:S(2)}) %collective-permute-start.13) | collective-permute-done | bytes 262176 | tf_op jit(solution)/shard_map/ppermute | solution.py:222
  65.6 1.7 %collective-permute-done.10 = bf16[1024,256]{1,0:T(8,128)(2,1)S(1)} collective-permute-done((bf16[1024,256]{1,0:T(8,128)(2,1)S(1)}, bf16[1024,256]{1,0:T(8,128)(2,1)S(1)}, u32[]{:S(2)}, u32[]{:S(2)}) %collective-permute-start.10) | collective-permute-done | bytes 524320 | tf_op jit(solution)/shard_map/ppermute | solution.py:255
  67.3 1.0 %add_convert_fusion = bf16[1024,256]{1,0:T(8,128)(2,1)} fusion(bf16[1024,256]{1,0:T(8,128)(2,1)S(1)} %collective-permute-done.10, bf16[1024,256]{1,0:T(8,128)(2,1)S(1)} %collective-permute-done.8, bf16[1024,256]{1,0:T(8,128)(2,1)S(1)} %get-tuple-element.50), kind=kLoop, calls=%fused_computation | loop fusion | flops 1572864 | bytes 2097152 | tf_op jit(solution)/shard_map/convert_element_type | solution.py:199
  68.3 2.7 %collective-permute-done.18 = bf16[128,1024]{1,0:T(8,128)(2,1)S(1)} collective-permute-done((bf16[128,1024]{1,0:T(8,128)(2,1)S(1)}, bf16[128,1024]{1,0:T(8,128)(2,1)S(1)}, u32[]{:S(2)}, u32[]{:S(2)}) %collective-permute-start.18) | collective-permute-done | bytes 262176 | tf_op jit(solution)/shard_map/ppermute | solution.py:222
  71.4 0.8 %add_convert_fusion.2 = bf16[128,1024]{1,0:T(8,128)(2,1)} fusion(bf16[128,1024]{1,0:T(8,128)(2,1)S(1)} %collective-permute-done.18, bf16[128,1024]{1,0:T(8,128)(2,1)S(1)} %collective-permute-done.14, bf16[128,1024]{1,0:T(8,128)(2,1)S(1)} %copy-done.28), kind=kLoop, calls=%fused_computation.2 | loop fusion | flops 786432 | bytes 1048576 | tf_op jit(solution)/shard_map/convert_element_type | solution.py:199
  (97 shorter events, 10.5 us)
Async XLA Ops:
  0.6 14.8 %copy-start.32 = (s32[8]{0:T(128)S(1)}, s32[8]{0:T(128)}, u32[]{:S(2)}) copy-start(s32[8]{0:T(128)} %size_ref.9) | copy-start | bytes 100
  3.0 10.0 %collective-permute-start = (bf16[136,1024]{1,0:T(8,128)(2,1)S(1)}, bf16[136,1024]{1,0:T(8,128)(2,1)S(1)}, u32[]{:S(2)}, u32[]{:S(2)}) collective-permute-start(bf16[136,1024]{1,0:T(8,128)(2,1)S(1)} %pack.1.refs_0_), channel_id=1, source_target_pairs={{0,2},{2,4},{4,6},{6,7},{7,5},{5,3},{3,1},{1,0},{9,11},{11,13},{13... | collective-permute-start | bytes 835592 | tf_op jit(solution)/shard_map/ppermute | solution.py:222
  6.1 8.5 %collective-permute-start.1 = (bf16[136,1024]{1,0:T(8,128)(2,1)S(1)}, bf16[136,1024]{1,0:T(8,128)(2,1)S(1)}, u32[]{:S(2)}, u32[]{:S(2)}) collective-permute-start(bf16[136,1024]{1,0:T(8,128)(2,1)S(1)} %pack.1.refs_0_), channel_id=1, source_target_pairs={{2,0},{4,2},{6,4},{7,6},{5,7},{3,5},{1,3},{0,1},{11,9},{13,11},{15... | collective-permute-start | bytes 835592 | tf_op jit(solution)/shard_map/ppermute | solution.py:222
  8.4 7.1 %copy-start.1 = (bf16[1024,1024]{1,0:T(8,128)(2,1)S(1)}, bf16[1024,1024]{1,0:T(8,128)(2,1)}, u32[]{:S(2)}) copy-start(bf16[1024,1024]{1,0:T(8,128)(2,1)} %refs_2_.7) | copy-start | bytes 6291460
  13.0 9.3 %collective-permute-start.2 = (bf16[136,1024]{1,0:T(8,128)(2,1)S(1)}, bf16[136,1024]{1,0:T(8,128)(2,1)S(1)}, u32[]{:S(2)}, u32[]{:S(2)}) collective-permute-start(bf16[136,1024]{1,0:T(8,128)(2,1)S(1)} %collective-permute-done.refs_0_.refs_1_), channel_id=1, source_target_pairs={{0,2},{2,4},{4,6},{6,7},{7,5},{5,3},{3,1},{1,0},{9,11},{11,13},{13... | collective-permute-start | bytes 835592 | tf_op jit(solution)/shard_map/ppermute | solution.py:222
  14.6 7.8 %copy-start.2 = (bf16[136,1024]{1,0:T(8,128)(2,1)}, bf16[136,1024]{1,0:T(8,128)(2,1)S(1)}, u32[]{:S(2)}) copy-start(bf16[136,1024]{1,0:T(8,128)(2,1)S(1)} %collective-permute-done.1.refs_1_.refs_2_) | copy-start | bytes 835588
  14.6 7.8 %collective-permute-start.3 = (bf16[136,1024]{1,0:T(8,128)(2,1)S(1)}, bf16[136,1024]{1,0:T(8,128)(2,1)S(1)}, u32[]{:S(2)}, u32[]{:S(2)}) collective-permute-start(bf16[136,1024]{1,0:T(8,128)(2,1)S(1)} %collective-permute-done.1.refs_1_.refs_2_), channel_id=1, source_target_pairs={{2,0},{4,2},{6,4},{7,6},{5,7},{3,5},{1,3},{0,1},{11,9},{13,11},{15... | collective-permute-start | bytes 835592 | tf_op jit(solution)/shard_map/ppermute | solution.py:222
  19.8 10.7 %copy-start.20 = (bf16[128,1024]{1,0:T(8,128)(2,1)}, bf16[128,1024]{1,0:T(8,128)(2,1)S(1)}, u32[]{:S(2)}) copy-start(bf16[128,1024]{1,0:T(8,128)(2,1)S(1)} %get-tuple-element.56) | copy-start | bytes 786436
  22.3 8.2 %copy-start.4 = (bf16[136,1024]{1,0:T(8,128)(2,1)}, bf16[136,1024]{1,0:T(8,128)(2,1)S(1)}, u32[]{:S(2)}) copy-start(bf16[136,1024]{1,0:T(8,128)(2,1)S(1)} %collective-permute-done.2.refs_0_.refs_3_) | copy-start | bytes 835588
  22.3 8.2 %collective-permute-start.4 = (bf16[136,1024]{1,0:T(8,128)(2,1)S(1)}, bf16[136,1024]{1,0:T(8,128)(2,1)S(1)}, u32[]{:S(2)}, u32[]{:S(2)}) collective-permute-start(bf16[136,1024]{1,0:T(8,128)(2,1)S(1)} %collective-permute-done.2.refs_0_.refs_3_), channel_id=1, source_target_pairs={{0,2},{2,4},{4,6},{6,7},{7,5},{5,3},{3,1},{1,0},{9,11},{11,13},{13... | collective-permute-start | bytes 835592 | tf_op jit(solution)/shard_map/ppermute | solution.py:222
  22.4 8.2 %copy-start.6 = (bf16[136,1024]{1,0:T(8,128)(2,1)}, bf16[136,1024]{1,0:T(8,128)(2,1)S(1)}, u32[]{:S(2)}) copy-start(bf16[136,1024]{1,0:T(8,128)(2,1)S(1)} %collective-permute-done.3.refs_1_.refs_4_) | copy-start | bytes 835588
  22.4 9.1 %collective-permute-start.5 = (bf16[136,1024]{1,0:T(8,128)(2,1)S(1)}, bf16[136,1024]{1,0:T(8,128)(2,1)S(1)}, u32[]{:S(2)}, u32[]{:S(2)}) collective-permute-start(bf16[136,1024]{1,0:T(8,128)(2,1)S(1)} %collective-permute-done.3.refs_1_.refs_4_), channel_id=1, source_target_pairs={{2,0},{4,2},{6,4},{7,6},{5,7},{3,5},{1,3},{0,1},{11,9},{13,11},{15... | collective-permute-start | bytes 835592 | tf_op jit(solution)/shard_map/ppermute | solution.py:222
  31.2 5.4 %collective-permute-start.6 = (bf16[72,1024]{1,0:T(8,128)(2,1)}, bf16[72,1024]{1,0:T(8,128)(2,1)S(1)}, u32[]{:S(2)}, u32[]{:S(2)}) collective-permute-start(bf16[72,1024]{1,0:T(8,128)(2,1)} %pad_maximum_fusion.2), channel_id=1, source_target_pairs={{0,2},{2,4},{4,6},{6,7},{7,5},{5,3},{3,1},{1,0},{9,11},{11,13},{13... | collective-permute-start | bytes 442376 | tf_op jit(solution)/shard_map/ppermute | solution.py:222
  32.2 5.2 %collective-permute-start.7 = (bf16[64,1024]{1,0:T(8,128)(2,1)}, bf16[64,1024]{1,0:T(8,128)(2,1)S(1)}, u32[]{:S(2)}, u32[]{:S(2)}) collective-permute-start(bf16[64,1024]{1,0:T(8,128)(2,1)} %slice.23), channel_id=1, source_target_pairs={{2,0},{4,2},{6,4},{7,6},{5,7},{3,5},{1,3},{0,1},{11,9},{13,11},{15... | collective-permute-start | bytes 393224 | tf_op jit(solution)/shard_map/ppermute | solution.py:222
  36.1 5.1 %copy-start.3 = (bf16[136,1024]{1,0:T(8,128)(2,1)S(1)}, bf16[136,1024]{1,0:T(8,128)(2,1)}, u32[]{:S(2)}) copy-start(bf16[136,1024]{1,0:T(8,128)(2,1)} %copy-done.2) | copy-start | bytes 835588
  36.2 5.1 %copy-start.5 = (bf16[136,1024]{1,0:T(8,128)(2,1)S(1)}, bf16[136,1024]{1,0:T(8,128)(2,1)}, u32[]{:S(2)}) copy-start(bf16[136,1024]{1,0:T(8,128)(2,1)} %copy-done.4) | copy-start | bytes 835588
  39.1 5.4 %collective-permute-start.15 = (bf16[64,1024]{1,0:T(8,128)(2,1)S(1)}, bf16[64,1024]{1,0:T(8,128)(2,1)S(1)}, u32[]{:S(2)}, u32[]{:S(2)}) collective-permute-start(bf16[64,1024]{1,0:T(8,128)(2,1)S(1)} %get-tuple-element.59), channel_id=1, source_target_pairs={{0,2},{2,4},{4,6},{6,7},{7,5},{5,3},{3,1},{1,0},{9,11},{11,13},{13... | collective-permute-start | bytes 393224 | tf_op jit(solution)/shard_map/ppermute | solution.py:222
  39.6 5.5 %collective-permute-start.11 = (bf16[64,1024]{1,0:T(8,128)(2,1)S(1)}, bf16[64,1024]{1,0:T(8,128)(2,1)S(1)}, u32[]{:S(2)}, u32[]{:S(2)}) collective-permute-start(bf16[64,1024]{1,0:T(8,128)(2,1)S(1)} %get-tuple-element.55), channel_id=1, source_target_pairs={{2,0},{4,2},{6,4},{7,6},{5,7},{3,5},{1,3},{0,1},{11,9},{13,11},{15... | collective-permute-start | bytes 393224 | tf_op jit(solution)/shard_map/ppermute | solution.py:222
  42.6 10.7 %copy-start.25 = (bf16[128,1024]{1,0:T(8,128)(2,1)S(1)}, bf16[128,1024]{1,0:T(8,128)(2,1)}, u32[]{:S(2)}) copy-start(bf16[128,1024]{1,0:T(8,128)(2,1)} %copy-done.24) | copy-start | bytes 786436
  42.6 11.4 %collective-permute-start.9 = (bf16[1024,256]{1,0:T(8,128)(2,1)S(1)}, bf16[1024,256]{1,0:T(8,128)(2,1)S(1)}, u32[]{:S(2)}, u32[]{:S(2)}) collective-permute-start(bf16[1024,256]{1,0:T(8,128)(2,1)S(1)} %get-tuple-element.53), channel_id=1, source_target_pairs={{0,8},{8,0},{16,24},{24,16},{1,9},{9,1},{17,25},{25,17},{2,10},{10... | collective-permute-start | bytes 1572872 | tf_op jit(solution)/shard_map/ppermute | solution.py:255
  44.0 12.6 %copy-start.23 = (bf16[128,1024]{1,0:T(8,128)(2,1)S(1)}, bf16[128,1024]{1,0:T(8,128)(2,1)}, u32[]{:S(2)}) copy-start(bf16[128,1024]{1,0:T(8,128)(2,1)} %copy-done.22) | copy-start | bytes 786436
  44.0 21.6 %collective-permute-start.8 = (bf16[1024,256]{1,0:T(8,128)(2,1)S(1)}, bf16[1024,256]{1,0:T(8,128)(2,1)S(1)}, u32[]{:S(2)}, u32[]{:S(2)}) collective-permute-start(bf16[1024,256]{1,0:T(8,128)(2,1)S(1)} %get-tuple-element.51), channel_id=1, source_target_pairs={{0,8},{8,0},{16,24},{24,16},{1,9},{9,1},{17,25},{25,17},{2,10},{10... | collective-permute-start | bytes 1572872 | tf_op jit(solution)/shard_map/ppermute | solution.py:255
  44.6 17.7 %copy-start.21 = (bf16[128,1024]{1,0:T(8,128)(2,1)S(1)}, bf16[128,1024]{1,0:T(8,128)(2,1)}, u32[]{:S(2)}) copy-start(bf16[128,1024]{1,0:T(8,128)(2,1)} %copy-done.20) | copy-start | bytes 786436
  44.6 8.6 %collective-permute-start.16 = (bf16[128,1024]{1,0:T(8,128)(2,1)S(1)}, bf16[128,1024]{1,0:T(8,128)(2,1)S(1)}, u32[]{:S(2)}, u32[]{:S(2)}) collective-permute-start(bf16[128,1024]{1,0:T(8,128)(2,1)S(1)} %pad_maximum_fusion.1), channel_id=1, source_target_pairs={{0,2},{2,4},{4,6},{6,7},{7,5},{5,3},{3,1},{1,0},{9,11},{11,13},{13... | collective-permute-start | bytes 786440 | tf_op jit(solution)/shard_map/ppermute | solution.py:222
  45.2 19.7 %copy-start.19 = (bf16[128,1024]{1,0:T(8,128)(2,1)S(1)}, bf16[128,1024]{1,0:T(8,128)(2,1)}, u32[]{:S(2)}) copy-start(bf16[128,1024]{1,0:T(8,128)(2,1)} %copy-done.18) | copy-start | bytes 786436
  45.2 11.4 %collective-permute-start.12 = (bf16[128,1024]{1,0:T(8,128)(2,1)S(1)}, bf16[128,1024]{1,0:T(8,128)(2,1)S(1)}, u32[]{:S(2)}, u32[]{:S(2)}) collective-permute-start(bf16[128,1024]{1,0:T(8,128)(2,1)S(1)} %pad_maximum_fusion), channel_id=1, source_target_pairs={{2,0},{4,2},{6,4},{7,6},{5,7},{3,5},{1,3},{0,1},{11,9},{13,11},{15... | collective-permute-start | bytes 786440 | tf_op jit(solution)/shard_map/ppermute | solution.py:222
  53.3 8.9 %collective-permute-start.17 = (bf16[128,1024]{1,0:T(8,128)(2,1)S(1)}, bf16[128,1024]{1,0:T(8,128)(2,1)S(1)}, u32[]{:S(2)}, u32[]{:S(2)}) collective-permute-start(bf16[128,1024]{1,0:T(8,128)(2,1)S(1)} %add_convert_fusion.4), channel_id=1, source_target_pairs={{0,2},{2,4},{4,6},{6,7},{7,5},{5,3},{3,1},{1,0},{9,11},{11,13},{13... | collective-permute-start | bytes 786440 | tf_op jit(solution)/shard_map/ppermute | solution.py:222
  54.2 17.2 %copy-start.28 = (bf16[128,1024]{1,0:T(8,128)(2,1)S(1)}, bf16[128,1024]{1,0:T(8,128)(2,1)}, u32[]{:S(2)}) copy-start(bf16[128,1024]{1,0:T(8,128)(2,1)} %copy-done.27) | copy-start | bytes 786436
  54.2 13.1 %collective-permute-start.10 = (bf16[1024,256]{1,0:T(8,128)(2,1)S(1)}, bf16[1024,256]{1,0:T(8,128)(2,1)S(1)}, u32[]{:S(2)}, u32[]{:S(2)}) collective-permute-start(bf16[1024,256]{1,0:T(8,128)(2,1)S(1)} %add_convert_fusion.1), channel_id=1, source_target_pairs={{0,16},{8,24},{16,0},{24,8},{1,17},{9,25},{17,1},{25,9},{2,18},{10... | collective-permute-start | bytes 1572872 | tf_op jit(solution)/shard_map/ppermute | solution.py:255
  56.7 8.2 %collective-permute-start.13 = (bf16[128,1024]{1,0:T(8,128)(2,1)S(1)}, bf16[128,1024]{1,0:T(8,128)(2,1)S(1)}, u32[]{:S(2)}, u32[]{:S(2)}) collective-permute-start(bf16[128,1024]{1,0:T(8,128)(2,1)S(1)} %add_convert_fusion.6), channel_id=1, source_target_pairs={{2,0},{4,2},{6,4},{7,6},{5,7},{3,5},{1,3},{0,1},{11,9},{13,11},{15... | collective-permute-start | bytes 786440 | tf_op jit(solution)/shard_map/ppermute | solution.py:222
  62.4 8.7 %collective-permute-start.18 = (bf16[128,1024]{1,0:T(8,128)(2,1)S(1)}, bf16[128,1024]{1,0:T(8,128)(2,1)S(1)}, u32[]{:S(2)}, u32[]{:S(2)}) collective-permute-start(bf16[128,1024]{1,0:T(8,128)(2,1)S(1)} %add_convert_fusion.3), channel_id=1, source_target_pairs={{0,2},{2,4},{4,6},{6,7},{7,5},{5,3},{3,1},{1,0},{9,11},{11,13},{13... | collective-permute-start | bytes 786440 | tf_op jit(solution)/shard_map/ppermute | solution.py:222
  65.0 6.4 %collective-permute-start.14 = (bf16[128,1024]{1,0:T(8,128)(2,1)S(1)}, bf16[128,1024]{1,0:T(8,128)(2,1)S(1)}, u32[]{:S(2)}, u32[]{:S(2)}) collective-permute-start(bf16[128,1024]{1,0:T(8,128)(2,1)S(1)} %add_convert_fusion.5), channel_id=1, source_target_pairs={{2,0},{4,2},{6,4},{7,6},{5,7},{3,5},{1,3},{0,1},{11,9},{13,11},{15... | collective-permute-start | bytes 786440 | tf_op jit(solution)/shard_map/ppermute | solution.py:222
  (20 other events, 52.9 us)

commit v5 on v4

--- a/solution.py
+++ b/solution.py
@@ -13,11 +13,21 @@
 FIELD_ROWS = 8
 CHUNK = 256
 VMEM_LIMIT = 40 * 1024 * 1024
-
-
-def pack_kernel(feat_ref, short_ref, pos_ref, out_ref):
+WHOLE_VMEM = 60 * 1024 * 1024
+
+
+def pack_kernel(feat_ref, short_in, pos_in, out_ref, short_ref, pos_ref, meta_ref, sems):
     rows, width = feat_ref.shape
-    out_ref[:rows, :] = feat_ref[...]
+    copies = [
+        pltpu.make_async_copy(short_in, short_ref, sems.at[0]),
+        pltpu.make_async_copy(pos_in, pos_ref, sems.at[1]),
+        pltpu.make_async_copy(feat_ref, out_ref.at[pl.ds(0, rows)], sems.at[2]),
+        pltpu.make_async_copy(meta_ref, out_ref.at[pl.ds(rows, FIELD_ROWS)], sems.at[3]),
+    ]
+    for copy in copies[:3]:
+        copy.start()
+    copies[0].wait()
+    copies[1].wait()
     short = short_ref[...]
     places = pos_ref[...] // BLOCK
     offsets = pos_ref[...] % BLOCK
@@ -30,7 +40,10 @@
     ]
     groups.append(jnp.zeros((FIELD_ROWS, width - rows * len(groups)), jnp.int32))
     meta = jnp.concatenate(groups, axis=1)
-    out_ref[rows:, :] = meta.astype(jnp.float32).astype(jnp.bfloat16)
+    meta_ref[...] = meta.astype(jnp.float32).astype(jnp.bfloat16)
+    copies[3].start()
+    copies[2].wait()
+    copies[3].wait()
 
 
 def pack(features, shortlist, positives):
@@ -38,33 +51,49 @@
     return pl.pallas_call(
         pack_kernel,
         out_shape=jax.ShapeDtypeStruct((rows + FIELD_ROWS, width), jnp.bfloat16),
-        in_specs=[pl.BlockSpec(memory_space=pltpu.VMEM)] * 3,
-        compiler_params=pltpu.CompilerParams(vmem_limit_bytes=VMEM_LIMIT),
+        in_specs=[pl.BlockSpec(memory_space=pl.ANY)] * 3,
+        out_specs=pl.BlockSpec(memory_space=pl.ANY),
+        scratch_shapes=[
+            pltpu.VMEM(shortlist.shape[::-1], jnp.int32),
+            pltpu.VMEM(positives.shape[::-1], jnp.int32),
+            pltpu.VMEM((FIELD_ROWS, width), jnp.bfloat16),
+            pltpu.SemaphoreType.DMA((4,)),
+        ],
+        compiler_params=pltpu.CompilerParams(vmem_limit_bytes=WHOLE_VMEM),
         name="pack",
     )(features, shortlist.T, positives.T)
 
 
-def block_kernel(piece_rows, top_count, pos_count, first_ref, size_ref, *refs):
+def live_kernel(size_ref, x_ref, w_ref, live_ref):
+    lane = lax.broadcasted_iota(jnp.int32, (LANES, BLOCK), 1)
+    row = lax.broadcasted_iota(jnp.int32, (LANES, BLOCK), 0)
+    for c in range(size_ref.shape[0]):
+        live = jnp.where((row == c) & (lane < size_ref[c]), 2.0, 0.0)
+        live_ref[:, c * BLOCK : (c + 1) * BLOCK] = live.astype(jnp.bfloat16)
+
+
+def live_labels(cluster_sizes, block, weights):
+    return pl.pallas_call(
+        live_kernel,
+        out_shape=jax.ShapeDtypeStruct((LANES, cluster_sizes.shape[0] * BLOCK), jnp.bfloat16),
+        in_specs=[pl.BlockSpec(memory_space=pltpu.SMEM)]
+        + [pl.BlockSpec(memory_space=pltpu.VMEM)] * 2,
+        compiler_params=pltpu.CompilerParams(vmem_limit_bytes=VMEM_LIMIT),
+        name="live_labels",
+    )(cluster_sizes, block, weights)
+
+
+def block_kernel(piece_rows, top_count, pos_count, *refs):
     block_count = len(piece_rows)
     piece_count = sum(len(pieces) for pieces in piece_rows)
     x_refs = refs[:piece_count]
-    w_ref = refs[piece_count]
-    grad_refs = refs[piece_count + 1 : 2 * piece_count + 1]
-    slope_refs = refs[2 * piece_count + 1 :]
+    w_ref, live_ref = refs[piece_count : piece_count + 2]
+    grad_refs = refs[piece_count + 2 : 2 * piece_count + 2]
+    slope_refs = refs[2 * piece_count + 2 :]
     labels, width = w_ref.shape
     local_count = labels // BLOCK
     rows = slope_refs[0].shape[0]
-    first = first_ref[0].astype(jnp.float32)
-
-    lane = lax.broadcasted_iota(jnp.int32, (LANES, BLOCK), 1)
-    row = lax.broadcasted_iota(jnp.int32, (LANES, BLOCK), 0)
-    live_table = jnp.concatenate(
-        [
-            jnp.where((row == c) & (lane < size_ref[c]), 2.0, 0.0).astype(jnp.bfloat16)
-            for c in range(local_count)
-        ],
-        axis=1,
-    )
+    first = (lax.axis_index("clus") * local_count).astype(jnp.float32)
 
     named, pieces = [], []
     cluster = lax.broadcasted_iota(jnp.int32, (FIELD_ROWS, rows), 0).astype(jnp.float32) + first
@@ -103,7 +132,7 @@
             preferred_element_type=jnp.float32,
         )
         live = jnp.dot(
-            member, live_table[:, start : start + CHUNK], preferred_element_type=jnp.float32
+            member, live_ref[:, start : start + CHUNK], preferred_element_type=jnp.float32
         )
         label = (
             lax.broadcasted_iota(jnp.int32, (1, CHUNK), 1) + start
@@ -127,7 +156,7 @@
             at += ref.shape[0]
 
 
-def block_work(blocks, weights, first, sizes, top_count, pos_count):
+def block_work(blocks, weights, live_table, top_count, pos_count):
     labels, width = weights.shape
     piece_rows = [
         [piece.shape[0] - (FIELD_ROWS if p == 0 else 0) for p, piece in enumerate(pieces)]
@@ -138,8 +167,7 @@
         functools.partial(block_kernel, piece_rows, top_count, pos_count),
         out_shape=[jax.ShapeDtypeStruct((rows, width), jnp.bfloat16) for rows in flat_rows]
         + [jax.ShapeDtypeStruct((sum(rows), labels), jnp.bfloat16) for rows in piece_rows],
-        in_specs=[pl.BlockSpec(memory_space=pltpu.SMEM)] * 2
-        + [pl.BlockSpec(memory_space=pltpu.VMEM)] * (len(flat_rows) + 1),
+        in_specs=[pl.BlockSpec(memory_space=pltpu.VMEM)] * (len(flat_rows) + 2),
         compiler_params=pltpu.CompilerParams(vmem_limit_bytes=VMEM_LIMIT),
         cost_estimate=pl.CostEstimate(
             flops=4 * sum(flat_rows) * labels * width,
@@ -147,18 +175,18 @@
             transcendentals=0,
         ),
         name="block_work",
-    )(first, sizes, *[piece for pieces in blocks for piece in pieces], weights)
+    )(*[piece for pieces in blocks for piece in pieces], weights, live_table)
     return list(out[: len(flat_rows)]), list(out[len(flat_rows) :])
 
 
-def weight_kernel(piece_rows, column_blocks, scale, own_ref, *refs):
+def weight_kernel(piece_rows, column_blocks, scale, *refs):
     piece_count = len(piece_rows)
     out_refs = refs[len(refs) - len(column_blocks) :]
     x_refs, s_refs = refs[:piece_count], refs[piece_count : len(refs) - len(column_blocks)]
     part_width = out_refs[0].shape[1]
     slopes = jnp.concatenate([ref[...] for ref in s_refs], axis=0)
     for ref, q in zip(out_refs, column_blocks):
-        at = pl.multiple_of((own_ref[0] ^ q) * part_width, part_width)
+        at = pl.multiple_of((lax.axis_index("seq") ^ q) * part_width, part_width)
         x = jnp.concatenate(
             [r[:rows, pl.ds(at, part_width)] for r, rows in zip(x_refs, piece_rows)], axis=0
         )
@@ -168,7 +196,7 @@
         ref[...] = (part * scale).astype(jnp.bfloat16)
 
 
-def weight_work(blocks, slopes, own, column_blocks, part_width, scale):
+def weight_work(blocks, slopes, column_blocks, part_width, scale):
     pieces = [piece for block in blocks for piece in block]
     piece_rows = [
         piece.shape[0] - (FIELD_ROWS if p == 0 else 0)
@@ -180,8 +208,7 @@
     return pl.pallas_call(
         functools.partial(weight_kernel, piece_rows, column_blocks, scale),
         out_shape=[jax.ShapeDtypeStruct((labels, part_width), jnp.bfloat16)] * len(column_blocks),
-        in_specs=[pl.BlockSpec(memory_space=pltpu.SMEM)]
-        + [pl.BlockSpec(memory_space=pltpu.VMEM)] * (len(pieces) + len(slopes)),
+        in_specs=[pl.BlockSpec(memory_space=pltpu.VMEM)] * (len(pieces) + len(slopes)),
         compiler_params=pltpu.CompilerParams(vmem_limit_bytes=VMEM_LIMIT),
         cost_estimate=pl.CostEstimate(
             flops=2 * rows * labels * part_width * len(column_blocks),
@@ -189,7 +216,7 @@
             transcendentals=0,
         ),
         name="weight_work",
-    )(own, *pieces, *slopes)
+    )(*pieces, *slopes)
 
 
 def add(*parts):
@@ -212,30 +239,28 @@
     half, steps = inst_rows // 2, clus_count // 2
 
     ring = list(range(0, clus_count, 2)) + list(range(1, clus_count, 2))[::-1]
-    onward = []
-    for s in range(seq_count):
-        places = [s * clus_count + c for c in (ring if s % 2 == 0 else ring[::-1])]
-        onward += list(zip(places, places[1:] + places[:1]))
+    onward = list(zip(ring, ring[1:] + ring[:1]))
     back = [(b, a) for a, b in onward]
 
     def send(array, pairs):
-        return lax.ppermute(array, ("seq", "clus"), pairs)
-
-    first = (lax.axis_index("clus") * local_count).astype(jnp.int32).reshape(1)
+        return lax.ppermute(array, "clus", pairs)
+
     used, slopes = [], []
 
     def take(*blocks):
-        grads, found = block_work(blocks, weights, first, cluster_sizes, top_count, pos_count)
+        grads, found = block_work(blocks, weights, live_table, top_count, pos_count)
         used.extend(blocks)
         slopes.extend(found)
         return grads
 
     own = pack(features, shortlist, positives)
+    live_table = live_labels(cluster_sizes, own, weights)
     behind_x, front_x = own, own
     parts = {}
     for k in range(1, steps + 1):
         if k > 1:
-            behind_x, front_x = after(behind_x, parts[k - 2][0]), after(front_x, parts[k - 2][0])
+            before = live_table if k == 2 else parts[k - 2][0]
+            behind_x, front_x = after(behind_x, before), after(front_x, before)
         if k < steps:
             going = behind_x, front_x
         else:
@@ -244,19 +269,21 @@
                 front_x[half:inst_rows],
             )
         arriving = send(going[0], onward), send(going[1], back)
-        parts[k - 1] = take([own]) if k == 1 else take([behind_x], [front_x])
+        if k == 2:
+            *parts[1], own_part = take([behind_x], [front_x], [own])
+        elif k > 2:
+            parts[k - 1] = take([behind_x], [front_x])
         behind_x, front_x = arriving
     to_back, to_front = take([after(behind_x, parts[steps - 1][0]), front_x])
 
     scale = 1.0 / math.sqrt(inst_rows * seq_count * top_count // local_count)
-    own_seq = lax.axis_index("seq").astype(jnp.int32).reshape(1)
 
     def seq_send(array, bit):
         return lax.ppermute(array, "seq", [(k, k ^ bit) for k in range(seq_count)])
 
     far, near = list(range(seq_count // 2, seq_count)), list(range(seq_count // 2))
-    terms = dict(zip(far, weight_work(used, slopes, own_seq, far, part_width, scale)))
-    terms.update(zip(near, weight_work(used, slopes, own_seq, near, part_width, scale)))
+    terms = dict(zip(far, weight_work(used, slopes, far, part_width, scale)))
+    terms.update(zip(near, weight_work(used, slopes, near, part_width, scale)))
     terms = {q: [term] for q, term in terms.items()}
     bit = 1
     while bit < seq_count:
@@ -275,7 +302,7 @@
         elif k > 1:
             near_behind, near_front = parts[k - 1]
             to_back, to_front = add(near_behind, from_front), add(near_front, from_behind)
-    feature_grad = add(after(parts[0][0], weight_grad), from_front, from_behind)
+    feature_grad = add(after(own_part, weight_grad), from_front, from_behind)
     return (feature_grad, weight_grad)
 
 

time: 72.7 us -> 73.8 us (1.015)
  local copies, waits for them, and re-layouts: 9.56 us -> 3.25 us
  Pallas kernels: 12.9 us -> 19.2 us
  waiting for transfers between devices: 26.1 us -> 28.1 us
    pallas_call x1, Pallas kernels: 0.05 us -> 9.08 us  [pack(): pl.pallas_call(pack_kernel, out_shape=jax.ShapeDtypeStruct((rows + FIELD_...]
    unnamed x66 -> x10, local copies, waits for them, and re-layouts: 8.86 us -> 3.21 us
    pallas_call x5 -> x4, Pallas kernels: 10.2 us -> 6.97 us  [block_work(): pl.pallas_call(functools.partial(block_kernel, piece_rows, top_count, pos...]
    ppermute x3, waiting for transfers between devices: 1.69 us -> 3.72 us  [seq_send(): return lax.ppermute(array, 'seq', [(k, k ^ bit) for k in range(seq_count)])]
    ppermute x16, starting transfers between devices: 16.6 us -> 17.7 us  [send(): return lax.ppermute(array, 'clus', pairs)]
    ppermute x3, starting transfers between devices: 3.07 us -> 2.18 us  [seq_send(): return lax.ppermute(array, 'seq', [(k, k ^ bit) for k in range(seq_count)])]
  transfers between devices with their start and end apart: 19 -> 19, of which waited for: 11 -> 10; matrix products, arithmetic and copies ran while one was open for 4% -> 2% of each run, Pallas kernels for 15% -> 12%
where the time goes in v5:
time: 73.8 us; the launch traced here: 73.6 us
  waiting for transfers between devices  28.1 us (38%)
  starting transfers between devices  19.9 us (27%)
  Pallas kernels  19.2 us (26%)
  local copies, waits for them, and re-layouts  3.25 us (4%)
  other arithmetic  2.32 us (3%)
  between operations  0.8 us (1%)
    ppermute x16, waiting for transfers between devices, send(): return lax.ppermute(array, 'clus', pairs)  24.4 us
    ppermute x16, starting transfers between devices, send(): return lax.ppermute(array, 'clus', pairs)  17.7 us
    pallas_call x1, Pallas kernels, pack(): pl.pallas_call(pack_kernel, out_shape=jax.ShapeDtypeStruct((rows + FIELD_...  9.08 us
    pallas_call x4, Pallas kernels, block_work(): pl.pallas_call(functools.partial(block_kernel, piece_rows, top_count, pos...  6.97 us
    ppermute x3, waiting for transfers between devices, seq_send(): return lax.ppermute(array, 'seq', [(k, k ^ bit) for k in range(seq_count)])  3.72 us
    unnamed x10, local copies, waits for them, and re-layouts  3.21 us
    pallas_call x2, Pallas kernels, weight_work(): pl.pallas_call(functools.partial(weight_kernel, piece_rows, column_blocks...  2.59 us
    convert_element_type x9, other arithmetic, add(): return total.astype(jnp.bfloat16)  2.27 us
  transfers between devices with their start and end apart: 19, of which 10 were waited for; matrix products, arithmetic and copies ran while one was open for 2% of the time, Pallas kernels for 12%

profile of v5, /device:TPU:0, one launch (start us, length us, event | category | flops | bytes accessed | tf_op | source)
XLA Modules:
  0.0 73.6 jit_solution(16731211662531310773)
XLA Ops:
  0.6 9.1 %pack.1.x_ref.refs_2_ = bf16[136,1024]{1,0:T(8,128)(2,1)} custom-call(bf16[128,1024]{1,0:T(8,128)(2,1)} %feat_ref.1, s32[16,128]{1,0:T(8,128)} %bitcast.2, s32[4,128]{1,0:T(4,128)} %bitcast.3), custom_call_target="tpu_custom_call" | custom-call | tf_op jit(solution)/shard_map/pack/pallas_call | solution.py:51
  9.7 3.1 %collective-permute-start = (bf16[136,1024]{1,0:T(8,128)(2,1)}, bf16[136,1024]{1,0:T(8,128)(2,1)S(1)}, u32[]{:S(2)}, u32[]{:S(2)}) collective-permute-start(bf16[136,1024]{1,0:T(8,128)(2,1)} %pack.1.x_ref.refs_2_), channel_id=1, source_target_pairs={{0,2},{2,4},{4,6},{6,7},{7,5},{5,3},{3,1},{1,0},{8,10},{10,12},{12... | collective-permute-start | bytes 835592 | tf_op jit(solution)/shard_map/ppermute | solution.py:246
  12.8 1.6 %copy-done = bf16[1024,1024]{1,0:T(8,128)(2,1)S(1)} copy-done((bf16[1024,1024]{1,0:T(8,128)(2,1)S(1)}, bf16[1024,1024]{1,0:T(8,128)(2,1)}, u32[]{:S(2)}) %copy-start) | copy-done | bytes 2097176
  14.4 1.0 %copy-done.2 = bf16[136,1024]{1,0:T(8,128)(2,1)S(1)} copy-done((bf16[136,1024]{1,0:T(8,128)(2,1)S(1)}, bf16[136,1024]{1,0:T(8,128)(2,1)}, u32[]{:S(2)}) %copy-start.2) | copy-done | bytes 278552
  15.4 0.7 copy-done.4
  16.0 0.6 live_labels.1.refs_4_.refs_3_
  16.6 3.0 %collective-permute-done.refs_0_ = bf16[136,1024]{1,0:T(8,128)(2,1)S(1)} collective-permute-done((bf16[136,1024]{1,0:T(8,128)(2,1)}, bf16[136,1024]{1,0:T(8,128)(2,1)S(1)}, u32[]{:S(2)}, u32[]{:S(2)}) %collective-permute-start) | collective-permute-done | bytes 278560 | tf_op jit(solution)/shard_map/ppermute | solution.py:246
  19.6 1.8 %collective-permute-start.2 = (bf16[136,1024]{1,0:T(8,128)(2,1)S(1)}, bf16[136,1024]{1,0:T(8,128)(2,1)S(1)}, u32[]{:S(2)}, u32[]{:S(2)}) collective-permute-start(bf16[136,1024]{1,0:T(8,128)(2,1)S(1)} %collective-permute-done.refs_0_), channel_id=1, source_target_pairs={{0,2},{2,4},{4,6},{6,7},{7,5},{5,3},{3,1},{1,0},{8,10},{10,12},{12... | collective-permute-start | bytes 835592 | tf_op jit(solution)/shard_map/ppermute | solution.py:246
  21.6 2.4 %block_work.4 = (bf16[128,1024]{1,0:T(8,128)(2,1)S(1)}, bf16[128,1024]{1,0:T(8,128)(2,1)S(1)}, bf16[128,1024]{1,0:T(8,128)(2,1)S(1)}, bf16[128,1024]{1,0:T(8,128...) custom-call(bf16[136,1024]{1,0:T(8,128)(2,1)S(1)} %collective-permute-done.refs_0_, ...), custom_call_target="tpu_custom_call" | custom-call | flops 1610612736 | bytes 4456448 | tf_op jit(solution)/shard_map/block_work/pallas_call | solution.py:166
  24.0 3.4 %collective-permute-done.2.refs_0_.refs_3_ = bf16[136,1024]{1,0:T(8,128)(2,1)S(1)} collective-permute-done((bf16[136,1024]{1,0:T(8,128)(2,1)S(1)}, bf16[136,1024]{1,0:T(8,128)(2,1)S(1)}, u32[]{:S(2)}, u32[]{:S(2)}) %collective-permute-start.2) | collective-permute-done | bytes 278560 | tf_op jit(solution)/shard_map/ppermute | solution.py:246
  27.4 1.5 %collective-permute-start.4 = (bf16[136,1024]{1,0:T(8,128)(2,1)S(1)}, bf16[136,1024]{1,0:T(8,128)(2,1)S(1)}, u32[]{:S(2)}, u32[]{:S(2)}) collective-permute-start(bf16[136,1024]{1,0:T(8,128)(2,1)S(1)} %collective-permute-done.2.refs_0_.refs_3_), channel_id=1, source_target_pairs={{0,2},{2,4},{4,6},{6,7},{7,5},{5,3},{3,1},{1,0},{8,10},{10,12},{12... | collective-permute-start | bytes 835592 | tf_op jit(solution)/shard_map/ppermute | solution.py:246
  29.5 1.7 %block_work.5 = (bf16[128,1024]{1,0:T(8,128)(2,1)S(1)}, bf16[128,1024]{1,0:T(8,128)(2,1)S(1)}, bf16[128,1024]{1,0:T(8,128)(2,1)S(1)}, bf16[128,1024]{1,0:T(8,128)(2,1)S(1)}) custom-call(bf16[136,1024]{1,0:T(8,128)(2,1)S(1)} %collective-permute-done.2.refs_0_.refs_3_, bf16[136,1024]{1,0:T(8,128)(2,1)S(1)} %collective-permute-done.3.refs_1_.refs_4_, ...), custom_call_target="tpu_custom_call" | custom-call | flops 1073741824 | bytes 3670016 | tf_op jit(solution)/shard_map/block_work/pallas_call | solution.py:166
  31.2 3.2 %collective-permute-done.4.refs_0_.refs_5_ = bf16[136,1024]{1,0:T(8,128)(2,1)S(1)} collective-permute-done((bf16[136,1024]{1,0:T(8,128)(2,1)S(1)}, bf16[136,1024]{1,0:T(8,128)(2,1)S(1)}, u32[]{:S(2)}, u32[]{:S(2)}) %collective-permute-start.4) | collective-permute-done | bytes 278560 | tf_op jit(solution)/shard_map/ppermute | solution.py:246
  34.4 1.6 %collective-permute-start.6 = (bf16[72,1024]{1,0:T(8,128)(2,1)S(1)}, bf16[72,1024]{1,0:T(8,128)(2,1)S(1)}, u32[]{:S(2)}, u32[]{:S(2)}) collective-permute-start(bf16[72,1024]{1,0:T(8,128)(2,1)S(1)} %pad_maximum_fusion.2), channel_id=1, source_target_pairs={{0,2},{2,4},{4,6},{6,7},{7,5},{5,3},{3,1},{1,0},{8,10},{10,12},{12... | collective-permute-start | bytes 442376 | tf_op jit(solution)/shard_map/ppermute | solution.py:246
  36.6 1.7 %block_work.6 = (bf16[128,1024]{1,0:T(8,128)(2,1)S(1)}, bf16[128,1024]{1,0:T(8,128)(2,1)S(1)}, bf16[128,1024]{1,0:T(8,128)(2,1)S(1)}, bf16[128,1024]{1,0:T(8,128)(2,1)S(1)}) custom-call(bf16[136,1024]{1,0:T(8,128)(2,1)S(1)} %collective-permute-done.4.refs_0_.refs_5_, bf16[136,1024]{1,0:T(8,128)(2,1)S(1)} %collective-permute-done.5.refs_1_.refs_6_, ...), custom_call_target="tpu_custom_call" | custom-call | flops 1073741824 | bytes 3670016 | tf_op jit(solution)/shard_map/block_work/pallas_call | solution.py:166
  38.3 1.3 %collective-permute-done.6.refs_0_.refs_7_ = bf16[72,1024]{1,0:T(8,128)(2,1)S(1)} collective-permute-done((bf16[72,1024]{1,0:T(8,128)(2,1)S(1)}, bf16[72,1024]{1,0:T(8,128)(2,1)S(1)}, u32[]{:S(2)}, u32[]{:S(2)}) %collective-permute-start.6) | collective-permute-done | bytes 147488 | tf_op jit(solution)/shard_map/ppermute | solution.py:246
  39.6 1.5 %collective-permute-done.7.refs_1_.refs_8_ = bf16[64,1024]{1,0:T(8,128)(2,1)S(1)} collective-permute-done((bf16[64,1024]{1,0:T(8,128)(2,1)S(1)}, bf16[64,1024]{1,0:T(8,128)(2,1)S(1)}, u32[]{:S(2)}, u32[]{:S(2)}) %collective-permute-start.7) | collective-permute-done | bytes 131104 | tf_op jit(solution)/shard_map/ppermute | solution.py:246
  41.1 1.2 %block_work.7 = (bf16[64,1024]{1,0:T(8,128)(2,1)S(1)}, bf16[64,1024]{1,0:T(8,128)(2,1)S(1)}, bf16[128,1024]{1,0:T(8,128)(2,1)S(1)}) custom-call(bf16[72,1024]{1,0:T(8,128)(2,1)S(1)} %collective-permute-done.6.refs_0_.refs_7_, bf16[64,1024]{1,0:T(8,128)(2,1)S(1)} %collective-permute-done.7.refs_1_.refs_8_, bf16[1024,1024]{1,0:T(8,128)(2,1)S(1)} %copy-done.1, ...), custom_call_target="tpu_custom_call" | custom-call | flops 536870912 | bytes 2883584 | tf_op jit(solution)/shard_map/block_work/pallas_call | solution.py:166
  42.3 1.6 %collective-permute-start.15 = (bf16[64,1024]{1,0:T(8,128)(2,1)S(1)}, bf16[64,1024]{1,0:T(8,128)(2,1)S(1)}, u32[]{:S(2)}, u32[]{:S(2)}) collective-permute-start(bf16[64,1024]{1,0:T(8,128)(2,1)S(1)} %get-tuple-element.59), channel_id=1, source_target_pairs={{0,2},{2,4},{4,6},{6,7},{7,5},{5,3},{3,1},{1,0},{8,10},{10,12},{12... | collective-permute-start | bytes 393224 | tf_op jit(solution)/shard_map/ppermute | solution.py:246
  44.4 1.3 %weight_work.3 = (bf16[1024,256]{1,0:T(8,128)(2,1)S(1)}, bf16[1024,256]{1,0:T(8,128)(2,1)S(1)}) custom-call(bf16[136,1024]{1,0:T(8,128)(2,1)S(1)} %collective-permute-done.refs_0_, bf16[136,1024]{1,0:T(8,128)(2,1)S(1)} %collective-permute-done.1.refs_1_, bf16[136,1024]{1,0:T(8,128)(2,1)S(1)} %copy-done.3, ...), custom_call_target="tpu_custom_call" | custom-call | flops 1073741824 | bytes 4718592 | tf_op jit(solution)/shard_map/weight_work/pallas_call | solution.py:208
  45.7 1.3 %weight_work.2 = (bf16[1024,256]{1,0:T(8,128)(2,1)S(1)}, bf16[1024,256]{1,0:T(8,128)(2,1)S(1)}) custom-call(bf16[136,1024]{1,0:T(8,128)(2,1)S(1)} %collective-permute-done.refs_0_, bf16[136,1024]{1,0:T(8,128)(2,1)S(1)} %collective-permute-done.1.refs_1_, bf16[136,1024]{1,0:T(8,128)(2,1)S(1)} %copy-done.3, ...), custom_call_target="tpu_custom_call" | custom-call | flops 1073741824 | bytes 4718592 | tf_op jit(solution)/shard_map/weight_work/pallas_call | solution.py:208
  47.7 1.6 %collective-permute-start.16 = (bf16[128,1024]{1,0:T(8,128)(2,1)S(1)}, bf16[128,1024]{1,0:T(8,128)(2,1)S(1)}, u32[]{:S(2)}, u32[]{:S(2)}) collective-permute-start(bf16[128,1024]{1,0:T(8,128)(2,1)S(1)} %pad_maximum_fusion.1), channel_id=1, source_target_pairs={{0,2},{2,4},{4,6},{6,7},{7,5},{5,3},{3,1},{1,0},{8,10},{10,12},{12... | collective-permute-start | bytes 786440 | tf_op jit(solution)/shard_map/ppermute | solution.py:246
  49.9 6.1 %collective-permute-done.16 = bf16[128,1024]{1,0:T(8,128)(2,1)S(1)} collective-permute-done((bf16[128,1024]{1,0:T(8,128)(2,1)S(1)}, bf16[128,1024]{1,0:T(8,128)(2,1)S(1)}, u32[]{:S(2)}, u32[]{:S(2)}) %collective-permute-start.16) | collective-permute-done | bytes 262176 | tf_op jit(solution)/shard_map/ppermute | solution.py:246
  56.0 1.6 %collective-permute-start.17 = (bf16[128,1024]{1,0:T(8,128)(2,1)S(1)}, bf16[128,1024]{1,0:T(8,128)(2,1)S(1)}, u32[]{:S(2)}, u32[]{:S(2)}) collective-permute-start(bf16[128,1024]{1,0:T(8,128)(2,1)S(1)} %add_convert_fusion.4), channel_id=1, source_target_pairs={{0,2},{2,4},{4,6},{6,7},{7,5},{5,3},{3,1},{1,0},{8,10},{10,12},{12... | collective-permute-start | bytes 786440 | tf_op jit(solution)/shard_map/ppermute | solution.py:246
  57.8 1.5 %collective-permute-start.10 = (bf16[1024,256]{1,0:T(8,128)(2,1)S(1)}, bf16[1024,256]{1,0:T(8,128)(2,1)S(1)}, u32[]{:S(2)}, u32[]{:S(2)}) collective-permute-start(bf16[1024,256]{1,0:T(8,128)(2,1)S(1)} %add_convert_fusion.1), channel_id=1, source_target_pairs={{0,16},{8,24},{16,0},{24,8},{1,17},{9,25},{17,1},{25,9},{2,18},{10... | collective-permute-start | bytes 1572872 | tf_op jit(solution)/shard_map/ppermute | solution.py:282
  59.9 3.5 %collective-permute-done.17 = bf16[128,1024]{1,0:T(8,128)(2,1)S(1)} collective-permute-done((bf16[128,1024]{1,0:T(8,128)(2,1)S(1)}, bf16[128,1024]{1,0:T(8,128)(2,1)S(1)}, u32[]{:S(2)}, u32[]{:S(2)}) %collective-permute-start.17) | collective-permute-done | bytes 262176 | tf_op jit(solution)/shard_map/ppermute | solution.py:246
  63.5 1.6 %collective-permute-start.18 = (bf16[128,1024]{1,0:T(8,128)(2,1)S(1)}, bf16[128,1024]{1,0:T(8,128)(2,1)S(1)}, u32[]{:S(2)}, u32[]{:S(2)}) collective-permute-start(bf16[128,1024]{1,0:T(8,128)(2,1)S(1)} %add_convert_fusion.3), channel_id=1, source_target_pairs={{0,2},{2,4},{4,6},{6,7},{7,5},{5,3},{3,1},{1,0},{8,10},{10,12},{12... | collective-permute-start | bytes 786440 | tf_op jit(solution)/shard_map/ppermute | solution.py:246
  65.2 1.1 %collective-permute-done.13 = bf16[128,1024]{1,0:T(8,128)(2,1)S(1)} collective-permute-done((bf16[128,1024]{1,0:T(8,128)(2,1)S(1)}, bf16[128,1024]{1,0:T(8,128)(2,1)S(1)}, u32[]{:S(2)}, u32[]{:S(2)}) %collective-permute-start.13) | collective-permute-done | bytes 262176 | tf_op jit(solution)/shard_map/ppermute | solution.py:246
  66.9 3.7 %collective-permute-done.10 = bf16[1024,256]{1,0:T(8,128)(2,1)S(1)} collective-permute-done((bf16[1024,256]{1,0:T(8,128)(2,1)S(1)}, bf16[1024,256]{1,0:T(8,128)(2,1)S(1)}, u32[]{:S(2)}, u32[]{:S(2)}) %collective-permute-start.10) | collective-permute-done | bytes 524320 | tf_op jit(solution)/shard_map/ppermute | solution.py:282
  70.6 1.0 %add_convert_fusion = bf16[1024,256]{1,0:T(8,128)(2,1)} fusion(bf16[1024,256]{1,0:T(8,128)(2,1)S(1)} %collective-permute-done.10, bf16[1024,256]{1,0:T(8,128)(2,1)S(1)} %collective-permute-done.8, bf16[1024,256]{1,0:T(8,128)(2,1)S(1)} %get-tuple-element.50), kind=kLoop, calls=%fused_computation | loop fusion | flops 1572864 | bytes 2097152 | tf_op jit(solution)/shard_map/convert_element_type | solution.py:226
  71.6 1.2 %collective-permute-done.14 = bf16[128,1024]{1,0:T(8,128)(2,1)S(1)} collective-permute-done((bf16[128,1024]{1,0:T(8,128)(2,1)S(1)}, bf16[128,1024]{1,0:T(8,128)(2,1)S(1)}, u32[]{:S(2)}, u32[]{:S(2)}) %collective-permute-start.14) | collective-permute-done | bytes 262176 | tf_op jit(solution)/shard_map/ppermute | solution.py:246
  72.8 0.8 %add_convert_fusion.2 = bf16[128,1024]{1,0:T(8,128)(2,1)} fusion(bf16[128,1024]{1,0:T(8,128)(2,1)S(1)} %collective-permute-done.18, bf16[128,1024]{1,0:T(8,128)(2,1)S(1)} %collective-permute-done.14, bf16[128,1024]{1,0:T(8,128)(2,1)S(1)} %get-tuple-element.54), kind=kLoop, calls=%fused_computation.2 | loop fusion | flops 786432 | bytes 1048576 | tf_op jit(solution)/shard_map/convert_element_type | solution.py:226
  (41 shorter events, 4.5 us)
Async XLA Ops:
  9.7 9.9 %collective-permute-start = (bf16[136,1024]{1,0:T(8,128)(2,1)}, bf16[136,1024]{1,0:T(8,128)(2,1)S(1)}, u32[]{:S(2)}, u32[]{:S(2)}) collective-permute-start(bf16[136,1024]{1,0:T(8,128)(2,1)} %pack.1.x_ref.refs_2_), channel_id=1, source_target_pairs={{0,2},{2,4},{4,6},{6,7},{7,5},{5,3},{3,1},{1,0},{8,10},{10,12},{12... | collective-permute-start | bytes 835592 | tf_op jit(solution)/shard_map/ppermute | solution.py:246
  12.8 8.6 %collective-permute-start.1 = (bf16[136,1024]{1,0:T(8,128)(2,1)}, bf16[136,1024]{1,0:T(8,128)(2,1)S(1)}, u32[]{:S(2)}, u32[]{:S(2)}) collective-permute-start(bf16[136,1024]{1,0:T(8,128)(2,1)} %pack.1.x_ref.refs_2_), channel_id=1, source_target_pairs={{2,0},{4,2},{6,4},{7,6},{5,7},{3,5},{1,3},{0,1},{10,8},{12,10},{14... | collective-permute-start | bytes 835592 | tf_op jit(solution)/shard_map/ppermute | solution.py:246
  12.8 1.6 %copy-start = (bf16[1024,1024]{1,0:T(8,128)(2,1)S(1)}, bf16[1024,1024]{1,0:T(8,128)(2,1)}, u32[]{:S(2)}) copy-start(bf16[1024,1024]{1,0:T(8,128)(2,1)} %refs_2_.5) | copy-start | bytes 6291460
  14.4 1.0 %copy-start.2 = (bf16[136,1024]{1,0:T(8,128)(2,1)S(1)}, bf16[136,1024]{1,0:T(8,128)(2,1)}, u32[]{:S(2)}) copy-start(bf16[136,1024]{1,0:T(8,128)(2,1)} %pack.1.x_ref.refs_2_) | copy-start | bytes 835588
  15.4 0.7 copy-start.4
  16.0 5.6 %copy-start.1 = (bf16[1024,1024]{1,0:T(8,128)(2,1)S(1)}, bf16[1024,1024]{1,0:T(8,128)(2,1)}, u32[]{:S(2)}) copy-start(bf16[1024,1024]{1,0:T(8,128)(2,1)} %refs_2_.5) | copy-start | bytes 6291460
  16.0 5.6 %copy-start.3 = (bf16[136,1024]{1,0:T(8,128)(2,1)S(1)}, bf16[136,1024]{1,0:T(8,128)(2,1)}, u32[]{:S(2)}) copy-start(bf16[136,1024]{1,0:T(8,128)(2,1)} %pack.1.x_ref.refs_2_) | copy-start | bytes 835588
  19.6 7.8 %collective-permute-start.2 = (bf16[136,1024]{1,0:T(8,128)(2,1)S(1)}, bf16[136,1024]{1,0:T(8,128)(2,1)S(1)}, u32[]{:S(2)}, u32[]{:S(2)}) collective-permute-start(bf16[136,1024]{1,0:T(8,128)(2,1)S(1)} %collective-permute-done.refs_0_), channel_id=1, source_target_pairs={{0,2},{2,4},{4,6},{6,7},{7,5},{5,3},{3,1},{1,0},{8,10},{10,12},{12... | collective-permute-start | bytes 835592 | tf_op jit(solution)/shard_map/ppermute | solution.py:246
  21.4 7.5 %collective-permute-start.3 = (bf16[136,1024]{1,0:T(8,128)(2,1)S(1)}, bf16[136,1024]{1,0:T(8,128)(2,1)S(1)}, u32[]{:S(2)}, u32[]{:S(2)}) collective-permute-start(bf16[136,1024]{1,0:T(8,128)(2,1)S(1)} %collective-permute-done.1.refs_1_), channel_id=1, source_target_pairs={{2,0},{4,2},{6,4},{7,6},{5,7},{3,5},{1,3},{0,1},{10,8},{12,10},{14... | collective-permute-start | bytes 835592 | tf_op jit(solution)/shard_map/ppermute | solution.py:246
  27.4 6.9 %collective-permute-start.4 = (bf16[136,1024]{1,0:T(8,128)(2,1)S(1)}, bf16[136,1024]{1,0:T(8,128)(2,1)S(1)}, u32[]{:S(2)}, u32[]{:S(2)}) collective-permute-start(bf16[136,1024]{1,0:T(8,128)(2,1)S(1)} %collective-permute-done.2.refs_0_.refs_3_), channel_id=1, source_target_pairs={{0,2},{2,4},{4,6},{6,7},{7,5},{5,3},{3,1},{1,0},{8,10},{10,12},{12... | collective-permute-start | bytes 835592 | tf_op jit(solution)/shard_map/ppermute | solution.py:246
  28.9 7.1 %collective-permute-start.5 = (bf16[136,1024]{1,0:T(8,128)(2,1)S(1)}, bf16[136,1024]{1,0:T(8,128)(2,1)S(1)}, u32[]{:S(2)}, u32[]{:S(2)}) collective-permute-start(bf16[136,1024]{1,0:T(8,128)(2,1)S(1)} %collective-permute-done.3.refs_1_.refs_4_), channel_id=1, source_target_pairs={{2,0},{4,2},{6,4},{7,6},{5,7},{3,5},{1,3},{0,1},{10,8},{12,10},{14... | collective-permute-start | bytes 835592 | tf_op jit(solution)/shard_map/ppermute | solution.py:246
  34.4 5.2 %collective-permute-start.6 = (bf16[72,1024]{1,0:T(8,128)(2,1)S(1)}, bf16[72,1024]{1,0:T(8,128)(2,1)S(1)}, u32[]{:S(2)}, u32[]{:S(2)}) collective-permute-start(bf16[72,1024]{1,0:T(8,128)(2,1)S(1)} %pad_maximum_fusion.2), channel_id=1, source_target_pairs={{0,2},{2,4},{4,6},{6,7},{7,5},{5,3},{3,1},{1,0},{8,10},{10,12},{12... | collective-permute-start | bytes 442376 | tf_op jit(solution)/shard_map/ppermute | solution.py:246
  36.0 5.0 %collective-permute-start.7 = (bf16[64,1024]{1,0:T(8,128)(2,1)S(1)}, bf16[64,1024]{1,0:T(8,128)(2,1)S(1)}, u32[]{:S(2)}, u32[]{:S(2)}) collective-permute-start(bf16[64,1024]{1,0:T(8,128)(2,1)S(1)} %slice.23), channel_id=1, source_target_pairs={{2,0},{4,2},{6,4},{7,6},{5,7},{3,5},{1,3},{0,1},{10,8},{12,10},{14... | collective-permute-start | bytes 393224 | tf_op jit(solution)/shard_map/ppermute | solution.py:246
  42.3 5.3 %collective-permute-start.15 = (bf16[64,1024]{1,0:T(8,128)(2,1)S(1)}, bf16[64,1024]{1,0:T(8,128)(2,1)S(1)}, u32[]{:S(2)}, u32[]{:S(2)}) collective-permute-start(bf16[64,1024]{1,0:T(8,128)(2,1)S(1)} %get-tuple-element.59), channel_id=1, source_target_pairs={{0,2},{2,4},{4,6},{6,7},{7,5},{5,3},{3,1},{1,0},{8,10},{10,12},{12... | collective-permute-start | bytes 393224 | tf_op jit(solution)/shard_map/ppermute | solution.py:246
  43.9 5.4 %collective-permute-start.11 = (bf16[64,1024]{1,0:T(8,128)(2,1)S(1)}, bf16[64,1024]{1,0:T(8,128)(2,1)S(1)}, u32[]{:S(2)}, u32[]{:S(2)}) collective-permute-start(bf16[64,1024]{1,0:T(8,128)(2,1)S(1)} %get-tuple-element.55), channel_id=1, source_target_pairs={{2,0},{4,2},{6,4},{7,6},{5,7},{3,5},{1,3},{0,1},{10,8},{12,10},{14... | collective-permute-start | bytes 393224 | tf_op jit(solution)/shard_map/ppermute | solution.py:246
  45.6 12.0 %collective-permute-start.9 = (bf16[1024,256]{1,0:T(8,128)(2,1)S(1)}, bf16[1024,256]{1,0:T(8,128)(2,1)S(1)}, u32[]{:S(2)}, u32[]{:S(2)}) collective-permute-start(bf16[1024,256]{1,0:T(8,128)(2,1)S(1)} %get-tuple-element.53), channel_id=1, source_target_pairs={{0,8},{8,0},{16,24},{24,16},{1,9},{9,1},{17,25},{25,17},{2,10},{10... | collective-permute-start | bytes 1572872 | tf_op jit(solution)/shard_map/ppermute | solution.py:282
  47.0 19.8 %collective-permute-start.8 = (bf16[1024,256]{1,0:T(8,128)(2,1)S(1)}, bf16[1024,256]{1,0:T(8,128)(2,1)S(1)}, u32[]{:S(2)}, u32[]{:S(2)}) collective-permute-start(bf16[1024,256]{1,0:T(8,128)(2,1)S(1)} %get-tuple-element.51), channel_id=1, source_target_pairs={{0,8},{8,0},{16,24},{24,16},{1,9},{9,1},{17,25},{25,17},{2,10},{10... | collective-permute-start | bytes 1572872 | tf_op jit(solution)/shard_map/ppermute | solution.py:282
  47.7 8.3 %collective-permute-start.16 = (bf16[128,1024]{1,0:T(8,128)(2,1)S(1)}, bf16[128,1024]{1,0:T(8,128)(2,1)S(1)}, u32[]{:S(2)}, u32[]{:S(2)}) collective-permute-start(bf16[128,1024]{1,0:T(8,128)(2,1)S(1)} %pad_maximum_fusion.1), channel_id=1, source_target_pairs={{0,2},{2,4},{4,6},{6,7},{7,5},{5,3},{3,1},{1,0},{8,10},{10,12},{12... | collective-permute-start | bytes 786440 | tf_op jit(solution)/shard_map/ppermute | solution.py:246
  49.4 10.0 %collective-permute-start.12 = (bf16[128,1024]{1,0:T(8,128)(2,1)S(1)}, bf16[128,1024]{1,0:T(8,128)(2,1)S(1)}, u32[]{:S(2)}, u32[]{:S(2)}) collective-permute-start(bf16[128,1024]{1,0:T(8,128)(2,1)S(1)} %pad_maximum_fusion), channel_id=1, source_target_pairs={{2,0},{4,2},{6,4},{7,6},{5,7},{3,5},{1,3},{0,1},{10,8},{12,10},{14... | collective-permute-start | bytes 786440 | tf_op jit(solution)/shard_map/ppermute | solution.py:246
  56.0 7.4 %collective-permute-start.17 = (bf16[128,1024]{1,0:T(8,128)(2,1)S(1)}, bf16[128,1024]{1,0:T(8,128)(2,1)S(1)}, u32[]{:S(2)}, u32[]{:S(2)}) collective-permute-start(bf16[128,1024]{1,0:T(8,128)(2,1)S(1)} %add_convert_fusion.4), channel_id=1, source_target_pairs={{0,2},{2,4},{4,6},{6,7},{7,5},{5,3},{3,1},{1,0},{8,10},{10,12},{12... | collective-permute-start | bytes 786440 | tf_op jit(solution)/shard_map/ppermute | solution.py:246
  57.8 12.8 %collective-permute-start.10 = (bf16[1024,256]{1,0:T(8,128)(2,1)S(1)}, bf16[1024,256]{1,0:T(8,128)(2,1)S(1)}, u32[]{:S(2)}, u32[]{:S(2)}) collective-permute-start(bf16[1024,256]{1,0:T(8,128)(2,1)S(1)} %add_convert_fusion.1), channel_id=1, source_target_pairs={{0,16},{8,24},{16,0},{24,8},{1,17},{9,25},{17,1},{25,9},{2,18},{10... | collective-permute-start | bytes 1572872 | tf_op jit(solution)/shard_map/ppermute | solution.py:282
  59.4 6.9 %collective-permute-start.13 = (bf16[128,1024]{1,0:T(8,128)(2,1)S(1)}, bf16[128,1024]{1,0:T(8,128)(2,1)S(1)}, u32[]{:S(2)}, u32[]{:S(2)}) collective-permute-start(bf16[128,1024]{1,0:T(8,128)(2,1)S(1)} %add_convert_fusion.6), channel_id=1, source_target_pairs={{2,0},{4,2},{6,4},{7,6},{5,7},{3,5},{1,3},{0,1},{10,8},{12,10},{14... | collective-permute-start | bytes 786440 | tf_op jit(solution)/shard_map/ppermute | solution.py:246
  63.5 8.0 %collective-permute-start.18 = (bf16[128,1024]{1,0:T(8,128)(2,1)S(1)}, bf16[128,1024]{1,0:T(8,128)(2,1)S(1)}, u32[]{:S(2)}, u32[]{:S(2)}) collective-permute-start(bf16[128,1024]{1,0:T(8,128)(2,1)S(1)} %add_convert_fusion.3), channel_id=1, source_target_pairs={{0,2},{2,4},{4,6},{6,7},{7,5},{5,3},{3,1},{1,0},{8,10},{10,12},{12... | collective-permute-start | bytes 786440 | tf_op jit(solution)/shard_map/ppermute | solution.py:246
  66.4 6.4 %collective-permute-start.14 = (bf16[128,1024]{1,0:T(8,128)(2,1)S(1)}, bf16[128,1024]{1,0:T(8,128)(2,1)S(1)}, u32[]{:S(2)}, u32[]{:S(2)}) collective-permute-start(bf16[128,1024]{1,0:T(8,128)(2,1)S(1)} %add_convert_fusion.5), channel_id=1, source_target_pairs={{2,0},{4,2},{6,4},{7,6},{5,7},{3,5},{1,3},{0,1},{10,8},{12,10},{14... | collective-permute-start | bytes 786440 | tf_op jit(solution)/shard_map/ppermute | solution.py:246

commit v6 on v5

--- a/solution.py
+++ b/solution.py
@@ -13,21 +13,13 @@
 FIELD_ROWS = 8
 CHUNK = 256
 VMEM_LIMIT = 40 * 1024 * 1024
-WHOLE_VMEM = 60 * 1024 * 1024
-
-
-def pack_kernel(feat_ref, short_in, pos_in, out_ref, short_ref, pos_ref, meta_ref, sems):
-    rows, width = feat_ref.shape
-    copies = [
-        pltpu.make_async_copy(short_in, short_ref, sems.at[0]),
-        pltpu.make_async_copy(pos_in, pos_ref, sems.at[1]),
-        pltpu.make_async_copy(feat_ref, out_ref.at[pl.ds(0, rows)], sems.at[2]),
-        pltpu.make_async_copy(meta_ref, out_ref.at[pl.ds(rows, FIELD_ROWS)], sems.at[3]),
-    ]
-    for copy in copies[:3]:
-        copy.start()
-    copies[0].wait()
-    copies[1].wait()
+
+
+def pack_kernel(feat_ref, short_ref, pos_ref, a_ref, b_ref):
+    half, width = b_ref.shape
+    rows = 2 * half
+    a_ref[:half, :] = feat_ref[:half, :]
+    b_ref[...] = feat_ref[half:, :]
     short = short_ref[...]
     places = pos_ref[...] // BLOCK
     offsets = pos_ref[...] % BLOCK
@@ -40,31 +32,25 @@
     ]
     groups.append(jnp.zeros((FIELD_ROWS, width - rows * len(groups)), jnp.int32))
     meta = jnp.concatenate(groups, axis=1)
-    meta_ref[...] = meta.astype(jnp.float32).astype(jnp.bfloat16)
-    copies[3].start()
-    copies[2].wait()
-    copies[3].wait()
+    a_ref[half:, :] = meta.astype(jnp.float32).astype(jnp.bfloat16)
 
 
 def pack(features, shortlist, positives):
     rows, width = features.shape
+    half = rows // 2
     return pl.pallas_call(
         pack_kernel,
-        out_shape=jax.ShapeDtypeStruct((rows + FIELD_ROWS, width), jnp.bfloat16),
-        in_specs=[pl.BlockSpec(memory_space=pl.ANY)] * 3,
-        out_specs=pl.BlockSpec(memory_space=pl.ANY),
-        scratch_shapes=[
-            pltpu.VMEM(shortlist.shape[::-1], jnp.int32),
-            pltpu.VMEM(positives.shape[::-1], jnp.int32),
-            pltpu.VMEM((FIELD_ROWS, width), jnp.bfloat16),
-            pltpu.SemaphoreType.DMA((4,)),
+        out_shape=[
+            jax.ShapeDtypeStruct((half + FIELD_ROWS, width), jnp.bfloat16),
+            jax.ShapeDtypeStruct((half, width), jnp.bfloat16),
         ],
-        compiler_params=pltpu.CompilerParams(vmem_limit_bytes=WHOLE_VMEM),
+        in_specs=[pl.BlockSpec(memory_space=pltpu.VMEM)] * 3,
+        compiler_params=pltpu.CompilerParams(vmem_limit_bytes=VMEM_LIMIT),
         name="pack",
     )(features, shortlist.T, positives.T)
 
 
-def live_kernel(size_ref, x_ref, w_ref, live_ref):
+def live_kernel(size_ref, w_ref, live_ref):
     lane = lax.broadcasted_iota(jnp.int32, (LANES, BLOCK), 1)
     row = lax.broadcasted_iota(jnp.int32, (LANES, BLOCK), 0)
     for c in range(size_ref.shape[0]):
@@ -72,15 +58,17 @@
         live_ref[:, c * BLOCK : (c + 1) * BLOCK] = live.astype(jnp.bfloat16)
 
 
-def live_labels(cluster_sizes, block, weights):
+def live_labels(cluster_sizes, weights):
     return pl.pallas_call(
         live_kernel,
         out_shape=jax.ShapeDtypeStruct((LANES, cluster_sizes.shape[0] * BLOCK), jnp.bfloat16),
-        in_specs=[pl.BlockSpec(memory_space=pltpu.SMEM)]
-        + [pl.BlockSpec(memory_space=pltpu.VMEM)] * 2,
+        in_specs=[
+            pl.BlockSpec(memory_space=pltpu.SMEM),
+            pl.BlockSpec(memory_space=pltpu.VMEM),
+        ],
         compiler_params=pltpu.CompilerParams(vmem_limit_bytes=VMEM_LIMIT),
         name="live_labels",
-    )(cluster_sizes, block, weights)
+    )(cluster_sizes, weights)
 
 
 def block_kernel(piece_rows, top_count, pos_count, *refs):
@@ -230,20 +218,38 @@
     return lax.optimization_barrier((array, *others))[0]
 
 
+class Turn:
+    def __init__(self):
+        self.before = []
+
+    def passed(self, array):
+        self.before.append(array)
+
+    def __call__(self, array):
+        if self.before:
+            array = after(array, *self.before)
+        self.before = [array]
+        return array
+
+
 def local(features, shortlist, positives, cluster_sizes, weights):
     inst_rows, width = features.shape
     top_count, pos_count = shortlist.shape[1], positives.shape[1]
     clus_count, seq_count = lax.axis_size("clus"), lax.axis_size("seq")
     local_count = cluster_sizes.shape[0]
     part_width = width // seq_count
-    half, steps = inst_rows // 2, clus_count // 2
+    steps = clus_count // 2
+    last = steps - 1
 
     ring = list(range(0, clus_count, 2)) + list(range(1, clus_count, 2))[::-1]
-    onward = list(zip(ring, ring[1:] + ring[:1]))
-    back = [(b, a) for a, b in onward]
-
-    def send(array, pairs):
-        return lax.ppermute(array, "clus", pairs)
+    up = list(zip(ring, ring[1:] + ring[:1]))
+    down = [(b, a) for a, b in up]
+
+    def send_up(array):
+        return lax.ppermute(array, "clus", up)
+
+    def send_down(array):
+        return lax.ppermute(array, "clus", down)
 
     used, slopes = [], []
 
@@ -251,58 +257,90 @@
         grads, found = block_work(blocks, weights, live_table, top_count, pos_count)
         used.extend(blocks)
         slopes.extend(found)
-        return grads
-
-    own = pack(features, shortlist, positives)
-    live_table = live_labels(cluster_sizes, own, weights)
-    behind_x, front_x = own, own
-    parts = {}
+        return [(grads[2 * b], grads[2 * b + 1]) for b in range(len(blocks))]
+
+    own = tuple(pack(features, shortlist, positives))
+    live_table = live_labels(cluster_sizes, weights)
+    below, above = {0: own}, {0: own}
+    below_grad, above_grad = {}, {}
     for k in range(1, steps + 1):
+        here_below, here_above = below[k - 1], above[k - 1]
         if k > 1:
-            before = live_table if k == 2 else parts[k - 2][0]
-            behind_x, front_x = after(behind_x, before), after(front_x, before)
+            before = live_table if k == 2 else below_grad[k - 2][0]
+            here_below = [after(piece, before) for piece in here_below]
+            here_above = [after(piece, before) for piece in here_above]
+        a_up = send_up(here_below[0])
+        b_down = send_down(here_above[1])
         if k < steps:
-            going = behind_x, front_x
+            b_up = send_up(here_below[1])
+            a_down = send_down(here_above[0])
+            below[k], above[k] = (a_up, b_up), (a_down, b_down)
         else:
-            going = (
-                jnp.concatenate([behind_x[:half], behind_x[inst_rows:]], axis=0),
-                front_x[half:inst_rows],
-            )
-        arriving = send(going[0], onward), send(going[1], back)
+            opposite = (a_up, b_down)
         if k == 2:
-            *parts[1], own_part = take([behind_x], [front_x], [own])
+            below_grad[1], above_grad[1], own_grad = take(below[1], above[1], own)
         elif k > 2:
-            parts[k - 1] = take([behind_x], [front_x])
-        behind_x, front_x = arriving
-    to_back, to_front = take([after(behind_x, parts[steps - 1][0]), front_x])
+            below_grad[k - 1], above_grad[k - 1] = take(below[k - 1], above[k - 1])
+
+    turn = Turn()
+    b_from_above = send_down(turn(below_grad[last][1]))
+    a_from_below = send_up(turn(above_grad[last][0]))
+    (far_grad,) = take(opposite)
+    turn.passed(far_grad[0])
+    a_from_above = send_down(turn(far_grad[0]))
+    b_from_below = send_up(turn(far_grad[1]))
+    b_from_above, a_from_below = after(b_from_above, far_grad[0]), after(a_from_below, far_grad[0])
 
     scale = 1.0 / math.sqrt(inst_rows * seq_count * top_count // local_count)
 
     def seq_send(array, bit):
         return lax.ppermute(array, "seq", [(k, k ^ bit) for k in range(seq_count)])
 
-    far, near = list(range(seq_count // 2, seq_count)), list(range(seq_count // 2))
-    terms = dict(zip(far, weight_work(used, slopes, far, part_width, scale)))
-    terms.update(zip(near, weight_work(used, slopes, near, part_width, scale)))
-    terms = {q: [term] for q, term in terms.items()}
-    bit = 1
-    while bit < seq_count:
-        for q in [q for q in sorted(terms, reverse=True) if q & bit]:
+    terms = {}
+
+    def weigh(slots):
+        parts = weight_work(used, slopes, slots, part_width, scale)
+        turn.passed(parts[0])
+        terms.update({q: [part] for q, part in zip(slots, parts)})
+
+    def halve(bit, slots):
+        for q in slots:
             values = terms.pop(q)
-            terms[q ^ bit].append(seq_send(add(*values) if len(values) > 1 else values[0], bit))
-        bit *= 2
+            going = turn(add(*values) if len(values) > 1 else values[0])
+            terms[q ^ bit].append(seq_send(going, bit))
+
+    near, far = list(range(seq_count // 2)), list(range(seq_count // 2, seq_count))
+    for k in range(last, 0, -1):
+        a_down, b_up = (below_grad[k][0], a_from_above), (above_grad[k][1], b_from_below)
+        if k > 1:
+            b_down, a_up = (below_grad[k - 1][1], b_from_above), (above_grad[k - 1][0], a_from_below)
+            b_from_above = send_down(turn(add(*b_down)))
+            a_from_below = send_up(turn(add(*a_up)))
+        else:
+            turn.passed(b_from_above)
+            turn.passed(a_from_below)
+        if k == last:
+            weigh(far)
+            halve(1, far[1::2])
+        a_from_above = send_down(turn(add(*a_down)))
+        b_from_below = send_up(turn(add(*b_up)))
+        if k == last:
+            weigh(near)
+            halve(1, near[1::2])
+        if k == max(last - 1, 1):
+            bit = 2
+            while bit < seq_count:
+                halve(bit, [q for q in sorted(terms, reverse=True) if q & bit])
+                bit *= 2
     weight_grad = add(*terms[0])
 
-    for k in range(steps, 0, -1):
-        from_front, from_behind = send(to_back, back), send(to_front, onward)
-        if k == steps:
-            near_behind, near_front = parts[k - 1]
-            to_back = jnp.concatenate([add(near_behind[:half], from_front), near_behind[half:]], axis=0)
-            to_front = jnp.concatenate([near_front[:half], add(near_front[half:], from_behind)], axis=0)
-        elif k > 1:
-            near_behind, near_front = parts[k - 1]
-            to_back, to_front = add(near_behind, from_front), add(near_front, from_behind)
-    feature_grad = add(after(own_part, weight_grad), from_front, from_behind)
+    feature_grad = jnp.concatenate(
+        [
+            add(after(own_grad[0], weight_grad), a_from_above, a_from_below),
+            add(after(own_grad[1], weight_grad), b_from_above, b_from_below),
+        ],
+        axis=0,
+    )
     return (feature_grad, weight_grad)
 
 

time: 73.8 us -> 69.7 us (0.944)
  starting transfers between devices: 19.9 us -> 33.6 us
  waiting for transfers between devices: 28.1 us -> 18 us
  Pallas kernels: 19.2 us -> 10.2 us
  local copies, waits for them, and re-layouts: 3.25 us -> 4.57 us
    ppermute x16 -> x28, starting transfers between devices: 17.7 us -> 32 us  [the longest x14 18.4 us: send_up(): return lax.ppermute(array, 'clus', up)]
    pallas_call x1, Pallas kernels: 9.08 us -> 0.05 us  [pack(): pl.pallas_call(pack_kernel, out_shape=[jax.ShapeDtypeStruct((half + FIELD...]
    ppermute x16 -> x28, waiting for transfers between devices: 24.4 us -> 17.1 us  [the longest x14 10.6 us: send_up(): return lax.ppermute(array, 'clus', up)]
    ppermute x3, waiting for transfers between devices: 3.72 us -> 0.93 us  [seq_send(): return lax.ppermute(array, 'seq', [(k, k ^ bit) for k in range(seq_count)])]
    unnamed x10 -> x12, local copies, waits for them, and re-layouts: 3.21 us -> 4.57 us
    convert_element_type x9 -> x13, other arithmetic: 2.27 us -> 1.56 us  [add(): return total.astype(jnp.bfloat16)]
  transfers between devices with their start and end apart: 19 -> 31, of which waited for: 10 -> 9; matrix products, arithmetic and copies ran while one was open for 2% -> 2% of each run, Pallas kernels for 12% -> 15%
where the time goes in v6:
time: 69.7 us; the launch traced here: 69.5 us
  starting transfers between devices  33.6 us (48%)
  waiting for transfers between devices  18 us (26%)
  Pallas kernels  10.2 us (15%)
  local copies, waits for them, and re-layouts  4.57 us (7%)
  other arithmetic  2.28 us (3%)
  between operations  0.84 us (1%)
    ppermute x14, starting transfers between devices, send_up(): return lax.ppermute(array, 'clus', up)  18.4 us
    ppermute x14, starting transfers between devices, send_down(): return lax.ppermute(array, 'clus', down)  13.6 us
    ppermute x14, waiting for transfers between devices, send_up(): return lax.ppermute(array, 'clus', up)  10.6 us
    pallas_call x4, Pallas kernels, block_work(): pl.pallas_call(functools.partial(block_kernel, piece_rows, top_count, pos...  6.96 us
    ppermute x14, waiting for transfers between devices, send_down(): return lax.ppermute(array, 'clus', down)  6.5 us
    unnamed x12, local copies, waits for them, and re-layouts  4.57 us
    pallas_call x2, Pallas kernels, weight_work(): pl.pallas_call(functools.partial(weight_kernel, piece_rows, column_blocks...  2.59 us
    ppermute x3, starting transfers between devices, seq_send(): return lax.ppermute(array, 'seq', [(k, k ^ bit) for k in range(seq_count)])  1.62 us
  transfers between devices with their start and end apart: 31, of which 9 were waited for; matrix products, arithmetic and copies ran while one was open for 2% of the time, Pallas kernels for 15%

profile of v6, /device:TPU:0, one launch (start us, length us, event | category | flops | bytes accessed | tf_op | source)
XLA Modules:
  0.0 69.5 jit_solution(7551223479789683270)
XLA Ops:
  0.6 0.9 %copy-done.2 = bf16[128,1024]{1,0:T(8,128)(2,1)S(1)} copy-done((bf16[128,1024]{1,0:T(8,128)(2,1)S(1)}, bf16[128,1024]{1,0:T(8,128)(2,1)}, u32[]{:S(2)}) %copy-start.2) | copy-done | bytes 262168
  3.0 3.1 %collective-permute-start = (bf16[72,1024]{1,0:T(8,128)(2,1)S(1)}, bf16[72,1024]{1,0:T(8,128)(2,1)S(1)}, u32[]{:S(2)}, u32[]{:S(2)}) collective-permute-start(bf16[72,1024]{1,0:T(8,128)(2,1)S(1)} %get-tuple-element.62.refs_4_), channel_id=1, source_target_pairs={{0,2},{2,4},{4,6},{6,7},{7,5},{5,3},{3,1},{1,0},{8,10},{10,12},{12... | collective-permute-start | bytes 442376 | tf_op jit(solution)/shard_map/ppermute | solution.py:249
  6.1 2.0 %collective-permute-start.1 = (bf16[64,1024]{1,0:T(8,128)(2,1)S(1)}, bf16[64,1024]{1,0:T(8,128)(2,1)S(1)}, u32[]{:S(2)}, u32[]{:S(2)}) collective-permute-start(bf16[64,1024]{1,0:T(8,128)(2,1)S(1)} %get-tuple-element.63.refs_5_), channel_id=1, source_target_pairs={{0,2},{2,4},{4,6},{6,7},{7,5},{5,3},{3,1},{1,0},{8,10},{10,12},{12... | collective-permute-start | bytes 393224 | tf_op jit(solution)/shard_map/ppermute | solution.py:249
  8.1 1.6 %copy-done = bf16[1024,1024]{1,0:T(8,128)(2,1)S(1)} copy-done((bf16[1024,1024]{1,0:T(8,128)(2,1)S(1)}, bf16[1024,1024]{1,0:T(8,128)(2,1)}, u32[]{:S(2)}) %copy-start) | copy-done | bytes 2097176
  11.0 1.7 %collective-permute-done.1.refs_1_ = bf16[64,1024]{1,0:T(8,128)(2,1)S(1)} collective-permute-done((bf16[64,1024]{1,0:T(8,128)(2,1)S(1)}, bf16[64,1024]{1,0:T(8,128)(2,1)S(1)}, u32[]{:S(2)}, u32[]{:S(2)}) %collective-permute-start.1) | collective-permute-done | bytes 131104 | tf_op jit(solution)/shard_map/ppermute | solution.py:249
  12.7 1.8 %collective-permute-start.5 = (bf16[64,1024]{1,0:T(8,128)(2,1)S(1)}, bf16[64,1024]{1,0:T(8,128)(2,1)S(1)}, u32[]{:S(2)}, u32[]{:S(2)}) collective-permute-start(bf16[64,1024]{1,0:T(8,128)(2,1)S(1)} %collective-permute-done.1.refs_1_), channel_id=1, source_target_pairs={{0,2},{2,4},{4,6},{6,7},{7,5},{5,3},{3,1},{1,0},{8,10},{10,12},{12... | collective-permute-start | bytes 393224 | tf_op jit(solution)/shard_map/ppermute | solution.py:249
  14.7 1.8 %collective-permute-start.4 = (bf16[72,1024]{1,0:T(8,128)(2,1)S(1)}, bf16[72,1024]{1,0:T(8,128)(2,1)S(1)}, u32[]{:S(2)}, u32[]{:S(2)}) collective-permute-start(bf16[72,1024]{1,0:T(8,128)(2,1)S(1)} %collective-permute-done.refs_0_), channel_id=1, source_target_pairs={{0,2},{2,4},{4,6},{6,7},{7,5},{5,3},{3,1},{1,0},{8,10},{10,12},{12... | collective-permute-start | bytes 442376 | tf_op jit(solution)/shard_map/ppermute | solution.py:249
  16.7 2.4 %block_work.4 = (bf16[64,1024]{1,0:T(8,128)(2,1)S(1)}, bf16[64,1024]{1,0:T(8,128)(2,1)S(1)}, bf16[64,1024]{1,0:T(8,128)(2,1)S(1)}, bf16[64,1024]{1,0:T(8,128)(2,...) custom-call(bf16[72,1024]{1,0:T(8,128)(2,1)S(1)} %collective-permute, ...), custom_call_target="tpu_custom_call" | custom-call | flops 1610612736 | bytes 4456448 | tf_op jit(solution)/shard_map/block_work/pallas_call | solution.py:154
  19.1 1.5 %collective-permute-done.4.refs_0_.refs_6_ = bf16[72,1024]{1,0:T(8,128)(2,1)S(1)} collective-permute-done((bf16[72,1024]{1,0:T(8,128)(2,1)S(1)}, bf16[72,1024]{1,0:T(8,128)(2,1)S(1)}, u32[]{:S(2)}, u32[]{:S(2)}) %collective-permute-start.4) | collective-permute-done | bytes 147488 | tf_op jit(solution)/shard_map/ppermute | solution.py:249
  20.6 1.5 %collective-permute-start.8 = (bf16[72,1024]{1,0:T(8,128)(2,1)S(1)}, bf16[72,1024]{1,0:T(8,128)(2,1)S(1)}, u32[]{:S(2)}, u32[]{:S(2)}) collective-permute-start(bf16[72,1024]{1,0:T(8,128)(2,1)S(1)} %collective-permute-done.4.refs_0_.refs_6_), channel_id=1, source_target_pairs={{0,2},{2,4},{4,6},{6,7},{7,5},{5,3},{3,1},{1,0},{8,10},{10,12},{12... | collective-permute-start | bytes 442376 | tf_op jit(solution)/shard_map/ppermute | solution.py:249
  22.6 1.4 %collective-permute-start.11 = (bf16[64,1024]{1,0:T(8,128)(2,1)S(1)}, bf16[64,1024]{1,0:T(8,128)(2,1)S(1)}, u32[]{:S(2)}, u32[]{:S(2)}) collective-permute-start(bf16[64,1024]{1,0:T(8,128)(2,1)S(1)} %collective-permute-done.7.refs_3_.refs_9_), channel_id=1, source_target_pairs={{2,0},{4,2},{6,4},{7,6},{5,7},{3,5},{1,3},{0,1},{10,8},{12,10},{14... | collective-permute-start | bytes 393224 | tf_op jit(solution)/shard_map/ppermute | solution.py:252
  24.7 1.7 %block_work.5 = (bf16[64,1024]{1,0:T(8,128)(2,1)S(1)}, bf16[64,1024]{1,0:T(8,128)(2,1)S(1)}, bf16[64,1024]{1,0:T(8,128)(2,1)S(1)}, bf16[64,1024]{1,0:T(8,128)(2,...) custom-call(bf16[72,1024]{1,0:T(8,128)(2,1)S(1)} %collective-permute-done.4.refs_0_.refs_6_, ...), custom_call_target="tpu_custom_call" | custom-call | flops 1073741824 | bytes 3670016 | tf_op jit(solution)/shard_map/block_work/pallas_call | solution.py:154
  26.3 2.5 %collective-permute-done.11.refs_3_.refs_13_ = bf16[64,1024]{1,0:T(8,128)(2,1)S(1)} collective-permute-done((bf16[64,1024]{1,0:T(8,128)(2,1)S(1)}, bf16[64,1024]{1,0:T(8,128)(2,1)S(1)}, u32[]{:S(2)}, u32[]{:S(2)}) %collective-permute-start.11) | collective-permute-done | bytes 131104 | tf_op jit(solution)/shard_map/ppermute | solution.py:252
  29.4 1.4 %collective-permute-start.12 = (bf16[72,1024]{1,0:T(8,128)(2,1)S(1)}, bf16[72,1024]{1,0:T(8,128)(2,1)S(1)}, u32[]{:S(2)}, u32[]{:S(2)}) collective-permute-start(bf16[72,1024]{1,0:T(8,128)(2,1)S(1)} %collective-permute-done.8.refs_0_.refs_10_), channel_id=1, source_target_pairs={{0,2},{2,4},{4,6},{6,7},{7,5},{5,3},{3,1},{1,0},{8,10},{10,12},{12... | collective-permute-start | bytes 442376 | tf_op jit(solution)/shard_map/ppermute | solution.py:249
  30.9 1.7 %block_work.6 = (bf16[64,1024]{1,0:T(8,128)(2,1)S(1)}, bf16[64,1024]{1,0:T(8,128)(2,1)S(1)}, bf16[64,1024]{1,0:T(8,128)(2,1)S(1)}, bf16[64,1024]{1,0:T(8,128)(2,...) custom-call(bf16[72,1024]{1,0:T(8,128)(2,1)S(1)} %collective-permute-done.8.refs_0_.refs_10_, ...), custom_call_target="tpu_custom_call" | custom-call | flops 1073741824 | bytes 3670016 | tf_op jit(solution)/shard_map/block_work/pallas_call | solution.py:154
  33.2 1.4 %collective-permute-start.16 = (bf16[64,1024]{1,0:T(8,128)(2,1)S(1)}, bf16[64,1024]{1,0:T(8,128)(2,1)S(1)}, u32[]{:S(2)}, u32[]{:S(2)}) collective-permute-start(bf16[64,1024]{1,0:T(8,128)(2,1)S(1)} %get-tuple-element.92), channel_id=1, source_target_pairs={{0,2},{2,4},{4,6},{6,7},{7,5},{5,3},{3,1},{1,0},{8,10},{10,12},{12... | collective-permute-start | bytes 393224 | tf_op jit(solution)/shard_map/ppermute | solution.py:249
  35.6 1.2 %block_work.7 = (bf16[64,1024]{1,0:T(8,128)(2,1)S(1)}, bf16[64,1024]{1,0:T(8,128)(2,1)S(1)}, bf16[128,1024]{1,0:T(8,128)(2,1)S(1)}) custom-call(bf16[72,1024]{1,0:T(8,128)(2,1)S(1)} %collective-permute-done.12.refs_0_.refs_14_, bf16[64,1024]{1,0:T(8,128)(2,1)S(1)} %collective-permute-done.13.refs_1_.refs_15_, bf16[1024,1024]{1,0:T(8,128)(2,1)S(1)} %copy-done.1, ...), custom_call_target="tpu_custom_call" | custom-call | flops 536870912 | bytes 2883584 | tf_op jit(solution)/shard_map/block_work/pallas_call | solution.py:154
  36.8 1.6 %collective-permute-start.15 = (bf16[64,1024]{1,0:T(8,128)(2,1)S(1)}, bf16[64,1024]{1,0:T(8,128)(2,1)S(1)}, u32[]{:S(2)}, u32[]{:S(2)}) collective-permute-start(bf16[64,1024]{1,0:T(8,128)(2,1)S(1)} %get-tuple-element.93), channel_id=1, source_target_pairs={{2,0},{4,2},{6,4},{7,6},{5,7},{3,5},{1,3},{0,1},{10,8},{12,10},{14... | collective-permute-start | bytes 393224 | tf_op jit(solution)/shard_map/ppermute | solution.py:252
  39.0 1.6 %collective-permute-start.23 = (bf16[64,1024]{1,0:T(8,128)(2,1)S(1)}, bf16[64,1024]{1,0:T(8,128)(2,1)S(1)}, u32[]{:S(2)}, u32[]{:S(2)}) collective-permute-start(bf16[64,1024]{1,0:T(8,128)(2,1)S(1)} %get-tuple-element.101), channel_id=1, source_target_pairs={{2,0},{4,2},{6,4},{7,6},{5,7},{3,5},{1,3},{0,1},{10,8},{12,10},{14... | collective-permute-start | bytes 393224 | tf_op jit(solution)/shard_map/ppermute | solution.py:252
  41.0 1.3 %weight_work.3 = (bf16[1024,256]{1,0:T(8,128)(2,1)S(1)}, bf16[1024,256]{1,0:T(8,128)(2,1)S(1)}) custom-call(bf16[72,1024]{1,0:T(8,128)(2,1)S(1)} %collective-permute-done.refs_0_, bf16[64,1024]{1,0:T(8,128)(2,1)S(1)} %collective-permute-done.1.refs_1_, bf16[72,1024]{1,0:T(8,128)(2,1)S(1)} %collective-permute-done.2.refs_2_, ...), custom_call_target="tpu_custom_call" | custom-call | flops 1073741824 | bytes 4718592 | tf_op jit(solution)/shard_map/weight_work/pallas_call | solution.py:196
  42.4 1.3 %weight_work.2 = (bf16[1024,256]{1,0:T(8,128)(2,1)S(1)}, bf16[1024,256]{1,0:T(8,128)(2,1)S(1)}) custom-call(bf16[72,1024]{1,0:T(8,128)(2,1)S(1)} %collective-permute-done.refs_0_, bf16[64,1024]{1,0:T(8,128)(2,1)S(1)} %collective-permute-done.1.refs_1_, bf16[72,1024]{1,0:T(8,128)(2,1)S(1)} %collective-permute-done.2.refs_2_, ...), custom_call_target="tpu_custom_call" | custom-call | flops 1073741824 | bytes 4718592 | tf_op jit(solution)/shard_map/weight_work/pallas_call | solution.py:196
  43.8 1.6 %collective-permute-start.21 = (bf16[64,1024]{1,0:T(8,128)(2,1)S(1)}, bf16[64,1024]{1,0:T(8,128)(2,1)S(1)}, u32[]{:S(2)}, u32[]{:S(2)}) collective-permute-start(bf16[64,1024]{1,0:T(8,128)(2,1)S(1)} %add_convert_fusion.12), channel_id=1, source_target_pairs={{2,0},{4,2},{6,4},{7,6},{5,7},{3,5},{1,3},{0,1},{10,8},{12,10},{14... | collective-permute-start | bytes 393224 | tf_op jit(solution)/shard_map/ppermute | solution.py:252
  46.0 3.7 %collective-permute-done.21 = bf16[64,1024]{1,0:T(8,128)(2,1)S(1)} collective-permute-done((bf16[64,1024]{1,0:T(8,128)(2,1)S(1)}, bf16[64,1024]{1,0:T(8,128)(2,1)S(1)}, u32[]{:S(2)}, u32[]{:S(2)}) %collective-permute-start.21) | collective-permute-done | bytes 131104 | tf_op jit(solution)/shard_map/ppermute | solution.py:252
  49.7 1.6 %collective-permute-start.25 = (bf16[64,1024]{1,0:T(8,128)(2,1)S(1)}, bf16[64,1024]{1,0:T(8,128)(2,1)S(1)}, u32[]{:S(2)}, u32[]{:S(2)}) collective-permute-start(bf16[64,1024]{1,0:T(8,128)(2,1)S(1)} %add_convert_fusion.8), channel_id=1, source_target_pairs={{2,0},{4,2},{6,4},{7,6},{5,7},{3,5},{1,3},{0,1},{10,8},{12,10},{14... | collective-permute-start | bytes 393224 | tf_op jit(solution)/shard_map/ppermute | solution.py:252
  51.6 1.6 %collective-permute-start.24 = (bf16[1024,256]{1,0:T(8,128)(2,1)S(1)}, bf16[1024,256]{1,0:T(8,128)(2,1)S(1)}, u32[]{:S(2)}, u32[]{:S(2)}) collective-permute-start(bf16[1024,256]{1,0:T(8,128)(2,1)S(1)} %add_convert_fusion.1), channel_id=1, source_target_pairs={{0,16},{8,24},{16,0},{24,8},{1,17},{9,25},{17,1},{25,9},{2,18},{10... | collective-permute-start | bytes 1572872 | tf_op jit(solution)/shard_map/ppermute | solution.py:297
  53.1 1.6 %collective-permute-start.26 = (bf16[64,1024]{1,0:T(8,128)(2,1)S(1)}, bf16[64,1024]{1,0:T(8,128)(2,1)S(1)}, u32[]{:S(2)}, u32[]{:S(2)}) collective-permute-start(bf16[64,1024]{1,0:T(8,128)(2,1)S(1)} %add_convert_fusion.6), channel_id=1, source_target_pairs={{2,0},{4,2},{6,4},{7,6},{5,7},{3,5},{1,3},{0,1},{10,8},{12,10},{14... | collective-permute-start | bytes 393224 | tf_op jit(solution)/shard_map/ppermute | solution.py:252
  55.4 2.6 %collective-permute-start.29 = (bf16[64,1024]{1,0:T(8,128)(2,1)S(1)}, bf16[64,1024]{1,0:T(8,128)(2,1)S(1)}, u32[]{:S(2)}, u32[]{:S(2)}) collective-permute-start(bf16[64,1024]{1,0:T(8,128)(2,1)S(1)} %add_convert_fusion.9), channel_id=1, source_target_pairs={{0,2},{2,4},{4,6},{6,7},{7,5},{5,3},{3,1},{1,0},{8,10},{10,12},{12... | collective-permute-start | bytes 393224 | tf_op jit(solution)/shard_map/ppermute | solution.py:249
  58.1 3.7 %collective-permute-done.29 = bf16[64,1024]{1,0:T(8,128)(2,1)S(1)} collective-permute-done((bf16[64,1024]{1,0:T(8,128)(2,1)S(1)}, bf16[64,1024]{1,0:T(8,128)(2,1)S(1)}, u32[]{:S(2)}, u32[]{:S(2)}) %collective-permute-start.29) | collective-permute-done | bytes 131104 | tf_op jit(solution)/shard_map/ppermute | solution.py:249
  61.9 1.8 %collective-permute-start.28 = (bf16[64,1024]{1,0:T(8,128)(2,1)S(1)}, bf16[64,1024]{1,0:T(8,128)(2,1)S(1)}, u32[]{:S(2)}, u32[]{:S(2)}) collective-permute-start(bf16[64,1024]{1,0:T(8,128)(2,1)S(1)} %add_convert_fusion.5), channel_id=1, source_target_pairs={{2,0},{4,2},{6,4},{7,6},{5,7},{3,5},{1,3},{0,1},{10,8},{12,10},{14... | collective-permute-start | bytes 393224 | tf_op jit(solution)/shard_map/ppermute | solution.py:252
  64.0 0.9 %collective-permute-done.24 = bf16[1024,256]{1,0:T(8,128)(2,1)S(1)} collective-permute-done((bf16[1024,256]{1,0:T(8,128)(2,1)S(1)}, bf16[1024,256]{1,0:T(8,128)(2,1)S(1)}, u32[]{:S(2)}, u32[]{:S(2)}) %collective-permute-start.24) | collective-permute-done | bytes 524320 | tf_op jit(solution)/shard_map/ppermute | solution.py:297
  64.9 1.0 %add_convert_fusion = bf16[1024,256]{1,0:T(8,128)(2,1)} fusion(bf16[1024,256]{1,0:T(8,128)(2,1)S(1)} %collective-permute-done.24, bf16[1024,256]{1,0:T(8,128)(2,1)S(1)} %collective-permute-done.18, bf16[1024,256]{1,0:T(8,128)(2,1)S(1)} %get-tuple-element.85), kind=kLoop, calls=%fused_computation | loop fusion | flops 1572864 | bytes 2097152 | tf_op jit(solution)/shard_map/convert_element_type | solution.py:214
  65.9 2.8 %collective-permute-done.30 = bf16[64,1024]{1,0:T(8,128)(2,1)S(1)} collective-permute-done((bf16[64,1024]{1,0:T(8,128)(2,1)S(1)}, bf16[64,1024]{1,0:T(8,128)(2,1)S(1)}, u32[]{:S(2)}, u32[]{:S(2)}) %collective-permute-start.30) | collective-permute-done | bytes 131104 | tf_op jit(solution)/shard_map/ppermute | solution.py:249
  (64 shorter events, 10.3 us)
Async XLA Ops:
  3.0 11.7 %collective-permute-start = (bf16[72,1024]{1,0:T(8,128)(2,1)S(1)}, bf16[72,1024]{1,0:T(8,128)(2,1)S(1)}, u32[]{:S(2)}, u32[]{:S(2)}) collective-permute-start(bf16[72,1024]{1,0:T(8,128)(2,1)S(1)} %get-tuple-element.62.refs_4_), channel_id=1, source_target_pairs={{0,2},{2,4},{4,6},{6,7},{7,5},{5,3},{3,1},{1,0},{8,10},{10,12},{12... | collective-permute-start | bytes 442376 | tf_op jit(solution)/shard_map/ppermute | solution.py:249
  6.1 10.4 %collective-permute-start.2 = (bf16[72,1024]{1,0:T(8,128)(2,1)S(1)}, bf16[72,1024]{1,0:T(8,128)(2,1)S(1)}, u32[]{:S(2)}, u32[]{:S(2)}) collective-permute-start(bf16[72,1024]{1,0:T(8,128)(2,1)S(1)} %get-tuple-element.62.refs_4_), channel_id=1, source_target_pairs={{2,0},{4,2},{6,4},{7,6},{5,7},{3,5},{1,3},{0,1},{10,8},{12,10},{14... | collective-permute-start | bytes 442376 | tf_op jit(solution)/shard_map/ppermute | solution.py:252
  6.1 6.6 %collective-permute-start.1 = (bf16[64,1024]{1,0:T(8,128)(2,1)S(1)}, bf16[64,1024]{1,0:T(8,128)(2,1)S(1)}, u32[]{:S(2)}, u32[]{:S(2)}) collective-permute-start(bf16[64,1024]{1,0:T(8,128)(2,1)S(1)} %get-tuple-element.63.refs_5_), channel_id=1, source_target_pairs={{0,2},{2,4},{4,6},{6,7},{7,5},{5,3},{3,1},{1,0},{8,10},{10,12},{12... | collective-permute-start | bytes 393224 | tf_op jit(solution)/shard_map/ppermute | solution.py:249
  8.1 6.4 %collective-permute-start.3 = (bf16[64,1024]{1,0:T(8,128)(2,1)S(1)}, bf16[64,1024]{1,0:T(8,128)(2,1)S(1)}, u32[]{:S(2)}, u32[]{:S(2)}) collective-permute-start(bf16[64,1024]{1,0:T(8,128)(2,1)S(1)} %get-tuple-element.63.refs_5_), channel_id=1, source_target_pairs={{2,0},{4,2},{6,4},{7,6},{5,7},{3,5},{1,3},{0,1},{10,8},{12,10},{14... | collective-permute-start | bytes 393224 | tf_op jit(solution)/shard_map/ppermute | solution.py:252
  10.4 6.4 %copy-start.1 = (bf16[1024,1024]{1,0:T(8,128)(2,1)S(1)}, bf16[1024,1024]{1,0:T(8,128)(2,1)}, u32[]{:S(2)}) copy-start(bf16[1024,1024]{1,0:T(8,128)(2,1)} %refs_2_.1) | copy-start | bytes 6291460
  12.7 11.4 %collective-permute-start.5 = (bf16[64,1024]{1,0:T(8,128)(2,1)S(1)}, bf16[64,1024]{1,0:T(8,128)(2,1)S(1)}, u32[]{:S(2)}, u32[]{:S(2)}) collective-permute-start(bf16[64,1024]{1,0:T(8,128)(2,1)S(1)} %collective-permute-done.1.refs_1_), channel_id=1, source_target_pairs={{0,2},{2,4},{4,6},{6,7},{7,5},{5,3},{3,1},{1,0},{8,10},{10,12},{12... | collective-permute-start | bytes 393224 | tf_op jit(solution)/shard_map/ppermute | solution.py:249
  14.5 8.1 %collective-permute-start.7 = (bf16[64,1024]{1,0:T(8,128)(2,1)S(1)}, bf16[64,1024]{1,0:T(8,128)(2,1)S(1)}, u32[]{:S(2)}, u32[]{:S(2)}) collective-permute-start(bf16[64,1024]{1,0:T(8,128)(2,1)S(1)} %collective-permute-done.3.refs_3_), channel_id=1, source_target_pairs={{2,0},{4,2},{6,4},{7,6},{5,7},{3,5},{1,3},{0,1},{10,8},{12,10},{14... | collective-permute-start | bytes 393224 | tf_op jit(solution)/shard_map/ppermute | solution.py:252
  14.7 5.9 %collective-permute-start.4 = (bf16[72,1024]{1,0:T(8,128)(2,1)S(1)}, bf16[72,1024]{1,0:T(8,128)(2,1)S(1)}, u32[]{:S(2)}, u32[]{:S(2)}) collective-permute-start(bf16[72,1024]{1,0:T(8,128)(2,1)S(1)} %collective-permute-done.refs_0_), channel_id=1, source_target_pairs={{0,2},{2,4},{4,6},{6,7},{7,5},{5,3},{3,1},{1,0},{8,10},{10,12},{12... | collective-permute-start | bytes 442376 | tf_op jit(solution)/shard_map/ppermute | solution.py:249
  16.5 5.6 %collective-permute-start.6 = (bf16[72,1024]{1,0:T(8,128)(2,1)S(1)}, bf16[72,1024]{1,0:T(8,128)(2,1)S(1)}, u32[]{:S(2)}, u32[]{:S(2)}) collective-permute-start(bf16[72,1024]{1,0:T(8,128)(2,1)S(1)} %collective-permute-done.2.refs_2_), channel_id=1, source_target_pairs={{2,0},{4,2},{6,4},{7,6},{5,7},{3,5},{1,3},{0,1},{10,8},{12,10},{14... | collective-permute-start | bytes 442376 | tf_op jit(solution)/shard_map/ppermute | solution.py:252
  20.6 8.9 %collective-permute-start.8 = (bf16[72,1024]{1,0:T(8,128)(2,1)S(1)}, bf16[72,1024]{1,0:T(8,128)(2,1)S(1)}, u32[]{:S(2)}, u32[]{:S(2)}) collective-permute-start(bf16[72,1024]{1,0:T(8,128)(2,1)S(1)} %collective-permute-done.4.refs_0_.refs_6_), channel_id=1, source_target_pairs={{0,2},{2,4},{4,6},{6,7},{7,5},{5,3},{3,1},{1,0},{8,10},{10,12},{12... | collective-permute-start | bytes 442376 | tf_op jit(solution)/shard_map/ppermute | solution.py:249
  22.1 8.8 %collective-permute-start.10 = (bf16[72,1024]{1,0:T(8,128)(2,1)S(1)}, bf16[72,1024]{1,0:T(8,128)(2,1)S(1)}, u32[]{:S(2)}, u32[]{:S(2)}) collective-permute-start(bf16[72,1024]{1,0:T(8,128)(2,1)S(1)} %collective-permute-done.6.refs_2_.refs_8_), channel_id=1, source_target_pairs={{2,0},{4,2},{6,4},{7,6},{5,7},{3,5},{1,3},{0,1},{10,8},{12,10},{14... | collective-permute-start | bytes 442376 | tf_op jit(solution)/shard_map/ppermute | solution.py:252
  22.6 6.2 %collective-permute-start.11 = (bf16[64,1024]{1,0:T(8,128)(2,1)S(1)}, bf16[64,1024]{1,0:T(8,128)(2,1)S(1)}, u32[]{:S(2)}, u32[]{:S(2)}) collective-permute-start(bf16[64,1024]{1,0:T(8,128)(2,1)S(1)} %collective-permute-done.7.refs_3_.refs_9_), channel_id=1, source_target_pairs={{2,0},{4,2},{6,4},{7,6},{5,7},{3,5},{1,3},{0,1},{10,8},{12,10},{14... | collective-permute-start | bytes 393224 | tf_op jit(solution)/shard_map/ppermute | solution.py:252
  24.1 6.8 %collective-permute-start.9 = (bf16[64,1024]{1,0:T(8,128)(2,1)S(1)}, bf16[64,1024]{1,0:T(8,128)(2,1)S(1)}, u32[]{:S(2)}, u32[]{:S(2)}) collective-permute-start(bf16[64,1024]{1,0:T(8,128)(2,1)S(1)} %collective-permute-done.5.refs_1_.refs_7_), channel_id=1, source_target_pairs={{0,2},{2,4},{4,6},{6,7},{7,5},{5,3},{3,1},{1,0},{8,10},{10,12},{12... | collective-permute-start | bytes 393224 | tf_op jit(solution)/shard_map/ppermute | solution.py:249
  28.9 5.8 %collective-permute-start.13 = (bf16[64,1024]{1,0:T(8,128)(2,1)S(1)}, bf16[64,1024]{1,0:T(8,128)(2,1)S(1)}, u32[]{:S(2)}, u32[]{:S(2)}) collective-permute-start(bf16[64,1024]{1,0:T(8,128)(2,1)S(1)} %collective-permute-done.11.refs_3_.refs_13_), channel_id=1, source_target_pairs={{2,0},{4,2},{6,4},{7,6},{5,7},{3,5},{1,3},{0,1},{10,8},{12,10},{14... | collective-permute-start | bytes 393224 | tf_op jit(solution)/shard_map/ppermute | solution.py:252
  29.4 6.1 %collective-permute-start.12 = (bf16[72,1024]{1,0:T(8,128)(2,1)S(1)}, bf16[72,1024]{1,0:T(8,128)(2,1)S(1)}, u32[]{:S(2)}, u32[]{:S(2)}) collective-permute-start(bf16[72,1024]{1,0:T(8,128)(2,1)S(1)} %collective-permute-done.8.refs_0_.refs_10_), channel_id=1, source_target_pairs={{0,2},{2,4},{4,6},{6,7},{7,5},{5,3},{3,1},{1,0},{8,10},{10,12},{12... | collective-permute-start | bytes 442376 | tf_op jit(solution)/shard_map/ppermute | solution.py:249
  32.6 6.3 %collective-permute-start.17 = (bf16[64,1024]{1,0:T(8,128)(2,1)S(1)}, bf16[64,1024]{1,0:T(8,128)(2,1)S(1)}, u32[]{:S(2)}, u32[]{:S(2)}) collective-permute-start(bf16[64,1024]{1,0:T(8,128)(2,1)S(1)} %get-tuple-element.91), channel_id=1, source_target_pairs={{2,0},{4,2},{6,4},{7,6},{5,7},{3,5},{1,3},{0,1},{10,8},{12,10},{14... | collective-permute-start | bytes 393224 | tf_op jit(solution)/shard_map/ppermute | solution.py:252
  33.2 5.6 %collective-permute-start.16 = (bf16[64,1024]{1,0:T(8,128)(2,1)S(1)}, bf16[64,1024]{1,0:T(8,128)(2,1)S(1)}, u32[]{:S(2)}, u32[]{:S(2)}) collective-permute-start(bf16[64,1024]{1,0:T(8,128)(2,1)S(1)} %get-tuple-element.92), channel_id=1, source_target_pairs={{0,2},{2,4},{4,6},{6,7},{7,5},{5,3},{3,1},{1,0},{8,10},{10,12},{12... | collective-permute-start | bytes 393224 | tf_op jit(solution)/shard_map/ppermute | solution.py:249
  36.8 6.9 %collective-permute-start.15 = (bf16[64,1024]{1,0:T(8,128)(2,1)S(1)}, bf16[64,1024]{1,0:T(8,128)(2,1)S(1)}, u32[]{:S(2)}, u32[]{:S(2)}) collective-permute-start(bf16[64,1024]{1,0:T(8,128)(2,1)S(1)} %get-tuple-element.93), channel_id=1, source_target_pairs={{2,0},{4,2},{6,4},{7,6},{5,7},{3,5},{1,3},{0,1},{10,8},{12,10},{14... | collective-permute-start | bytes 393224 | tf_op jit(solution)/shard_map/ppermute | solution.py:252
  38.4 7.0 %collective-permute-start.14 = (bf16[64,1024]{1,0:T(8,128)(2,1)S(1)}, bf16[64,1024]{1,0:T(8,128)(2,1)S(1)}, u32[]{:S(2)}, u32[]{:S(2)}) collective-permute-start(bf16[64,1024]{1,0:T(8,128)(2,1)S(1)} %get-tuple-element.94), channel_id=1, source_target_pairs={{0,2},{2,4},{4,6},{6,7},{7,5},{5,3},{3,1},{1,0},{8,10},{10,12},{12... | collective-permute-start | bytes 393224 | tf_op jit(solution)/shard_map/ppermute | solution.py:249
  39.0 7.0 %collective-permute-start.23 = (bf16[64,1024]{1,0:T(8,128)(2,1)S(1)}, bf16[64,1024]{1,0:T(8,128)(2,1)S(1)}, u32[]{:S(2)}, u32[]{:S(2)}) collective-permute-start(bf16[64,1024]{1,0:T(8,128)(2,1)S(1)} %get-tuple-element.101), channel_id=1, source_target_pairs={{2,0},{4,2},{6,4},{7,6},{5,7},{3,5},{1,3},{0,1},{10,8},{12,10},{14... | collective-permute-start | bytes 393224 | tf_op jit(solution)/shard_map/ppermute | solution.py:252
  40.6 5.3 %collective-permute-start.22 = (bf16[64,1024]{1,0:T(8,128)(2,1)S(1)}, bf16[64,1024]{1,0:T(8,128)(2,1)S(1)}, u32[]{:S(2)}, u32[]{:S(2)}) collective-permute-start(bf16[64,1024]{1,0:T(8,128)(2,1)S(1)} %get-tuple-element.102), channel_id=1, source_target_pairs={{0,2},{2,4},{4,6},{6,7},{7,5},{5,3},{3,1},{1,0},{8,10},{10,12},{12... | collective-permute-start | bytes 393224 | tf_op jit(solution)/shard_map/ppermute | solution.py:249
  42.3 9.1 %collective-permute-start.19 = (bf16[1024,256]{1,0:T(8,128)(2,1)S(1)}, bf16[1024,256]{1,0:T(8,128)(2,1)S(1)}, u32[]{:S(2)}, u32[]{:S(2)}) collective-permute-start(bf16[1024,256]{1,0:T(8,128)(2,1)S(1)} %get-tuple-element.104), channel_id=1, source_target_pairs={{0,8},{8,0},{16,24},{24,16},{1,9},{9,1},{17,25},{25,17},{2,10},{10... | collective-permute-start | bytes 1572872 | tf_op jit(solution)/shard_map/ppermute | solution.py:297
  43.8 5.9 %collective-permute-start.21 = (bf16[64,1024]{1,0:T(8,128)(2,1)S(1)}, bf16[64,1024]{1,0:T(8,128)(2,1)S(1)}, u32[]{:S(2)}, u32[]{:S(2)}) collective-permute-start(bf16[64,1024]{1,0:T(8,128)(2,1)S(1)} %add_convert_fusion.12), channel_id=1, source_target_pairs={{2,0},{4,2},{6,4},{7,6},{5,7},{3,5},{1,3},{0,1},{10,8},{12,10},{14... | collective-permute-start | bytes 393224 | tf_op jit(solution)/shard_map/ppermute | solution.py:252
  45.4 5.9 %collective-permute-start.20 = (bf16[64,1024]{1,0:T(8,128)(2,1)S(1)}, bf16[64,1024]{1,0:T(8,128)(2,1)S(1)}, u32[]{:S(2)}, u32[]{:S(2)}) collective-permute-start(bf16[64,1024]{1,0:T(8,128)(2,1)S(1)} %add_convert_fusion.13), channel_id=1, source_target_pairs={{0,2},{2,4},{4,6},{6,7},{7,5},{5,3},{3,1},{1,0},{8,10},{10,12},{12... | collective-permute-start | bytes 393224 | tf_op jit(solution)/shard_map/ppermute | solution.py:249
  45.9 18.0 %collective-permute-start.18 = (bf16[1024,256]{1,0:T(8,128)(2,1)S(1)}, bf16[1024,256]{1,0:T(8,128)(2,1)S(1)}, u32[]{:S(2)}, u32[]{:S(2)}) collective-permute-start(bf16[1024,256]{1,0:T(8,128)(2,1)S(1)} %get-tuple-element.107), channel_id=1, source_target_pairs={{0,8},{8,0},{16,24},{24,16},{1,9},{9,1},{17,25},{25,17},{2,10},{10... | collective-permute-start | bytes 1572872 | tf_op jit(solution)/shard_map/ppermute | solution.py:297
  49.7 5.7 %collective-permute-start.25 = (bf16[64,1024]{1,0:T(8,128)(2,1)S(1)}, bf16[64,1024]{1,0:T(8,128)(2,1)S(1)}, u32[]{:S(2)}, u32[]{:S(2)}) collective-permute-start(bf16[64,1024]{1,0:T(8,128)(2,1)S(1)} %add_convert_fusion.8), channel_id=1, source_target_pairs={{2,0},{4,2},{6,4},{7,6},{5,7},{3,5},{1,3},{0,1},{10,8},{12,10},{14... | collective-permute-start | bytes 393224 | tf_op jit(solution)/shard_map/ppermute | solution.py:252
  51.6 13.3 %collective-permute-start.24 = (bf16[1024,256]{1,0:T(8,128)(2,1)S(1)}, bf16[1024,256]{1,0:T(8,128)(2,1)S(1)}, u32[]{:S(2)}, u32[]{:S(2)}) collective-permute-start(bf16[1024,256]{1,0:T(8,128)(2,1)S(1)} %add_convert_fusion.1), channel_id=1, source_target_pairs={{0,16},{8,24},{16,0},{24,8},{1,17},{9,25},{17,1},{25,9},{2,18},{10... | collective-permute-start | bytes 1572872 | tf_op jit(solution)/shard_map/ppermute | solution.py:297
  53.1 8.7 %collective-permute-start.26 = (bf16[64,1024]{1,0:T(8,128)(2,1)S(1)}, bf16[64,1024]{1,0:T(8,128)(2,1)S(1)}, u32[]{:S(2)}, u32[]{:S(2)}) collective-permute-start(bf16[64,1024]{1,0:T(8,128)(2,1)S(1)} %add_convert_fusion.6), channel_id=1, source_target_pairs={{2,0},{4,2},{6,4},{7,6},{5,7},{3,5},{1,3},{0,1},{10,8},{12,10},{14... | collective-permute-start | bytes 393224 | tf_op jit(solution)/shard_map/ppermute | solution.py:252
  54.7 7.2 %collective-permute-start.27 = (bf16[64,1024]{1,0:T(8,128)(2,1)S(1)}, bf16[64,1024]{1,0:T(8,128)(2,1)S(1)}, u32[]{:S(2)}, u32[]{:S(2)}) collective-permute-start(bf16[64,1024]{1,0:T(8,128)(2,1)S(1)} %add_convert_fusion.7), channel_id=1, source_target_pairs={{0,2},{2,4},{4,6},{6,7},{7,5},{5,3},{3,1},{1,0},{8,10},{10,12},{12... | collective-permute-start | bytes 393224 | tf_op jit(solution)/shard_map/ppermute | solution.py:249
  55.4 6.4 %collective-permute-start.29 = (bf16[64,1024]{1,0:T(8,128)(2,1)S(1)}, bf16[64,1024]{1,0:T(8,128)(2,1)S(1)}, u32[]{:S(2)}, u32[]{:S(2)}) collective-permute-start(bf16[64,1024]{1,0:T(8,128)(2,1)S(1)} %add_convert_fusion.9), channel_id=1, source_target_pairs={{0,2},{2,4},{4,6},{6,7},{7,5},{5,3},{3,1},{1,0},{8,10},{10,12},{12... | collective-permute-start | bytes 393224 | tf_op jit(solution)/shard_map/ppermute | solution.py:249
  61.9 6.8 %collective-permute-start.28 = (bf16[64,1024]{1,0:T(8,128)(2,1)S(1)}, bf16[64,1024]{1,0:T(8,128)(2,1)S(1)}, u32[]{:S(2)}, u32[]{:S(2)}) collective-permute-start(bf16[64,1024]{1,0:T(8,128)(2,1)S(1)} %add_convert_fusion.5), channel_id=1, source_target_pairs={{2,0},{4,2},{6,4},{7,6},{5,7},{3,5},{1,3},{0,1},{10,8},{12,10},{14... | collective-permute-start | bytes 393224 | tf_op jit(solution)/shard_map/ppermute | solution.py:252
  63.7 5.0 %collective-permute-start.30 = (bf16[64,1024]{1,0:T(8,128)(2,1)S(1)}, bf16[64,1024]{1,0:T(8,128)(2,1)S(1)}, u32[]{:S(2)}, u32[]{:S(2)}) collective-permute-start(bf16[64,1024]{1,0:T(8,128)(2,1)S(1)} %add_convert_fusion.3), channel_id=1, source_target_pairs={{0,2},{2,4},{4,6},{6,7},{7,5},{5,3},{3,1},{1,0},{8,10},{10,12},{12... | collective-permute-start | bytes 393224 | tf_op jit(solution)/shard_map/ppermute | solution.py:249
  (5 other events, 4.6 us)

commit v7 on v5

--- a/solution.py
+++ b/solution.py
@@ -13,21 +13,11 @@
 FIELD_ROWS = 8
 CHUNK = 256
 VMEM_LIMIT = 40 * 1024 * 1024
-WHOLE_VMEM = 60 * 1024 * 1024
-
-
-def pack_kernel(feat_ref, short_in, pos_in, out_ref, short_ref, pos_ref, meta_ref, sems):
+
+
+def pack_kernel(feat_ref, short_ref, pos_ref, out_ref):
     rows, width = feat_ref.shape
-    copies = [
-        pltpu.make_async_copy(short_in, short_ref, sems.at[0]),
-        pltpu.make_async_copy(pos_in, pos_ref, sems.at[1]),
-        pltpu.make_async_copy(feat_ref, out_ref.at[pl.ds(0, rows)], sems.at[2]),
-        pltpu.make_async_copy(meta_ref, out_ref.at[pl.ds(rows, FIELD_ROWS)], sems.at[3]),
-    ]
-    for copy in copies[:3]:
-        copy.start()
-    copies[0].wait()
-    copies[1].wait()
+    out_ref[:rows, :] = feat_ref[...]
     short = short_ref[...]
     places = pos_ref[...] // BLOCK
     offsets = pos_ref[...] % BLOCK
@@ -40,10 +30,7 @@
     ]
     groups.append(jnp.zeros((FIELD_ROWS, width - rows * len(groups)), jnp.int32))
     meta = jnp.concatenate(groups, axis=1)
-    meta_ref[...] = meta.astype(jnp.float32).astype(jnp.bfloat16)
-    copies[3].start()
-    copies[2].wait()
-    copies[3].wait()
+    out_ref[rows:, :] = meta.astype(jnp.float32).astype(jnp.bfloat16)
 
 
 def pack(features, shortlist, positives):
@@ -51,20 +38,13 @@
     return pl.pallas_call(
         pack_kernel,
         out_shape=jax.ShapeDtypeStruct((rows + FIELD_ROWS, width), jnp.bfloat16),
-        in_specs=[pl.BlockSpec(memory_space=pl.ANY)] * 3,
-        out_specs=pl.BlockSpec(memory_space=pl.ANY),
-        scratch_shapes=[
-            pltpu.VMEM(shortlist.shape[::-1], jnp.int32),
-            pltpu.VMEM(positives.shape[::-1], jnp.int32),
-            pltpu.VMEM((FIELD_ROWS, width), jnp.bfloat16),
-            pltpu.SemaphoreType.DMA((4,)),
-        ],
-        compiler_params=pltpu.CompilerParams(vmem_limit_bytes=WHOLE_VMEM),
+        in_specs=[pl.BlockSpec(memory_space=pltpu.VMEM)] * 3,
+        compiler_params=pltpu.CompilerParams(vmem_limit_bytes=VMEM_LIMIT),
         name="pack",
     )(features, shortlist.T, positives.T)
 
 
-def live_kernel(size_ref, x_ref, w_ref, live_ref):
+def live_kernel(size_ref, w_ref, live_ref):
     lane = lax.broadcasted_iota(jnp.int32, (LANES, BLOCK), 1)
     row = lax.broadcasted_iota(jnp.int32, (LANES, BLOCK), 0)
     for c in range(size_ref.shape[0]):
@@ -72,15 +52,15 @@
         live_ref[:, c * BLOCK : (c + 1) * BLOCK] = live.astype(jnp.bfloat16)
 
 
-def live_labels(cluster_sizes, block, weights):
+def live_labels(cluster_sizes, weights):
     return pl.pallas_call(
         live_kernel,
         out_shape=jax.ShapeDtypeStruct((LANES, cluster_sizes.shape[0] * BLOCK), jnp.bfloat16),
         in_specs=[pl.BlockSpec(memory_space=pltpu.SMEM)]
-        + [pl.BlockSpec(memory_space=pltpu.VMEM)] * 2,
+        + [pl.BlockSpec(memory_space=pltpu.VMEM)],
         compiler_params=pltpu.CompilerParams(vmem_limit_bytes=VMEM_LIMIT),
         name="live_labels",
-    )(cluster_sizes, block, weights)
+    )(cluster_sizes, weights)
 
 
 def block_kernel(piece_rows, top_count, pos_count, *refs):
@@ -88,8 +68,8 @@
     piece_count = sum(len(pieces) for pieces in piece_rows)
     x_refs = refs[:piece_count]
     w_ref, live_ref = refs[piece_count : piece_count + 2]
-    grad_refs = refs[piece_count + 2 : 2 * piece_count + 2]
-    slope_refs = refs[2 * piece_count + 2 :]
+    grad_refs = refs[piece_count + 2 : piece_count + 2 + 2 * block_count]
+    slope_refs = refs[piece_count + 2 + 2 * block_count :]
     labels, width = w_ref.shape
     local_count = labels // BLOCK
     rows = slope_refs[0].shape[0]
@@ -163,9 +143,10 @@
         for pieces in blocks
     ]
     flat_rows = sum(piece_rows, [])
+    half = sum(piece_rows[0]) // 2
     out = pl.pallas_call(
         functools.partial(block_kernel, piece_rows, top_count, pos_count),
-        out_shape=[jax.ShapeDtypeStruct((rows, width), jnp.bfloat16) for rows in flat_rows]
+        out_shape=[jax.ShapeDtypeStruct((half, width), jnp.bfloat16)] * (2 * len(blocks))
         + [jax.ShapeDtypeStruct((sum(rows), labels), jnp.bfloat16) for rows in piece_rows],
         in_specs=[pl.BlockSpec(memory_space=pltpu.VMEM)] * (len(flat_rows) + 2),
         compiler_params=pltpu.CompilerParams(vmem_limit_bytes=VMEM_LIMIT),
@@ -176,7 +157,8 @@
         ),
         name="block_work",
     )(*[piece for pieces in blocks for piece in pieces], weights, live_table)
-    return list(out[: len(flat_rows)]), list(out[len(flat_rows) :])
+    grads = [(out[2 * b], out[2 * b + 1]) for b in range(len(blocks))]
+    return grads, list(out[2 * len(blocks) :])
 
 
 def weight_kernel(piece_rows, column_blocks, scale, *refs):
@@ -239,11 +221,14 @@
     half, steps = inst_rows // 2, clus_count // 2
 
     ring = list(range(0, clus_count, 2)) + list(range(1, clus_count, 2))[::-1]
-    onward = list(zip(ring, ring[1:] + ring[:1]))
-    back = [(b, a) for a, b in onward]
-
-    def send(array, pairs):
-        return lax.ppermute(array, "clus", pairs)
+    up = list(zip(ring, ring[1:] + ring[:1]))
+    down = [(b, a) for a, b in up]
+
+    def send_up(array):
+        return lax.ppermute(array, "clus", up)
+
+    def send_down(array):
+        return lax.ppermute(array, "clus", down)
 
     used, slopes = [], []
 
@@ -254,27 +239,37 @@
         return grads
 
     own = pack(features, shortlist, positives)
-    live_table = live_labels(cluster_sizes, own, weights)
-    behind_x, front_x = own, own
-    parts = {}
+    live_table = live_labels(cluster_sizes, weights)
+    (own_grad,) = take([own])
+    below, above = own, own
+    below_grad, above_grad = {}, {}
+    sum_up = sum_down = None
+
+    def advance(j):
+        nonlocal sum_up, sum_down
+        first = below_grad[j][0] if j in below_grad else above_grad[clus_count - j][0]
+        second = above_grad[j][1] if j in above_grad else below_grad[clus_count - j][1]
+        if sum_up is not None:
+            first, second = add(first, sum_up), add(second, sum_down)
+        sum_up, sum_down = send_up(first), send_down(second)
+
     for k in range(1, steps + 1):
         if k > 1:
-            before = live_table if k == 2 else parts[k - 2][0]
-            behind_x, front_x = after(behind_x, before), after(front_x, before)
+            before = own_grad[0] if k == 2 else below_grad[k - 2][0]
+            below, above = after(below, before), after(above, before)
         if k < steps:
-            going = behind_x, front_x
+            arriving = send_up(below), send_down(above)
         else:
-            going = (
-                jnp.concatenate([behind_x[:half], behind_x[inst_rows:]], axis=0),
-                front_x[half:inst_rows],
-            )
-        arriving = send(going[0], onward), send(going[1], back)
-        if k == 2:
-            *parts[1], own_part = take([behind_x], [front_x], [own])
-        elif k > 2:
-            parts[k - 1] = take([behind_x], [front_x])
-        behind_x, front_x = arriving
-    to_back, to_front = take([after(behind_x, parts[steps - 1][0]), front_x])
+            ends = jnp.concatenate([below[:half], below[inst_rows:]], axis=0)
+            opposite = [send_up(ends), send_down(above[half:inst_rows])]
+        if k > 1:
+            below_grad[k - 1], above_grad[k - 1] = take([below], [above])
+            advance(k - 1)
+        if k < steps:
+            below, above = arriving
+    (far_grad,) = take([after(opposite[0], below_grad[steps - 1][0]), opposite[1]])
+    below_grad[steps] = above_grad[steps] = far_grad
+    advance(steps)
 
     scale = 1.0 / math.sqrt(inst_rows * seq_count * top_count // local_count)
 
@@ -283,26 +278,26 @@
 
     far, near = list(range(seq_count // 2, seq_count)), list(range(seq_count // 2))
     terms = dict(zip(far, weight_work(used, slopes, far, part_width, scale)))
+    sum_up, sum_down = after(sum_up, terms[far[0]]), after(sum_down, terms[far[0]])
+    advance(steps + 1)
     terms.update(zip(near, weight_work(used, slopes, near, part_width, scale)))
     terms = {q: [term] for q, term in terms.items()}
     bit = 1
     while bit < seq_count:
         for q in [q for q in sorted(terms, reverse=True) if q & bit]:
             values = terms.pop(q)
-            terms[q ^ bit].append(seq_send(add(*values) if len(values) > 1 else values[0], bit))
+            going = add(*values) if len(values) > 1 else values[0]
+            if bit == 2:
+                sum_up, sum_down = after(sum_up, going), after(sum_down, going)
+            terms[q ^ bit].append(seq_send(going, bit))
         bit *= 2
     weight_grad = add(*terms[0])
 
-    for k in range(steps, 0, -1):
-        from_front, from_behind = send(to_back, back), send(to_front, onward)
-        if k == steps:
-            near_behind, near_front = parts[k - 1]
-            to_back = jnp.concatenate([add(near_behind[:half], from_front), near_behind[half:]], axis=0)
-            to_front = jnp.concatenate([near_front[:half], add(near_front[half:], from_behind)], axis=0)
-        elif k > 1:
-            near_behind, near_front = parts[k - 1]
-            to_back, to_front = add(near_behind, from_front), add(near_front, from_behind)
-    feature_grad = add(after(own_part, weight_grad), from_front, from_behind)
+    for j in range(steps + 2, clus_count):
+        advance(j)
+    feature_grad = jnp.concatenate(
+        [add(after(own_grad[0], weight_grad), sum_up), add(own_grad[1], sum_down)], axis=0
+    )
     return (feature_grad, weight_grad)
 
 

time: 73.8 us -> 68.9 us (0.934)
  Pallas kernels: 19.2 us -> 10.7 us
  starting transfers between devices: 19.9 us -> 25.8 us
  waiting for transfers between devices: 28.1 us -> 23.4 us
  local copies, waits for them, and re-layouts: 3.25 us -> 5.59 us
    pallas_call x1, Pallas kernels: 9.08 us -> 0.05 us  [pack(): pl.pallas_call(pack_kernel, out_shape=jax.ShapeDtypeStruct((rows + FIELD_...]
    ppermute x16 -> x22, starting transfers between devices: 17.7 us -> 23.9 us  [the longest x11 17.6 us: send_up(): return lax.ppermute(array, 'clus', up)]
    ppermute x16 -> x22, waiting for transfers between devices: 24.4 us -> 21.8 us  [the longest x11 13 us: send_up(): return lax.ppermute(array, 'clus', up)]
    unnamed x10 -> x12, local copies, waits for them, and re-layouts: 3.21 us -> 5.57 us
    ppermute x3, waiting for transfers between devices: 3.72 us -> 1.59 us  [seq_send(): return lax.ppermute(array, 'seq', [(k, k ^ bit) for k in range(seq_count)])]
    convert_element_type x9 -> x16, other arithmetic: 2.27 us -> 1.6 us  [add(): return total.astype(jnp.bfloat16)]
    pallas_call x4 -> x5, Pallas kernels: 6.97 us -> 7.46 us  [block_work(): pl.pallas_call(functools.partial(block_kernel, piece_rows, top_count, pos...]
  transfers between devices with their start and end apart: 19 -> 25, of which waited for: 10 -> 14; matrix products, arithmetic and copies ran while one was open for 2% -> 2% of each run, Pallas kernels for 12% -> 15%
where the time goes in v7:
time: 68.9 us; the launch traced here: 68.7 us
  starting transfers between devices  25.8 us (37%)
  waiting for transfers between devices  23.4 us (34%)
  Pallas kernels  10.7 us (16%)
  local copies, waits for them, and re-layouts  5.59 us (8%)
  other arithmetic  2.33 us (3%)
  between operations  0.86 us (1%)
    ppermute x11, starting transfers between devices, send_up(): return lax.ppermute(array, 'clus', up)  17.6 us
    ppermute x11, waiting for transfers between devices, send_up(): return lax.ppermute(array, 'clus', up)  13 us
    ppermute x11, waiting for transfers between devices, send_down(): return lax.ppermute(array, 'clus', down)  8.8 us
    pallas_call x5, Pallas kernels, block_work(): pl.pallas_call(functools.partial(block_kernel, piece_rows, top_count, pos...  7.46 us
    ppermute x11, starting transfers between devices, send_down(): return lax.ppermute(array, 'clus', down)  6.22 us
    unnamed x12, local copies, waits for them, and re-layouts  5.57 us
    pallas_call x2, Pallas kernels, weight_work(): pl.pallas_call(functools.partial(weight_kernel, piece_rows, column_blocks...  2.58 us
    ppermute x3, starting transfers between devices, seq_send(): return lax.ppermute(array, 'seq', [(k, k ^ bit) for k in range(seq_count)])  1.9 us
  transfers between devices with their start and end apart: 25, of which 14 were waited for; matrix products, arithmetic and copies ran while one was open for 2% of the time, Pallas kernels for 15%

profile of v7, /device:TPU:0, one launch (start us, length us, event | category | flops | bytes accessed | tf_op | source)
XLA Modules:
  0.0 68.7 jit_solution(3162541985350007665)
XLA Ops:
  3.0 3.1 %collective-permute-start = (bf16[136,1024]{1,0:T(8,128)(2,1)S(1)}, bf16[136,1024]{1,0:T(8,128)(2,1)S(1)}, u32[]{:S(2)}, u32[]{:S(2)}) collective-permute-start(bf16[136,1024]{1,0:T(8,128)(2,1)S(1)} %pack.1.refs_0_), channel_id=1, source_target_pairs={{0,2},{2,4},{4,6},{6,7},{7,5},{5,3},{3,1},{1,0},{8,10},{10,12},{12... | collective-permute-start | bytes 835592 | tf_op jit(solution)/shard_map/ppermute | solution.py:228
  6.1 1.6 %copy-done = bf16[1024,1024]{1,0:T(8,128)(2,1)S(1)} copy-done((bf16[1024,1024]{1,0:T(8,128)(2,1)S(1)}, bf16[1024,1024]{1,0:T(8,128)(2,1)}, u32[]{:S(2)}) %copy-start) | copy-done | bytes 2097176
  9.9 1.2 %block_work.5 = (bf16[64,1024]{1,0:T(8,128)(2,1)S(1)}, bf16[64,1024]{1,0:T(8,128)(2,1)S(1)}, bf16[128,1024]{1,0:T(8,128)(2,1)S(1)}) custom-call(bf16[136,1024]{1,0:T(8,128)(2,1)S(1)} %pack.1.refs_0_, bf16[1024,1024]{1,0:T(8,128)(2,1)S(1)} %copy-done.1, bf16[128,1024]{1,0:T(8,128)(2,1)S(1)} %live_labels.1.refs_2_.refs_3_), custom_call_target="tpu_custom_call" | custom-call | flops 536870912 | bytes 2883584 | tf_op jit(solution)/shard_map/block_work/pallas_call | solution.py:147
  11.1 1.5 %collective-permute-done.refs_0_.refs_1_ = bf16[136,1024]{1,0:T(8,128)(2,1)S(1)} collective-permute-done((bf16[136,1024]{1,0:T(8,128)(2,1)S(1)}, bf16[136,1024]{1,0:T(8,128)(2,1)S(1)}, u32[]{:S(2)}, u32[]{:S(2)}) %collective-permute-start) | collective-permute-done | bytes 278560 | tf_op jit(solution)/shard_map/ppermute | solution.py:228
  12.7 1.8 %collective-permute-start.2 = (bf16[136,1024]{1,0:T(8,128)(2,1)S(1)}, bf16[136,1024]{1,0:T(8,128)(2,1)S(1)}, u32[]{:S(2)}, u32[]{:S(2)}) collective-permute-start(bf16[136,1024]{1,0:T(8,128)(2,1)S(1)} %collective-permute-done.refs_0_.refs_1_), channel_id=1, source_target_pairs={{0,2},{2,4},{4,6},{6,7},{7,5},{5,3},{3,1},{1,0},{8,10},{10,12},{12... | collective-permute-start | bytes 835592 | tf_op jit(solution)/shard_map/ppermute | solution.py:228
  14.7 1.7 %block_work.6 = (bf16[64,1024]{1,0:T(8,128)(2,1)S(1)}, bf16[64,1024]{1,0:T(8,128)(2,1)S(1)}, bf16[64,1024]{1,0:T(8,128)(2,1)S(1)}, bf16[64,1024]{1,0:T(8,128)(2,...) custom-call(bf16[136,1024]{1,0:T(8,128)(2,1)S(1)} %collective-permute-done.refs_0_.refs_1_, ...), custom_call_target="tpu_custom_call" | custom-call | flops 1073741824 | bytes 3670016 | tf_op jit(solution)/shard_map/block_work/pallas_call | solution.py:147
  16.4 1.8 %collective-permute-start.18 = (bf16[64,1024]{1,0:T(8,128)(2,1)S(1)}, bf16[64,1024]{1,0:T(8,128)(2,1)S(1)}, u32[]{:S(2)}, u32[]{:S(2)}) collective-permute-start(bf16[64,1024]{1,0:T(8,128)(2,1)S(1)} %get-tuple-element.79), channel_id=1, source_target_pairs={{2,0},{4,2},{6,4},{7,6},{5,7},{3,5},{1,3},{0,1},{10,8},{12,10},{14... | collective-permute-start | bytes 393224 | tf_op jit(solution)/shard_map/ppermute | solution.py:231
  18.5 3.4 %collective-permute-done.2.refs_0_.refs_3_ = bf16[136,1024]{1,0:T(8,128)(2,1)S(1)} collective-permute-done((bf16[136,1024]{1,0:T(8,128)(2,1)S(1)}, bf16[136,1024]{1,0:T(8,128)(2,1)S(1)}, u32[]{:S(2)}, u32[]{:S(2)}) %collective-permute-start.2) | collective-permute-done | bytes 278560 | tf_op jit(solution)/shard_map/ppermute | solution.py:228
  21.9 1.2 %collective-permute-done.3.refs_1_.refs_4_ = bf16[136,1024]{1,0:T(8,128)(2,1)S(1)} collective-permute-done((bf16[136,1024]{1,0:T(8,128)(2,1)S(1)}, bf16[136,1024]{1,0:T(8,128)(2,1)S(1)}, u32[]{:S(2)}, u32[]{:S(2)}) %collective-permute-start.3) | collective-permute-done | bytes 278560 | tf_op jit(solution)/shard_map/ppermute | solution.py:231
  23.1 1.6 %collective-permute-start.4 = (bf16[136,1024]{1,0:T(8,128)(2,1)S(1)}, bf16[136,1024]{1,0:T(8,128)(2,1)S(1)}, u32[]{:S(2)}, u32[]{:S(2)}) collective-permute-start(bf16[136,1024]{1,0:T(8,128)(2,1)S(1)} %collective-permute-done.2.refs_0_.refs_3_), channel_id=1, source_target_pairs={{0,2},{2,4},{4,6},{6,7},{7,5},{5,3},{3,1},{1,0},{8,10},{10,12},{12... | collective-permute-start | bytes 835592 | tf_op jit(solution)/shard_map/ppermute | solution.py:228
  25.2 1.7 %block_work.7 = (bf16[64,1024]{1,0:T(8,128)(2,1)S(1)}, bf16[64,1024]{1,0:T(8,128)(2,1)S(1)}, bf16[64,1024]{1,0:T(8,128)(2,1)S(1)}, bf16[64,1024]{1,0:T(8,128)(2,...) custom-call(bf16[136,1024]{1,0:T(8,128)(2,1)S(1)} %collective-permute-done.2.refs_0_.refs_3_, ...), custom_call_target="tpu_custom_call" | custom-call | flops 1073741824 | bytes 3670016 | tf_op jit(solution)/shard_map/block_work/pallas_call | solution.py:147
  27.6 1.5 %collective-permute-start.12 = (bf16[64,1024]{1,0:T(8,128)(2,1)S(1)}, bf16[64,1024]{1,0:T(8,128)(2,1)S(1)}, u32[]{:S(2)}, u32[]{:S(2)}) collective-permute-start(bf16[64,1024]{1,0:T(8,128)(2,1)S(1)} %add_convert_fusion.15), channel_id=1, source_target_pairs={{0,2},{2,4},{4,6},{6,7},{7,5},{5,3},{3,1},{1,0},{8,10},{10,12},{12... | collective-permute-start | bytes 393224 | tf_op jit(solution)/shard_map/ppermute | solution.py:228
  29.1 1.6 %collective-permute-done.4.refs_0_.refs_5_ = bf16[136,1024]{1,0:T(8,128)(2,1)S(1)} collective-permute-done((bf16[136,1024]{1,0:T(8,128)(2,1)S(1)}, bf16[136,1024]{1,0:T(8,128)(2,1)S(1)}, u32[]{:S(2)}, u32[]{:S(2)}) %collective-permute-start.4) | collective-permute-done | bytes 278560 | tf_op jit(solution)/shard_map/ppermute | solution.py:228
  30.7 1.2 %collective-permute-done.5.refs_1_.refs_6_ = bf16[136,1024]{1,0:T(8,128)(2,1)S(1)} collective-permute-done((bf16[136,1024]{1,0:T(8,128)(2,1)S(1)}, bf16[136,1024]{1,0:T(8,128)(2,1)S(1)}, u32[]{:S(2)}, u32[]{:S(2)}) %collective-permute-start.5) | collective-permute-done | bytes 278560 | tf_op jit(solution)/shard_map/ppermute | solution.py:231
  31.9 1.7 %block_work.8 = (bf16[64,1024]{1,0:T(8,128)(2,1)S(1)}, bf16[64,1024]{1,0:T(8,128)(2,1)S(1)}, bf16[64,1024]{1,0:T(8,128)(2,1)S(1)}, bf16[64,1024]{1,0:T(8,128)(2,...) custom-call(bf16[136,1024]{1,0:T(8,128)(2,1)S(1)} %collective-permute-done.4.refs_0_.refs_5_, ...), custom_call_target="tpu_custom_call" | custom-call | flops 1073741824 | bytes 3670016 | tf_op jit(solution)/shard_map/block_work/pallas_call | solution.py:147
  34.8 1.6 %collective-permute-start.6 = (bf16[72,1024]{1,0:T(8,128)(2,1)S(1)}, bf16[72,1024]{1,0:T(8,128)(2,1)S(1)}, u32[]{:S(2)}, u32[]{:S(2)}) collective-permute-start(bf16[72,1024]{1,0:T(8,128)(2,1)S(1)} %pad_maximum_fusion.1), channel_id=1, source_target_pairs={{0,2},{2,4},{4,6},{6,7},{7,5},{5,3},{3,1},{1,0},{8,10},{10,12},{12... | collective-permute-start | bytes 442376 | tf_op jit(solution)/shard_map/ppermute | solution.py:228
  36.9 1.6 %collective-permute-start.13 = (bf16[64,1024]{1,0:T(8,128)(2,1)S(1)}, bf16[64,1024]{1,0:T(8,128)(2,1)S(1)}, u32[]{:S(2)}, u32[]{:S(2)}) collective-permute-start(bf16[64,1024]{1,0:T(8,128)(2,1)S(1)} %add_convert_fusion.14), channel_id=1, source_target_pairs={{0,2},{2,4},{4,6},{6,7},{7,5},{5,3},{3,1},{1,0},{8,10},{10,12},{12... | collective-permute-start | bytes 393224 | tf_op jit(solution)/shard_map/ppermute | solution.py:228
  38.6 1.5 %collective-permute-done.6.refs_0_.refs_7_ = bf16[72,1024]{1,0:T(8,128)(2,1)S(1)} collective-permute-done((bf16[72,1024]{1,0:T(8,128)(2,1)S(1)}, bf16[72,1024]{1,0:T(8,128)(2,1)S(1)}, u32[]{:S(2)}, u32[]{:S(2)}) %collective-permute-start.6) | collective-permute-done | bytes 147488 | tf_op jit(solution)/shard_map/ppermute | solution.py:228
  40.0 2.7 %collective-permute-done.7.refs_1_.refs_8_ = bf16[64,1024]{1,0:T(8,128)(2,1)S(1)} collective-permute-done((bf16[64,1024]{1,0:T(8,128)(2,1)S(1)}, bf16[64,1024]{1,0:T(8,128)(2,1)S(1)}, u32[]{:S(2)}, u32[]{:S(2)}) %collective-permute-start.7) | collective-permute-done | bytes 131104 | tf_op jit(solution)/shard_map/ppermute | solution.py:231
  44.5 1.3 %weight_work.3 = (bf16[1024,256]{1,0:T(8,128)(2,1)S(1)}, bf16[1024,256]{1,0:T(8,128)(2,1)S(1)}) custom-call(bf16[136,1024]{1,0:T(8,128)(2,1)S(1)} %pack.1.refs_0_, bf16[136,1024]{1,0:T(8,128)(2,1)S(1)} %collective-permute-done.refs_0_.refs_1_, bf16[136,1024]{1,0:T(8,128)(2,1)S(1)} %collective-permute-done.1.refs_1_.refs_2_, ...), custom_call_target="tpu_custom_call" | custom-call | flops 1073741824 | bytes 4718592 | tf_op jit(solution)/shard_map/weight_work/pallas_call | solution.py:190
  45.9 1.5 %collective-permute-start.14 = (bf16[64,1024]{1,0:T(8,128)(2,1)S(1)}, bf16[64,1024]{1,0:T(8,128)(2,1)S(1)}, u32[]{:S(2)}, u32[]{:S(2)}) collective-permute-start(bf16[64,1024]{1,0:T(8,128)(2,1)S(1)} %add_convert_fusion.13), channel_id=1, source_target_pairs={{0,2},{2,4},{4,6},{6,7},{7,5},{5,3},{3,1},{1,0},{8,10},{10,12},{12... | collective-permute-start | bytes 393224 | tf_op jit(solution)/shard_map/ppermute | solution.py:228
  47.5 1.3 %weight_work.2 = (bf16[1024,256]{1,0:T(8,128)(2,1)S(1)}, bf16[1024,256]{1,0:T(8,128)(2,1)S(1)}) custom-call(bf16[136,1024]{1,0:T(8,128)(2,1)S(1)} %pack.1.refs_0_, bf16[136,1024]{1,0:T(8,128)(2,1)S(1)} %collective-permute-done.refs_0_.refs_1_, bf16[136,1024]{1,0:T(8,128)(2,1)S(1)} %collective-permute-done.1.refs_1_.refs_2_, ...), custom_call_target="tpu_custom_call" | custom-call | flops 1073741824 | bytes 4718592 | tf_op jit(solution)/shard_map/weight_work/pallas_call | solution.py:190
  49.7 2.2 %collective-permute-done.14 = bf16[64,1024]{1,0:T(8,128)(2,1)S(1)} collective-permute-done((bf16[64,1024]{1,0:T(8,128)(2,1)S(1)}, bf16[64,1024]{1,0:T(8,128)(2,1)S(1)}, u32[]{:S(2)}, u32[]{:S(2)}) %collective-permute-start.14) | collective-permute-done | bytes 131104 | tf_op jit(solution)/shard_map/ppermute | solution.py:228
  51.9 1.5 %collective-permute-start.15 = (bf16[64,1024]{1,0:T(8,128)(2,1)S(1)}, bf16[64,1024]{1,0:T(8,128)(2,1)S(1)}, u32[]{:S(2)}, u32[]{:S(2)}) collective-permute-start(bf16[64,1024]{1,0:T(8,128)(2,1)S(1)} %add_convert_fusion.12), channel_id=1, source_target_pairs={{0,2},{2,4},{4,6},{6,7},{7,5},{5,3},{3,1},{1,0},{8,10},{10,12},{12... | collective-permute-start | bytes 393224 | tf_op jit(solution)/shard_map/ppermute | solution.py:228
  53.6 1.6 %collective-permute-start.10 = (bf16[1024,256]{1,0:T(8,128)(2,1)S(1)}, bf16[1024,256]{1,0:T(8,128)(2,1)S(1)}, u32[]{:S(2)}, u32[]{:S(2)}) collective-permute-start(bf16[1024,256]{1,0:T(8,128)(2,1)S(1)} %add_convert_fusion.1), channel_id=1, source_target_pairs={{0,16},{8,24},{16,0},{24,8},{1,17},{9,25},{17,1},{25,9},{2,18},{10... | collective-permute-start | bytes 1572872 | tf_op jit(solution)/shard_map/ppermute | solution.py:277
  55.7 1.4 %collective-permute-done.15 = bf16[64,1024]{1,0:T(8,128)(2,1)S(1)} collective-permute-done((bf16[64,1024]{1,0:T(8,128)(2,1)S(1)}, bf16[64,1024]{1,0:T(8,128)(2,1)S(1)}, u32[]{:S(2)}, u32[]{:S(2)}) %collective-permute-start.15) | collective-permute-done | bytes 131104 | tf_op jit(solution)/shard_map/ppermute | solution.py:228
  57.1 1.5 %collective-permute-start.16 = (bf16[64,1024]{1,0:T(8,128)(2,1)S(1)}, bf16[64,1024]{1,0:T(8,128)(2,1)S(1)}, u32[]{:S(2)}, u32[]{:S(2)}) collective-permute-start(bf16[64,1024]{1,0:T(8,128)(2,1)S(1)} %add_convert_fusion.11), channel_id=1, source_target_pairs={{0,2},{2,4},{4,6},{6,7},{7,5},{5,3},{3,1},{1,0},{8,10},{10,12},{12... | collective-permute-start | bytes 393224 | tf_op jit(solution)/shard_map/ppermute | solution.py:228
  58.6 1.6 %collective-permute-done.23 = bf16[64,1024]{1,0:T(8,128)(2,1)S(1)} collective-permute-done((bf16[64,1024]{1,0:T(8,128)(2,1)S(1)}, bf16[64,1024]{1,0:T(8,128)(2,1)S(1)}, u32[]{:S(2)}, u32[]{:S(2)}) %collective-permute-start.23) | collective-permute-done | bytes 131104 | tf_op jit(solution)/shard_map/ppermute | solution.py:231
  60.7 1.4 %collective-permute-done.16 = bf16[64,1024]{1,0:T(8,128)(2,1)S(1)} collective-permute-done((bf16[64,1024]{1,0:T(8,128)(2,1)S(1)}, bf16[64,1024]{1,0:T(8,128)(2,1)S(1)}, u32[]{:S(2)}, u32[]{:S(2)}) %collective-permute-start.16) | collective-permute-done | bytes 131104 | tf_op jit(solution)/shard_map/ppermute | solution.py:228
  62.2 1.5 %collective-permute-start.17 = (bf16[64,1024]{1,0:T(8,128)(2,1)S(1)}, bf16[64,1024]{1,0:T(8,128)(2,1)S(1)}, u32[]{:S(2)}, u32[]{:S(2)}) collective-permute-start(bf16[64,1024]{1,0:T(8,128)(2,1)S(1)} %add_convert_fusion.10), channel_id=1, source_target_pairs={{0,2},{2,4},{4,6},{6,7},{7,5},{5,3},{3,1},{1,0},{8,10},{10,12},{12... | collective-permute-start | bytes 393224 | tf_op jit(solution)/shard_map/ppermute | solution.py:228
  63.7 1.6 %collective-permute-done.24 = bf16[64,1024]{1,0:T(8,128)(2,1)S(1)} collective-permute-done((bf16[64,1024]{1,0:T(8,128)(2,1)S(1)}, bf16[64,1024]{1,0:T(8,128)(2,1)S(1)}, u32[]{:S(2)}, u32[]{:S(2)}) %collective-permute-start.24) | collective-permute-done | bytes 131104 | tf_op jit(solution)/shard_map/ppermute | solution.py:231
  65.3 1.6 %collective-permute-done.10 = bf16[1024,256]{1,0:T(8,128)(2,1)S(1)} collective-permute-done((bf16[1024,256]{1,0:T(8,128)(2,1)S(1)}, bf16[1024,256]{1,0:T(8,128)(2,1)S(1)}, u32[]{:S(2)}, u32[]{:S(2)}) %collective-permute-start.10) | collective-permute-done | bytes 524320 | tf_op jit(solution)/shard_map/ppermute | solution.py:277
  (60 shorter events, 13.8 us)
Async XLA Ops:
  0.6 1.0 %copy-start.2 = (bf16[128,1024]{1,0:T(8,128)(2,1)S(1)}, bf16[128,1024]{1,0:T(8,128)(2,1)}, u32[]{:S(2)}) copy-start(bf16[128,1024]{1,0:T(8,128)(2,1)} %feat_ref.1) | copy-start | bytes 786436
  1.6 0.7 %copy-start.3 = (s32[128,16]{0,1:T(8,128)S(1)}, s32[128,16]{0,1:T(8,128)}, u32[]{:S(2)}) copy-start(s32[128,16]{0,1:T(8,128)} %param.6) | copy-start | bytes 24580
  2.3 0.7 copy-start.4
  3.0 9.7 %collective-permute-start = (bf16[136,1024]{1,0:T(8,128)(2,1)S(1)}, bf16[136,1024]{1,0:T(8,128)(2,1)S(1)}, u32[]{:S(2)}, u32[]{:S(2)}) collective-permute-start(bf16[136,1024]{1,0:T(8,128)(2,1)S(1)} %pack.1.refs_0_), channel_id=1, source_target_pairs={{0,2},{2,4},{4,6},{6,7},{7,5},{5,3},{3,1},{1,0},{8,10},{10,12},{12... | collective-permute-start | bytes 835592 | tf_op jit(solution)/shard_map/ppermute | solution.py:228
  6.1 8.4 %collective-permute-start.1 = (bf16[136,1024]{1,0:T(8,128)(2,1)S(1)}, bf16[136,1024]{1,0:T(8,128)(2,1)S(1)}, u32[]{:S(2)}, u32[]{:S(2)}) collective-permute-start(bf16[136,1024]{1,0:T(8,128)(2,1)S(1)} %pack.1.refs_0_), channel_id=1, source_target_pairs={{2,0},{4,2},{6,4},{7,6},{5,7},{3,5},{1,3},{0,1},{10,8},{12,10},{14... | collective-permute-start | bytes 835592 | tf_op jit(solution)/shard_map/ppermute | solution.py:231
  6.1 1.6 %copy-start = (bf16[1024,1024]{1,0:T(8,128)(2,1)S(1)}, bf16[1024,1024]{1,0:T(8,128)(2,1)}, u32[]{:S(2)}) copy-start(bf16[1024,1024]{1,0:T(8,128)(2,1)} %refs_2_.7) | copy-start | bytes 6291460
  7.7 0.7 copy-start.5
  8.3 1.6 %copy-start.1 = (bf16[1024,1024]{1,0:T(8,128)(2,1)S(1)}, bf16[1024,1024]{1,0:T(8,128)(2,1)}, u32[]{:S(2)}) copy-start(bf16[1024,1024]{1,0:T(8,128)(2,1)} %refs_2_.7) | copy-start | bytes 6291460
  12.7 9.2 %collective-permute-start.2 = (bf16[136,1024]{1,0:T(8,128)(2,1)S(1)}, bf16[136,1024]{1,0:T(8,128)(2,1)S(1)}, u32[]{:S(2)}, u32[]{:S(2)}) collective-permute-start(bf16[136,1024]{1,0:T(8,128)(2,1)S(1)} %collective-permute-done.refs_0_.refs_1_), channel_id=1, source_target_pairs={{0,2},{2,4},{4,6},{6,7},{7,5},{5,3},{3,1},{1,0},{8,10},{10,12},{12... | collective-permute-start | bytes 835592 | tf_op jit(solution)/shard_map/ppermute | solution.py:228
  14.5 8.7 %collective-permute-start.3 = (bf16[136,1024]{1,0:T(8,128)(2,1)S(1)}, bf16[136,1024]{1,0:T(8,128)(2,1)S(1)}, u32[]{:S(2)}, u32[]{:S(2)}) collective-permute-start(bf16[136,1024]{1,0:T(8,128)(2,1)S(1)} %collective-permute-done.1.refs_1_.refs_2_), channel_id=1, source_target_pairs={{2,0},{4,2},{6,4},{7,6},{5,7},{3,5},{1,3},{0,1},{10,8},{12,10},{14... | collective-permute-start | bytes 835592 | tf_op jit(solution)/shard_map/ppermute | solution.py:231
  16.4 10.5 %collective-permute-start.18 = (bf16[64,1024]{1,0:T(8,128)(2,1)S(1)}, bf16[64,1024]{1,0:T(8,128)(2,1)S(1)}, u32[]{:S(2)}, u32[]{:S(2)}) collective-permute-start(bf16[64,1024]{1,0:T(8,128)(2,1)S(1)} %get-tuple-element.79), channel_id=1, source_target_pairs={{2,0},{4,2},{6,4},{7,6},{5,7},{3,5},{1,3},{0,1},{10,8},{12,10},{14... | collective-permute-start | bytes 393224 | tf_op jit(solution)/shard_map/ppermute | solution.py:231
  18.2 9.3 %collective-permute-start.11 = (bf16[64,1024]{1,0:T(8,128)(2,1)S(1)}, bf16[64,1024]{1,0:T(8,128)(2,1)S(1)}, u32[]{:S(2)}, u32[]{:S(2)}) collective-permute-start(bf16[64,1024]{1,0:T(8,128)(2,1)S(1)} %get-tuple-element.45), channel_id=1, source_target_pairs={{0,2},{2,4},{4,6},{6,7},{7,5},{5,3},{3,1},{1,0},{8,10},{10,12},{12... | collective-permute-start | bytes 393224 | tf_op jit(solution)/shard_map/ppermute | solution.py:228
  23.1 7.6 %collective-permute-start.4 = (bf16[136,1024]{1,0:T(8,128)(2,1)S(1)}, bf16[136,1024]{1,0:T(8,128)(2,1)S(1)}, u32[]{:S(2)}, u32[]{:S(2)}) collective-permute-start(bf16[136,1024]{1,0:T(8,128)(2,1)S(1)} %collective-permute-done.2.refs_0_.refs_3_), channel_id=1, source_target_pairs={{0,2},{2,4},{4,6},{6,7},{7,5},{5,3},{3,1},{1,0},{8,10},{10,12},{12... | collective-permute-start | bytes 835592 | tf_op jit(solution)/shard_map/ppermute | solution.py:228
  24.7 7.2 %collective-permute-start.5 = (bf16[136,1024]{1,0:T(8,128)(2,1)S(1)}, bf16[136,1024]{1,0:T(8,128)(2,1)S(1)}, u32[]{:S(2)}, u32[]{:S(2)}) collective-permute-start(bf16[136,1024]{1,0:T(8,128)(2,1)S(1)} %collective-permute-done.3.refs_1_.refs_4_), channel_id=1, source_target_pairs={{2,0},{4,2},{6,4},{7,6},{5,7},{3,5},{1,3},{0,1},{10,8},{12,10},{14... | collective-permute-start | bytes 835592 | tf_op jit(solution)/shard_map/ppermute | solution.py:231
  26.9 7.3 %collective-permute-start.19 = (bf16[64,1024]{1,0:T(8,128)(2,1)S(1)}, bf16[64,1024]{1,0:T(8,128)(2,1)S(1)}, u32[]{:S(2)}, u32[]{:S(2)}) collective-permute-start(bf16[64,1024]{1,0:T(8,128)(2,1)S(1)} %add_convert_fusion.8), channel_id=1, source_target_pairs={{2,0},{4,2},{6,4},{7,6},{5,7},{3,5},{1,3},{0,1},{10,8},{12,10},{14... | collective-permute-start | bytes 393224 | tf_op jit(solution)/shard_map/ppermute | solution.py:231
  27.6 9.3 %collective-permute-start.12 = (bf16[64,1024]{1,0:T(8,128)(2,1)S(1)}, bf16[64,1024]{1,0:T(8,128)(2,1)S(1)}, u32[]{:S(2)}, u32[]{:S(2)}) collective-permute-start(bf16[64,1024]{1,0:T(8,128)(2,1)S(1)} %add_convert_fusion.15), channel_id=1, source_target_pairs={{0,2},{2,4},{4,6},{6,7},{7,5},{5,3},{3,1},{1,0},{8,10},{10,12},{12... | collective-permute-start | bytes 393224 | tf_op jit(solution)/shard_map/ppermute | solution.py:228
  34.3 9.6 %collective-permute-start.20 = (bf16[64,1024]{1,0:T(8,128)(2,1)S(1)}, bf16[64,1024]{1,0:T(8,128)(2,1)S(1)}, u32[]{:S(2)}, u32[]{:S(2)}) collective-permute-start(bf16[64,1024]{1,0:T(8,128)(2,1)S(1)} %add_convert_fusion.7), channel_id=1, source_target_pairs={{2,0},{4,2},{6,4},{7,6},{5,7},{3,5},{1,3},{0,1},{10,8},{12,10},{14... | collective-permute-start | bytes 393224 | tf_op jit(solution)/shard_map/ppermute | solution.py:231
  34.8 5.2 %collective-permute-start.6 = (bf16[72,1024]{1,0:T(8,128)(2,1)S(1)}, bf16[72,1024]{1,0:T(8,128)(2,1)S(1)}, u32[]{:S(2)}, u32[]{:S(2)}) collective-permute-start(bf16[72,1024]{1,0:T(8,128)(2,1)S(1)} %pad_maximum_fusion.1), channel_id=1, source_target_pairs={{0,2},{2,4},{4,6},{6,7},{7,5},{5,3},{3,1},{1,0},{8,10},{10,12},{12... | collective-permute-start | bytes 442376 | tf_op jit(solution)/shard_map/ppermute | solution.py:228
  36.4 6.2 %collective-permute-start.7 = (bf16[64,1024]{1,0:T(8,128)(2,1)S(1)}, bf16[64,1024]{1,0:T(8,128)(2,1)S(1)}, u32[]{:S(2)}, u32[]{:S(2)}) collective-permute-start(bf16[64,1024]{1,0:T(8,128)(2,1)S(1)} %slice.11), channel_id=1, source_target_pairs={{2,0},{4,2},{6,4},{7,6},{5,7},{3,5},{1,3},{0,1},{10,8},{12,10},{14... | collective-permute-start | bytes 393224 | tf_op jit(solution)/shard_map/ppermute | solution.py:231
  36.9 9.0 %collective-permute-start.13 = (bf16[64,1024]{1,0:T(8,128)(2,1)S(1)}, bf16[64,1024]{1,0:T(8,128)(2,1)S(1)}, u32[]{:S(2)}, u32[]{:S(2)}) collective-permute-start(bf16[64,1024]{1,0:T(8,128)(2,1)S(1)} %add_convert_fusion.14), channel_id=1, source_target_pairs={{0,2},{2,4},{4,6},{6,7},{7,5},{5,3},{3,1},{1,0},{8,10},{10,12},{12... | collective-permute-start | bytes 393224 | tf_op jit(solution)/shard_map/ppermute | solution.py:228
  43.9 5.1 %collective-permute-start.21 = (bf16[64,1024]{1,0:T(8,128)(2,1)S(1)}, bf16[64,1024]{1,0:T(8,128)(2,1)S(1)}, u32[]{:S(2)}, u32[]{:S(2)}) collective-permute-start(bf16[64,1024]{1,0:T(8,128)(2,1)S(1)} %add_convert_fusion.6), channel_id=1, source_target_pairs={{2,0},{4,2},{6,4},{7,6},{5,7},{3,5},{1,3},{0,1},{10,8},{12,10},{14... | collective-permute-start | bytes 393224 | tf_op jit(solution)/shard_map/ppermute | solution.py:231
  45.8 7.6 %collective-permute-start.9 = (bf16[1024,256]{1,0:T(8,128)(2,1)S(1)}, bf16[1024,256]{1,0:T(8,128)(2,1)S(1)}, u32[]{:S(2)}, u32[]{:S(2)}) collective-permute-start(bf16[1024,256]{1,0:T(8,128)(2,1)S(1)} %get-tuple-element.64), channel_id=1, source_target_pairs={{0,8},{8,0},{16,24},{24,16},{1,9},{9,1},{17,25},{25,17},{2,10},{10... | collective-permute-start | bytes 1572872 | tf_op jit(solution)/shard_map/ppermute | solution.py:277
  45.9 5.9 %collective-permute-start.14 = (bf16[64,1024]{1,0:T(8,128)(2,1)S(1)}, bf16[64,1024]{1,0:T(8,128)(2,1)S(1)}, u32[]{:S(2)}, u32[]{:S(2)}) collective-permute-start(bf16[64,1024]{1,0:T(8,128)(2,1)S(1)} %add_convert_fusion.13), channel_id=1, source_target_pairs={{0,2},{2,4},{4,6},{6,7},{7,5},{5,3},{3,1},{1,0},{8,10},{10,12},{12... | collective-permute-start | bytes 393224 | tf_op jit(solution)/shard_map/ppermute | solution.py:228
  48.8 16.5 %collective-permute-start.8 = (bf16[1024,256]{1,0:T(8,128)(2,1)S(1)}, bf16[1024,256]{1,0:T(8,128)(2,1)S(1)}, u32[]{:S(2)}, u32[]{:S(2)}) collective-permute-start(bf16[1024,256]{1,0:T(8,128)(2,1)S(1)} %get-tuple-element.62), channel_id=1, source_target_pairs={{0,8},{8,0},{16,24},{24,16},{1,9},{9,1},{17,25},{25,17},{2,10},{10... | collective-permute-start | bytes 1572872 | tf_op jit(solution)/shard_map/ppermute | solution.py:277
  49.1 6.1 %collective-permute-start.22 = (bf16[64,1024]{1,0:T(8,128)(2,1)S(1)}, bf16[64,1024]{1,0:T(8,128)(2,1)S(1)}, u32[]{:S(2)}, u32[]{:S(2)}) collective-permute-start(bf16[64,1024]{1,0:T(8,128)(2,1)S(1)} %add_convert_fusion.5), channel_id=1, source_target_pairs={{2,0},{4,2},{6,4},{7,6},{5,7},{3,5},{1,3},{0,1},{10,8},{12,10},{14... | collective-permute-start | bytes 393224 | tf_op jit(solution)/shard_map/ppermute | solution.py:231
  51.9 5.2 %collective-permute-start.15 = (bf16[64,1024]{1,0:T(8,128)(2,1)S(1)}, bf16[64,1024]{1,0:T(8,128)(2,1)S(1)}, u32[]{:S(2)}, u32[]{:S(2)}) collective-permute-start(bf16[64,1024]{1,0:T(8,128)(2,1)S(1)} %add_convert_fusion.12), channel_id=1, source_target_pairs={{0,2},{2,4},{4,6},{6,7},{7,5},{5,3},{3,1},{1,0},{8,10},{10,12},{12... | collective-permute-start | bytes 393224 | tf_op jit(solution)/shard_map/ppermute | solution.py:228
  53.6 13.3 %collective-permute-start.10 = (bf16[1024,256]{1,0:T(8,128)(2,1)S(1)}, bf16[1024,256]{1,0:T(8,128)(2,1)S(1)}, u32[]{:S(2)}, u32[]{:S(2)}) collective-permute-start(bf16[1024,256]{1,0:T(8,128)(2,1)S(1)} %add_convert_fusion.1), channel_id=1, source_target_pairs={{0,16},{8,24},{16,0},{24,8},{1,17},{9,25},{17,1},{25,9},{2,18},{10... | collective-permute-start | bytes 1572872 | tf_op jit(solution)/shard_map/ppermute | solution.py:277
  55.2 5.0 %collective-permute-start.23 = (bf16[64,1024]{1,0:T(8,128)(2,1)S(1)}, bf16[64,1024]{1,0:T(8,128)(2,1)S(1)}, u32[]{:S(2)}, u32[]{:S(2)}) collective-permute-start(bf16[64,1024]{1,0:T(8,128)(2,1)S(1)} %add_convert_fusion.4), channel_id=1, source_target_pairs={{2,0},{4,2},{6,4},{7,6},{5,7},{3,5},{1,3},{0,1},{10,8},{12,10},{14... | collective-permute-start | bytes 393224 | tf_op jit(solution)/shard_map/ppermute | solution.py:231
  57.1 5.0 %collective-permute-start.16 = (bf16[64,1024]{1,0:T(8,128)(2,1)S(1)}, bf16[64,1024]{1,0:T(8,128)(2,1)S(1)}, u32[]{:S(2)}, u32[]{:S(2)}) collective-permute-start(bf16[64,1024]{1,0:T(8,128)(2,1)S(1)} %add_convert_fusion.11), channel_id=1, source_target_pairs={{0,2},{2,4},{4,6},{6,7},{7,5},{5,3},{3,1},{1,0},{8,10},{10,12},{12... | collective-permute-start | bytes 393224 | tf_op jit(solution)/shard_map/ppermute | solution.py:228
  60.2 5.0 %collective-permute-start.24 = (bf16[64,1024]{1,0:T(8,128)(2,1)S(1)}, bf16[64,1024]{1,0:T(8,128)(2,1)S(1)}, u32[]{:S(2)}, u32[]{:S(2)}) collective-permute-start(bf16[64,1024]{1,0:T(8,128)(2,1)S(1)} %add_convert_fusion.3), channel_id=1, source_target_pairs={{2,0},{4,2},{6,4},{7,6},{5,7},{3,5},{1,3},{0,1},{10,8},{12,10},{14... | collective-permute-start | bytes 393224 | tf_op jit(solution)/shard_map/ppermute | solution.py:231
  62.2 5.7 %collective-permute-start.17 = (bf16[64,1024]{1,0:T(8,128)(2,1)S(1)}, bf16[64,1024]{1,0:T(8,128)(2,1)S(1)}, u32[]{:S(2)}, u32[]{:S(2)}) collective-permute-start(bf16[64,1024]{1,0:T(8,128)(2,1)S(1)} %add_convert_fusion.10), channel_id=1, source_target_pairs={{0,2},{2,4},{4,6},{6,7},{7,5},{5,3},{3,1},{1,0},{8,10},{10,12},{12... | collective-permute-start | bytes 393224 | tf_op jit(solution)/shard_map/ppermute | solution.py:228

commit v8 on v7

--- a/solution.py
+++ b/solution.py
@@ -15,9 +15,8 @@
 VMEM_LIMIT = 40 * 1024 * 1024
 
 
-def pack_kernel(feat_ref, short_ref, pos_ref, out_ref):
-    rows, width = feat_ref.shape
-    out_ref[:rows, :] = feat_ref[...]
+def ids_kernel(width, short_ref, pos_ref, out_ref):
+    rows = short_ref.shape[1]
     short = short_ref[...]
     places = pos_ref[...] // BLOCK
     offsets = pos_ref[...] % BLOCK
@@ -30,21 +29,20 @@
     ]
     groups.append(jnp.zeros((FIELD_ROWS, width - rows * len(groups)), jnp.int32))
     meta = jnp.concatenate(groups, axis=1)
-    out_ref[rows:, :] = meta.astype(jnp.float32).astype(jnp.bfloat16)
-
-
-def pack(features, shortlist, positives):
-    rows, width = features.shape
+    out_ref[...] = meta.astype(jnp.float32).astype(jnp.bfloat16)
+
+
+def instance_ids(shortlist, positives, width):
     return pl.pallas_call(
-        pack_kernel,
-        out_shape=jax.ShapeDtypeStruct((rows + FIELD_ROWS, width), jnp.bfloat16),
-        in_specs=[pl.BlockSpec(memory_space=pltpu.VMEM)] * 3,
+        functools.partial(ids_kernel, width),
+        out_shape=jax.ShapeDtypeStruct((FIELD_ROWS, width), jnp.bfloat16),
+        in_specs=[pl.BlockSpec(memory_space=pltpu.VMEM)] * 2,
         compiler_params=pltpu.CompilerParams(vmem_limit_bytes=VMEM_LIMIT),
-        name="pack",
-    )(features, shortlist.T, positives.T)
-
-
-def live_kernel(size_ref, w_ref, live_ref):
+        name="instance_ids",
+    )(shortlist.T, positives.T)
+
+
+def live_kernel(size_ref, live_ref):
     lane = lax.broadcasted_iota(jnp.int32, (LANES, BLOCK), 1)
     row = lax.broadcasted_iota(jnp.int32, (LANES, BLOCK), 0)
     for c in range(size_ref.shape[0]):
@@ -52,15 +50,14 @@
         live_ref[:, c * BLOCK : (c + 1) * BLOCK] = live.astype(jnp.bfloat16)
 
 
-def live_labels(cluster_sizes, weights):
+def live_labels(cluster_sizes):
     return pl.pallas_call(
         live_kernel,
         out_shape=jax.ShapeDtypeStruct((LANES, cluster_sizes.shape[0] * BLOCK), jnp.bfloat16),
-        in_specs=[pl.BlockSpec(memory_space=pltpu.SMEM)]
-        + [pl.BlockSpec(memory_space=pltpu.VMEM)],
+        in_specs=[pl.BlockSpec(memory_space=pltpu.SMEM)],
         compiler_params=pltpu.CompilerParams(vmem_limit_bytes=VMEM_LIMIT),
         name="live_labels",
-    )(cluster_sizes, weights)
+    )(cluster_sizes)
 
 
 def block_kernel(piece_rows, top_count, pos_count, *refs):
@@ -238,38 +235,45 @@
         slopes.extend(found)
         return grads
 
-    own = pack(features, shortlist, positives)
-    live_table = live_labels(cluster_sizes, weights)
-    (own_grad,) = take([own])
-    below, above = own, own
+    ids = instance_ids(shortlist, positives, width)
+    live_table = live_labels(cluster_sizes)
+    own = jnp.concatenate([features, ids], axis=0)
     below_grad, above_grad = {}, {}
-    sum_up = sum_down = None
+    sum_up = sum_down = last_sent = None
 
     def advance(j):
-        nonlocal sum_up, sum_down
+        nonlocal sum_up, sum_down, last_sent
         first = below_grad[j][0] if j in below_grad else above_grad[clus_count - j][0]
         second = above_grad[j][1] if j in above_grad else below_grad[clus_count - j][1]
         if sum_up is not None:
             first, second = add(first, sum_up), add(second, sum_down)
+        last_sent = first, second
         sum_up, sum_down = send_up(first), send_down(second)
 
-    for k in range(1, steps + 1):
-        if k > 1:
-            before = own_grad[0] if k == 2 else below_grad[k - 2][0]
+    below, below_ids = send_up(features), send_up(ids)
+    above, above_ids = send_down(features), send_down(ids)
+    below = jnp.concatenate([below, below_ids], axis=0)
+    above = jnp.concatenate([above, above_ids], axis=0)
+    for k in range(2, steps + 1):
+        if k > 2:
+            before = below_grad[k - 2][0]
             below, above = after(below, before), after(above, before)
         if k < steps:
             arriving = send_up(below), send_down(above)
         else:
             ends = jnp.concatenate([below[:half], below[inst_rows:]], axis=0)
             opposite = [send_up(ends), send_down(above[half:inst_rows])]
-        if k > 1:
+        if k == 3 or steps < 3:
+            below_grad[k - 1], above_grad[k - 1], own_grad = take([below], [above], [own])
+        else:
             below_grad[k - 1], above_grad[k - 1] = take([below], [above])
-            advance(k - 1)
+        advance(k - 1)
         if k < steps:
             below, above = arriving
     (far_grad,) = take([after(opposite[0], below_grad[steps - 1][0]), opposite[1]])
     below_grad[steps] = above_grad[steps] = far_grad
     advance(steps)
+    slopes[-1] = after(slopes[-1], *last_sent)
 
     scale = 1.0 / math.sqrt(inst_rows * seq_count * top_count // local_count)
 
@@ -278,9 +282,9 @@
 
     far, near = list(range(seq_count // 2, seq_count)), list(range(seq_count // 2))
     terms = dict(zip(far, weight_work(used, slopes, far, part_width, scale)))
-    sum_up, sum_down = after(sum_up, terms[far[0]]), after(sum_down, terms[far[0]])
+    terms.update(zip(near, weight_work(used, slopes, near, part_width, scale)))
+    sum_up, sum_down = after(sum_up, terms[near[0]]), after(sum_down, terms[near[0]])
     advance(steps + 1)
-    terms.update(zip(near, weight_work(used, slopes, near, part_width, scale)))
     terms = {q: [term] for q, term in terms.items()}
     bit = 1
     while bit < seq_count:

time: 68.9 us -> 65.9 us (0.956)
  waiting for transfers between devices: 23.4 us -> 18.9 us
  starting transfers between devices: 25.8 us -> 28.7 us
  local copies, waits for them, and re-layouts: 5.59 us -> 3.68 us
  other arithmetic: 2.33 us -> 3.3 us
    ppermute x11 -> x12, starting transfers between devices: 6.22 us -> 15.7 us  [send_down(): return lax.ppermute(array, 'clus', down)]
    ppermute x11 -> x12, starting transfers between devices: 17.6 us -> 10.6 us  [send_up(): return lax.ppermute(array, 'clus', up)]
    ppermute x11 -> x12, waiting for transfers between devices: 13 us -> 10.6 us  [send_up(): return lax.ppermute(array, 'clus', up)]
    unnamed x12 -> x10, local copies, waits for them, and re-layouts: 5.57 us -> 3.65 us
    ppermute x3, waiting for transfers between devices: 1.59 us -> 0.32 us  [seq_send(): return lax.ppermute(array, 'seq', [(k, k ^ bit) for k in range(seq_count)])]
    concatenate x0 -> x1, other arithmetic: none -> 0.97 us  [local(): own = jnp.concatenate([features, ids], axis=0)]
    ppermute x11 -> x12, waiting for transfers between devices: 8.8 us -> 8 us  [send_down(): return lax.ppermute(array, 'clus', down)]
    pallas_call x5 -> x4, Pallas kernels: 7.46 us -> 6.98 us  [block_work(): pl.pallas_call(functools.partial(block_kernel, piece_rows, top_count, pos...]
  transfers between devices with their start and end apart: 25 -> 27, of which waited for: 14 -> 10; matrix products, arithmetic and copies ran while one was open for 2% -> 4% of each run, Pallas kernels for 15% -> 16%
where the time goes in v8:
time: 65.9 us; the launch traced here: 65.6 us
  starting transfers between devices  28.7 us (44%)
  waiting for transfers between devices  18.9 us (29%)
  Pallas kernels  10.2 us (15%)
  local copies, waits for them, and re-layouts  3.68 us (6%)
  other arithmetic  3.3 us (5%)
  between operations  0.89 us (1%)
    ppermute x12, starting transfers between devices, send_down(): return lax.ppermute(array, 'clus', down)  15.7 us
    ppermute x12, starting transfers between devices, send_up(): return lax.ppermute(array, 'clus', up)  10.6 us
    ppermute x12, waiting for transfers between devices, send_up(): return lax.ppermute(array, 'clus', up)  10.6 us
    ppermute x12, waiting for transfers between devices, send_down(): return lax.ppermute(array, 'clus', down)  8 us
    pallas_call x4, Pallas kernels, block_work(): pl.pallas_call(functools.partial(block_kernel, piece_rows, top_count, pos...  6.98 us
    unnamed x10, local copies, waits for them, and re-layouts  3.65 us
    pallas_call x2, Pallas kernels, weight_work(): pl.pallas_call(functools.partial(weight_kernel, piece_rows, column_blocks...  2.6 us
    ppermute x3, starting transfers between devices, seq_send(): return lax.ppermute(array, 'seq', [(k, k ^ bit) for k in range(seq_count)])  2.3 us
  transfers between devices with their start and end apart: 27, of which 10 were waited for; matrix products, arithmetic and copies ran while one was open for 4% of the time, Pallas kernels for 16%

profile of v8, /device:TPU:0, one launch (start us, length us, event | category | flops | bytes accessed | tf_op | source)
XLA Modules:
  0.0 65.6 jit_solution(3185658944541559635)
XLA Ops:
  0.6 3.1 %collective-permute-start = (bf16[128,1024]{1,0:T(8,128)(2,1)}, bf16[128,1024]{1,0:T(8,128)(2,1)S(1)}, u32[]{:S(2)}, u32[]{:S(2)}) collective-permute-start(bf16[128,1024]{1,0:T(8,128)(2,1)} %param.5), channel_id=1, source_target_pairs={{0,2},{2,4},{4,6},{6,7},{7,5},{5,3},{3,1},{1,0},{8,10},{10,12},{12... | collective-permute-start | bytes 786440 | tf_op jit(solution)/shard_map/ppermute | solution.py:225
  3.7 0.7 %copy-done.1 = s32[128,16]{0,1:T(8,128)S(1)} copy-done((s32[128,16]{0,1:T(8,128)S(1)}, s32[128,16]{0,1:T(8,128)}, u32[]{:S(2)}) %copy-start.1) | copy-done | bytes 8216
  5.1 2.1 %collective-permute-start.1 = (bf16[8,1024]{1,0:T(8,128)(2,1)S(1)}, bf16[8,1024]{1,0:T(8,128)(2,1)S(1)}, u32[]{:S(2)}, u32[]{:S(2)}) collective-permute-start(bf16[8,1024]{1,0:T(8,128)(2,1)S(1)} %instance_ids.1), channel_id=1, source_target_pairs={{0,2},{2,4},{4,6},{6,7},{7,5},{5,3},{3,1},{1,0},{8,10},{10,12},{12... | collective-permute-start | bytes 49160 | tf_op jit(solution)/shard_map/ppermute | solution.py:225
  7.2 3.1 %collective-permute-done = bf16[128,1024]{1,0:T(8,128)(2,1)S(1)} collective-permute-done((bf16[128,1024]{1,0:T(8,128)(2,1)}, bf16[128,1024]{1,0:T(8,128)(2,1)S(1)}, u32[]{:S(2)}, u32[]{:S(2)}) %collective-permute-start) | collective-permute-done | bytes 262176 | tf_op jit(solution)/shard_map/ppermute | solution.py:225
  10.5 1.8 %collective-permute-start.2 = (bf16[136,1024]{1,0:T(8,128)(2,1)S(1)}, bf16[136,1024]{1,0:T(8,128)(2,1)S(1)}, u32[]{:S(2)}, u32[]{:S(2)}) collective-permute-start(bf16[136,1024]{1,0:T(8,128)(2,1)S(1)} %constant_dynamic-update-slice_fusion.refs_0_), channel_id=1, source_target_pairs={{0,2},{2,4},{4,6},{6,7},{7,5},{5,3},{3,1},{1,0},{8,10},{10,12},{12... | collective-permute-start | bytes 835592 | tf_op jit(solution)/shard_map/ppermute | solution.py:225
  13.9 1.0 %pad_maximum_fusion.refs_2_.refs_4_ = bf16[136,1024]{1,0:T(8,128)(2,1)S(1)} fusion(bf16[8,1024]{1,0:T(8,128)(2,1)S(1)} %instance_ids.1, bf16[128,1024]{1,0:T(8,128)(2,1)} %param.5), kind=kLoop, calls=%fused_computation.2 | loop fusion | flops 557056 | bytes 557056 | tf_op jit(solution)/shard_map/concatenate | solution.py:240
  14.9 1.6 %copy-done = bf16[1024,1024]{1,0:T(8,128)(2,1)S(1)} copy-done((bf16[1024,1024]{1,0:T(8,128)(2,1)S(1)}, bf16[1024,1024]{1,0:T(8,128)(2,1)}, u32[]{:S(2)}) %copy-start) | copy-done | bytes 2097176
  16.5 1.7 %block_work.4 = (bf16[64,1024]{1,0:T(8,128)(2,1)S(1)}, bf16[64,1024]{1,0:T(8,128)(2,1)S(1)}, bf16[64,1024]{1,0:T(8,128)(2,1)S(1)}, bf16[64,1024]{1,0:T(8,128)(2,...) custom-call(bf16[136,1024]{1,0:T(8,128)(2,1)S(1)} %constant_dynamic-update-slice_fusion.refs_0_, ...), custom_call_target="tpu_custom_call" | custom-call | flops 1073741824 | bytes 3670016 | tf_op jit(solution)/shard_map/block_work/pallas_call | solution.py:144
  18.2 1.8 %collective-permute-start.13 = (bf16[64,1024]{1,0:T(8,128)(2,1)S(1)}, bf16[64,1024]{1,0:T(8,128)(2,1)S(1)}, u32[]{:S(2)}, u32[]{:S(2)}) collective-permute-start(bf16[64,1024]{1,0:T(8,128)(2,1)S(1)} %get-tuple-element.62), channel_id=1, source_target_pairs={{2,0},{4,2},{6,4},{7,6},{5,7},{3,5},{1,3},{0,1},{10,8},{12,10},{14... | collective-permute-start | bytes 393224 | tf_op jit(solution)/shard_map/ppermute | solution.py:228
  20.2 1.8 %collective-permute-start.6 = (bf16[136,1024]{1,0:T(8,128)(2,1)S(1)}, bf16[136,1024]{1,0:T(8,128)(2,1)S(1)}, u32[]{:S(2)}, u32[]{:S(2)}) collective-permute-start(bf16[136,1024]{1,0:T(8,128)(2,1)S(1)} %collective-permute-done.2.refs_0_.refs_2_), channel_id=1, source_target_pairs={{0,2},{2,4},{4,6},{6,7},{7,5},{5,3},{3,1},{1,0},{8,10},{10,12},{12... | collective-permute-start | bytes 835592 | tf_op jit(solution)/shard_map/ppermute | solution.py:225
  22.3 2.4 %block_work.5 = (bf16[64,1024]{1,0:T(8,128)(2,1)S(1)}, bf16[64,1024]{1,0:T(8,128)(2,1)S(1)}, bf16[64,1024]{1,0:T(8,128)(2,1)S(1)}, bf16[64,1024]{1,0:T(8,128)(2,...) custom-call(bf16[136,1024]{1,0:T(8,128)(2,1)S(1)} %collective-permut, ...), custom_call_target="tpu_custom_call" | custom-call | flops 1610612736 | bytes 4456448 | tf_op jit(solution)/shard_map/block_work/pallas_call | solution.py:144
  24.7 1.8 %collective-permute-start.14 = (bf16[64,1024]{1,0:T(8,128)(2,1)S(1)}, bf16[64,1024]{1,0:T(8,128)(2,1)S(1)}, u32[]{:S(2)}, u32[]{:S(2)}) collective-permute-start(bf16[64,1024]{1,0:T(8,128)(2,1)S(1)} %add_convert_fusion.12), channel_id=1, source_target_pairs={{2,0},{4,2},{6,4},{7,6},{5,7},{3,5},{1,3},{0,1},{10,8},{12,10},{14... | collective-permute-start | bytes 393224 | tf_op jit(solution)/shard_map/ppermute | solution.py:228
  26.9 3.9 %collective-permute-done.6.refs_0_.refs_5_ = bf16[136,1024]{1,0:T(8,128)(2,1)S(1)} collective-permute-done((bf16[136,1024]{1,0:T(8,128)(2,1)S(1)}, bf16[136,1024]{1,0:T(8,128)(2,1)S(1)}, u32[]{:S(2)}, u32[]{:S(2)}) %collective-permute-start.6) | collective-permute-done | bytes 278560 | tf_op jit(solution)/shard_map/ppermute | solution.py:225
  30.8 1.7 %block_work.6 = (bf16[64,1024]{1,0:T(8,128)(2,1)S(1)}, bf16[64,1024]{1,0:T(8,128)(2,1)S(1)}, bf16[64,1024]{1,0:T(8,128)(2,1)S(1)}, bf16[64,1024]{1,0:T(8,128)(2,...) custom-call(bf16[136,1024]{1,0:T(8,128)(2,1)S(1)} %collective-permute-done.6.refs_0_.refs_5_, ...), custom_call_target="tpu_custom_call" | custom-call | flops 1073741824 | bytes 3670016 | tf_op jit(solution)/shard_map/block_work/pallas_call | solution.py:144
  32.6 1.6 %collective-permute-start.15 = (bf16[64,1024]{1,0:T(8,128)(2,1)S(1)}, bf16[64,1024]{1,0:T(8,128)(2,1)S(1)}, u32[]{:S(2)}, u32[]{:S(2)}) collective-permute-start(bf16[64,1024]{1,0:T(8,128)(2,1)S(1)} %add_convert_fusion.11), channel_id=1, source_target_pairs={{2,0},{4,2},{6,4},{7,6},{5,7},{3,5},{1,3},{0,1},{10,8},{12,10},{14... | collective-permute-start | bytes 393224 | tf_op jit(solution)/shard_map/ppermute | solution.py:228
  34.8 1.6 %collective-permute-start.9 = (bf16[64,1024]{1,0:T(8,128)(2,1)S(1)}, bf16[64,1024]{1,0:T(8,128)(2,1)S(1)}, u32[]{:S(2)}, u32[]{:S(2)}) collective-permute-start(bf16[64,1024]{1,0:T(8,128)(2,1)S(1)} %slice.11), channel_id=1, source_target_pairs={{2,0},{4,2},{6,4},{7,6},{5,7},{3,5},{1,3},{0,1},{10,8},{12,10},{14... | collective-permute-start | bytes 393224 | tf_op jit(solution)/shard_map/ppermute | solution.py:228
  36.9 2.6 %collective-permute-done.8.refs_0_.refs_7_ = bf16[72,1024]{1,0:T(8,128)(2,1)S(1)} collective-permute-done((bf16[72,1024]{1,0:T(8,128)(2,1)S(1)}, bf16[72,1024]{1,0:T(8,128)(2,1)S(1)}, u32[]{:S(2)}, u32[]{:S(2)}) %collective-permute-start.8) | collective-permute-done | bytes 147488 | tf_op jit(solution)/shard_map/ppermute | solution.py:225
  39.5 0.8 %collective-permute-done.9.refs_1_.refs_8_ = bf16[64,1024]{1,0:T(8,128)(2,1)S(1)} collective-permute-done((bf16[64,1024]{1,0:T(8,128)(2,1)S(1)}, bf16[64,1024]{1,0:T(8,128)(2,1)S(1)}, u32[]{:S(2)}, u32[]{:S(2)}) %collective-permute-start.9) | collective-permute-done | bytes 131104 | tf_op jit(solution)/shard_map/ppermute | solution.py:228
  40.3 1.2 %block_work.7 = (bf16[64,1024]{1,0:T(8,128)(2,1)S(1)}, bf16[64,1024]{1,0:T(8,128)(2,1)S(1)}, bf16[128,1024]{1,0:T(8,128)(2,1)S(1)}) custom-call(bf16[72,1024]{1,0:T(8,128)(2,1)S(1)} %collective-permute-done.8.refs_0_.refs_7_, bf16[64,1024]{1,0:T(8,128)(2,1)S(1)} %collective-permute-done.9.refs_1_.refs_8_, bf16[1024,1024]{1,0:T(8,128)(2,1)S(1)} %copy-done, ...), custom_call_target="tpu_custom_call" | custom-call | flops 536870912 | bytes 2883584 | tf_op jit(solution)/shard_map/block_work/pallas_call | solution.py:144
  41.5 2.2 %collective-permute-start.23 = (bf16[64,1024]{1,0:T(8,128)(2,1)S(1)}, bf16[64,1024]{1,0:T(8,128)(2,1)S(1)}, u32[]{:S(2)}, u32[]{:S(2)}) collective-permute-start(bf16[64,1024]{1,0:T(8,128)(2,1)S(1)} %add_convert_fusion.10), channel_id=1, source_target_pairs={{2,0},{4,2},{6,4},{7,6},{5,7},{3,5},{1,3},{0,1},{10,8},{12,10},{14... | collective-permute-start | bytes 393224 | tf_op jit(solution)/shard_map/ppermute | solution.py:228
  43.9 1.3 %weight_work.3 = (bf16[1024,256]{1,0:T(8,128)(2,1)S(1)}, bf16[1024,256]{1,0:T(8,128)(2,1)S(1)}) custom-call(bf16[136,1024]{1,0:T(8,128)(2,1)S(1)} %constant_dynamic-update-slice_fusion.refs_0_, bf16[136,1024]{1,0:T(8,128)(2,1)S(1)} %constant_dynamic-update-slice_fusion.2.refs_1_, bf16[136,1024]{1,0:T(8,128)(2,1)S(1)} %collective-permute-done.2.refs_0_.refs_2_, ...), custom_call_target="tpu_custom_call" | custom-call | flops 1073741824 | bytes 4718592 | tf_op jit(solution)/shard_map/weight_work/pallas_call | solution.py:187
  45.3 1.3 %weight_work.2 = (bf16[1024,256]{1,0:T(8,128)(2,1)S(1)}, bf16[1024,256]{1,0:T(8,128)(2,1)S(1)}) custom-call(bf16[136,1024]{1,0:T(8,128)(2,1)S(1)} %constant_dynamic-update-slice_fusion.refs_0_, bf16[136,1024]{1,0:T(8,128)(2,1)S(1)} %constant_dynamic-update-slice_fusion.2.refs_1_, bf16[136,1024]{1,0:T(8,128)(2,1)S(1)} %collective-permute-done.2.refs_0_.refs_2_, ...), custom_call_target="tpu_custom_call" | custom-call | flops 1073741824 | bytes 4718592 | tf_op jit(solution)/shard_map/weight_work/pallas_call | solution.py:187
  47.2 2.1 %collective-permute-start.24 = (bf16[64,1024]{1,0:T(8,128)(2,1)S(1)}, bf16[64,1024]{1,0:T(8,128)(2,1)S(1)}, u32[]{:S(2)}, u32[]{:S(2)}) collective-permute-start(bf16[64,1024]{1,0:T(8,128)(2,1)S(1)} %add_convert_fusion.5), channel_id=1, source_target_pairs={{2,0},{4,2},{6,4},{7,6},{5,7},{3,5},{1,3},{0,1},{10,8},{12,10},{14... | collective-permute-start | bytes 393224 | tf_op jit(solution)/shard_map/ppermute | solution.py:228
  49.5 1.7 %collective-permute-start.18 = (bf16[1024,256]{1,0:T(8,128)(2,1)S(1)}, bf16[1024,256]{1,0:T(8,128)(2,1)S(1)}, u32[]{:S(2)}, u32[]{:S(2)}) collective-permute-start(bf16[1024,256]{1,0:T(8,128)(2,1)S(1)} %add_convert_fusion.1), channel_id=1, source_target_pairs={{0,16},{8,24},{16,0},{24,8},{1,17},{9,25},{17,1},{25,9},{2,18},{10... | collective-permute-start | bytes 1572872 | tf_op jit(solution)/shard_map/ppermute | solution.py:281
  51.2 1.5 %collective-permute-done.24 = bf16[64,1024]{1,0:T(8,128)(2,1)S(1)} collective-permute-done((bf16[64,1024]{1,0:T(8,128)(2,1)S(1)}, bf16[64,1024]{1,0:T(8,128)(2,1)S(1)}, u32[]{:S(2)}, u32[]{:S(2)}) %collective-permute-start.24) | collective-permute-done | bytes 131104 | tf_op jit(solution)/shard_map/ppermute | solution.py:228
  52.7 2.1 %collective-permute-start.25 = (bf16[64,1024]{1,0:T(8,128)(2,1)S(1)}, bf16[64,1024]{1,0:T(8,128)(2,1)S(1)}, u32[]{:S(2)}, u32[]{:S(2)}) collective-permute-start(bf16[64,1024]{1,0:T(8,128)(2,1)S(1)} %add_convert_fusion.4), channel_id=1, source_target_pairs={{2,0},{4,2},{6,4},{7,6},{5,7},{3,5},{1,3},{0,1},{10,8},{12,10},{14... | collective-permute-start | bytes 393224 | tf_op jit(solution)/shard_map/ppermute | solution.py:228
  54.9 2.8 %collective-permute-done.25 = bf16[64,1024]{1,0:T(8,128)(2,1)S(1)} collective-permute-done((bf16[64,1024]{1,0:T(8,128)(2,1)S(1)}, bf16[64,1024]{1,0:T(8,128)(2,1)S(1)}, u32[]{:S(2)}, u32[]{:S(2)}) %collective-permute-start.25) | collective-permute-done | bytes 131104 | tf_op jit(solution)/shard_map/ppermute | solution.py:228
  57.7 2.1 %collective-permute-start.26 = (bf16[64,1024]{1,0:T(8,128)(2,1)S(1)}, bf16[64,1024]{1,0:T(8,128)(2,1)S(1)}, u32[]{:S(2)}, u32[]{:S(2)}) collective-permute-start(bf16[64,1024]{1,0:T(8,128)(2,1)S(1)} %add_convert_fusion.3), channel_id=1, source_target_pairs={{2,0},{4,2},{6,4},{7,6},{5,7},{3,5},{1,3},{0,1},{10,8},{12,10},{14... | collective-permute-start | bytes 393224 | tf_op jit(solution)/shard_map/ppermute | solution.py:228
  59.9 2.8 %collective-permute-done.26 = bf16[64,1024]{1,0:T(8,128)(2,1)S(1)} collective-permute-done((bf16[64,1024]{1,0:T(8,128)(2,1)S(1)}, bf16[64,1024]{1,0:T(8,128)(2,1)S(1)}, u32[]{:S(2)}, u32[]{:S(2)}) %collective-permute-start.26) | collective-permute-done | bytes 131104 | tf_op jit(solution)/shard_map/ppermute | solution.py:228
  63.1 1.0 %add_convert_fusion = bf16[1024,256]{1,0:T(8,128)(2,1)} fusion(bf16[1024,256]{1,0:T(8,128)(2,1)S(1)} %collective-permute-done.18, bf16[1024,256]{1,0:T(8,128)(2,1)S(1)} %collective-permute-done.16, bf16[1024,256]{1,0:T(8,128)(2,1)S(1)} %get-tuple-element.64), kind=kLoop, calls=%fused_computation | loop fusion | flops 1572864 | bytes 2097152 | tf_op jit(solution)/shard_map/convert_element_type | solution.py:205
  64.1 0.8 %collective-permute-done.22 = bf16[64,1024]{1,0:T(8,128)(2,1)S(1)} collective-permute-done((bf16[64,1024]{1,0:T(8,128)(2,1)S(1)}, bf16[64,1024]{1,0:T(8,128)(2,1)S(1)}, u32[]{:S(2)}, u32[]{:S(2)}) %collective-permute-start.22) | collective-permute-done | bytes 131104 | tf_op jit(solution)/shard_map/ppermute | solution.py:225
  64.9 0.7 %pad_maximum_fusion.1 = bf16[128,1024]{1,0:T(8,128)(2,1)} fusion(bf16[64,1024]{1,0:T(8,128)(2,1)S(1)} %add_convert_fusion.2, bf16[64,1024]{1,0:T(8,128)(2,1)S(1)} %add_convert_fusion.6), kind=kLoop, calls=%fused_computation.3 | loop fusion | flops 524288 | bytes 524288 | tf_op jit(solution)/shard_map/concatenate | solution.py:302
  (64 shorter events, 6.2 us)
Async XLA Ops:
  0.6 9.7 %collective-permute-start = (bf16[128,1024]{1,0:T(8,128)(2,1)}, bf16[128,1024]{1,0:T(8,128)(2,1)S(1)}, u32[]{:S(2)}, u32[]{:S(2)}) collective-permute-start(bf16[128,1024]{1,0:T(8,128)(2,1)} %param.5), channel_id=1, source_target_pairs={{0,2},{2,4},{4,6},{6,7},{7,5},{5,3},{3,1},{1,0},{8,10},{10,12},{12... | collective-permute-start | bytes 786440 | tf_op jit(solution)/shard_map/ppermute | solution.py:225
  3.7 8.6 %collective-permute-start.3 = (bf16[128,1024]{1,0:T(8,128)(2,1)}, bf16[128,1024]{1,0:T(8,128)(2,1)S(1)}, u32[]{:S(2)}, u32[]{:S(2)}) collective-permute-start(bf16[128,1024]{1,0:T(8,128)(2,1)} %param.5), channel_id=1, source_target_pairs={{2,0},{4,2},{6,4},{7,6},{5,7},{3,5},{1,3},{0,1},{10,8},{12,10},{14... | collective-permute-start | bytes 786440 | tf_op jit(solution)/shard_map/ppermute | solution.py:228
  3.7 0.7 %copy-start.1 = (s32[128,16]{0,1:T(8,128)S(1)}, s32[128,16]{0,1:T(8,128)}, u32[]{:S(2)}) copy-start(s32[128,16]{0,1:T(8,128)} %param.6) | copy-start | bytes 24580
  4.4 0.7 %copy-start.2 = (s32[128,4]{0,1:T(4,128)S(1)}, s32[128,4]{0,1:T(4,128)}, u32[]{:S(2)}) copy-start(s32[128,4]{0,1:T(4,128)} %param.7) | copy-start | bytes 6148
  5.1 5.4 %collective-permute-start.1 = (bf16[8,1024]{1,0:T(8,128)(2,1)S(1)}, bf16[8,1024]{1,0:T(8,128)(2,1)S(1)}, u32[]{:S(2)}, u32[]{:S(2)}) collective-permute-start(bf16[8,1024]{1,0:T(8,128)(2,1)S(1)} %instance_ids.1), channel_id=1, source_target_pairs={{0,2},{2,4},{4,6},{6,7},{7,5},{5,3},{3,1},{1,0},{8,10},{10,12},{12... | collective-permute-start | bytes 49160 | tf_op jit(solution)/shard_map/ppermute | solution.py:225
  7.2 5.2 %collective-permute-start.4 = (bf16[8,1024]{1,0:T(8,128)(2,1)S(1)}, bf16[8,1024]{1,0:T(8,128)(2,1)S(1)}, u32[]{:S(2)}, u32[]{:S(2)}) collective-permute-start(bf16[8,1024]{1,0:T(8,128)(2,1)S(1)} %instance_ids.1), channel_id=1, source_target_pairs={{2,0},{4,2},{6,4},{7,6},{5,7},{3,5},{1,3},{0,1},{10,8},{12,10},{14... | collective-permute-start | bytes 49160 | tf_op jit(solution)/shard_map/ppermute | solution.py:228
  10.5 9.7 %collective-permute-start.2 = (bf16[136,1024]{1,0:T(8,128)(2,1)S(1)}, bf16[136,1024]{1,0:T(8,128)(2,1)S(1)}, u32[]{:S(2)}, u32[]{:S(2)}) collective-permute-start(bf16[136,1024]{1,0:T(8,128)(2,1)S(1)} %constant_dynamic-update-slice_fusion.refs_0_), channel_id=1, source_target_pairs={{0,2},{2,4},{4,6},{6,7},{7,5},{5,3},{3,1},{1,0},{8,10},{10,12},{12... | collective-permute-start | bytes 835592 | tf_op jit(solution)/shard_map/ppermute | solution.py:225
  12.4 7.9 %collective-permute-start.5 = (bf16[136,1024]{1,0:T(8,128)(2,1)S(1)}, bf16[136,1024]{1,0:T(8,128)(2,1)S(1)}, u32[]{:S(2)}, u32[]{:S(2)}) collective-permute-start(bf16[136,1024]{1,0:T(8,128)(2,1)S(1)} %constant_dynamic-update-slice_fusion.2.refs_1_), channel_id=1, source_target_pairs={{2,0},{4,2},{6,4},{7,6},{5,7},{3,5},{1,3},{0,1},{10,8},{12,10},{14... | collective-permute-start | bytes 835592 | tf_op jit(solution)/shard_map/ppermute | solution.py:228
  12.6 0.7 copy-start.3
  14.9 1.6 %copy-start = (bf16[1024,1024]{1,0:T(8,128)(2,1)S(1)}, bf16[1024,1024]{1,0:T(8,128)(2,1)}, u32[]{:S(2)}) copy-start(bf16[1024,1024]{1,0:T(8,128)(2,1)} %refs_2_.5) | copy-start | bytes 6291460
  18.2 6.5 %collective-permute-start.13 = (bf16[64,1024]{1,0:T(8,128)(2,1)S(1)}, bf16[64,1024]{1,0:T(8,128)(2,1)S(1)}, u32[]{:S(2)}, u32[]{:S(2)}) collective-permute-start(bf16[64,1024]{1,0:T(8,128)(2,1)S(1)} %get-tuple-element.62), channel_id=1, source_target_pairs={{2,0},{4,2},{6,4},{7,6},{5,7},{3,5},{1,3},{0,1},{10,8},{12,10},{14... | collective-permute-start | bytes 393224 | tf_op jit(solution)/shard_map/ppermute | solution.py:228
  19.9 6.6 %collective-permute-start.10 = (bf16[64,1024]{1,0:T(8,128)(2,1)S(1)}, bf16[64,1024]{1,0:T(8,128)(2,1)S(1)}, u32[]{:S(2)}, u32[]{:S(2)}) collective-permute-start(bf16[64,1024]{1,0:T(8,128)(2,1)S(1)} %get-tuple-element.41), channel_id=1, source_target_pairs={{0,2},{2,4},{4,6},{6,7},{7,5},{5,3},{3,1},{1,0},{8,10},{10,12},{12... | collective-permute-start | bytes 393224 | tf_op jit(solution)/shard_map/ppermute | solution.py:225
  20.2 10.6 %collective-permute-start.6 = (bf16[136,1024]{1,0:T(8,128)(2,1)S(1)}, bf16[136,1024]{1,0:T(8,128)(2,1)S(1)}, u32[]{:S(2)}, u32[]{:S(2)}) collective-permute-start(bf16[136,1024]{1,0:T(8,128)(2,1)S(1)} %collective-permute-done.2.refs_0_.refs_2_), channel_id=1, source_target_pairs={{0,2},{2,4},{4,6},{6,7},{7,5},{5,3},{3,1},{1,0},{8,10},{10,12},{12... | collective-permute-start | bytes 835592 | tf_op jit(solution)/shard_map/ppermute | solution.py:225
  22.0 8.8 %collective-permute-start.7 = (bf16[136,1024]{1,0:T(8,128)(2,1)S(1)}, bf16[136,1024]{1,0:T(8,128)(2,1)S(1)}, u32[]{:S(2)}, u32[]{:S(2)}) collective-permute-start(bf16[136,1024]{1,0:T(8,128)(2,1)S(1)} %collective-permute-done.5.refs_1_.refs_3_), channel_id=1, source_target_pairs={{2,0},{4,2},{6,4},{7,6},{5,7},{3,5},{1,3},{0,1},{10,8},{12,10},{14... | collective-permute-start | bytes 835592 | tf_op jit(solution)/shard_map/ppermute | solution.py:228
  24.7 7.8 %collective-permute-start.14 = (bf16[64,1024]{1,0:T(8,128)(2,1)S(1)}, bf16[64,1024]{1,0:T(8,128)(2,1)S(1)}, u32[]{:S(2)}, u32[]{:S(2)}) collective-permute-start(bf16[64,1024]{1,0:T(8,128)(2,1)S(1)} %add_convert_fusion.12), channel_id=1, source_target_pairs={{2,0},{4,2},{6,4},{7,6},{5,7},{3,5},{1,3},{0,1},{10,8},{12,10},{14... | collective-permute-start | bytes 393224 | tf_op jit(solution)/shard_map/ppermute | solution.py:228
  26.6 9.8 %collective-permute-start.11 = (bf16[64,1024]{1,0:T(8,128)(2,1)S(1)}, bf16[64,1024]{1,0:T(8,128)(2,1)S(1)}, u32[]{:S(2)}, u32[]{:S(2)}) collective-permute-start(bf16[64,1024]{1,0:T(8,128)(2,1)S(1)} %add_convert_fusion.15), channel_id=1, source_target_pairs={{0,2},{2,4},{4,6},{6,7},{7,5},{5,3},{3,1},{1,0},{8,10},{10,12},{12... | collective-permute-start | bytes 393224 | tf_op jit(solution)/shard_map/ppermute | solution.py:225
  32.6 8.8 %collective-permute-start.15 = (bf16[64,1024]{1,0:T(8,128)(2,1)S(1)}, bf16[64,1024]{1,0:T(8,128)(2,1)S(1)}, u32[]{:S(2)}, u32[]{:S(2)}) collective-permute-start(bf16[64,1024]{1,0:T(8,128)(2,1)S(1)} %add_convert_fusion.11), channel_id=1, source_target_pairs={{2,0},{4,2},{6,4},{7,6},{5,7},{3,5},{1,3},{0,1},{10,8},{12,10},{14... | collective-permute-start | bytes 393224 | tf_op jit(solution)/shard_map/ppermute | solution.py:228
  34.3 5.2 %collective-permute-start.8 = (bf16[72,1024]{1,0:T(8,128)(2,1)S(1)}, bf16[72,1024]{1,0:T(8,128)(2,1)S(1)}, u32[]{:S(2)}, u32[]{:S(2)}) collective-permute-start(bf16[72,1024]{1,0:T(8,128)(2,1)S(1)} %pad_maximum_fusion.2), channel_id=1, source_target_pairs={{0,2},{2,4},{4,6},{6,7},{7,5},{5,3},{3,1},{1,0},{8,10},{10,12},{12... | collective-permute-start | bytes 442376 | tf_op jit(solution)/shard_map/ppermute | solution.py:225
  34.8 5.5 %collective-permute-start.9 = (bf16[64,1024]{1,0:T(8,128)(2,1)S(1)}, bf16[64,1024]{1,0:T(8,128)(2,1)S(1)}, u32[]{:S(2)}, u32[]{:S(2)}) collective-permute-start(bf16[64,1024]{1,0:T(8,128)(2,1)S(1)} %slice.11), channel_id=1, source_target_pairs={{2,0},{4,2},{6,4},{7,6},{5,7},{3,5},{1,3},{0,1},{10,8},{12,10},{14... | collective-permute-start | bytes 393224 | tf_op jit(solution)/shard_map/ppermute | solution.py:228
  36.4 7.4 %collective-permute-start.12 = (bf16[64,1024]{1,0:T(8,128)(2,1)S(1)}, bf16[64,1024]{1,0:T(8,128)(2,1)S(1)}, u32[]{:S(2)}, u32[]{:S(2)}) collective-permute-start(bf16[64,1024]{1,0:T(8,128)(2,1)S(1)} %add_convert_fusion.14), channel_id=1, source_target_pairs={{0,2},{2,4},{4,6},{6,7},{7,5},{5,3},{3,1},{1,0},{8,10},{10,12},{12... | collective-permute-start | bytes 393224 | tf_op jit(solution)/shard_map/ppermute | solution.py:225
  41.5 5.6 %collective-permute-start.23 = (bf16[64,1024]{1,0:T(8,128)(2,1)S(1)}, bf16[64,1024]{1,0:T(8,128)(2,1)S(1)}, u32[]{:S(2)}, u32[]{:S(2)}) collective-permute-start(bf16[64,1024]{1,0:T(8,128)(2,1)S(1)} %add_convert_fusion.10), channel_id=1, source_target_pairs={{2,0},{4,2},{6,4},{7,6},{5,7},{3,5},{1,3},{0,1},{10,8},{12,10},{14... | collective-permute-start | bytes 393224 | tf_op jit(solution)/shard_map/ppermute | solution.py:228
  43.8 5.4 %collective-permute-start.19 = (bf16[64,1024]{1,0:T(8,128)(2,1)S(1)}, bf16[64,1024]{1,0:T(8,128)(2,1)S(1)}, u32[]{:S(2)}, u32[]{:S(2)}) collective-permute-start(bf16[64,1024]{1,0:T(8,128)(2,1)S(1)} %add_convert_fusion.13), channel_id=1, source_target_pairs={{0,2},{2,4},{4,6},{6,7},{7,5},{5,3},{3,1},{1,0},{8,10},{10,12},{12... | collective-permute-start | bytes 393224 | tf_op jit(solution)/shard_map/ppermute | solution.py:225
  45.2 4.2 %collective-permute-start.17 = (bf16[1024,256]{1,0:T(8,128)(2,1)S(1)}, bf16[1024,256]{1,0:T(8,128)(2,1)S(1)}, u32[]{:S(2)}, u32[]{:S(2)}) collective-permute-start(bf16[1024,256]{1,0:T(8,128)(2,1)S(1)} %get-tuple-element.67), channel_id=1, source_target_pairs={{0,8},{8,0},{16,24},{24,16},{1,9},{9,1},{17,25},{25,17},{2,10},{10... | collective-permute-start | bytes 1572872 | tf_op jit(solution)/shard_map/ppermute | solution.py:281
  46.6 16.2 %collective-permute-start.16 = (bf16[1024,256]{1,0:T(8,128)(2,1)S(1)}, bf16[1024,256]{1,0:T(8,128)(2,1)S(1)}, u32[]{:S(2)}, u32[]{:S(2)}) collective-permute-start(bf16[1024,256]{1,0:T(8,128)(2,1)S(1)} %get-tuple-element.65), channel_id=1, source_target_pairs={{0,8},{8,0},{16,24},{24,16},{1,9},{9,1},{17,25},{25,17},{2,10},{10... | collective-permute-start | bytes 1572872 | tf_op jit(solution)/shard_map/ppermute | solution.py:281
  47.2 5.5 %collective-permute-start.24 = (bf16[64,1024]{1,0:T(8,128)(2,1)S(1)}, bf16[64,1024]{1,0:T(8,128)(2,1)S(1)}, u32[]{:S(2)}, u32[]{:S(2)}) collective-permute-start(bf16[64,1024]{1,0:T(8,128)(2,1)S(1)} %add_convert_fusion.5), channel_id=1, source_target_pairs={{2,0},{4,2},{6,4},{7,6},{5,7},{3,5},{1,3},{0,1},{10,8},{12,10},{14... | collective-permute-start | bytes 393224 | tf_op jit(solution)/shard_map/ppermute | solution.py:228
  49.3 5.5 %collective-permute-start.20 = (bf16[64,1024]{1,0:T(8,128)(2,1)S(1)}, bf16[64,1024]{1,0:T(8,128)(2,1)S(1)}, u32[]{:S(2)}, u32[]{:S(2)}) collective-permute-start(bf16[64,1024]{1,0:T(8,128)(2,1)S(1)} %add_convert_fusion.9), channel_id=1, source_target_pairs={{0,2},{2,4},{4,6},{6,7},{7,5},{5,3},{3,1},{1,0},{8,10},{10,12},{12... | collective-permute-start | bytes 393224 | tf_op jit(solution)/shard_map/ppermute | solution.py:225
  49.5 13.6 %collective-permute-start.18 = (bf16[1024,256]{1,0:T(8,128)(2,1)S(1)}, bf16[1024,256]{1,0:T(8,128)(2,1)S(1)}, u32[]{:S(2)}, u32[]{:S(2)}) collective-permute-start(bf16[1024,256]{1,0:T(8,128)(2,1)S(1)} %add_convert_fusion.1), channel_id=1, source_target_pairs={{0,16},{8,24},{16,0},{24,8},{1,17},{9,25},{17,1},{25,9},{2,18},{10... | collective-permute-start | bytes 1572872 | tf_op jit(solution)/shard_map/ppermute | solution.py:281
  52.7 5.0 %collective-permute-start.25 = (bf16[64,1024]{1,0:T(8,128)(2,1)S(1)}, bf16[64,1024]{1,0:T(8,128)(2,1)S(1)}, u32[]{:S(2)}, u32[]{:S(2)}) collective-permute-start(bf16[64,1024]{1,0:T(8,128)(2,1)S(1)} %add_convert_fusion.4), channel_id=1, source_target_pairs={{2,0},{4,2},{6,4},{7,6},{5,7},{3,5},{1,3},{0,1},{10,8},{12,10},{14... | collective-permute-start | bytes 393224 | tf_op jit(solution)/shard_map/ppermute | solution.py:228
  54.8 5.0 %collective-permute-start.21 = (bf16[64,1024]{1,0:T(8,128)(2,1)S(1)}, bf16[64,1024]{1,0:T(8,128)(2,1)S(1)}, u32[]{:S(2)}, u32[]{:S(2)}) collective-permute-start(bf16[64,1024]{1,0:T(8,128)(2,1)S(1)} %add_convert_fusion.8), channel_id=1, source_target_pairs={{0,2},{2,4},{4,6},{6,7},{7,5},{5,3},{3,1},{1,0},{8,10},{10,12},{12... | collective-permute-start | bytes 393224 | tf_op jit(solution)/shard_map/ppermute | solution.py:225
  57.7 5.0 %collective-permute-start.26 = (bf16[64,1024]{1,0:T(8,128)(2,1)S(1)}, bf16[64,1024]{1,0:T(8,128)(2,1)S(1)}, u32[]{:S(2)}, u32[]{:S(2)}) collective-permute-start(bf16[64,1024]{1,0:T(8,128)(2,1)S(1)} %add_convert_fusion.3), channel_id=1, source_target_pairs={{2,0},{4,2},{6,4},{7,6},{5,7},{3,5},{1,3},{0,1},{10,8},{12,10},{14... | collective-permute-start | bytes 393224 | tf_op jit(solution)/shard_map/ppermute | solution.py:228
  59.8 5.0 %collective-permute-start.22 = (bf16[64,1024]{1,0:T(8,128)(2,1)S(1)}, bf16[64,1024]{1,0:T(8,128)(2,1)S(1)}, u32[]{:S(2)}, u32[]{:S(2)}) collective-permute-start(bf16[64,1024]{1,0:T(8,128)(2,1)S(1)} %add_convert_fusion.7), channel_id=1, source_target_pairs={{0,2},{2,4},{4,6},{6,7},{7,5},{5,3},{3,1},{1,0},{8,10},{10,12},{12... | collective-permute-start | bytes 393224 | tf_op jit(solution)/shard_map/ppermute | solution.py:225

commit v9 on v8

--- a/solution.py
+++ b/solution.py
@@ -42,7 +42,7 @@
     )(shortlist.T, positives.T)
 
 
-def live_kernel(size_ref, live_ref):
+def live_kernel(size_ref, w_ref, live_ref):
     lane = lax.broadcasted_iota(jnp.int32, (LANES, BLOCK), 1)
     row = lax.broadcasted_iota(jnp.int32, (LANES, BLOCK), 0)
     for c in range(size_ref.shape[0]):
@@ -50,14 +50,17 @@
         live_ref[:, c * BLOCK : (c + 1) * BLOCK] = live.astype(jnp.bfloat16)
 
 
-def live_labels(cluster_sizes):
+def live_labels(cluster_sizes, weights):
     return pl.pallas_call(
         live_kernel,
         out_shape=jax.ShapeDtypeStruct((LANES, cluster_sizes.shape[0] * BLOCK), jnp.bfloat16),
-        in_specs=[pl.BlockSpec(memory_space=pltpu.SMEM)],
+        in_specs=[
+            pl.BlockSpec(memory_space=pltpu.SMEM),
+            pl.BlockSpec(memory_space=pltpu.VMEM),
+        ],
         compiler_params=pltpu.CompilerParams(vmem_limit_bytes=VMEM_LIMIT),
         name="live_labels",
-    )(cluster_sizes)
+    )(cluster_sizes, weights)
 
 
 def block_kernel(piece_rows, top_count, pos_count, *refs):
@@ -65,8 +68,8 @@
     piece_count = sum(len(pieces) for pieces in piece_rows)
     x_refs = refs[:piece_count]
     w_ref, live_ref = refs[piece_count : piece_count + 2]
-    grad_refs = refs[piece_count + 2 : piece_count + 2 + 2 * block_count]
-    slope_refs = refs[piece_count + 2 + 2 * block_count :]
+    grad_refs = refs[piece_count + 2 : 2 * piece_count + 2]
+    slope_refs = refs[2 * piece_count + 2 :]
     labels, width = w_ref.shape
     local_count = labels // BLOCK
     rows = slope_refs[0].shape[0]
@@ -140,10 +143,9 @@
         for pieces in blocks
     ]
     flat_rows = sum(piece_rows, [])
-    half = sum(piece_rows[0]) // 2
     out = pl.pallas_call(
         functools.partial(block_kernel, piece_rows, top_count, pos_count),
-        out_shape=[jax.ShapeDtypeStruct((half, width), jnp.bfloat16)] * (2 * len(blocks))
+        out_shape=[jax.ShapeDtypeStruct((rows, width), jnp.bfloat16) for rows in flat_rows]
         + [jax.ShapeDtypeStruct((sum(rows), labels), jnp.bfloat16) for rows in piece_rows],
         in_specs=[pl.BlockSpec(memory_space=pltpu.VMEM)] * (len(flat_rows) + 2),
         compiler_params=pltpu.CompilerParams(vmem_limit_bytes=VMEM_LIMIT),
@@ -154,8 +156,7 @@
         ),
         name="block_work",
     )(*[piece for pieces in blocks for piece in pieces], weights, live_table)
-    grads = [(out[2 * b], out[2 * b + 1]) for b in range(len(blocks))]
-    return grads, list(out[2 * len(blocks) :])
+    return list(out[: len(flat_rows)]), list(out[len(flat_rows) :])
 
 
 def weight_kernel(piece_rows, column_blocks, scale, *refs):
@@ -236,44 +237,28 @@
         return grads
 
     ids = instance_ids(shortlist, positives, width)
-    live_table = live_labels(cluster_sizes)
+    live_table = live_labels(cluster_sizes, weights)
     own = jnp.concatenate([features, ids], axis=0)
-    below_grad, above_grad = {}, {}
-    sum_up = sum_down = last_sent = None
-
-    def advance(j):
-        nonlocal sum_up, sum_down, last_sent
-        first = below_grad[j][0] if j in below_grad else above_grad[clus_count - j][0]
-        second = above_grad[j][1] if j in above_grad else below_grad[clus_count - j][1]
-        if sum_up is not None:
-            first, second = add(first, sum_up), add(second, sum_down)
-        last_sent = first, second
-        sum_up, sum_down = send_up(first), send_down(second)
-
     below, below_ids = send_up(features), send_up(ids)
     above, above_ids = send_down(features), send_down(ids)
-    below = jnp.concatenate([below, below_ids], axis=0)
-    above = jnp.concatenate([above, above_ids], axis=0)
+    below = jnp.concatenate([after(below, live_table), below_ids], axis=0)
+    above = jnp.concatenate([after(above, live_table), above_ids], axis=0)
+    below_grad, above_grad = {}, {}
     for k in range(2, steps + 1):
         if k > 2:
-            before = below_grad[k - 2][0]
+            before = below_grad[k - 2]
             below, above = after(below, before), after(above, before)
         if k < steps:
             arriving = send_up(below), send_down(above)
         else:
             ends = jnp.concatenate([below[:half], below[inst_rows:]], axis=0)
-            opposite = [send_up(ends), send_down(above[half:inst_rows])]
+            arriving = send_up(ends), send_down(above[half:inst_rows])
         if k == 3 or steps < 3:
             below_grad[k - 1], above_grad[k - 1], own_grad = take([below], [above], [own])
         else:
             below_grad[k - 1], above_grad[k - 1] = take([below], [above])
-        advance(k - 1)
-        if k < steps:
-            below, above = arriving
-    (far_grad,) = take([after(opposite[0], below_grad[steps - 1][0]), opposite[1]])
-    below_grad[steps] = above_grad[steps] = far_grad
-    advance(steps)
-    slopes[-1] = after(slopes[-1], *last_sent)
+        below, above = arriving
+    to_down, to_up = take([after(below, below_grad[steps - 1]), above])
 
     scale = 1.0 / math.sqrt(inst_rows * seq_count * top_count // local_count)
 
@@ -283,25 +268,24 @@
     far, near = list(range(seq_count // 2, seq_count)), list(range(seq_count // 2))
     terms = dict(zip(far, weight_work(used, slopes, far, part_width, scale)))
     terms.update(zip(near, weight_work(used, slopes, near, part_width, scale)))
-    sum_up, sum_down = after(sum_up, terms[near[0]]), after(sum_down, terms[near[0]])
-    advance(steps + 1)
     terms = {q: [term] for q, term in terms.items()}
     bit = 1
     while bit < seq_count:
         for q in [q for q in sorted(terms, reverse=True) if q & bit]:
             values = terms.pop(q)
-            going = add(*values) if len(values) > 1 else values[0]
-            if bit == 2:
-                sum_up, sum_down = after(sum_up, going), after(sum_down, going)
-            terms[q ^ bit].append(seq_send(going, bit))
+            terms[q ^ bit].append(seq_send(add(*values) if len(values) > 1 else values[0], bit))
         bit *= 2
+
+    for k in range(steps, 0, -1):
+        from_above, from_below = send_down(to_down), send_up(to_up)
+        if k == steps:
+            near_below, near_above = below_grad[k - 1], above_grad[k - 1]
+            to_down = jnp.concatenate([add(near_below[:half], from_above), near_below[half:]], axis=0)
+            to_up = jnp.concatenate([near_above[:half], add(near_above[half:], from_below)], axis=0)
+        elif k > 1:
+            to_down, to_up = add(below_grad[k - 1], from_above), add(above_grad[k - 1], from_below)
     weight_grad = add(*terms[0])
-
-    for j in range(steps + 2, clus_count):
-        advance(j)
-    feature_grad = jnp.concatenate(
-        [add(after(own_grad[0], weight_grad), sum_up), add(own_grad[1], sum_down)], axis=0
-    )
+    feature_grad = add(after(own_grad, weight_grad), from_above, from_below)
     return (feature_grad, weight_grad)
 
 

time: 65.9 us -> 64.8 us (0.983)
  starting transfers between devices: 28.7 us -> 22.1 us
  waiting for transfers between devices: 18.9 us -> 25.4 us
  other arithmetic: 3.3 us -> 2.34 us
    ppermute x12 -> x9, starting transfers between devices: 15.7 us -> 3.36 us  [send_down(): return lax.ppermute(array, 'clus', down)]
    ppermute x12 -> x9, waiting for transfers between devices: 10.6 us -> 17.8 us  [send_up(): return lax.ppermute(array, 'clus', up)]
    ppermute x12 -> x9, starting transfers between devices: 10.6 us -> 16.5 us  [send_up(): return lax.ppermute(array, 'clus', up)]
    ppermute x12 -> x9, waiting for transfers between devices: 8 us -> 3.83 us  [send_down(): return lax.ppermute(array, 'clus', down)]
    ppermute x3, waiting for transfers between devices: 0.32 us -> 3.72 us  [seq_send(): return lax.ppermute(array, 'seq', [(k, k ^ bit) for k in range(seq_count)])]
    concatenate x1, other arithmetic: 0.97 us -> 0.02 us  [local(): own = jnp.concatenate([features, ids], axis=0)]
    concatenate x1 -> x2, other arithmetic: 0.72 us -> 0.04 us  [the longest x1 0.02 us: local(): jnp.concatenate([add(near_below[:half], from_above), near_below[half:]],...]
    convert_element_type x16 -> x9, other arithmetic: 1.6 us -> 2.27 us  [add(): return total.astype(jnp.bfloat16)]
  transfers between devices with their start and end apart: 27 -> 21, of which waited for: 10 -> 11; matrix products, arithmetic and copies ran while one was open for 4% -> 2% of each run, Pallas kernels for 16% -> 14%
where the time goes in v9:
time: 64.8 us; the launch traced here: 64.5 us
  waiting for transfers between devices  25.4 us (39%)
  starting transfers between devices  22.1 us (34%)
  Pallas kernels  10.2 us (16%)
  local copies, waits for them, and re-layouts  3.72 us (6%)
  other arithmetic  2.34 us (4%)
  between operations  0.84 us (1%)
    ppermute x9, waiting for transfers between devices, send_up(): return lax.ppermute(array, 'clus', up)  17.8 us
    ppermute x9, starting transfers between devices, send_up(): return lax.ppermute(array, 'clus', up)  16.5 us
    pallas_call x4, Pallas kernels, block_work(): pl.pallas_call(functools.partial(block_kernel, piece_rows, top_count, pos...  6.97 us
    ppermute x9, waiting for transfers between devices, send_down(): return lax.ppermute(array, 'clus', down)  3.83 us
    ppermute x3, waiting for transfers between devices, seq_send(): return lax.ppermute(array, 'seq', [(k, k ^ bit) for k in range(seq_count)])  3.72 us
    unnamed x14, local copies, waits for them, and re-layouts  3.67 us
    ppermute x9, starting transfers between devices, send_down(): return lax.ppermute(array, 'clus', down)  3.36 us
    pallas_call x2, Pallas kernels, weight_work(): pl.pallas_call(functools.partial(weight_kernel, piece_rows, column_blocks...  2.59 us
  transfers between devices with their start and end apart: 21, of which 11 were waited for; matrix products, arithmetic and copies ran while one was open for 2% of the time, Pallas kernels for 14%

profile of v9, /device:TPU:0, one launch (start us, length us, event | category | flops | bytes accessed | tf_op | source)
XLA Modules:
  0.0 64.5 jit_solution(4335223904329782571)
XLA Ops:
  0.6 3.1 %collective-permute-start = (bf16[128,1024]{1,0:T(8,128)(2,1)}, bf16[128,1024]{1,0:T(8,128)(2,1)S(1)}, u32[]{:S(2)}, u32[]{:S(2)}) collective-permute-start(bf16[128,1024]{1,0:T(8,128)(2,1)} %param.5), channel_id=1, source_target_pairs={{0,2},{2,4},{4,6},{6,7},{7,5},{5,3},{3,1},{1,0},{8,10},{10,12},{12... | collective-permute-start | bytes 786440 | tf_op jit(solution)/shard_map/ppermute | solution.py:226
  3.7 0.7 %copy-done.2 = s32[128,16]{0,1:T(8,128)S(1)} copy-done((s32[128,16]{0,1:T(8,128)S(1)}, s32[128,16]{0,1:T(8,128)}, u32[]{:S(2)}) %copy-start.2) | copy-done | bytes 8216
  4.4 0.7 %copy-done.3 = s32[128,4]{0,1:T(4,128)S(1)} copy-done((s32[128,4]{0,1:T(4,128)S(1)}, s32[128,4]{0,1:T(4,128)}, u32[]{:S(2)}) %copy-start.3) | copy-done | bytes 2072
  5.1 2.1 %collective-permute-start.1 = (bf16[8,1024]{1,0:T(8,128)(2,1)S(1)}, bf16[8,1024]{1,0:T(8,128)(2,1)S(1)}, u32[]{:S(2)}, u32[]{:S(2)}) collective-permute-start(bf16[8,1024]{1,0:T(8,128)(2,1)S(1)} %instance_ids.1), channel_id=1, source_target_pairs={{0,2},{2,4},{4,6},{6,7},{7,5},{5,3},{3,1},{1,0},{8,10},{10,12},{12... | collective-permute-start | bytes 49160 | tf_op jit(solution)/shard_map/ppermute | solution.py:226
  7.2 1.6 %copy-done = bf16[1024,1024]{1,0:T(8,128)(2,1)S(1)} copy-done((bf16[1024,1024]{1,0:T(8,128)(2,1)S(1)}, bf16[1024,1024]{1,0:T(8,128)(2,1)}, u32[]{:S(2)}) %copy-start) | copy-done | bytes 2097176
  8.8 0.7 %copy-done.4 = s32[8]{0:T(128)S(1)} copy-done((s32[8]{0:T(128)S(1)}, s32[8]{0:T(128)}, u32[]{:S(2)}) %copy-start.4) | copy-done | bytes 56
  10.5 1.8 %collective-permute-start.2 = (bf16[136,1024]{1,0:T(8,128)(2,1)S(1)}, bf16[136,1024]{1,0:T(8,128)(2,1)S(1)}, u32[]{:S(2)}, u32[]{:S(2)}) collective-permute-start(bf16[136,1024]{1,0:T(8,128)(2,1)S(1)} %constant_dynamic-update-slice_fusion.refs_0_), channel_id=1, source_target_pairs={{0,2},{2,4},{4,6},{6,7},{7,5},{5,3},{3,1},{1,0},{8,10},{10,12},{12... | collective-permute-start | bytes 835592 | tf_op jit(solution)/shard_map/ppermute | solution.py:226
  12.7 1.7 %block_work.4 = (bf16[128,1024]{1,0:T(8,128)(2,1)S(1)}, bf16[128,1024]{1,0:T(8,128)(2,1)S(1)}, bf16[128,1024]{1,0:T(8,128)(2,1)S(1)}, bf16[128,1024]{1,0:T(8,128)(2,1)S(1)}) custom-call(bf16[136,1024]{1,0:T(8,128)(2,1)S(1)} %constant_dynamic-update-slice_fusion.refs_0_, bf16[136,1024]{1,0:T(8,128)(2,1)S(1)} %constant_dynamic-update-slice_fusion.2.refs_1_, ...), custom_call_target="tpu_custom_call" | custom-call | flops 1073741824 | bytes 3670016 | tf_op jit(solution)/shard_map/block_work/pallas_call | solution.py:146
  14.4 4.0 %collective-permute-done.2.refs_0_.refs_2_ = bf16[136,1024]{1,0:T(8,128)(2,1)S(1)} collective-permute-done((bf16[136,1024]{1,0:T(8,128)(2,1)S(1)}, bf16[136,1024]{1,0:T(8,128)(2,1)S(1)}, u32[]{:S(2)}, u32[]{:S(2)}) %collective-permute-start.2) | collective-permute-done | bytes 278560 | tf_op jit(solution)/shard_map/ppermute | solution.py:226
  18.4 1.5 %collective-permute-start.6 = (bf16[136,1024]{1,0:T(8,128)(2,1)S(1)}, bf16[136,1024]{1,0:T(8,128)(2,1)S(1)}, u32[]{:S(2)}, u32[]{:S(2)}) collective-permute-start(bf16[136,1024]{1,0:T(8,128)(2,1)S(1)} %collective-permute-done.2.refs_0_.refs_2_), channel_id=1, source_target_pairs={{0,2},{2,4},{4,6},{6,7},{7,5},{5,3},{3,1},{1,0},{8,10},{10,12},{12... | collective-permute-start | bytes 835592 | tf_op jit(solution)/shard_map/ppermute | solution.py:226
  19.9 0.6 collective-permute-start.7
  20.5 2.4 %block_work.5 = (bf16[128,1024]{1,0:T(8,128)(2,1)S(1)}, bf16[128,1024]{1,0:T(8,128)(2,1)S(1)}, bf16[128,1024]{1,0:T(8,128)(2,1)S(1)}, bf16[128,1024]{1,0:T(8,128...) custom-call(bf16[136,1024]{1,0:T(8,128)(2,1)S(1)} %collective-permute-done.2.refs_0_.refs_2_, ...), custom_call_target="tpu_custom_call" | custom-call | flops 1610612736 | bytes 4456448 | tf_op jit(solution)/shard_map/block_work/pallas_call | solution.py:146
  22.9 2.4 %collective-permute-done.6.refs_0_.refs_5_ = bf16[136,1024]{1,0:T(8,128)(2,1)S(1)} collective-permute-done((bf16[136,1024]{1,0:T(8,128)(2,1)S(1)}, bf16[136,1024]{1,0:T(8,128)(2,1)S(1)}, u32[]{:S(2)}, u32[]{:S(2)}) %collective-permute-start.6) | collective-permute-done | bytes 278560 | tf_op jit(solution)/shard_map/ppermute | solution.py:226
  25.3 1.6 %collective-permute-start.8 = (bf16[72,1024]{1,0:T(8,128)(2,1)S(1)}, bf16[72,1024]{1,0:T(8,128)(2,1)S(1)}, u32[]{:S(2)}, u32[]{:S(2)}) collective-permute-start(bf16[72,1024]{1,0:T(8,128)(2,1)S(1)} %pad_maximum_fusion.3), channel_id=1, source_target_pairs={{0,2},{2,4},{4,6},{6,7},{7,5},{5,3},{3,1},{1,0},{8,10},{10,12},{12... | collective-permute-start | bytes 442376 | tf_op jit(solution)/shard_map/ppermute | solution.py:226
  27.5 1.7 %block_work.6 = (bf16[128,1024]{1,0:T(8,128)(2,1)S(1)}, bf16[128,1024]{1,0:T(8,128)(2,1)S(1)}, bf16[128,1024]{1,0:T(8,128)(2,1)S(1)}, bf16[128,1024]{1,0:T(8,128)(2,1)S(1)}) custom-call(bf16[136,1024]{1,0:T(8,128)(2,1)S(1)} %collective-permute-done.6.refs_0_.refs_5_, bf16[136,1024]{1,0:T(8,128)(2,1)S(1)} %collective-permute-done.7.refs_1_.refs_6_, ...), custom_call_target="tpu_custom_call" | custom-call | flops 1073741824 | bytes 3670016 | tf_op jit(solution)/shard_map/block_work/pallas_call | solution.py:146
  29.2 1.3 %collective-permute-done.8.refs_0_.refs_7_ = bf16[72,1024]{1,0:T(8,128)(2,1)S(1)} collective-permute-done((bf16[72,1024]{1,0:T(8,128)(2,1)S(1)}, bf16[72,1024]{1,0:T(8,128)(2,1)S(1)}, u32[]{:S(2)}, u32[]{:S(2)}) %collective-permute-start.8) | collective-permute-done | bytes 147488 | tf_op jit(solution)/shard_map/ppermute | solution.py:226
  30.5 1.5 %collective-permute-done.9.refs_1_.refs_8_ = bf16[64,1024]{1,0:T(8,128)(2,1)S(1)} collective-permute-done((bf16[64,1024]{1,0:T(8,128)(2,1)S(1)}, bf16[64,1024]{1,0:T(8,128)(2,1)S(1)}, u32[]{:S(2)}, u32[]{:S(2)}) %collective-permute-start.9) | collective-permute-done | bytes 131104 | tf_op jit(solution)/shard_map/ppermute | solution.py:229
  32.0 1.2 %block_work.7 = (bf16[64,1024]{1,0:T(8,128)(2,1)S(1)}, bf16[64,1024]{1,0:T(8,128)(2,1)S(1)}, bf16[128,1024]{1,0:T(8,128)(2,1)S(1)}) custom-call(bf16[72,1024]{1,0:T(8,128)(2,1)S(1)} %collective-permute-done.8.refs_0_.refs_7_, bf16[64,1024]{1,0:T(8,128)(2,1)S(1)} %collective-permute-done.9.refs_1_.refs_8_, bf16[1024,1024]{1,0:T(8,128)(2,1)S(1)} %copy-done.1, ...), custom_call_target="tpu_custom_call" | custom-call | flops 536870912 | bytes 2883584 | tf_op jit(solution)/shard_map/block_work/pallas_call | solution.py:146
  33.2 1.6 %collective-permute-start.17 = (bf16[64,1024]{1,0:T(8,128)(2,1)S(1)}, bf16[64,1024]{1,0:T(8,128)(2,1)S(1)}, u32[]{:S(2)}, u32[]{:S(2)}) collective-permute-start(bf16[64,1024]{1,0:T(8,128)(2,1)S(1)} %get-tuple-element.59), channel_id=1, source_target_pairs={{0,2},{2,4},{4,6},{6,7},{7,5},{5,3},{3,1},{1,0},{8,10},{10,12},{12... | collective-permute-start | bytes 393224 | tf_op jit(solution)/shard_map/ppermute | solution.py:226
  35.3 1.3 %weight_work.3 = (bf16[1024,256]{1,0:T(8,128)(2,1)S(1)}, bf16[1024,256]{1,0:T(8,128)(2,1)S(1)}) custom-call(bf16[136,1024]{1,0:T(8,128)(2,1)S(1)} %constant_dynamic-update-slice_fusion.refs_0_, bf16[136,1024]{1,0:T(8,128)(2,1)S(1)} %constant_dynamic-update-slice_fusion.2.refs_1_, bf16[136,1024]{1,0:T(8,128)(2,1)S(1)} %collective-permute-done.2.refs_0_.refs_2_, ...), custom_call_target="tpu_custom_call" | custom-call | flops 1073741824 | bytes 4718592 | tf_op jit(solution)/shard_map/weight_work/pallas_call | solution.py:188
  36.6 1.3 %weight_work.2 = (bf16[1024,256]{1,0:T(8,128)(2,1)S(1)}, bf16[1024,256]{1,0:T(8,128)(2,1)S(1)}) custom-call(bf16[136,1024]{1,0:T(8,128)(2,1)S(1)} %constant_dynamic-update-slice_fusion.refs_0_, bf16[136,1024]{1,0:T(8,128)(2,1)S(1)} %constant_dynamic-update-slice_fusion.2.refs_1_, bf16[136,1024]{1,0:T(8,128)(2,1)S(1)} %collective-permute-done.2.refs_0_.refs_2_, ...), custom_call_target="tpu_custom_call" | custom-call | flops 1073741824 | bytes 4718592 | tf_op jit(solution)/shard_map/weight_work/pallas_call | solution.py:188
  38.6 1.6 %collective-permute-start.18 = (bf16[128,1024]{1,0:T(8,128)(2,1)S(1)}, bf16[128,1024]{1,0:T(8,128)(2,1)S(1)}, u32[]{:S(2)}, u32[]{:S(2)}) collective-permute-start(bf16[128,1024]{1,0:T(8,128)(2,1)S(1)} %pad_maximum_fusion.2), channel_id=1, source_target_pairs={{0,2},{2,4},{4,6},{6,7},{7,5},{5,3},{3,1},{1,0},{8,10},{10,12},{12... | collective-permute-start | bytes 786440 | tf_op jit(solution)/shard_map/ppermute | solution.py:226
  40.8 6.1 %collective-permute-done.18 = bf16[128,1024]{1,0:T(8,128)(2,1)S(1)} collective-permute-done((bf16[128,1024]{1,0:T(8,128)(2,1)S(1)}, bf16[128,1024]{1,0:T(8,128)(2,1)S(1)}, u32[]{:S(2)}, u32[]{:S(2)}) %collective-permute-start.18) | collective-permute-done | bytes 262176 | tf_op jit(solution)/shard_map/ppermute | solution.py:226
  46.9 1.6 %collective-permute-start.19 = (bf16[128,1024]{1,0:T(8,128)(2,1)S(1)}, bf16[128,1024]{1,0:T(8,128)(2,1)S(1)}, u32[]{:S(2)}, u32[]{:S(2)}) collective-permute-start(bf16[128,1024]{1,0:T(8,128)(2,1)S(1)} %add_convert_fusion.4), channel_id=1, source_target_pairs={{0,2},{2,4},{4,6},{6,7},{7,5},{5,3},{3,1},{1,0},{8,10},{10,12},{12... | collective-permute-start | bytes 786440 | tf_op jit(solution)/shard_map/ppermute | solution.py:226
  48.7 1.5 %collective-permute-start.12 = (bf16[1024,256]{1,0:T(8,128)(2,1)S(1)}, bf16[1024,256]{1,0:T(8,128)(2,1)S(1)}, u32[]{:S(2)}, u32[]{:S(2)}) collective-permute-start(bf16[1024,256]{1,0:T(8,128)(2,1)S(1)} %add_convert_fusion.1), channel_id=1, source_target_pairs={{0,16},{8,24},{16,0},{24,8},{1,17},{9,25},{17,1},{25,9},{2,18},{10... | collective-permute-start | bytes 1572872 | tf_op jit(solution)/shard_map/ppermute | solution.py:266
  50.8 3.5 %collective-permute-done.19 = bf16[128,1024]{1,0:T(8,128)(2,1)S(1)} collective-permute-done((bf16[128,1024]{1,0:T(8,128)(2,1)S(1)}, bf16[128,1024]{1,0:T(8,128)(2,1)S(1)}, u32[]{:S(2)}, u32[]{:S(2)}) %collective-permute-start.19) | collective-permute-done | bytes 262176 | tf_op jit(solution)/shard_map/ppermute | solution.py:226
  54.4 1.6 %collective-permute-start.20 = (bf16[128,1024]{1,0:T(8,128)(2,1)S(1)}, bf16[128,1024]{1,0:T(8,128)(2,1)S(1)}, u32[]{:S(2)}, u32[]{:S(2)}) collective-permute-start(bf16[128,1024]{1,0:T(8,128)(2,1)S(1)} %add_convert_fusion.3), channel_id=1, source_target_pairs={{0,2},{2,4},{4,6},{6,7},{7,5},{5,3},{3,1},{1,0},{8,10},{10,12},{12... | collective-permute-start | bytes 786440 | tf_op jit(solution)/shard_map/ppermute | solution.py:226
  56.1 1.1 %collective-permute-done.15 = bf16[128,1024]{1,0:T(8,128)(2,1)S(1)} collective-permute-done((bf16[128,1024]{1,0:T(8,128)(2,1)S(1)}, bf16[128,1024]{1,0:T(8,128)(2,1)S(1)}, u32[]{:S(2)}, u32[]{:S(2)}) %collective-permute-start.15) | collective-permute-done | bytes 262176 | tf_op jit(solution)/shard_map/ppermute | solution.py:229
  57.8 3.7 %collective-permute-done.12 = bf16[1024,256]{1,0:T(8,128)(2,1)S(1)} collective-permute-done((bf16[1024,256]{1,0:T(8,128)(2,1)S(1)}, bf16[1024,256]{1,0:T(8,128)(2,1)S(1)}, u32[]{:S(2)}, u32[]{:S(2)}) %collective-permute-start.12) | collective-permute-done | bytes 524320 | tf_op jit(solution)/shard_map/ppermute | solution.py:266
  61.5 1.0 %add_convert_fusion = bf16[1024,256]{1,0:T(8,128)(2,1)} fusion(bf16[1024,256]{1,0:T(8,128)(2,1)S(1)} %collective-permute-done.12, bf16[1024,256]{1,0:T(8,128)(2,1)S(1)} %collective-permute-done.10, bf16[1024,256]{1,0:T(8,128)(2,1)S(1)} %get-tuple-element.50), kind=kLoop, calls=%fused_computation | loop fusion | flops 1572864 | bytes 2097152 | tf_op jit(solution)/shard_map/convert_element_type | solution.py:206
  62.5 1.2 %collective-permute-done.16 = bf16[128,1024]{1,0:T(8,128)(2,1)S(1)} collective-permute-done((bf16[128,1024]{1,0:T(8,128)(2,1)S(1)}, bf16[128,1024]{1,0:T(8,128)(2,1)S(1)}, u32[]{:S(2)}, u32[]{:S(2)}) %collective-permute-start.16) | collective-permute-done | bytes 262176 | tf_op jit(solution)/shard_map/ppermute | solution.py:229
  63.7 0.8 %add_convert_fusion.2 = bf16[128,1024]{1,0:T(8,128)(2,1)} fusion(bf16[128,1024]{1,0:T(8,128)(2,1)S(1)} %collective-permute-done.20, bf16[128,1024]{1,0:T(8,128)(2,1)S(1)} %collective-permute-done.16, bf16[128,1024]{1,0:T(8,128)(2,1)S(1)} %get-tuple-element.54), kind=kLoop, calls=%fused_computation.2 | loop fusion | flops 786432 | bytes 1048576 | tf_op jit(solution)/shard_map/convert_element_type | solution.py:206
  (52 shorter events, 5.1 us)
Async XLA Ops:
  0.6 9.7 %collective-permute-start = (bf16[128,1024]{1,0:T(8,128)(2,1)}, bf16[128,1024]{1,0:T(8,128)(2,1)S(1)}, u32[]{:S(2)}, u32[]{:S(2)}) collective-permute-start(bf16[128,1024]{1,0:T(8,128)(2,1)} %param.5), channel_id=1, source_target_pairs={{0,2},{2,4},{4,6},{6,7},{7,5},{5,3},{3,1},{1,0},{8,10},{10,12},{12... | collective-permute-start | bytes 786440 | tf_op jit(solution)/shard_map/ppermute | solution.py:226
  3.7 8.6 %collective-permute-start.3 = (bf16[128,1024]{1,0:T(8,128)(2,1)}, bf16[128,1024]{1,0:T(8,128)(2,1)S(1)}, u32[]{:S(2)}, u32[]{:S(2)}) collective-permute-start(bf16[128,1024]{1,0:T(8,128)(2,1)} %param.5), channel_id=1, source_target_pairs={{2,0},{4,2},{6,4},{7,6},{5,7},{3,5},{1,3},{0,1},{10,8},{12,10},{14... | collective-permute-start | bytes 786440 | tf_op jit(solution)/shard_map/ppermute | solution.py:229
  3.7 0.7 %copy-start.2 = (s32[128,16]{0,1:T(8,128)S(1)}, s32[128,16]{0,1:T(8,128)}, u32[]{:S(2)}) copy-start(s32[128,16]{0,1:T(8,128)} %param.6) | copy-start | bytes 24580
  4.4 0.7 %copy-start.3 = (s32[128,4]{0,1:T(4,128)S(1)}, s32[128,4]{0,1:T(4,128)}, u32[]{:S(2)}) copy-start(s32[128,4]{0,1:T(4,128)} %param.7) | copy-start | bytes 6148
  5.1 5.4 %collective-permute-start.1 = (bf16[8,1024]{1,0:T(8,128)(2,1)S(1)}, bf16[8,1024]{1,0:T(8,128)(2,1)S(1)}, u32[]{:S(2)}, u32[]{:S(2)}) collective-permute-start(bf16[8,1024]{1,0:T(8,128)(2,1)S(1)} %instance_ids.1), channel_id=1, source_target_pairs={{0,2},{2,4},{4,6},{6,7},{7,5},{5,3},{3,1},{1,0},{8,10},{10,12},{12... | collective-permute-start | bytes 49160 | tf_op jit(solution)/shard_map/ppermute | solution.py:226
  7.2 5.2 %collective-permute-start.4 = (bf16[8,1024]{1,0:T(8,128)(2,1)S(1)}, bf16[8,1024]{1,0:T(8,128)(2,1)S(1)}, u32[]{:S(2)}, u32[]{:S(2)}) collective-permute-start(bf16[8,1024]{1,0:T(8,128)(2,1)S(1)} %instance_ids.1), channel_id=1, source_target_pairs={{2,0},{4,2},{6,4},{7,6},{5,7},{3,5},{1,3},{0,1},{10,8},{12,10},{14... | collective-permute-start | bytes 49160 | tf_op jit(solution)/shard_map/ppermute | solution.py:229
  7.2 1.6 %copy-start = (bf16[1024,1024]{1,0:T(8,128)(2,1)S(1)}, bf16[1024,1024]{1,0:T(8,128)(2,1)}, u32[]{:S(2)}) copy-start(bf16[1024,1024]{1,0:T(8,128)(2,1)} %refs_2_.5) | copy-start | bytes 6291460
  8.8 0.7 %copy-start.4 = (s32[8]{0:T(128)S(1)}, s32[8]{0:T(128)}, u32[]{:S(2)}) copy-start(s32[8]{0:T(128)} %size_ref.1) | copy-start | bytes 100
  9.4 3.2 %copy-start.1 = (bf16[1024,1024]{1,0:T(8,128)(2,1)S(1)}, bf16[1024,1024]{1,0:T(8,128)(2,1)}, u32[]{:S(2)}) copy-start(bf16[1024,1024]{1,0:T(8,128)(2,1)} %refs_2_.5) | copy-start | bytes 6291460
  10.5 7.8 %collective-permute-start.2 = (bf16[136,1024]{1,0:T(8,128)(2,1)S(1)}, bf16[136,1024]{1,0:T(8,128)(2,1)S(1)}, u32[]{:S(2)}, u32[]{:S(2)}) collective-permute-start(bf16[136,1024]{1,0:T(8,128)(2,1)S(1)} %constant_dynamic-update-slice_fusion.refs_0_), channel_id=1, source_target_pairs={{0,2},{2,4},{4,6},{6,7},{7,5},{5,3},{3,1},{1,0},{8,10},{10,12},{12... | collective-permute-start | bytes 835592 | tf_op jit(solution)/shard_map/ppermute | solution.py:226
  12.3 7.5 %copy-start.5 = (bf16[128,1024]{1,0:T(8,128)(2,1)S(1)}, bf16[128,1024]{1,0:T(8,128)(2,1)}, u32[]{:S(2)}) copy-start(bf16[128,1024]{1,0:T(8,128)(2,1)} %param.5) | copy-start | bytes 786436
  12.4 7.5 %collective-permute-start.5 = (bf16[136,1024]{1,0:T(8,128)(2,1)S(1)}, bf16[136,1024]{1,0:T(8,128)(2,1)S(1)}, u32[]{:S(2)}, u32[]{:S(2)}) collective-permute-start(bf16[136,1024]{1,0:T(8,128)(2,1)S(1)} %constant_dynamic-update-slice_fusion.2.refs_1_), channel_id=1, source_target_pairs={{2,0},{4,2},{6,4},{7,6},{5,7},{3,5},{1,3},{0,1},{10,8},{12,10},{14... | collective-permute-start | bytes 835592 | tf_op jit(solution)/shard_map/ppermute | solution.py:229
  18.4 6.9 %collective-permute-start.6 = (bf16[136,1024]{1,0:T(8,128)(2,1)S(1)}, bf16[136,1024]{1,0:T(8,128)(2,1)S(1)}, u32[]{:S(2)}, u32[]{:S(2)}) collective-permute-start(bf16[136,1024]{1,0:T(8,128)(2,1)S(1)} %collective-permute-done.2.refs_0_.refs_2_), channel_id=1, source_target_pairs={{0,2},{2,4},{4,6},{6,7},{7,5},{5,3},{3,1},{1,0},{8,10},{10,12},{12... | collective-permute-start | bytes 835592 | tf_op jit(solution)/shard_map/ppermute | solution.py:226
  19.9 7.1 %collective-permute-start.7 = (bf16[136,1024]{1,0:T(8,128)(2,1)S(1)}, bf16[136,1024]{1,0:T(8,128)(2,1)S(1)}, u32[]{:S(2)}, u32[]{:S(2)}) collective-permute-start(bf16[136,1024]{1,0:T(8,128)(2,1)S(1)} %collective-permute-done.5.refs_1_.refs_3_), channel_id=1, source_target_pairs={{2,0},{4,2},{6,4},{7,6},{5,7},{3,5},{1,3},{0,1},{10,8},{12,10},{14... | collective-permute-start | bytes 835592 | tf_op jit(solution)/shard_map/ppermute | solution.py:229
  25.3 5.2 %collective-permute-start.8 = (bf16[72,1024]{1,0:T(8,128)(2,1)S(1)}, bf16[72,1024]{1,0:T(8,128)(2,1)S(1)}, u32[]{:S(2)}, u32[]{:S(2)}) collective-permute-start(bf16[72,1024]{1,0:T(8,128)(2,1)S(1)} %pad_maximum_fusion.3), channel_id=1, source_target_pairs={{0,2},{2,4},{4,6},{6,7},{7,5},{5,3},{3,1},{1,0},{8,10},{10,12},{12... | collective-permute-start | bytes 442376 | tf_op jit(solution)/shard_map/ppermute | solution.py:226
  27.0 5.0 %collective-permute-start.9 = (bf16[64,1024]{1,0:T(8,128)(2,1)S(1)}, bf16[64,1024]{1,0:T(8,128)(2,1)S(1)}, u32[]{:S(2)}, u32[]{:S(2)}) collective-permute-start(bf16[64,1024]{1,0:T(8,128)(2,1)S(1)} %slice.23), channel_id=1, source_target_pairs={{2,0},{4,2},{6,4},{7,6},{5,7},{3,5},{1,3},{0,1},{10,8},{12,10},{14... | collective-permute-start | bytes 393224 | tf_op jit(solution)/shard_map/ppermute | solution.py:229
  33.2 5.3 %collective-permute-start.17 = (bf16[64,1024]{1,0:T(8,128)(2,1)S(1)}, bf16[64,1024]{1,0:T(8,128)(2,1)S(1)}, u32[]{:S(2)}, u32[]{:S(2)}) collective-permute-start(bf16[64,1024]{1,0:T(8,128)(2,1)S(1)} %get-tuple-element.59), channel_id=1, source_target_pairs={{0,2},{2,4},{4,6},{6,7},{7,5},{5,3},{3,1},{1,0},{8,10},{10,12},{12... | collective-permute-start | bytes 393224 | tf_op jit(solution)/shard_map/ppermute | solution.py:226
  34.8 5.4 %collective-permute-start.13 = (bf16[64,1024]{1,0:T(8,128)(2,1)S(1)}, bf16[64,1024]{1,0:T(8,128)(2,1)S(1)}, u32[]{:S(2)}, u32[]{:S(2)}) collective-permute-start(bf16[64,1024]{1,0:T(8,128)(2,1)S(1)} %get-tuple-element.55), channel_id=1, source_target_pairs={{2,0},{4,2},{6,4},{7,6},{5,7},{3,5},{1,3},{0,1},{10,8},{12,10},{14... | collective-permute-start | bytes 393224 | tf_op jit(solution)/shard_map/ppermute | solution.py:229
  36.6 12.0 %collective-permute-start.11 = (bf16[1024,256]{1,0:T(8,128)(2,1)S(1)}, bf16[1024,256]{1,0:T(8,128)(2,1)S(1)}, u32[]{:S(2)}, u32[]{:S(2)}) collective-permute-start(bf16[1024,256]{1,0:T(8,128)(2,1)S(1)} %get-tuple-element.53), channel_id=1, source_target_pairs={{0,8},{8,0},{16,24},{24,16},{1,9},{9,1},{17,25},{25,17},{2,10},{10... | collective-permute-start | bytes 1572872 | tf_op jit(solution)/shard_map/ppermute | solution.py:266
  37.9 19.8 %collective-permute-start.10 = (bf16[1024,256]{1,0:T(8,128)(2,1)S(1)}, bf16[1024,256]{1,0:T(8,128)(2,1)S(1)}, u32[]{:S(2)}, u32[]{:S(2)}) collective-permute-start(bf16[1024,256]{1,0:T(8,128)(2,1)S(1)} %get-tuple-element.51), channel_id=1, source_target_pairs={{0,8},{8,0},{16,24},{24,16},{1,9},{9,1},{17,25},{25,17},{2,10},{10... | collective-permute-start | bytes 1572872 | tf_op jit(solution)/shard_map/ppermute | solution.py:266
  38.6 8.3 %collective-permute-start.18 = (bf16[128,1024]{1,0:T(8,128)(2,1)S(1)}, bf16[128,1024]{1,0:T(8,128)(2,1)S(1)}, u32[]{:S(2)}, u32[]{:S(2)}) collective-permute-start(bf16[128,1024]{1,0:T(8,128)(2,1)S(1)} %pad_maximum_fusion.2), channel_id=1, source_target_pairs={{0,2},{2,4},{4,6},{6,7},{7,5},{5,3},{3,1},{1,0},{8,10},{10,12},{12... | collective-permute-start | bytes 786440 | tf_op jit(solution)/shard_map/ppermute | solution.py:226
  40.3 10.0 %collective-permute-start.14 = (bf16[128,1024]{1,0:T(8,128)(2,1)S(1)}, bf16[128,1024]{1,0:T(8,128)(2,1)S(1)}, u32[]{:S(2)}, u32[]{:S(2)}) collective-permute-start(bf16[128,1024]{1,0:T(8,128)(2,1)S(1)} %pad_maximum_fusion.1), channel_id=1, source_target_pairs={{2,0},{4,2},{6,4},{7,6},{5,7},{3,5},{1,3},{0,1},{10,8},{12,10},{14... | collective-permute-start | bytes 786440 | tf_op jit(solution)/shard_map/ppermute | solution.py:229
  46.9 7.4 %collective-permute-start.19 = (bf16[128,1024]{1,0:T(8,128)(2,1)S(1)}, bf16[128,1024]{1,0:T(8,128)(2,1)S(1)}, u32[]{:S(2)}, u32[]{:S(2)}) collective-permute-start(bf16[128,1024]{1,0:T(8,128)(2,1)S(1)} %add_convert_fusion.4), channel_id=1, source_target_pairs={{0,2},{2,4},{4,6},{6,7},{7,5},{5,3},{3,1},{1,0},{8,10},{10,12},{12... | collective-permute-start | bytes 786440 | tf_op jit(solution)/shard_map/ppermute | solution.py:226
  48.7 12.8 %collective-permute-start.12 = (bf16[1024,256]{1,0:T(8,128)(2,1)S(1)}, bf16[1024,256]{1,0:T(8,128)(2,1)S(1)}, u32[]{:S(2)}, u32[]{:S(2)}) collective-permute-start(bf16[1024,256]{1,0:T(8,128)(2,1)S(1)} %add_convert_fusion.1), channel_id=1, source_target_pairs={{0,16},{8,24},{16,0},{24,8},{1,17},{9,25},{17,1},{25,9},{2,18},{10... | collective-permute-start | bytes 1572872 | tf_op jit(solution)/shard_map/ppermute | solution.py:266
  50.3 6.9 %collective-permute-start.15 = (bf16[128,1024]{1,0:T(8,128)(2,1)S(1)}, bf16[128,1024]{1,0:T(8,128)(2,1)S(1)}, u32[]{:S(2)}, u32[]{:S(2)}) collective-permute-start(bf16[128,1024]{1,0:T(8,128)(2,1)S(1)} %add_convert_fusion.6), channel_id=1, source_target_pairs={{2,0},{4,2},{6,4},{7,6},{5,7},{3,5},{1,3},{0,1},{10,8},{12,10},{14... | collective-permute-start | bytes 786440 | tf_op jit(solution)/shard_map/ppermute | solution.py:229
  54.4 8.0 %collective-permute-start.20 = (bf16[128,1024]{1,0:T(8,128)(2,1)S(1)}, bf16[128,1024]{1,0:T(8,128)(2,1)S(1)}, u32[]{:S(2)}, u32[]{:S(2)}) collective-permute-start(bf16[128,1024]{1,0:T(8,128)(2,1)S(1)} %add_convert_fusion.3), channel_id=1, source_target_pairs={{0,2},{2,4},{4,6},{6,7},{7,5},{5,3},{3,1},{1,0},{8,10},{10,12},{12... | collective-permute-start | bytes 786440 | tf_op jit(solution)/shard_map/ppermute | solution.py:226
  57.3 6.4 %collective-permute-start.16 = (bf16[128,1024]{1,0:T(8,128)(2,1)S(1)}, bf16[128,1024]{1,0:T(8,128)(2,1)S(1)}, u32[]{:S(2)}, u32[]{:S(2)}) collective-permute-start(bf16[128,1024]{1,0:T(8,128)(2,1)S(1)} %add_convert_fusion.5), channel_id=1, source_target_pairs={{2,0},{4,2},{6,4},{7,6},{5,7},{3,5},{1,3},{0,1},{10,8},{12,10},{14... | collective-permute-start | bytes 786440 | tf_op jit(solution)/shard_map/ppermute | solution.py:229

commit v10 on v9

--- a/solution.py
+++ b/solution.py
@@ -68,8 +68,8 @@
     piece_count = sum(len(pieces) for pieces in piece_rows)
     x_refs = refs[:piece_count]
     w_ref, live_ref = refs[piece_count : piece_count + 2]
-    grad_refs = refs[piece_count + 2 : 2 * piece_count + 2]
-    slope_refs = refs[2 * piece_count + 2 :]
+    grad_refs = refs[piece_count + 2 : piece_count + 2 + 2 * block_count]
+    slope_refs = refs[piece_count + 2 + 2 * block_count :]
     labels, width = w_ref.shape
     local_count = labels // BLOCK
     rows = slope_refs[0].shape[0]
@@ -143,9 +143,10 @@
         for pieces in blocks
     ]
     flat_rows = sum(piece_rows, [])
+    half = sum(piece_rows[0]) // 2
     out = pl.pallas_call(
         functools.partial(block_kernel, piece_rows, top_count, pos_count),
-        out_shape=[jax.ShapeDtypeStruct((rows, width), jnp.bfloat16) for rows in flat_rows]
+        out_shape=[jax.ShapeDtypeStruct((half, width), jnp.bfloat16)] * (2 * len(blocks))
         + [jax.ShapeDtypeStruct((sum(rows), labels), jnp.bfloat16) for rows in piece_rows],
         in_specs=[pl.BlockSpec(memory_space=pltpu.VMEM)] * (len(flat_rows) + 2),
         compiler_params=pltpu.CompilerParams(vmem_limit_bytes=VMEM_LIMIT),
@@ -156,7 +157,8 @@
         ),
         name="block_work",
     )(*[piece for pieces in blocks for piece in pieces], weights, live_table)
-    return list(out[: len(flat_rows)]), list(out[len(flat_rows) :])
+    grads = [(out[2 * b], out[2 * b + 1]) for b in range(len(blocks))]
+    return grads, list(out[2 * len(blocks) :])
 
 
 def weight_kernel(piece_rows, column_blocks, scale, *refs):
@@ -206,6 +208,26 @@
     return total.astype(jnp.bfloat16)
 
 
+def sum_kernel(*refs):
+    total = refs[0][...].astype(jnp.float32)
+    for ref in refs[1:-1]:
+        total = total + ref[...].astype(jnp.float32)
+    refs[-1][...] = total.astype(jnp.bfloat16)
+
+
+def weight_sum(parts):
+    return pl.pallas_call(
+        sum_kernel,
+        out_shape=jax.ShapeDtypeStruct(parts[0].shape, jnp.bfloat16),
+        in_specs=[pl.BlockSpec(memory_space=pltpu.VMEM)] * len(parts),
+        compiler_params=pltpu.CompilerParams(vmem_limit_bytes=VMEM_LIMIT),
+        cost_estimate=pl.CostEstimate(
+            flops=8_000_000_000, bytes_accessed=2 * parts[0].size * (len(parts) + 1), transcendentals=0
+        ),
+        name="weight_sum",
+    )(*parts)
+
+
 def after(array, *others):
     return lax.optimization_barrier((array, *others))[0]
 
@@ -246,7 +268,7 @@
     below_grad, above_grad = {}, {}
     for k in range(2, steps + 1):
         if k > 2:
-            before = below_grad[k - 2]
+            before = below_grad[k - 2][0]
             below, above = after(below, before), after(above, before)
         if k < steps:
             arriving = send_up(below), send_down(above)
@@ -258,34 +280,61 @@
         else:
             below_grad[k - 1], above_grad[k - 1] = take([below], [above])
         below, above = arriving
-    to_down, to_up = take([after(below, below_grad[steps - 1]), above])
+    last = steps - 1
+    early_above, early_below = send_down(below_grad[last][1]), send_up(above_grad[last][0])
+    (opposite,) = take([after(below, below_grad[last][0]), above])
+    from_above, from_below = send_down(opposite[0]), send_up(opposite[1])
+    slopes[-1] = after(slopes[-1], *opposite)
+    early_above, early_below = after(early_above, opposite[0]), after(early_below, opposite[0])
 
     scale = 1.0 / math.sqrt(inst_rows * seq_count * top_count // local_count)
 
-    def seq_send(array, bit):
-        return lax.ppermute(array, "seq", [(k, k ^ bit) for k in range(seq_count)])
-
     far, near = list(range(seq_count // 2, seq_count)), list(range(seq_count // 2))
-    terms = dict(zip(far, weight_work(used, slopes, far, part_width, scale)))
-    terms.update(zip(near, weight_work(used, slopes, near, part_width, scale)))
-    terms = {q: [term] for q, term in terms.items()}
-    bit = 1
-    while bit < seq_count:
-        for q in [q for q in sorted(terms, reverse=True) if q & bit]:
-            values = terms.pop(q)
-            terms[q ^ bit].append(seq_send(add(*values) if len(values) > 1 else values[0], bit))
-        bit *= 2
-
-    for k in range(steps, 0, -1):
-        from_above, from_below = send_down(to_down), send_up(to_up)
-        if k == steps:
-            near_below, near_above = below_grad[k - 1], above_grad[k - 1]
-            to_down = jnp.concatenate([add(near_below[:half], from_above), near_below[half:]], axis=0)
-            to_up = jnp.concatenate([near_above[:half], add(near_above[half:], from_below)], axis=0)
-        elif k > 1:
-            to_down, to_up = add(below_grad[k - 1], from_above), add(above_grad[k - 1], from_below)
-    weight_grad = add(*terms[0])
-    feature_grad = add(after(own_grad, weight_grad), from_above, from_below)
+    terms, arrived = {}, {}
+
+    def weigh(slots):
+        parts = weight_work(used, slopes, slots, part_width, scale)
+        terms.update({q: [part] for q, part in zip(slots, parts)})
+        return parts[0]
+
+    def halve(bit, slots):
+        for q in slots:
+            values = terms.pop(q) + arrived.pop(q, [])
+            going = add(*values) if len(values) > 1 else values[0]
+            sent = lax.ppermute(going, "seq", [(k, k ^ bit) for k in range(seq_count)])
+            arrived.setdefault(q ^ bit, []).append(sent)
+        return going
+
+    weigh(far)
+    halve(1, far[1::2])
+    passed = weigh(near)
+    halve(1, near[1::2])
+    for level in range(last, 0, -1):
+        to_down = add(below_grad[level][0], from_above)
+        to_up = add(above_grad[level][1], from_below)
+        if level > 1:
+            to_down = jnp.concatenate([to_down, add(below_grad[level - 1][1], early_above)], axis=0)
+            to_up = jnp.concatenate([to_up, add(above_grad[level - 1][0], early_below)], axis=0)
+        if level == last:
+            bit = 2
+            while bit < seq_count:
+                going = halve(bit, [q for q in sorted(terms, reverse=True) if q & bit])
+                bit *= 2
+            to_down, to_up = after(to_down, passed), after(to_up, going)
+        if level == 1:
+            early_above, early_below = after(early_above, to_down, to_up), after(early_below, to_down, to_up)
+        got_above, got_below = send_down(to_down), send_up(to_up)
+        from_above, from_below = got_above[:half], got_below[:half]
+        if level > 1:
+            early_above, early_below = got_above[half:], got_below[half:]
+    weight_grad = weight_sum(terms[0] + arrived[0])
+    feature_grad = jnp.concatenate(
+        [
+            add(after(own_grad[0], weight_grad), from_above, early_below),
+            add(after(own_grad[1], weight_grad), early_above, from_below),
+        ],
+        axis=0,
+    )
     return (feature_grad, weight_grad)
 
 

time: 64.8 us -> 65.3 us (level)
  starting transfers between devices: 22.1 us -> 24.1 us
  waiting for transfers between devices: 25.4 us -> 23.9 us
  Pallas kernels: 10.2 us -> 11.2 us
  other arithmetic: 2.34 us -> 1.41 us
    ppermute x9 -> x10, waiting for transfers between devices: 17.8 us -> 6.68 us  [send_up(): return lax.ppermute(array, 'clus', up)]
    ppermute x9 -> x10, waiting for transfers between devices: 3.83 us -> 14.6 us  [send_down(): return lax.ppermute(array, 'clus', down)]
    convert_element_type x9 -> x11, other arithmetic: 2.27 us -> 0.58 us  [add(): return total.astype(jnp.bfloat16)]
    ppermute x9 -> x10, starting transfers between devices: 16.5 us -> 18.1 us  [send_up(): return lax.ppermute(array, 'clus', up)]
    ppermute x3, waiting for transfers between devices: 3.72 us -> 2.57 us  [halve(): sent = lax.ppermute(going, 'seq', [(k, k ^ bit) for k in range(seq_count)])]
    pallas_call x0 -> x1, Pallas kernels: none -> 0.98 us  [weight_sum(): pl.pallas_call(sum_kernel, out_shape=jax.ShapeDtypeStruct(parts[0].shape,...]
    concatenate x2 -> x5, other arithmetic: 0.04 us -> 0.8 us  [the longest x1 0.72 us: local(): jnp.concatenate([add(after(own_grad[0], weight_grad), from_above, early_b...]
    ppermute x9 -> x10, starting transfers between devices: 3.36 us -> 3.87 us  [send_down(): return lax.ppermute(array, 'clus', down)]
  transfers between devices with their start and end apart: 21 -> 23, of which waited for: 11 -> 10; matrix products, arithmetic and copies ran while one was open for 2% -> 1% of each run, Pallas kernels for 14% -> 17%
where the time goes in v10:
time: 65.3 us; the launch traced here: 65.1 us
  starting transfers between devices  24.1 us (37%)
  waiting for transfers between devices  23.9 us (37%)
  Pallas kernels  11.2 us (17%)
  local copies, waits for them, and re-layouts  3.71 us (6%)
  other arithmetic  1.41 us (2%)
  between operations  0.89 us (1%)
    ppermute x10, starting transfers between devices, send_up(): return lax.ppermute(array, 'clus', up)  18.1 us
    ppermute x10, waiting for transfers between devices, send_down(): return lax.ppermute(array, 'clus', down)  14.6 us
    pallas_call x4, Pallas kernels, block_work(): pl.pallas_call(functools.partial(block_kernel, piece_rows, top_count, pos...  6.98 us
    ppermute x10, waiting for transfers between devices, send_up(): return lax.ppermute(array, 'clus', up)  6.68 us
    ppermute x10, starting transfers between devices, send_down(): return lax.ppermute(array, 'clus', down)  3.87 us
    unnamed x14, local copies, waits for them, and re-layouts  3.67 us
    pallas_call x2, Pallas kernels, weight_work(): pl.pallas_call(functools.partial(weight_kernel, piece_rows, column_blocks...  2.58 us
    ppermute x3, waiting for transfers between devices, halve(): sent = lax.ppermute(going, 'seq', [(k, k ^ bit) for k in range(seq_count)])  2.57 us
  transfers between devices with their start and end apart: 23, of which 10 were waited for; matrix products, arithmetic and copies ran while one was open for 1% of the time, Pallas kernels for 17%

profile of v10, /device:TPU:0, one launch (start us, length us, event | category | flops | bytes accessed | tf_op | source)
XLA Modules:
  0.0 65.1 jit_solution(16778805243850548484)
XLA Ops:
  0.6 3.1 %collective-permute-start = (bf16[128,1024]{1,0:T(8,128)(2,1)}, bf16[128,1024]{1,0:T(8,128)(2,1)S(1)}, u32[]{:S(2)}, u32[]{:S(2)}) collective-permute-start(bf16[128,1024]{1,0:T(8,128)(2,1)} %param.5), channel_id=1, source_target_pairs={{0,2},{2,4},{4,6},{6,7},{7,5},{5,3},{3,1},{1,0},{8,10},{10,12},{12... | collective-permute-start | bytes 786440 | tf_op jit(solution)/shard_map/ppermute | solution.py:248
  3.7 0.7 %copy-done.2 = s32[128,16]{0,1:T(8,128)S(1)} copy-done((s32[128,16]{0,1:T(8,128)S(1)}, s32[128,16]{0,1:T(8,128)}, u32[]{:S(2)}) %copy-start.2) | copy-done | bytes 8216
  4.4 0.7 %copy-done.3 = s32[128,4]{0,1:T(4,128)S(1)} copy-done((s32[128,4]{0,1:T(4,128)S(1)}, s32[128,4]{0,1:T(4,128)}, u32[]{:S(2)}) %copy-start.3) | copy-done | bytes 2072
  5.1 2.1 %collective-permute-start.1 = (bf16[8,1024]{1,0:T(8,128)(2,1)S(1)}, bf16[8,1024]{1,0:T(8,128)(2,1)S(1)}, u32[]{:S(2)}, u32[]{:S(2)}) collective-permute-start(bf16[8,1024]{1,0:T(8,128)(2,1)S(1)} %instance_ids.1), channel_id=1, source_target_pairs={{0,2},{2,4},{4,6},{6,7},{7,5},{5,3},{3,1},{1,0},{8,10},{10,12},{12... | collective-permute-start | bytes 49160 | tf_op jit(solution)/shard_map/ppermute | solution.py:248
  7.2 1.6 %copy-done = bf16[1024,1024]{1,0:T(8,128)(2,1)S(1)} copy-done((bf16[1024,1024]{1,0:T(8,128)(2,1)S(1)}, bf16[1024,1024]{1,0:T(8,128)(2,1)}, u32[]{:S(2)}) %copy-start) | copy-done | bytes 2097176
  8.8 0.7 %copy-done.4 = s32[8]{0:T(128)S(1)} copy-done((s32[8]{0:T(128)S(1)}, s32[8]{0:T(128)}, u32[]{:S(2)}) %copy-start.4) | copy-done | bytes 56
  10.4 1.5 %collective-permute-done.3 = bf16[128,1024]{1,0:T(8,128)(2,1)S(1)} collective-permute-done((bf16[128,1024]{1,0:T(8,128)(2,1)}, bf16[128,1024]{1,0:T(8,128)(2,1)S(1)}, u32[]{:S(2)}, u32[]{:S(2)}) %collective-permute-start.3) | collective-permute-done | bytes 262176 | tf_op jit(solution)/shard_map/ppermute | solution.py:251
  11.9 1.6 %collective-permute-start.2 = (bf16[136,1024]{1,0:T(8,128)(2,1)S(1)}, bf16[136,1024]{1,0:T(8,128)(2,1)S(1)}, u32[]{:S(2)}, u32[]{:S(2)}) collective-permute-start(bf16[136,1024]{1,0:T(8,128)(2,1)S(1)} %constant_dynamic-update-slice_fusion.refs_0_), channel_id=1, source_target_pairs={{0,2},{2,4},{4,6},{6,7},{7,5},{5,3},{3,1},{1,0},{8,10},{10,12},{12... | collective-permute-start | bytes 835592 | tf_op jit(solution)/shard_map/ppermute | solution.py:248
  14.0 1.7 %block_work.4 = (bf16[64,1024]{1,0:T(8,128)(2,1)S(1)}, bf16[64,1024]{1,0:T(8,128)(2,1)S(1)}, bf16[64,1024]{1,0:T(8,128)(2,1)S(1)}, bf16[64,1024]{1,0:T(8,128)(2,...) custom-call(bf16[136,1024]{1,0:T(8,128)(2,1)S(1)} %constant_dynamic-update-slice_fusion.refs_0_, ...), custom_call_target="tpu_custom_call" | custom-call | flops 1073741824 | bytes 3670016 | tf_op jit(solution)/shard_map/block_work/pallas_call | solution.py:147
  15.7 3.3 %collective-permute-done.2.refs_0_.refs_2_ = bf16[136,1024]{1,0:T(8,128)(2,1)S(1)} collective-permute-done((bf16[136,1024]{1,0:T(8,128)(2,1)S(1)}, bf16[136,1024]{1,0:T(8,128)(2,1)S(1)}, u32[]{:S(2)}, u32[]{:S(2)}) %collective-permute-start.2) | collective-permute-done | bytes 278560 | tf_op jit(solution)/shard_map/ppermute | solution.py:248
  19.0 1.6 %collective-permute-start.6 = (bf16[136,1024]{1,0:T(8,128)(2,1)S(1)}, bf16[136,1024]{1,0:T(8,128)(2,1)S(1)}, u32[]{:S(2)}, u32[]{:S(2)}) collective-permute-start(bf16[136,1024]{1,0:T(8,128)(2,1)S(1)} %collective-permute-done.2.refs_0_.refs_2_), channel_id=1, source_target_pairs={{0,2},{2,4},{4,6},{6,7},{7,5},{5,3},{3,1},{1,0},{8,10},{10,12},{12... | collective-permute-start | bytes 835592 | tf_op jit(solution)/shard_map/ppermute | solution.py:248
  21.1 2.4 %block_work.5 = (bf16[64,1024]{1,0:T(8,128)(2,1)S(1)}, bf16[64,1024]{1,0:T(8,128)(2,1)S(1)}, bf16[64,1024]{1,0:T(8,128)(2,1)S(1)}, bf16[64,1024]{1,0:T(8,128)(2,...) custom-call(bf16[136,1024]{1,0:T(8,128)(2,1)S(1)} %collective-permut, ...), custom_call_target="tpu_custom_call" | custom-call | flops 1610612736 | bytes 4456448 | tf_op jit(solution)/shard_map/block_work/pallas_call | solution.py:147
  23.5 2.1 %collective-permute-done.6.refs_0_.refs_5_ = bf16[136,1024]{1,0:T(8,128)(2,1)S(1)} collective-permute-done((bf16[136,1024]{1,0:T(8,128)(2,1)S(1)}, bf16[136,1024]{1,0:T(8,128)(2,1)S(1)}, u32[]{:S(2)}, u32[]{:S(2)}) %collective-permute-start.6) | collective-permute-done | bytes 278560 | tf_op jit(solution)/shard_map/ppermute | solution.py:248
  25.6 1.6 %collective-permute-done.7.refs_1_.refs_6_ = bf16[136,1024]{1,0:T(8,128)(2,1)S(1)} collective-permute-done((bf16[136,1024]{1,0:T(8,128)(2,1)S(1)}, bf16[136,1024]{1,0:T(8,128)(2,1)S(1)}, u32[]{:S(2)}, u32[]{:S(2)}) %collective-permute-start.7) | collective-permute-done | bytes 278560 | tf_op jit(solution)/shard_map/ppermute | solution.py:251
  27.1 1.6 %collective-permute-start.8 = (bf16[72,1024]{1,0:T(8,128)(2,1)S(1)}, bf16[72,1024]{1,0:T(8,128)(2,1)S(1)}, u32[]{:S(2)}, u32[]{:S(2)}) collective-permute-start(bf16[72,1024]{1,0:T(8,128)(2,1)S(1)} %pad_maximum_fusion.6), channel_id=1, source_target_pairs={{0,2},{2,4},{4,6},{6,7},{7,5},{5,3},{3,1},{1,0},{8,10},{10,12},{12... | collective-permute-start | bytes 442376 | tf_op jit(solution)/shard_map/ppermute | solution.py:248
  29.3 1.7 %block_work.6 = (bf16[64,1024]{1,0:T(8,128)(2,1)S(1)}, bf16[64,1024]{1,0:T(8,128)(2,1)S(1)}, bf16[64,1024]{1,0:T(8,128)(2,1)S(1)}, bf16[64,1024]{1,0:T(8,128)(2,...) custom-call(bf16[136,1024]{1,0:T(8,128)(2,1)S(1)} %collective-permute-done.6.refs_0_.refs_5_, ...), custom_call_target="tpu_custom_call" | custom-call | flops 1073741824 | bytes 3670016 | tf_op jit(solution)/shard_map/block_work/pallas_call | solution.py:147
  31.0 1.6 %collective-permute-start.19 = (bf16[64,1024]{1,0:T(8,128)(2,1)S(1)}, bf16[64,1024]{1,0:T(8,128)(2,1)S(1)}, u32[]{:S(2)}, u32[]{:S(2)}) collective-permute-start(bf16[64,1024]{1,0:T(8,128)(2,1)S(1)} %get-tuple-element.81), channel_id=1, source_target_pairs={{0,2},{2,4},{4,6},{6,7},{7,5},{5,3},{3,1},{1,0},{8,10},{10,12},{12... | collective-permute-start | bytes 393224 | tf_op jit(solution)/shard_map/ppermute | solution.py:248
  33.1 1.9 %collective-permute-done.9.refs_1_.refs_8_ = bf16[64,1024]{1,0:T(8,128)(2,1)S(1)} collective-permute-done((bf16[64,1024]{1,0:T(8,128)(2,1)S(1)}, bf16[64,1024]{1,0:T(8,128)(2,1)S(1)}, u32[]{:S(2)}, u32[]{:S(2)}) %collective-permute-start.9) | collective-permute-done | bytes 131104 | tf_op jit(solution)/shard_map/ppermute | solution.py:251
  35.0 1.2 %block_work.7 = (bf16[64,1024]{1,0:T(8,128)(2,1)S(1)}, bf16[64,1024]{1,0:T(8,128)(2,1)S(1)}, bf16[128,1024]{1,0:T(8,128)(2,1)S(1)}) custom-call(bf16[72,1024]{1,0:T(8,128)(2,1)S(1)} %collective-permute-done.8.refs_0_.refs_7_, bf16[64,1024]{1,0:T(8,128)(2,1)S(1)} %collective-permute-done.9.refs_1_.refs_8_, bf16[1024,1024]{1,0:T(8,128)(2,1)S(1)} %copy-done.1, ...), custom_call_target="tpu_custom_call" | custom-call | flops 536870912 | bytes 2883584 | tf_op jit(solution)/shard_map/block_work/pallas_call | solution.py:147
  36.7 1.6 %collective-permute-start.18 = (bf16[64,1024]{1,0:T(8,128)(2,1)S(1)}, bf16[64,1024]{1,0:T(8,128)(2,1)S(1)}, u32[]{:S(2)}, u32[]{:S(2)}) collective-permute-start(bf16[64,1024]{1,0:T(8,128)(2,1)S(1)} %get-tuple-element.66), channel_id=1, source_target_pairs={{0,2},{2,4},{4,6},{6,7},{7,5},{5,3},{3,1},{1,0},{8,10},{10,12},{12... | collective-permute-start | bytes 393224 | tf_op jit(solution)/shard_map/ppermute | solution.py:248
  38.3 1.3 %weight_work.3 = (bf16[1024,256]{1,0:T(8,128)(2,1)S(1)}, bf16[1024,256]{1,0:T(8,128)(2,1)S(1)}) custom-call(bf16[136,1024]{1,0:T(8,128)(2,1)S(1)} %constant_dynamic-update-slice_fusion.refs_0_, bf16[136,1024]{1,0:T(8,128)(2,1)S(1)} %constant_dynamic-update-slice_fusion.2.refs_1_, bf16[136,1024]{1,0:T(8,128)(2,1)S(1)} %collective-permute-done.2.refs_0_.refs_2_, ...), custom_call_target="tpu_custom_call" | custom-call | flops 1073741824 | bytes 4718592 | tf_op jit(solution)/shard_map/weight_work/pallas_call | solution.py:190
  39.6 1.3 %weight_work.2 = (bf16[1024,256]{1,0:T(8,128)(2,1)S(1)}, bf16[1024,256]{1,0:T(8,128)(2,1)S(1)}) custom-call(bf16[136,1024]{1,0:T(8,128)(2,1)S(1)} %constant_dynamic-update-slice_fusion.refs_0_, bf16[136,1024]{1,0:T(8,128)(2,1)S(1)} %constant_dynamic-update-slice_fusion.2.refs_1_, bf16[136,1024]{1,0:T(8,128)(2,1)S(1)} %collective-permute-done.2.refs_0_.refs_2_, ...), custom_call_target="tpu_custom_call" | custom-call | flops 1073741824 | bytes 4718592 | tf_op jit(solution)/shard_map/weight_work/pallas_call | solution.py:190
  42.4 1.6 %collective-permute-start.20 = (bf16[128,1024]{1,0:T(8,128)(2,1)S(1)}, bf16[128,1024]{1,0:T(8,128)(2,1)S(1)}, u32[]{:S(2)}, u32[]{:S(2)}) collective-permute-start(bf16[128,1024]{1,0:T(8,128)(2,1)S(1)} %pad_maximum_fusion.3), channel_id=1, source_target_pairs={{0,2},{2,4},{4,6},{6,7},{7,5},{5,3},{3,1},{1,0},{8,10},{10,12},{12... | collective-permute-start | bytes 786440 | tf_op jit(solution)/shard_map/ppermute | solution.py:248
  44.0 5.9 %collective-permute-done.15 = bf16[128,1024]{1,0:T(8,128)(2,1)S(1)} collective-permute-done((bf16[128,1024]{1,0:T(8,128)(2,1)S(1)}, bf16[128,1024]{1,0:T(8,128)(2,1)S(1)}, u32[]{:S(2)}, u32[]{:S(2)}) %collective-permute-start.15) | collective-permute-done | bytes 262176 | tf_op jit(solution)/shard_map/ppermute | solution.py:251
  50.5 1.5 %collective-permute-start.12 = (bf16[1024,256]{1,0:T(8,128)(2,1)S(1)}, bf16[1024,256]{1,0:T(8,128)(2,1)S(1)}, u32[]{:S(2)}, u32[]{:S(2)}) collective-permute-start(bf16[1024,256]{1,0:T(8,128)(2,1)S(1)} %add_convert_fusion), channel_id=1, source_target_pairs={{0,16},{8,24},{16,0},{24,8},{1,17},{9,25},{17,1},{25,9},{2,18},{10... | collective-permute-start | bytes 1572872 | tf_op jit(solution)/shard_map/ppermute | solution.py:304
  52.1 1.6 %collective-permute-start.21 = (bf16[128,1024]{1,0:T(8,128)(2,1)S(1)}, bf16[128,1024]{1,0:T(8,128)(2,1)S(1)}, u32[]{:S(2)}, u32[]{:S(2)}) collective-permute-start(bf16[128,1024]{1,0:T(8,128)(2,1)S(1)} %pad_maximum_fusion.4), channel_id=1, source_target_pairs={{0,2},{2,4},{4,6},{6,7},{7,5},{5,3},{3,1},{1,0},{8,10},{10,12},{12... | collective-permute-start | bytes 786440 | tf_op jit(solution)/shard_map/ppermute | solution.py:248
  53.8 3.7 %collective-permute-done.16 = bf16[128,1024]{1,0:T(8,128)(2,1)S(1)} collective-permute-done((bf16[128,1024]{1,0:T(8,128)(2,1)S(1)}, bf16[128,1024]{1,0:T(8,128)(2,1)S(1)}, u32[]{:S(2)}, u32[]{:S(2)}) %collective-permute-start.16) | collective-permute-done | bytes 262176 | tf_op jit(solution)/shard_map/ppermute | solution.py:251
  58.0 1.0 %collective-permute-done.21 = bf16[128,1024]{1,0:T(8,128)(2,1)S(1)} collective-permute-done((bf16[128,1024]{1,0:T(8,128)(2,1)S(1)}, bf16[128,1024]{1,0:T(8,128)(2,1)S(1)}, u32[]{:S(2)}, u32[]{:S(2)}) %collective-permute-start.21) | collective-permute-done | bytes 262176 | tf_op jit(solution)/shard_map/ppermute | solution.py:248
  59.1 1.6 %collective-permute-start.22 = (bf16[64,1024]{1,0:T(8,128)(2,1)S(1)}, bf16[64,1024]{1,0:T(8,128)(2,1)S(1)}, u32[]{:S(2)}, u32[]{:S(2)}) collective-permute-start(bf16[64,1024]{1,0:T(8,128)(2,1)S(1)} %add_convert_fusion.3), channel_id=1, source_target_pairs={{0,2},{2,4},{4,6},{6,7},{7,5},{5,3},{3,1},{1,0},{8,10},{10,12},{12... | collective-permute-start | bytes 393224 | tf_op jit(solution)/shard_map/ppermute | solution.py:248
  60.7 2.6 %collective-permute-done.12.refs_2_ = bf16[1024,256]{1,0:T(8,128)(2,1)S(1)} collective-permute-done((bf16[1024,256]{1,0:T(8,128)(2,1)S(1)}, bf16[1024,256]{1,0:T(8,128)(2,1)S(1)}, u32[]{:S(2)}, u32[]{:S(2)}) %collective-permute-start.12) | collective-permute-done | bytes 524320 | tf_op jit(solution)/shard_map/ppermute | solution.py:304
  63.3 1.0 %weight_sum.1 = bf16[1024,256]{1,0:T(8,128)(2,1)} custom-call(bf16[1024,256]{1,0:T(8,128)(2,1)S(1)} %get-tuple-element.68.refs_0_, bf16[1024,256]{1,0:T(8,128)(2,1)S(1)} %collective-permute-done.10.refs_1_, bf16[1024,256]{1,0:T(8,128)(2,1)S(1)} %collective-permute-done.12.refs_2_), custom_call_target="tpu_custom_call" | custom-call | flops 8000000000 | bytes 2097152 | tf_op jit(solution)/shard_map/weight_sum/pallas_call | solution.py:219
  64.4 0.7 %pad_maximum_fusion.5 = bf16[128,1024]{1,0:T(8,128)(2,1)} fusion(bf16[64,1024]{1,0:T(8,128)(2,1)S(1)} %add_convert_fusion.1, bf16[64,1024]{1,0:T(8,128)(2,1)S(1)} %add_convert_fusion.2), kind=kLoop, calls=%fused_computation.6 | loop fusion | flops 524288 | bytes 524288 | tf_op jit(solution)/shard_map/concatenate | solution.py:331
  (62 shorter events, 6.2 us)
Async XLA Ops:
  0.6 9.7 %collective-permute-start = (bf16[128,1024]{1,0:T(8,128)(2,1)}, bf16[128,1024]{1,0:T(8,128)(2,1)S(1)}, u32[]{:S(2)}, u32[]{:S(2)}) collective-permute-start(bf16[128,1024]{1,0:T(8,128)(2,1)} %param.5), channel_id=1, source_target_pairs={{0,2},{2,4},{4,6},{6,7},{7,5},{5,3},{3,1},{1,0},{8,10},{10,12},{12... | collective-permute-start | bytes 786440 | tf_op jit(solution)/shard_map/ppermute | solution.py:248
  3.7 8.2 %collective-permute-start.3 = (bf16[128,1024]{1,0:T(8,128)(2,1)}, bf16[128,1024]{1,0:T(8,128)(2,1)S(1)}, u32[]{:S(2)}, u32[]{:S(2)}) collective-permute-start(bf16[128,1024]{1,0:T(8,128)(2,1)} %param.5), channel_id=1, source_target_pairs={{2,0},{4,2},{6,4},{7,6},{5,7},{3,5},{1,3},{0,1},{10,8},{12,10},{14... | collective-permute-start | bytes 786440 | tf_op jit(solution)/shard_map/ppermute | solution.py:251
  3.7 0.7 %copy-start.2 = (s32[128,16]{0,1:T(8,128)S(1)}, s32[128,16]{0,1:T(8,128)}, u32[]{:S(2)}) copy-start(s32[128,16]{0,1:T(8,128)} %param.6) | copy-start | bytes 24580
  4.4 0.7 %copy-start.3 = (s32[128,4]{0,1:T(4,128)S(1)}, s32[128,4]{0,1:T(4,128)}, u32[]{:S(2)}) copy-start(s32[128,4]{0,1:T(4,128)} %param.7) | copy-start | bytes 6148
  5.1 6.8 %collective-permute-start.1 = (bf16[8,1024]{1,0:T(8,128)(2,1)S(1)}, bf16[8,1024]{1,0:T(8,128)(2,1)S(1)}, u32[]{:S(2)}, u32[]{:S(2)}) collective-permute-start(bf16[8,1024]{1,0:T(8,128)(2,1)S(1)} %instance_ids.1), channel_id=1, source_target_pairs={{0,2},{2,4},{4,6},{6,7},{7,5},{5,3},{3,1},{1,0},{8,10},{10,12},{12... | collective-permute-start | bytes 49160 | tf_op jit(solution)/shard_map/ppermute | solution.py:248
  7.2 6.4 %collective-permute-start.4 = (bf16[8,1024]{1,0:T(8,128)(2,1)S(1)}, bf16[8,1024]{1,0:T(8,128)(2,1)S(1)}, u32[]{:S(2)}, u32[]{:S(2)}) collective-permute-start(bf16[8,1024]{1,0:T(8,128)(2,1)S(1)} %instance_ids.1), channel_id=1, source_target_pairs={{2,0},{4,2},{6,4},{7,6},{5,7},{3,5},{1,3},{0,1},{10,8},{12,10},{14... | collective-permute-start | bytes 49160 | tf_op jit(solution)/shard_map/ppermute | solution.py:251
  7.2 1.6 %copy-start = (bf16[1024,1024]{1,0:T(8,128)(2,1)S(1)}, bf16[1024,1024]{1,0:T(8,128)(2,1)}, u32[]{:S(2)}) copy-start(bf16[1024,1024]{1,0:T(8,128)(2,1)} %refs_2_.5) | copy-start | bytes 6291460
  8.8 0.7 %copy-start.4 = (s32[8]{0:T(128)S(1)}, s32[8]{0:T(128)}, u32[]{:S(2)}) copy-start(s32[8]{0:T(128)} %size_ref.1) | copy-start | bytes 100
  9.4 4.6 %copy-start.1 = (bf16[1024,1024]{1,0:T(8,128)(2,1)S(1)}, bf16[1024,1024]{1,0:T(8,128)(2,1)}, u32[]{:S(2)}) copy-start(bf16[1024,1024]{1,0:T(8,128)(2,1)} %refs_2_.5) | copy-start | bytes 6291460
  11.9 9.2 %copy-start.5 = (bf16[128,1024]{1,0:T(8,128)(2,1)S(1)}, bf16[128,1024]{1,0:T(8,128)(2,1)}, u32[]{:S(2)}) copy-start(bf16[128,1024]{1,0:T(8,128)(2,1)} %param.5) | copy-start | bytes 786436
  11.9 7.1 %collective-permute-start.2 = (bf16[136,1024]{1,0:T(8,128)(2,1)S(1)}, bf16[136,1024]{1,0:T(8,128)(2,1)S(1)}, u32[]{:S(2)}, u32[]{:S(2)}) collective-permute-start(bf16[136,1024]{1,0:T(8,128)(2,1)S(1)} %constant_dynamic-update-slice_fusion.refs_0_), channel_id=1, source_target_pairs={{0,2},{2,4},{4,6},{6,7},{7,5},{5,3},{3,1},{1,0},{8,10},{10,12},{12... | collective-permute-start | bytes 835592 | tf_op jit(solution)/shard_map/ppermute | solution.py:248
  13.5 7.0 %collective-permute-start.5 = (bf16[136,1024]{1,0:T(8,128)(2,1)S(1)}, bf16[136,1024]{1,0:T(8,128)(2,1)S(1)}, u32[]{:S(2)}, u32[]{:S(2)}) collective-permute-start(bf16[136,1024]{1,0:T(8,128)(2,1)S(1)} %constant_dynamic-update-slice_fusion.2.refs_1_), channel_id=1, source_target_pairs={{2,0},{4,2},{6,4},{7,6},{5,7},{3,5},{1,3},{0,1},{10,8},{12,10},{14... | collective-permute-start | bytes 835592 | tf_op jit(solution)/shard_map/ppermute | solution.py:251
  19.0 6.5 %collective-permute-start.6 = (bf16[136,1024]{1,0:T(8,128)(2,1)S(1)}, bf16[136,1024]{1,0:T(8,128)(2,1)S(1)}, u32[]{:S(2)}, u32[]{:S(2)}) collective-permute-start(bf16[136,1024]{1,0:T(8,128)(2,1)S(1)} %collective-permute-done.2.refs_0_.refs_2_), channel_id=1, source_target_pairs={{0,2},{2,4},{4,6},{6,7},{7,5},{5,3},{3,1},{1,0},{8,10},{10,12},{12... | collective-permute-start | bytes 835592 | tf_op jit(solution)/shard_map/ppermute | solution.py:248
  20.6 6.5 %collective-permute-start.7 = (bf16[136,1024]{1,0:T(8,128)(2,1)S(1)}, bf16[136,1024]{1,0:T(8,128)(2,1)S(1)}, u32[]{:S(2)}, u32[]{:S(2)}) collective-permute-start(bf16[136,1024]{1,0:T(8,128)(2,1)S(1)} %collective-permute-done.5.refs_1_.refs_3_), channel_id=1, source_target_pairs={{2,0},{4,2},{6,4},{7,6},{5,7},{3,5},{1,3},{0,1},{10,8},{12,10},{14... | collective-permute-start | bytes 835592 | tf_op jit(solution)/shard_map/ppermute | solution.py:251
  27.1 5.9 %collective-permute-start.8 = (bf16[72,1024]{1,0:T(8,128)(2,1)S(1)}, bf16[72,1024]{1,0:T(8,128)(2,1)S(1)}, u32[]{:S(2)}, u32[]{:S(2)}) collective-permute-start(bf16[72,1024]{1,0:T(8,128)(2,1)S(1)} %pad_maximum_fusion.6), channel_id=1, source_target_pairs={{0,2},{2,4},{4,6},{6,7},{7,5},{5,3},{3,1},{1,0},{8,10},{10,12},{12... | collective-permute-start | bytes 442376 | tf_op jit(solution)/shard_map/ppermute | solution.py:248
  28.8 6.2 %collective-permute-start.9 = (bf16[64,1024]{1,0:T(8,128)(2,1)S(1)}, bf16[64,1024]{1,0:T(8,128)(2,1)S(1)}, u32[]{:S(2)}, u32[]{:S(2)}) collective-permute-start(bf16[64,1024]{1,0:T(8,128)(2,1)S(1)} %slice.35), channel_id=1, source_target_pairs={{2,0},{4,2},{6,4},{7,6},{5,7},{3,5},{1,3},{0,1},{10,8},{12,10},{14... | collective-permute-start | bytes 393224 | tf_op jit(solution)/shard_map/ppermute | solution.py:251
  31.0 5.7 %collective-permute-start.19 = (bf16[64,1024]{1,0:T(8,128)(2,1)S(1)}, bf16[64,1024]{1,0:T(8,128)(2,1)S(1)}, u32[]{:S(2)}, u32[]{:S(2)}) collective-permute-start(bf16[64,1024]{1,0:T(8,128)(2,1)S(1)} %get-tuple-element.81), channel_id=1, source_target_pairs={{0,2},{2,4},{4,6},{6,7},{7,5},{5,3},{3,1},{1,0},{8,10},{10,12},{12... | collective-permute-start | bytes 393224 | tf_op jit(solution)/shard_map/ppermute | solution.py:248
  32.6 7.0 %collective-permute-start.14 = (bf16[64,1024]{1,0:T(8,128)(2,1)S(1)}, bf16[64,1024]{1,0:T(8,128)(2,1)S(1)}, u32[]{:S(2)}, u32[]{:S(2)}) collective-permute-start(bf16[64,1024]{1,0:T(8,128)(2,1)S(1)} %get-tuple-element.74), channel_id=1, source_target_pairs={{2,0},{4,2},{6,4},{7,6},{5,7},{3,5},{1,3},{0,1},{10,8},{12,10},{14... | collective-permute-start | bytes 393224 | tf_op jit(solution)/shard_map/ppermute | solution.py:251
  36.2 5.4 %collective-permute-start.13 = (bf16[64,1024]{1,0:T(8,128)(2,1)S(1)}, bf16[64,1024]{1,0:T(8,128)(2,1)S(1)}, u32[]{:S(2)}, u32[]{:S(2)}) collective-permute-start(bf16[64,1024]{1,0:T(8,128)(2,1)S(1)} %get-tuple-element.65), channel_id=1, source_target_pairs={{2,0},{4,2},{6,4},{7,6},{5,7},{3,5},{1,3},{0,1},{10,8},{12,10},{14... | collective-permute-start | bytes 393224 | tf_op jit(solution)/shard_map/ppermute | solution.py:251
  36.7 5.5 %collective-permute-start.18 = (bf16[64,1024]{1,0:T(8,128)(2,1)S(1)}, bf16[64,1024]{1,0:T(8,128)(2,1)S(1)}, u32[]{:S(2)}, u32[]{:S(2)}) collective-permute-start(bf16[64,1024]{1,0:T(8,128)(2,1)S(1)} %get-tuple-element.66), channel_id=1, source_target_pairs={{0,2},{2,4},{4,6},{6,7},{7,5},{5,3},{3,1},{1,0},{8,10},{10,12},{12... | collective-permute-start | bytes 393224 | tf_op jit(solution)/shard_map/ppermute | solution.py:248
  39.5 2.7 %collective-permute-start.11 = (bf16[1024,256]{1,0:T(8,128)(2,1)S(1)}, bf16[1024,256]{1,0:T(8,128)(2,1)S(1)}, u32[]{:S(2)}, u32[]{:S(2)}) collective-permute-start(bf16[1024,256]{1,0:T(8,128)(2,1)S(1)} %get-tuple-element.71), channel_id=1, source_target_pairs={{0,8},{8,0},{16,24},{24,16},{1,9},{9,1},{17,25},{25,17},{2,10},{10... | collective-permute-start | bytes 1572872 | tf_op jit(solution)/shard_map/ppermute | solution.py:304
  40.9 19.8 %collective-permute-start.10 = (bf16[1024,256]{1,0:T(8,128)(2,1)S(1)}, bf16[1024,256]{1,0:T(8,128)(2,1)S(1)}, u32[]{:S(2)}, u32[]{:S(2)}) collective-permute-start(bf16[1024,256]{1,0:T(8,128)(2,1)S(1)} %get-tuple-element.69), channel_id=1, source_target_pairs={{0,8},{8,0},{16,24},{24,16},{1,9},{9,1},{17,25},{25,17},{2,10},{10... | collective-permute-start | bytes 1572872 | tf_op jit(solution)/shard_map/ppermute | solution.py:304
  41.6 8.3 %collective-permute-start.15 = (bf16[128,1024]{1,0:T(8,128)(2,1)S(1)}, bf16[128,1024]{1,0:T(8,128)(2,1)S(1)}, u32[]{:S(2)}, u32[]{:S(2)}) collective-permute-start(bf16[128,1024]{1,0:T(8,128)(2,1)S(1)} %pad_maximum_fusion.1), channel_id=1, source_target_pairs={{2,0},{4,2},{6,4},{7,6},{5,7},{3,5},{1,3},{0,1},{10,8},{12,10},{14... | collective-permute-start | bytes 786440 | tf_op jit(solution)/shard_map/ppermute | solution.py:251
  42.4 9.7 %collective-permute-start.20 = (bf16[128,1024]{1,0:T(8,128)(2,1)S(1)}, bf16[128,1024]{1,0:T(8,128)(2,1)S(1)}, u32[]{:S(2)}, u32[]{:S(2)}) collective-permute-start(bf16[128,1024]{1,0:T(8,128)(2,1)S(1)} %pad_maximum_fusion.3), channel_id=1, source_target_pairs={{0,2},{2,4},{4,6},{6,7},{7,5},{5,3},{3,1},{1,0},{8,10},{10,12},{12... | collective-permute-start | bytes 786440 | tf_op jit(solution)/shard_map/ppermute | solution.py:248
  50.0 7.4 %collective-permute-start.16 = (bf16[128,1024]{1,0:T(8,128)(2,1)S(1)}, bf16[128,1024]{1,0:T(8,128)(2,1)S(1)}, u32[]{:S(2)}, u32[]{:S(2)}) collective-permute-start(bf16[128,1024]{1,0:T(8,128)(2,1)S(1)} %pad_maximum_fusion.2), channel_id=1, source_target_pairs={{2,0},{4,2},{6,4},{7,6},{5,7},{3,5},{1,3},{0,1},{10,8},{12,10},{14... | collective-permute-start | bytes 786440 | tf_op jit(solution)/shard_map/ppermute | solution.py:251
  50.5 12.7 %collective-permute-start.12 = (bf16[1024,256]{1,0:T(8,128)(2,1)S(1)}, bf16[1024,256]{1,0:T(8,128)(2,1)S(1)}, u32[]{:S(2)}, u32[]{:S(2)}) collective-permute-start(bf16[1024,256]{1,0:T(8,128)(2,1)S(1)} %add_convert_fusion), channel_id=1, source_target_pairs={{0,16},{8,24},{16,0},{24,8},{1,17},{9,25},{17,1},{25,9},{2,18},{10... | collective-permute-start | bytes 1572872 | tf_op jit(solution)/shard_map/ppermute | solution.py:304
  52.1 6.9 %collective-permute-start.21 = (bf16[128,1024]{1,0:T(8,128)(2,1)S(1)}, bf16[128,1024]{1,0:T(8,128)(2,1)S(1)}, u32[]{:S(2)}, u32[]{:S(2)}) collective-permute-start(bf16[128,1024]{1,0:T(8,128)(2,1)S(1)} %pad_maximum_fusion.4), channel_id=1, source_target_pairs={{0,2},{2,4},{4,6},{6,7},{7,5},{5,3},{3,1},{1,0},{8,10},{10,12},{12... | collective-permute-start | bytes 786440 | tf_op jit(solution)/shard_map/ppermute | solution.py:248
  57.5 6.7 %collective-permute-start.17 = (bf16[64,1024]{1,0:T(8,128)(2,1)S(1)}, bf16[64,1024]{1,0:T(8,128)(2,1)S(1)}, u32[]{:S(2)}, u32[]{:S(2)}) collective-permute-start(bf16[64,1024]{1,0:T(8,128)(2,1)S(1)} %add_convert_fusion.8), channel_id=1, source_target_pairs={{2,0},{4,2},{6,4},{7,6},{5,7},{3,5},{1,3},{0,1},{10,8},{12,10},{14... | collective-permute-start | bytes 393224 | tf_op jit(solution)/shard_map/ppermute | solution.py:251
  59.1 5.3 %collective-permute-start.22 = (bf16[64,1024]{1,0:T(8,128)(2,1)S(1)}, bf16[64,1024]{1,0:T(8,128)(2,1)S(1)}, u32[]{:S(2)}, u32[]{:S(2)}) collective-permute-start(bf16[64,1024]{1,0:T(8,128)(2,1)S(1)} %add_convert_fusion.3), channel_id=1, source_target_pairs={{0,2},{2,4},{4,6},{6,7},{7,5},{5,3},{3,1},{1,0},{8,10},{10,12},{12... | collective-permute-start | bytes 393224 | tf_op jit(solution)/shard_map/ppermute | solution.py:248

commit v11 on v9

--- a/solution.py
+++ b/solution.py
@@ -219,14 +219,17 @@
     half, steps = inst_rows // 2, clus_count // 2
 
     ring = list(range(0, clus_count, 2)) + list(range(1, clus_count, 2))[::-1]
-    up = list(zip(ring, ring[1:] + ring[:1]))
+    up = []
+    for s in range(seq_count):
+        places = [s * clus_count + c for c in (ring if s % 2 == 0 else ring[::-1])]
+        up += list(zip(places, places[1:] + places[:1]))
     down = [(b, a) for a, b in up]
 
     def send_up(array):
-        return lax.ppermute(array, "clus", up)
+        return lax.ppermute(array, ("seq", "clus"), up)
 
     def send_down(array):
-        return lax.ppermute(array, "clus", down)
+        return lax.ppermute(array, ("seq", "clus"), down)
 
     used, slopes = [], []
 
@@ -240,9 +243,9 @@
     live_table = live_labels(cluster_sizes, weights)
     own = jnp.concatenate([features, ids], axis=0)
     below, below_ids = send_up(features), send_up(ids)
-    above, above_ids = send_down(features), send_down(ids)
-    below = jnp.concatenate([after(below, live_table), below_ids], axis=0)
-    above = jnp.concatenate([after(above, live_table), above_ids], axis=0)
+    above, above_ids = send_down(after(features, live_table)), send_down(ids)
+    below = jnp.concatenate([below, below_ids], axis=0)
+    above = jnp.concatenate([above, above_ids], axis=0)
     below_grad, above_grad = {}, {}
     for k in range(2, steps + 1):
         if k > 2:

time: 64.8 us -> 71.7 us (1.11)
  waiting for transfers between devices: 25.4 us -> 32.9 us
  local copies, waits for them, and re-layouts: 3.72 us -> 2.38 us
    ppermute x18, waiting for transfers between devices: 21.7 us -> 32.9 us  [the longest x9 20.4 us: send_up(): return lax.ppermute(array, ('seq', 'clus'), up)]
    ppermute x3, waiting for transfers between devices: 3.72 us -> 0.01 us  [seq_send(): return lax.ppermute(array, 'seq', [(k, k ^ bit) for k in range(seq_count)])]
    unnamed x14, local copies, waits for them, and re-layouts: 3.67 us -> 2.33 us
  transfers between devices with their start and end apart: 21 -> 21, of which waited for: 11 -> 15; matrix products, arithmetic and copies ran while one was open for 2% -> 2% of each run, Pallas kernels for 14% -> 13%
where the time goes in v11:
time: 71.7 us; the launch traced here: 71.5 us
  waiting for transfers between devices  32.9 us (46%)
  starting transfers between devices  22.8 us (32%)
  Pallas kernels  10.2 us (14%)
  local copies, waits for them, and re-layouts  2.38 us (3%)
  other arithmetic  2.34 us (3%)
  between operations  0.83 us (1%)
    ppermute x9, waiting for transfers between devices, send_up(): return lax.ppermute(array, ('seq', 'clus'), up)  20.4 us
    ppermute x9, starting transfers between devices, send_up(): return lax.ppermute(array, ('seq', 'clus'), up)  19.4 us
    ppermute x9, waiting for transfers between devices, send_down(): return lax.ppermute(array, ('seq', 'clus'), down)  12.6 us
    pallas_call x4, Pallas kernels, block_work(): pl.pallas_call(functools.partial(block_kernel, piece_rows, top_count, pos...  6.97 us
    pallas_call x2, Pallas kernels, weight_work(): pl.pallas_call(functools.partial(weight_kernel, piece_rows, column_blocks...  2.59 us
    unnamed x14, local copies, waits for them, and re-layouts  2.33 us
    convert_element_type x9, other arithmetic, add(): return total.astype(jnp.bfloat16)  2.27 us
    ppermute x3, starting transfers between devices, seq_send(): return lax.ppermute(array, 'seq', [(k, k ^ bit) for k in range(seq_count)])  2.24 us
  transfers between devices with their start and end apart: 21, of which 15 were waited for; matrix products, arithmetic and copies ran while one was open for 2% of the time, Pallas kernels for 13%

profile of v11, /device:TPU:0, one launch (start us, length us, event | category | flops | bytes accessed | tf_op | source)
XLA Modules:
  0.0 71.5 jit_solution(6907354564760228457)
XLA Ops:
  0.6 3.1 %collective-permute-start = (bf16[128,1024]{1,0:T(8,128)(2,1)}, bf16[128,1024]{1,0:T(8,128)(2,1)S(1)}, u32[]{:S(2)}, u32[]{:S(2)}) collective-permute-start(bf16[128,1024]{1,0:T(8,128)(2,1)} %param.5), channel_id=1, source_target_pairs={{0,2},{2,4},{4,6},{6,7},{7,5},{5,3},{3,1},{1,0},{9,11},{11,13},{13... | collective-permute-start | bytes 786440 | tf_op jit(solution)/shard_map/ppermute | solution.py:229
  3.7 1.6 %copy-done = bf16[1024,1024]{1,0:T(8,128)(2,1)S(1)} copy-done((bf16[1024,1024]{1,0:T(8,128)(2,1)S(1)}, bf16[1024,1024]{1,0:T(8,128)(2,1)}, u32[]{:S(2)}) %copy-start) | copy-done | bytes 2097176
  5.3 0.7 copy-done.4
  6.7 2.0 %collective-permute-start.1 = (bf16[8,1024]{1,0:T(8,128)(2,1)S(1)}, bf16[8,1024]{1,0:T(8,128)(2,1)S(1)}, u32[]{:S(2)}, u32[]{:S(2)}) collective-permute-start(bf16[8,1024]{1,0:T(8,128)(2,1)S(1)} %instance_ids.1), channel_id=1, source_target_pairs={{0,2},{2,4},{4,6},{6,7},{7,5},{5,3},{3,1},{1,0},{9,11},{11,13},{13... | collective-permute-start | bytes 49160 | tf_op jit(solution)/shard_map/ppermute | solution.py:229
  8.9 1.8 %collective-permute-done.1 = bf16[8,1024]{1,0:T(8,128)(2,1)S(1)} collective-permute-done((bf16[8,1024]{1,0:T(8,128)(2,1)S(1)}, bf16[8,1024]{1,0:T(8,128)(2,1)S(1)}, u32[]{:S(2)}, u32[]{:S(2)}) %collective-permute-start.1) | collective-permute-done | bytes 16416 | tf_op jit(solution)/shard_map/ppermute | solution.py:229
  10.7 2.0 %collective-permute-start.2 = (bf16[136,1024]{1,0:T(8,128)(2,1)S(1)}, bf16[136,1024]{1,0:T(8,128)(2,1)S(1)}, u32[]{:S(2)}, u32[]{:S(2)}) collective-permute-start(bf16[136,1024]{1,0:T(8,128)(2,1)S(1)} %constant_dynamic-update-slice_fusion.refs_0_), channel_id=1, source_target_pairs={{0,2},{2,4},{4,6},{6,7},{7,5},{5,3},{3,1},{1,0},{9,11},{11,13},{13... | collective-permute-start | bytes 835592 | tf_op jit(solution)/shard_map/ppermute | solution.py:229
  12.7 1.9 %collective-permute-done.3 = bf16[128,1024]{1,0:T(8,128)(2,1)S(1)} collective-permute-done((bf16[128,1024]{1,0:T(8,128)(2,1)}, bf16[128,1024]{1,0:T(8,128)(2,1)S(1)}, u32[]{:S(2)}, u32[]{:S(2)}) %collective-permute-start.3) | collective-permute-done | bytes 262176 | tf_op jit(solution)/shard_map/ppermute | solution.py:232
  15.0 1.7 %block_work.4 = (bf16[128,1024]{1,0:T(8,128)(2,1)S(1)}, bf16[128,1024]{1,0:T(8,128)(2,1)S(1)}, bf16[128,1024]{1,0:T(8,128)(2,1)S(1)}, bf16[128,1024]{1,0:T(8,128)(2,1)S(1)}) custom-call(bf16[136,1024]{1,0:T(8,128)(2,1)S(1)} %constant_dynamic-update-slice_fusion.refs_0_, bf16[136,1024]{1,0:T(8,128)(2,1)S(1)} %constant_dynamic-update-slice_fusion.2.refs_1_, ...), custom_call_target="tpu_custom_call" | custom-call | flops 1073741824 | bytes 3670016 | tf_op jit(solution)/shard_map/block_work/pallas_call | solution.py:146
  16.6 3.1 %collective-permute-done.2.refs_0_.refs_2_ = bf16[136,1024]{1,0:T(8,128)(2,1)S(1)} collective-permute-done((bf16[136,1024]{1,0:T(8,128)(2,1)S(1)}, bf16[136,1024]{1,0:T(8,128)(2,1)S(1)}, u32[]{:S(2)}, u32[]{:S(2)}) %collective-permute-start.2) | collective-permute-done | bytes 278560 | tf_op jit(solution)/shard_map/ppermute | solution.py:229
  19.8 2.3 %collective-permute-start.6 = (bf16[136,1024]{1,0:T(8,128)(2,1)S(1)}, bf16[136,1024]{1,0:T(8,128)(2,1)S(1)}, u32[]{:S(2)}, u32[]{:S(2)}) collective-permute-start(bf16[136,1024]{1,0:T(8,128)(2,1)S(1)} %collective-permute-done.2.refs_0_.refs_2_), channel_id=1, source_target_pairs={{0,2},{2,4},{4,6},{6,7},{7,5},{5,3},{3,1},{1,0},{9,11},{11,13},{13... | collective-permute-start | bytes 835592 | tf_op jit(solution)/shard_map/ppermute | solution.py:229
  22.2 1.8 %collective-permute-done.5.refs_1_.refs_3_ = bf16[136,1024]{1,0:T(8,128)(2,1)S(1)} collective-permute-done((bf16[136,1024]{1,0:T(8,128)(2,1)S(1)}, bf16[136,1024]{1,0:T(8,128)(2,1)S(1)}, u32[]{:S(2)}, u32[]{:S(2)}) %collective-permute-start.5) | collective-permute-done | bytes 278560 | tf_op jit(solution)/shard_map/ppermute | solution.py:232
  24.0 2.4 %block_work.5 = (bf16[128,1024]{1,0:T(8,128)(2,1)S(1)}, bf16[128,1024]{1,0:T(8,128)(2,1)S(1)}, bf16[128,1024]{1,0:T(8,128)(2,1)S(1)}, bf16[128,1024]{1,0:T(8,128...) custom-call(bf16[136,1024]{1,0:T(8,128)(2,1)S(1)} %collective-permute-done.2.refs_0_.refs_2_, ...), custom_call_target="tpu_custom_call" | custom-call | flops 1610612736 | bytes 4456448 | tf_op jit(solution)/shard_map/block_work/pallas_call | solution.py:146
  26.4 2.7 %collective-permute-done.6.refs_0_.refs_5_ = bf16[136,1024]{1,0:T(8,128)(2,1)S(1)} collective-permute-done((bf16[136,1024]{1,0:T(8,128)(2,1)S(1)}, bf16[136,1024]{1,0:T(8,128)(2,1)S(1)}, u32[]{:S(2)}, u32[]{:S(2)}) %collective-permute-start.6) | collective-permute-done | bytes 278560 | tf_op jit(solution)/shard_map/ppermute | solution.py:229
  29.1 1.7 %collective-permute-start.8 = (bf16[72,1024]{1,0:T(8,128)(2,1)S(1)}, bf16[72,1024]{1,0:T(8,128)(2,1)S(1)}, u32[]{:S(2)}, u32[]{:S(2)}) collective-permute-start(bf16[72,1024]{1,0:T(8,128)(2,1)S(1)} %pad_maximum_fusion.3), channel_id=1, source_target_pairs={{0,2},{2,4},{4,6},{6,7},{7,5},{5,3},{3,1},{1,0},{9,11},{11,13},{13... | collective-permute-start | bytes 442376 | tf_op jit(solution)/shard_map/ppermute | solution.py:229
  30.8 1.0 %collective-permute-done.7.refs_1_.refs_6_ = bf16[136,1024]{1,0:T(8,128)(2,1)S(1)} collective-permute-done((bf16[136,1024]{1,0:T(8,128)(2,1)S(1)}, bf16[136,1024]{1,0:T(8,128)(2,1)S(1)}, u32[]{:S(2)}, u32[]{:S(2)}) %collective-permute-start.7) | collective-permute-done | bytes 278560 | tf_op jit(solution)/shard_map/ppermute | solution.py:232
  32.2 1.7 %block_work.6 = (bf16[128,1024]{1,0:T(8,128)(2,1)S(1)}, bf16[128,1024]{1,0:T(8,128)(2,1)S(1)}, bf16[128,1024]{1,0:T(8,128)(2,1)S(1)}, bf16[128,1024]{1,0:T(8,128)(2,1)S(1)}) custom-call(bf16[136,1024]{1,0:T(8,128)(2,1)S(1)} %collective-permute-done.6.refs_0_.refs_5_, bf16[136,1024]{1,0:T(8,128)(2,1)S(1)} %collective-permute-done.7.refs_1_.refs_6_, ...), custom_call_target="tpu_custom_call" | custom-call | flops 1073741824 | bytes 3670016 | tf_op jit(solution)/shard_map/block_work/pallas_call | solution.py:146
  34.4 2.4 %collective-permute-done.9.refs_1_.refs_8_ = bf16[64,1024]{1,0:T(8,128)(2,1)S(1)} collective-permute-done((bf16[64,1024]{1,0:T(8,128)(2,1)S(1)}, bf16[64,1024]{1,0:T(8,128)(2,1)S(1)}, u32[]{:S(2)}, u32[]{:S(2)}) %collective-permute-start.9) | collective-permute-done | bytes 131104 | tf_op jit(solution)/shard_map/ppermute | solution.py:232
  36.9 1.2 %block_work.7 = (bf16[64,1024]{1,0:T(8,128)(2,1)S(1)}, bf16[64,1024]{1,0:T(8,128)(2,1)S(1)}, bf16[128,1024]{1,0:T(8,128)(2,1)S(1)}) custom-call(bf16[72,1024]{1,0:T(8,128)(2,1)S(1)} %collective-permute-done.8.refs_0_.refs_7_, bf16[64,1024]{1,0:T(8,128)(2,1)S(1)} %collective-permute-done.9.refs_1_.refs_8_, bf16[1024,1024]{1,0:T(8,128)(2,1)S(1)} %copy-done.1, ...), custom_call_target="tpu_custom_call" | custom-call | flops 536870912 | bytes 2883584 | tf_op jit(solution)/shard_map/block_work/pallas_call | solution.py:146
  38.1 2.1 %collective-permute-start.17 = (bf16[64,1024]{1,0:T(8,128)(2,1)S(1)}, bf16[64,1024]{1,0:T(8,128)(2,1)S(1)}, u32[]{:S(2)}, u32[]{:S(2)}) collective-permute-start(bf16[64,1024]{1,0:T(8,128)(2,1)S(1)} %get-tuple-element.57), channel_id=1, source_target_pairs={{0,2},{2,4},{4,6},{6,7},{7,5},{5,3},{3,1},{1,0},{9,11},{11,13},{13... | collective-permute-start | bytes 393224 | tf_op jit(solution)/shard_map/ppermute | solution.py:229
  40.2 1.3 %weight_work.3 = (bf16[1024,256]{1,0:T(8,128)(2,1)S(1)}, bf16[1024,256]{1,0:T(8,128)(2,1)S(1)}) custom-call(bf16[136,1024]{1,0:T(8,128)(2,1)S(1)} %constant_dynamic-update-slice_fusion.refs_0_, bf16[136,1024]{1,0:T(8,128)(2,1)S(1)} %constant_dynamic-update-slice_fusion.2.refs_1_, bf16[136,1024]{1,0:T(8,128)(2,1)S(1)} %collective-permute-done.2.refs_0_.refs_2_, ...), custom_call_target="tpu_custom_call" | custom-call | flops 1073741824 | bytes 4718592 | tf_op jit(solution)/shard_map/weight_work/pallas_call | solution.py:188
  41.6 1.3 %weight_work.2 = (bf16[1024,256]{1,0:T(8,128)(2,1)S(1)}, bf16[1024,256]{1,0:T(8,128)(2,1)S(1)}) custom-call(bf16[136,1024]{1,0:T(8,128)(2,1)S(1)} %constant_dynamic-update-slice_fusion.refs_0_, bf16[136,1024]{1,0:T(8,128)(2,1)S(1)} %constant_dynamic-update-slice_fusion.2.refs_1_, bf16[136,1024]{1,0:T(8,128)(2,1)S(1)} %collective-permute-done.2.refs_0_.refs_2_, ...), custom_call_target="tpu_custom_call" | custom-call | flops 1073741824 | bytes 4718592 | tf_op jit(solution)/shard_map/weight_work/pallas_call | solution.py:188
  43.5 2.1 %collective-permute-start.18 = (bf16[128,1024]{1,0:T(8,128)(2,1)S(1)}, bf16[128,1024]{1,0:T(8,128)(2,1)S(1)}, u32[]{:S(2)}, u32[]{:S(2)}) collective-permute-start(bf16[128,1024]{1,0:T(8,128)(2,1)S(1)} %pad_maximum_fusion.2), channel_id=1, source_target_pairs={{0,2},{2,4},{4,6},{6,7},{7,5},{5,3},{3,1},{1,0},{9,11},{11,13},{13... | collective-permute-start | bytes 786440 | tf_op jit(solution)/shard_map/ppermute | solution.py:229
  45.7 6.2 %collective-permute-done.18 = bf16[128,1024]{1,0:T(8,128)(2,1)S(1)} collective-permute-done((bf16[128,1024]{1,0:T(8,128)(2,1)S(1)}, bf16[128,1024]{1,0:T(8,128)(2,1)S(1)}, u32[]{:S(2)}, u32[]{:S(2)}) %collective-permute-start.18) | collective-permute-done | bytes 262176 | tf_op jit(solution)/shard_map/ppermute | solution.py:229
  52.0 2.1 %collective-permute-start.19 = (bf16[128,1024]{1,0:T(8,128)(2,1)S(1)}, bf16[128,1024]{1,0:T(8,128)(2,1)S(1)}, u32[]{:S(2)}, u32[]{:S(2)}) collective-permute-start(bf16[128,1024]{1,0:T(8,128)(2,1)S(1)} %add_convert_fusion.4), channel_id=1, source_target_pairs={{0,2},{2,4},{4,6},{6,7},{7,5},{5,3},{3,1},{1,0},{9,11},{11,13},{13... | collective-permute-start | bytes 786440 | tf_op jit(solution)/shard_map/ppermute | solution.py:229
  54.2 1.6 %collective-permute-start.12 = (bf16[1024,256]{1,0:T(8,128)(2,1)S(1)}, bf16[1024,256]{1,0:T(8,128)(2,1)S(1)}, u32[]{:S(2)}, u32[]{:S(2)}) collective-permute-start(bf16[1024,256]{1,0:T(8,128)(2,1)S(1)} %add_convert_fusion.1), channel_id=1, source_target_pairs={{0,16},{8,24},{16,0},{24,8},{1,17},{9,25},{17,1},{25,9},{2,18},{10... | collective-permute-start | bytes 1572872 | tf_op jit(solution)/shard_map/ppermute | solution.py:269
  56.3 3.3 %collective-permute-done.19 = bf16[128,1024]{1,0:T(8,128)(2,1)S(1)} collective-permute-done((bf16[128,1024]{1,0:T(8,128)(2,1)S(1)}, bf16[128,1024]{1,0:T(8,128)(2,1)S(1)}, u32[]{:S(2)}, u32[]{:S(2)}) %collective-permute-start.19) | collective-permute-done | bytes 262176 | tf_op jit(solution)/shard_map/ppermute | solution.py:229
  59.7 2.1 %collective-permute-start.20 = (bf16[128,1024]{1,0:T(8,128)(2,1)S(1)}, bf16[128,1024]{1,0:T(8,128)(2,1)S(1)}, u32[]{:S(2)}, u32[]{:S(2)}) collective-permute-start(bf16[128,1024]{1,0:T(8,128)(2,1)S(1)} %add_convert_fusion.3), channel_id=1, source_target_pairs={{0,2},{2,4},{4,6},{6,7},{7,5},{5,3},{3,1},{1,0},{9,11},{11,13},{13... | collective-permute-start | bytes 786440 | tf_op jit(solution)/shard_map/ppermute | solution.py:229
  61.8 1.5 %collective-permute-done.15 = bf16[128,1024]{1,0:T(8,128)(2,1)S(1)} collective-permute-done((bf16[128,1024]{1,0:T(8,128)(2,1)S(1)}, bf16[128,1024]{1,0:T(8,128)(2,1)S(1)}, u32[]{:S(2)}, u32[]{:S(2)}) %collective-permute-start.15) | collective-permute-done | bytes 262176 | tf_op jit(solution)/shard_map/ppermute | solution.py:232
  63.6 1.0 %add_convert_fusion = bf16[1024,256]{1,0:T(8,128)(2,1)} fusion(bf16[1024,256]{1,0:T(8,128)(2,1)S(1)} %collective-permute-done.12, bf16[1024,256]{1,0:T(8,128)(2,1)S(1)} %collective-permute-done.10, bf16[1024,256]{1,0:T(8,128)(2,1)S(1)} %get-tuple-element.48), kind=kLoop, calls=%fused_computation | loop fusion | flops 1572864 | bytes 2097152 | tf_op jit(solution)/shard_map/convert_element_type | solution.py:206
  64.6 2.5 %collective-permute-done.20 = bf16[128,1024]{1,0:T(8,128)(2,1)S(1)} collective-permute-done((bf16[128,1024]{1,0:T(8,128)(2,1)S(1)}, bf16[128,1024]{1,0:T(8,128)(2,1)S(1)}, u32[]{:S(2)}, u32[]{:S(2)}) %collective-permute-start.20) | collective-permute-done | bytes 262176 | tf_op jit(solution)/shard_map/ppermute | solution.py:229
  67.1 3.6 %collective-permute-done.16 = bf16[128,1024]{1,0:T(8,128)(2,1)S(1)} collective-permute-done((bf16[128,1024]{1,0:T(8,128)(2,1)S(1)}, bf16[128,1024]{1,0:T(8,128)(2,1)S(1)}, u32[]{:S(2)}, u32[]{:S(2)}) %collective-permute-start.16) | collective-permute-done | bytes 262176 | tf_op jit(solution)/shard_map/ppermute | solution.py:232
  70.7 0.8 %add_convert_fusion.2 = bf16[128,1024]{1,0:T(8,128)(2,1)} fusion(bf16[128,1024]{1,0:T(8,128)(2,1)S(1)} %collective-permute-done.20, bf16[128,1024]{1,0:T(8,128)(2,1)S(1)} %collective-permute-done.16, bf16[128,1024]{1,0:T(8,128)(2,1)S(1)} %get-tuple-element.52), kind=kLoop, calls=%fused_computation.2 | loop fusion | flops 786432 | bytes 1048576 | tf_op jit(solution)/shard_map/convert_element_type | solution.py:206
  (52 shorter events, 4.0 us)
Async XLA Ops:
  0.6 8.2 %collective-permute-start = (bf16[128,1024]{1,0:T(8,128)(2,1)}, bf16[128,1024]{1,0:T(8,128)(2,1)S(1)}, u32[]{:S(2)}, u32[]{:S(2)}) collective-permute-start(bf16[128,1024]{1,0:T(8,128)(2,1)} %param.5), channel_id=1, source_target_pairs={{0,2},{2,4},{4,6},{6,7},{7,5},{5,3},{3,1},{1,0},{9,11},{11,13},{13... | collective-permute-start | bytes 786440 | tf_op jit(solution)/shard_map/ppermute | solution.py:229
  3.7 1.6 %copy-start = (bf16[1024,1024]{1,0:T(8,128)(2,1)S(1)}, bf16[1024,1024]{1,0:T(8,128)(2,1)}, u32[]{:S(2)}) copy-start(bf16[1024,1024]{1,0:T(8,128)(2,1)} %refs_2_.5) | copy-start | bytes 6291460
  5.3 0.7 copy-start.4
  6.0 0.7 copy-start.2
  6.0 0.7 copy-start.3
  6.0 9.0 %copy-start.1 = (bf16[1024,1024]{1,0:T(8,128)(2,1)S(1)}, bf16[1024,1024]{1,0:T(8,128)(2,1)}, u32[]{:S(2)}) copy-start(bf16[1024,1024]{1,0:T(8,128)(2,1)} %refs_2_.5) | copy-start | bytes 6291460
  6.5 8.0 %collective-permute-start.3 = (bf16[128,1024]{1,0:T(8,128)(2,1)}, bf16[128,1024]{1,0:T(8,128)(2,1)S(1)}, u32[]{:S(2)}, u32[]{:S(2)}) collective-permute-start(bf16[128,1024]{1,0:T(8,128)(2,1)} %param.5), channel_id=1, source_target_pairs={{2,0},{4,2},{6,4},{7,6},{5,7},{3,5},{1,3},{0,1},{11,9},{13,11},{15... | collective-permute-start | bytes 786440 | tf_op jit(solution)/shard_map/ppermute | solution.py:232
  6.7 4.0 %collective-permute-start.1 = (bf16[8,1024]{1,0:T(8,128)(2,1)S(1)}, bf16[8,1024]{1,0:T(8,128)(2,1)S(1)}, u32[]{:S(2)}, u32[]{:S(2)}) collective-permute-start(bf16[8,1024]{1,0:T(8,128)(2,1)S(1)} %instance_ids.1), channel_id=1, source_target_pairs={{0,2},{2,4},{4,6},{6,7},{7,5},{5,3},{3,1},{1,0},{9,11},{11,13},{13... | collective-permute-start | bytes 49160 | tf_op jit(solution)/shard_map/ppermute | solution.py:229
  8.7 6.2 %collective-permute-start.4 = (bf16[8,1024]{1,0:T(8,128)(2,1)S(1)}, bf16[8,1024]{1,0:T(8,128)(2,1)S(1)}, u32[]{:S(2)}, u32[]{:S(2)}) collective-permute-start(bf16[8,1024]{1,0:T(8,128)(2,1)S(1)} %instance_ids.1), channel_id=1, source_target_pairs={{2,0},{4,2},{6,4},{7,6},{5,7},{3,5},{1,3},{0,1},{11,9},{13,11},{15... | collective-permute-start | bytes 49160 | tf_op jit(solution)/shard_map/ppermute | solution.py:232
  10.7 9.1 %collective-permute-start.2 = (bf16[136,1024]{1,0:T(8,128)(2,1)S(1)}, bf16[136,1024]{1,0:T(8,128)(2,1)S(1)}, u32[]{:S(2)}, u32[]{:S(2)}) collective-permute-start(bf16[136,1024]{1,0:T(8,128)(2,1)S(1)} %constant_dynamic-update-slice_fusion.refs_0_), channel_id=1, source_target_pairs={{0,2},{2,4},{4,6},{6,7},{7,5},{5,3},{3,1},{1,0},{9,11},{11,13},{13... | collective-permute-start | bytes 835592 | tf_op jit(solution)/shard_map/ppermute | solution.py:229
  14.6 7.5 %copy-start.5 = (bf16[128,1024]{1,0:T(8,128)(2,1)S(1)}, bf16[128,1024]{1,0:T(8,128)(2,1)}, u32[]{:S(2)}) copy-start(bf16[128,1024]{1,0:T(8,128)(2,1)} %param.5) | copy-start | bytes 786436
  14.9 9.0 %collective-permute-start.5 = (bf16[136,1024]{1,0:T(8,128)(2,1)S(1)}, bf16[136,1024]{1,0:T(8,128)(2,1)S(1)}, u32[]{:S(2)}, u32[]{:S(2)}) collective-permute-start(bf16[136,1024]{1,0:T(8,128)(2,1)S(1)} %constant_dynamic-update-slice_fusion.2.refs_1_), channel_id=1, source_target_pairs={{2,0},{4,2},{6,4},{7,6},{5,7},{3,5},{1,3},{0,1},{11,9},{13,11},{15... | collective-permute-start | bytes 835592 | tf_op jit(solution)/shard_map/ppermute | solution.py:232
  19.8 9.3 %collective-permute-start.6 = (bf16[136,1024]{1,0:T(8,128)(2,1)S(1)}, bf16[136,1024]{1,0:T(8,128)(2,1)S(1)}, u32[]{:S(2)}, u32[]{:S(2)}) collective-permute-start(bf16[136,1024]{1,0:T(8,128)(2,1)S(1)} %collective-permute-done.2.refs_0_.refs_2_), channel_id=1, source_target_pairs={{0,2},{2,4},{4,6},{6,7},{7,5},{5,3},{3,1},{1,0},{9,11},{11,13},{13... | collective-permute-start | bytes 835592 | tf_op jit(solution)/shard_map/ppermute | solution.py:229
  24.0 7.8 %collective-permute-start.7 = (bf16[136,1024]{1,0:T(8,128)(2,1)S(1)}, bf16[136,1024]{1,0:T(8,128)(2,1)S(1)}, u32[]{:S(2)}, u32[]{:S(2)}) collective-permute-start(bf16[136,1024]{1,0:T(8,128)(2,1)S(1)} %collective-permute-done.5.refs_1_.refs_3_), channel_id=1, source_target_pairs={{2,0},{4,2},{6,4},{7,6},{5,7},{3,5},{1,3},{0,1},{11,9},{13,11},{15... | collective-permute-start | bytes 835592 | tf_op jit(solution)/shard_map/ppermute | solution.py:232
  29.1 5.3 %collective-permute-start.8 = (bf16[72,1024]{1,0:T(8,128)(2,1)S(1)}, bf16[72,1024]{1,0:T(8,128)(2,1)S(1)}, u32[]{:S(2)}, u32[]{:S(2)}) collective-permute-start(bf16[72,1024]{1,0:T(8,128)(2,1)S(1)} %pad_maximum_fusion.3), channel_id=1, source_target_pairs={{0,2},{2,4},{4,6},{6,7},{7,5},{5,3},{3,1},{1,0},{9,11},{11,13},{13... | collective-permute-start | bytes 442376 | tf_op jit(solution)/shard_map/ppermute | solution.py:229
  31.8 5.0 %collective-permute-start.9 = (bf16[64,1024]{1,0:T(8,128)(2,1)S(1)}, bf16[64,1024]{1,0:T(8,128)(2,1)S(1)}, u32[]{:S(2)}, u32[]{:S(2)}) collective-permute-start(bf16[64,1024]{1,0:T(8,128)(2,1)S(1)} %slice.23), channel_id=1, source_target_pairs={{2,0},{4,2},{6,4},{7,6},{5,7},{3,5},{1,3},{0,1},{11,9},{13,11},{15... | collective-permute-start | bytes 393224 | tf_op jit(solution)/shard_map/ppermute | solution.py:232
  38.1 5.3 %collective-permute-start.17 = (bf16[64,1024]{1,0:T(8,128)(2,1)S(1)}, bf16[64,1024]{1,0:T(8,128)(2,1)S(1)}, u32[]{:S(2)}, u32[]{:S(2)}) collective-permute-start(bf16[64,1024]{1,0:T(8,128)(2,1)S(1)} %get-tuple-element.57), channel_id=1, source_target_pairs={{0,2},{2,4},{4,6},{6,7},{7,5},{5,3},{3,1},{1,0},{9,11},{11,13},{13... | collective-permute-start | bytes 393224 | tf_op jit(solution)/shard_map/ppermute | solution.py:229
  40.2 5.4 %collective-permute-start.13 = (bf16[64,1024]{1,0:T(8,128)(2,1)S(1)}, bf16[64,1024]{1,0:T(8,128)(2,1)S(1)}, u32[]{:S(2)}, u32[]{:S(2)}) collective-permute-start(bf16[64,1024]{1,0:T(8,128)(2,1)S(1)} %get-tuple-element.53), channel_id=1, source_target_pairs={{2,0},{4,2},{6,4},{7,6},{5,7},{3,5},{1,3},{0,1},{11,9},{13,11},{15... | collective-permute-start | bytes 393224 | tf_op jit(solution)/shard_map/ppermute | solution.py:232
  41.5 12.6 %collective-permute-start.11 = (bf16[1024,256]{1,0:T(8,128)(2,1)S(1)}, bf16[1024,256]{1,0:T(8,128)(2,1)S(1)}, u32[]{:S(2)}, u32[]{:S(2)}) collective-permute-start(bf16[1024,256]{1,0:T(8,128)(2,1)S(1)} %get-tuple-element.51), channel_id=1, source_target_pairs={{0,8},{8,0},{16,24},{24,16},{1,9},{9,1},{17,25},{25,17},{2,10},{10... | collective-permute-start | bytes 1572872 | tf_op jit(solution)/shard_map/ppermute | solution.py:269
  42.9 20.7 %collective-permute-start.10 = (bf16[1024,256]{1,0:T(8,128)(2,1)S(1)}, bf16[1024,256]{1,0:T(8,128)(2,1)S(1)}, u32[]{:S(2)}, u32[]{:S(2)}) collective-permute-start(bf16[1024,256]{1,0:T(8,128)(2,1)S(1)} %get-tuple-element.49), channel_id=1, source_target_pairs={{0,8},{8,0},{16,24},{24,16},{1,9},{9,1},{17,25},{25,17},{2,10},{10... | collective-permute-start | bytes 1572872 | tf_op jit(solution)/shard_map/ppermute | solution.py:269
  43.5 8.4 %collective-permute-start.18 = (bf16[128,1024]{1,0:T(8,128)(2,1)S(1)}, bf16[128,1024]{1,0:T(8,128)(2,1)S(1)}, u32[]{:S(2)}, u32[]{:S(2)}) collective-permute-start(bf16[128,1024]{1,0:T(8,128)(2,1)S(1)} %pad_maximum_fusion.2), channel_id=1, source_target_pairs={{0,2},{2,4},{4,6},{6,7},{7,5},{5,3},{3,1},{1,0},{9,11},{11,13},{13... | collective-permute-start | bytes 786440 | tf_op jit(solution)/shard_map/ppermute | solution.py:229
  45.6 10.2 %collective-permute-start.14 = (bf16[128,1024]{1,0:T(8,128)(2,1)S(1)}, bf16[128,1024]{1,0:T(8,128)(2,1)S(1)}, u32[]{:S(2)}, u32[]{:S(2)}) collective-permute-start(bf16[128,1024]{1,0:T(8,128)(2,1)S(1)} %pad_maximum_fusion.1), channel_id=1, source_target_pairs={{2,0},{4,2},{6,4},{7,6},{5,7},{3,5},{1,3},{0,1},{11,9},{13,11},{15... | collective-permute-start | bytes 786440 | tf_op jit(solution)/shard_map/ppermute | solution.py:232
  52.0 7.6 %collective-permute-start.19 = (bf16[128,1024]{1,0:T(8,128)(2,1)S(1)}, bf16[128,1024]{1,0:T(8,128)(2,1)S(1)}, u32[]{:S(2)}, u32[]{:S(2)}) collective-permute-start(bf16[128,1024]{1,0:T(8,128)(2,1)S(1)} %add_convert_fusion.4), channel_id=1, source_target_pairs={{0,2},{2,4},{4,6},{6,7},{7,5},{5,3},{3,1},{1,0},{9,11},{11,13},{13... | collective-permute-start | bytes 786440 | tf_op jit(solution)/shard_map/ppermute | solution.py:229
  54.2 9.4 %collective-permute-start.12 = (bf16[1024,256]{1,0:T(8,128)(2,1)S(1)}, bf16[1024,256]{1,0:T(8,128)(2,1)S(1)}, u32[]{:S(2)}, u32[]{:S(2)}) collective-permute-start(bf16[1024,256]{1,0:T(8,128)(2,1)S(1)} %add_convert_fusion.1), channel_id=1, source_target_pairs={{0,16},{8,24},{16,0},{24,8},{1,17},{9,25},{17,1},{25,9},{2,18},{10... | collective-permute-start | bytes 1572872 | tf_op jit(solution)/shard_map/ppermute | solution.py:269
  55.9 7.3 %collective-permute-start.15 = (bf16[128,1024]{1,0:T(8,128)(2,1)S(1)}, bf16[128,1024]{1,0:T(8,128)(2,1)S(1)}, u32[]{:S(2)}, u32[]{:S(2)}) collective-permute-start(bf16[128,1024]{1,0:T(8,128)(2,1)S(1)} %add_convert_fusion.6), channel_id=1, source_target_pairs={{2,0},{4,2},{6,4},{7,6},{5,7},{3,5},{1,3},{0,1},{11,9},{13,11},{15... | collective-permute-start | bytes 786440 | tf_op jit(solution)/shard_map/ppermute | solution.py:232
  59.7 7.4 %collective-permute-start.20 = (bf16[128,1024]{1,0:T(8,128)(2,1)S(1)}, bf16[128,1024]{1,0:T(8,128)(2,1)S(1)}, u32[]{:S(2)}, u32[]{:S(2)}) collective-permute-start(bf16[128,1024]{1,0:T(8,128)(2,1)S(1)} %add_convert_fusion.3), channel_id=1, source_target_pairs={{0,2},{2,4},{4,6},{6,7},{7,5},{5,3},{3,1},{1,0},{9,11},{11,13},{13... | collective-permute-start | bytes 786440 | tf_op jit(solution)/shard_map/ppermute | solution.py:229
  63.3 7.4 %collective-permute-start.16 = (bf16[128,1024]{1,0:T(8,128)(2,1)S(1)}, bf16[128,1024]{1,0:T(8,128)(2,1)S(1)}, u32[]{:S(2)}, u32[]{:S(2)}) collective-permute-start(bf16[128,1024]{1,0:T(8,128)(2,1)S(1)} %add_convert_fusion.5), channel_id=1, source_target_pairs={{2,0},{4,2},{6,4},{7,6},{5,7},{3,5},{1,3},{0,1},{11,9},{13,11},{15... | collective-permute-start | bytes 786440 | tf_op jit(solution)/shard_map/ppermute | solution.py:232

commit v12 on v9

--- a/solution.py
+++ b/solution.py
@@ -206,6 +206,43 @@
     return total.astype(jnp.bfloat16)
 
 
+def sum_kernel(pieces, *refs):
+    *in_refs, out_ref, held, sems = refs
+    rows = out_ref.shape[0] // pieces
+    copies = []
+    for p in range(pieces):
+        at = pl.ds(p * rows, rows)
+        total = in_refs[0][at, :].astype(jnp.float32)
+        for ref in in_refs[1:]:
+            total = total + ref[at, :].astype(jnp.float32)
+        held[at, :] = total.astype(jnp.bfloat16)
+        copies.append(pltpu.make_async_copy(held.at[at], out_ref.at[at], sems.at[p]))
+        copies[-1].start()
+    for copy in copies:
+        copy.wait()
+
+
+def final_sum(parts, pieces):
+    shape = parts[0].shape
+    return pl.pallas_call(
+        functools.partial(sum_kernel, pieces),
+        out_shape=jax.ShapeDtypeStruct(shape, jnp.bfloat16),
+        in_specs=[pl.BlockSpec(memory_space=pltpu.VMEM)] * len(parts),
+        out_specs=pl.BlockSpec(memory_space=pl.ANY),
+        scratch_shapes=[
+            pltpu.VMEM(shape, jnp.bfloat16),
+            pltpu.SemaphoreType.DMA((pieces,)),
+        ],
+        compiler_params=pltpu.CompilerParams(vmem_limit_bytes=VMEM_LIMIT),
+        cost_estimate=pl.CostEstimate(
+            flops=len(parts) * parts[0].size,
+            bytes_accessed=2 * (len(parts) + 1) * parts[0].size,
+            transcendentals=0,
+        ),
+        name="final_sum",
+    )(*parts)
+
+
 def after(array, *others):
     return lax.optimization_barrier((array, *others))[0]
 
@@ -265,10 +302,9 @@
     def seq_send(array, bit):
         return lax.ppermute(array, "seq", [(k, k ^ bit) for k in range(seq_count)])
 
-    far, near = list(range(seq_count // 2, seq_count)), list(range(seq_count // 2))
-    terms = dict(zip(far, weight_work(used, slopes, far, part_width, scale)))
-    terms.update(zip(near, weight_work(used, slopes, near, part_width, scale)))
-    terms = {q: [term] for q, term in terms.items()}
+    slots = list(range(seq_count))[::-1]
+    parts = weight_work(used, slopes, slots, part_width, scale)
+    terms = {q: [part] for q, part in zip(slots, parts)}
     bit = 1
     while bit < seq_count:
         for q in [q for q in sorted(terms, reverse=True) if q & bit]:
@@ -284,8 +320,8 @@
             to_up = jnp.concatenate([near_above[:half], add(near_above[half:], from_below)], axis=0)
         elif k > 1:
             to_down, to_up = add(below_grad[k - 1], from_above), add(above_grad[k - 1], from_below)
-    weight_grad = add(*terms[0])
-    feature_grad = add(after(own_grad, weight_grad), from_above, from_below)
+    weight_grad = final_sum(terms[0], 4)
+    feature_grad = final_sum([after(own_grad, weight_grad), from_above, from_below], 4)
     return (feature_grad, weight_grad)
 
 

time: 64.8 us -> 64.4 us (level)
  other arithmetic: 2.34 us -> 0.53 us
  Pallas kernels: 10.2 us -> 11.6 us
    convert_element_type x9 -> x7, other arithmetic: 2.27 us -> 0.46 us  [add(): return total.astype(jnp.bfloat16)]
    pallas_call x0 -> x2, Pallas kernels: none -> 1.64 us  [final_sum(): pl.pallas_call(functools.partial(sum_kernel, pieces), out_shape=jax.Shape...]
    ppermute x3, waiting for transfers between devices: 3.72 us -> 5.14 us  [seq_send(): return lax.ppermute(array, 'seq', [(k, k ^ bit) for k in range(seq_count)])]
    ppermute x9, waiting for transfers between devices: 3.83 us -> 2.99 us  [send_down(): return lax.ppermute(array, 'clus', down)]
    pallas_call x2 -> x1, Pallas kernels: 2.59 us -> 2.37 us  [weight_work(): pl.pallas_call(functools.partial(weight_kernel, piece_rows, column_blocks...]
  transfers between devices with their start and end apart: 21 -> 21, of which waited for: 11 -> 10; matrix products, arithmetic and copies ran while one was open for 2% -> 1% of each run, Pallas kernels for 14% -> 15%
where the time goes in v12:
time: 64.4 us; the launch traced here: 64.1 us
  waiting for transfers between devices  25.9 us (40%)
  starting transfers between devices  21.5 us (33%)
  Pallas kernels  11.6 us (18%)
  local copies, waits for them, and re-layouts  3.72 us (6%)
  between operations  0.86 us (1%)
    ppermute x9, waiting for transfers between devices, send_up(): return lax.ppermute(array, 'clus', up)  17.8 us
    ppermute x9, starting transfers between devices, send_up(): return lax.ppermute(array, 'clus', up)  16.4 us
    pallas_call x4, Pallas kernels, block_work(): pl.pallas_call(functools.partial(block_kernel, piece_rows, top_count, pos...  6.97 us
    ppermute x3, waiting for transfers between devices, seq_send(): return lax.ppermute(array, 'seq', [(k, k ^ bit) for k in range(seq_count)])  5.14 us
    unnamed x14, local copies, waits for them, and re-layouts  3.67 us
    ppermute x9, starting transfers between devices, send_down(): return lax.ppermute(array, 'clus', down)  3.49 us
    ppermute x9, waiting for transfers between devices, send_down(): return lax.ppermute(array, 'clus', down)  2.99 us
    pallas_call x1, Pallas kernels, weight_work(): pl.pallas_call(functools.partial(weight_kernel, piece_rows, column_blocks...  2.37 us
  transfers between devices with their start and end apart: 21, of which 10 were waited for; matrix products, arithmetic and copies ran while one was open for 1% of the time, Pallas kernels for 15%

profile of v12, /device:TPU:0, one launch (start us, length us, event | category | flops | bytes accessed | tf_op | source)
XLA Modules:
  0.0 64.1 jit_solution(7091733448248826093)
XLA Ops:
  0.6 3.1 %collective-permute-start = (bf16[128,1024]{1,0:T(8,128)(2,1)}, bf16[128,1024]{1,0:T(8,128)(2,1)S(1)}, u32[]{:S(2)}, u32[]{:S(2)}) collective-permute-start(bf16[128,1024]{1,0:T(8,128)(2,1)} %param.5), channel_id=1, source_target_pairs={{0,2},{2,4},{4,6},{6,7},{7,5},{5,3},{3,1},{1,0},{8,10},{10,12},{12... | collective-permute-start | bytes 786440 | tf_op jit(solution)/shard_map/ppermute | solution.py:263
  3.7 0.7 %copy-done.2 = s32[128,16]{0,1:T(8,128)S(1)} copy-done((s32[128,16]{0,1:T(8,128)S(1)}, s32[128,16]{0,1:T(8,128)}, u32[]{:S(2)}) %copy-start.2) | copy-done | bytes 8216
  4.4 0.7 %copy-done.3 = s32[128,4]{0,1:T(4,128)S(1)} copy-done((s32[128,4]{0,1:T(4,128)S(1)}, s32[128,4]{0,1:T(4,128)}, u32[]{:S(2)}) %copy-start.3) | copy-done | bytes 2072
  5.1 2.1 %collective-permute-start.1 = (bf16[8,1024]{1,0:T(8,128)(2,1)S(1)}, bf16[8,1024]{1,0:T(8,128)(2,1)S(1)}, u32[]{:S(2)}, u32[]{:S(2)}) collective-permute-start(bf16[8,1024]{1,0:T(8,128)(2,1)S(1)} %instance_ids.1), channel_id=1, source_target_pairs={{0,2},{2,4},{4,6},{6,7},{7,5},{5,3},{3,1},{1,0},{8,10},{10,12},{12... | collective-permute-start | bytes 49160 | tf_op jit(solution)/shard_map/ppermute | solution.py:263
  7.2 1.6 %copy-done = bf16[1024,1024]{1,0:T(8,128)(2,1)S(1)} copy-done((bf16[1024,1024]{1,0:T(8,128)(2,1)S(1)}, bf16[1024,1024]{1,0:T(8,128)(2,1)}, u32[]{:S(2)}) %copy-start) | copy-done | bytes 2097176
  8.8 0.7 %copy-done.4 = s32[8]{0:T(128)S(1)} copy-done((s32[8]{0:T(128)S(1)}, s32[8]{0:T(128)}, u32[]{:S(2)}) %copy-start.4) | copy-done | bytes 56
  9.5 0.6 live_labels.1.refs_3_.refs_4_
  10.4 1.5 %collective-permute-done.3 = bf16[128,1024]{1,0:T(8,128)(2,1)S(1)} collective-permute-done((bf16[128,1024]{1,0:T(8,128)(2,1)}, bf16[128,1024]{1,0:T(8,128)(2,1)S(1)}, u32[]{:S(2)}, u32[]{:S(2)}) %collective-permute-start.3) | collective-permute-done | bytes 262176 | tf_op jit(solution)/shard_map/ppermute | solution.py:266
  11.9 1.6 %collective-permute-start.2 = (bf16[136,1024]{1,0:T(8,128)(2,1)S(1)}, bf16[136,1024]{1,0:T(8,128)(2,1)S(1)}, u32[]{:S(2)}, u32[]{:S(2)}) collective-permute-start(bf16[136,1024]{1,0:T(8,128)(2,1)S(1)} %constant_dynamic-update-slice_fusion.refs_0_), channel_id=1, source_target_pairs={{0,2},{2,4},{4,6},{6,7},{7,5},{5,3},{3,1},{1,0},{8,10},{10,12},{12... | collective-permute-start | bytes 835592 | tf_op jit(solution)/shard_map/ppermute | solution.py:263
  14.0 1.7 %block_work.4 = (bf16[128,1024]{1,0:T(8,128)(2,1)S(1)}, bf16[128,1024]{1,0:T(8,128)(2,1)S(1)}, bf16[128,1024]{1,0:T(8,128)(2,1)S(1)}, bf16[128,1024]{1,0:T(8,128)(2,1)S(1)}) custom-call(bf16[136,1024]{1,0:T(8,128)(2,1)S(1)} %constant_dynamic-update-slice_fusion.refs_0_, bf16[136,1024]{1,0:T(8,128)(2,1)S(1)} %constant_dynamic-update-slice_fusion.2.refs_1_, ...), custom_call_target="tpu_custom_call" | custom-call | flops 1073741824 | bytes 3670016 | tf_op jit(solution)/shard_map/block_work/pallas_call | solution.py:146
  15.7 3.2 %collective-permute-done.2.refs_0_.refs_2_ = bf16[136,1024]{1,0:T(8,128)(2,1)S(1)} collective-permute-done((bf16[136,1024]{1,0:T(8,128)(2,1)S(1)}, bf16[136,1024]{1,0:T(8,128)(2,1)S(1)}, u32[]{:S(2)}, u32[]{:S(2)}) %collective-permute-start.2) | collective-permute-done | bytes 278560 | tf_op jit(solution)/shard_map/ppermute | solution.py:263
  18.9 1.6 %collective-permute-start.6 = (bf16[136,1024]{1,0:T(8,128)(2,1)S(1)}, bf16[136,1024]{1,0:T(8,128)(2,1)S(1)}, u32[]{:S(2)}, u32[]{:S(2)}) collective-permute-start(bf16[136,1024]{1,0:T(8,128)(2,1)S(1)} %collective-permute-done.2.refs_0_.refs_2_), channel_id=1, source_target_pairs={{0,2},{2,4},{4,6},{6,7},{7,5},{5,3},{3,1},{1,0},{8,10},{10,12},{12... | collective-permute-start | bytes 835592 | tf_op jit(solution)/shard_map/ppermute | solution.py:263
  21.0 2.4 %block_work.5 = (bf16[128,1024]{1,0:T(8,128)(2,1)S(1)}, bf16[128,1024]{1,0:T(8,128)(2,1)S(1)}, bf16[128,1024]{1,0:T(8,128)(2,1)S(1)}, bf16[128,1024]{1,0:T(8,128...) custom-call(bf16[136,1024]{1,0:T(8,128)(2,1)S(1)} %collective-permute-done.2.refs_0_.refs_2_, ...), custom_call_target="tpu_custom_call" | custom-call | flops 1610612736 | bytes 4456448 | tf_op jit(solution)/shard_map/block_work/pallas_call | solution.py:146
  23.4 2.9 %collective-permute-done.6.refs_0_.refs_5_ = bf16[136,1024]{1,0:T(8,128)(2,1)S(1)} collective-permute-done((bf16[136,1024]{1,0:T(8,128)(2,1)S(1)}, bf16[136,1024]{1,0:T(8,128)(2,1)S(1)}, u32[]{:S(2)}, u32[]{:S(2)}) %collective-permute-start.6) | collective-permute-done | bytes 278560 | tf_op jit(solution)/shard_map/ppermute | solution.py:263
  26.3 1.6 %collective-permute-start.8 = (bf16[72,1024]{1,0:T(8,128)(2,1)S(1)}, bf16[72,1024]{1,0:T(8,128)(2,1)S(1)}, u32[]{:S(2)}, u32[]{:S(2)}) collective-permute-start(bf16[72,1024]{1,0:T(8,128)(2,1)S(1)} %pad_maximum_fusion.3), channel_id=1, source_target_pairs={{0,2},{2,4},{4,6},{6,7},{7,5},{5,3},{3,1},{1,0},{8,10},{10,12},{12... | collective-permute-start | bytes 442376 | tf_op jit(solution)/shard_map/ppermute | solution.py:263
  28.5 1.7 %block_work.6 = (bf16[128,1024]{1,0:T(8,128)(2,1)S(1)}, bf16[128,1024]{1,0:T(8,128)(2,1)S(1)}, bf16[128,1024]{1,0:T(8,128)(2,1)S(1)}, bf16[128,1024]{1,0:T(8,128)(2,1)S(1)}) custom-call(bf16[136,1024]{1,0:T(8,128)(2,1)S(1)} %collective-permute-done.6.refs_0_.refs_5_, bf16[136,1024]{1,0:T(8,128)(2,1)S(1)} %collective-permute-done.7.refs_1_.refs_6_, ...), custom_call_target="tpu_custom_call" | custom-call | flops 1073741824 | bytes 3670016 | tf_op jit(solution)/shard_map/block_work/pallas_call | solution.py:146
  30.2 1.3 %collective-permute-done.8.refs_0_.refs_7_ = bf16[72,1024]{1,0:T(8,128)(2,1)S(1)} collective-permute-done((bf16[72,1024]{1,0:T(8,128)(2,1)S(1)}, bf16[72,1024]{1,0:T(8,128)(2,1)S(1)}, u32[]{:S(2)}, u32[]{:S(2)}) %collective-permute-start.8) | collective-permute-done | bytes 147488 | tf_op jit(solution)/shard_map/ppermute | solution.py:263
  31.5 1.5 %collective-permute-done.9.refs_1_.refs_8_ = bf16[64,1024]{1,0:T(8,128)(2,1)S(1)} collective-permute-done((bf16[64,1024]{1,0:T(8,128)(2,1)S(1)}, bf16[64,1024]{1,0:T(8,128)(2,1)S(1)}, u32[]{:S(2)}, u32[]{:S(2)}) %collective-permute-start.9) | collective-permute-done | bytes 131104 | tf_op jit(solution)/shard_map/ppermute | solution.py:266
  33.0 1.2 %block_work.7 = (bf16[64,1024]{1,0:T(8,128)(2,1)S(1)}, bf16[64,1024]{1,0:T(8,128)(2,1)S(1)}, bf16[128,1024]{1,0:T(8,128)(2,1)S(1)}) custom-call(bf16[72,1024]{1,0:T(8,128)(2,1)S(1)} %collective-permute-done.8.refs_0_.refs_7_, bf16[64,1024]{1,0:T(8,128)(2,1)S(1)} %collective-permute-done.9.refs_1_.refs_8_, bf16[1024,1024]{1,0:T(8,128)(2,1)S(1)} %copy-done.1, ...), custom_call_target="tpu_custom_call" | custom-call | flops 536870912 | bytes 2883584 | tf_op jit(solution)/shard_map/block_work/pallas_call | solution.py:146
  34.2 1.6 %collective-permute-start.17 = (bf16[64,1024]{1,0:T(8,128)(2,1)S(1)}, bf16[64,1024]{1,0:T(8,128)(2,1)S(1)}, u32[]{:S(2)}, u32[]{:S(2)}) collective-permute-start(bf16[64,1024]{1,0:T(8,128)(2,1)S(1)} %get-tuple-element.59), channel_id=1, source_target_pairs={{0,2},{2,4},{4,6},{6,7},{7,5},{5,3},{3,1},{1,0},{8,10},{10,12},{12... | collective-permute-start | bytes 393224 | tf_op jit(solution)/shard_map/ppermute | solution.py:263
  36.3 2.4 %weight_work.1 = (bf16[1024,256]{1,0:T(8,128)(2,1)S(1)}, bf16[1024,256]{1,0:T(8,128)(2,1)S(1)}, bf16[1024,256]{1,0:T(8,128)(2,1)S(1)}, bf16[1024,256]{1,0:T(8,128)(2,1)S(1)}) custom-call(bf16[136,1024]{1,0:T(8,128)(2,1)S(1)} %constant_dynamic-update-slice_fusion.refs_0_, bf16[136,1024]{1,0:T(8,128)(2,1)S(1)} %constant_dynamic-update-slice_fusion.2.refs_1_, ...), custom_call_target="tpu_custom_call" | custom-call | flops 2147483648 | bytes 4718592 | tf_op jit(solution)/shard_map/weight_work/pallas_call | solution.py:188
  39.3 1.6 %collective-permute-start.18 = (bf16[128,1024]{1,0:T(8,128)(2,1)S(1)}, bf16[128,1024]{1,0:T(8,128)(2,1)S(1)}, u32[]{:S(2)}, u32[]{:S(2)}) collective-permute-start(bf16[128,1024]{1,0:T(8,128)(2,1)S(1)} %pad_maximum_fusion.2), channel_id=1, source_target_pairs={{0,2},{2,4},{4,6},{6,7},{7,5},{5,3},{3,1},{1,0},{8,10},{10,12},{12... | collective-permute-start | bytes 786440 | tf_op jit(solution)/shard_map/ppermute | solution.py:263
  41.0 0.5 collective-permute-start.14
  41.5 6.1 %collective-permute-done.18 = bf16[128,1024]{1,0:T(8,128)(2,1)S(1)} collective-permute-done((bf16[128,1024]{1,0:T(8,128)(2,1)S(1)}, bf16[128,1024]{1,0:T(8,128)(2,1)S(1)}, u32[]{:S(2)}, u32[]{:S(2)}) %collective-permute-start.18) | collective-permute-done | bytes 262176 | tf_op jit(solution)/shard_map/ppermute | solution.py:263
  47.6 1.6 %collective-permute-start.19 = (bf16[128,1024]{1,0:T(8,128)(2,1)S(1)}, bf16[128,1024]{1,0:T(8,128)(2,1)S(1)}, u32[]{:S(2)}, u32[]{:S(2)}) collective-permute-start(bf16[128,1024]{1,0:T(8,128)(2,1)S(1)} %add_convert_fusion.2), channel_id=1, source_target_pairs={{0,2},{2,4},{4,6},{6,7},{7,5},{5,3},{3,1},{1,0},{8,10},{10,12},{12... | collective-permute-start | bytes 786440 | tf_op jit(solution)/shard_map/ppermute | solution.py:263
  50.0 1.6 %collective-permute-start.12 = (bf16[1024,256]{1,0:T(8,128)(2,1)S(1)}, bf16[1024,256]{1,0:T(8,128)(2,1)S(1)}, u32[]{:S(2)}, u32[]{:S(2)}) collective-permute-start(bf16[1024,256]{1,0:T(8,128)(2,1)S(1)} %add_convert_fusion), channel_id=1, source_target_pairs={{0,16},{8,24},{16,0},{24,8},{1,17},{9,25},{17,1},{25,9},{2,18},{10... | collective-permute-start | bytes 1572872 | tf_op jit(solution)/shard_map/ppermute | solution.py:303
  51.5 3.5 %collective-permute-done.19 = bf16[128,1024]{1,0:T(8,128)(2,1)S(1)} collective-permute-done((bf16[128,1024]{1,0:T(8,128)(2,1)S(1)}, bf16[128,1024]{1,0:T(8,128)(2,1)S(1)}, u32[]{:S(2)}, u32[]{:S(2)}) %collective-permute-start.19) | collective-permute-done | bytes 262176 | tf_op jit(solution)/shard_map/ppermute | solution.py:263
  55.1 1.6 %collective-permute-start.20 = (bf16[128,1024]{1,0:T(8,128)(2,1)S(1)}, bf16[128,1024]{1,0:T(8,128)(2,1)S(1)}, u32[]{:S(2)}, u32[]{:S(2)}) collective-permute-start(bf16[128,1024]{1,0:T(8,128)(2,1)S(1)} %add_convert_fusion.1), channel_id=1, source_target_pairs={{0,2},{2,4},{4,6},{6,7},{7,5},{5,3},{3,1},{1,0},{8,10},{10,12},{12... | collective-permute-start | bytes 786440 | tf_op jit(solution)/shard_map/ppermute | solution.py:263
  56.8 0.5 collective-permute-start.16
  57.3 5.1 %collective-permute-done.12.refs_2_ = bf16[1024,256]{1,0:T(8,128)(2,1)S(1)} collective-permute-done((bf16[1024,256]{1,0:T(8,128)(2,1)S(1)}, bf16[1024,256]{1,0:T(8,128)(2,1)S(1)}, u32[]{:S(2)}, u32[]{:S(2)}) %collective-permute-start.12) | collective-permute-done | bytes 524320 | tf_op jit(solution)/shard_map/ppermute | solution.py:303
  62.5 0.9 %final_sum.2 = bf16[1024,256]{1,0:T(8,128)(2,1)} custom-call(bf16[1024,256]{1,0:T(8,128)(2,1)S(1)} %get-tuple-element.50.refs_0_, bf16[1024,256]{1,0:T(8,128)(2,1)S(1)} %collective-permute-done.10.refs_1_, bf16[1024,256]{1,0:T(8,128)(2,1)S(1)} %collective-permute-done.12.refs_2_), custom_call_target="tpu_custom_call" | custom-call | flops 786432 | bytes 2097152 | tf_op jit(solution)/shard_map/final_sum/pallas_call | solution.py:227
  63.4 0.8 %final_sum.3 = bf16[128,1024]{1,0:T(8,128)(2,1)} custom-call(bf16[128,1024]{1,0:T(8,128)(2,1)S(1)} %get-tuple-element.54.refs_0_, bf16[128,1024]{1,0:T(8,128)(2,1)S(1)} %collective-permute-done.16.refs_1_, bf16[128,1024]{1,0:T(8,128)(2,1)S(1)} %collective-permute-done.20.refs_2_), custom_call_target="tpu_custom_call" | custom-call | flops 393216 | bytes 1048576 | tf_op jit(solution)/shard_map/final_sum/pallas_call | solution.py:227
  (51 shorter events, 4.0 us)
Async XLA Ops:
  0.6 9.7 %collective-permute-start = (bf16[128,1024]{1,0:T(8,128)(2,1)}, bf16[128,1024]{1,0:T(8,128)(2,1)S(1)}, u32[]{:S(2)}, u32[]{:S(2)}) collective-permute-start(bf16[128,1024]{1,0:T(8,128)(2,1)} %param.5), channel_id=1, source_target_pairs={{0,2},{2,4},{4,6},{6,7},{7,5},{5,3},{3,1},{1,0},{8,10},{10,12},{12... | collective-permute-start | bytes 786440 | tf_op jit(solution)/shard_map/ppermute | solution.py:263
  3.7 8.2 %collective-permute-start.3 = (bf16[128,1024]{1,0:T(8,128)(2,1)}, bf16[128,1024]{1,0:T(8,128)(2,1)S(1)}, u32[]{:S(2)}, u32[]{:S(2)}) collective-permute-start(bf16[128,1024]{1,0:T(8,128)(2,1)} %param.5), channel_id=1, source_target_pairs={{2,0},{4,2},{6,4},{7,6},{5,7},{3,5},{1,3},{0,1},{10,8},{12,10},{14... | collective-permute-start | bytes 786440 | tf_op jit(solution)/shard_map/ppermute | solution.py:266
  3.7 0.7 %copy-start.2 = (s32[128,16]{0,1:T(8,128)S(1)}, s32[128,16]{0,1:T(8,128)}, u32[]{:S(2)}) copy-start(s32[128,16]{0,1:T(8,128)} %param.6) | copy-start | bytes 24580
  4.4 0.7 %copy-start.3 = (s32[128,4]{0,1:T(4,128)S(1)}, s32[128,4]{0,1:T(4,128)}, u32[]{:S(2)}) copy-start(s32[128,4]{0,1:T(4,128)} %param.7) | copy-start | bytes 6148
  5.1 6.7 %collective-permute-start.1 = (bf16[8,1024]{1,0:T(8,128)(2,1)S(1)}, bf16[8,1024]{1,0:T(8,128)(2,1)S(1)}, u32[]{:S(2)}, u32[]{:S(2)}) collective-permute-start(bf16[8,1024]{1,0:T(8,128)(2,1)S(1)} %instance_ids.1), channel_id=1, source_target_pairs={{0,2},{2,4},{4,6},{6,7},{7,5},{5,3},{3,1},{1,0},{8,10},{10,12},{12... | collective-permute-start | bytes 49160 | tf_op jit(solution)/shard_map/ppermute | solution.py:263
  7.2 6.3 %collective-permute-start.4 = (bf16[8,1024]{1,0:T(8,128)(2,1)S(1)}, bf16[8,1024]{1,0:T(8,128)(2,1)S(1)}, u32[]{:S(2)}, u32[]{:S(2)}) collective-permute-start(bf16[8,1024]{1,0:T(8,128)(2,1)S(1)} %instance_ids.1), channel_id=1, source_target_pairs={{2,0},{4,2},{6,4},{7,6},{5,7},{3,5},{1,3},{0,1},{10,8},{12,10},{14... | collective-permute-start | bytes 49160 | tf_op jit(solution)/shard_map/ppermute | solution.py:266
  7.2 1.6 %copy-start = (bf16[1024,1024]{1,0:T(8,128)(2,1)S(1)}, bf16[1024,1024]{1,0:T(8,128)(2,1)}, u32[]{:S(2)}) copy-start(bf16[1024,1024]{1,0:T(8,128)(2,1)} %refs_2_.5) | copy-start | bytes 6291460
  8.8 0.7 %copy-start.4 = (s32[8]{0:T(128)S(1)}, s32[8]{0:T(128)}, u32[]{:S(2)}) copy-start(s32[8]{0:T(128)} %size_ref.1) | copy-start | bytes 100
  9.4 4.6 %copy-start.1 = (bf16[1024,1024]{1,0:T(8,128)(2,1)S(1)}, bf16[1024,1024]{1,0:T(8,128)(2,1)}, u32[]{:S(2)}) copy-start(bf16[1024,1024]{1,0:T(8,128)(2,1)} %refs_2_.5) | copy-start | bytes 6291460
  11.9 7.0 %collective-permute-start.2 = (bf16[136,1024]{1,0:T(8,128)(2,1)S(1)}, bf16[136,1024]{1,0:T(8,128)(2,1)S(1)}, u32[]{:S(2)}, u32[]{:S(2)}) collective-permute-start(bf16[136,1024]{1,0:T(8,128)(2,1)S(1)} %constant_dynamic-update-slice_fusion.refs_0_), channel_id=1, source_target_pairs={{0,2},{2,4},{4,6},{6,7},{7,5},{5,3},{3,1},{1,0},{8,10},{10,12},{12... | collective-permute-start | bytes 835592 | tf_op jit(solution)/shard_map/ppermute | solution.py:263
  13.5 7.0 %copy-start.5 = (bf16[128,1024]{1,0:T(8,128)(2,1)S(1)}, bf16[128,1024]{1,0:T(8,128)(2,1)}, u32[]{:S(2)}) copy-start(bf16[128,1024]{1,0:T(8,128)(2,1)} %param.5) | copy-start | bytes 786436
  13.5 7.0 %collective-permute-start.5 = (bf16[136,1024]{1,0:T(8,128)(2,1)S(1)}, bf16[136,1024]{1,0:T(8,128)(2,1)S(1)}, u32[]{:S(2)}, u32[]{:S(2)}) collective-permute-start(bf16[136,1024]{1,0:T(8,128)(2,1)S(1)} %constant_dynamic-update-slice_fusion.2.refs_1_), channel_id=1, source_target_pairs={{2,0},{4,2},{6,4},{7,6},{5,7},{3,5},{1,3},{0,1},{10,8},{12,10},{14... | collective-permute-start | bytes 835592 | tf_op jit(solution)/shard_map/ppermute | solution.py:266
  18.9 7.4 %collective-permute-start.6 = (bf16[136,1024]{1,0:T(8,128)(2,1)S(1)}, bf16[136,1024]{1,0:T(8,128)(2,1)S(1)}, u32[]{:S(2)}, u32[]{:S(2)}) collective-permute-start(bf16[136,1024]{1,0:T(8,128)(2,1)S(1)} %collective-permute-done.2.refs_0_.refs_2_), channel_id=1, source_target_pairs={{0,2},{2,4},{4,6},{6,7},{7,5},{5,3},{3,1},{1,0},{8,10},{10,12},{12... | collective-permute-start | bytes 835592 | tf_op jit(solution)/shard_map/ppermute | solution.py:263
  20.5 7.5 %collective-permute-start.7 = (bf16[136,1024]{1,0:T(8,128)(2,1)S(1)}, bf16[136,1024]{1,0:T(8,128)(2,1)S(1)}, u32[]{:S(2)}, u32[]{:S(2)}) collective-permute-start(bf16[136,1024]{1,0:T(8,128)(2,1)S(1)} %collective-permute-done.5.refs_1_.refs_3_), channel_id=1, source_target_pairs={{2,0},{4,2},{6,4},{7,6},{5,7},{3,5},{1,3},{0,1},{10,8},{12,10},{14... | collective-permute-start | bytes 835592 | tf_op jit(solution)/shard_map/ppermute | solution.py:266
  26.3 5.2 %collective-permute-start.8 = (bf16[72,1024]{1,0:T(8,128)(2,1)S(1)}, bf16[72,1024]{1,0:T(8,128)(2,1)S(1)}, u32[]{:S(2)}, u32[]{:S(2)}) collective-permute-start(bf16[72,1024]{1,0:T(8,128)(2,1)S(1)} %pad_maximum_fusion.3), channel_id=1, source_target_pairs={{0,2},{2,4},{4,6},{6,7},{7,5},{5,3},{3,1},{1,0},{8,10},{10,12},{12... | collective-permute-start | bytes 442376 | tf_op jit(solution)/shard_map/ppermute | solution.py:263
  28.0 5.0 %collective-permute-start.9 = (bf16[64,1024]{1,0:T(8,128)(2,1)S(1)}, bf16[64,1024]{1,0:T(8,128)(2,1)S(1)}, u32[]{:S(2)}, u32[]{:S(2)}) collective-permute-start(bf16[64,1024]{1,0:T(8,128)(2,1)S(1)} %slice.23), channel_id=1, source_target_pairs={{2,0},{4,2},{6,4},{7,6},{5,7},{3,5},{1,3},{0,1},{10,8},{12,10},{14... | collective-permute-start | bytes 393224 | tf_op jit(solution)/shard_map/ppermute | solution.py:266
  34.2 5.0 %collective-permute-start.17 = (bf16[64,1024]{1,0:T(8,128)(2,1)S(1)}, bf16[64,1024]{1,0:T(8,128)(2,1)S(1)}, u32[]{:S(2)}, u32[]{:S(2)}) collective-permute-start(bf16[64,1024]{1,0:T(8,128)(2,1)S(1)} %get-tuple-element.59), channel_id=1, source_target_pairs={{0,2},{2,4},{4,6},{6,7},{7,5},{5,3},{3,1},{1,0},{8,10},{10,12},{12... | collective-permute-start | bytes 393224 | tf_op jit(solution)/shard_map/ppermute | solution.py:263
  35.8 5.1 %collective-permute-start.13 = (bf16[64,1024]{1,0:T(8,128)(2,1)S(1)}, bf16[64,1024]{1,0:T(8,128)(2,1)S(1)}, u32[]{:S(2)}, u32[]{:S(2)}) collective-permute-start(bf16[64,1024]{1,0:T(8,128)(2,1)S(1)} %get-tuple-element.55), channel_id=1, source_target_pairs={{2,0},{4,2},{6,4},{7,6},{5,7},{3,5},{1,3},{0,1},{10,8},{12,10},{14... | collective-permute-start | bytes 393224 | tf_op jit(solution)/shard_map/ppermute | solution.py:266
  38.7 11.2 %collective-permute-start.11 = (bf16[1024,256]{1,0:T(8,128)(2,1)S(1)}, bf16[1024,256]{1,0:T(8,128)(2,1)S(1)}, u32[]{:S(2)}, u32[]{:S(2)}) collective-permute-start(bf16[1024,256]{1,0:T(8,128)(2,1)S(1)} %get-tuple-element.53), channel_id=1, source_target_pairs={{0,8},{8,0},{16,24},{24,16},{1,9},{9,1},{17,25},{25,17},{2,10},{10... | collective-permute-start | bytes 1572872 | tf_op jit(solution)/shard_map/ppermute | solution.py:303
  39.3 8.3 %collective-permute-start.18 = (bf16[128,1024]{1,0:T(8,128)(2,1)S(1)}, bf16[128,1024]{1,0:T(8,128)(2,1)S(1)}, u32[]{:S(2)}, u32[]{:S(2)}) collective-permute-start(bf16[128,1024]{1,0:T(8,128)(2,1)S(1)} %pad_maximum_fusion.2), channel_id=1, source_target_pairs={{0,2},{2,4},{4,6},{6,7},{7,5},{5,3},{3,1},{1,0},{8,10},{10,12},{12... | collective-permute-start | bytes 786440 | tf_op jit(solution)/shard_map/ppermute | solution.py:263
  41.0 8.3 %collective-permute-start.14 = (bf16[128,1024]{1,0:T(8,128)(2,1)S(1)}, bf16[128,1024]{1,0:T(8,128)(2,1)S(1)}, u32[]{:S(2)}, u32[]{:S(2)}) collective-permute-start(bf16[128,1024]{1,0:T(8,128)(2,1)S(1)} %pad_maximum_fusion.1), channel_id=1, source_target_pairs={{2,0},{4,2},{6,4},{7,6},{5,7},{3,5},{1,3},{0,1},{10,8},{12,10},{14... | collective-permute-start | bytes 786440 | tf_op jit(solution)/shard_map/ppermute | solution.py:266
  41.5 15.8 %collective-permute-start.10 = (bf16[1024,256]{1,0:T(8,128)(2,1)S(1)}, bf16[1024,256]{1,0:T(8,128)(2,1)S(1)}, u32[]{:S(2)}, u32[]{:S(2)}) collective-permute-start(bf16[1024,256]{1,0:T(8,128)(2,1)S(1)} %get-tuple-element.51), channel_id=1, source_target_pairs={{0,8},{8,0},{16,24},{24,16},{1,9},{9,1},{17,25},{25,17},{2,10},{10... | collective-permute-start | bytes 1572872 | tf_op jit(solution)/shard_map/ppermute | solution.py:303
  47.6 7.4 %collective-permute-start.19 = (bf16[128,1024]{1,0:T(8,128)(2,1)S(1)}, bf16[128,1024]{1,0:T(8,128)(2,1)S(1)}, u32[]{:S(2)}, u32[]{:S(2)}) collective-permute-start(bf16[128,1024]{1,0:T(8,128)(2,1)S(1)} %add_convert_fusion.2), channel_id=1, source_target_pairs={{0,2},{2,4},{4,6},{6,7},{7,5},{5,3},{3,1},{1,0},{8,10},{10,12},{12... | collective-permute-start | bytes 786440 | tf_op jit(solution)/shard_map/ppermute | solution.py:263
  49.3 7.4 %collective-permute-start.15 = (bf16[128,1024]{1,0:T(8,128)(2,1)S(1)}, bf16[128,1024]{1,0:T(8,128)(2,1)S(1)}, u32[]{:S(2)}, u32[]{:S(2)}) collective-permute-start(bf16[128,1024]{1,0:T(8,128)(2,1)S(1)} %add_convert_fusion.4), channel_id=1, source_target_pairs={{2,0},{4,2},{6,4},{7,6},{5,7},{3,5},{1,3},{0,1},{10,8},{12,10},{14... | collective-permute-start | bytes 786440 | tf_op jit(solution)/shard_map/ppermute | solution.py:266
  50.0 12.5 %collective-permute-start.12 = (bf16[1024,256]{1,0:T(8,128)(2,1)S(1)}, bf16[1024,256]{1,0:T(8,128)(2,1)S(1)}, u32[]{:S(2)}, u32[]{:S(2)}) collective-permute-start(bf16[1024,256]{1,0:T(8,128)(2,1)S(1)} %add_convert_fusion), channel_id=1, source_target_pairs={{0,16},{8,24},{16,0},{24,8},{1,17},{9,25},{17,1},{25,9},{2,18},{10... | collective-permute-start | bytes 1572872 | tf_op jit(solution)/shard_map/ppermute | solution.py:303
  55.1 8.2 %collective-permute-start.20 = (bf16[128,1024]{1,0:T(8,128)(2,1)S(1)}, bf16[128,1024]{1,0:T(8,128)(2,1)S(1)}, u32[]{:S(2)}, u32[]{:S(2)}) collective-permute-start(bf16[128,1024]{1,0:T(8,128)(2,1)S(1)} %add_convert_fusion.1), channel_id=1, source_target_pairs={{0,2},{2,4},{4,6},{6,7},{7,5},{5,3},{3,1},{1,0},{8,10},{10,12},{12... | collective-permute-start | bytes 786440 | tf_op jit(solution)/shard_map/ppermute | solution.py:263
  56.8 6.5 %collective-permute-start.16 = (bf16[128,1024]{1,0:T(8,128)(2,1)S(1)}, bf16[128,1024]{1,0:T(8,128)(2,1)S(1)}, u32[]{:S(2)}, u32[]{:S(2)}) collective-permute-start(bf16[128,1024]{1,0:T(8,128)(2,1)S(1)} %add_convert_fusion.3), channel_id=1, source_target_pairs={{2,0},{4,2},{6,4},{7,6},{5,7},{3,5},{1,3},{0,1},{10,8},{12,10},{14... | collective-permute-start | bytes 786440 | tf_op jit(solution)/shard_map/ppermute | solution.py:266

commit v13 on v12

--- a/solution.py
+++ b/solution.py
@@ -206,41 +206,67 @@
     return total.astype(jnp.bfloat16)
 
 
-def sum_kernel(pieces, *refs):
-    *in_refs, out_ref, held, sems = refs
-    rows = out_ref.shape[0] // pieces
-    copies = []
+def total_of(refs, at):
+    total = refs[0][at, :].astype(jnp.float32)
+    for ref in refs[1:]:
+        total = total + ref[at, :].astype(jnp.float32)
+    return total.astype(jnp.bfloat16)
+
+
+def sum_kernel(*refs):
+    *in_refs, out_ref = refs
+    out_ref[...] = total_of(in_refs, slice(None))
+
+
+def weight_sum(parts):
+    return pl.pallas_call(
+        sum_kernel,
+        out_shape=jax.ShapeDtypeStruct(parts[0].shape, jnp.bfloat16),
+        in_specs=[pl.BlockSpec(memory_space=pltpu.VMEM)] * len(parts),
+        compiler_params=pltpu.CompilerParams(vmem_limit_bytes=VMEM_LIMIT),
+        cost_estimate=pl.CostEstimate(
+            flops=4_000_000_000, bytes_accessed=2 * (len(parts) + 1) * parts[0].size, transcendentals=0
+        ),
+        name="weight_sum",
+    )(*parts)
+
+
+def final_kernel(pieces, weight_ref, *refs):
+    *in_refs, feature_out, weight_out, held, sems = refs
+    copies = [pltpu.make_async_copy(weight_ref, weight_out, sems.at[pieces])]
+    copies[0].start()
+    rows = held.shape[0] // pieces
     for p in range(pieces):
         at = pl.ds(p * rows, rows)
-        total = in_refs[0][at, :].astype(jnp.float32)
-        for ref in in_refs[1:]:
-            total = total + ref[at, :].astype(jnp.float32)
-        held[at, :] = total.astype(jnp.bfloat16)
-        copies.append(pltpu.make_async_copy(held.at[at], out_ref.at[at], sems.at[p]))
+        held[at, :] = total_of(in_refs, at)
+        copies.append(pltpu.make_async_copy(held.at[at], feature_out.at[at], sems.at[p]))
         copies[-1].start()
     for copy in copies:
         copy.wait()
 
 
-def final_sum(parts, pieces):
+def finish(weight_grad, parts, pieces):
     shape = parts[0].shape
     return pl.pallas_call(
-        functools.partial(sum_kernel, pieces),
-        out_shape=jax.ShapeDtypeStruct(shape, jnp.bfloat16),
-        in_specs=[pl.BlockSpec(memory_space=pltpu.VMEM)] * len(parts),
-        out_specs=pl.BlockSpec(memory_space=pl.ANY),
+        functools.partial(final_kernel, pieces),
+        out_shape=[
+            jax.ShapeDtypeStruct(shape, jnp.bfloat16),
+            jax.ShapeDtypeStruct(weight_grad.shape, jnp.bfloat16),
+        ],
+        in_specs=[pl.BlockSpec(memory_space=pltpu.VMEM)] * (len(parts) + 1),
+        out_specs=[pl.BlockSpec(memory_space=pl.ANY)] * 2,
         scratch_shapes=[
             pltpu.VMEM(shape, jnp.bfloat16),
-            pltpu.SemaphoreType.DMA((pieces,)),
+            pltpu.SemaphoreType.DMA((pieces + 1,)),
         ],
         compiler_params=pltpu.CompilerParams(vmem_limit_bytes=VMEM_LIMIT),
         cost_estimate=pl.CostEstimate(
             flops=len(parts) * parts[0].size,
-            bytes_accessed=2 * (len(parts) + 1) * parts[0].size,
+            bytes_accessed=2 * (len(parts) + 1) * parts[0].size + 4 * weight_grad.size,
             transcendentals=0,
         ),
-        name="final_sum",
-    )(*parts)
+        name="finish",
+    )(weight_grad, *parts)
 
 
 def after(array, *others):
@@ -253,7 +279,7 @@
     clus_count, seq_count = lax.axis_size("clus"), lax.axis_size("seq")
     local_count = cluster_sizes.shape[0]
     part_width = width // seq_count
-    half, steps = inst_rows // 2, clus_count // 2
+    split, steps = inst_rows * 5 // 8, clus_count // 2
 
     ring = list(range(0, clus_count, 2)) + list(range(1, clus_count, 2))[::-1]
     up = list(zip(ring, ring[1:] + ring[:1]))
@@ -288,8 +314,8 @@
         if k < steps:
             arriving = send_up(below), send_down(above)
         else:
-            ends = jnp.concatenate([below[:half], below[inst_rows:]], axis=0)
-            arriving = send_up(ends), send_down(above[half:inst_rows])
+            ends = jnp.concatenate([below[:split], below[inst_rows:]], axis=0)
+            arriving = send_up(ends), send_down(above[split:inst_rows])
         if k == 3 or steps < 3:
             below_grad[k - 1], above_grad[k - 1], own_grad = take([below], [above], [own])
         else:
@@ -316,12 +342,11 @@
         from_above, from_below = send_down(to_down), send_up(to_up)
         if k == steps:
             near_below, near_above = below_grad[k - 1], above_grad[k - 1]
-            to_down = jnp.concatenate([add(near_below[:half], from_above), near_below[half:]], axis=0)
-            to_up = jnp.concatenate([near_above[:half], add(near_above[half:], from_below)], axis=0)
+            to_down = jnp.concatenate([add(near_below[:split], from_above), near_below[split:]], axis=0)
+            to_up = jnp.concatenate([near_above[:split], add(near_above[split:], from_below)], axis=0)
         elif k > 1:
             to_down, to_up = add(below_grad[k - 1], from_above), add(above_grad[k - 1], from_below)
-    weight_grad = final_sum(terms[0], 4)
-    feature_grad = final_sum([after(own_grad, weight_grad), from_above, from_below], 4)
+    feature_grad, weight_grad = finish(weight_sum(terms[0]), [own_grad, from_above, from_below], 2)
     return (feature_grad, weight_grad)
 
 

time: 64.4 us -> 65.3 us (1.014)
  waiting for transfers between devices: 25.9 us -> 26.9 us
    ppermute x9, waiting for transfers between devices: 2.99 us -> 5.68 us  [send_down(): return lax.ppermute(array, 'clus', down)]
    ppermute x3, waiting for transfers between devices: 5.14 us -> 3.7 us  [seq_send(): return lax.ppermute(array, 'seq', [(k, k ^ bit) for k in range(seq_count)])]
  transfers between devices with their start and end apart: 21 -> 21, of which waited for: 10 -> 12; matrix products, arithmetic and copies ran while one was open for 1% -> 1% of each run, Pallas kernels for 15% -> 14%
where the time goes in v13:
time: 65.3 us; the launch traced here: 65.1 us
  waiting for transfers between devices  26.9 us (41%)
  starting transfers between devices  22 us (34%)
  Pallas kernels  11 us (17%)
  local copies, waits for them, and re-layouts  3.72 us (6%)
  between operations  0.85 us (1%)
    ppermute x9, waiting for transfers between devices, send_up(): return lax.ppermute(array, 'clus', up)  17.5 us
    ppermute x9, starting transfers between devices, send_up(): return lax.ppermute(array, 'clus', up)  16.4 us
    pallas_call x4, Pallas kernels, block_work(): pl.pallas_call(functools.partial(block_kernel, piece_rows, top_count, pos...  6.97 us
    ppermute x9, waiting for transfers between devices, send_down(): return lax.ppermute(array, 'clus', down)  5.68 us
    ppermute x3, waiting for transfers between devices, seq_send(): return lax.ppermute(array, 'seq', [(k, k ^ bit) for k in range(seq_count)])  3.7 us
    unnamed x14, local copies, waits for them, and re-layouts  3.67 us
    ppermute x9, starting transfers between devices, send_down(): return lax.ppermute(array, 'clus', down)  3.48 us
    pallas_call x1, Pallas kernels, weight_work(): pl.pallas_call(functools.partial(weight_kernel, piece_rows, column_blocks...  2.37 us
  transfers between devices with their start and end apart: 21, of which 12 were waited for; matrix products, arithmetic and copies ran while one was open for 1% of the time, Pallas kernels for 14%

profile of v13, /device:TPU:0, one launch (start us, length us, event | category | flops | bytes accessed | tf_op | source)
XLA Modules:
  0.0 65.1 jit_solution(10488486057774859057)
XLA Ops:
  0.6 3.1 %collective-permute-start = (bf16[128,1024]{1,0:T(8,128)(2,1)}, bf16[128,1024]{1,0:T(8,128)(2,1)S(1)}, u32[]{:S(2)}, u32[]{:S(2)}) collective-permute-start(bf16[128,1024]{1,0:T(8,128)(2,1)} %param.5), channel_id=1, source_target_pairs={{0,2},{2,4},{4,6},{6,7},{7,5},{5,3},{3,1},{1,0},{8,10},{10,12},{12... | collective-permute-start | bytes 786440 | tf_op jit(solution)/shard_map/ppermute | solution.py:289
  3.7 0.7 %copy-done.2 = s32[128,16]{0,1:T(8,128)S(1)} copy-done((s32[128,16]{0,1:T(8,128)S(1)}, s32[128,16]{0,1:T(8,128)}, u32[]{:S(2)}) %copy-start.2) | copy-done | bytes 8216
  4.4 0.7 %copy-done.3 = s32[128,4]{0,1:T(4,128)S(1)} copy-done((s32[128,4]{0,1:T(4,128)S(1)}, s32[128,4]{0,1:T(4,128)}, u32[]{:S(2)}) %copy-start.3) | copy-done | bytes 2072
  5.1 2.1 %collective-permute-start.1 = (bf16[8,1024]{1,0:T(8,128)(2,1)S(1)}, bf16[8,1024]{1,0:T(8,128)(2,1)S(1)}, u32[]{:S(2)}, u32[]{:S(2)}) collective-permute-start(bf16[8,1024]{1,0:T(8,128)(2,1)S(1)} %instance_ids.1), channel_id=1, source_target_pairs={{0,2},{2,4},{4,6},{6,7},{7,5},{5,3},{3,1},{1,0},{8,10},{10,12},{12... | collective-permute-start | bytes 49160 | tf_op jit(solution)/shard_map/ppermute | solution.py:289
  7.2 1.6 %copy-done = bf16[1024,1024]{1,0:T(8,128)(2,1)S(1)} copy-done((bf16[1024,1024]{1,0:T(8,128)(2,1)S(1)}, bf16[1024,1024]{1,0:T(8,128)(2,1)}, u32[]{:S(2)}) %copy-start) | copy-done | bytes 2097176
  8.8 0.7 %copy-done.4 = s32[8]{0:T(128)S(1)} copy-done((s32[8]{0:T(128)S(1)}, s32[8]{0:T(128)}, u32[]{:S(2)}) %copy-start.4) | copy-done | bytes 56
  9.5 0.6 live_labels.1.refs_3_.refs_4_
  10.4 1.5 %collective-permute-done.2 = bf16[128,1024]{1,0:T(8,128)(2,1)S(1)} collective-permute-done((bf16[128,1024]{1,0:T(8,128)(2,1)}, bf16[128,1024]{1,0:T(8,128)(2,1)S(1)}, u32[]{:S(2)}, u32[]{:S(2)}) %collective-permute-start.2) | collective-permute-done | bytes 262176 | tf_op jit(solution)/shard_map/ppermute | solution.py:292
  11.9 1.6 %collective-permute-start.4 = (bf16[136,1024]{1,0:T(8,128)(2,1)S(1)}, bf16[136,1024]{1,0:T(8,128)(2,1)S(1)}, u32[]{:S(2)}, u32[]{:S(2)}) collective-permute-start(bf16[136,1024]{1,0:T(8,128)(2,1)S(1)} %constant_dynamic-update-slice_fusion.refs_0_), channel_id=1, source_target_pairs={{0,2},{2,4},{4,6},{6,7},{7,5},{5,3},{3,1},{1,0},{8,10},{10,12},{12... | collective-permute-start | bytes 835592 | tf_op jit(solution)/shard_map/ppermute | solution.py:289
  14.0 1.7 %block_work.4 = (bf16[128,1024]{1,0:T(8,128)(2,1)S(1)}, bf16[128,1024]{1,0:T(8,128)(2,1)S(1)}, bf16[128,1024]{1,0:T(8,128)(2,1)S(1)}, bf16[128,1024]{1,0:T(8,128)(2,1)S(1)}) custom-call(bf16[136,1024]{1,0:T(8,128)(2,1)S(1)} %constant_dynamic-update-slice_fusion.refs_0_, bf16[136,1024]{1,0:T(8,128)(2,1)S(1)} %constant_dynamic-update-slice_fusion.2.refs_1_, ...), custom_call_target="tpu_custom_call" | custom-call | flops 1073741824 | bytes 3670016 | tf_op jit(solution)/shard_map/block_work/pallas_call | solution.py:146
  15.7 3.2 %collective-permute-done.4.refs_0_.refs_2_ = bf16[136,1024]{1,0:T(8,128)(2,1)S(1)} collective-permute-done((bf16[136,1024]{1,0:T(8,128)(2,1)S(1)}, bf16[136,1024]{1,0:T(8,128)(2,1)S(1)}, u32[]{:S(2)}, u32[]{:S(2)}) %collective-permute-start.4) | collective-permute-done | bytes 278560 | tf_op jit(solution)/shard_map/ppermute | solution.py:289
  18.9 1.6 %collective-permute-start.6 = (bf16[136,1024]{1,0:T(8,128)(2,1)S(1)}, bf16[136,1024]{1,0:T(8,128)(2,1)S(1)}, u32[]{:S(2)}, u32[]{:S(2)}) collective-permute-start(bf16[136,1024]{1,0:T(8,128)(2,1)S(1)} %collective-permute-done.4.refs_0_.refs_2_), channel_id=1, source_target_pairs={{0,2},{2,4},{4,6},{6,7},{7,5},{5,3},{3,1},{1,0},{8,10},{10,12},{12... | collective-permute-start | bytes 835592 | tf_op jit(solution)/shard_map/ppermute | solution.py:289
  21.0 2.4 %block_work.5 = (bf16[128,1024]{1,0:T(8,128)(2,1)S(1)}, bf16[128,1024]{1,0:T(8,128)(2,1)S(1)}, bf16[128,1024]{1,0:T(8,128)(2,1)S(1)}, bf16[128,1024]{1,0:T(8,128...) custom-call(bf16[136,1024]{1,0:T(8,128)(2,1)S(1)} %collective-permute-done.4.refs_0_.refs_2_, ...), custom_call_target="tpu_custom_call" | custom-call | flops 1610612736 | bytes 4456448 | tf_op jit(solution)/shard_map/block_work/pallas_call | solution.py:146
  23.4 2.9 %collective-permute-done.6.refs_0_.refs_5_ = bf16[136,1024]{1,0:T(8,128)(2,1)S(1)} collective-permute-done((bf16[136,1024]{1,0:T(8,128)(2,1)S(1)}, bf16[136,1024]{1,0:T(8,128)(2,1)S(1)}, u32[]{:S(2)}, u32[]{:S(2)}) %collective-permute-start.6) | collective-permute-done | bytes 278560 | tf_op jit(solution)/shard_map/ppermute | solution.py:289
  26.3 1.6 %collective-permute-start.8 = (bf16[88,1024]{1,0:T(8,128)(2,1)S(1)}, bf16[88,1024]{1,0:T(8,128)(2,1)S(1)}, u32[]{:S(2)}, u32[]{:S(2)}) collective-permute-start(bf16[88,1024]{1,0:T(8,128)(2,1)S(1)} %pad_maximum_fusion.3), channel_id=1, source_target_pairs={{0,2},{2,4},{4,6},{6,7},{7,5},{5,3},{3,1},{1,0},{8,10},{10,12},{12... | collective-permute-start | bytes 540680 | tf_op jit(solution)/shard_map/ppermute | solution.py:289
  28.5 1.7 %block_work.6 = (bf16[128,1024]{1,0:T(8,128)(2,1)S(1)}, bf16[128,1024]{1,0:T(8,128)(2,1)S(1)}, bf16[128,1024]{1,0:T(8,128)(2,1)S(1)}, bf16[128,1024]{1,0:T(8,128)(2,1)S(1)}) custom-call(bf16[136,1024]{1,0:T(8,128)(2,1)S(1)} %collective-permute-done.6.refs_0_.refs_5_, bf16[136,1024]{1,0:T(8,128)(2,1)S(1)} %collective-permute-done.7.refs_1_.refs_6_, ...), custom_call_target="tpu_custom_call" | custom-call | flops 1073741824 | bytes 3670016 | tf_op jit(solution)/shard_map/block_work/pallas_call | solution.py:146
  30.2 1.7 %collective-permute-done.8.refs_0_.refs_7_ = bf16[88,1024]{1,0:T(8,128)(2,1)S(1)} collective-permute-done((bf16[88,1024]{1,0:T(8,128)(2,1)S(1)}, bf16[88,1024]{1,0:T(8,128)(2,1)S(1)}, u32[]{:S(2)}, u32[]{:S(2)}) %collective-permute-start.8) | collective-permute-done | bytes 180256 | tf_op jit(solution)/shard_map/ppermute | solution.py:289
  31.9 0.8 %collective-permute-done.9.refs_1_.refs_8_ = bf16[48,1024]{1,0:T(8,128)(2,1)S(1)} collective-permute-done((bf16[48,1024]{1,0:T(8,128)(2,1)S(1)}, bf16[48,1024]{1,0:T(8,128)(2,1)S(1)}, u32[]{:S(2)}, u32[]{:S(2)}) %collective-permute-start.9) | collective-permute-done | bytes 98336 | tf_op jit(solution)/shard_map/ppermute | solution.py:292
  32.7 1.2 %block_work.7 = (bf16[80,1024]{1,0:T(8,128)(2,1)S(1)}, bf16[48,1024]{1,0:T(8,128)(2,1)S(1)}, bf16[128,1024]{1,0:T(8,128)(2,1)S(1)}) custom-call(bf16[88,1024]{1,0:T(8,128)(2,1)S(1)} %collective-permute-done.8.refs_0_.refs_7_, bf16[48,1024]{1,0:T(8,128)(2,1)S(1)} %collective-permute-done.9.refs_1_.refs_8_, bf16[1024,1024]{1,0:T(8,128)(2,1)S(1)} %copy-done.1, ...), custom_call_target="tpu_custom_call" | custom-call | flops 536870912 | bytes 2883584 | tf_op jit(solution)/shard_map/block_work/pallas_call | solution.py:146
  33.9 1.6 %collective-permute-start.17 = (bf16[48,1024]{1,0:T(8,128)(2,1)S(1)}, bf16[48,1024]{1,0:T(8,128)(2,1)S(1)}, u32[]{:S(2)}, u32[]{:S(2)}) collective-permute-start(bf16[48,1024]{1,0:T(8,128)(2,1)S(1)} %get-tuple-element.57), channel_id=1, source_target_pairs={{0,2},{2,4},{4,6},{6,7},{7,5},{5,3},{3,1},{1,0},{8,10},{10,12},{12... | collective-permute-start | bytes 294920 | tf_op jit(solution)/shard_map/ppermute | solution.py:289
  35.9 2.4 %weight_work.1 = (bf16[1024,256]{1,0:T(8,128)(2,1)S(1)}, bf16[1024,256]{1,0:T(8,128)(2,1)S(1)}, bf16[1024,256]{1,0:T(8,128)(2,1)S(1)}, bf16[1024,256]{1,0:T(8,128)(2,1)S(1)}) custom-call(bf16[136,1024]{1,0:T(8,128)(2,1)S(1)} %constant_dynamic-update-slice_fusion.refs_0_, bf16[136,1024]{1,0:T(8,128)(2,1)S(1)} %constant_dynamic-update-slice_fusion.2.refs_1_, ...), custom_call_target="tpu_custom_call" | custom-call | flops 2147483648 | bytes 4718592 | tf_op jit(solution)/shard_map/weight_work/pallas_call | solution.py:188
  38.9 1.6 %collective-permute-start.18 = (bf16[128,1024]{1,0:T(8,128)(2,1)S(1)}, bf16[128,1024]{1,0:T(8,128)(2,1)S(1)}, u32[]{:S(2)}, u32[]{:S(2)}) collective-permute-start(bf16[128,1024]{1,0:T(8,128)(2,1)S(1)} %pad_maximum_fusion.2), channel_id=1, source_target_pairs={{0,2},{2,4},{4,6},{6,7},{7,5},{5,3},{3,1},{1,0},{8,10},{10,12},{12... | collective-permute-start | bytes 786440 | tf_op jit(solution)/shard_map/ppermute | solution.py:289
  40.9 0.5 collective-permute-start.14
  41.4 5.9 %collective-permute-done.18 = bf16[128,1024]{1,0:T(8,128)(2,1)S(1)} collective-permute-done((bf16[128,1024]{1,0:T(8,128)(2,1)S(1)}, bf16[128,1024]{1,0:T(8,128)(2,1)S(1)}, u32[]{:S(2)}, u32[]{:S(2)}) %collective-permute-start.18) | collective-permute-done | bytes 262176 | tf_op jit(solution)/shard_map/ppermute | solution.py:289
  47.4 1.6 %collective-permute-start.19 = (bf16[128,1024]{1,0:T(8,128)(2,1)S(1)}, bf16[128,1024]{1,0:T(8,128)(2,1)S(1)}, u32[]{:S(2)}, u32[]{:S(2)}) collective-permute-start(bf16[128,1024]{1,0:T(8,128)(2,1)S(1)} %add_convert_fusion.2), channel_id=1, source_target_pairs={{0,2},{2,4},{4,6},{6,7},{7,5},{5,3},{3,1},{1,0},{8,10},{10,12},{12... | collective-permute-start | bytes 786440 | tf_op jit(solution)/shard_map/ppermute | solution.py:289
  49.1 1.6 %collective-permute-start.12 = (bf16[1024,256]{1,0:T(8,128)(2,1)S(1)}, bf16[1024,256]{1,0:T(8,128)(2,1)S(1)}, u32[]{:S(2)}, u32[]{:S(2)}) collective-permute-start(bf16[1024,256]{1,0:T(8,128)(2,1)S(1)} %add_convert_fusion), channel_id=1, source_target_pairs={{0,16},{8,24},{16,0},{24,8},{1,17},{9,25},{17,1},{25,9},{2,18},{10... | collective-permute-start | bytes 1572872 | tf_op jit(solution)/shard_map/ppermute | solution.py:329
  51.3 3.6 %collective-permute-done.19 = bf16[128,1024]{1,0:T(8,128)(2,1)S(1)} collective-permute-done((bf16[128,1024]{1,0:T(8,128)(2,1)S(1)}, bf16[128,1024]{1,0:T(8,128)(2,1)S(1)}, u32[]{:S(2)}, u32[]{:S(2)}) %collective-permute-start.19) | collective-permute-done | bytes 262176 | tf_op jit(solution)/shard_map/ppermute | solution.py:289
  54.9 1.6 %collective-permute-start.20 = (bf16[128,1024]{1,0:T(8,128)(2,1)S(1)}, bf16[128,1024]{1,0:T(8,128)(2,1)S(1)}, u32[]{:S(2)}, u32[]{:S(2)}) collective-permute-start(bf16[128,1024]{1,0:T(8,128)(2,1)S(1)} %add_convert_fusion.1), channel_id=1, source_target_pairs={{0,2},{2,4},{4,6},{6,7},{7,5},{5,3},{3,1},{1,0},{8,10},{10,12},{12... | collective-permute-start | bytes 786440 | tf_op jit(solution)/shard_map/ppermute | solution.py:289
  56.6 1.1 %collective-permute-done.15 = bf16[128,1024]{1,0:T(8,128)(2,1)S(1)} collective-permute-done((bf16[128,1024]{1,0:T(8,128)(2,1)S(1)}, bf16[128,1024]{1,0:T(8,128)(2,1)S(1)}, u32[]{:S(2)}, u32[]{:S(2)}) %collective-permute-start.15) | collective-permute-done | bytes 262176 | tf_op jit(solution)/shard_map/ppermute | solution.py:292
  58.3 3.7 %collective-permute-done.12.refs_2_ = bf16[1024,256]{1,0:T(8,128)(2,1)S(1)} collective-permute-done((bf16[1024,256]{1,0:T(8,128)(2,1)S(1)}, bf16[1024,256]{1,0:T(8,128)(2,1)S(1)}, u32[]{:S(2)}, u32[]{:S(2)}) %collective-permute-start.12) | collective-permute-done | bytes 524320 | tf_op jit(solution)/shard_map/ppermute | solution.py:329
  62.2 2.0 %collective-permute-done.16.refs_1_ = bf16[128,1024]{1,0:T(8,128)(2,1)S(1)} collective-permute-done((bf16[128,1024]{1,0:T(8,128)(2,1)S(1)}, bf16[128,1024]{1,0:T(8,128)(2,1)S(1)}, u32[]{:S(2)}, u32[]{:S(2)}) %collective-permute-start.16) | collective-permute-done | bytes 262176 | tf_op jit(solution)/shard_map/ppermute | solution.py:292
  64.2 0.9 %finish.1 = (bf16[128,1024]{1,0:T(8,128)(2,1)}, bf16[1024,256]{1,0:T(8,128)(2,1)}) custom-call(bf16[1024,256]{1,0:T(8,128)(2,1)S(1)} %weight_sum.1.weight_ref, bf16[128,1024]{1,0:T(8,128)(2,1)S(1)} %get-tuple-element.52.refs_0_, bf16[128,1024]{1,0:T(8,128)(2,1)S(1)} %collective-permute-done.16.refs_1_, bf16[128,1024]{1,0:T(8,128)(2,1)S(1)} %collective-permute-done.20.refs_2_), custom_call_target="tpu_custom_call" | custom-call | flops 393216 | bytes 2097152 | tf_op jit(solution)/shard_map/finish/pallas_call | solution.py:250
  (51 shorter events, 5.0 us)
Async XLA Ops:
  0.6 9.7 %collective-permute-start = (bf16[128,1024]{1,0:T(8,128)(2,1)}, bf16[128,1024]{1,0:T(8,128)(2,1)S(1)}, u32[]{:S(2)}, u32[]{:S(2)}) collective-permute-start(bf16[128,1024]{1,0:T(8,128)(2,1)} %param.5), channel_id=1, source_target_pairs={{0,2},{2,4},{4,6},{6,7},{7,5},{5,3},{3,1},{1,0},{8,10},{10,12},{12... | collective-permute-start | bytes 786440 | tf_op jit(solution)/shard_map/ppermute | solution.py:289
  3.7 8.2 %collective-permute-start.2 = (bf16[128,1024]{1,0:T(8,128)(2,1)}, bf16[128,1024]{1,0:T(8,128)(2,1)S(1)}, u32[]{:S(2)}, u32[]{:S(2)}) collective-permute-start(bf16[128,1024]{1,0:T(8,128)(2,1)} %param.5), channel_id=1, source_target_pairs={{2,0},{4,2},{6,4},{7,6},{5,7},{3,5},{1,3},{0,1},{10,8},{12,10},{14... | collective-permute-start | bytes 786440 | tf_op jit(solution)/shard_map/ppermute | solution.py:292
  3.7 0.7 %copy-start.2 = (s32[128,16]{0,1:T(8,128)S(1)}, s32[128,16]{0,1:T(8,128)}, u32[]{:S(2)}) copy-start(s32[128,16]{0,1:T(8,128)} %param.6) | copy-start | bytes 24580
  4.4 0.7 %copy-start.3 = (s32[128,4]{0,1:T(4,128)S(1)}, s32[128,4]{0,1:T(4,128)}, u32[]{:S(2)}) copy-start(s32[128,4]{0,1:T(4,128)} %param.7) | copy-start | bytes 6148
  5.1 6.7 %collective-permute-start.1 = (bf16[8,1024]{1,0:T(8,128)(2,1)S(1)}, bf16[8,1024]{1,0:T(8,128)(2,1)S(1)}, u32[]{:S(2)}, u32[]{:S(2)}) collective-permute-start(bf16[8,1024]{1,0:T(8,128)(2,1)S(1)} %instance_ids.1), channel_id=1, source_target_pairs={{0,2},{2,4},{4,6},{6,7},{7,5},{5,3},{3,1},{1,0},{8,10},{10,12},{12... | collective-permute-start | bytes 49160 | tf_op jit(solution)/shard_map/ppermute | solution.py:289
  7.2 6.3 %collective-permute-start.3 = (bf16[8,1024]{1,0:T(8,128)(2,1)S(1)}, bf16[8,1024]{1,0:T(8,128)(2,1)S(1)}, u32[]{:S(2)}, u32[]{:S(2)}) collective-permute-start(bf16[8,1024]{1,0:T(8,128)(2,1)S(1)} %instance_ids.1), channel_id=1, source_target_pairs={{2,0},{4,2},{6,4},{7,6},{5,7},{3,5},{1,3},{0,1},{10,8},{12,10},{14... | collective-permute-start | bytes 49160 | tf_op jit(solution)/shard_map/ppermute | solution.py:292
  7.2 1.6 %copy-start = (bf16[1024,1024]{1,0:T(8,128)(2,1)S(1)}, bf16[1024,1024]{1,0:T(8,128)(2,1)}, u32[]{:S(2)}) copy-start(bf16[1024,1024]{1,0:T(8,128)(2,1)} %refs_2_.5) | copy-start | bytes 6291460
  8.8 0.7 %copy-start.4 = (s32[8]{0:T(128)S(1)}, s32[8]{0:T(128)}, u32[]{:S(2)}) copy-start(s32[8]{0:T(128)} %size_ref.1) | copy-start | bytes 100
  9.4 4.6 %copy-start.1 = (bf16[1024,1024]{1,0:T(8,128)(2,1)S(1)}, bf16[1024,1024]{1,0:T(8,128)(2,1)}, u32[]{:S(2)}) copy-start(bf16[1024,1024]{1,0:T(8,128)(2,1)} %refs_2_.5) | copy-start | bytes 6291460
  11.9 7.0 %collective-permute-start.4 = (bf16[136,1024]{1,0:T(8,128)(2,1)S(1)}, bf16[136,1024]{1,0:T(8,128)(2,1)S(1)}, u32[]{:S(2)}, u32[]{:S(2)}) collective-permute-start(bf16[136,1024]{1,0:T(8,128)(2,1)S(1)} %constant_dynamic-update-slice_fusion.refs_0_), channel_id=1, source_target_pairs={{0,2},{2,4},{4,6},{6,7},{7,5},{5,3},{3,1},{1,0},{8,10},{10,12},{12... | collective-permute-start | bytes 835592 | tf_op jit(solution)/shard_map/ppermute | solution.py:289
  13.5 7.0 %copy-start.5 = (bf16[128,1024]{1,0:T(8,128)(2,1)S(1)}, bf16[128,1024]{1,0:T(8,128)(2,1)}, u32[]{:S(2)}) copy-start(bf16[128,1024]{1,0:T(8,128)(2,1)} %param.5) | copy-start | bytes 786436
  13.5 7.0 %collective-permute-start.5 = (bf16[136,1024]{1,0:T(8,128)(2,1)S(1)}, bf16[136,1024]{1,0:T(8,128)(2,1)S(1)}, u32[]{:S(2)}, u32[]{:S(2)}) collective-permute-start(bf16[136,1024]{1,0:T(8,128)(2,1)S(1)} %constant_dynamic-update-slice_fusion.2.refs_1_), channel_id=1, source_target_pairs={{2,0},{4,2},{6,4},{7,6},{5,7},{3,5},{1,3},{0,1},{10,8},{12,10},{14... | collective-permute-start | bytes 835592 | tf_op jit(solution)/shard_map/ppermute | solution.py:292
  18.9 7.4 %collective-permute-start.6 = (bf16[136,1024]{1,0:T(8,128)(2,1)S(1)}, bf16[136,1024]{1,0:T(8,128)(2,1)S(1)}, u32[]{:S(2)}, u32[]{:S(2)}) collective-permute-start(bf16[136,1024]{1,0:T(8,128)(2,1)S(1)} %collective-permute-done.4.refs_0_.refs_2_), channel_id=1, source_target_pairs={{0,2},{2,4},{4,6},{6,7},{7,5},{5,3},{3,1},{1,0},{8,10},{10,12},{12... | collective-permute-start | bytes 835592 | tf_op jit(solution)/shard_map/ppermute | solution.py:289
  20.5 7.5 %collective-permute-start.7 = (bf16[136,1024]{1,0:T(8,128)(2,1)S(1)}, bf16[136,1024]{1,0:T(8,128)(2,1)S(1)}, u32[]{:S(2)}, u32[]{:S(2)}) collective-permute-start(bf16[136,1024]{1,0:T(8,128)(2,1)S(1)} %collective-permute-done.5.refs_1_.refs_3_), channel_id=1, source_target_pairs={{2,0},{4,2},{6,4},{7,6},{5,7},{3,5},{1,3},{0,1},{10,8},{12,10},{14... | collective-permute-start | bytes 835592 | tf_op jit(solution)/shard_map/ppermute | solution.py:292
  26.3 5.5 %collective-permute-start.8 = (bf16[88,1024]{1,0:T(8,128)(2,1)S(1)}, bf16[88,1024]{1,0:T(8,128)(2,1)S(1)}, u32[]{:S(2)}, u32[]{:S(2)}) collective-permute-start(bf16[88,1024]{1,0:T(8,128)(2,1)S(1)} %pad_maximum_fusion.3), channel_id=1, source_target_pairs={{0,2},{2,4},{4,6},{6,7},{7,5},{5,3},{3,1},{1,0},{8,10},{10,12},{12... | collective-permute-start | bytes 540680 | tf_op jit(solution)/shard_map/ppermute | solution.py:289
  28.0 4.7 %collective-permute-start.9 = (bf16[48,1024]{1,0:T(8,128)(2,1)S(1)}, bf16[48,1024]{1,0:T(8,128)(2,1)S(1)}, u32[]{:S(2)}, u32[]{:S(2)}) collective-permute-start(bf16[48,1024]{1,0:T(8,128)(2,1)S(1)} %slice.23), channel_id=1, source_target_pairs={{2,0},{4,2},{6,4},{7,6},{5,7},{3,5},{1,3},{0,1},{10,8},{12,10},{14... | collective-permute-start | bytes 294920 | tf_op jit(solution)/shard_map/ppermute | solution.py:292
  33.9 5.0 %collective-permute-start.17 = (bf16[48,1024]{1,0:T(8,128)(2,1)S(1)}, bf16[48,1024]{1,0:T(8,128)(2,1)S(1)}, u32[]{:S(2)}, u32[]{:S(2)}) collective-permute-start(bf16[48,1024]{1,0:T(8,128)(2,1)S(1)} %get-tuple-element.57), channel_id=1, source_target_pairs={{0,2},{2,4},{4,6},{6,7},{7,5},{5,3},{3,1},{1,0},{8,10},{10,12},{12... | collective-permute-start | bytes 294920 | tf_op jit(solution)/shard_map/ppermute | solution.py:289
  35.5 5.3 %collective-permute-start.13 = (bf16[80,1024]{1,0:T(8,128)(2,1)S(1)}, bf16[80,1024]{1,0:T(8,128)(2,1)S(1)}, u32[]{:S(2)}, u32[]{:S(2)}) collective-permute-start(bf16[80,1024]{1,0:T(8,128)(2,1)S(1)} %get-tuple-element.53), channel_id=1, source_target_pairs={{2,0},{4,2},{6,4},{7,6},{5,7},{3,5},{1,3},{0,1},{10,8},{12,10},{14... | collective-permute-start | bytes 491528 | tf_op jit(solution)/shard_map/ppermute | solution.py:292
  38.3 10.7 %collective-permute-start.11 = (bf16[1024,256]{1,0:T(8,128)(2,1)S(1)}, bf16[1024,256]{1,0:T(8,128)(2,1)S(1)}, u32[]{:S(2)}, u32[]{:S(2)}) collective-permute-start(bf16[1024,256]{1,0:T(8,128)(2,1)S(1)} %get-tuple-element.51), channel_id=1, source_target_pairs={{0,8},{8,0},{16,24},{24,16},{1,9},{9,1},{17,25},{25,17},{2,10},{10... | collective-permute-start | bytes 1572872 | tf_op jit(solution)/shard_map/ppermute | solution.py:329
  38.4 19.9 %collective-permute-start.10 = (bf16[1024,256]{1,0:T(8,128)(2,1)S(1)}, bf16[1024,256]{1,0:T(8,128)(2,1)S(1)}, u32[]{:S(2)}, u32[]{:S(2)}) collective-permute-start(bf16[1024,256]{1,0:T(8,128)(2,1)S(1)} %get-tuple-element.49), channel_id=1, source_target_pairs={{0,8},{8,0},{16,24},{24,16},{1,9},{9,1},{17,25},{25,17},{2,10},{10... | collective-permute-start | bytes 1572872 | tf_op jit(solution)/shard_map/ppermute | solution.py:329
  38.9 8.3 %collective-permute-start.18 = (bf16[128,1024]{1,0:T(8,128)(2,1)S(1)}, bf16[128,1024]{1,0:T(8,128)(2,1)S(1)}, u32[]{:S(2)}, u32[]{:S(2)}) collective-permute-start(bf16[128,1024]{1,0:T(8,128)(2,1)S(1)} %pad_maximum_fusion.2), channel_id=1, source_target_pairs={{0,2},{2,4},{4,6},{6,7},{7,5},{5,3},{3,1},{1,0},{8,10},{10,12},{12... | collective-permute-start | bytes 786440 | tf_op jit(solution)/shard_map/ppermute | solution.py:289
  40.9 9.8 %collective-permute-start.14 = (bf16[128,1024]{1,0:T(8,128)(2,1)S(1)}, bf16[128,1024]{1,0:T(8,128)(2,1)S(1)}, u32[]{:S(2)}, u32[]{:S(2)}) collective-permute-start(bf16[128,1024]{1,0:T(8,128)(2,1)S(1)} %pad_maximum_fusion.1), channel_id=1, source_target_pairs={{2,0},{4,2},{6,4},{7,6},{5,7},{3,5},{1,3},{0,1},{10,8},{12,10},{14... | collective-permute-start | bytes 786440 | tf_op jit(solution)/shard_map/ppermute | solution.py:292
  47.4 7.5 %collective-permute-start.19 = (bf16[128,1024]{1,0:T(8,128)(2,1)S(1)}, bf16[128,1024]{1,0:T(8,128)(2,1)S(1)}, u32[]{:S(2)}, u32[]{:S(2)}) collective-permute-start(bf16[128,1024]{1,0:T(8,128)(2,1)S(1)} %add_convert_fusion.2), channel_id=1, source_target_pairs={{0,2},{2,4},{4,6},{6,7},{7,5},{5,3},{3,1},{1,0},{8,10},{10,12},{12... | collective-permute-start | bytes 786440 | tf_op jit(solution)/shard_map/ppermute | solution.py:289
  49.1 12.9 %collective-permute-start.12 = (bf16[1024,256]{1,0:T(8,128)(2,1)S(1)}, bf16[1024,256]{1,0:T(8,128)(2,1)S(1)}, u32[]{:S(2)}, u32[]{:S(2)}) collective-permute-start(bf16[1024,256]{1,0:T(8,128)(2,1)S(1)} %add_convert_fusion), channel_id=1, source_target_pairs={{0,16},{8,24},{16,0},{24,8},{1,17},{9,25},{17,1},{25,9},{2,18},{10... | collective-permute-start | bytes 1572872 | tf_op jit(solution)/shard_map/ppermute | solution.py:329
  50.8 6.9 %collective-permute-start.15 = (bf16[128,1024]{1,0:T(8,128)(2,1)S(1)}, bf16[128,1024]{1,0:T(8,128)(2,1)S(1)}, u32[]{:S(2)}, u32[]{:S(2)}) collective-permute-start(bf16[128,1024]{1,0:T(8,128)(2,1)S(1)} %add_convert_fusion.4), channel_id=1, source_target_pairs={{2,0},{4,2},{6,4},{7,6},{5,7},{3,5},{1,3},{0,1},{10,8},{12,10},{14... | collective-permute-start | bytes 786440 | tf_op jit(solution)/shard_map/ppermute | solution.py:292
  54.9 7.2 %collective-permute-start.20 = (bf16[128,1024]{1,0:T(8,128)(2,1)S(1)}, bf16[128,1024]{1,0:T(8,128)(2,1)S(1)}, u32[]{:S(2)}, u32[]{:S(2)}) collective-permute-start(bf16[128,1024]{1,0:T(8,128)(2,1)S(1)} %add_convert_fusion.1), channel_id=1, source_target_pairs={{0,2},{2,4},{4,6},{6,7},{7,5},{5,3},{3,1},{1,0},{8,10},{10,12},{12... | collective-permute-start | bytes 786440 | tf_op jit(solution)/shard_map/ppermute | solution.py:289
  57.8 6.4 %collective-permute-start.16 = (bf16[128,1024]{1,0:T(8,128)(2,1)S(1)}, bf16[128,1024]{1,0:T(8,128)(2,1)S(1)}, u32[]{:S(2)}, u32[]{:S(2)}) collective-permute-start(bf16[128,1024]{1,0:T(8,128)(2,1)S(1)} %add_convert_fusion.3), channel_id=1, source_target_pairs={{2,0},{4,2},{6,4},{7,6},{5,7},{3,5},{1,3},{0,1},{10,8},{12,10},{14... | collective-permute-start | bytes 786440 | tf_op jit(solution)/shard_map/ppermute | solution.py:292

commit v14 on v13

--- a/solution.py
+++ b/solution.py
@@ -225,7 +225,9 @@
         in_specs=[pl.BlockSpec(memory_space=pltpu.VMEM)] * len(parts),
         compiler_params=pltpu.CompilerParams(vmem_limit_bytes=VMEM_LIMIT),
         cost_estimate=pl.CostEstimate(
-            flops=4_000_000_000, bytes_accessed=2 * (len(parts) + 1) * parts[0].size, transcendentals=0
+            flops=len(parts) * parts[0].size,
+            bytes_accessed=2 * (len(parts) + 1) * parts[0].size,
+            transcendentals=0,
         ),
         name="weight_sum",
     )(*parts)

time: 65.3 us -> 64.6 us (0.989)
    ppermute x9, waiting for transfers between devices: 5.68 us -> 3.63 us  [send_down(): return lax.ppermute(array, 'clus', down)]
    ppermute x3, waiting for transfers between devices: 3.7 us -> 5.14 us  [seq_send(): return lax.ppermute(array, 'seq', [(k, k ^ bit) for k in range(seq_count)])]
where the time goes in v14:
time: 64.6 us; the launch traced here: 64.4 us
  waiting for transfers between devices  26.7 us (41%)
  starting transfers between devices  21.6 us (33%)
  Pallas kernels  11 us (17%)
  local copies, waits for them, and re-layouts  3.72 us (6%)
  between operations  0.85 us (1%)
    ppermute x9, waiting for transfers between devices, send_up(): return lax.ppermute(array, 'clus', up)  17.9 us
    ppermute x9, starting transfers between devices, send_up(): return lax.ppermute(array, 'clus', up)  16.4 us
    pallas_call x4, Pallas kernels, block_work(): pl.pallas_call(functools.partial(block_kernel, piece_rows, top_count, pos...  6.97 us
    ppermute x3, waiting for transfers between devices, seq_send(): return lax.ppermute(array, 'seq', [(k, k ^ bit) for k in range(seq_count)])  5.14 us
    unnamed x14, local copies, waits for them, and re-layouts  3.67 us
    ppermute x9, waiting for transfers between devices, send_down(): return lax.ppermute(array, 'clus', down)  3.63 us
    ppermute x9, starting transfers between devices, send_down(): return lax.ppermute(array, 'clus', down)  3.49 us
    pallas_call x1, Pallas kernels, weight_work(): pl.pallas_call(functools.partial(weight_kernel, piece_rows, column_blocks...  2.37 us
  transfers between devices with their start and end apart: 21, of which 12 were waited for; matrix products, arithmetic and copies ran while one was open for 1% of the time, Pallas kernels for 14%

profile of v14, /device:TPU:0, one launch (start us, length us, event | category | flops | bytes accessed | tf_op | source)
XLA Modules:
  0.0 64.4 jit_solution(14659292254208452379)
XLA Ops:
  0.6 3.1 %collective-permute-start = (bf16[128,1024]{1,0:T(8,128)(2,1)}, bf16[128,1024]{1,0:T(8,128)(2,1)S(1)}, u32[]{:S(2)}, u32[]{:S(2)}) collective-permute-start(bf16[128,1024]{1,0:T(8,128)(2,1)} %param.5), channel_id=1, source_target_pairs={{0,2},{2,4},{4,6},{6,7},{7,5},{5,3},{3,1},{1,0},{8,10},{10,12},{12... | collective-permute-start | bytes 786440 | tf_op jit(solution)/shard_map/ppermute | solution.py:291
  3.7 0.7 %copy-done.2 = s32[128,16]{0,1:T(8,128)S(1)} copy-done((s32[128,16]{0,1:T(8,128)S(1)}, s32[128,16]{0,1:T(8,128)}, u32[]{:S(2)}) %copy-start.2) | copy-done | bytes 8216
  4.4 0.7 %copy-done.3 = s32[128,4]{0,1:T(4,128)S(1)} copy-done((s32[128,4]{0,1:T(4,128)S(1)}, s32[128,4]{0,1:T(4,128)}, u32[]{:S(2)}) %copy-start.3) | copy-done | bytes 2072
  5.1 2.1 %collective-permute-start.1 = (bf16[8,1024]{1,0:T(8,128)(2,1)S(1)}, bf16[8,1024]{1,0:T(8,128)(2,1)S(1)}, u32[]{:S(2)}, u32[]{:S(2)}) collective-permute-start(bf16[8,1024]{1,0:T(8,128)(2,1)S(1)} %instance_ids.1), channel_id=1, source_target_pairs={{0,2},{2,4},{4,6},{6,7},{7,5},{5,3},{3,1},{1,0},{8,10},{10,12},{12... | collective-permute-start | bytes 49160 | tf_op jit(solution)/shard_map/ppermute | solution.py:291
  7.2 1.6 %copy-done = bf16[1024,1024]{1,0:T(8,128)(2,1)S(1)} copy-done((bf16[1024,1024]{1,0:T(8,128)(2,1)S(1)}, bf16[1024,1024]{1,0:T(8,128)(2,1)}, u32[]{:S(2)}) %copy-start) | copy-done | bytes 2097176
  8.8 0.7 %copy-done.4 = s32[8]{0:T(128)S(1)} copy-done((s32[8]{0:T(128)S(1)}, s32[8]{0:T(128)}, u32[]{:S(2)}) %copy-start.4) | copy-done | bytes 56
  9.5 0.6 live_labels.1.refs_3_.refs_4_
  10.4 1.5 %collective-permute-done.2 = bf16[128,1024]{1,0:T(8,128)(2,1)S(1)} collective-permute-done((bf16[128,1024]{1,0:T(8,128)(2,1)}, bf16[128,1024]{1,0:T(8,128)(2,1)S(1)}, u32[]{:S(2)}, u32[]{:S(2)}) %collective-permute-start.2) | collective-permute-done | bytes 262176 | tf_op jit(solution)/shard_map/ppermute | solution.py:294
  11.9 1.6 %collective-permute-start.4 = (bf16[136,1024]{1,0:T(8,128)(2,1)S(1)}, bf16[136,1024]{1,0:T(8,128)(2,1)S(1)}, u32[]{:S(2)}, u32[]{:S(2)}) collective-permute-start(bf16[136,1024]{1,0:T(8,128)(2,1)S(1)} %constant_dynamic-update-slice_fusion.refs_0_), channel_id=1, source_target_pairs={{0,2},{2,4},{4,6},{6,7},{7,5},{5,3},{3,1},{1,0},{8,10},{10,12},{12... | collective-permute-start | bytes 835592 | tf_op jit(solution)/shard_map/ppermute | solution.py:291
  14.0 1.7 %block_work.4 = (bf16[128,1024]{1,0:T(8,128)(2,1)S(1)}, bf16[128,1024]{1,0:T(8,128)(2,1)S(1)}, bf16[128,1024]{1,0:T(8,128)(2,1)S(1)}, bf16[128,1024]{1,0:T(8,128)(2,1)S(1)}) custom-call(bf16[136,1024]{1,0:T(8,128)(2,1)S(1)} %constant_dynamic-update-slice_fusion.refs_0_, bf16[136,1024]{1,0:T(8,128)(2,1)S(1)} %constant_dynamic-update-slice_fusion.2.refs_1_, ...), custom_call_target="tpu_custom_call" | custom-call | flops 1073741824 | bytes 3670016 | tf_op jit(solution)/shard_map/block_work/pallas_call | solution.py:146
  15.7 3.2 %collective-permute-done.4.refs_0_.refs_2_ = bf16[136,1024]{1,0:T(8,128)(2,1)S(1)} collective-permute-done((bf16[136,1024]{1,0:T(8,128)(2,1)S(1)}, bf16[136,1024]{1,0:T(8,128)(2,1)S(1)}, u32[]{:S(2)}, u32[]{:S(2)}) %collective-permute-start.4) | collective-permute-done | bytes 278560 | tf_op jit(solution)/shard_map/ppermute | solution.py:291
  18.9 1.6 %collective-permute-start.6 = (bf16[136,1024]{1,0:T(8,128)(2,1)S(1)}, bf16[136,1024]{1,0:T(8,128)(2,1)S(1)}, u32[]{:S(2)}, u32[]{:S(2)}) collective-permute-start(bf16[136,1024]{1,0:T(8,128)(2,1)S(1)} %collective-permute-done.4.refs_0_.refs_2_), channel_id=1, source_target_pairs={{0,2},{2,4},{4,6},{6,7},{7,5},{5,3},{3,1},{1,0},{8,10},{10,12},{12... | collective-permute-start | bytes 835592 | tf_op jit(solution)/shard_map/ppermute | solution.py:291
  21.0 2.4 %block_work.5 = (bf16[128,1024]{1,0:T(8,128)(2,1)S(1)}, bf16[128,1024]{1,0:T(8,128)(2,1)S(1)}, bf16[128,1024]{1,0:T(8,128)(2,1)S(1)}, bf16[128,1024]{1,0:T(8,128...) custom-call(bf16[136,1024]{1,0:T(8,128)(2,1)S(1)} %collective-permute-done.4.refs_0_.refs_2_, ...), custom_call_target="tpu_custom_call" | custom-call | flops 1610612736 | bytes 4456448 | tf_op jit(solution)/shard_map/block_work/pallas_call | solution.py:146
  23.4 2.9 %collective-permute-done.6.refs_0_.refs_5_ = bf16[136,1024]{1,0:T(8,128)(2,1)S(1)} collective-permute-done((bf16[136,1024]{1,0:T(8,128)(2,1)S(1)}, bf16[136,1024]{1,0:T(8,128)(2,1)S(1)}, u32[]{:S(2)}, u32[]{:S(2)}) %collective-permute-start.6) | collective-permute-done | bytes 278560 | tf_op jit(solution)/shard_map/ppermute | solution.py:291
  26.3 1.6 %collective-permute-start.8 = (bf16[88,1024]{1,0:T(8,128)(2,1)S(1)}, bf16[88,1024]{1,0:T(8,128)(2,1)S(1)}, u32[]{:S(2)}, u32[]{:S(2)}) collective-permute-start(bf16[88,1024]{1,0:T(8,128)(2,1)S(1)} %pad_maximum_fusion.3), channel_id=1, source_target_pairs={{0,2},{2,4},{4,6},{6,7},{7,5},{5,3},{3,1},{1,0},{8,10},{10,12},{12... | collective-permute-start | bytes 540680 | tf_op jit(solution)/shard_map/ppermute | solution.py:291
  28.5 1.7 %block_work.6 = (bf16[128,1024]{1,0:T(8,128)(2,1)S(1)}, bf16[128,1024]{1,0:T(8,128)(2,1)S(1)}, bf16[128,1024]{1,0:T(8,128)(2,1)S(1)}, bf16[128,1024]{1,0:T(8,128)(2,1)S(1)}) custom-call(bf16[136,1024]{1,0:T(8,128)(2,1)S(1)} %collective-permute-done.6.refs_0_.refs_5_, bf16[136,1024]{1,0:T(8,128)(2,1)S(1)} %collective-permute-done.7.refs_1_.refs_6_, ...), custom_call_target="tpu_custom_call" | custom-call | flops 1073741824 | bytes 3670016 | tf_op jit(solution)/shard_map/block_work/pallas_call | solution.py:146
  30.2 1.7 %collective-permute-done.8.refs_0_.refs_7_ = bf16[88,1024]{1,0:T(8,128)(2,1)S(1)} collective-permute-done((bf16[88,1024]{1,0:T(8,128)(2,1)S(1)}, bf16[88,1024]{1,0:T(8,128)(2,1)S(1)}, u32[]{:S(2)}, u32[]{:S(2)}) %collective-permute-start.8) | collective-permute-done | bytes 180256 | tf_op jit(solution)/shard_map/ppermute | solution.py:291
  31.9 0.8 %collective-permute-done.9.refs_1_.refs_8_ = bf16[48,1024]{1,0:T(8,128)(2,1)S(1)} collective-permute-done((bf16[48,1024]{1,0:T(8,128)(2,1)S(1)}, bf16[48,1024]{1,0:T(8,128)(2,1)S(1)}, u32[]{:S(2)}, u32[]{:S(2)}) %collective-permute-start.9) | collective-permute-done | bytes 98336 | tf_op jit(solution)/shard_map/ppermute | solution.py:294
  32.7 1.2 %block_work.7 = (bf16[80,1024]{1,0:T(8,128)(2,1)S(1)}, bf16[48,1024]{1,0:T(8,128)(2,1)S(1)}, bf16[128,1024]{1,0:T(8,128)(2,1)S(1)}) custom-call(bf16[88,1024]{1,0:T(8,128)(2,1)S(1)} %collective-permute-done.8.refs_0_.refs_7_, bf16[48,1024]{1,0:T(8,128)(2,1)S(1)} %collective-permute-done.9.refs_1_.refs_8_, bf16[1024,1024]{1,0:T(8,128)(2,1)S(1)} %copy-done.1, ...), custom_call_target="tpu_custom_call" | custom-call | flops 536870912 | bytes 2883584 | tf_op jit(solution)/shard_map/block_work/pallas_call | solution.py:146
  33.9 1.6 %collective-permute-start.17 = (bf16[48,1024]{1,0:T(8,128)(2,1)S(1)}, bf16[48,1024]{1,0:T(8,128)(2,1)S(1)}, u32[]{:S(2)}, u32[]{:S(2)}) collective-permute-start(bf16[48,1024]{1,0:T(8,128)(2,1)S(1)} %get-tuple-element.57), channel_id=1, source_target_pairs={{0,2},{2,4},{4,6},{6,7},{7,5},{5,3},{3,1},{1,0},{8,10},{10,12},{12... | collective-permute-start | bytes 294920 | tf_op jit(solution)/shard_map/ppermute | solution.py:291
  35.9 2.4 %weight_work.1 = (bf16[1024,256]{1,0:T(8,128)(2,1)S(1)}, bf16[1024,256]{1,0:T(8,128)(2,1)S(1)}, bf16[1024,256]{1,0:T(8,128)(2,1)S(1)}, bf16[1024,256]{1,0:T(8,128)(2,1)S(1)}) custom-call(bf16[136,1024]{1,0:T(8,128)(2,1)S(1)} %constant_dynamic-update-slice_fusion.refs_0_, bf16[136,1024]{1,0:T(8,128)(2,1)S(1)} %constant_dynamic-update-slice_fusion.2.refs_1_, ...), custom_call_target="tpu_custom_call" | custom-call | flops 2147483648 | bytes 4718592 | tf_op jit(solution)/shard_map/weight_work/pallas_call | solution.py:188
  38.6 1.6 %collective-permute-start.18 = (bf16[128,1024]{1,0:T(8,128)(2,1)S(1)}, bf16[128,1024]{1,0:T(8,128)(2,1)S(1)}, u32[]{:S(2)}, u32[]{:S(2)}) collective-permute-start(bf16[128,1024]{1,0:T(8,128)(2,1)S(1)} %pad_maximum_fusion.2), channel_id=1, source_target_pairs={{0,2},{2,4},{4,6},{6,7},{7,5},{5,3},{3,1},{1,0},{8,10},{10,12},{12... | collective-permute-start | bytes 786440 | tf_op jit(solution)/shard_map/ppermute | solution.py:291
  40.2 0.6 collective-permute-done.13
  40.9 0.5 collective-permute-start.14
  41.4 5.8 %collective-permute-done.18 = bf16[128,1024]{1,0:T(8,128)(2,1)S(1)} collective-permute-done((bf16[128,1024]{1,0:T(8,128)(2,1)S(1)}, bf16[128,1024]{1,0:T(8,128)(2,1)S(1)}, u32[]{:S(2)}, u32[]{:S(2)}) %collective-permute-start.18) | collective-permute-done | bytes 262176 | tf_op jit(solution)/shard_map/ppermute | solution.py:291
  47.3 1.6 %collective-permute-start.19 = (bf16[128,1024]{1,0:T(8,128)(2,1)S(1)}, bf16[128,1024]{1,0:T(8,128)(2,1)S(1)}, u32[]{:S(2)}, u32[]{:S(2)}) collective-permute-start(bf16[128,1024]{1,0:T(8,128)(2,1)S(1)} %add_convert_fusion.2), channel_id=1, source_target_pairs={{0,2},{2,4},{4,6},{6,7},{7,5},{5,3},{3,1},{1,0},{8,10},{10,12},{12... | collective-permute-start | bytes 786440 | tf_op jit(solution)/shard_map/ppermute | solution.py:291
  49.6 1.6 %collective-permute-start.12 = (bf16[1024,256]{1,0:T(8,128)(2,1)S(1)}, bf16[1024,256]{1,0:T(8,128)(2,1)S(1)}, u32[]{:S(2)}, u32[]{:S(2)}) collective-permute-start(bf16[1024,256]{1,0:T(8,128)(2,1)S(1)} %add_convert_fusion), channel_id=1, source_target_pairs={{0,16},{8,24},{16,0},{24,8},{1,17},{9,25},{17,1},{25,9},{2,18},{10... | collective-permute-start | bytes 1572872 | tf_op jit(solution)/shard_map/ppermute | solution.py:331
  51.2 3.9 %collective-permute-done.19 = bf16[128,1024]{1,0:T(8,128)(2,1)S(1)} collective-permute-done((bf16[128,1024]{1,0:T(8,128)(2,1)S(1)}, bf16[128,1024]{1,0:T(8,128)(2,1)S(1)}, u32[]{:S(2)}, u32[]{:S(2)}) %collective-permute-start.19) | collective-permute-done | bytes 262176 | tf_op jit(solution)/shard_map/ppermute | solution.py:291
  55.2 1.6 %collective-permute-start.20 = (bf16[128,1024]{1,0:T(8,128)(2,1)S(1)}, bf16[128,1024]{1,0:T(8,128)(2,1)S(1)}, u32[]{:S(2)}, u32[]{:S(2)}) collective-permute-start(bf16[128,1024]{1,0:T(8,128)(2,1)S(1)} %add_convert_fusion.1), channel_id=1, source_target_pairs={{0,2},{2,4},{4,6},{6,7},{7,5},{5,3},{3,1},{1,0},{8,10},{10,12},{12... | collective-permute-start | bytes 786440 | tf_op jit(solution)/shard_map/ppermute | solution.py:291
  57.4 5.1 %collective-permute-done.12.refs_2_ = bf16[1024,256]{1,0:T(8,128)(2,1)S(1)} collective-permute-done((bf16[1024,256]{1,0:T(8,128)(2,1)S(1)}, bf16[1024,256]{1,0:T(8,128)(2,1)S(1)}, u32[]{:S(2)}, u32[]{:S(2)}) %collective-permute-start.12) | collective-permute-done | bytes 524320 | tf_op jit(solution)/shard_map/ppermute | solution.py:331
  62.7 0.8 %collective-permute-done.16.refs_1_ = bf16[128,1024]{1,0:T(8,128)(2,1)S(1)} collective-permute-done((bf16[128,1024]{1,0:T(8,128)(2,1)S(1)}, bf16[128,1024]{1,0:T(8,128)(2,1)S(1)}, u32[]{:S(2)}, u32[]{:S(2)}) %collective-permute-start.16) | collective-permute-done | bytes 262176 | tf_op jit(solution)/shard_map/ppermute | solution.py:294
  63.5 0.9 %finish.1 = (bf16[128,1024]{1,0:T(8,128)(2,1)}, bf16[1024,256]{1,0:T(8,128)(2,1)}) custom-call(bf16[1024,256]{1,0:T(8,128)(2,1)S(1)} %weight_sum.1.weight_ref, bf16[128,1024]{1,0:T(8,128)(2,1)S(1)} %get-tuple-element.52.refs_0_, bf16[128,1024]{1,0:T(8,128)(2,1)S(1)} %collective-permute-done.16.refs_1_, bf16[128,1024]{1,0:T(8,128)(2,1)S(1)} %collective-permute-done.20.refs_2_), custom_call_target="tpu_custom_call" | custom-call | flops 393216 | bytes 2097152 | tf_op jit(solution)/shard_map/finish/pallas_call | solution.py:252
  (51 shorter events, 4.4 us)
Async XLA Ops:
  0.6 9.7 %collective-permute-start = (bf16[128,1024]{1,0:T(8,128)(2,1)}, bf16[128,1024]{1,0:T(8,128)(2,1)S(1)}, u32[]{:S(2)}, u32[]{:S(2)}) collective-permute-start(bf16[128,1024]{1,0:T(8,128)(2,1)} %param.5), channel_id=1, source_target_pairs={{0,2},{2,4},{4,6},{6,7},{7,5},{5,3},{3,1},{1,0},{8,10},{10,12},{12... | collective-permute-start | bytes 786440 | tf_op jit(solution)/shard_map/ppermute | solution.py:291
  3.7 8.2 %collective-permute-start.2 = (bf16[128,1024]{1,0:T(8,128)(2,1)}, bf16[128,1024]{1,0:T(8,128)(2,1)S(1)}, u32[]{:S(2)}, u32[]{:S(2)}) collective-permute-start(bf16[128,1024]{1,0:T(8,128)(2,1)} %param.5), channel_id=1, source_target_pairs={{2,0},{4,2},{6,4},{7,6},{5,7},{3,5},{1,3},{0,1},{10,8},{12,10},{14... | collective-permute-start | bytes 786440 | tf_op jit(solution)/shard_map/ppermute | solution.py:294
  3.7 0.7 %copy-start.2 = (s32[128,16]{0,1:T(8,128)S(1)}, s32[128,16]{0,1:T(8,128)}, u32[]{:S(2)}) copy-start(s32[128,16]{0,1:T(8,128)} %param.6) | copy-start | bytes 24580
  4.4 0.7 %copy-start.3 = (s32[128,4]{0,1:T(4,128)S(1)}, s32[128,4]{0,1:T(4,128)}, u32[]{:S(2)}) copy-start(s32[128,4]{0,1:T(4,128)} %param.7) | copy-start | bytes 6148
  5.1 6.7 %collective-permute-start.1 = (bf16[8,1024]{1,0:T(8,128)(2,1)S(1)}, bf16[8,1024]{1,0:T(8,128)(2,1)S(1)}, u32[]{:S(2)}, u32[]{:S(2)}) collective-permute-start(bf16[8,1024]{1,0:T(8,128)(2,1)S(1)} %instance_ids.1), channel_id=1, source_target_pairs={{0,2},{2,4},{4,6},{6,7},{7,5},{5,3},{3,1},{1,0},{8,10},{10,12},{12... | collective-permute-start | bytes 49160 | tf_op jit(solution)/shard_map/ppermute | solution.py:291
  7.2 6.3 %collective-permute-start.3 = (bf16[8,1024]{1,0:T(8,128)(2,1)S(1)}, bf16[8,1024]{1,0:T(8,128)(2,1)S(1)}, u32[]{:S(2)}, u32[]{:S(2)}) collective-permute-start(bf16[8,1024]{1,0:T(8,128)(2,1)S(1)} %instance_ids.1), channel_id=1, source_target_pairs={{2,0},{4,2},{6,4},{7,6},{5,7},{3,5},{1,3},{0,1},{10,8},{12,10},{14... | collective-permute-start | bytes 49160 | tf_op jit(solution)/shard_map/ppermute | solution.py:294
  7.2 1.6 %copy-start = (bf16[1024,1024]{1,0:T(8,128)(2,1)S(1)}, bf16[1024,1024]{1,0:T(8,128)(2,1)}, u32[]{:S(2)}) copy-start(bf16[1024,1024]{1,0:T(8,128)(2,1)} %refs_2_.5) | copy-start | bytes 6291460
  8.8 0.7 %copy-start.4 = (s32[8]{0:T(128)S(1)}, s32[8]{0:T(128)}, u32[]{:S(2)}) copy-start(s32[8]{0:T(128)} %size_ref.1) | copy-start | bytes 100
  9.4 4.6 %copy-start.1 = (bf16[1024,1024]{1,0:T(8,128)(2,1)S(1)}, bf16[1024,1024]{1,0:T(8,128)(2,1)}, u32[]{:S(2)}) copy-start(bf16[1024,1024]{1,0:T(8,128)(2,1)} %refs_2_.5) | copy-start | bytes 6291460
  11.9 7.0 %collective-permute-start.4 = (bf16[136,1024]{1,0:T(8,128)(2,1)S(1)}, bf16[136,1024]{1,0:T(8,128)(2,1)S(1)}, u32[]{:S(2)}, u32[]{:S(2)}) collective-permute-start(bf16[136,1024]{1,0:T(8,128)(2,1)S(1)} %constant_dynamic-update-slice_fusion.refs_0_), channel_id=1, source_target_pairs={{0,2},{2,4},{4,6},{6,7},{7,5},{5,3},{3,1},{1,0},{8,10},{10,12},{12... | collective-permute-start | bytes 835592 | tf_op jit(solution)/shard_map/ppermute | solution.py:291
  13.5 7.0 %copy-start.5 = (bf16[128,1024]{1,0:T(8,128)(2,1)S(1)}, bf16[128,1024]{1,0:T(8,128)(2,1)}, u32[]{:S(2)}) copy-start(bf16[128,1024]{1,0:T(8,128)(2,1)} %param.5) | copy-start | bytes 786436
  13.5 7.0 %collective-permute-start.5 = (bf16[136,1024]{1,0:T(8,128)(2,1)S(1)}, bf16[136,1024]{1,0:T(8,128)(2,1)S(1)}, u32[]{:S(2)}, u32[]{:S(2)}) collective-permute-start(bf16[136,1024]{1,0:T(8,128)(2,1)S(1)} %constant_dynamic-update-slice_fusion.2.refs_1_), channel_id=1, source_target_pairs={{2,0},{4,2},{6,4},{7,6},{5,7},{3,5},{1,3},{0,1},{10,8},{12,10},{14... | collective-permute-start | bytes 835592 | tf_op jit(solution)/shard_map/ppermute | solution.py:294
  18.9 7.4 %collective-permute-start.6 = (bf16[136,1024]{1,0:T(8,128)(2,1)S(1)}, bf16[136,1024]{1,0:T(8,128)(2,1)S(1)}, u32[]{:S(2)}, u32[]{:S(2)}) collective-permute-start(bf16[136,1024]{1,0:T(8,128)(2,1)S(1)} %collective-permute-done.4.refs_0_.refs_2_), channel_id=1, source_target_pairs={{0,2},{2,4},{4,6},{6,7},{7,5},{5,3},{3,1},{1,0},{8,10},{10,12},{12... | collective-permute-start | bytes 835592 | tf_op jit(solution)/shard_map/ppermute | solution.py:291
  20.5 7.5 %collective-permute-start.7 = (bf16[136,1024]{1,0:T(8,128)(2,1)S(1)}, bf16[136,1024]{1,0:T(8,128)(2,1)S(1)}, u32[]{:S(2)}, u32[]{:S(2)}) collective-permute-start(bf16[136,1024]{1,0:T(8,128)(2,1)S(1)} %collective-permute-done.5.refs_1_.refs_3_), channel_id=1, source_target_pairs={{2,0},{4,2},{6,4},{7,6},{5,7},{3,5},{1,3},{0,1},{10,8},{12,10},{14... | collective-permute-start | bytes 835592 | tf_op jit(solution)/shard_map/ppermute | solution.py:294
  26.3 5.5 %collective-permute-start.8 = (bf16[88,1024]{1,0:T(8,128)(2,1)S(1)}, bf16[88,1024]{1,0:T(8,128)(2,1)S(1)}, u32[]{:S(2)}, u32[]{:S(2)}) collective-permute-start(bf16[88,1024]{1,0:T(8,128)(2,1)S(1)} %pad_maximum_fusion.3), channel_id=1, source_target_pairs={{0,2},{2,4},{4,6},{6,7},{7,5},{5,3},{3,1},{1,0},{8,10},{10,12},{12... | collective-permute-start | bytes 540680 | tf_op jit(solution)/shard_map/ppermute | solution.py:291
  28.0 4.7 %collective-permute-start.9 = (bf16[48,1024]{1,0:T(8,128)(2,1)S(1)}, bf16[48,1024]{1,0:T(8,128)(2,1)S(1)}, u32[]{:S(2)}, u32[]{:S(2)}) collective-permute-start(bf16[48,1024]{1,0:T(8,128)(2,1)S(1)} %slice.23), channel_id=1, source_target_pairs={{2,0},{4,2},{6,4},{7,6},{5,7},{3,5},{1,3},{0,1},{10,8},{12,10},{14... | collective-permute-start | bytes 294920 | tf_op jit(solution)/shard_map/ppermute | solution.py:294
  33.9 4.7 %collective-permute-start.17 = (bf16[48,1024]{1,0:T(8,128)(2,1)S(1)}, bf16[48,1024]{1,0:T(8,128)(2,1)S(1)}, u32[]{:S(2)}, u32[]{:S(2)}) collective-permute-start(bf16[48,1024]{1,0:T(8,128)(2,1)S(1)} %get-tuple-element.57), channel_id=1, source_target_pairs={{0,2},{2,4},{4,6},{6,7},{7,5},{5,3},{3,1},{1,0},{8,10},{10,12},{12... | collective-permute-start | bytes 294920 | tf_op jit(solution)/shard_map/ppermute | solution.py:291
  35.5 5.3 %collective-permute-start.13 = (bf16[80,1024]{1,0:T(8,128)(2,1)S(1)}, bf16[80,1024]{1,0:T(8,128)(2,1)S(1)}, u32[]{:S(2)}, u32[]{:S(2)}) collective-permute-start(bf16[80,1024]{1,0:T(8,128)(2,1)S(1)} %get-tuple-element.53), channel_id=1, source_target_pairs={{2,0},{4,2},{6,4},{7,6},{5,7},{3,5},{1,3},{0,1},{10,8},{12,10},{14... | collective-permute-start | bytes 491528 | tf_op jit(solution)/shard_map/ppermute | solution.py:294
  38.3 11.2 %collective-permute-start.11 = (bf16[1024,256]{1,0:T(8,128)(2,1)S(1)}, bf16[1024,256]{1,0:T(8,128)(2,1)S(1)}, u32[]{:S(2)}, u32[]{:S(2)}) collective-permute-start(bf16[1024,256]{1,0:T(8,128)(2,1)S(1)} %get-tuple-element.51), channel_id=1, source_target_pairs={{0,8},{8,0},{16,24},{24,16},{1,9},{9,1},{17,25},{25,17},{2,10},{10... | collective-permute-start | bytes 1572872 | tf_op jit(solution)/shard_map/ppermute | solution.py:331
  38.6 8.6 %collective-permute-start.18 = (bf16[128,1024]{1,0:T(8,128)(2,1)S(1)}, bf16[128,1024]{1,0:T(8,128)(2,1)S(1)}, u32[]{:S(2)}, u32[]{:S(2)}) collective-permute-start(bf16[128,1024]{1,0:T(8,128)(2,1)S(1)} %pad_maximum_fusion.2), channel_id=1, source_target_pairs={{0,2},{2,4},{4,6},{6,7},{7,5},{5,3},{3,1},{1,0},{8,10},{10,12},{12... | collective-permute-start | bytes 786440 | tf_op jit(solution)/shard_map/ppermute | solution.py:291
  40.9 8.0 %collective-permute-start.14 = (bf16[128,1024]{1,0:T(8,128)(2,1)S(1)}, bf16[128,1024]{1,0:T(8,128)(2,1)S(1)}, u32[]{:S(2)}, u32[]{:S(2)}) collective-permute-start(bf16[128,1024]{1,0:T(8,128)(2,1)S(1)} %pad_maximum_fusion.1), channel_id=1, source_target_pairs={{2,0},{4,2},{6,4},{7,6},{5,7},{3,5},{1,3},{0,1},{10,8},{12,10},{14... | collective-permute-start | bytes 786440 | tf_op jit(solution)/shard_map/ppermute | solution.py:294
  41.4 16.0 %collective-permute-start.10 = (bf16[1024,256]{1,0:T(8,128)(2,1)S(1)}, bf16[1024,256]{1,0:T(8,128)(2,1)S(1)}, u32[]{:S(2)}, u32[]{:S(2)}) collective-permute-start(bf16[1024,256]{1,0:T(8,128)(2,1)S(1)} %get-tuple-element.49), channel_id=1, source_target_pairs={{0,8},{8,0},{16,24},{24,16},{1,9},{9,1},{17,25},{25,17},{2,10},{10... | collective-permute-start | bytes 1572872 | tf_op jit(solution)/shard_map/ppermute | solution.py:331
  47.3 7.8 %collective-permute-start.19 = (bf16[128,1024]{1,0:T(8,128)(2,1)S(1)}, bf16[128,1024]{1,0:T(8,128)(2,1)S(1)}, u32[]{:S(2)}, u32[]{:S(2)}) collective-permute-start(bf16[128,1024]{1,0:T(8,128)(2,1)S(1)} %add_convert_fusion.2), channel_id=1, source_target_pairs={{0,2},{2,4},{4,6},{6,7},{7,5},{5,3},{3,1},{1,0},{8,10},{10,12},{12... | collective-permute-start | bytes 786440 | tf_op jit(solution)/shard_map/ppermute | solution.py:291
  49.0 7.8 %collective-permute-start.15 = (bf16[128,1024]{1,0:T(8,128)(2,1)S(1)}, bf16[128,1024]{1,0:T(8,128)(2,1)S(1)}, u32[]{:S(2)}, u32[]{:S(2)}) collective-permute-start(bf16[128,1024]{1,0:T(8,128)(2,1)S(1)} %add_convert_fusion.4), channel_id=1, source_target_pairs={{2,0},{4,2},{6,4},{7,6},{5,7},{3,5},{1,3},{0,1},{10,8},{12,10},{14... | collective-permute-start | bytes 786440 | tf_op jit(solution)/shard_map/ppermute | solution.py:294
  49.6 12.9 %collective-permute-start.12 = (bf16[1024,256]{1,0:T(8,128)(2,1)S(1)}, bf16[1024,256]{1,0:T(8,128)(2,1)S(1)}, u32[]{:S(2)}, u32[]{:S(2)}) collective-permute-start(bf16[1024,256]{1,0:T(8,128)(2,1)S(1)} %add_convert_fusion), channel_id=1, source_target_pairs={{0,16},{8,24},{16,0},{24,8},{1,17},{9,25},{17,1},{25,9},{2,18},{10... | collective-permute-start | bytes 1572872 | tf_op jit(solution)/shard_map/ppermute | solution.py:331
  55.2 7.5 %collective-permute-start.20 = (bf16[128,1024]{1,0:T(8,128)(2,1)S(1)}, bf16[128,1024]{1,0:T(8,128)(2,1)S(1)}, u32[]{:S(2)}, u32[]{:S(2)}) collective-permute-start(bf16[128,1024]{1,0:T(8,128)(2,1)S(1)} %add_convert_fusion.1), channel_id=1, source_target_pairs={{0,2},{2,4},{4,6},{6,7},{7,5},{5,3},{3,1},{1,0},{8,10},{10,12},{12... | collective-permute-start | bytes 786440 | tf_op jit(solution)/shard_map/ppermute | solution.py:291
  56.9 6.6 %collective-permute-start.16 = (bf16[128,1024]{1,0:T(8,128)(2,1)S(1)}, bf16[128,1024]{1,0:T(8,128)(2,1)S(1)}, u32[]{:S(2)}, u32[]{:S(2)}) collective-permute-start(bf16[128,1024]{1,0:T(8,128)(2,1)S(1)} %add_convert_fusion.3), channel_id=1, source_target_pairs={{2,0},{4,2},{6,4},{7,6},{5,7},{3,5},{1,3},{0,1},{10,8},{12,10},{14... | collective-permute-start | bytes 786440 | tf_op jit(solution)/shard_map/ppermute | solution.py:294

commit v15 on v14

--- a/solution.py
+++ b/solution.py
@@ -206,19 +206,14 @@
     return total.astype(jnp.bfloat16)
 
 
-def total_of(refs, at):
-    total = refs[0][at, :].astype(jnp.float32)
-    for ref in refs[1:]:
-        total = total + ref[at, :].astype(jnp.float32)
-    return total.astype(jnp.bfloat16)
-
-
 def sum_kernel(*refs):
-    *in_refs, out_ref = refs
-    out_ref[...] = total_of(in_refs, slice(None))
-
-
-def weight_sum(parts):
+    total = refs[0][...].astype(jnp.float32)
+    for ref in refs[1:-1]:
+        total = total + ref[...].astype(jnp.float32)
+    refs[-1][...] = total.astype(jnp.bfloat16)
+
+
+def kernel_sum(*parts):
     return pl.pallas_call(
         sum_kernel,
         out_shape=jax.ShapeDtypeStruct(parts[0].shape, jnp.bfloat16),
@@ -229,46 +224,48 @@
             bytes_accessed=2 * (len(parts) + 1) * parts[0].size,
             transcendentals=0,
         ),
-        name="weight_sum",
+        name="kernel_sum",
     )(*parts)
 
 
-def final_kernel(pieces, weight_ref, *refs):
+def final_kernel(weight_ref, own_ref, *refs):
     *in_refs, feature_out, weight_out, held, sems = refs
+    pieces = len(in_refs) // 2
     copies = [pltpu.make_async_copy(weight_ref, weight_out, sems.at[pieces])]
     copies[0].start()
     rows = held.shape[0] // pieces
     for p in range(pieces):
         at = pl.ds(p * rows, rows)
-        held[at, :] = total_of(in_refs, at)
+        total = own_ref[at, :].astype(jnp.float32) + in_refs[p][...].astype(jnp.float32)
+        held[at, :] = (total + in_refs[pieces + p][...].astype(jnp.float32)).astype(jnp.bfloat16)
         copies.append(pltpu.make_async_copy(held.at[at], feature_out.at[at], sems.at[p]))
         copies[-1].start()
     for copy in copies:
         copy.wait()
 
 
-def finish(weight_grad, parts, pieces):
-    shape = parts[0].shape
-    return pl.pallas_call(
-        functools.partial(final_kernel, pieces),
+def finish(weight_grad, own_grad, from_above, from_below):
+    shape = own_grad.shape
+    return pl.pallas_call(
+        final_kernel,
         out_shape=[
             jax.ShapeDtypeStruct(shape, jnp.bfloat16),
             jax.ShapeDtypeStruct(weight_grad.shape, jnp.bfloat16),
         ],
-        in_specs=[pl.BlockSpec(memory_space=pltpu.VMEM)] * (len(parts) + 1),
+        in_specs=[pl.BlockSpec(memory_space=pltpu.VMEM)] * (2 + 2 * len(from_above)),
         out_specs=[pl.BlockSpec(memory_space=pl.ANY)] * 2,
         scratch_shapes=[
             pltpu.VMEM(shape, jnp.bfloat16),
-            pltpu.SemaphoreType.DMA((pieces + 1,)),
+            pltpu.SemaphoreType.DMA((len(from_above) + 1,)),
         ],
         compiler_params=pltpu.CompilerParams(vmem_limit_bytes=VMEM_LIMIT),
         cost_estimate=pl.CostEstimate(
-            flops=len(parts) * parts[0].size,
-            bytes_accessed=2 * (len(parts) + 1) * parts[0].size + 4 * weight_grad.size,
+            flops=3 * own_grad.size,
+            bytes_accessed=8 * own_grad.size + 4 * weight_grad.size,
             transcendentals=0,
         ),
         name="finish",
-    )(weight_grad, *parts)
+    )(weight_grad, own_grad, *from_above, *from_below)
 
 
 def after(array, *others):
@@ -281,7 +278,7 @@
     clus_count, seq_count = lax.axis_size("clus"), lax.axis_size("seq")
     local_count = cluster_sizes.shape[0]
     part_width = width // seq_count
-    split, steps = inst_rows * 5 // 8, clus_count // 2
+    split, steps = inst_rows // 2, clus_count // 2
 
     ring = list(range(0, clus_count, 2)) + list(range(1, clus_count, 2))[::-1]
     up = list(zip(ring, ring[1:] + ring[:1]))
@@ -340,15 +337,22 @@
             terms[q ^ bit].append(seq_send(add(*values) if len(values) > 1 else values[0], bit))
         bit *= 2
 
-    for k in range(steps, 0, -1):
-        from_above, from_below = send_down(to_down), send_up(to_up)
-        if k == steps:
-            near_below, near_above = below_grad[k - 1], above_grad[k - 1]
-            to_down = jnp.concatenate([add(near_below[:split], from_above), near_below[split:]], axis=0)
-            to_up = jnp.concatenate([near_above[:split], add(near_above[split:], from_below)], axis=0)
-        elif k > 1:
-            to_down, to_up = add(below_grad[k - 1], from_above), add(above_grad[k - 1], from_below)
-    feature_grad, weight_grad = finish(weight_sum(terms[0]), [own_grad, from_above, from_below], 2)
+    last = steps - 1
+
+    def halves(array):
+        return array[:split], array[split:]
+
+    from_above, from_below = send_down(to_down), send_up(to_up)
+    low, high = halves(below_grad[last])
+    going_down = [kernel_sum(low, from_above), after(high, to_down, to_up)]
+    low, high = halves(above_grad[last])
+    going_up = [after(low, to_down, to_up), kernel_sum(high, from_below)]
+    for k in range(last, 0, -1):
+        from_above, from_below = [send_down(part) for part in going_down], [send_up(part) for part in going_up]
+        if k > 1:
+            going_down = [kernel_sum(*pair) for pair in zip(halves(below_grad[k - 1]), from_above)]
+            going_up = [kernel_sum(*pair) for pair in zip(halves(above_grad[k - 1]), from_below)]
+    feature_grad, weight_grad = finish(kernel_sum(*terms[0]), own_grad, from_above, from_below)
     return (feature_grad, weight_grad)
 
 

time: 64.6 us -> 69.6 us (1.077)
  starting transfers between devices: 21.6 us -> 27.6 us
  waiting for transfers between devices: 26.7 us -> 25.6 us
    ppermute x9 -> x12, waiting for transfers between devices: 3.63 us -> 11.2 us  [send_down(): return lax.ppermute(array, 'clus', down)]
    ppermute x3, waiting for transfers between devices: 5.14 us -> 0.01 us  [seq_send(): return lax.ppermute(array, 'seq', [(k, k ^ bit) for k in range(seq_count)])]
    ppermute x9 -> x12, starting transfers between devices: 3.49 us -> 7.12 us  [send_down(): return lax.ppermute(array, 'clus', down)]
    ppermute x9 -> x12, waiting for transfers between devices: 17.9 us -> 14.4 us  [send_up(): return lax.ppermute(array, 'clus', up)]
    ppermute x9 -> x12, starting transfers between devices: 16.4 us -> 18.8 us  [send_up(): return lax.ppermute(array, 'clus', up)]
    pallas_call x2 -> x12, Pallas kernels: 1.09 us -> 1.42 us  [the longest x1 0.9 us: finish(): pl.pallas_call(final_kernel, out_shape=[jax.ShapeDtypeStruct(shape, jnp.b...]
  transfers between devices with their start and end apart: 21 -> 27, of which waited for: 12 -> 16; matrix products, arithmetic and copies ran while one was open for 1% -> 0% of each run, Pallas kernels for 14% -> 10%
where the time goes in v15:
time: 69.6 us; the launch traced here: 69.4 us
  starting transfers between devices  27.6 us (40%)
  waiting for transfers between devices  25.6 us (37%)
  Pallas kernels  11.4 us (16%)
  local copies, waits for them, and re-layouts  3.81 us (5%)
  between operations  0.89 us (1%)
    ppermute x12, starting transfers between devices, send_up(): return lax.ppermute(array, 'clus', up)  18.8 us
    ppermute x12, waiting for transfers between devices, send_up(): return lax.ppermute(array, 'clus', up)  14.4 us
    ppermute x12, waiting for transfers between devices, send_down(): return lax.ppermute(array, 'clus', down)  11.2 us
    ppermute x12, starting transfers between devices, send_down(): return lax.ppermute(array, 'clus', down)  7.12 us
    pallas_call x4, Pallas kernels, block_work(): pl.pallas_call(functools.partial(block_kernel, piece_rows, top_count, pos...  6.98 us
    unnamed x14, local copies, waits for them, and re-layouts  3.67 us
    pallas_call x1, Pallas kernels, weight_work(): pl.pallas_call(functools.partial(weight_kernel, piece_rows, column_blocks...  2.38 us
    ppermute x3, starting transfers between devices, seq_send(): return lax.ppermute(array, 'seq', [(k, k ^ bit) for k in range(seq_count)])  1.64 us
  transfers between devices with their start and end apart: 27, of which 16 were waited for; matrix products, arithmetic and copies ran while one was open for 0% of the time, Pallas kernels for 10%

profile of v15, /device:TPU:0, one launch (start us, length us, event | category | flops | bytes accessed | tf_op | source)
XLA Modules:
  0.0 69.4 jit_solution(8559915118510930035)
XLA Ops:
  0.6 3.1 %collective-permute-start = (bf16[128,1024]{1,0:T(8,128)(2,1)}, bf16[128,1024]{1,0:T(8,128)(2,1)S(1)}, u32[]{:S(2)}, u32[]{:S(2)}) collective-permute-start(bf16[128,1024]{1,0:T(8,128)(2,1)} %param.5), channel_id=1, source_target_pairs={{0,2},{2,4},{4,6},{6,7},{7,5},{5,3},{3,1},{1,0},{8,10},{10,12},{12... | collective-permute-start | bytes 786440 | tf_op jit(solution)/shard_map/ppermute | solution.py:288
  5.1 2.1 %collective-permute-start.1 = (bf16[8,1024]{1,0:T(8,128)(2,1)S(1)}, bf16[8,1024]{1,0:T(8,128)(2,1)S(1)}, u32[]{:S(2)}, u32[]{:S(2)}) collective-permute-start(bf16[8,1024]{1,0:T(8,128)(2,1)S(1)} %instance_ids.1), channel_id=1, source_target_pairs={{0,2},{2,4},{4,6},{6,7},{7,5},{5,3},{3,1},{1,0},{8,10},{10,12},{12... | collective-permute-start | bytes 49160 | tf_op jit(solution)/shard_map/ppermute | solution.py:288
  7.2 1.6 %copy-done = bf16[1024,1024]{1,0:T(8,128)(2,1)S(1)} copy-done((bf16[1024,1024]{1,0:T(8,128)(2,1)S(1)}, bf16[1024,1024]{1,0:T(8,128)(2,1)}, u32[]{:S(2)}) %copy-start) | copy-done | bytes 2097176
  10.4 1.5 %collective-permute-done.2 = bf16[128,1024]{1,0:T(8,128)(2,1)S(1)} collective-permute-done((bf16[128,1024]{1,0:T(8,128)(2,1)}, bf16[128,1024]{1,0:T(8,128)(2,1)S(1)}, u32[]{:S(2)}, u32[]{:S(2)}) %collective-permute-start.2) | collective-permute-done | bytes 262176 | tf_op jit(solution)/shard_map/ppermute | solution.py:291
  11.9 1.6 %collective-permute-start.4 = (bf16[136,1024]{1,0:T(8,128)(2,1)S(1)}, bf16[136,1024]{1,0:T(8,128)(2,1)S(1)}, u32[]{:S(2)}, u32[]{:S(2)}) collective-permute-start(bf16[136,1024]{1,0:T(8,128)(2,1)S(1)} %constant_dynamic-update-slice_fusion.refs_0_), channel_id=1, source_target_pairs={{0,2},{2,4},{4,6},{6,7},{7,5},{5,3},{3,1},{1,0},{8,10},{10,12},{12... | collective-permute-start | bytes 835592 | tf_op jit(solution)/shard_map/ppermute | solution.py:288
  14.0 1.7 %block_work.4 = (bf16[128,1024]{1,0:T(8,128)(2,1)S(1)}, bf16[128,1024]{1,0:T(8,128)(2,1)S(1)}, bf16[128,1024]{1,0:T(8,128)(2,1)S(1)}, bf16[128,1024]{1,0:T(8,128)(2,1)S(1)}) custom-call(bf16[136,1024]{1,0:T(8,128)(2,1)S(1)} %constant_dynamic-update-slice_fusion.refs_0_, bf16[136,1024]{1,0:T(8,128)(2,1)S(1)} %constant_dynamic-update-slice_fusion.2.refs_1_, ...), custom_call_target="tpu_custom_call" | custom-call | flops 1073741824 | bytes 3670016 | tf_op jit(solution)/shard_map/block_work/pallas_call | solution.py:146
  15.7 3.3 %collective-permute-done.4.refs_0_.refs_2_ = bf16[136,1024]{1,0:T(8,128)(2,1)S(1)} collective-permute-done((bf16[136,1024]{1,0:T(8,128)(2,1)S(1)}, bf16[136,1024]{1,0:T(8,128)(2,1)S(1)}, u32[]{:S(2)}, u32[]{:S(2)}) %collective-permute-start.4) | collective-permute-done | bytes 278560 | tf_op jit(solution)/shard_map/ppermute | solution.py:288
  19.0 1.6 %collective-permute-start.6 = (bf16[136,1024]{1,0:T(8,128)(2,1)S(1)}, bf16[136,1024]{1,0:T(8,128)(2,1)S(1)}, u32[]{:S(2)}, u32[]{:S(2)}) collective-permute-start(bf16[136,1024]{1,0:T(8,128)(2,1)S(1)} %collective-permute-done.4.refs_0_.refs_2_), channel_id=1, source_target_pairs={{0,2},{2,4},{4,6},{6,7},{7,5},{5,3},{3,1},{1,0},{8,10},{10,12},{12... | collective-permute-start | bytes 835592 | tf_op jit(solution)/shard_map/ppermute | solution.py:288
  21.1 2.4 %block_work.5 = (bf16[128,1024]{1,0:T(8,128)(2,1)S(1)}, bf16[128,1024]{1,0:T(8,128)(2,1)S(1)}, bf16[128,1024]{1,0:T(8,128)(2,1)S(1)}, bf16[128,1024]{1,0:T(8,128...) custom-call(bf16[136,1024]{1,0:T(8,128)(2,1)S(1)} %collective-permute-done.4.refs_0_.refs_2_, ...), custom_call_target="tpu_custom_call" | custom-call | flops 1610612736 | bytes 4456448 | tf_op jit(solution)/shard_map/block_work/pallas_call | solution.py:146
  23.5 2.1 %collective-permute-done.6.refs_0_.refs_5_ = bf16[136,1024]{1,0:T(8,128)(2,1)S(1)} collective-permute-done((bf16[136,1024]{1,0:T(8,128)(2,1)S(1)}, bf16[136,1024]{1,0:T(8,128)(2,1)S(1)}, u32[]{:S(2)}, u32[]{:S(2)}) %collective-permute-start.6) | collective-permute-done | bytes 278560 | tf_op jit(solution)/shard_map/ppermute | solution.py:288
  25.6 1.6 %collective-permute-done.7.refs_1_.refs_6_ = bf16[136,1024]{1,0:T(8,128)(2,1)S(1)} collective-permute-done((bf16[136,1024]{1,0:T(8,128)(2,1)S(1)}, bf16[136,1024]{1,0:T(8,128)(2,1)S(1)}, u32[]{:S(2)}, u32[]{:S(2)}) %collective-permute-start.7) | collective-permute-done | bytes 278560 | tf_op jit(solution)/shard_map/ppermute | solution.py:291
  27.1 1.6 %collective-permute-start.8 = (bf16[72,1024]{1,0:T(8,128)(2,1)S(1)}, bf16[72,1024]{1,0:T(8,128)(2,1)S(1)}, u32[]{:S(2)}, u32[]{:S(2)}) collective-permute-start(bf16[72,1024]{1,0:T(8,128)(2,1)S(1)} %pad_maximum_fusion.1), channel_id=1, source_target_pairs={{0,2},{2,4},{4,6},{6,7},{7,5},{5,3},{3,1},{1,0},{8,10},{10,12},{12... | collective-permute-start | bytes 442376 | tf_op jit(solution)/shard_map/ppermute | solution.py:288
  29.3 1.7 %block_work.6 = (bf16[128,1024]{1,0:T(8,128)(2,1)S(1)}, bf16[128,1024]{1,0:T(8,128)(2,1)S(1)}, bf16[128,1024]{1,0:T(8,128)(2,1)S(1)}, bf16[128,1024]{1,0:T(8,128)(2,1)S(1)}) custom-call(bf16[136,1024]{1,0:T(8,128)(2,1)S(1)} %collective-permute-done.6.refs_0_.refs_5_, bf16[136,1024]{1,0:T(8,128)(2,1)S(1)} %collective-permute-done.7.refs_1_.refs_6_, ...), custom_call_target="tpu_custom_call" | custom-call | flops 1073741824 | bytes 3670016 | tf_op jit(solution)/shard_map/block_work/pallas_call | solution.py:146
  31.0 1.3 %collective-permute-done.8.refs_0_.refs_7_ = bf16[72,1024]{1,0:T(8,128)(2,1)S(1)} collective-permute-done((bf16[72,1024]{1,0:T(8,128)(2,1)S(1)}, bf16[72,1024]{1,0:T(8,128)(2,1)S(1)}, u32[]{:S(2)}, u32[]{:S(2)}) %collective-permute-start.8) | collective-permute-done | bytes 147488 | tf_op jit(solution)/shard_map/ppermute | solution.py:288
  32.3 1.5 %collective-permute-done.9.refs_1_.refs_8_ = bf16[64,1024]{1,0:T(8,128)(2,1)S(1)} collective-permute-done((bf16[64,1024]{1,0:T(8,128)(2,1)S(1)}, bf16[64,1024]{1,0:T(8,128)(2,1)S(1)}, u32[]{:S(2)}, u32[]{:S(2)}) %collective-permute-start.9) | collective-permute-done | bytes 131104 | tf_op jit(solution)/shard_map/ppermute | solution.py:291
  33.8 1.2 %block_work.7 = (bf16[64,1024]{1,0:T(8,128)(2,1)S(1)}, bf16[64,1024]{1,0:T(8,128)(2,1)S(1)}, bf16[128,1024]{1,0:T(8,128)(2,1)S(1)}) custom-call(bf16[72,1024]{1,0:T(8,128)(2,1)S(1)} %collective-permute-done.8.refs_0_.refs_7_, bf16[64,1024]{1,0:T(8,128)(2,1)S(1)} %collective-permute-done.9.refs_1_.refs_8_, bf16[1024,1024]{1,0:T(8,128)(2,1)S(1)} %copy-done.1, ...), custom_call_target="tpu_custom_call" | custom-call | flops 536870912 | bytes 2883584 | tf_op jit(solution)/shard_map/block_work/pallas_call | solution.py:146
  35.0 2.4 %weight_work.1 = (bf16[1024,256]{1,0:T(8,128)(2,1)S(1)}, bf16[1024,256]{1,0:T(8,128)(2,1)S(1)}, bf16[1024,256]{1,0:T(8,128)(2,1)S(1)}, bf16[1024,256]{1,0:T(8,128)(2,1)S(1)}) custom-call(bf16[136,1024]{1,0:T(8,128)(2,1)S(1)} %constant_dynamic-update-slice_fusion.refs_0_, bf16[136,1024]{1,0:T(8,128)(2,1)S(1)} %constant_dynamic-update-slice_fusion.2.refs_1_, ...), custom_call_target="tpu_custom_call" | custom-call | flops 2147483648 | bytes 4718592 | tf_op jit(solution)/shard_map/weight_work/pallas_call | solution.py:188
  37.5 1.6 %collective-permute-start.23 = (bf16[64,1024]{1,0:T(8,128)(2,1)S(1)}, bf16[64,1024]{1,0:T(8,128)(2,1)S(1)}, u32[]{:S(2)}, u32[]{:S(2)}) collective-permute-start(bf16[64,1024]{1,0:T(8,128)(2,1)S(1)} %get-tuple-element.56), channel_id=1, source_target_pairs={{0,2},{2,4},{4,6},{6,7},{7,5},{5,3},{3,1},{1,0},{8,10},{10,12},{12... | collective-permute-start | bytes 393224 | tf_op jit(solution)/shard_map/ppermute | solution.py:288
  39.6 1.5 %collective-permute-start.20 = (bf16[64,1024]{1,0:T(8,128)(2,1)S(1)}, bf16[64,1024]{1,0:T(8,128)(2,1)S(1)}, u32[]{:S(2)}, u32[]{:S(2)}) collective-permute-start(bf16[64,1024]{1,0:T(8,128)(2,1)S(1)} %get-tuple-element.61), channel_id=1, source_target_pairs={{0,2},{2,4},{4,6},{6,7},{7,5},{5,3},{3,1},{1,0},{8,10},{10,12},{12... | collective-permute-start | bytes 393224 | tf_op jit(solution)/shard_map/ppermute | solution.py:288
  41.7 2.2 %collective-permute-done.23.refs_1_ = bf16[64,1024]{1,0:T(8,128)(2,1)S(1)} collective-permute-done((bf16[64,1024]{1,0:T(8,128)(2,1)S(1)}, bf16[64,1024]{1,0:T(8,128)(2,1)S(1)}, u32[]{:S(2)}, u32[]{:S(2)}) %collective-permute-start.23) | collective-permute-done | bytes 131104 | tf_op jit(solution)/shard_map/ppermute | solution.py:288
  43.9 2.4 %collective-permute-done.20.refs_1_ = bf16[64,1024]{1,0:T(8,128)(2,1)S(1)} collective-permute-done((bf16[64,1024]{1,0:T(8,128)(2,1)S(1)}, bf16[64,1024]{1,0:T(8,128)(2,1)S(1)}, u32[]{:S(2)}, u32[]{:S(2)}) %collective-permute-start.20) | collective-permute-done | bytes 131104 | tf_op jit(solution)/shard_map/ppermute | solution.py:288
  46.3 1.5 %collective-permute-start.24 = (bf16[64,1024]{1,0:T(8,128)(2,1)S(1)}, bf16[64,1024]{1,0:T(8,128)(2,1)S(1)}, u32[]{:S(2)}, u32[]{:S(2)}) collective-permute-start(bf16[64,1024]{1,0:T(8,128)(2,1)S(1)} %kernel_sum.19), channel_id=1, source_target_pairs={{0,2},{2,4},{4,6},{6,7},{7,5},{5,3},{3,1},{1,0},{8,10},{10,12},{12... | collective-permute-start | bytes 393224 | tf_op jit(solution)/shard_map/ppermute | solution.py:288
  47.8 1.1 %collective-permute-start.21 = (bf16[64,1024]{1,0:T(8,128)(2,1)S(1)}, bf16[64,1024]{1,0:T(8,128)(2,1)S(1)}, u32[]{:S(2)}, u32[]{:S(2)}) collective-permute-start(bf16[64,1024]{1,0:T(8,128)(2,1)S(1)} %kernel_sum.17), channel_id=1, source_target_pairs={{0,2},{2,4},{4,6},{6,7},{7,5},{5,3},{3,1},{1,0},{8,10},{10,12},{12... | collective-permute-start | bytes 393224 | tf_op jit(solution)/shard_map/ppermute | solution.py:288
  50.2 1.6 %collective-permute-start.12 = (bf16[1024,256]{1,0:T(8,128)(2,1)S(1)}, bf16[1024,256]{1,0:T(8,128)(2,1)S(1)}, u32[]{:S(2)}, u32[]{:S(2)}) collective-permute-start(bf16[1024,256]{1,0:T(8,128)(2,1)S(1)} %add_convert_fusion), channel_id=1, source_target_pairs={{0,16},{8,24},{16,0},{24,8},{1,17},{9,25},{17,1},{25,9},{2,18},{10... | collective-permute-start | bytes 1572872 | tf_op jit(solution)/shard_map/ppermute | solution.py:328
  53.2 2.0 %collective-permute-done.14.refs_1_ = bf16[64,1024]{1,0:T(8,128)(2,1)S(1)} collective-permute-done((bf16[64,1024]{1,0:T(8,128)(2,1)S(1)}, bf16[64,1024]{1,0:T(8,128)(2,1)S(1)}, u32[]{:S(2)}, u32[]{:S(2)}) %collective-permute-start.14) | collective-permute-done | bytes 131104 | tf_op jit(solution)/shard_map/ppermute | solution.py:291
  55.2 2.1 %collective-permute-start.15 = (bf16[64,1024]{1,0:T(8,128)(2,1)S(1)}, bf16[64,1024]{1,0:T(8,128)(2,1)S(1)}, u32[]{:S(2)}, u32[]{:S(2)}) collective-permute-start(bf16[64,1024]{1,0:T(8,128)(2,1)S(1)} %kernel_sum.13), channel_id=1, source_target_pairs={{2,0},{4,2},{6,4},{7,6},{5,7},{3,5},{1,3},{0,1},{10,8},{12,10},{14... | collective-permute-start | bytes 393224 | tf_op jit(solution)/shard_map/ppermute | solution.py:291
  57.3 1.1 %collective-permute-done.18.refs_1_ = bf16[64,1024]{1,0:T(8,128)(2,1)S(1)} collective-permute-done((bf16[64,1024]{1,0:T(8,128)(2,1)S(1)}, bf16[64,1024]{1,0:T(8,128)(2,1)S(1)}, u32[]{:S(2)}, u32[]{:S(2)}) %collective-permute-start.18) | collective-permute-done | bytes 131104 | tf_op jit(solution)/shard_map/ppermute | solution.py:291
  58.4 1.6 %collective-permute-start.22 = (bf16[64,1024]{1,0:T(8,128)(2,1)S(1)}, bf16[64,1024]{1,0:T(8,128)(2,1)S(1)}, u32[]{:S(2)}, u32[]{:S(2)}) collective-permute-start(bf16[64,1024]{1,0:T(8,128)(2,1)S(1)} %kernel_sum.18), channel_id=1, source_target_pairs={{0,2},{2,4},{4,6},{6,7},{7,5},{5,3},{3,1},{1,0},{8,10},{10,12},{12... | collective-permute-start | bytes 393224 | tf_op jit(solution)/shard_map/ppermute | solution.py:288
  60.0 1.3 %collective-permute-done.25.refs_1_ = bf16[64,1024]{1,0:T(8,128)(2,1)S(1)} collective-permute-done((bf16[64,1024]{1,0:T(8,128)(2,1)S(1)}, bf16[64,1024]{1,0:T(8,128)(2,1)S(1)}, u32[]{:S(2)}, u32[]{:S(2)}) %collective-permute-start.25) | collective-permute-done | bytes 131104 | tf_op jit(solution)/shard_map/ppermute | solution.py:288
  61.9 1.5 %collective-permute-start.26 = (bf16[64,1024]{1,0:T(8,128)(2,1)S(1)}, bf16[64,1024]{1,0:T(8,128)(2,1)S(1)}, u32[]{:S(2)}, u32[]{:S(2)}) collective-permute-start(bf16[64,1024]{1,0:T(8,128)(2,1)S(1)} %kernel_sum.21), channel_id=1, source_target_pairs={{0,2},{2,4},{4,6},{6,7},{7,5},{5,3},{3,1},{1,0},{8,10},{10,12},{12... | collective-permute-start | bytes 393224 | tf_op jit(solution)/shard_map/ppermute | solution.py:288
  64.3 2.0 %collective-permute-done.19.refs_1_ = bf16[64,1024]{1,0:T(8,128)(2,1)S(1)} collective-permute-done((bf16[64,1024]{1,0:T(8,128)(2,1)S(1)}, bf16[64,1024]{1,0:T(8,128)(2,1)S(1)}, u32[]{:S(2)}, u32[]{:S(2)}) %collective-permute-start.19) | collective-permute-done | bytes 131104 | tf_op jit(solution)/shard_map/ppermute | solution.py:291
  66.9 1.6 %collective-permute-done.16.refs_0_ = bf16[64,1024]{1,0:T(8,128)(2,1)S(1)} collective-permute-done((bf16[64,1024]{1,0:T(8,128)(2,1)S(1)}, bf16[64,1024]{1,0:T(8,128)(2,1)S(1)}, u32[]{:S(2)}, u32[]{:S(2)}) %collective-permute-start.16) | collective-permute-done | bytes 131104 | tf_op jit(solution)/shard_map/ppermute | solution.py:291
  (69 shorter events, 11.4 us)
Async XLA Ops:
  0.6 9.7 %collective-permute-start = (bf16[128,1024]{1,0:T(8,128)(2,1)}, bf16[128,1024]{1,0:T(8,128)(2,1)S(1)}, u32[]{:S(2)}, u32[]{:S(2)}) collective-permute-start(bf16[128,1024]{1,0:T(8,128)(2,1)} %param.5), channel_id=1, source_target_pairs={{0,2},{2,4},{4,6},{6,7},{7,5},{5,3},{3,1},{1,0},{8,10},{10,12},{12... | collective-permute-start | bytes 786440 | tf_op jit(solution)/shard_map/ppermute | solution.py:288
  3.7 8.2 %collective-permute-start.2 = (bf16[128,1024]{1,0:T(8,128)(2,1)}, bf16[128,1024]{1,0:T(8,128)(2,1)S(1)}, u32[]{:S(2)}, u32[]{:S(2)}) collective-permute-start(bf16[128,1024]{1,0:T(8,128)(2,1)} %param.5), channel_id=1, source_target_pairs={{2,0},{4,2},{6,4},{7,6},{5,7},{3,5},{1,3},{0,1},{10,8},{12,10},{14... | collective-permute-start | bytes 786440 | tf_op jit(solution)/shard_map/ppermute | solution.py:291
  3.7 0.7 %copy-start.2 = (s32[128,16]{0,1:T(8,128)S(1)}, s32[128,16]{0,1:T(8,128)}, u32[]{:S(2)}) copy-start(s32[128,16]{0,1:T(8,128)} %param.6) | copy-start | bytes 24580
  4.4 0.7 copy-start.3
  5.1 6.8 %collective-permute-start.1 = (bf16[8,1024]{1,0:T(8,128)(2,1)S(1)}, bf16[8,1024]{1,0:T(8,128)(2,1)S(1)}, u32[]{:S(2)}, u32[]{:S(2)}) collective-permute-start(bf16[8,1024]{1,0:T(8,128)(2,1)S(1)} %instance_ids.1), channel_id=1, source_target_pairs={{0,2},{2,4},{4,6},{6,7},{7,5},{5,3},{3,1},{1,0},{8,10},{10,12},{12... | collective-permute-start | bytes 49160 | tf_op jit(solution)/shard_map/ppermute | solution.py:288
  7.2 6.4 %collective-permute-start.3 = (bf16[8,1024]{1,0:T(8,128)(2,1)S(1)}, bf16[8,1024]{1,0:T(8,128)(2,1)S(1)}, u32[]{:S(2)}, u32[]{:S(2)}) collective-permute-start(bf16[8,1024]{1,0:T(8,128)(2,1)S(1)} %instance_ids.1), channel_id=1, source_target_pairs={{2,0},{4,2},{6,4},{7,6},{5,7},{3,5},{1,3},{0,1},{10,8},{12,10},{14... | collective-permute-start | bytes 49160 | tf_op jit(solution)/shard_map/ppermute | solution.py:291
  7.2 1.6 %copy-start = (bf16[1024,1024]{1,0:T(8,128)(2,1)S(1)}, bf16[1024,1024]{1,0:T(8,128)(2,1)}, u32[]{:S(2)}) copy-start(bf16[1024,1024]{1,0:T(8,128)(2,1)} %refs_2_.5) | copy-start | bytes 6291460
  9.4 4.6 %copy-start.1 = (bf16[1024,1024]{1,0:T(8,128)(2,1)S(1)}, bf16[1024,1024]{1,0:T(8,128)(2,1)}, u32[]{:S(2)}) copy-start(bf16[1024,1024]{1,0:T(8,128)(2,1)} %refs_2_.5) | copy-start | bytes 6291460
  11.9 9.2 %copy-start.5 = (bf16[128,1024]{1,0:T(8,128)(2,1)S(1)}, bf16[128,1024]{1,0:T(8,128)(2,1)}, u32[]{:S(2)}) copy-start(bf16[128,1024]{1,0:T(8,128)(2,1)} %param.5) | copy-start | bytes 786436
  11.9 7.1 %collective-permute-start.4 = (bf16[136,1024]{1,0:T(8,128)(2,1)S(1)}, bf16[136,1024]{1,0:T(8,128)(2,1)S(1)}, u32[]{:S(2)}, u32[]{:S(2)}) collective-permute-start(bf16[136,1024]{1,0:T(8,128)(2,1)S(1)} %constant_dynamic-update-slice_fusion.refs_0_), channel_id=1, source_target_pairs={{0,2},{2,4},{4,6},{6,7},{7,5},{5,3},{3,1},{1,0},{8,10},{10,12},{12... | collective-permute-start | bytes 835592 | tf_op jit(solution)/shard_map/ppermute | solution.py:288
  13.5 7.0 %collective-permute-start.5 = (bf16[136,1024]{1,0:T(8,128)(2,1)S(1)}, bf16[136,1024]{1,0:T(8,128)(2,1)S(1)}, u32[]{:S(2)}, u32[]{:S(2)}) collective-permute-start(bf16[136,1024]{1,0:T(8,128)(2,1)S(1)} %constant_dynamic-update-slice_fusion.2.refs_1_), channel_id=1, source_target_pairs={{2,0},{4,2},{6,4},{7,6},{5,7},{3,5},{1,3},{0,1},{10,8},{12,10},{14... | collective-permute-start | bytes 835592 | tf_op jit(solution)/shard_map/ppermute | solution.py:291
  19.0 6.5 %collective-permute-start.6 = (bf16[136,1024]{1,0:T(8,128)(2,1)S(1)}, bf16[136,1024]{1,0:T(8,128)(2,1)S(1)}, u32[]{:S(2)}, u32[]{:S(2)}) collective-permute-start(bf16[136,1024]{1,0:T(8,128)(2,1)S(1)} %collective-permute-done.4.refs_0_.refs_2_), channel_id=1, source_target_pairs={{0,2},{2,4},{4,6},{6,7},{7,5},{5,3},{3,1},{1,0},{8,10},{10,12},{12... | collective-permute-start | bytes 835592 | tf_op jit(solution)/shard_map/ppermute | solution.py:288
  20.6 6.5 %collective-permute-start.7 = (bf16[136,1024]{1,0:T(8,128)(2,1)S(1)}, bf16[136,1024]{1,0:T(8,128)(2,1)S(1)}, u32[]{:S(2)}, u32[]{:S(2)}) collective-permute-start(bf16[136,1024]{1,0:T(8,128)(2,1)S(1)} %collective-permute-done.5.refs_1_.refs_3_), channel_id=1, source_target_pairs={{2,0},{4,2},{6,4},{7,6},{5,7},{3,5},{1,3},{0,1},{10,8},{12,10},{14... | collective-permute-start | bytes 835592 | tf_op jit(solution)/shard_map/ppermute | solution.py:291
  27.1 5.2 %collective-permute-start.8 = (bf16[72,1024]{1,0:T(8,128)(2,1)S(1)}, bf16[72,1024]{1,0:T(8,128)(2,1)S(1)}, u32[]{:S(2)}, u32[]{:S(2)}) collective-permute-start(bf16[72,1024]{1,0:T(8,128)(2,1)S(1)} %pad_maximum_fusion.1), channel_id=1, source_target_pairs={{0,2},{2,4},{4,6},{6,7},{7,5},{5,3},{3,1},{1,0},{8,10},{10,12},{12... | collective-permute-start | bytes 442376 | tf_op jit(solution)/shard_map/ppermute | solution.py:288
  28.8 5.0 %collective-permute-start.9 = (bf16[64,1024]{1,0:T(8,128)(2,1)S(1)}, bf16[64,1024]{1,0:T(8,128)(2,1)S(1)}, u32[]{:S(2)}, u32[]{:S(2)}) collective-permute-start(bf16[64,1024]{1,0:T(8,128)(2,1)S(1)} %slice.47), channel_id=1, source_target_pairs={{2,0},{4,2},{6,4},{7,6},{5,7},{3,5},{1,3},{0,1},{10,8},{12,10},{14... | collective-permute-start | bytes 393224 | tf_op jit(solution)/shard_map/ppermute | solution.py:291
  37.4 11.6 %collective-permute-start.11 = (bf16[1024,256]{1,0:T(8,128)(2,1)S(1)}, bf16[1024,256]{1,0:T(8,128)(2,1)S(1)}, u32[]{:S(2)}, u32[]{:S(2)}) collective-permute-start(bf16[1024,256]{1,0:T(8,128)(2,1)S(1)} %get-tuple-element.53), channel_id=1, source_target_pairs={{0,8},{8,0},{16,24},{24,16},{1,9},{9,1},{17,25},{25,17},{2,10},{10... | collective-permute-start | bytes 1572872 | tf_op jit(solution)/shard_map/ppermute | solution.py:328
  37.5 6.3 %collective-permute-start.23 = (bf16[64,1024]{1,0:T(8,128)(2,1)S(1)}, bf16[64,1024]{1,0:T(8,128)(2,1)S(1)}, u32[]{:S(2)}, u32[]{:S(2)}) collective-permute-start(bf16[64,1024]{1,0:T(8,128)(2,1)S(1)} %get-tuple-element.56), channel_id=1, source_target_pairs={{0,2},{2,4},{4,6},{6,7},{7,5},{5,3},{3,1},{1,0},{8,10},{10,12},{12... | collective-permute-start | bytes 393224 | tf_op jit(solution)/shard_map/ppermute | solution.py:288
  39.1 8.7 %collective-permute-start.13 = (bf16[64,1024]{1,0:T(8,128)(2,1)S(1)}, bf16[64,1024]{1,0:T(8,128)(2,1)S(1)}, u32[]{:S(2)}, u32[]{:S(2)}) collective-permute-start(bf16[64,1024]{1,0:T(8,128)(2,1)S(1)} %get-tuple-element.55), channel_id=1, source_target_pairs={{2,0},{4,2},{6,4},{7,6},{5,7},{3,5},{1,3},{0,1},{10,8},{12,10},{14... | collective-permute-start | bytes 393224 | tf_op jit(solution)/shard_map/ppermute | solution.py:291
  39.6 6.7 %collective-permute-start.20 = (bf16[64,1024]{1,0:T(8,128)(2,1)S(1)}, bf16[64,1024]{1,0:T(8,128)(2,1)S(1)}, u32[]{:S(2)}, u32[]{:S(2)}) collective-permute-start(bf16[64,1024]{1,0:T(8,128)(2,1)S(1)} %get-tuple-element.61), channel_id=1, source_target_pairs={{0,2},{2,4},{4,6},{6,7},{7,5},{5,3},{3,1},{1,0},{8,10},{10,12},{12... | collective-permute-start | bytes 393224 | tf_op jit(solution)/shard_map/ppermute | solution.py:288
  41.1 9.0 %collective-permute-start.17 = (bf16[64,1024]{1,0:T(8,128)(2,1)S(1)}, bf16[64,1024]{1,0:T(8,128)(2,1)S(1)}, u32[]{:S(2)}, u32[]{:S(2)}) collective-permute-start(bf16[64,1024]{1,0:T(8,128)(2,1)S(1)} %get-tuple-element.57), channel_id=1, source_target_pairs={{2,0},{4,2},{6,4},{7,6},{5,7},{3,5},{1,3},{0,1},{10,8},{12,10},{14... | collective-permute-start | bytes 393224 | tf_op jit(solution)/shard_map/ppermute | solution.py:291
  43.9 19.6 %collective-permute-start.10 = (bf16[1024,256]{1,0:T(8,128)(2,1)S(1)}, bf16[1024,256]{1,0:T(8,128)(2,1)S(1)}, u32[]{:S(2)}, u32[]{:S(2)}) collective-permute-start(bf16[1024,256]{1,0:T(8,128)(2,1)S(1)} %get-tuple-element.51), channel_id=1, source_target_pairs={{0,8},{8,0},{16,24},{24,16},{1,9},{9,1},{17,25},{25,17},{2,10},{10... | collective-permute-start | bytes 1572872 | tf_op jit(solution)/shard_map/ppermute | solution.py:328
  46.3 6.4 %collective-permute-start.24 = (bf16[64,1024]{1,0:T(8,128)(2,1)S(1)}, bf16[64,1024]{1,0:T(8,128)(2,1)S(1)}, u32[]{:S(2)}, u32[]{:S(2)}) collective-permute-start(bf16[64,1024]{1,0:T(8,128)(2,1)S(1)} %kernel_sum.19), channel_id=1, source_target_pairs={{0,2},{2,4},{4,6},{6,7},{7,5},{5,3},{3,1},{1,0},{8,10},{10,12},{12... | collective-permute-start | bytes 393224 | tf_op jit(solution)/shard_map/ppermute | solution.py:288
  47.8 7.3 %collective-permute-start.21 = (bf16[64,1024]{1,0:T(8,128)(2,1)S(1)}, bf16[64,1024]{1,0:T(8,128)(2,1)S(1)}, u32[]{:S(2)}, u32[]{:S(2)}) collective-permute-start(bf16[64,1024]{1,0:T(8,128)(2,1)S(1)} %kernel_sum.17), channel_id=1, source_target_pairs={{0,2},{2,4},{4,6},{6,7},{7,5},{5,3},{3,1},{1,0},{8,10},{10,12},{12... | collective-permute-start | bytes 393224 | tf_op jit(solution)/shard_map/ppermute | solution.py:288
  49.0 6.1 %collective-permute-start.14 = (bf16[64,1024]{1,0:T(8,128)(2,1)S(1)}, bf16[64,1024]{1,0:T(8,128)(2,1)S(1)}, u32[]{:S(2)}, u32[]{:S(2)}) collective-permute-start(bf16[64,1024]{1,0:T(8,128)(2,1)S(1)} %kernel_sum.12), channel_id=1, source_target_pairs={{2,0},{4,2},{6,4},{7,6},{5,7},{3,5},{1,3},{0,1},{10,8},{12,10},{14... | collective-permute-start | bytes 393224 | tf_op jit(solution)/shard_map/ppermute | solution.py:291
  50.2 13.9 %collective-permute-start.12 = (bf16[1024,256]{1,0:T(8,128)(2,1)S(1)}, bf16[1024,256]{1,0:T(8,128)(2,1)S(1)}, u32[]{:S(2)}, u32[]{:S(2)}) collective-permute-start(bf16[1024,256]{1,0:T(8,128)(2,1)S(1)} %add_convert_fusion), channel_id=1, source_target_pairs={{0,16},{8,24},{16,0},{24,8},{1,17},{9,25},{17,1},{25,9},{2,18},{10... | collective-permute-start | bytes 1572872 | tf_op jit(solution)/shard_map/ppermute | solution.py:328
  52.7 5.7 %collective-permute-start.18 = (bf16[64,1024]{1,0:T(8,128)(2,1)S(1)}, bf16[64,1024]{1,0:T(8,128)(2,1)S(1)}, u32[]{:S(2)}, u32[]{:S(2)}) collective-permute-start(bf16[64,1024]{1,0:T(8,128)(2,1)S(1)} %kernel_sum.15), channel_id=1, source_target_pairs={{2,0},{4,2},{6,4},{7,6},{5,7},{3,5},{1,3},{0,1},{10,8},{12,10},{14... | collective-permute-start | bytes 393224 | tf_op jit(solution)/shard_map/ppermute | solution.py:291
  55.1 6.2 %collective-permute-start.25 = (bf16[64,1024]{1,0:T(8,128)(2,1)S(1)}, bf16[64,1024]{1,0:T(8,128)(2,1)S(1)}, u32[]{:S(2)}, u32[]{:S(2)}) collective-permute-start(bf16[64,1024]{1,0:T(8,128)(2,1)S(1)} %kernel_sum.20), channel_id=1, source_target_pairs={{0,2},{2,4},{4,6},{6,7},{7,5},{5,3},{3,1},{1,0},{8,10},{10,12},{12... | collective-permute-start | bytes 393224 | tf_op jit(solution)/shard_map/ppermute | solution.py:288
  55.2 6.7 %collective-permute-start.15 = (bf16[64,1024]{1,0:T(8,128)(2,1)S(1)}, bf16[64,1024]{1,0:T(8,128)(2,1)S(1)}, u32[]{:S(2)}, u32[]{:S(2)}) collective-permute-start(bf16[64,1024]{1,0:T(8,128)(2,1)S(1)} %kernel_sum.13), channel_id=1, source_target_pairs={{2,0},{4,2},{6,4},{7,6},{5,7},{3,5},{1,3},{0,1},{10,8},{12,10},{14... | collective-permute-start | bytes 393224 | tf_op jit(solution)/shard_map/ppermute | solution.py:291
  58.4 5.8 %collective-permute-start.22 = (bf16[64,1024]{1,0:T(8,128)(2,1)S(1)}, bf16[64,1024]{1,0:T(8,128)(2,1)S(1)}, u32[]{:S(2)}, u32[]{:S(2)}) collective-permute-start(bf16[64,1024]{1,0:T(8,128)(2,1)S(1)} %kernel_sum.18), channel_id=1, source_target_pairs={{0,2},{2,4},{4,6},{6,7},{7,5},{5,3},{3,1},{1,0},{8,10},{10,12},{12... | collective-permute-start | bytes 393224 | tf_op jit(solution)/shard_map/ppermute | solution.py:288
  61.3 5.0 %collective-permute-start.19 = (bf16[64,1024]{1,0:T(8,128)(2,1)S(1)}, bf16[64,1024]{1,0:T(8,128)(2,1)S(1)}, u32[]{:S(2)}, u32[]{:S(2)}) collective-permute-start(bf16[64,1024]{1,0:T(8,128)(2,1)S(1)} %kernel_sum.16), channel_id=1, source_target_pairs={{2,0},{4,2},{6,4},{7,6},{5,7},{3,5},{1,3},{0,1},{10,8},{12,10},{14... | collective-permute-start | bytes 393224 | tf_op jit(solution)/shard_map/ppermute | solution.py:291
  61.9 5.0 %collective-permute-start.26 = (bf16[64,1024]{1,0:T(8,128)(2,1)S(1)}, bf16[64,1024]{1,0:T(8,128)(2,1)S(1)}, u32[]{:S(2)}, u32[]{:S(2)}) collective-permute-start(bf16[64,1024]{1,0:T(8,128)(2,1)S(1)} %kernel_sum.21), channel_id=1, source_target_pairs={{0,2},{2,4},{4,6},{6,7},{7,5},{5,3},{3,1},{1,0},{8,10},{10,12},{12... | collective-permute-start | bytes 393224 | tf_op jit(solution)/shard_map/ppermute | solution.py:288
  63.5 5.0 %collective-permute-start.16 = (bf16[64,1024]{1,0:T(8,128)(2,1)S(1)}, bf16[64,1024]{1,0:T(8,128)(2,1)S(1)}, u32[]{:S(2)}, u32[]{:S(2)}) collective-permute-start(bf16[64,1024]{1,0:T(8,128)(2,1)S(1)} %kernel_sum.14), channel_id=1, source_target_pairs={{2,0},{4,2},{6,4},{7,6},{5,7},{3,5},{1,3},{0,1},{10,8},{12,10},{14... | collective-permute-start | bytes 393224 | tf_op jit(solution)/shard_map/ppermute | solution.py:291
  (1 other events, 0.7 us)

commit v16 on v14

--- a/solution.py
+++ b/solution.py
@@ -68,8 +68,8 @@
     piece_count = sum(len(pieces) for pieces in piece_rows)
     x_refs = refs[:piece_count]
     w_ref, live_ref = refs[piece_count : piece_count + 2]
-    grad_refs = refs[piece_count + 2 : 2 * piece_count + 2]
-    slope_refs = refs[2 * piece_count + 2 :]
+    grad_refs = refs[piece_count + 2 : len(refs) - block_count]
+    slope_refs = refs[len(refs) - block_count :]
     labels, width = w_ref.shape
     local_count = labels // BLOCK
     rows = slope_refs[0].shape[0]
@@ -136,16 +136,17 @@
             at += ref.shape[0]
 
 
-def block_work(blocks, weights, live_table, top_count, pos_count):
+def block_work(blocks, weights, live_table, top_count, pos_count, grad_rows=None):
     labels, width = weights.shape
     piece_rows = [
         [piece.shape[0] - (FIELD_ROWS if p == 0 else 0) for p, piece in enumerate(pieces)]
         for pieces in blocks
     ]
     flat_rows = sum(piece_rows, [])
+    grad_rows = grad_rows or flat_rows
     out = pl.pallas_call(
         functools.partial(block_kernel, piece_rows, top_count, pos_count),
-        out_shape=[jax.ShapeDtypeStruct((rows, width), jnp.bfloat16) for rows in flat_rows]
+        out_shape=[jax.ShapeDtypeStruct((rows, width), jnp.bfloat16) for rows in grad_rows]
         + [jax.ShapeDtypeStruct((sum(rows), labels), jnp.bfloat16) for rows in piece_rows],
         in_specs=[pl.BlockSpec(memory_space=pltpu.VMEM)] * (len(flat_rows) + 2),
         compiler_params=pltpu.CompilerParams(vmem_limit_bytes=VMEM_LIMIT),
@@ -156,7 +157,7 @@
         ),
         name="block_work",
     )(*[piece for pieces in blocks for piece in pieces], weights, live_table)
-    return list(out[: len(flat_rows)]), list(out[len(flat_rows) :])
+    return list(out[: len(grad_rows)]), list(out[len(grad_rows) :])
 
 
 def weight_kernel(piece_rows, column_blocks, scale, *refs):
@@ -281,7 +282,7 @@
     clus_count, seq_count = lax.axis_size("clus"), lax.axis_size("seq")
     local_count = cluster_sizes.shape[0]
     part_width = width // seq_count
-    split, steps = inst_rows * 5 // 8, clus_count // 2
+    first_part, half, steps = inst_rows * 5 // 8, inst_rows // 2, clus_count // 2
 
     ring = list(range(0, clus_count, 2)) + list(range(1, clus_count, 2))[::-1]
     up = list(zip(ring, ring[1:] + ring[:1]))
@@ -295,8 +296,8 @@
 
     used, slopes = [], []
 
-    def take(*blocks):
-        grads, found = block_work(blocks, weights, live_table, top_count, pos_count)
+    def take(*blocks, grad_rows=None):
+        grads, found = block_work(blocks, weights, live_table, top_count, pos_count, grad_rows)
         used.extend(blocks)
         slopes.extend(found)
         return grads
@@ -316,14 +317,15 @@
         if k < steps:
             arriving = send_up(below), send_down(above)
         else:
-            ends = jnp.concatenate([below[:split], below[inst_rows:]], axis=0)
-            arriving = send_up(ends), send_down(above[split:inst_rows])
+            ends = jnp.concatenate([below[:first_part], below[inst_rows:]], axis=0)
+            arriving = send_up(ends), send_down(above[first_part:inst_rows])
         if k == 3 or steps < 3:
             below_grad[k - 1], above_grad[k - 1], own_grad = take([below], [above], [own])
         else:
             below_grad[k - 1], above_grad[k - 1] = take([below], [above])
         below, above = arriving
-    to_down, to_up = take([after(below, below_grad[steps - 1]), above])
+    opposite = [after(below, below_grad[steps - 1]), above]
+    to_down, to_up = take(opposite, grad_rows=[half, half])
 
     scale = 1.0 / math.sqrt(inst_rows * seq_count * top_count // local_count)
 
@@ -344,8 +346,8 @@
         from_above, from_below = send_down(to_down), send_up(to_up)
         if k == steps:
             near_below, near_above = below_grad[k - 1], above_grad[k - 1]
-            to_down = jnp.concatenate([add(near_below[:split], from_above), near_below[split:]], axis=0)
-            to_up = jnp.concatenate([near_above[:split], add(near_above[split:], from_below)], axis=0)
+            to_down = jnp.concatenate([add(near_below[:half], from_above), near_below[half:]], axis=0)
+            to_up = jnp.concatenate([near_above[:half], add(near_above[half:], from_below)], axis=0)
         elif k > 1:
             to_down, to_up = add(below_grad[k - 1], from_above), add(above_grad[k - 1], from_below)
     feature_grad, weight_grad = finish(weight_sum(terms[0]), [own_grad, from_above, from_below], 2)

time: 64.6 us -> 64 us (level)
    ppermute x9, waiting for transfers between devices: 3.63 us -> 2.86 us  [send_down(): return lax.ppermute(array, 'clus', down)]
  transfers between devices with their start and end apart: 21 -> 21, of which waited for: 12 -> 11; matrix products, arithmetic and copies ran while one was open for 1% -> 1% of each run, Pallas kernels for 14% -> 14%
where the time goes in v16:
time: 64 us; the launch traced here: 63.8 us
  waiting for transfers between devices  26.1 us (41%)
  starting transfers between devices  21.5 us (34%)
  Pallas kernels  11 us (17%)
  local copies, waits for them, and re-layouts  3.72 us (6%)
  between operations  0.85 us (1%)
    ppermute x9, waiting for transfers between devices, send_up(): return lax.ppermute(array, 'clus', up)  18.1 us
    ppermute x9, starting transfers between devices, send_up(): return lax.ppermute(array, 'clus', up)  16.4 us
    pallas_call x4, Pallas kernels, block_work(): pl.pallas_call(functools.partial(block_kernel, piece_rows, top_count, pos...  6.97 us
    ppermute x3, waiting for transfers between devices, seq_send(): return lax.ppermute(array, 'seq', [(k, k ^ bit) for k in range(seq_count)])  5.14 us
    unnamed x14, local copies, waits for them, and re-layouts  3.67 us
    ppermute x9, starting transfers between devices, send_down(): return lax.ppermute(array, 'clus', down)  3.49 us
    ppermute x9, waiting for transfers between devices, send_down(): return lax.ppermute(array, 'clus', down)  2.86 us
    pallas_call x1, Pallas kernels, weight_work(): pl.pallas_call(functools.partial(weight_kernel, piece_rows, column_blocks...  2.37 us
  transfers between devices with their start and end apart: 21, of which 11 were waited for; matrix products, arithmetic and copies ran while one was open for 1% of the time, Pallas kernels for 14%

profile of v16, /device:TPU:0, one launch (start us, length us, event | category | flops | bytes accessed | tf_op | source)
XLA Modules:
  0.0 63.8 jit_solution(8095796923344711717)
XLA Ops:
  0.6 3.1 %collective-permute-start = (bf16[128,1024]{1,0:T(8,128)(2,1)}, bf16[128,1024]{1,0:T(8,128)(2,1)S(1)}, u32[]{:S(2)}, u32[]{:S(2)}) collective-permute-start(bf16[128,1024]{1,0:T(8,128)(2,1)} %param.5), channel_id=1, source_target_pairs={{0,2},{2,4},{4,6},{6,7},{7,5},{5,3},{3,1},{1,0},{8,10},{10,12},{12... | collective-permute-start | bytes 786440 | tf_op jit(solution)/shard_map/ppermute | solution.py:292
  3.7 0.7 %copy-done.2 = s32[128,16]{0,1:T(8,128)S(1)} copy-done((s32[128,16]{0,1:T(8,128)S(1)}, s32[128,16]{0,1:T(8,128)}, u32[]{:S(2)}) %copy-start.2) | copy-done | bytes 8216
  4.4 0.7 %copy-done.3 = s32[128,4]{0,1:T(4,128)S(1)} copy-done((s32[128,4]{0,1:T(4,128)S(1)}, s32[128,4]{0,1:T(4,128)}, u32[]{:S(2)}) %copy-start.3) | copy-done | bytes 2072
  5.1 2.1 %collective-permute-start.1 = (bf16[8,1024]{1,0:T(8,128)(2,1)S(1)}, bf16[8,1024]{1,0:T(8,128)(2,1)S(1)}, u32[]{:S(2)}, u32[]{:S(2)}) collective-permute-start(bf16[8,1024]{1,0:T(8,128)(2,1)S(1)} %instance_ids.1), channel_id=1, source_target_pairs={{0,2},{2,4},{4,6},{6,7},{7,5},{5,3},{3,1},{1,0},{8,10},{10,12},{12... | collective-permute-start | bytes 49160 | tf_op jit(solution)/shard_map/ppermute | solution.py:292
  7.2 1.6 %copy-done = bf16[1024,1024]{1,0:T(8,128)(2,1)S(1)} copy-done((bf16[1024,1024]{1,0:T(8,128)(2,1)S(1)}, bf16[1024,1024]{1,0:T(8,128)(2,1)}, u32[]{:S(2)}) %copy-start) | copy-done | bytes 2097176
  8.8 0.7 %copy-done.4 = s32[8]{0:T(128)S(1)} copy-done((s32[8]{0:T(128)S(1)}, s32[8]{0:T(128)}, u32[]{:S(2)}) %copy-start.4) | copy-done | bytes 56
  9.5 0.6 live_labels.1.refs_3_.refs_4_
  10.4 1.5 %collective-permute-done.2 = bf16[128,1024]{1,0:T(8,128)(2,1)S(1)} collective-permute-done((bf16[128,1024]{1,0:T(8,128)(2,1)}, bf16[128,1024]{1,0:T(8,128)(2,1)S(1)}, u32[]{:S(2)}, u32[]{:S(2)}) %collective-permute-start.2) | collective-permute-done | bytes 262176 | tf_op jit(solution)/shard_map/ppermute | solution.py:295
  11.9 1.6 %collective-permute-start.4 = (bf16[136,1024]{1,0:T(8,128)(2,1)S(1)}, bf16[136,1024]{1,0:T(8,128)(2,1)S(1)}, u32[]{:S(2)}, u32[]{:S(2)}) collective-permute-start(bf16[136,1024]{1,0:T(8,128)(2,1)S(1)} %constant_dynamic-update-slice_fusion.refs_0_), channel_id=1, source_target_pairs={{0,2},{2,4},{4,6},{6,7},{7,5},{5,3},{3,1},{1,0},{8,10},{10,12},{12... | collective-permute-start | bytes 835592 | tf_op jit(solution)/shard_map/ppermute | solution.py:292
  14.0 1.7 %block_work.4 = (bf16[128,1024]{1,0:T(8,128)(2,1)S(1)}, bf16[128,1024]{1,0:T(8,128)(2,1)S(1)}, bf16[128,1024]{1,0:T(8,128)(2,1)S(1)}, bf16[128,1024]{1,0:T(8,128)(2,1)S(1)}) custom-call(bf16[136,1024]{1,0:T(8,128)(2,1)S(1)} %constant_dynamic-update-slice_fusion.refs_0_, bf16[136,1024]{1,0:T(8,128)(2,1)S(1)} %constant_dynamic-update-slice_fusion.2.refs_1_, ...), custom_call_target="tpu_custom_call" | custom-call | flops 1073741824 | bytes 3670016 | tf_op jit(solution)/shard_map/block_work/pallas_call | solution.py:147
  15.7 3.2 %collective-permute-done.4.refs_0_.refs_2_ = bf16[136,1024]{1,0:T(8,128)(2,1)S(1)} collective-permute-done((bf16[136,1024]{1,0:T(8,128)(2,1)S(1)}, bf16[136,1024]{1,0:T(8,128)(2,1)S(1)}, u32[]{:S(2)}, u32[]{:S(2)}) %collective-permute-start.4) | collective-permute-done | bytes 278560 | tf_op jit(solution)/shard_map/ppermute | solution.py:292
  18.9 1.6 %collective-permute-start.6 = (bf16[136,1024]{1,0:T(8,128)(2,1)S(1)}, bf16[136,1024]{1,0:T(8,128)(2,1)S(1)}, u32[]{:S(2)}, u32[]{:S(2)}) collective-permute-start(bf16[136,1024]{1,0:T(8,128)(2,1)S(1)} %collective-permute-done.4.refs_0_.refs_2_), channel_id=1, source_target_pairs={{0,2},{2,4},{4,6},{6,7},{7,5},{5,3},{3,1},{1,0},{8,10},{10,12},{12... | collective-permute-start | bytes 835592 | tf_op jit(solution)/shard_map/ppermute | solution.py:292
  21.0 2.4 %block_work.5 = (bf16[128,1024]{1,0:T(8,128)(2,1)S(1)}, bf16[128,1024]{1,0:T(8,128)(2,1)S(1)}, bf16[128,1024]{1,0:T(8,128)(2,1)S(1)}, bf16[128,1024]{1,0:T(8,128...) custom-call(bf16[136,1024]{1,0:T(8,128)(2,1)S(1)} %collective-permute-done.4.refs_0_.refs_2_, ...), custom_call_target="tpu_custom_call" | custom-call | flops 1610612736 | bytes 4456448 | tf_op jit(solution)/shard_map/block_work/pallas_call | solution.py:147
  23.4 2.9 %collective-permute-done.6.refs_0_.refs_5_ = bf16[136,1024]{1,0:T(8,128)(2,1)S(1)} collective-permute-done((bf16[136,1024]{1,0:T(8,128)(2,1)S(1)}, bf16[136,1024]{1,0:T(8,128)(2,1)S(1)}, u32[]{:S(2)}, u32[]{:S(2)}) %collective-permute-start.6) | collective-permute-done | bytes 278560 | tf_op jit(solution)/shard_map/ppermute | solution.py:292
  26.3 1.6 %collective-permute-start.8 = (bf16[88,1024]{1,0:T(8,128)(2,1)S(1)}, bf16[88,1024]{1,0:T(8,128)(2,1)S(1)}, u32[]{:S(2)}, u32[]{:S(2)}) collective-permute-start(bf16[88,1024]{1,0:T(8,128)(2,1)S(1)} %pad_maximum_fusion.3), channel_id=1, source_target_pairs={{0,2},{2,4},{4,6},{6,7},{7,5},{5,3},{3,1},{1,0},{8,10},{10,12},{12... | collective-permute-start | bytes 540680 | tf_op jit(solution)/shard_map/ppermute | solution.py:292
  28.5 1.7 %block_work.6 = (bf16[128,1024]{1,0:T(8,128)(2,1)S(1)}, bf16[128,1024]{1,0:T(8,128)(2,1)S(1)}, bf16[128,1024]{1,0:T(8,128)(2,1)S(1)}, bf16[128,1024]{1,0:T(8,128)(2,1)S(1)}) custom-call(bf16[136,1024]{1,0:T(8,128)(2,1)S(1)} %collective-permute-done.6.refs_0_.refs_5_, bf16[136,1024]{1,0:T(8,128)(2,1)S(1)} %collective-permute-done.7.refs_1_.refs_6_, ...), custom_call_target="tpu_custom_call" | custom-call | flops 1073741824 | bytes 3670016 | tf_op jit(solution)/shard_map/block_work/pallas_call | solution.py:147
  30.2 1.7 %collective-permute-done.8.refs_0_.refs_7_ = bf16[88,1024]{1,0:T(8,128)(2,1)S(1)} collective-permute-done((bf16[88,1024]{1,0:T(8,128)(2,1)S(1)}, bf16[88,1024]{1,0:T(8,128)(2,1)S(1)}, u32[]{:S(2)}, u32[]{:S(2)}) %collective-permute-start.8) | collective-permute-done | bytes 180256 | tf_op jit(solution)/shard_map/ppermute | solution.py:292
  31.9 0.8 %collective-permute-done.9.refs_1_.refs_8_ = bf16[48,1024]{1,0:T(8,128)(2,1)S(1)} collective-permute-done((bf16[48,1024]{1,0:T(8,128)(2,1)S(1)}, bf16[48,1024]{1,0:T(8,128)(2,1)S(1)}, u32[]{:S(2)}, u32[]{:S(2)}) %collective-permute-start.9) | collective-permute-done | bytes 98336 | tf_op jit(solution)/shard_map/ppermute | solution.py:295
  32.7 1.2 %block_work.7 = (bf16[64,1024]{1,0:T(8,128)(2,1)S(1)}, bf16[64,1024]{1,0:T(8,128)(2,1)S(1)}, bf16[128,1024]{1,0:T(8,128)(2,1)S(1)}) custom-call(bf16[88,1024]{1,0:T(8,128)(2,1)S(1)} %collective-permute-done.8.refs_0_.refs_7_, bf16[48,1024]{1,0:T(8,128)(2,1)S(1)} %collective-permute-done.9.refs_1_.refs_8_, bf16[1024,1024]{1,0:T(8,128)(2,1)S(1)} %copy-done.1, ...), custom_call_target="tpu_custom_call" | custom-call | flops 536870912 | bytes 2883584 | tf_op jit(solution)/shard_map/block_work/pallas_call | solution.py:147
  33.9 1.6 %collective-permute-start.17 = (bf16[64,1024]{1,0:T(8,128)(2,1)S(1)}, bf16[64,1024]{1,0:T(8,128)(2,1)S(1)}, u32[]{:S(2)}, u32[]{:S(2)}) collective-permute-start(bf16[64,1024]{1,0:T(8,128)(2,1)S(1)} %get-tuple-element.57), channel_id=1, source_target_pairs={{0,2},{2,4},{4,6},{6,7},{7,5},{5,3},{3,1},{1,0},{8,10},{10,12},{12... | collective-permute-start | bytes 393224 | tf_op jit(solution)/shard_map/ppermute | solution.py:292
  35.9 2.4 %weight_work.1 = (bf16[1024,256]{1,0:T(8,128)(2,1)S(1)}, bf16[1024,256]{1,0:T(8,128)(2,1)S(1)}, bf16[1024,256]{1,0:T(8,128)(2,1)S(1)}, bf16[1024,256]{1,0:T(8,128)(2,1)S(1)}) custom-call(bf16[136,1024]{1,0:T(8,128)(2,1)S(1)} %constant_dynamic-update-slice_fusion.refs_0_, bf16[136,1024]{1,0:T(8,128)(2,1)S(1)} %constant_dynamic-update-slice_fusion.2.refs_1_, ...), custom_call_target="tpu_custom_call" | custom-call | flops 2147483648 | bytes 4718592 | tf_op jit(solution)/shard_map/weight_work/pallas_call | solution.py:189
  38.9 1.6 %collective-permute-start.18 = (bf16[128,1024]{1,0:T(8,128)(2,1)S(1)}, bf16[128,1024]{1,0:T(8,128)(2,1)S(1)}, u32[]{:S(2)}, u32[]{:S(2)}) collective-permute-start(bf16[128,1024]{1,0:T(8,128)(2,1)S(1)} %pad_maximum_fusion.2), channel_id=1, source_target_pairs={{0,2},{2,4},{4,6},{6,7},{7,5},{5,3},{3,1},{1,0},{8,10},{10,12},{12... | collective-permute-start | bytes 786440 | tf_op jit(solution)/shard_map/ppermute | solution.py:292
  40.6 0.5 collective-permute-start.14
  41.1 6.1 %collective-permute-done.18 = bf16[128,1024]{1,0:T(8,128)(2,1)S(1)} collective-permute-done((bf16[128,1024]{1,0:T(8,128)(2,1)S(1)}, bf16[128,1024]{1,0:T(8,128)(2,1)S(1)}, u32[]{:S(2)}, u32[]{:S(2)}) %collective-permute-start.18) | collective-permute-done | bytes 262176 | tf_op jit(solution)/shard_map/ppermute | solution.py:292
  47.3 1.6 %collective-permute-start.19 = (bf16[128,1024]{1,0:T(8,128)(2,1)S(1)}, bf16[128,1024]{1,0:T(8,128)(2,1)S(1)}, u32[]{:S(2)}, u32[]{:S(2)}) collective-permute-start(bf16[128,1024]{1,0:T(8,128)(2,1)S(1)} %add_convert_fusion.2), channel_id=1, source_target_pairs={{0,2},{2,4},{4,6},{6,7},{7,5},{5,3},{3,1},{1,0},{8,10},{10,12},{12... | collective-permute-start | bytes 786440 | tf_op jit(solution)/shard_map/ppermute | solution.py:292
  49.6 1.6 %collective-permute-start.12 = (bf16[1024,256]{1,0:T(8,128)(2,1)S(1)}, bf16[1024,256]{1,0:T(8,128)(2,1)S(1)}, u32[]{:S(2)}, u32[]{:S(2)}) collective-permute-start(bf16[1024,256]{1,0:T(8,128)(2,1)S(1)} %add_convert_fusion), channel_id=1, source_target_pairs={{0,16},{8,24},{16,0},{24,8},{1,17},{9,25},{17,1},{25,9},{2,18},{10... | collective-permute-start | bytes 1572872 | tf_op jit(solution)/shard_map/ppermute | solution.py:333
  51.2 3.5 %collective-permute-done.19 = bf16[128,1024]{1,0:T(8,128)(2,1)S(1)} collective-permute-done((bf16[128,1024]{1,0:T(8,128)(2,1)S(1)}, bf16[128,1024]{1,0:T(8,128)(2,1)S(1)}, u32[]{:S(2)}, u32[]{:S(2)}) %collective-permute-start.19) | collective-permute-done | bytes 262176 | tf_op jit(solution)/shard_map/ppermute | solution.py:292
  54.8 1.6 %collective-permute-start.20 = (bf16[128,1024]{1,0:T(8,128)(2,1)S(1)}, bf16[128,1024]{1,0:T(8,128)(2,1)S(1)}, u32[]{:S(2)}, u32[]{:S(2)}) collective-permute-start(bf16[128,1024]{1,0:T(8,128)(2,1)S(1)} %add_convert_fusion.1), channel_id=1, source_target_pairs={{0,2},{2,4},{4,6},{6,7},{7,5},{5,3},{3,1},{1,0},{8,10},{10,12},{12... | collective-permute-start | bytes 786440 | tf_op jit(solution)/shard_map/ppermute | solution.py:292
  56.5 0.5 collective-permute-start.16
  57.0 5.1 %collective-permute-done.12.refs_2_ = bf16[1024,256]{1,0:T(8,128)(2,1)S(1)} collective-permute-done((bf16[1024,256]{1,0:T(8,128)(2,1)S(1)}, bf16[1024,256]{1,0:T(8,128)(2,1)S(1)}, u32[]{:S(2)}, u32[]{:S(2)}) %collective-permute-start.12) | collective-permute-done | bytes 524320 | tf_op jit(solution)/shard_map/ppermute | solution.py:333
  62.3 0.6 collective-permute-done.16.refs_1_
  62.9 0.9 %finish.1 = (bf16[128,1024]{1,0:T(8,128)(2,1)}, bf16[1024,256]{1,0:T(8,128)(2,1)}) custom-call(bf16[1024,256]{1,0:T(8,128)(2,1)S(1)} %weight_sum.1.weight_ref, bf16[128,1024]{1,0:T(8,128)(2,1)S(1)} %get-tuple-element.52.refs_0_, bf16[128,1024]{1,0:T(8,128)(2,1)S(1)} %collective-permute-done.16.refs_1_, bf16[128,1024]{1,0:T(8,128)(2,1)S(1)} %collective-permute-done.20.refs_2_), custom_call_target="tpu_custom_call" | custom-call | flops 393216 | bytes 2097152 | tf_op jit(solution)/shard_map/finish/pallas_call | solution.py:253
  (51 shorter events, 4.2 us)
Async XLA Ops:
  0.6 9.7 %collective-permute-start = (bf16[128,1024]{1,0:T(8,128)(2,1)}, bf16[128,1024]{1,0:T(8,128)(2,1)S(1)}, u32[]{:S(2)}, u32[]{:S(2)}) collective-permute-start(bf16[128,1024]{1,0:T(8,128)(2,1)} %param.5), channel_id=1, source_target_pairs={{0,2},{2,4},{4,6},{6,7},{7,5},{5,3},{3,1},{1,0},{8,10},{10,12},{12... | collective-permute-start | bytes 786440 | tf_op jit(solution)/shard_map/ppermute | solution.py:292
  3.7 8.2 %collective-permute-start.2 = (bf16[128,1024]{1,0:T(8,128)(2,1)}, bf16[128,1024]{1,0:T(8,128)(2,1)S(1)}, u32[]{:S(2)}, u32[]{:S(2)}) collective-permute-start(bf16[128,1024]{1,0:T(8,128)(2,1)} %param.5), channel_id=1, source_target_pairs={{2,0},{4,2},{6,4},{7,6},{5,7},{3,5},{1,3},{0,1},{10,8},{12,10},{14... | collective-permute-start | bytes 786440 | tf_op jit(solution)/shard_map/ppermute | solution.py:295
  3.7 0.7 %copy-start.2 = (s32[128,16]{0,1:T(8,128)S(1)}, s32[128,16]{0,1:T(8,128)}, u32[]{:S(2)}) copy-start(s32[128,16]{0,1:T(8,128)} %param.6) | copy-start | bytes 24580
  4.4 0.7 %copy-start.3 = (s32[128,4]{0,1:T(4,128)S(1)}, s32[128,4]{0,1:T(4,128)}, u32[]{:S(2)}) copy-start(s32[128,4]{0,1:T(4,128)} %param.7) | copy-start | bytes 6148
  5.1 6.7 %collective-permute-start.1 = (bf16[8,1024]{1,0:T(8,128)(2,1)S(1)}, bf16[8,1024]{1,0:T(8,128)(2,1)S(1)}, u32[]{:S(2)}, u32[]{:S(2)}) collective-permute-start(bf16[8,1024]{1,0:T(8,128)(2,1)S(1)} %instance_ids.1), channel_id=1, source_target_pairs={{0,2},{2,4},{4,6},{6,7},{7,5},{5,3},{3,1},{1,0},{8,10},{10,12},{12... | collective-permute-start | bytes 49160 | tf_op jit(solution)/shard_map/ppermute | solution.py:292
  7.2 6.3 %collective-permute-start.3 = (bf16[8,1024]{1,0:T(8,128)(2,1)S(1)}, bf16[8,1024]{1,0:T(8,128)(2,1)S(1)}, u32[]{:S(2)}, u32[]{:S(2)}) collective-permute-start(bf16[8,1024]{1,0:T(8,128)(2,1)S(1)} %instance_ids.1), channel_id=1, source_target_pairs={{2,0},{4,2},{6,4},{7,6},{5,7},{3,5},{1,3},{0,1},{10,8},{12,10},{14... | collective-permute-start | bytes 49160 | tf_op jit(solution)/shard_map/ppermute | solution.py:295
  7.2 1.6 %copy-start = (bf16[1024,1024]{1,0:T(8,128)(2,1)S(1)}, bf16[1024,1024]{1,0:T(8,128)(2,1)}, u32[]{:S(2)}) copy-start(bf16[1024,1024]{1,0:T(8,128)(2,1)} %refs_2_.5) | copy-start | bytes 6291460
  8.8 0.7 %copy-start.4 = (s32[8]{0:T(128)S(1)}, s32[8]{0:T(128)}, u32[]{:S(2)}) copy-start(s32[8]{0:T(128)} %size_ref.1) | copy-start | bytes 100
  9.4 4.6 %copy-start.1 = (bf16[1024,1024]{1,0:T(8,128)(2,1)S(1)}, bf16[1024,1024]{1,0:T(8,128)(2,1)}, u32[]{:S(2)}) copy-start(bf16[1024,1024]{1,0:T(8,128)(2,1)} %refs_2_.5) | copy-start | bytes 6291460
  11.9 7.0 %collective-permute-start.4 = (bf16[136,1024]{1,0:T(8,128)(2,1)S(1)}, bf16[136,1024]{1,0:T(8,128)(2,1)S(1)}, u32[]{:S(2)}, u32[]{:S(2)}) collective-permute-start(bf16[136,1024]{1,0:T(8,128)(2,1)S(1)} %constant_dynamic-update-slice_fusion.refs_0_), channel_id=1, source_target_pairs={{0,2},{2,4},{4,6},{6,7},{7,5},{5,3},{3,1},{1,0},{8,10},{10,12},{12... | collective-permute-start | bytes 835592 | tf_op jit(solution)/shard_map/ppermute | solution.py:292
  13.5 7.0 %copy-start.5 = (bf16[128,1024]{1,0:T(8,128)(2,1)S(1)}, bf16[128,1024]{1,0:T(8,128)(2,1)}, u32[]{:S(2)}) copy-start(bf16[128,1024]{1,0:T(8,128)(2,1)} %param.5) | copy-start | bytes 786436
  13.5 7.0 %collective-permute-start.5 = (bf16[136,1024]{1,0:T(8,128)(2,1)S(1)}, bf16[136,1024]{1,0:T(8,128)(2,1)S(1)}, u32[]{:S(2)}, u32[]{:S(2)}) collective-permute-start(bf16[136,1024]{1,0:T(8,128)(2,1)S(1)} %constant_dynamic-update-slice_fusion.2.refs_1_), channel_id=1, source_target_pairs={{2,0},{4,2},{6,4},{7,6},{5,7},{3,5},{1,3},{0,1},{10,8},{12,10},{14... | collective-permute-start | bytes 835592 | tf_op jit(solution)/shard_map/ppermute | solution.py:295
  18.9 7.4 %collective-permute-start.6 = (bf16[136,1024]{1,0:T(8,128)(2,1)S(1)}, bf16[136,1024]{1,0:T(8,128)(2,1)S(1)}, u32[]{:S(2)}, u32[]{:S(2)}) collective-permute-start(bf16[136,1024]{1,0:T(8,128)(2,1)S(1)} %collective-permute-done.4.refs_0_.refs_2_), channel_id=1, source_target_pairs={{0,2},{2,4},{4,6},{6,7},{7,5},{5,3},{3,1},{1,0},{8,10},{10,12},{12... | collective-permute-start | bytes 835592 | tf_op jit(solution)/shard_map/ppermute | solution.py:292
  20.5 7.5 %collective-permute-start.7 = (bf16[136,1024]{1,0:T(8,128)(2,1)S(1)}, bf16[136,1024]{1,0:T(8,128)(2,1)S(1)}, u32[]{:S(2)}, u32[]{:S(2)}) collective-permute-start(bf16[136,1024]{1,0:T(8,128)(2,1)S(1)} %collective-permute-done.5.refs_1_.refs_3_), channel_id=1, source_target_pairs={{2,0},{4,2},{6,4},{7,6},{5,7},{3,5},{1,3},{0,1},{10,8},{12,10},{14... | collective-permute-start | bytes 835592 | tf_op jit(solution)/shard_map/ppermute | solution.py:295
  26.3 5.5 %collective-permute-start.8 = (bf16[88,1024]{1,0:T(8,128)(2,1)S(1)}, bf16[88,1024]{1,0:T(8,128)(2,1)S(1)}, u32[]{:S(2)}, u32[]{:S(2)}) collective-permute-start(bf16[88,1024]{1,0:T(8,128)(2,1)S(1)} %pad_maximum_fusion.3), channel_id=1, source_target_pairs={{0,2},{2,4},{4,6},{6,7},{7,5},{5,3},{3,1},{1,0},{8,10},{10,12},{12... | collective-permute-start | bytes 540680 | tf_op jit(solution)/shard_map/ppermute | solution.py:292
  28.0 4.7 %collective-permute-start.9 = (bf16[48,1024]{1,0:T(8,128)(2,1)S(1)}, bf16[48,1024]{1,0:T(8,128)(2,1)S(1)}, u32[]{:S(2)}, u32[]{:S(2)}) collective-permute-start(bf16[48,1024]{1,0:T(8,128)(2,1)S(1)} %slice.23), channel_id=1, source_target_pairs={{2,0},{4,2},{6,4},{7,6},{5,7},{3,5},{1,3},{0,1},{10,8},{12,10},{14... | collective-permute-start | bytes 294920 | tf_op jit(solution)/shard_map/ppermute | solution.py:295
  33.9 5.0 %collective-permute-start.17 = (bf16[64,1024]{1,0:T(8,128)(2,1)S(1)}, bf16[64,1024]{1,0:T(8,128)(2,1)S(1)}, u32[]{:S(2)}, u32[]{:S(2)}) collective-permute-start(bf16[64,1024]{1,0:T(8,128)(2,1)S(1)} %get-tuple-element.57), channel_id=1, source_target_pairs={{0,2},{2,4},{4,6},{6,7},{7,5},{5,3},{3,1},{1,0},{8,10},{10,12},{12... | collective-permute-start | bytes 393224 | tf_op jit(solution)/shard_map/ppermute | solution.py:292
  35.5 5.1 %collective-permute-start.13 = (bf16[64,1024]{1,0:T(8,128)(2,1)S(1)}, bf16[64,1024]{1,0:T(8,128)(2,1)S(1)}, u32[]{:S(2)}, u32[]{:S(2)}) collective-permute-start(bf16[64,1024]{1,0:T(8,128)(2,1)S(1)} %get-tuple-element.53), channel_id=1, source_target_pairs={{2,0},{4,2},{6,4},{7,6},{5,7},{3,5},{1,3},{0,1},{10,8},{12,10},{14... | collective-permute-start | bytes 393224 | tf_op jit(solution)/shard_map/ppermute | solution.py:295
  38.3 11.2 %collective-permute-start.11 = (bf16[1024,256]{1,0:T(8,128)(2,1)S(1)}, bf16[1024,256]{1,0:T(8,128)(2,1)S(1)}, u32[]{:S(2)}, u32[]{:S(2)}) collective-permute-start(bf16[1024,256]{1,0:T(8,128)(2,1)S(1)} %get-tuple-element.51), channel_id=1, source_target_pairs={{0,8},{8,0},{16,24},{24,16},{1,9},{9,1},{17,25},{25,17},{2,10},{10... | collective-permute-start | bytes 1572872 | tf_op jit(solution)/shard_map/ppermute | solution.py:333
  38.9 8.3 %collective-permute-start.18 = (bf16[128,1024]{1,0:T(8,128)(2,1)S(1)}, bf16[128,1024]{1,0:T(8,128)(2,1)S(1)}, u32[]{:S(2)}, u32[]{:S(2)}) collective-permute-start(bf16[128,1024]{1,0:T(8,128)(2,1)S(1)} %pad_maximum_fusion.2), channel_id=1, source_target_pairs={{0,2},{2,4},{4,6},{6,7},{7,5},{5,3},{3,1},{1,0},{8,10},{10,12},{12... | collective-permute-start | bytes 786440 | tf_op jit(solution)/shard_map/ppermute | solution.py:292
  40.6 8.3 %collective-permute-start.14 = (bf16[128,1024]{1,0:T(8,128)(2,1)S(1)}, bf16[128,1024]{1,0:T(8,128)(2,1)S(1)}, u32[]{:S(2)}, u32[]{:S(2)}) collective-permute-start(bf16[128,1024]{1,0:T(8,128)(2,1)S(1)} %pad_maximum_fusion.1), channel_id=1, source_target_pairs={{2,0},{4,2},{6,4},{7,6},{5,7},{3,5},{1,3},{0,1},{10,8},{12,10},{14... | collective-permute-start | bytes 786440 | tf_op jit(solution)/shard_map/ppermute | solution.py:295
  41.1 15.8 %collective-permute-start.10 = (bf16[1024,256]{1,0:T(8,128)(2,1)S(1)}, bf16[1024,256]{1,0:T(8,128)(2,1)S(1)}, u32[]{:S(2)}, u32[]{:S(2)}) collective-permute-start(bf16[1024,256]{1,0:T(8,128)(2,1)S(1)} %get-tuple-element.49), channel_id=1, source_target_pairs={{0,8},{8,0},{16,24},{24,16},{1,9},{9,1},{17,25},{25,17},{2,10},{10... | collective-permute-start | bytes 1572872 | tf_op jit(solution)/shard_map/ppermute | solution.py:333
  47.3 7.4 %collective-permute-start.19 = (bf16[128,1024]{1,0:T(8,128)(2,1)S(1)}, bf16[128,1024]{1,0:T(8,128)(2,1)S(1)}, u32[]{:S(2)}, u32[]{:S(2)}) collective-permute-start(bf16[128,1024]{1,0:T(8,128)(2,1)S(1)} %add_convert_fusion.2), channel_id=1, source_target_pairs={{0,2},{2,4},{4,6},{6,7},{7,5},{5,3},{3,1},{1,0},{8,10},{10,12},{12... | collective-permute-start | bytes 786440 | tf_op jit(solution)/shard_map/ppermute | solution.py:292
  49.0 7.4 %collective-permute-start.15 = (bf16[128,1024]{1,0:T(8,128)(2,1)S(1)}, bf16[128,1024]{1,0:T(8,128)(2,1)S(1)}, u32[]{:S(2)}, u32[]{:S(2)}) collective-permute-start(bf16[128,1024]{1,0:T(8,128)(2,1)S(1)} %add_convert_fusion.4), channel_id=1, source_target_pairs={{2,0},{4,2},{6,4},{7,6},{5,7},{3,5},{1,3},{0,1},{10,8},{12,10},{14... | collective-permute-start | bytes 786440 | tf_op jit(solution)/shard_map/ppermute | solution.py:295
  49.6 12.5 %collective-permute-start.12 = (bf16[1024,256]{1,0:T(8,128)(2,1)S(1)}, bf16[1024,256]{1,0:T(8,128)(2,1)S(1)}, u32[]{:S(2)}, u32[]{:S(2)}) collective-permute-start(bf16[1024,256]{1,0:T(8,128)(2,1)S(1)} %add_convert_fusion), channel_id=1, source_target_pairs={{0,16},{8,24},{16,0},{24,8},{1,17},{9,25},{17,1},{25,9},{2,18},{10... | collective-permute-start | bytes 1572872 | tf_op jit(solution)/shard_map/ppermute | solution.py:333
  54.8 7.5 %collective-permute-start.20 = (bf16[128,1024]{1,0:T(8,128)(2,1)S(1)}, bf16[128,1024]{1,0:T(8,128)(2,1)S(1)}, u32[]{:S(2)}, u32[]{:S(2)}) collective-permute-start(bf16[128,1024]{1,0:T(8,128)(2,1)S(1)} %add_convert_fusion.1), channel_id=1, source_target_pairs={{0,2},{2,4},{4,6},{6,7},{7,5},{5,3},{3,1},{1,0},{8,10},{10,12},{12... | collective-permute-start | bytes 786440 | tf_op jit(solution)/shard_map/ppermute | solution.py:292
  56.5 6.4 %collective-permute-start.16 = (bf16[128,1024]{1,0:T(8,128)(2,1)S(1)}, bf16[128,1024]{1,0:T(8,128)(2,1)S(1)}, u32[]{:S(2)}, u32[]{:S(2)}) collective-permute-start(bf16[128,1024]{1,0:T(8,128)(2,1)S(1)} %add_convert_fusion.3), channel_id=1, source_target_pairs={{2,0},{4,2},{6,4},{7,6},{5,7},{3,5},{1,3},{0,1},{10,8},{12,10},{14... | collective-permute-start | bytes 786440 | tf_op jit(solution)/shard_map/ppermute | solution.py:295

commit v17 on v16

--- a/solution.py
+++ b/solution.py
@@ -282,7 +282,7 @@
     clus_count, seq_count = lax.axis_size("clus"), lax.axis_size("seq")
     local_count = cluster_sizes.shape[0]
     part_width = width // seq_count
-    first_part, half, steps = inst_rows * 5 // 8, inst_rows // 2, clus_count // 2
+    first_part, half, steps = inst_rows * 3 // 4, inst_rows // 2, clus_count // 2
 
     ring = list(range(0, clus_count, 2)) + list(range(1, clus_count, 2))[::-1]
     up = list(zip(ring, ring[1:] + ring[:1]))

time: 64 us -> 64.1 us (level)
    ppermute x9, waiting for transfers between devices: 18.1 us -> 18.9 us  [send_up(): return lax.ppermute(array, 'clus', up)]
    ppermute x9, waiting for transfers between devices: 2.86 us -> 2.1 us  [send_down(): return lax.ppermute(array, 'clus', down)]
  transfers between devices with their start and end apart: 21 -> 21, of which waited for: 11 -> 10; matrix products, arithmetic and copies ran while one was open for 1% -> 1% of each run, Pallas kernels for 14% -> 14%
where the time goes in v17:
time: 64.1 us; the launch traced here: 63.9 us
  waiting for transfers between devices  26.2 us (41%)
  starting transfers between devices  21.6 us (34%)
  Pallas kernels  11 us (17%)
  local copies, waits for them, and re-layouts  3.72 us (6%)
  between operations  0.85 us (1%)
    ppermute x9, waiting for transfers between devices, send_up(): return lax.ppermute(array, 'clus', up)  18.9 us
    ppermute x9, starting transfers between devices, send_up(): return lax.ppermute(array, 'clus', up)  16.4 us
    pallas_call x4, Pallas kernels, block_work(): pl.pallas_call(functools.partial(block_kernel, piece_rows, top_count, pos...  6.97 us
    ppermute x3, waiting for transfers between devices, seq_send(): return lax.ppermute(array, 'seq', [(k, k ^ bit) for k in range(seq_count)])  5.14 us
    unnamed x14, local copies, waits for them, and re-layouts  3.67 us
    ppermute x9, starting transfers between devices, send_down(): return lax.ppermute(array, 'clus', down)  3.48 us
    pallas_call x1, Pallas kernels, weight_work(): pl.pallas_call(functools.partial(weight_kernel, piece_rows, column_blocks...  2.37 us
    ppermute x9, waiting for transfers between devices, send_down(): return lax.ppermute(array, 'clus', down)  2.1 us
  transfers between devices with their start and end apart: 21, of which 10 were waited for; matrix products, arithmetic and copies ran while one was open for 1% of the time, Pallas kernels for 14%

profile of v17, /device:TPU:0, one launch (start us, length us, event | category | flops | bytes accessed | tf_op | source)
XLA Modules:
  0.0 63.9 jit_solution(10704340670248134427)
XLA Ops:
  0.6 3.1 %collective-permute-start = (bf16[128,1024]{1,0:T(8,128)(2,1)}, bf16[128,1024]{1,0:T(8,128)(2,1)S(1)}, u32[]{:S(2)}, u32[]{:S(2)}) collective-permute-start(bf16[128,1024]{1,0:T(8,128)(2,1)} %param.5), channel_id=1, source_target_pairs={{0,2},{2,4},{4,6},{6,7},{7,5},{5,3},{3,1},{1,0},{8,10},{10,12},{12... | collective-permute-start | bytes 786440 | tf_op jit(solution)/shard_map/ppermute | solution.py:292
  3.7 0.7 %copy-done.2 = s32[128,16]{0,1:T(8,128)S(1)} copy-done((s32[128,16]{0,1:T(8,128)S(1)}, s32[128,16]{0,1:T(8,128)}, u32[]{:S(2)}) %copy-start.2) | copy-done | bytes 8216
  4.4 0.7 %copy-done.3 = s32[128,4]{0,1:T(4,128)S(1)} copy-done((s32[128,4]{0,1:T(4,128)S(1)}, s32[128,4]{0,1:T(4,128)}, u32[]{:S(2)}) %copy-start.3) | copy-done | bytes 2072
  5.1 2.1 %collective-permute-start.1 = (bf16[8,1024]{1,0:T(8,128)(2,1)S(1)}, bf16[8,1024]{1,0:T(8,128)(2,1)S(1)}, u32[]{:S(2)}, u32[]{:S(2)}) collective-permute-start(bf16[8,1024]{1,0:T(8,128)(2,1)S(1)} %instance_ids.1), channel_id=1, source_target_pairs={{0,2},{2,4},{4,6},{6,7},{7,5},{5,3},{3,1},{1,0},{8,10},{10,12},{12... | collective-permute-start | bytes 49160 | tf_op jit(solution)/shard_map/ppermute | solution.py:292
  7.2 1.6 %copy-done = bf16[1024,1024]{1,0:T(8,128)(2,1)S(1)} copy-done((bf16[1024,1024]{1,0:T(8,128)(2,1)S(1)}, bf16[1024,1024]{1,0:T(8,128)(2,1)}, u32[]{:S(2)}) %copy-start) | copy-done | bytes 2097176
  8.8 0.7 %copy-done.4 = s32[8]{0:T(128)S(1)} copy-done((s32[8]{0:T(128)S(1)}, s32[8]{0:T(128)}, u32[]{:S(2)}) %copy-start.4) | copy-done | bytes 56
  9.5 0.6 live_labels.1.refs_3_.refs_4_
  10.4 1.5 %collective-permute-done.2 = bf16[128,1024]{1,0:T(8,128)(2,1)S(1)} collective-permute-done((bf16[128,1024]{1,0:T(8,128)(2,1)}, bf16[128,1024]{1,0:T(8,128)(2,1)S(1)}, u32[]{:S(2)}, u32[]{:S(2)}) %collective-permute-start.2) | collective-permute-done | bytes 262176 | tf_op jit(solution)/shard_map/ppermute | solution.py:295
  11.9 1.6 %collective-permute-start.4 = (bf16[136,1024]{1,0:T(8,128)(2,1)S(1)}, bf16[136,1024]{1,0:T(8,128)(2,1)S(1)}, u32[]{:S(2)}, u32[]{:S(2)}) collective-permute-start(bf16[136,1024]{1,0:T(8,128)(2,1)S(1)} %constant_dynamic-update-slice_fusion.refs_0_), channel_id=1, source_target_pairs={{0,2},{2,4},{4,6},{6,7},{7,5},{5,3},{3,1},{1,0},{8,10},{10,12},{12... | collective-permute-start | bytes 835592 | tf_op jit(solution)/shard_map/ppermute | solution.py:292
  13.5 0.5 collective-permute-start.5
  14.0 1.7 %block_work.4 = (bf16[128,1024]{1,0:T(8,128)(2,1)S(1)}, bf16[128,1024]{1,0:T(8,128)(2,1)S(1)}, bf16[128,1024]{1,0:T(8,128)(2,1)S(1)}, bf16[128,1024]{1,0:T(8,128)(2,1)S(1)}) custom-call(bf16[136,1024]{1,0:T(8,128)(2,1)S(1)} %constant_dynamic-update-slice_fusion.refs_0_, bf16[136,1024]{1,0:T(8,128)(2,1)S(1)} %constant_dynamic-update-slice_fusion.2.refs_1_, ...), custom_call_target="tpu_custom_call" | custom-call | flops 1073741824 | bytes 3670016 | tf_op jit(solution)/shard_map/block_work/pallas_call | solution.py:147
  15.7 3.2 %collective-permute-done.4.refs_0_.refs_2_ = bf16[136,1024]{1,0:T(8,128)(2,1)S(1)} collective-permute-done((bf16[136,1024]{1,0:T(8,128)(2,1)S(1)}, bf16[136,1024]{1,0:T(8,128)(2,1)S(1)}, u32[]{:S(2)}, u32[]{:S(2)}) %collective-permute-start.4) | collective-permute-done | bytes 278560 | tf_op jit(solution)/shard_map/ppermute | solution.py:292
  18.9 1.6 %collective-permute-start.6 = (bf16[136,1024]{1,0:T(8,128)(2,1)S(1)}, bf16[136,1024]{1,0:T(8,128)(2,1)S(1)}, u32[]{:S(2)}, u32[]{:S(2)}) collective-permute-start(bf16[136,1024]{1,0:T(8,128)(2,1)S(1)} %collective-permute-done.4.refs_0_.refs_2_), channel_id=1, source_target_pairs={{0,2},{2,4},{4,6},{6,7},{7,5},{5,3},{3,1},{1,0},{8,10},{10,12},{12... | collective-permute-start | bytes 835592 | tf_op jit(solution)/shard_map/ppermute | solution.py:292
  21.0 2.4 %block_work.5 = (bf16[128,1024]{1,0:T(8,128)(2,1)S(1)}, bf16[128,1024]{1,0:T(8,128)(2,1)S(1)}, bf16[128,1024]{1,0:T(8,128)(2,1)S(1)}, bf16[128,1024]{1,0:T(8,128...) custom-call(bf16[136,1024]{1,0:T(8,128)(2,1)S(1)} %collective-permute-done.4.refs_0_.refs_2_, ...), custom_call_target="tpu_custom_call" | custom-call | flops 1610612736 | bytes 4456448 | tf_op jit(solution)/shard_map/block_work/pallas_call | solution.py:147
  23.4 2.9 %collective-permute-done.6.refs_0_.refs_5_ = bf16[136,1024]{1,0:T(8,128)(2,1)S(1)} collective-permute-done((bf16[136,1024]{1,0:T(8,128)(2,1)S(1)}, bf16[136,1024]{1,0:T(8,128)(2,1)S(1)}, u32[]{:S(2)}, u32[]{:S(2)}) %collective-permute-start.6) | collective-permute-done | bytes 278560 | tf_op jit(solution)/shard_map/ppermute | solution.py:292
  26.3 1.6 %collective-permute-start.8 = (bf16[104,1024]{1,0:T(8,128)(2,1)S(1)}, bf16[104,1024]{1,0:T(8,128)(2,1)S(1)}, u32[]{:S(2)}, u32[]{:S(2)}) collective-permute-start(bf16[104,1024]{1,0:T(8,128)(2,1)S(1)} %pad_maximum_fusion.3), channel_id=1, source_target_pairs={{0,2},{2,4},{4,6},{6,7},{7,5},{5,3},{3,1},{1,0},{8,10},{10,12},{12... | collective-permute-start | bytes 638984 | tf_op jit(solution)/shard_map/ppermute | solution.py:292
  28.5 1.7 %block_work.6 = (bf16[128,1024]{1,0:T(8,128)(2,1)S(1)}, bf16[128,1024]{1,0:T(8,128)(2,1)S(1)}, bf16[128,1024]{1,0:T(8,128)(2,1)S(1)}, bf16[128,1024]{1,0:T(8,128)(2,1)S(1)}) custom-call(bf16[136,1024]{1,0:T(8,128)(2,1)S(1)} %collective-permute-done.6.refs_0_.refs_5_, bf16[136,1024]{1,0:T(8,128)(2,1)S(1)} %collective-permute-done.7.refs_1_.refs_6_, ...), custom_call_target="tpu_custom_call" | custom-call | flops 1073741824 | bytes 3670016 | tf_op jit(solution)/shard_map/block_work/pallas_call | solution.py:147
  30.2 2.5 %collective-permute-done.8.refs_0_.refs_7_ = bf16[104,1024]{1,0:T(8,128)(2,1)S(1)} collective-permute-done((bf16[104,1024]{1,0:T(8,128)(2,1)S(1)}, bf16[104,1024]{1,0:T(8,128)(2,1)S(1)}, u32[]{:S(2)}, u32[]{:S(2)}) %collective-permute-start.8) | collective-permute-done | bytes 213024 | tf_op jit(solution)/shard_map/ppermute | solution.py:292
  32.7 1.2 %block_work.7 = (bf16[64,1024]{1,0:T(8,128)(2,1)S(1)}, bf16[64,1024]{1,0:T(8,128)(2,1)S(1)}, bf16[128,1024]{1,0:T(8,128)(2,1)S(1)}) custom-call(bf16[104,1024]{1,0:T(8,128)(2,1)S(1)} %collective-permute-done.8.refs_0_.refs_7_, bf16[32,1024]{1,0:T(8,128)(2,1)S(1)} %collective-permute-done.9.refs_1_.refs_8_, bf16[1024,1024]{1,0:T(8,128)(2,1)S(1)} %copy-done.1, ...), custom_call_target="tpu_custom_call" | custom-call | flops 536870912 | bytes 2883584 | tf_op jit(solution)/shard_map/block_work/pallas_call | solution.py:147
  33.9 1.6 %collective-permute-start.17 = (bf16[64,1024]{1,0:T(8,128)(2,1)S(1)}, bf16[64,1024]{1,0:T(8,128)(2,1)S(1)}, u32[]{:S(2)}, u32[]{:S(2)}) collective-permute-start(bf16[64,1024]{1,0:T(8,128)(2,1)S(1)} %get-tuple-element.57), channel_id=1, source_target_pairs={{0,2},{2,4},{4,6},{6,7},{7,5},{5,3},{3,1},{1,0},{8,10},{10,12},{12... | collective-permute-start | bytes 393224 | tf_op jit(solution)/shard_map/ppermute | solution.py:292
  36.0 2.4 %weight_work.1 = (bf16[1024,256]{1,0:T(8,128)(2,1)S(1)}, bf16[1024,256]{1,0:T(8,128)(2,1)S(1)}, bf16[1024,256]{1,0:T(8,128)(2,1)S(1)}, bf16[1024,256]{1,0:T(8,128)(2,1)S(1)}) custom-call(bf16[136,1024]{1,0:T(8,128)(2,1)S(1)} %constant_dynamic-update-slice_fusion.refs_0_, bf16[136,1024]{1,0:T(8,128)(2,1)S(1)} %constant_dynamic-update-slice_fusion.2.refs_1_, ...), custom_call_target="tpu_custom_call" | custom-call | flops 2147483648 | bytes 4718592 | tf_op jit(solution)/shard_map/weight_work/pallas_call | solution.py:189
  39.0 1.6 %collective-permute-start.18 = (bf16[128,1024]{1,0:T(8,128)(2,1)S(1)}, bf16[128,1024]{1,0:T(8,128)(2,1)S(1)}, u32[]{:S(2)}, u32[]{:S(2)}) collective-permute-start(bf16[128,1024]{1,0:T(8,128)(2,1)S(1)} %pad_maximum_fusion.2), channel_id=1, source_target_pairs={{0,2},{2,4},{4,6},{6,7},{7,5},{5,3},{3,1},{1,0},{8,10},{10,12},{12... | collective-permute-start | bytes 786440 | tf_op jit(solution)/shard_map/ppermute | solution.py:292
  40.7 0.5 collective-permute-start.14
  41.2 6.1 %collective-permute-done.18 = bf16[128,1024]{1,0:T(8,128)(2,1)S(1)} collective-permute-done((bf16[128,1024]{1,0:T(8,128)(2,1)S(1)}, bf16[128,1024]{1,0:T(8,128)(2,1)S(1)}, u32[]{:S(2)}, u32[]{:S(2)}) %collective-permute-start.18) | collective-permute-done | bytes 262176 | tf_op jit(solution)/shard_map/ppermute | solution.py:292
  47.3 1.6 %collective-permute-start.19 = (bf16[128,1024]{1,0:T(8,128)(2,1)S(1)}, bf16[128,1024]{1,0:T(8,128)(2,1)S(1)}, u32[]{:S(2)}, u32[]{:S(2)}) collective-permute-start(bf16[128,1024]{1,0:T(8,128)(2,1)S(1)} %add_convert_fusion.2), channel_id=1, source_target_pairs={{0,2},{2,4},{4,6},{6,7},{7,5},{5,3},{3,1},{1,0},{8,10},{10,12},{12... | collective-permute-start | bytes 786440 | tf_op jit(solution)/shard_map/ppermute | solution.py:292
  49.0 0.5 collective-permute-start.15
  49.7 1.6 %collective-permute-start.12 = (bf16[1024,256]{1,0:T(8,128)(2,1)S(1)}, bf16[1024,256]{1,0:T(8,128)(2,1)S(1)}, u32[]{:S(2)}, u32[]{:S(2)}) collective-permute-start(bf16[1024,256]{1,0:T(8,128)(2,1)S(1)} %add_convert_fusion), channel_id=1, source_target_pairs={{0,16},{8,24},{16,0},{24,8},{1,17},{9,25},{17,1},{25,9},{2,18},{10... | collective-permute-start | bytes 1572872 | tf_op jit(solution)/shard_map/ppermute | solution.py:333
  51.2 3.5 %collective-permute-done.19 = bf16[128,1024]{1,0:T(8,128)(2,1)S(1)} collective-permute-done((bf16[128,1024]{1,0:T(8,128)(2,1)S(1)}, bf16[128,1024]{1,0:T(8,128)(2,1)S(1)}, u32[]{:S(2)}, u32[]{:S(2)}) %collective-permute-start.19) | collective-permute-done | bytes 262176 | tf_op jit(solution)/shard_map/ppermute | solution.py:292
  54.8 1.6 %collective-permute-start.20 = (bf16[128,1024]{1,0:T(8,128)(2,1)S(1)}, bf16[128,1024]{1,0:T(8,128)(2,1)S(1)}, u32[]{:S(2)}, u32[]{:S(2)}) collective-permute-start(bf16[128,1024]{1,0:T(8,128)(2,1)S(1)} %add_convert_fusion.1), channel_id=1, source_target_pairs={{0,2},{2,4},{4,6},{6,7},{7,5},{5,3},{3,1},{1,0},{8,10},{10,12},{12... | collective-permute-start | bytes 786440 | tf_op jit(solution)/shard_map/ppermute | solution.py:292
  57.0 5.1 %collective-permute-done.12.refs_2_ = bf16[1024,256]{1,0:T(8,128)(2,1)S(1)} collective-permute-done((bf16[1024,256]{1,0:T(8,128)(2,1)S(1)}, bf16[1024,256]{1,0:T(8,128)(2,1)S(1)}, u32[]{:S(2)}, u32[]{:S(2)}) %collective-permute-start.12) | collective-permute-done | bytes 524320 | tf_op jit(solution)/shard_map/ppermute | solution.py:333
  62.4 0.6 collective-permute-done.16.refs_1_
  63.0 0.9 %finish.1 = (bf16[128,1024]{1,0:T(8,128)(2,1)}, bf16[1024,256]{1,0:T(8,128)(2,1)}) custom-call(bf16[1024,256]{1,0:T(8,128)(2,1)S(1)} %weight_sum.1.weight_ref, bf16[128,1024]{1,0:T(8,128)(2,1)S(1)} %get-tuple-element.52.refs_0_, bf16[128,1024]{1,0:T(8,128)(2,1)S(1)} %collective-permute-done.16.refs_1_, bf16[128,1024]{1,0:T(8,128)(2,1)S(1)} %collective-permute-done.20.refs_2_), custom_call_target="tpu_custom_call" | custom-call | flops 393216 | bytes 2097152 | tf_op jit(solution)/shard_map/finish/pallas_call | solution.py:253
  (51 shorter events, 3.7 us)
Async XLA Ops:
  0.6 9.7 %collective-permute-start = (bf16[128,1024]{1,0:T(8,128)(2,1)}, bf16[128,1024]{1,0:T(8,128)(2,1)S(1)}, u32[]{:S(2)}, u32[]{:S(2)}) collective-permute-start(bf16[128,1024]{1,0:T(8,128)(2,1)} %param.5), channel_id=1, source_target_pairs={{0,2},{2,4},{4,6},{6,7},{7,5},{5,3},{3,1},{1,0},{8,10},{10,12},{12... | collective-permute-start | bytes 786440 | tf_op jit(solution)/shard_map/ppermute | solution.py:292
  3.7 8.2 %collective-permute-start.2 = (bf16[128,1024]{1,0:T(8,128)(2,1)}, bf16[128,1024]{1,0:T(8,128)(2,1)S(1)}, u32[]{:S(2)}, u32[]{:S(2)}) collective-permute-start(bf16[128,1024]{1,0:T(8,128)(2,1)} %param.5), channel_id=1, source_target_pairs={{2,0},{4,2},{6,4},{7,6},{5,7},{3,5},{1,3},{0,1},{10,8},{12,10},{14... | collective-permute-start | bytes 786440 | tf_op jit(solution)/shard_map/ppermute | solution.py:295
  3.7 0.7 %copy-start.2 = (s32[128,16]{0,1:T(8,128)S(1)}, s32[128,16]{0,1:T(8,128)}, u32[]{:S(2)}) copy-start(s32[128,16]{0,1:T(8,128)} %param.6) | copy-start | bytes 24580
  4.4 0.7 %copy-start.3 = (s32[128,4]{0,1:T(4,128)S(1)}, s32[128,4]{0,1:T(4,128)}, u32[]{:S(2)}) copy-start(s32[128,4]{0,1:T(4,128)} %param.7) | copy-start | bytes 6148
  5.1 6.7 %collective-permute-start.1 = (bf16[8,1024]{1,0:T(8,128)(2,1)S(1)}, bf16[8,1024]{1,0:T(8,128)(2,1)S(1)}, u32[]{:S(2)}, u32[]{:S(2)}) collective-permute-start(bf16[8,1024]{1,0:T(8,128)(2,1)S(1)} %instance_ids.1), channel_id=1, source_target_pairs={{0,2},{2,4},{4,6},{6,7},{7,5},{5,3},{3,1},{1,0},{8,10},{10,12},{12... | collective-permute-start | bytes 49160 | tf_op jit(solution)/shard_map/ppermute | solution.py:292
  7.2 6.3 %collective-permute-start.3 = (bf16[8,1024]{1,0:T(8,128)(2,1)S(1)}, bf16[8,1024]{1,0:T(8,128)(2,1)S(1)}, u32[]{:S(2)}, u32[]{:S(2)}) collective-permute-start(bf16[8,1024]{1,0:T(8,128)(2,1)S(1)} %instance_ids.1), channel_id=1, source_target_pairs={{2,0},{4,2},{6,4},{7,6},{5,7},{3,5},{1,3},{0,1},{10,8},{12,10},{14... | collective-permute-start | bytes 49160 | tf_op jit(solution)/shard_map/ppermute | solution.py:295
  7.2 1.6 %copy-start = (bf16[1024,1024]{1,0:T(8,128)(2,1)S(1)}, bf16[1024,1024]{1,0:T(8,128)(2,1)}, u32[]{:S(2)}) copy-start(bf16[1024,1024]{1,0:T(8,128)(2,1)} %refs_2_.5) | copy-start | bytes 6291460
  8.8 0.7 %copy-start.4 = (s32[8]{0:T(128)S(1)}, s32[8]{0:T(128)}, u32[]{:S(2)}) copy-start(s32[8]{0:T(128)} %size_ref.1) | copy-start | bytes 100
  9.4 4.6 %copy-start.1 = (bf16[1024,1024]{1,0:T(8,128)(2,1)S(1)}, bf16[1024,1024]{1,0:T(8,128)(2,1)}, u32[]{:S(2)}) copy-start(bf16[1024,1024]{1,0:T(8,128)(2,1)} %refs_2_.5) | copy-start | bytes 6291460
  11.9 7.0 %collective-permute-start.4 = (bf16[136,1024]{1,0:T(8,128)(2,1)S(1)}, bf16[136,1024]{1,0:T(8,128)(2,1)S(1)}, u32[]{:S(2)}, u32[]{:S(2)}) collective-permute-start(bf16[136,1024]{1,0:T(8,128)(2,1)S(1)} %constant_dynamic-update-slice_fusion.refs_0_), channel_id=1, source_target_pairs={{0,2},{2,4},{4,6},{6,7},{7,5},{5,3},{3,1},{1,0},{8,10},{10,12},{12... | collective-permute-start | bytes 835592 | tf_op jit(solution)/shard_map/ppermute | solution.py:292
  13.5 7.0 %copy-start.5 = (bf16[128,1024]{1,0:T(8,128)(2,1)S(1)}, bf16[128,1024]{1,0:T(8,128)(2,1)}, u32[]{:S(2)}) copy-start(bf16[128,1024]{1,0:T(8,128)(2,1)} %param.5) | copy-start | bytes 786436
  13.5 7.0 %collective-permute-start.5 = (bf16[136,1024]{1,0:T(8,128)(2,1)S(1)}, bf16[136,1024]{1,0:T(8,128)(2,1)S(1)}, u32[]{:S(2)}, u32[]{:S(2)}) collective-permute-start(bf16[136,1024]{1,0:T(8,128)(2,1)S(1)} %constant_dynamic-update-slice_fusion.2.refs_1_), channel_id=1, source_target_pairs={{2,0},{4,2},{6,4},{7,6},{5,7},{3,5},{1,3},{0,1},{10,8},{12,10},{14... | collective-permute-start | bytes 835592 | tf_op jit(solution)/shard_map/ppermute | solution.py:295
  18.9 7.4 %collective-permute-start.6 = (bf16[136,1024]{1,0:T(8,128)(2,1)S(1)}, bf16[136,1024]{1,0:T(8,128)(2,1)S(1)}, u32[]{:S(2)}, u32[]{:S(2)}) collective-permute-start(bf16[136,1024]{1,0:T(8,128)(2,1)S(1)} %collective-permute-done.4.refs_0_.refs_2_), channel_id=1, source_target_pairs={{0,2},{2,4},{4,6},{6,7},{7,5},{5,3},{3,1},{1,0},{8,10},{10,12},{12... | collective-permute-start | bytes 835592 | tf_op jit(solution)/shard_map/ppermute | solution.py:292
  20.5 7.5 %collective-permute-start.7 = (bf16[136,1024]{1,0:T(8,128)(2,1)S(1)}, bf16[136,1024]{1,0:T(8,128)(2,1)S(1)}, u32[]{:S(2)}, u32[]{:S(2)}) collective-permute-start(bf16[136,1024]{1,0:T(8,128)(2,1)S(1)} %collective-permute-done.5.refs_1_.refs_3_), channel_id=1, source_target_pairs={{2,0},{4,2},{6,4},{7,6},{5,7},{3,5},{1,3},{0,1},{10,8},{12,10},{14... | collective-permute-start | bytes 835592 | tf_op jit(solution)/shard_map/ppermute | solution.py:295
  26.3 6.4 %collective-permute-start.8 = (bf16[104,1024]{1,0:T(8,128)(2,1)S(1)}, bf16[104,1024]{1,0:T(8,128)(2,1)S(1)}, u32[]{:S(2)}, u32[]{:S(2)}) collective-permute-start(bf16[104,1024]{1,0:T(8,128)(2,1)S(1)} %pad_maximum_fusion.3), channel_id=1, source_target_pairs={{0,2},{2,4},{4,6},{6,7},{7,5},{5,3},{3,1},{1,0},{8,10},{10,12},{12... | collective-permute-start | bytes 638984 | tf_op jit(solution)/shard_map/ppermute | solution.py:292
  28.0 4.7 %collective-permute-start.9 = (bf16[32,1024]{1,0:T(8,128)(2,1)S(1)}, bf16[32,1024]{1,0:T(8,128)(2,1)S(1)}, u32[]{:S(2)}, u32[]{:S(2)}) collective-permute-start(bf16[32,1024]{1,0:T(8,128)(2,1)S(1)} %slice.23), channel_id=1, source_target_pairs={{2,0},{4,2},{6,4},{7,6},{5,7},{3,5},{1,3},{0,1},{10,8},{12,10},{14... | collective-permute-start | bytes 196616 | tf_op jit(solution)/shard_map/ppermute | solution.py:295
  33.9 5.0 %collective-permute-start.17 = (bf16[64,1024]{1,0:T(8,128)(2,1)S(1)}, bf16[64,1024]{1,0:T(8,128)(2,1)S(1)}, u32[]{:S(2)}, u32[]{:S(2)}) collective-permute-start(bf16[64,1024]{1,0:T(8,128)(2,1)S(1)} %get-tuple-element.57), channel_id=1, source_target_pairs={{0,2},{2,4},{4,6},{6,7},{7,5},{5,3},{3,1},{1,0},{8,10},{10,12},{12... | collective-permute-start | bytes 393224 | tf_op jit(solution)/shard_map/ppermute | solution.py:292
  35.5 5.1 %collective-permute-start.13 = (bf16[64,1024]{1,0:T(8,128)(2,1)S(1)}, bf16[64,1024]{1,0:T(8,128)(2,1)S(1)}, u32[]{:S(2)}, u32[]{:S(2)}) collective-permute-start(bf16[64,1024]{1,0:T(8,128)(2,1)S(1)} %get-tuple-element.53), channel_id=1, source_target_pairs={{2,0},{4,2},{6,4},{7,6},{5,7},{3,5},{1,3},{0,1},{10,8},{12,10},{14... | collective-permute-start | bytes 393224 | tf_op jit(solution)/shard_map/ppermute | solution.py:295
  38.4 11.2 %collective-permute-start.11 = (bf16[1024,256]{1,0:T(8,128)(2,1)S(1)}, bf16[1024,256]{1,0:T(8,128)(2,1)S(1)}, u32[]{:S(2)}, u32[]{:S(2)}) collective-permute-start(bf16[1024,256]{1,0:T(8,128)(2,1)S(1)} %get-tuple-element.51), channel_id=1, source_target_pairs={{0,8},{8,0},{16,24},{24,16},{1,9},{9,1},{17,25},{25,17},{2,10},{10... | collective-permute-start | bytes 1572872 | tf_op jit(solution)/shard_map/ppermute | solution.py:333
  39.0 8.3 %collective-permute-start.18 = (bf16[128,1024]{1,0:T(8,128)(2,1)S(1)}, bf16[128,1024]{1,0:T(8,128)(2,1)S(1)}, u32[]{:S(2)}, u32[]{:S(2)}) collective-permute-start(bf16[128,1024]{1,0:T(8,128)(2,1)S(1)} %pad_maximum_fusion.2), channel_id=1, source_target_pairs={{0,2},{2,4},{4,6},{6,7},{7,5},{5,3},{3,1},{1,0},{8,10},{10,12},{12... | collective-permute-start | bytes 786440 | tf_op jit(solution)/shard_map/ppermute | solution.py:292
  40.7 8.3 %collective-permute-start.14 = (bf16[128,1024]{1,0:T(8,128)(2,1)S(1)}, bf16[128,1024]{1,0:T(8,128)(2,1)S(1)}, u32[]{:S(2)}, u32[]{:S(2)}) collective-permute-start(bf16[128,1024]{1,0:T(8,128)(2,1)S(1)} %pad_maximum_fusion.1), channel_id=1, source_target_pairs={{2,0},{4,2},{6,4},{7,6},{5,7},{3,5},{1,3},{0,1},{10,8},{12,10},{14... | collective-permute-start | bytes 786440 | tf_op jit(solution)/shard_map/ppermute | solution.py:295
  41.2 15.8 %collective-permute-start.10 = (bf16[1024,256]{1,0:T(8,128)(2,1)S(1)}, bf16[1024,256]{1,0:T(8,128)(2,1)S(1)}, u32[]{:S(2)}, u32[]{:S(2)}) collective-permute-start(bf16[1024,256]{1,0:T(8,128)(2,1)S(1)} %get-tuple-element.49), channel_id=1, source_target_pairs={{0,8},{8,0},{16,24},{24,16},{1,9},{9,1},{17,25},{25,17},{2,10},{10... | collective-permute-start | bytes 1572872 | tf_op jit(solution)/shard_map/ppermute | solution.py:333
  47.3 7.4 %collective-permute-start.19 = (bf16[128,1024]{1,0:T(8,128)(2,1)S(1)}, bf16[128,1024]{1,0:T(8,128)(2,1)S(1)}, u32[]{:S(2)}, u32[]{:S(2)}) collective-permute-start(bf16[128,1024]{1,0:T(8,128)(2,1)S(1)} %add_convert_fusion.2), channel_id=1, source_target_pairs={{0,2},{2,4},{4,6},{6,7},{7,5},{5,3},{3,1},{1,0},{8,10},{10,12},{12... | collective-permute-start | bytes 786440 | tf_op jit(solution)/shard_map/ppermute | solution.py:292
  49.0 7.4 %collective-permute-start.15 = (bf16[128,1024]{1,0:T(8,128)(2,1)S(1)}, bf16[128,1024]{1,0:T(8,128)(2,1)S(1)}, u32[]{:S(2)}, u32[]{:S(2)}) collective-permute-start(bf16[128,1024]{1,0:T(8,128)(2,1)S(1)} %add_convert_fusion.4), channel_id=1, source_target_pairs={{2,0},{4,2},{6,4},{7,6},{5,7},{3,5},{1,3},{0,1},{10,8},{12,10},{14... | collective-permute-start | bytes 786440 | tf_op jit(solution)/shard_map/ppermute | solution.py:295
  49.7 12.5 %collective-permute-start.12 = (bf16[1024,256]{1,0:T(8,128)(2,1)S(1)}, bf16[1024,256]{1,0:T(8,128)(2,1)S(1)}, u32[]{:S(2)}, u32[]{:S(2)}) collective-permute-start(bf16[1024,256]{1,0:T(8,128)(2,1)S(1)} %add_convert_fusion), channel_id=1, source_target_pairs={{0,16},{8,24},{16,0},{24,8},{1,17},{9,25},{17,1},{25,9},{2,18},{10... | collective-permute-start | bytes 1572872 | tf_op jit(solution)/shard_map/ppermute | solution.py:333
  54.8 7.5 %collective-permute-start.20 = (bf16[128,1024]{1,0:T(8,128)(2,1)S(1)}, bf16[128,1024]{1,0:T(8,128)(2,1)S(1)}, u32[]{:S(2)}, u32[]{:S(2)}) collective-permute-start(bf16[128,1024]{1,0:T(8,128)(2,1)S(1)} %add_convert_fusion.1), channel_id=1, source_target_pairs={{0,2},{2,4},{4,6},{6,7},{7,5},{5,3},{3,1},{1,0},{8,10},{10,12},{12... | collective-permute-start | bytes 786440 | tf_op jit(solution)/shard_map/ppermute | solution.py:292
  56.5 6.4 %collective-permute-start.16 = (bf16[128,1024]{1,0:T(8,128)(2,1)S(1)}, bf16[128,1024]{1,0:T(8,128)(2,1)S(1)}, u32[]{:S(2)}, u32[]{:S(2)}) collective-permute-start(bf16[128,1024]{1,0:T(8,128)(2,1)S(1)} %add_convert_fusion.3), channel_id=1, source_target_pairs={{2,0},{4,2},{6,4},{7,6},{5,7},{3,5},{1,3},{0,1},{10,8},{12,10},{14... | collective-permute-start | bytes 786440 | tf_op jit(solution)/shard_map/ppermute | solution.py:295

commit v18 on v16

--- a/solution.py
+++ b/solution.py
@@ -335,14 +335,9 @@
     slots = list(range(seq_count))[::-1]
     parts = weight_work(used, slopes, slots, part_width, scale)
     terms = {q: [part] for q, part in zip(slots, parts)}
-    bit = 1
-    while bit < seq_count:
-        for q in [q for q in sorted(terms, reverse=True) if q & bit]:
-            values = terms.pop(q)
-            terms[q ^ bit].append(seq_send(add(*values) if len(values) > 1 else values[0], bit))
-        bit *= 2
-
     for k in range(steps, 0, -1):
+        if k == max(steps - 2, 1):
+            third = to_down
         from_above, from_below = send_down(to_down), send_up(to_up)
         if k == steps:
             near_below, near_above = below_grad[k - 1], above_grad[k - 1]
@@ -350,6 +345,16 @@
             to_up = jnp.concatenate([near_above[:half], add(near_above[half:], from_below)], axis=0)
         elif k > 1:
             to_down, to_up = add(below_grad[k - 1], from_above), add(above_grad[k - 1], from_below)
+
+    bit = 1
+    while bit < seq_count:
+        for q in [q for q in sorted(terms, reverse=True) if q & bit]:
+            values = terms.pop(q)
+            if bit == 1 and q < seq_count // 2:
+                values = [after(values[0], third)]
+            terms[q ^ bit].append(seq_send(add(*values) if len(values) > 1 else values[0], bit))
+        bit *= 2
+
     feature_grad, weight_grad = finish(weight_sum(terms[0]), [own_grad, from_above, from_below], 2)
     return (feature_grad, weight_grad)
 

time: 64 us -> 65.4 us (1.022)
  waiting for transfers between devices: 26.1 us -> 27.5 us
    ppermute x3, waiting for transfers between devices: 5.14 us -> 7.06 us  [seq_send(): return lax.ppermute(array, 'seq', [(k, k ^ bit) for k in range(seq_count)])]
  transfers between devices with their start and end apart: 21 -> 21, of which waited for: 11 -> 10; matrix products, arithmetic and copies ran while one was open for 1% -> 1% of each run, Pallas kernels for 14% -> 14%
where the time goes in v18:
time: 65.4 us; the launch traced here: 65.1 us
  waiting for transfers between devices  27.5 us (42%)
  starting transfers between devices  21.5 us (33%)
  Pallas kernels  11 us (17%)
  local copies, waits for them, and re-layouts  3.72 us (6%)
  between operations  0.85 us (1%)
    ppermute x9, waiting for transfers between devices, send_up(): return lax.ppermute(array, 'clus', up)  18.1 us
    ppermute x9, starting transfers between devices, send_up(): return lax.ppermute(array, 'clus', up)  16.4 us
    ppermute x3, waiting for transfers between devices, seq_send(): return lax.ppermute(array, 'seq', [(k, k ^ bit) for k in range(seq_count)])  7.06 us
    pallas_call x4, Pallas kernels, block_work(): pl.pallas_call(functools.partial(block_kernel, piece_rows, top_count, pos...  6.97 us
    unnamed x14, local copies, waits for them, and re-layouts  3.67 us
    ppermute x9, starting transfers between devices, send_down(): return lax.ppermute(array, 'clus', down)  3.49 us
    pallas_call x1, Pallas kernels, weight_work(): pl.pallas_call(functools.partial(weight_kernel, piece_rows, column_blocks...  2.37 us
    ppermute x9, waiting for transfers between devices, send_down(): return lax.ppermute(array, 'clus', down)  2.29 us
  transfers between devices with their start and end apart: 21, of which 10 were waited for; matrix products, arithmetic and copies ran while one was open for 1% of the time, Pallas kernels for 14%

profile of v18, /device:TPU:0, one launch (start us, length us, event | category | flops | bytes accessed | tf_op | source)
XLA Modules:
  0.0 65.1 jit_solution(9031892447535701367)
XLA Ops:
  0.6 3.1 %collective-permute-start = (bf16[128,1024]{1,0:T(8,128)(2,1)}, bf16[128,1024]{1,0:T(8,128)(2,1)S(1)}, u32[]{:S(2)}, u32[]{:S(2)}) collective-permute-start(bf16[128,1024]{1,0:T(8,128)(2,1)} %param.5), channel_id=1, source_target_pairs={{0,2},{2,4},{4,6},{6,7},{7,5},{5,3},{3,1},{1,0},{8,10},{10,12},{12... | collective-permute-start | bytes 786440 | tf_op jit(solution)/shard_map/ppermute | solution.py:292
  3.7 0.7 %copy-done.2 = s32[128,16]{0,1:T(8,128)S(1)} copy-done((s32[128,16]{0,1:T(8,128)S(1)}, s32[128,16]{0,1:T(8,128)}, u32[]{:S(2)}) %copy-start.2) | copy-done | bytes 8216
  4.4 0.7 %copy-done.3 = s32[128,4]{0,1:T(4,128)S(1)} copy-done((s32[128,4]{0,1:T(4,128)S(1)}, s32[128,4]{0,1:T(4,128)}, u32[]{:S(2)}) %copy-start.3) | copy-done | bytes 2072
  5.1 2.1 %collective-permute-start.1 = (bf16[8,1024]{1,0:T(8,128)(2,1)S(1)}, bf16[8,1024]{1,0:T(8,128)(2,1)S(1)}, u32[]{:S(2)}, u32[]{:S(2)}) collective-permute-start(bf16[8,1024]{1,0:T(8,128)(2,1)S(1)} %instance_ids.1), channel_id=1, source_target_pairs={{0,2},{2,4},{4,6},{6,7},{7,5},{5,3},{3,1},{1,0},{8,10},{10,12},{12... | collective-permute-start | bytes 49160 | tf_op jit(solution)/shard_map/ppermute | solution.py:292
  7.2 1.6 %copy-done = bf16[1024,1024]{1,0:T(8,128)(2,1)S(1)} copy-done((bf16[1024,1024]{1,0:T(8,128)(2,1)S(1)}, bf16[1024,1024]{1,0:T(8,128)(2,1)}, u32[]{:S(2)}) %copy-start) | copy-done | bytes 2097176
  8.8 0.7 %copy-done.4 = s32[8]{0:T(128)S(1)} copy-done((s32[8]{0:T(128)S(1)}, s32[8]{0:T(128)}, u32[]{:S(2)}) %copy-start.4) | copy-done | bytes 56
  9.5 0.6 live_labels.1.refs_3_.refs_4_
  10.4 1.5 %collective-permute-done.2 = bf16[128,1024]{1,0:T(8,128)(2,1)S(1)} collective-permute-done((bf16[128,1024]{1,0:T(8,128)(2,1)}, bf16[128,1024]{1,0:T(8,128)(2,1)S(1)}, u32[]{:S(2)}, u32[]{:S(2)}) %collective-permute-start.2) | collective-permute-done | bytes 262176 | tf_op jit(solution)/shard_map/ppermute | solution.py:295
  11.9 1.6 %collective-permute-start.4 = (bf16[136,1024]{1,0:T(8,128)(2,1)S(1)}, bf16[136,1024]{1,0:T(8,128)(2,1)S(1)}, u32[]{:S(2)}, u32[]{:S(2)}) collective-permute-start(bf16[136,1024]{1,0:T(8,128)(2,1)S(1)} %constant_dynamic-update-slice_fusion.refs_0_), channel_id=1, source_target_pairs={{0,2},{2,4},{4,6},{6,7},{7,5},{5,3},{3,1},{1,0},{8,10},{10,12},{12... | collective-permute-start | bytes 835592 | tf_op jit(solution)/shard_map/ppermute | solution.py:292
  14.0 1.7 %block_work.4 = (bf16[128,1024]{1,0:T(8,128)(2,1)S(1)}, bf16[128,1024]{1,0:T(8,128)(2,1)S(1)}, bf16[128,1024]{1,0:T(8,128)(2,1)S(1)}, bf16[128,1024]{1,0:T(8,128)(2,1)S(1)}) custom-call(bf16[136,1024]{1,0:T(8,128)(2,1)S(1)} %constant_dynamic-update-slice_fusion.refs_0_, bf16[136,1024]{1,0:T(8,128)(2,1)S(1)} %constant_dynamic-update-slice_fusion.2.refs_1_, ...), custom_call_target="tpu_custom_call" | custom-call | flops 1073741824 | bytes 3670016 | tf_op jit(solution)/shard_map/block_work/pallas_call | solution.py:147
  15.7 3.2 %collective-permute-done.4.refs_0_.refs_2_ = bf16[136,1024]{1,0:T(8,128)(2,1)S(1)} collective-permute-done((bf16[136,1024]{1,0:T(8,128)(2,1)S(1)}, bf16[136,1024]{1,0:T(8,128)(2,1)S(1)}, u32[]{:S(2)}, u32[]{:S(2)}) %collective-permute-start.4) | collective-permute-done | bytes 278560 | tf_op jit(solution)/shard_map/ppermute | solution.py:292
  18.9 1.6 %collective-permute-start.6 = (bf16[136,1024]{1,0:T(8,128)(2,1)S(1)}, bf16[136,1024]{1,0:T(8,128)(2,1)S(1)}, u32[]{:S(2)}, u32[]{:S(2)}) collective-permute-start(bf16[136,1024]{1,0:T(8,128)(2,1)S(1)} %collective-permute-done.4.refs_0_.refs_2_), channel_id=1, source_target_pairs={{0,2},{2,4},{4,6},{6,7},{7,5},{5,3},{3,1},{1,0},{8,10},{10,12},{12... | collective-permute-start | bytes 835592 | tf_op jit(solution)/shard_map/ppermute | solution.py:292
  21.0 2.4 %block_work.5 = (bf16[128,1024]{1,0:T(8,128)(2,1)S(1)}, bf16[128,1024]{1,0:T(8,128)(2,1)S(1)}, bf16[128,1024]{1,0:T(8,128)(2,1)S(1)}, bf16[128,1024]{1,0:T(8,128...) custom-call(bf16[136,1024]{1,0:T(8,128)(2,1)S(1)} %collective-permute-done.4.refs_0_.refs_2_, ...), custom_call_target="tpu_custom_call" | custom-call | flops 1610612736 | bytes 4456448 | tf_op jit(solution)/shard_map/block_work/pallas_call | solution.py:147
  23.4 2.9 %collective-permute-done.6.refs_0_.refs_5_ = bf16[136,1024]{1,0:T(8,128)(2,1)S(1)} collective-permute-done((bf16[136,1024]{1,0:T(8,128)(2,1)S(1)}, bf16[136,1024]{1,0:T(8,128)(2,1)S(1)}, u32[]{:S(2)}, u32[]{:S(2)}) %collective-permute-start.6) | collective-permute-done | bytes 278560 | tf_op jit(solution)/shard_map/ppermute | solution.py:292
  26.3 1.6 %collective-permute-start.8 = (bf16[88,1024]{1,0:T(8,128)(2,1)S(1)}, bf16[88,1024]{1,0:T(8,128)(2,1)S(1)}, u32[]{:S(2)}, u32[]{:S(2)}) collective-permute-start(bf16[88,1024]{1,0:T(8,128)(2,1)S(1)} %pad_maximum_fusion.3), channel_id=1, source_target_pairs={{0,2},{2,4},{4,6},{6,7},{7,5},{5,3},{3,1},{1,0},{8,10},{10,12},{12... | collective-permute-start | bytes 540680 | tf_op jit(solution)/shard_map/ppermute | solution.py:292
  28.5 1.7 %block_work.6 = (bf16[128,1024]{1,0:T(8,128)(2,1)S(1)}, bf16[128,1024]{1,0:T(8,128)(2,1)S(1)}, bf16[128,1024]{1,0:T(8,128)(2,1)S(1)}, bf16[128,1024]{1,0:T(8,128)(2,1)S(1)}) custom-call(bf16[136,1024]{1,0:T(8,128)(2,1)S(1)} %collective-permute-done.6.refs_0_.refs_5_, bf16[136,1024]{1,0:T(8,128)(2,1)S(1)} %collective-permute-done.7.refs_1_.refs_6_, ...), custom_call_target="tpu_custom_call" | custom-call | flops 1073741824 | bytes 3670016 | tf_op jit(solution)/shard_map/block_work/pallas_call | solution.py:147
  30.2 1.7 %collective-permute-done.8.refs_0_.refs_7_ = bf16[88,1024]{1,0:T(8,128)(2,1)S(1)} collective-permute-done((bf16[88,1024]{1,0:T(8,128)(2,1)S(1)}, bf16[88,1024]{1,0:T(8,128)(2,1)S(1)}, u32[]{:S(2)}, u32[]{:S(2)}) %collective-permute-start.8) | collective-permute-done | bytes 180256 | tf_op jit(solution)/shard_map/ppermute | solution.py:292
  31.9 0.8 %collective-permute-done.9.refs_1_.refs_8_ = bf16[48,1024]{1,0:T(8,128)(2,1)S(1)} collective-permute-done((bf16[48,1024]{1,0:T(8,128)(2,1)S(1)}, bf16[48,1024]{1,0:T(8,128)(2,1)S(1)}, u32[]{:S(2)}, u32[]{:S(2)}) %collective-permute-start.9) | collective-permute-done | bytes 98336 | tf_op jit(solution)/shard_map/ppermute | solution.py:295
  32.7 1.2 %block_work.7 = (bf16[64,1024]{1,0:T(8,128)(2,1)S(1)}, bf16[64,1024]{1,0:T(8,128)(2,1)S(1)}, bf16[128,1024]{1,0:T(8,128)(2,1)S(1)}) custom-call(bf16[88,1024]{1,0:T(8,128)(2,1)S(1)} %collective-permute-done.8.refs_0_.refs_7_, bf16[48,1024]{1,0:T(8,128)(2,1)S(1)} %collective-permute-done.9.refs_1_.refs_8_, bf16[1024,1024]{1,0:T(8,128)(2,1)S(1)} %copy-done.1, ...), custom_call_target="tpu_custom_call" | custom-call | flops 536870912 | bytes 2883584 | tf_op jit(solution)/shard_map/block_work/pallas_call | solution.py:147
  33.9 1.6 %collective-permute-start.17 = (bf16[64,1024]{1,0:T(8,128)(2,1)S(1)}, bf16[64,1024]{1,0:T(8,128)(2,1)S(1)}, u32[]{:S(2)}, u32[]{:S(2)}) collective-permute-start(bf16[64,1024]{1,0:T(8,128)(2,1)S(1)} %get-tuple-element.59), channel_id=1, source_target_pairs={{0,2},{2,4},{4,6},{6,7},{7,5},{5,3},{3,1},{1,0},{8,10},{10,12},{12... | collective-permute-start | bytes 393224 | tf_op jit(solution)/shard_map/ppermute | solution.py:292
  35.9 2.4 %weight_work.1 = (bf16[1024,256]{1,0:T(8,128)(2,1)S(1)}, bf16[1024,256]{1,0:T(8,128)(2,1)S(1)}, bf16[1024,256]{1,0:T(8,128)(2,1)S(1)}, bf16[1024,256]{1,0:T(8,128)(2,1)S(1)}) custom-call(bf16[136,1024]{1,0:T(8,128)(2,1)S(1)} %constant_dynamic-update-slice_fusion.refs_0_, bf16[136,1024]{1,0:T(8,128)(2,1)S(1)} %constant_dynamic-update-slice_fusion.2.refs_1_, ...), custom_call_target="tpu_custom_call" | custom-call | flops 2147483648 | bytes 4718592 | tf_op jit(solution)/shard_map/weight_work/pallas_call | solution.py:189
  38.9 1.6 %collective-permute-start.18 = (bf16[128,1024]{1,0:T(8,128)(2,1)S(1)}, bf16[128,1024]{1,0:T(8,128)(2,1)S(1)}, u32[]{:S(2)}, u32[]{:S(2)}) collective-permute-start(bf16[128,1024]{1,0:T(8,128)(2,1)S(1)} %pad_maximum_fusion.2), channel_id=1, source_target_pairs={{0,2},{2,4},{4,6},{6,7},{7,5},{5,3},{3,1},{1,0},{8,10},{10,12},{12... | collective-permute-start | bytes 786440 | tf_op jit(solution)/shard_map/ppermute | solution.py:292
  40.6 0.5 collective-permute-start.11
  41.1 6.1 %collective-permute-done.18 = bf16[128,1024]{1,0:T(8,128)(2,1)S(1)} collective-permute-done((bf16[128,1024]{1,0:T(8,128)(2,1)S(1)}, bf16[128,1024]{1,0:T(8,128)(2,1)S(1)}, u32[]{:S(2)}, u32[]{:S(2)}) %collective-permute-start.18) | collective-permute-done | bytes 262176 | tf_op jit(solution)/shard_map/ppermute | solution.py:292
  47.3 1.6 %collective-permute-start.19 = (bf16[128,1024]{1,0:T(8,128)(2,1)S(1)}, bf16[128,1024]{1,0:T(8,128)(2,1)S(1)}, u32[]{:S(2)}, u32[]{:S(2)}) collective-permute-start(bf16[128,1024]{1,0:T(8,128)(2,1)S(1)} %add_convert_fusion.2), channel_id=1, source_target_pairs={{0,2},{2,4},{4,6},{6,7},{7,5},{5,3},{3,1},{1,0},{8,10},{10,12},{12... | collective-permute-start | bytes 786440 | tf_op jit(solution)/shard_map/ppermute | solution.py:292
  49.0 0.5 collective-permute-start.15
  49.6 1.6 %collective-permute-start.14 = (bf16[1024,256]{1,0:T(8,128)(2,1)S(1)}, bf16[1024,256]{1,0:T(8,128)(2,1)S(1)}, u32[]{:S(2)}, u32[]{:S(2)}) collective-permute-start(bf16[1024,256]{1,0:T(8,128)(2,1)S(1)} %add_convert_fusion), channel_id=1, source_target_pairs={{0,16},{8,24},{16,0},{24,8},{1,17},{9,25},{17,1},{25,9},{2,18},{10... | collective-permute-start | bytes 1572872 | tf_op jit(solution)/shard_map/ppermute | solution.py:333
  51.2 3.5 %collective-permute-done.19 = bf16[128,1024]{1,0:T(8,128)(2,1)S(1)} collective-permute-done((bf16[128,1024]{1,0:T(8,128)(2,1)S(1)}, bf16[128,1024]{1,0:T(8,128)(2,1)S(1)}, u32[]{:S(2)}, u32[]{:S(2)}) %collective-permute-start.19) | collective-permute-done | bytes 262176 | tf_op jit(solution)/shard_map/ppermute | solution.py:292
  54.8 1.6 %collective-permute-start.20 = (bf16[128,1024]{1,0:T(8,128)(2,1)S(1)}, bf16[128,1024]{1,0:T(8,128)(2,1)S(1)}, u32[]{:S(2)}, u32[]{:S(2)}) collective-permute-start(bf16[128,1024]{1,0:T(8,128)(2,1)S(1)} %add_convert_fusion.1), channel_id=1, source_target_pairs={{0,2},{2,4},{4,6},{6,7},{7,5},{5,3},{3,1},{1,0},{8,10},{10,12},{12... | collective-permute-start | bytes 786440 | tf_op jit(solution)/shard_map/ppermute | solution.py:292
  56.5 0.5 collective-permute-start.16
  57.0 7.0 %collective-permute-done.14.refs_2_ = bf16[1024,256]{1,0:T(8,128)(2,1)S(1)} collective-permute-done((bf16[1024,256]{1,0:T(8,128)(2,1)S(1)}, bf16[1024,256]{1,0:T(8,128)(2,1)S(1)}, u32[]{:S(2)}, u32[]{:S(2)}) %collective-permute-start.14) | collective-permute-done | bytes 524320 | tf_op jit(solution)/shard_map/ppermute | solution.py:333
  64.2 0.9 %finish.1 = (bf16[128,1024]{1,0:T(8,128)(2,1)}, bf16[1024,256]{1,0:T(8,128)(2,1)}) custom-call(bf16[1024,256]{1,0:T(8,128)(2,1)S(1)} %weight_sum.1.weight_ref, bf16[128,1024]{1,0:T(8,128)(2,1)S(1)} %get-tuple-element.55.refs_0_, bf16[128,1024]{1,0:T(8,128)(2,1)S(1)} %collective-permute-done.16.refs_1_, bf16[128,1024]{1,0:T(8,128)(2,1)S(1)} %collective-permute-done.20.refs_2_), custom_call_target="tpu_custom_call" | custom-call | flops 393216 | bytes 2097152 | tf_op jit(solution)/shard_map/finish/pallas_call | solution.py:253
  (51 shorter events, 3.7 us)
Async XLA Ops:
  0.6 9.7 %collective-permute-start = (bf16[128,1024]{1,0:T(8,128)(2,1)}, bf16[128,1024]{1,0:T(8,128)(2,1)S(1)}, u32[]{:S(2)}, u32[]{:S(2)}) collective-permute-start(bf16[128,1024]{1,0:T(8,128)(2,1)} %param.5), channel_id=1, source_target_pairs={{0,2},{2,4},{4,6},{6,7},{7,5},{5,3},{3,1},{1,0},{8,10},{10,12},{12... | collective-permute-start | bytes 786440 | tf_op jit(solution)/shard_map/ppermute | solution.py:292
  3.7 8.2 %collective-permute-start.2 = (bf16[128,1024]{1,0:T(8,128)(2,1)}, bf16[128,1024]{1,0:T(8,128)(2,1)S(1)}, u32[]{:S(2)}, u32[]{:S(2)}) collective-permute-start(bf16[128,1024]{1,0:T(8,128)(2,1)} %param.5), channel_id=1, source_target_pairs={{2,0},{4,2},{6,4},{7,6},{5,7},{3,5},{1,3},{0,1},{10,8},{12,10},{14... | collective-permute-start | bytes 786440 | tf_op jit(solution)/shard_map/ppermute | solution.py:295
  3.7 0.7 %copy-start.2 = (s32[128,16]{0,1:T(8,128)S(1)}, s32[128,16]{0,1:T(8,128)}, u32[]{:S(2)}) copy-start(s32[128,16]{0,1:T(8,128)} %param.6) | copy-start | bytes 24580
  4.4 0.7 %copy-start.3 = (s32[128,4]{0,1:T(4,128)S(1)}, s32[128,4]{0,1:T(4,128)}, u32[]{:S(2)}) copy-start(s32[128,4]{0,1:T(4,128)} %param.7) | copy-start | bytes 6148
  5.1 6.7 %collective-permute-start.1 = (bf16[8,1024]{1,0:T(8,128)(2,1)S(1)}, bf16[8,1024]{1,0:T(8,128)(2,1)S(1)}, u32[]{:S(2)}, u32[]{:S(2)}) collective-permute-start(bf16[8,1024]{1,0:T(8,128)(2,1)S(1)} %instance_ids.1), channel_id=1, source_target_pairs={{0,2},{2,4},{4,6},{6,7},{7,5},{5,3},{3,1},{1,0},{8,10},{10,12},{12... | collective-permute-start | bytes 49160 | tf_op jit(solution)/shard_map/ppermute | solution.py:292
  7.2 6.3 %collective-permute-start.3 = (bf16[8,1024]{1,0:T(8,128)(2,1)S(1)}, bf16[8,1024]{1,0:T(8,128)(2,1)S(1)}, u32[]{:S(2)}, u32[]{:S(2)}) collective-permute-start(bf16[8,1024]{1,0:T(8,128)(2,1)S(1)} %instance_ids.1), channel_id=1, source_target_pairs={{2,0},{4,2},{6,4},{7,6},{5,7},{3,5},{1,3},{0,1},{10,8},{12,10},{14... | collective-permute-start | bytes 49160 | tf_op jit(solution)/shard_map/ppermute | solution.py:295
  7.2 1.6 %copy-start = (bf16[1024,1024]{1,0:T(8,128)(2,1)S(1)}, bf16[1024,1024]{1,0:T(8,128)(2,1)}, u32[]{:S(2)}) copy-start(bf16[1024,1024]{1,0:T(8,128)(2,1)} %refs_2_.5) | copy-start | bytes 6291460
  8.8 0.7 %copy-start.4 = (s32[8]{0:T(128)S(1)}, s32[8]{0:T(128)}, u32[]{:S(2)}) copy-start(s32[8]{0:T(128)} %size_ref.1) | copy-start | bytes 100
  9.4 4.6 %copy-start.1 = (bf16[1024,1024]{1,0:T(8,128)(2,1)S(1)}, bf16[1024,1024]{1,0:T(8,128)(2,1)}, u32[]{:S(2)}) copy-start(bf16[1024,1024]{1,0:T(8,128)(2,1)} %refs_2_.5) | copy-start | bytes 6291460
  11.9 7.0 %collective-permute-start.4 = (bf16[136,1024]{1,0:T(8,128)(2,1)S(1)}, bf16[136,1024]{1,0:T(8,128)(2,1)S(1)}, u32[]{:S(2)}, u32[]{:S(2)}) collective-permute-start(bf16[136,1024]{1,0:T(8,128)(2,1)S(1)} %constant_dynamic-update-slice_fusion.refs_0_), channel_id=1, source_target_pairs={{0,2},{2,4},{4,6},{6,7},{7,5},{5,3},{3,1},{1,0},{8,10},{10,12},{12... | collective-permute-start | bytes 835592 | tf_op jit(solution)/shard_map/ppermute | solution.py:292
  13.5 7.0 %copy-start.5 = (bf16[128,1024]{1,0:T(8,128)(2,1)S(1)}, bf16[128,1024]{1,0:T(8,128)(2,1)}, u32[]{:S(2)}) copy-start(bf16[128,1024]{1,0:T(8,128)(2,1)} %param.5) | copy-start | bytes 786436
  13.5 7.0 %collective-permute-start.5 = (bf16[136,1024]{1,0:T(8,128)(2,1)S(1)}, bf16[136,1024]{1,0:T(8,128)(2,1)S(1)}, u32[]{:S(2)}, u32[]{:S(2)}) collective-permute-start(bf16[136,1024]{1,0:T(8,128)(2,1)S(1)} %constant_dynamic-update-slice_fusion.2.refs_1_), channel_id=1, source_target_pairs={{2,0},{4,2},{6,4},{7,6},{5,7},{3,5},{1,3},{0,1},{10,8},{12,10},{14... | collective-permute-start | bytes 835592 | tf_op jit(solution)/shard_map/ppermute | solution.py:295
  18.9 7.4 %collective-permute-start.6 = (bf16[136,1024]{1,0:T(8,128)(2,1)S(1)}, bf16[136,1024]{1,0:T(8,128)(2,1)S(1)}, u32[]{:S(2)}, u32[]{:S(2)}) collective-permute-start(bf16[136,1024]{1,0:T(8,128)(2,1)S(1)} %collective-permute-done.4.refs_0_.refs_2_), channel_id=1, source_target_pairs={{0,2},{2,4},{4,6},{6,7},{7,5},{5,3},{3,1},{1,0},{8,10},{10,12},{12... | collective-permute-start | bytes 835592 | tf_op jit(solution)/shard_map/ppermute | solution.py:292
  20.5 7.5 %collective-permute-start.7 = (bf16[136,1024]{1,0:T(8,128)(2,1)S(1)}, bf16[136,1024]{1,0:T(8,128)(2,1)S(1)}, u32[]{:S(2)}, u32[]{:S(2)}) collective-permute-start(bf16[136,1024]{1,0:T(8,128)(2,1)S(1)} %collective-permute-done.5.refs_1_.refs_3_), channel_id=1, source_target_pairs={{2,0},{4,2},{6,4},{7,6},{5,7},{3,5},{1,3},{0,1},{10,8},{12,10},{14... | collective-permute-start | bytes 835592 | tf_op jit(solution)/shard_map/ppermute | solution.py:295
  26.3 5.5 %collective-permute-start.8 = (bf16[88,1024]{1,0:T(8,128)(2,1)S(1)}, bf16[88,1024]{1,0:T(8,128)(2,1)S(1)}, u32[]{:S(2)}, u32[]{:S(2)}) collective-permute-start(bf16[88,1024]{1,0:T(8,128)(2,1)S(1)} %pad_maximum_fusion.3), channel_id=1, source_target_pairs={{0,2},{2,4},{4,6},{6,7},{7,5},{5,3},{3,1},{1,0},{8,10},{10,12},{12... | collective-permute-start | bytes 540680 | tf_op jit(solution)/shard_map/ppermute | solution.py:292
  28.0 4.7 %collective-permute-start.9 = (bf16[48,1024]{1,0:T(8,128)(2,1)S(1)}, bf16[48,1024]{1,0:T(8,128)(2,1)S(1)}, u32[]{:S(2)}, u32[]{:S(2)}) collective-permute-start(bf16[48,1024]{1,0:T(8,128)(2,1)S(1)} %slice.23), channel_id=1, source_target_pairs={{2,0},{4,2},{6,4},{7,6},{5,7},{3,5},{1,3},{0,1},{10,8},{12,10},{14... | collective-permute-start | bytes 294920 | tf_op jit(solution)/shard_map/ppermute | solution.py:295
  33.9 5.0 %collective-permute-start.17 = (bf16[64,1024]{1,0:T(8,128)(2,1)S(1)}, bf16[64,1024]{1,0:T(8,128)(2,1)S(1)}, u32[]{:S(2)}, u32[]{:S(2)}) collective-permute-start(bf16[64,1024]{1,0:T(8,128)(2,1)S(1)} %get-tuple-element.59), channel_id=1, source_target_pairs={{0,2},{2,4},{4,6},{6,7},{7,5},{5,3},{3,1},{1,0},{8,10},{10,12},{12... | collective-permute-start | bytes 393224 | tf_op jit(solution)/shard_map/ppermute | solution.py:292
  35.5 5.1 %collective-permute-start.10 = (bf16[64,1024]{1,0:T(8,128)(2,1)S(1)}, bf16[64,1024]{1,0:T(8,128)(2,1)S(1)}, u32[]{:S(2)}, u32[]{:S(2)}) collective-permute-start(bf16[64,1024]{1,0:T(8,128)(2,1)S(1)} %get-tuple-element.51), channel_id=1, source_target_pairs={{2,0},{4,2},{6,4},{7,6},{5,7},{3,5},{1,3},{0,1},{10,8},{12,10},{14... | collective-permute-start | bytes 393224 | tf_op jit(solution)/shard_map/ppermute | solution.py:295
  38.3 11.2 %collective-permute-start.13 = (bf16[1024,256]{1,0:T(8,128)(2,1)S(1)}, bf16[1024,256]{1,0:T(8,128)(2,1)S(1)}, u32[]{:S(2)}, u32[]{:S(2)}) collective-permute-start(bf16[1024,256]{1,0:T(8,128)(2,1)S(1)} %get-tuple-element.54), channel_id=1, source_target_pairs={{0,8},{8,0},{16,24},{24,16},{1,9},{9,1},{17,25},{25,17},{2,10},{10... | collective-permute-start | bytes 1572872 | tf_op jit(solution)/shard_map/ppermute | solution.py:333
  38.9 8.3 %collective-permute-start.18 = (bf16[128,1024]{1,0:T(8,128)(2,1)S(1)}, bf16[128,1024]{1,0:T(8,128)(2,1)S(1)}, u32[]{:S(2)}, u32[]{:S(2)}) collective-permute-start(bf16[128,1024]{1,0:T(8,128)(2,1)S(1)} %pad_maximum_fusion.2), channel_id=1, source_target_pairs={{0,2},{2,4},{4,6},{6,7},{7,5},{5,3},{3,1},{1,0},{8,10},{10,12},{12... | collective-permute-start | bytes 786440 | tf_op jit(solution)/shard_map/ppermute | solution.py:292
  40.6 8.3 %collective-permute-start.11 = (bf16[128,1024]{1,0:T(8,128)(2,1)S(1)}, bf16[128,1024]{1,0:T(8,128)(2,1)S(1)}, u32[]{:S(2)}, u32[]{:S(2)}) collective-permute-start(bf16[128,1024]{1,0:T(8,128)(2,1)S(1)} %pad_maximum_fusion.1), channel_id=1, source_target_pairs={{2,0},{4,2},{6,4},{7,6},{5,7},{3,5},{1,3},{0,1},{10,8},{12,10},{14... | collective-permute-start | bytes 786440 | tf_op jit(solution)/shard_map/ppermute | solution.py:295
  47.3 7.4 %collective-permute-start.19 = (bf16[128,1024]{1,0:T(8,128)(2,1)S(1)}, bf16[128,1024]{1,0:T(8,128)(2,1)S(1)}, u32[]{:S(2)}, u32[]{:S(2)}) collective-permute-start(bf16[128,1024]{1,0:T(8,128)(2,1)S(1)} %add_convert_fusion.2), channel_id=1, source_target_pairs={{0,2},{2,4},{4,6},{6,7},{7,5},{5,3},{3,1},{1,0},{8,10},{10,12},{12... | collective-permute-start | bytes 786440 | tf_op jit(solution)/shard_map/ppermute | solution.py:292
  49.0 7.4 %collective-permute-start.15 = (bf16[128,1024]{1,0:T(8,128)(2,1)S(1)}, bf16[128,1024]{1,0:T(8,128)(2,1)S(1)}, u32[]{:S(2)}, u32[]{:S(2)}) collective-permute-start(bf16[128,1024]{1,0:T(8,128)(2,1)S(1)} %add_convert_fusion.4), channel_id=1, source_target_pairs={{2,0},{4,2},{6,4},{7,6},{5,7},{3,5},{1,3},{0,1},{10,8},{12,10},{14... | collective-permute-start | bytes 786440 | tf_op jit(solution)/shard_map/ppermute | solution.py:295
  49.5 7.5 %collective-permute-start.12 = (bf16[1024,256]{1,0:T(8,128)(2,1)S(1)}, bf16[1024,256]{1,0:T(8,128)(2,1)S(1)}, u32[]{:S(2)}, u32[]{:S(2)}) collective-permute-start(bf16[1024,256]{1,0:T(8,128)(2,1)S(1)} %get-tuple-element.52), channel_id=1, source_target_pairs={{0,8},{8,0},{16,24},{24,16},{1,9},{9,1},{17,25},{25,17},{2,10},{10... | collective-permute-start | bytes 1572872 | tf_op jit(solution)/shard_map/ppermute | solution.py:333
  49.6 14.4 %collective-permute-start.14 = (bf16[1024,256]{1,0:T(8,128)(2,1)S(1)}, bf16[1024,256]{1,0:T(8,128)(2,1)S(1)}, u32[]{:S(2)}, u32[]{:S(2)}) collective-permute-start(bf16[1024,256]{1,0:T(8,128)(2,1)S(1)} %add_convert_fusion), channel_id=1, source_target_pairs={{0,16},{8,24},{16,0},{24,8},{1,17},{9,25},{17,1},{25,9},{2,18},{10... | collective-permute-start | bytes 1572872 | tf_op jit(solution)/shard_map/ppermute | solution.py:333
  54.8 9.5 %collective-permute-start.20 = (bf16[128,1024]{1,0:T(8,128)(2,1)S(1)}, bf16[128,1024]{1,0:T(8,128)(2,1)S(1)}, u32[]{:S(2)}, u32[]{:S(2)}) collective-permute-start(bf16[128,1024]{1,0:T(8,128)(2,1)S(1)} %add_convert_fusion.1), channel_id=1, source_target_pairs={{0,2},{2,4},{4,6},{6,7},{7,5},{5,3},{3,1},{1,0},{8,10},{10,12},{12... | collective-permute-start | bytes 786440 | tf_op jit(solution)/shard_map/ppermute | solution.py:292
  56.5 7.8 %collective-permute-start.16 = (bf16[128,1024]{1,0:T(8,128)(2,1)S(1)}, bf16[128,1024]{1,0:T(8,128)(2,1)S(1)}, u32[]{:S(2)}, u32[]{:S(2)}) collective-permute-start(bf16[128,1024]{1,0:T(8,128)(2,1)S(1)} %add_convert_fusion.3), channel_id=1, source_target_pairs={{2,0},{4,2},{6,4},{7,6},{5,7},{3,5},{1,3},{0,1},{10,8},{12,10},{14... | collective-permute-start | bytes 786440 | tf_op jit(solution)/shard_map/ppermute | solution.py:295

commit v19 on v16

--- a/solution.py
+++ b/solution.py
@@ -332,9 +332,11 @@
     def seq_send(array, bit):
         return lax.ppermute(array, "seq", [(k, k ^ bit) for k in range(seq_count)])
 
-    slots = list(range(seq_count))[::-1]
-    parts = weight_work(used, slopes, slots, part_width, scale)
-    terms = {q: [part] for q, part in zip(slots, parts)}
+    far, near = list(range(seq_count // 2, seq_count))[::-1], list(range(seq_count // 2))[::-1]
+    terms = {}
+    for slots in (far, near):
+        parts = weight_work(used, slopes, slots, part_width, scale)
+        terms.update({q: [part] for q, part in zip(slots, parts)})
     bit = 1
     while bit < seq_count:
         for q in [q for q in sorted(terms, reverse=True) if q & bit]:

time: 64 us -> 62.3 us (0.973)
  waiting for transfers between devices: 26.1 us -> 24.1 us
    ppermute x9, waiting for transfers between devices: 18.1 us -> 16.1 us  [send_up(): return lax.ppermute(array, 'clus', up)]
    pallas_call x1 -> x2, Pallas kernels: 2.37 us -> 2.58 us  [weight_work(): pl.pallas_call(functools.partial(weight_kernel, piece_rows, column_blocks...]
  transfers between devices with their start and end apart: 21 -> 21, of which waited for: 11 -> 11; matrix products, arithmetic and copies ran while one was open for 1% -> 1% of each run, Pallas kernels for 14% -> 15%
where the time goes in v19:
time: 62.3 us; the launch traced here: 62.1 us
  waiting for transfers between devices  24.1 us (39%)
  starting transfers between devices  21.7 us (35%)
  Pallas kernels  11.2 us (18%)
  local copies, waits for them, and re-layouts  3.72 us (6%)
  between operations  0.85 us (1%)
    ppermute x9, starting transfers between devices, send_up(): return lax.ppermute(array, 'clus', up)  16.4 us
    ppermute x9, waiting for transfers between devices, send_up(): return lax.ppermute(array, 'clus', up)  16.1 us
    pallas_call x4, Pallas kernels, block_work(): pl.pallas_call(functools.partial(block_kernel, piece_rows, top_count, pos...  6.97 us
    ppermute x3, waiting for transfers between devices, seq_send(): return lax.ppermute(array, 'seq', [(k, k ^ bit) for k in range(seq_count)])  4.8 us
    unnamed x14, local copies, waits for them, and re-layouts  3.67 us
    ppermute x9, starting transfers between devices, send_down(): return lax.ppermute(array, 'clus', down)  3.55 us
    ppermute x9, waiting for transfers between devices, send_down(): return lax.ppermute(array, 'clus', down)  3.2 us
    pallas_call x2, Pallas kernels, weight_work(): pl.pallas_call(functools.partial(weight_kernel, piece_rows, column_blocks...  2.58 us
  transfers between devices with their start and end apart: 21, of which 11 were waited for; matrix products, arithmetic and copies ran while one was open for 1% of the time, Pallas kernels for 15%

profile of v19, /device:TPU:0, one launch (start us, length us, event | category | flops | bytes accessed | tf_op | source)
XLA Modules:
  0.0 62.1 jit_solution(14960920571237485714)
XLA Ops:
  0.6 3.1 %collective-permute-start = (bf16[128,1024]{1,0:T(8,128)(2,1)}, bf16[128,1024]{1,0:T(8,128)(2,1)S(1)}, u32[]{:S(2)}, u32[]{:S(2)}) collective-permute-start(bf16[128,1024]{1,0:T(8,128)(2,1)} %param.5), channel_id=1, source_target_pairs={{0,2},{2,4},{4,6},{6,7},{7,5},{5,3},{3,1},{1,0},{8,10},{10,12},{12... | collective-permute-start | bytes 786440 | tf_op jit(solution)/shard_map/ppermute | solution.py:292
  3.7 0.7 %copy-done.2 = s32[128,16]{0,1:T(8,128)S(1)} copy-done((s32[128,16]{0,1:T(8,128)S(1)}, s32[128,16]{0,1:T(8,128)}, u32[]{:S(2)}) %copy-start.2) | copy-done | bytes 8216
  4.4 0.7 %copy-done.3 = s32[128,4]{0,1:T(4,128)S(1)} copy-done((s32[128,4]{0,1:T(4,128)S(1)}, s32[128,4]{0,1:T(4,128)}, u32[]{:S(2)}) %copy-start.3) | copy-done | bytes 2072
  5.1 2.1 %collective-permute-start.1 = (bf16[8,1024]{1,0:T(8,128)(2,1)S(1)}, bf16[8,1024]{1,0:T(8,128)(2,1)S(1)}, u32[]{:S(2)}, u32[]{:S(2)}) collective-permute-start(bf16[8,1024]{1,0:T(8,128)(2,1)S(1)} %instance_ids.1), channel_id=1, source_target_pairs={{0,2},{2,4},{4,6},{6,7},{7,5},{5,3},{3,1},{1,0},{8,10},{10,12},{12... | collective-permute-start | bytes 49160 | tf_op jit(solution)/shard_map/ppermute | solution.py:292
  7.2 1.6 %copy-done = bf16[1024,1024]{1,0:T(8,128)(2,1)S(1)} copy-done((bf16[1024,1024]{1,0:T(8,128)(2,1)S(1)}, bf16[1024,1024]{1,0:T(8,128)(2,1)}, u32[]{:S(2)}) %copy-start) | copy-done | bytes 2097176
  8.8 0.7 %copy-done.4 = s32[8]{0:T(128)S(1)} copy-done((s32[8]{0:T(128)S(1)}, s32[8]{0:T(128)}, u32[]{:S(2)}) %copy-start.4) | copy-done | bytes 56
  9.5 0.6 live_labels.1.refs_3_.refs_4_
  10.4 1.5 %collective-permute-done.2 = bf16[128,1024]{1,0:T(8,128)(2,1)S(1)} collective-permute-done((bf16[128,1024]{1,0:T(8,128)(2,1)}, bf16[128,1024]{1,0:T(8,128)(2,1)S(1)}, u32[]{:S(2)}, u32[]{:S(2)}) %collective-permute-start.2) | collective-permute-done | bytes 262176 | tf_op jit(solution)/shard_map/ppermute | solution.py:295
  11.9 1.6 %collective-permute-start.4 = (bf16[136,1024]{1,0:T(8,128)(2,1)S(1)}, bf16[136,1024]{1,0:T(8,128)(2,1)S(1)}, u32[]{:S(2)}, u32[]{:S(2)}) collective-permute-start(bf16[136,1024]{1,0:T(8,128)(2,1)S(1)} %constant_dynamic-update-slice_fusion.refs_0_), channel_id=1, source_target_pairs={{0,2},{2,4},{4,6},{6,7},{7,5},{5,3},{3,1},{1,0},{8,10},{10,12},{12... | collective-permute-start | bytes 835592 | tf_op jit(solution)/shard_map/ppermute | solution.py:292
  14.0 1.7 %block_work.4 = (bf16[128,1024]{1,0:T(8,128)(2,1)S(1)}, bf16[128,1024]{1,0:T(8,128)(2,1)S(1)}, bf16[128,1024]{1,0:T(8,128)(2,1)S(1)}, bf16[128,1024]{1,0:T(8,128)(2,1)S(1)}) custom-call(bf16[136,1024]{1,0:T(8,128)(2,1)S(1)} %constant_dynamic-update-slice_fusion.refs_0_, bf16[136,1024]{1,0:T(8,128)(2,1)S(1)} %constant_dynamic-update-slice_fusion.2.refs_1_, ...), custom_call_target="tpu_custom_call" | custom-call | flops 1073741824 | bytes 3670016 | tf_op jit(solution)/shard_map/block_work/pallas_call | solution.py:147
  15.7 3.2 %collective-permute-done.4.refs_0_.refs_2_ = bf16[136,1024]{1,0:T(8,128)(2,1)S(1)} collective-permute-done((bf16[136,1024]{1,0:T(8,128)(2,1)S(1)}, bf16[136,1024]{1,0:T(8,128)(2,1)S(1)}, u32[]{:S(2)}, u32[]{:S(2)}) %collective-permute-start.4) | collective-permute-done | bytes 278560 | tf_op jit(solution)/shard_map/ppermute | solution.py:292
  18.9 1.6 %collective-permute-start.6 = (bf16[136,1024]{1,0:T(8,128)(2,1)S(1)}, bf16[136,1024]{1,0:T(8,128)(2,1)S(1)}, u32[]{:S(2)}, u32[]{:S(2)}) collective-permute-start(bf16[136,1024]{1,0:T(8,128)(2,1)S(1)} %collective-permute-done.4.refs_0_.refs_2_), channel_id=1, source_target_pairs={{0,2},{2,4},{4,6},{6,7},{7,5},{5,3},{3,1},{1,0},{8,10},{10,12},{12... | collective-permute-start | bytes 835592 | tf_op jit(solution)/shard_map/ppermute | solution.py:292
  21.0 2.4 %block_work.5 = (bf16[128,1024]{1,0:T(8,128)(2,1)S(1)}, bf16[128,1024]{1,0:T(8,128)(2,1)S(1)}, bf16[128,1024]{1,0:T(8,128)(2,1)S(1)}, bf16[128,1024]{1,0:T(8,128...) custom-call(bf16[136,1024]{1,0:T(8,128)(2,1)S(1)} %collective-permute-done.4.refs_0_.refs_2_, ...), custom_call_target="tpu_custom_call" | custom-call | flops 1610612736 | bytes 4456448 | tf_op jit(solution)/shard_map/block_work/pallas_call | solution.py:147
  23.4 2.9 %collective-permute-done.6.refs_0_.refs_5_ = bf16[136,1024]{1,0:T(8,128)(2,1)S(1)} collective-permute-done((bf16[136,1024]{1,0:T(8,128)(2,1)S(1)}, bf16[136,1024]{1,0:T(8,128)(2,1)S(1)}, u32[]{:S(2)}, u32[]{:S(2)}) %collective-permute-start.6) | collective-permute-done | bytes 278560 | tf_op jit(solution)/shard_map/ppermute | solution.py:292
  26.3 1.6 %collective-permute-start.8 = (bf16[88,1024]{1,0:T(8,128)(2,1)S(1)}, bf16[88,1024]{1,0:T(8,128)(2,1)S(1)}, u32[]{:S(2)}, u32[]{:S(2)}) collective-permute-start(bf16[88,1024]{1,0:T(8,128)(2,1)S(1)} %pad_maximum_fusion.3), channel_id=1, source_target_pairs={{0,2},{2,4},{4,6},{6,7},{7,5},{5,3},{3,1},{1,0},{8,10},{10,12},{12... | collective-permute-start | bytes 540680 | tf_op jit(solution)/shard_map/ppermute | solution.py:292
  28.5 1.7 %block_work.6 = (bf16[128,1024]{1,0:T(8,128)(2,1)S(1)}, bf16[128,1024]{1,0:T(8,128)(2,1)S(1)}, bf16[128,1024]{1,0:T(8,128)(2,1)S(1)}, bf16[128,1024]{1,0:T(8,128)(2,1)S(1)}) custom-call(bf16[136,1024]{1,0:T(8,128)(2,1)S(1)} %collective-permute-done.6.refs_0_.refs_5_, bf16[136,1024]{1,0:T(8,128)(2,1)S(1)} %collective-permute-done.7.refs_1_.refs_6_, ...), custom_call_target="tpu_custom_call" | custom-call | flops 1073741824 | bytes 3670016 | tf_op jit(solution)/shard_map/block_work/pallas_call | solution.py:147
  30.2 1.7 %collective-permute-done.8.refs_0_.refs_7_ = bf16[88,1024]{1,0:T(8,128)(2,1)S(1)} collective-permute-done((bf16[88,1024]{1,0:T(8,128)(2,1)S(1)}, bf16[88,1024]{1,0:T(8,128)(2,1)S(1)}, u32[]{:S(2)}, u32[]{:S(2)}) %collective-permute-start.8) | collective-permute-done | bytes 180256 | tf_op jit(solution)/shard_map/ppermute | solution.py:292
  31.9 0.8 %collective-permute-done.9.refs_1_.refs_8_ = bf16[48,1024]{1,0:T(8,128)(2,1)S(1)} collective-permute-done((bf16[48,1024]{1,0:T(8,128)(2,1)S(1)}, bf16[48,1024]{1,0:T(8,128)(2,1)S(1)}, u32[]{:S(2)}, u32[]{:S(2)}) %collective-permute-start.9) | collective-permute-done | bytes 98336 | tf_op jit(solution)/shard_map/ppermute | solution.py:295
  32.7 1.2 %block_work.7 = (bf16[64,1024]{1,0:T(8,128)(2,1)S(1)}, bf16[64,1024]{1,0:T(8,128)(2,1)S(1)}, bf16[128,1024]{1,0:T(8,128)(2,1)S(1)}) custom-call(bf16[88,1024]{1,0:T(8,128)(2,1)S(1)} %collective-permute-done.8.refs_0_.refs_7_, bf16[48,1024]{1,0:T(8,128)(2,1)S(1)} %collective-permute-done.9.refs_1_.refs_8_, bf16[1024,1024]{1,0:T(8,128)(2,1)S(1)} %copy-done.1, ...), custom_call_target="tpu_custom_call" | custom-call | flops 536870912 | bytes 2883584 | tf_op jit(solution)/shard_map/block_work/pallas_call | solution.py:147
  33.9 1.6 %collective-permute-start.17 = (bf16[64,1024]{1,0:T(8,128)(2,1)S(1)}, bf16[64,1024]{1,0:T(8,128)(2,1)S(1)}, u32[]{:S(2)}, u32[]{:S(2)}) collective-permute-start(bf16[64,1024]{1,0:T(8,128)(2,1)S(1)} %get-tuple-element.57), channel_id=1, source_target_pairs={{0,2},{2,4},{4,6},{6,7},{7,5},{5,3},{3,1},{1,0},{8,10},{10,12},{12... | collective-permute-start | bytes 393224 | tf_op jit(solution)/shard_map/ppermute | solution.py:292
  36.0 1.3 %weight_work.3 = (bf16[1024,256]{1,0:T(8,128)(2,1)S(1)}, bf16[1024,256]{1,0:T(8,128)(2,1)S(1)}) custom-call(bf16[136,1024]{1,0:T(8,128)(2,1)S(1)} %constant_dynamic-update-slice_fusion.refs_0_, bf16[136,1024]{1,0:T(8,128)(2,1)S(1)} %constant_dynamic-update-slice_fusion.2.refs_1_, bf16[136,1024]{1,0:T(8,128)(2,1)S(1)} %collective-permute-done.4.refs_0_.refs_2_, ...), custom_call_target="tpu_custom_call" | custom-call | flops 1073741824 | bytes 4718592 | tf_op jit(solution)/shard_map/weight_work/pallas_call | solution.py:189
  37.4 1.5 %collective-permute-done.17 = bf16[64,1024]{1,0:T(8,128)(2,1)S(1)} collective-permute-done((bf16[64,1024]{1,0:T(8,128)(2,1)S(1)}, bf16[64,1024]{1,0:T(8,128)(2,1)S(1)}, u32[]{:S(2)}, u32[]{:S(2)}) %collective-permute-start.17) | collective-permute-done | bytes 131104 | tf_op jit(solution)/shard_map/ppermute | solution.py:292
  38.9 1.6 %collective-permute-start.18 = (bf16[128,1024]{1,0:T(8,128)(2,1)S(1)}, bf16[128,1024]{1,0:T(8,128)(2,1)S(1)}, u32[]{:S(2)}, u32[]{:S(2)}) collective-permute-start(bf16[128,1024]{1,0:T(8,128)(2,1)S(1)} %pad_maximum_fusion.2), channel_id=1, source_target_pairs={{0,2},{2,4},{4,6},{6,7},{7,5},{5,3},{3,1},{1,0},{8,10},{10,12},{12... | collective-permute-start | bytes 786440 | tf_op jit(solution)/shard_map/ppermute | solution.py:292
  41.1 1.3 %weight_work.2 = (bf16[1024,256]{1,0:T(8,128)(2,1)S(1)}, bf16[1024,256]{1,0:T(8,128)(2,1)S(1)}) custom-call(bf16[136,1024]{1,0:T(8,128)(2,1)S(1)} %constant_dynamic-update-slice_fusion.refs_0_, bf16[136,1024]{1,0:T(8,128)(2,1)S(1)} %constant_dynamic-update-slice_fusion.2.refs_1_, bf16[136,1024]{1,0:T(8,128)(2,1)S(1)} %collective-permute-done.4.refs_0_.refs_2_, ...), custom_call_target="tpu_custom_call" | custom-call | flops 1073741824 | bytes 4718592 | tf_op jit(solution)/shard_map/weight_work/pallas_call | solution.py:189
  42.5 3.7 %collective-permute-done.18 = bf16[128,1024]{1,0:T(8,128)(2,1)S(1)} collective-permute-done((bf16[128,1024]{1,0:T(8,128)(2,1)S(1)}, bf16[128,1024]{1,0:T(8,128)(2,1)S(1)}, u32[]{:S(2)}, u32[]{:S(2)}) %collective-permute-start.18) | collective-permute-done | bytes 262176 | tf_op jit(solution)/shard_map/ppermute | solution.py:292
  46.3 1.6 %collective-permute-start.19 = (bf16[128,1024]{1,0:T(8,128)(2,1)S(1)}, bf16[128,1024]{1,0:T(8,128)(2,1)S(1)}, u32[]{:S(2)}, u32[]{:S(2)}) collective-permute-start(bf16[128,1024]{1,0:T(8,128)(2,1)S(1)} %add_convert_fusion.2), channel_id=1, source_target_pairs={{0,2},{2,4},{4,6},{6,7},{7,5},{5,3},{3,1},{1,0},{8,10},{10,12},{12... | collective-permute-start | bytes 786440 | tf_op jit(solution)/shard_map/ppermute | solution.py:292
  48.6 1.6 %collective-permute-start.12 = (bf16[1024,256]{1,0:T(8,128)(2,1)S(1)}, bf16[1024,256]{1,0:T(8,128)(2,1)S(1)}, u32[]{:S(2)}, u32[]{:S(2)}) collective-permute-start(bf16[1024,256]{1,0:T(8,128)(2,1)S(1)} %add_convert_fusion), channel_id=1, source_target_pairs={{0,16},{8,24},{16,0},{24,8},{1,17},{9,25},{17,1},{25,9},{2,18},{10... | collective-permute-start | bytes 1572872 | tf_op jit(solution)/shard_map/ppermute | solution.py:333
  50.2 2.8 %collective-permute-done.19 = bf16[128,1024]{1,0:T(8,128)(2,1)S(1)} collective-permute-done((bf16[128,1024]{1,0:T(8,128)(2,1)S(1)}, bf16[128,1024]{1,0:T(8,128)(2,1)S(1)}, u32[]{:S(2)}, u32[]{:S(2)}) %collective-permute-start.19) | collective-permute-done | bytes 262176 | tf_op jit(solution)/shard_map/ppermute | solution.py:292
  53.1 1.6 %collective-permute-start.20 = (bf16[128,1024]{1,0:T(8,128)(2,1)S(1)}, bf16[128,1024]{1,0:T(8,128)(2,1)S(1)}, u32[]{:S(2)}, u32[]{:S(2)}) collective-permute-start(bf16[128,1024]{1,0:T(8,128)(2,1)S(1)} %add_convert_fusion.1), channel_id=1, source_target_pairs={{0,2},{2,4},{4,6},{6,7},{7,5},{5,3},{3,1},{1,0},{8,10},{10,12},{12... | collective-permute-start | bytes 786440 | tf_op jit(solution)/shard_map/ppermute | solution.py:292
  55.3 4.8 %collective-permute-done.12.refs_2_ = bf16[1024,256]{1,0:T(8,128)(2,1)S(1)} collective-permute-done((bf16[1024,256]{1,0:T(8,128)(2,1)S(1)}, bf16[1024,256]{1,0:T(8,128)(2,1)S(1)}, u32[]{:S(2)}, u32[]{:S(2)}) %collective-permute-start.12) | collective-permute-done | bytes 524320 | tf_op jit(solution)/shard_map/ppermute | solution.py:333
  60.3 0.9 %collective-permute-done.16.refs_1_ = bf16[128,1024]{1,0:T(8,128)(2,1)S(1)} collective-permute-done((bf16[128,1024]{1,0:T(8,128)(2,1)S(1)}, bf16[128,1024]{1,0:T(8,128)(2,1)S(1)}, u32[]{:S(2)}, u32[]{:S(2)}) %collective-permute-start.16) | collective-permute-done | bytes 262176 | tf_op jit(solution)/shard_map/ppermute | solution.py:295
  61.2 0.9 %finish.1 = (bf16[128,1024]{1,0:T(8,128)(2,1)}, bf16[1024,256]{1,0:T(8,128)(2,1)}) custom-call(bf16[1024,256]{1,0:T(8,128)(2,1)S(1)} %weight_sum.1.weight_ref, bf16[128,1024]{1,0:T(8,128)(2,1)S(1)} %get-tuple-element.52.refs_0_, bf16[128,1024]{1,0:T(8,128)(2,1)S(1)} %collective-permute-done.16.refs_1_, bf16[128,1024]{1,0:T(8,128)(2,1)S(1)} %collective-permute-done.20.refs_2_), custom_call_target="tpu_custom_call" | custom-call | flops 393216 | bytes 2097152 | tf_op jit(solution)/shard_map/finish/pallas_call | solution.py:253
  (52 shorter events, 4.9 us)
Async XLA Ops:
  0.6 9.7 %collective-permute-start = (bf16[128,1024]{1,0:T(8,128)(2,1)}, bf16[128,1024]{1,0:T(8,128)(2,1)S(1)}, u32[]{:S(2)}, u32[]{:S(2)}) collective-permute-start(bf16[128,1024]{1,0:T(8,128)(2,1)} %param.5), channel_id=1, source_target_pairs={{0,2},{2,4},{4,6},{6,7},{7,5},{5,3},{3,1},{1,0},{8,10},{10,12},{12... | collective-permute-start | bytes 786440 | tf_op jit(solution)/shard_map/ppermute | solution.py:292
  3.7 8.2 %collective-permute-start.2 = (bf16[128,1024]{1,0:T(8,128)(2,1)}, bf16[128,1024]{1,0:T(8,128)(2,1)S(1)}, u32[]{:S(2)}, u32[]{:S(2)}) collective-permute-start(bf16[128,1024]{1,0:T(8,128)(2,1)} %param.5), channel_id=1, source_target_pairs={{2,0},{4,2},{6,4},{7,6},{5,7},{3,5},{1,3},{0,1},{10,8},{12,10},{14... | collective-permute-start | bytes 786440 | tf_op jit(solution)/shard_map/ppermute | solution.py:295
  3.7 0.7 %copy-start.2 = (s32[128,16]{0,1:T(8,128)S(1)}, s32[128,16]{0,1:T(8,128)}, u32[]{:S(2)}) copy-start(s32[128,16]{0,1:T(8,128)} %param.6) | copy-start | bytes 24580
  4.4 0.7 %copy-start.3 = (s32[128,4]{0,1:T(4,128)S(1)}, s32[128,4]{0,1:T(4,128)}, u32[]{:S(2)}) copy-start(s32[128,4]{0,1:T(4,128)} %param.7) | copy-start | bytes 6148
  5.1 6.7 %collective-permute-start.1 = (bf16[8,1024]{1,0:T(8,128)(2,1)S(1)}, bf16[8,1024]{1,0:T(8,128)(2,1)S(1)}, u32[]{:S(2)}, u32[]{:S(2)}) collective-permute-start(bf16[8,1024]{1,0:T(8,128)(2,1)S(1)} %instance_ids.1), channel_id=1, source_target_pairs={{0,2},{2,4},{4,6},{6,7},{7,5},{5,3},{3,1},{1,0},{8,10},{10,12},{12... | collective-permute-start | bytes 49160 | tf_op jit(solution)/shard_map/ppermute | solution.py:292
  7.2 6.3 %collective-permute-start.3 = (bf16[8,1024]{1,0:T(8,128)(2,1)S(1)}, bf16[8,1024]{1,0:T(8,128)(2,1)S(1)}, u32[]{:S(2)}, u32[]{:S(2)}) collective-permute-start(bf16[8,1024]{1,0:T(8,128)(2,1)S(1)} %instance_ids.1), channel_id=1, source_target_pairs={{2,0},{4,2},{6,4},{7,6},{5,7},{3,5},{1,3},{0,1},{10,8},{12,10},{14... | collective-permute-start | bytes 49160 | tf_op jit(solution)/shard_map/ppermute | solution.py:295
  7.2 1.6 %copy-start = (bf16[1024,1024]{1,0:T(8,128)(2,1)S(1)}, bf16[1024,1024]{1,0:T(8,128)(2,1)}, u32[]{:S(2)}) copy-start(bf16[1024,1024]{1,0:T(8,128)(2,1)} %refs_2_.5) | copy-start | bytes 6291460
  8.8 0.7 %copy-start.4 = (s32[8]{0:T(128)S(1)}, s32[8]{0:T(128)}, u32[]{:S(2)}) copy-start(s32[8]{0:T(128)} %size_ref.1) | copy-start | bytes 100
  9.4 4.6 %copy-start.1 = (bf16[1024,1024]{1,0:T(8,128)(2,1)S(1)}, bf16[1024,1024]{1,0:T(8,128)(2,1)}, u32[]{:S(2)}) copy-start(bf16[1024,1024]{1,0:T(8,128)(2,1)} %refs_2_.5) | copy-start | bytes 6291460
  11.9 7.0 %collective-permute-start.4 = (bf16[136,1024]{1,0:T(8,128)(2,1)S(1)}, bf16[136,1024]{1,0:T(8,128)(2,1)S(1)}, u32[]{:S(2)}, u32[]{:S(2)}) collective-permute-start(bf16[136,1024]{1,0:T(8,128)(2,1)S(1)} %constant_dynamic-update-slice_fusion.refs_0_), channel_id=1, source_target_pairs={{0,2},{2,4},{4,6},{6,7},{7,5},{5,3},{3,1},{1,0},{8,10},{10,12},{12... | collective-permute-start | bytes 835592 | tf_op jit(solution)/shard_map/ppermute | solution.py:292
  13.5 7.0 %copy-start.5 = (bf16[128,1024]{1,0:T(8,128)(2,1)S(1)}, bf16[128,1024]{1,0:T(8,128)(2,1)}, u32[]{:S(2)}) copy-start(bf16[128,1024]{1,0:T(8,128)(2,1)} %param.5) | copy-start | bytes 786436
  13.5 7.0 %collective-permute-start.5 = (bf16[136,1024]{1,0:T(8,128)(2,1)S(1)}, bf16[136,1024]{1,0:T(8,128)(2,1)S(1)}, u32[]{:S(2)}, u32[]{:S(2)}) collective-permute-start(bf16[136,1024]{1,0:T(8,128)(2,1)S(1)} %constant_dynamic-update-slice_fusion.2.refs_1_), channel_id=1, source_target_pairs={{2,0},{4,2},{6,4},{7,6},{5,7},{3,5},{1,3},{0,1},{10,8},{12,10},{14... | collective-permute-start | bytes 835592 | tf_op jit(solution)/shard_map/ppermute | solution.py:295
  18.9 7.4 %collective-permute-start.6 = (bf16[136,1024]{1,0:T(8,128)(2,1)S(1)}, bf16[136,1024]{1,0:T(8,128)(2,1)S(1)}, u32[]{:S(2)}, u32[]{:S(2)}) collective-permute-start(bf16[136,1024]{1,0:T(8,128)(2,1)S(1)} %collective-permute-done.4.refs_0_.refs_2_), channel_id=1, source_target_pairs={{0,2},{2,4},{4,6},{6,7},{7,5},{5,3},{3,1},{1,0},{8,10},{10,12},{12... | collective-permute-start | bytes 835592 | tf_op jit(solution)/shard_map/ppermute | solution.py:292
  20.5 7.5 %collective-permute-start.7 = (bf16[136,1024]{1,0:T(8,128)(2,1)S(1)}, bf16[136,1024]{1,0:T(8,128)(2,1)S(1)}, u32[]{:S(2)}, u32[]{:S(2)}) collective-permute-start(bf16[136,1024]{1,0:T(8,128)(2,1)S(1)} %collective-permute-done.5.refs_1_.refs_3_), channel_id=1, source_target_pairs={{2,0},{4,2},{6,4},{7,6},{5,7},{3,5},{1,3},{0,1},{10,8},{12,10},{14... | collective-permute-start | bytes 835592 | tf_op jit(solution)/shard_map/ppermute | solution.py:295
  26.3 5.5 %collective-permute-start.8 = (bf16[88,1024]{1,0:T(8,128)(2,1)S(1)}, bf16[88,1024]{1,0:T(8,128)(2,1)S(1)}, u32[]{:S(2)}, u32[]{:S(2)}) collective-permute-start(bf16[88,1024]{1,0:T(8,128)(2,1)S(1)} %pad_maximum_fusion.3), channel_id=1, source_target_pairs={{0,2},{2,4},{4,6},{6,7},{7,5},{5,3},{3,1},{1,0},{8,10},{10,12},{12... | collective-permute-start | bytes 540680 | tf_op jit(solution)/shard_map/ppermute | solution.py:292
  28.0 4.7 %collective-permute-start.9 = (bf16[48,1024]{1,0:T(8,128)(2,1)S(1)}, bf16[48,1024]{1,0:T(8,128)(2,1)S(1)}, u32[]{:S(2)}, u32[]{:S(2)}) collective-permute-start(bf16[48,1024]{1,0:T(8,128)(2,1)S(1)} %slice.23), channel_id=1, source_target_pairs={{2,0},{4,2},{6,4},{7,6},{5,7},{3,5},{1,3},{0,1},{10,8},{12,10},{14... | collective-permute-start | bytes 294920 | tf_op jit(solution)/shard_map/ppermute | solution.py:295
  33.9 5.0 %collective-permute-start.17 = (bf16[64,1024]{1,0:T(8,128)(2,1)S(1)}, bf16[64,1024]{1,0:T(8,128)(2,1)S(1)}, u32[]{:S(2)}, u32[]{:S(2)}) collective-permute-start(bf16[64,1024]{1,0:T(8,128)(2,1)S(1)} %get-tuple-element.57), channel_id=1, source_target_pairs={{0,2},{2,4},{4,6},{6,7},{7,5},{5,3},{3,1},{1,0},{8,10},{10,12},{12... | collective-permute-start | bytes 393224 | tf_op jit(solution)/shard_map/ppermute | solution.py:292
  35.5 5.1 %collective-permute-start.13 = (bf16[64,1024]{1,0:T(8,128)(2,1)S(1)}, bf16[64,1024]{1,0:T(8,128)(2,1)S(1)}, u32[]{:S(2)}, u32[]{:S(2)}) collective-permute-start(bf16[64,1024]{1,0:T(8,128)(2,1)S(1)} %get-tuple-element.53), channel_id=1, source_target_pairs={{2,0},{4,2},{6,4},{7,6},{5,7},{3,5},{1,3},{0,1},{10,8},{12,10},{14... | collective-permute-start | bytes 393224 | tf_op jit(solution)/shard_map/ppermute | solution.py:295
  37.3 11.2 %collective-permute-start.11 = (bf16[1024,256]{1,0:T(8,128)(2,1)S(1)}, bf16[1024,256]{1,0:T(8,128)(2,1)S(1)}, u32[]{:S(2)}, u32[]{:S(2)}) collective-permute-start(bf16[1024,256]{1,0:T(8,128)(2,1)S(1)} %get-tuple-element.51), channel_id=1, source_target_pairs={{0,8},{8,0},{16,24},{24,16},{1,9},{9,1},{17,25},{25,17},{2,10},{10... | collective-permute-start | bytes 1572872 | tf_op jit(solution)/shard_map/ppermute | solution.py:333
  38.9 7.3 %collective-permute-start.18 = (bf16[128,1024]{1,0:T(8,128)(2,1)S(1)}, bf16[128,1024]{1,0:T(8,128)(2,1)S(1)}, u32[]{:S(2)}, u32[]{:S(2)}) collective-permute-start(bf16[128,1024]{1,0:T(8,128)(2,1)S(1)} %pad_maximum_fusion.2), channel_id=1, source_target_pairs={{0,2},{2,4},{4,6},{6,7},{7,5},{5,3},{3,1},{1,0},{8,10},{10,12},{12... | collective-permute-start | bytes 786440 | tf_op jit(solution)/shard_map/ppermute | solution.py:292
  40.6 7.3 %collective-permute-start.14 = (bf16[128,1024]{1,0:T(8,128)(2,1)S(1)}, bf16[128,1024]{1,0:T(8,128)(2,1)S(1)}, u32[]{:S(2)}, u32[]{:S(2)}) collective-permute-start(bf16[128,1024]{1,0:T(8,128)(2,1)S(1)} %pad_maximum_fusion.1), channel_id=1, source_target_pairs={{2,0},{4,2},{6,4},{7,6},{5,7},{3,5},{1,3},{0,1},{10,8},{12,10},{14... | collective-permute-start | bytes 786440 | tf_op jit(solution)/shard_map/ppermute | solution.py:295
  42.4 12.8 %collective-permute-start.10 = (bf16[1024,256]{1,0:T(8,128)(2,1)S(1)}, bf16[1024,256]{1,0:T(8,128)(2,1)S(1)}, u32[]{:S(2)}, u32[]{:S(2)}) collective-permute-start(bf16[1024,256]{1,0:T(8,128)(2,1)S(1)} %get-tuple-element.49), channel_id=1, source_target_pairs={{0,8},{8,0},{16,24},{24,16},{1,9},{9,1},{17,25},{25,17},{2,10},{10... | collective-permute-start | bytes 1572872 | tf_op jit(solution)/shard_map/ppermute | solution.py:333
  46.3 6.7 %collective-permute-start.19 = (bf16[128,1024]{1,0:T(8,128)(2,1)S(1)}, bf16[128,1024]{1,0:T(8,128)(2,1)S(1)}, u32[]{:S(2)}, u32[]{:S(2)}) collective-permute-start(bf16[128,1024]{1,0:T(8,128)(2,1)S(1)} %add_convert_fusion.2), channel_id=1, source_target_pairs={{0,2},{2,4},{4,6},{6,7},{7,5},{5,3},{3,1},{1,0},{8,10},{10,12},{12... | collective-permute-start | bytes 786440 | tf_op jit(solution)/shard_map/ppermute | solution.py:292
  48.0 6.7 %collective-permute-start.15 = (bf16[128,1024]{1,0:T(8,128)(2,1)S(1)}, bf16[128,1024]{1,0:T(8,128)(2,1)S(1)}, u32[]{:S(2)}, u32[]{:S(2)}) collective-permute-start(bf16[128,1024]{1,0:T(8,128)(2,1)S(1)} %add_convert_fusion.4), channel_id=1, source_target_pairs={{2,0},{4,2},{6,4},{7,6},{5,7},{3,5},{1,3},{0,1},{10,8},{12,10},{14... | collective-permute-start | bytes 786440 | tf_op jit(solution)/shard_map/ppermute | solution.py:295
  48.6 11.4 %collective-permute-start.12 = (bf16[1024,256]{1,0:T(8,128)(2,1)S(1)}, bf16[1024,256]{1,0:T(8,128)(2,1)S(1)}, u32[]{:S(2)}, u32[]{:S(2)}) collective-permute-start(bf16[1024,256]{1,0:T(8,128)(2,1)S(1)} %add_convert_fusion), channel_id=1, source_target_pairs={{0,16},{8,24},{16,0},{24,8},{1,17},{9,25},{17,1},{25,9},{2,18},{10... | collective-permute-start | bytes 1572872 | tf_op jit(solution)/shard_map/ppermute | solution.py:333
  53.1 7.2 %collective-permute-start.20 = (bf16[128,1024]{1,0:T(8,128)(2,1)S(1)}, bf16[128,1024]{1,0:T(8,128)(2,1)S(1)}, u32[]{:S(2)}, u32[]{:S(2)}) collective-permute-start(bf16[128,1024]{1,0:T(8,128)(2,1)S(1)} %add_convert_fusion.1), channel_id=1, source_target_pairs={{0,2},{2,4},{4,6},{6,7},{7,5},{5,3},{3,1},{1,0},{8,10},{10,12},{12... | collective-permute-start | bytes 786440 | tf_op jit(solution)/shard_map/ppermute | solution.py:292
  54.8 6.4 %collective-permute-start.16 = (bf16[128,1024]{1,0:T(8,128)(2,1)S(1)}, bf16[128,1024]{1,0:T(8,128)(2,1)S(1)}, u32[]{:S(2)}, u32[]{:S(2)}) collective-permute-start(bf16[128,1024]{1,0:T(8,128)(2,1)S(1)} %add_convert_fusion.3), channel_id=1, source_target_pairs={{2,0},{4,2},{6,4},{7,6},{5,7},{3,5},{1,3},{0,1},{10,8},{12,10},{14... | collective-permute-start | bytes 786440 | tf_op jit(solution)/shard_map/ppermute | solution.py:295
